TPU v7x, 32 devices: a whole 2x2x4 slice. The times are simulated.
32 devices in a mesh: tm: 16 (over z, x, core), head: 2 (over y).
Axes of the slice: x: 2, y: 2, z: 4, core: 2. Of those that a mesh axis runs over, the one named last changes fastest.
Arguments:
- audio_frames: bfloat16 [4096, 1024], P('tm', 'head'), may hold values from -50 to 50
- video_frames: bfloat16 [4096, 1024], P('tm', 'head'), may hold values from -50 to 50
- recording: int32 [4096], P('tm'), may hold values from 0 to 3, never falling along the last dimension, each value on 1 to 2048 neighbouring positions
- audio_query: bfloat16 [1024, 1024], P(None, 'head'), may hold values from -0.1875 to 0.1875
- video_key: bfloat16 [1024, 1024], P(None, 'head'), may hold values from -0.1875 to 0.1875
Outputs:
- audio_attended: bfloat16 [4096, 1024], P('tm', 'head')
- video_attended: bfloat16 [4096, 1024], P('tm', 'head')
Inputs may be any that keep to these rules, and one draw needn't show every extreme that they name: Ids never fall along the frames; each recording holds 1 to 2048 frames, and one holds exactly 2048.
All inputs are finite; a program needn't handle non-finite values.
Results may differ from a plain program's by a relative error of at most 0.019.
The roundings to bfloat16 on the way count: a program that leaves them out, or rounds other values in their place, can miss the bound.
Values may be sent and summed in bfloat16 or wider, within the bound.
No kernel may reach another device: no remote copies, remote signals or barrier semaphores. Data moves between devices by JAX's collectives and lax.ppermute only.
A program may use at most 128 MiB of HBM per device.

v0:
```python
import jax
import jax.numpy as jnp
from jax import lax
from jax.sharding import PartitionSpec as P

HEAD = 64
RADIUS = 3


NEG = -1e30


def shifted(x, axis, by):
    length = lax.axis_size(axis)
    return lax.ppermute(x, axis, [(i, (i + by) % length) for i in range(length)])


def as_sent(x):

    def short(part):
        return part.astype(jnp.bfloat16) if part.dtype == jnp.float32 else part

    return jax.tree.map(short, x)


def tile_scores(queries, key_block):
    return jnp.einsum(
        "the,uhe->htu", queries, key_block, preferred_element_type=jnp.float32
    ) * HEAD ** (-0.5)


def scale_rows(numerator, factor, head_count):
    row_count = numerator.shape[0]
    return (numerator.reshape(row_count, head_count, -1) * factor.T[:, :, None]).reshape(
        row_count, -1
    )


def audio_update(carried, scores, allowed, values):
    running_max, totals, numerator = carried
    head_count = scores.shape[0]
    new_peak = jnp.maximum(running_max, jnp.max(jnp.where(allowed[None], scores, NEG), axis=2))
    factor = jnp.exp(running_max - new_peak)
    weights = jnp.where(allowed[None], jnp.exp(scores - new_peak[:, :, None]), 0.0)
    totals = totals * factor + jnp.sum(weights, axis=2)
    mixed = jnp.einsum(
        "htu,uhe->the",
        weights.astype(jnp.bfloat16),
        values.reshape(values.shape[0], head_count, -1),
        preferred_element_type=jnp.float32,
    )
    numerator = scale_rows(numerator, factor, head_count) + mixed.reshape(mixed.shape[0], -1)
    return (new_peak, totals, numerator)


def video_update(carried, scores, allowed, values):
    running_max, totals, numerator = carried
    head_count = scores.shape[0]
    new_peak = jnp.maximum(running_max, jnp.max(jnp.where(allowed[None], scores, NEG), axis=1))
    factor = jnp.exp(running_max - new_peak)
    weights = jnp.where(allowed[None], jnp.exp(scores - new_peak[:, None, :]), 0.0)
    totals = totals * factor + jnp.sum(weights, axis=1)
    mixed = jnp.einsum(
        "htu,the->uhe",
        weights.astype(jnp.bfloat16),
        values.reshape(values.shape[0], head_count, -1),
        preferred_element_type=jnp.float32,
    )
    numerator = scale_rows(numerator, factor, head_count) + mixed.reshape(mixed.shape[0], -1)
    return (new_peak, totals, numerator)


def finish(carried):
    head_count = carried[0].shape[0]
    row_count = carried[2].shape[0]
    shaped = carried[2].reshape(row_count, head_count, -1) / carried[1].T[:, :, None]
    return shaped.reshape(row_count, -1).astype(jnp.bfloat16)


def visit_tile(queries, recording, audio_frames, audio_state, moving_pack, video_state):
    block_keys, block_values, block_ids = moving_pack
    allowed = recording[:, None] == block_ids[None, :]
    key_block = block_keys.reshape(block_keys.shape[0], queries.shape[1], -1)
    scores = tile_scores(queries, key_block)
    return (
        audio_update(audio_state, scores, allowed, block_values),
        video_update(video_state, scores, allowed, audio_frames),
    )


def local(audio_frames, video_frames, recording, audio_query, video_key):
    row_count = audio_frames.shape[0]
    head_count = audio_query.shape[1] // HEAD
    whole_audio, whole_video = (
        lax.all_gather(audio_frames, "head", axis=1, tiled=True),
        lax.all_gather(video_frames, "head", axis=1, tiled=True),
    )
    queries = jnp.dot(whole_audio, audio_query, preferred_element_type=jnp.float32).astype(
        jnp.bfloat16
    )
    key_rows = jnp.dot(whole_video, video_key, preferred_element_type=jnp.float32).astype(
        jnp.bfloat16
    )
    queries = queries.reshape(row_count, head_count, HEAD)
    neutral = (
        jnp.full((head_count, row_count), NEG, jnp.float32),
        jnp.zeros((head_count, row_count), jnp.float32),
        jnp.zeros((row_count, head_count * HEAD), jnp.float32),
    )
    moving_pack = tuple(shifted((key_rows, video_frames, recording), "tm", -RADIUS))
    audio_state, video_state = visit_tile(
        queries, recording, audio_frames, neutral, moving_pack, neutral
    )
    for offset in range(2 * RADIUS):
        moved = shifted(
            (
                moving_pack[0],
                moving_pack[1],
                as_sent(moving_pack[2]),
                as_sent(video_state[0]),
                as_sent(video_state[1]),
                as_sent(video_state[2]),
            ),
            "tm",
            1,
        )
        moving_pack, video_state = (tuple(moved[:3]), tuple(moved[3:]))
        audio_state, video_state = visit_tile(
            queries, recording, audio_frames, audio_state, moving_pack, video_state
        )
    video_state = tuple(
        shifted(
            (as_sent(video_state[0]), as_sent(video_state[1]), as_sent(video_state[2])),
            "tm",
            -RADIUS,
        )
    )
    return (finish(audio_state), finish(video_state))


def solution(mesh):
    return jax.shard_map(
        local,
        mesh=mesh,
        in_specs=(P("tm", "head"), P("tm", "head"), P("tm"), P(None, "head"), P(None, "head")),
        out_specs=(P("tm", "head"), P("tm", "head")),
        check_vma=False,
    )
```

profile of v0, /device:TPU:0, one launch (start us, length us, event | category | flops | bytes accessed | tf_op | source)
XLA Modules:
  0.0 220.8 jit_solution(17172767227695402163)
XLA Ops:
  0.7 4.5 %collective-permute-start = (s32[256]{0:T(256)}, s32[256]{0:T(256)S(1)}, u32[]{:S(2)}, u32[]{:S(2)}) collective-permute-start(s32[256]{0:T(256)} %param.7), channel_id=1, source_target_pairs={{0,26},{2,28},{4,30},{6,0},{8,2},{10,4},{12,6},{14,8},{16,10},{18,... | collective-permute-start | bytes 3080 | tf_op jit(solution)/shard_map/ppermute | solution.py:15
  5.2 1.5 collective-permute-done
  6.7 1.0 collective-permute-start.3
  7.7 4.7 %collective-permute-done.3 = s32[256]{0:T(256)S(1)} collective-permute-done((s32[256]{0:T(256)S(1)}, s32[256]{0:T(256)S(1)}, u32[]{:S(2)}, u32[]{:S(2)}) %collective-permute-start.3) | collective-permute-done | bytes 1056 | tf_op jit(solution)/shard_map/ppermute | solution.py:15
  12.4 3.5 %collective-permute-start.2 = (bf16[256,512]{1,0:T(8,128)(2,1)}, bf16[256,512]{1,0:T(8,128)(2,1)}, u32[]{:S(2)}, u32[]{:S(2)}) collective-permute-start(bf16[256,512]{1,0:T(8,128)(2,1)} %param.6), channel_id=1, source_target_pairs={{0,26},{2,28},{4,30},{6,0},{8,2},{10,4},{12,6},{14,8},{16,10},{18,... | collective-permute-start | bytes 786440 | tf_op jit(solution)/shard_map/ppermute | solution.py:15
  15.9 2.2 %collective-permute-done.6 = s32[256]{0:T(256)S(1)} collective-permute-done((s32[256]{0:T(256)S(1)}, s32[256]{0:T(256)S(1)}, u32[]{:S(2)}, u32[]{:S(2)}) %collective-permute-start.6) | collective-permute-done | bytes 1056 | tf_op jit(solution)/shard_map/ppermute | solution.py:15
  18.1 8.5 %all_gather.7 = bf16[256,1024]{1,0:T(8,128)(2,1)S(1)} all-gather(bf16[256,512]{1,0:T(8,128)(2,1)} %param.6), channel_id=1, replica_groups=mesh['tm'=16,'head'=2] {'head'}, dimensions={1}, use_global_device_ids=true | all-gather | bytes 786432 | tf_op jit(solution)/shard_map/all_gather | solution.py:96
  27.2 5.2 %collective-permute-done.12 = s32[256]{0:T(256)S(1)} collective-permute-done((s32[256]{0:T(256)S(1)}, s32[256]{0:T(256)S(1)}, u32[]{:S(2)}, u32[]{:S(2)}) %collective-permute-start.12) | collective-permute-done | bytes 1056 | tf_op jit(solution)/shard_map/ppermute | solution.py:15
  32.3 8.8 %all_gather.6 = bf16[256,1024]{1,0:T(8,128)(2,1)S(1)} all-gather(bf16[256,512]{1,0:T(8,128)(2,1)S(1)} %copy-done.14), channel_id=1, replica_groups=mesh['tm'=16,'head'=2] {'head'}, dimensions={1}, use_global_device_ids=true | all-gather | bytes 786432 | tf_op jit(solution)/shard_map/all_gather | solution.py:95
  41.9 5.0 %collective-permute-done.18 = s32[256]{0:T(256)S(1)} collective-permute-done((s32[256]{0:T(256)S(1)}, s32[256]{0:T(256)S(1)}, u32[]{:S(2)}, u32[]{:S(2)}) %collective-permute-start.18) | collective-permute-done | bytes 1056 | tf_op jit(solution)/shard_map/ppermute | solution.py:15
  46.8 1.0 broadcast_compare_fusion.4
  47.9 1.1 copy.51
  49.0 2.5 %select_reduce_fusion.12 = (f32[8,256]{1,0:T(8,128)S(1)}, f32[8,256]{1,0:T(8,128)}, f32[8,256,256]{2,1,0:T(8,128)}) fusion(pred[256,256]{1,0:T(8,128)(4,1)S(1)} %get-tuple-element.79, bf16[256,8,64]{0,2,1:T(8,128)(2,1)S(1)} %bitcast.303, bf16[256,8,64]{0,2,1:T(8,128)(2,1)S(1)} %bitcast.316), kind=kOutput, calls=%fused_computation.26 | convolution fusion | flops 69201920 | bytes 2703360 | tf_op jit(solution)/shard_map/the,uhe->htu/dot_general | solution.py:27
  51.6 1.8 copy.52
  54.0 6.3 %collective-permute-done.4 = bf16[256,512]{1,0:T(8,128)(2,1)} collective-permute-done((bf16[256,512]{1,0:T(8,128)(2,1)}, bf16[256,512]{1,0:T(8,128)(2,1)}, u32[]{:S(2)}, u32[]{:S(2)}) %collective-permute-start.4) | collective-permute-done | bytes 262176 | tf_op jit(solution)/shard_map/ppermute | solution.py:15
  60.3 1.8 copy.53
  62.1 2.3 %select_reduce_fusion.10 = (f32[8,256]{1,0:T(8,128)}, f32[8,256]{1,0:T(8,128)}, f32[8,256,256]{2,1,0:T(8,128)S(1)}) fusion(pred[256,256]{1,0:T(8,128)(4,1)} %get-tuple-element.74, bf16[256,8,64]{0,2,1:T(8,128)(2,1)} %bitcast.304, bf16[256,8,64]{0,2,1:T(8,128)(2,1)} %bitcast.317), kind=kOutput, calls=%fused_computation.24 | convolution fusion | flops 69201920 | bytes 2703360 | tf_op jit(solution)/shard_map/the,uhe->htu/dot_general | solution.py:27
  64.4 1.8 copy.54
  66.2 1.3 fusion.135
  67.5 2.1 fusion.55
  69.6 3.6 %collective-permute-done.7 = bf16[256,512]{1,0:T(8,128)(2,1)} collective-permute-done((bf16[256,512]{1,0:T(8,128)(2,1)}, bf16[256,512]{1,0:T(8,128)(2,1)}, u32[]{:S(2)}, u32[]{:S(2)}) %collective-permute-start.7) | collective-permute-done | bytes 262176 | tf_op jit(solution)/shard_map/ppermute | solution.py:15
  73.2 1.8 copy.55
  75.0 1.0 collective-permute-done.8
  76.0 1.8 copy.56
  77.8 3.5 %select_reduce_fusion.8 = (f32[8,256]{1,0:T(8,128)}, f32[8,256]{1,0:T(8,128)}, f32[8,256,256]{2,1,0:T(8,128)}) fusion(pred[256,256]{1,0:T(8,128)(4,1)} %get-tuple-element.73, bf16[256,8,64]{0,2,1:T(8,128)(2,1)} %bitcast.305, bf16[256,8,64]{0,2,1:T(8,128)(2,1)} %bitcast.310), kind=kOutput, calls=%fused_computation.22 | convolution fusion | flops 69201920 | bytes 2703360 | tf_op jit(solution)/shard_map/the,uhe->htu/dot_general | solution.py:27
  82.0 1.8 copy.57
  83.8 2.8 %collective-permute-done.11 = bf16[256,512]{1,0:T(8,128)(2,1)} collective-permute-done((bf16[256,512]{1,0:T(8,128)(2,1)}, bf16[256,512]{1,0:T(8,128)(2,1)}, u32[]{:S(2)}, u32[]{:S(2)}) %collective-permute-start.11) | collective-permute-done | bytes 262176 | tf_op jit(solution)/shard_map/ppermute | solution.py:15
  86.6 1.8 copy.58
  88.4 3.6 %select_reduce_fusion.6 = (f32[8,256]{1,0:T(8,128)}, f32[8,256]{1,0:T(8,128)}, f32[8,256,256]{2,1,0:T(8,128)}) fusion(pred[256,256]{1,0:T(8,128)(4,1)} %get-tuple-element.75, bf16[256,8,64]{0,2,1:T(8,128)(2,1)} %bitcast.306, bf16[256,8,64]{0,2,1:T(8,128)(2,1)} %bitcast.311), kind=kOutput, calls=%fused_computation.20 | convolution fusion | flops 69201920 | bytes 2703360 | tf_op jit(solution)/shard_map/the,uhe->htu/dot_general | solution.py:27
  92.0 1.8 copy.59
  93.8 3.4 %collective-permute-done.14 = bf16[256,512]{1,0:T(8,128)(2,1)} collective-permute-done((bf16[256,512]{1,0:T(8,128)(2,1)}, bf16[256,512]{1,0:T(8,128)(2,1)}, u32[]{:S(2)}, u32[]{:S(2)}) %collective-permute-start.14) | collective-permute-done | bytes 262176 | tf_op jit(solution)/shard_map/ppermute | solution.py:15
  97.2 1.8 copy.60
  99.0 3.6 %select_reduce_fusion.4 = (f32[8,256]{1,0:T(8,128)}, f32[8,256]{1,0:T(8,128)}, f32[8,256,256]{2,1,0:T(8,128)}) fusion(pred[256,256]{1,0:T(8,128)(4,1)S(1)} %get-tuple-element.76, bf16[256,8,64]{0,2,1:T(8,128)(2,1)} %bitcast.307, bf16[256,8,64]{0,2,1:T(8,128)(2,1)} %bitcast.312), kind=kOutput, calls=%fused_computation.18 | convolution fusion | flops 69201920 | bytes 2703360 | tf_op jit(solution)/shard_map/the,uhe->htu/dot_general | solution.py:27
  102.6 1.8 copy.61
  104.4 3.4 %collective-permute-done.17 = bf16[256,512]{1,0:T(8,128)(2,1)} collective-permute-done((bf16[256,512]{1,0:T(8,128)(2,1)}, bf16[256,512]{1,0:T(8,128)(2,1)}, u32[]{:S(2)}, u32[]{:S(2)}) %collective-permute-start.17) | collective-permute-done | bytes 262176 | tf_op jit(solution)/shard_map/ppermute | solution.py:15
  107.8 1.8 copy.62
  109.6 3.5 %select_reduce_fusion.2 = (f32[8,256]{1,0:T(8,128)}, f32[8,256]{1,0:T(8,128)}, f32[8,256,256]{2,1,0:T(8,128)}) fusion(pred[256,256]{1,0:T(8,128)(4,1)S(1)} %get-tuple-element.77, bf16[256,8,64]{0,2,1:T(8,128)(2,1)} %bitcast.308, bf16[256,8,64]{0,2,1:T(8,128)(2,1)} %bitcast.313), kind=kOutput, calls=%fused_computation.16 | convolution fusion | flops 69201920 | bytes 2703360 | tf_op jit(solution)/shard_map/the,uhe->htu/dot_general | solution.py:27
  113.2 1.8 copy.63
  115.0 3.7 %select_reduce_fusion = (f32[8,256]{1,0:T(8,128)}, f32[8,256]{1,0:T(8,128)S(1)}, f32[8,256,256]{2,1,0:T(8,128)}) fusion(pred[256,256]{1,0:T(8,128)(4,1)} %get-tuple-element.78, bf16[256,8,64]{0,2,1:T(8,128)(2,1)} %bitcast.309, bf16[256,8,64]{0,2,1:T(8,128)(2,1)} %bitcast.314), kind=kOutput, calls=%fused_computation.14 | convolution fusion | flops 69201920 | bytes 2703360 | tf_op jit(solution)/shard_map/the,uhe->htu/dot_general | solution.py:27
  118.7 1.4 fusion.153
  120.2 2.5 %fusion.14 = (f32[8,256]{1,0:T(8,128)S(1)}, f32[8,256]{1,0:T(8,128)}) fusion(f32[8,256,256]{2,1,0:T(8,128)S(1)} %copy-done.6, f32[8,256]{1,0:T(8,128)} %broadcast_maximum_fusion, pred[256,256]{1,0:T(8,128)(4,1)S(1)} %copy-done.22, f32[8,256]{1,0:T(8,128)S(1)} %get-tuple-element.72), kind=kLoop, calls=%fused_computation.42 | loop fusion | flops 3141632 | bytes 2195456 | tf_op jit(solution)/shard_map/reduce_sum | solution.py:62
  123.0 1.8 fusion.16
  124.8 3.9 %collective-permute-done.34 = bf16[8,256]{1,0:T(8,128)(2,1)S(1)} collective-permute-done((bf16[8,256]{1,0:T(8,128)(2,1)S(1)}, bf16[8,256]{1,0:T(8,128)(2,1)S(1)}, u32[]{:S(2)}, u32[]{:S(2)}) %collective-permute-start.34) | collective-permute-done | bytes 4128 | tf_op jit(solution)/shard_map/ppermute | solution.py:15
  129.3 1.2 fusion.43
  130.5 1.8 copy.64
  132.3 2.9 %collective-permute-done.24 = bf16[8,256]{1,0:T(8,128)(2,1)S(1)} collective-permute-done((bf16[8,256]{1,0:T(8,128)(2,1)}, bf16[8,256]{1,0:T(8,128)(2,1)S(1)}, u32[]{:S(2)}, u32[]{:S(2)}) %collective-permute-start.24) | collective-permute-done | bytes 4128 | tf_op jit(solution)/shard_map/ppermute | solution.py:15
  136.0 2.9 %fusion.18 = (f32[8,256]{1,0:T(8,128)S(1)}, f32[8,256]{1,0:T(8,128)S(1)}) fusion(f32[8,256,256]{2,1,0:T(8,128)} %get-tuple-element.86, f32[8,256]{1,0:T(8,128)S(1)} %get-tuple-element.41, pred[256,256]{1,0:T(8,128)(4,1)} %get-tuple-element.73, f32[8,256]{1,0:T(8,128)} %get-tuple-element.54), kind=kLoop, calls=%fused_computation.46 | loop fusion | flops 3141632 | bytes 2195456 | tf_op jit(solution)/shard_map/reduce_sum | solution.py:62
  139.9 5.2 %collective-permute-done.26 = bf16[8,256]{1,0:T(8,128)(2,1)S(1)} collective-permute-done((bf16[8,256]{1,0:T(8,128)(2,1)S(1)}, bf16[8,256]{1,0:T(8,128)(2,1)S(1)}, u32[]{:S(2)}, u32[]{:S(2)}) %collective-permute-start.26) | collective-permute-done | bytes 4128 | tf_op jit(solution)/shard_map/ppermute | solution.py:15
  145.2 1.2 fusion.20
  147.0 5.2 %collective-permute-done.28 = bf16[8,256]{1,0:T(8,128)(2,1)S(1)} collective-permute-done((bf16[8,256]{1,0:T(8,128)(2,1)S(1)}, bf16[8,256]{1,0:T(8,128)(2,1)S(1)}, u32[]{:S(2)}, u32[]{:S(2)}) %collective-permute-start.28) | collective-permute-done | bytes 4128 | tf_op jit(solution)/shard_map/ppermute | solution.py:15
  152.2 1.2 fusion.22
  154.1 5.2 %collective-permute-done.30 = bf16[8,256]{1,0:T(8,128)(2,1)S(1)} collective-permute-done((bf16[8,256]{1,0:T(8,128)(2,1)S(1)}, bf16[8,256]{1,0:T(8,128)(2,1)S(1)}, u32[]{:S(2)}, u32[]{:S(2)}) %collective-permute-start.30) | collective-permute-done | bytes 4128 | tf_op jit(solution)/shard_map/ppermute | solution.py:15
  159.3 1.2 fusion.24
  161.3 5.2 %collective-permute-done.32 = bf16[8,256]{1,0:T(8,128)(2,1)S(1)} collective-permute-done((bf16[8,256]{1,0:T(8,128)(2,1)S(1)}, bf16[8,256]{1,0:T(8,128)(2,1)S(1)}, u32[]{:S(2)}, u32[]{:S(2)}) %collective-permute-start.32) | collective-permute-done | bytes 4128 | tf_op jit(solution)/shard_map/ppermute | solution.py:15
  166.5 1.2 fusion.26
  169.6 1.1 fusion.112
  171.5 7.9 %collective-permute-done.23 = bf16[256,512]{0,1:T(8,128)(2,1)S(1)} collective-permute-done((bf16[256,512]{0,1:T(8,128)(2,1)S(1)}, bf16[256,512]{0,1:T(8,128)(2,1)S(1)}, u32[]{:S(2)}, u32[]{:S(2)}) %collective-permute-start.23) | collective-permute-done | bytes 262176 | tf_op jit(solution)/shard_map/ppermute | solution.py:15
  180.2 7.9 %collective-permute-done.25 = bf16[256,512]{0,1:T(8,128)(2,1)S(1)} collective-permute-done((bf16[256,512]{0,1:T(8,128)(2,1)S(1)}, bf16[256,512]{0,1:T(8,128)(2,1)S(1)}, u32[]{:S(2)}, u32[]{:S(2)}) %collective-permute-start.25) | collective-permute-done | bytes 262176 | tf_op jit(solution)/shard_map/ppermute | solution.py:15
  188.8 7.9 %collective-permute-done.27 = bf16[256,512]{0,1:T(8,128)(2,1)S(1)} collective-permute-done((bf16[256,512]{0,1:T(8,128)(2,1)S(1)}, bf16[256,512]{0,1:T(8,128)(2,1)S(1)}, u32[]{:S(2)}, u32[]{:S(2)}) %collective-permute-start.27) | collective-permute-done | bytes 262176 | tf_op jit(solution)/shard_map/ppermute | solution.py:15
  197.4 7.9 %collective-permute-done.29 = bf16[256,512]{0,1:T(8,128)(2,1)S(1)} collective-permute-done((bf16[256,512]{0,1:T(8,128)(2,1)S(1)}, bf16[256,512]{0,1:T(8,128)(2,1)S(1)}, u32[]{:S(2)}, u32[]{:S(2)}) %collective-permute-start.29) | collective-permute-done | bytes 262176 | tf_op jit(solution)/shard_map/ppermute | solution.py:15
  206.0 8.0 %collective-permute-done.31 = bf16[256,512]{0,1:T(8,128)(2,1)S(1)} collective-permute-done((bf16[256,512]{0,1:T(8,128)(2,1)S(1)}, bf16[256,512]{0,1:T(8,128)(2,1)S(1)}, u32[]{:S(2)}, u32[]{:S(2)}) %collective-permute-start.31) | collective-permute-done | bytes 262176 | tf_op jit(solution)/shard_map/ppermute | solution.py:15
  214.7 0.8 copy.66
  215.5 4.4 %collective-permute-done.33 = bf16[256,512]{0,1:T(8,128)(2,1)S(1)} collective-permute-done((bf16[256,512]{0,1:T(8,128)(2,1)S(1)}, bf16[256,512]{0,1:T(8,128)(2,1)S(1)}, u32[]{:S(2)}, u32[]{:S(2)}) %collective-permute-start.33) | collective-permute-done | bytes 262176 | tf_op jit(solution)/shard_map/ppermute | solution.py:15
  219.9 0.8 copy.67
  (209 shorter events, 13.1 us)
Async XLA Ops:
  0.6 26.0 %copy-start = (bf16[1024,512]{1,0:T(8,128)(2,1)S(1)}, bf16[1024,512]{1,0:T(8,128)(2,1)}, u32[]{:S(2)}) copy-start(bf16[1024,512]{1,0:T(8,128)(2,1)} %param.9) | copy-start | bytes 3145732
  0.6 31.7 %copy-start.14 = (bf16[256,512]{1,0:T(8,128)(2,1)S(1)}, bf16[256,512]{1,0:T(8,128)(2,1)}, u32[]{:S(2)}) copy-start(bf16[256,512]{1,0:T(8,128)(2,1)} %param.5) | copy-start | bytes 786436
  0.7 40.5 %copy-start.13 = (bf16[1024,512]{1,0:T(8,128)(2,1)S(1)}, bf16[1024,512]{1,0:T(8,128)(2,1)}, u32[]{:S(2)}) copy-start(bf16[1024,512]{1,0:T(8,128)(2,1)} %param.8) | copy-start | bytes 3145732
  0.7 6.1 %collective-permute-start = (s32[256]{0:T(256)}, s32[256]{0:T(256)S(1)}, u32[]{:S(2)}, u32[]{:S(2)}) collective-permute-start(s32[256]{0:T(256)} %param.7), channel_id=1, source_target_pairs={{0,26},{2,28},{4,30},{6,0},{8,2},{10,4},{12,6},{14,8},{16,10},{18,... | collective-permute-start | bytes 3080 | tf_op jit(solution)/shard_map/ppermute | solution.py:15
  6.7 5.7 %collective-permute-start.3 = (s32[256]{0:T(256)S(1)}, s32[256]{0:T(256)S(1)}, u32[]{:S(2)}, u32[]{:S(2)}) collective-permute-start(s32[256]{0:T(256)S(1)} %collective-permute-done), channel_id=1, source_target_pairs={{0,2},{2,4},{4,6},{6,8},{8,10},{10,12},{12,14},{14,16},{16,18},{18... | collective-permute-start | bytes 3080 | tf_op jit(solution)/shard_map/ppermute | solution.py:15
  12.4 5.7 %collective-permute-start.6 = (s32[256]{0:T(256)S(1)}, s32[256]{0:T(256)S(1)}, u32[]{:S(2)}, u32[]{:S(2)}) collective-permute-start(s32[256]{0:T(256)S(1)} %collective-permute-done.3), channel_id=1, source_target_pairs={{0,2},{2,4},{4,6},{6,8},{8,10},{10,12},{12,14},{14,16},{16,18},{18... | collective-permute-start | bytes 3080 | tf_op jit(solution)/shard_map/ppermute | solution.py:15
  12.4 39.1 %collective-permute-start.2 = (bf16[256,512]{1,0:T(8,128)(2,1)}, bf16[256,512]{1,0:T(8,128)(2,1)}, u32[]{:S(2)}, u32[]{:S(2)}) collective-permute-start(bf16[256,512]{1,0:T(8,128)(2,1)} %param.6), channel_id=1, source_target_pairs={{0,26},{2,28},{4,30},{6,0},{8,2},{10,4},{12,6},{14,8},{16,10},{18,... | collective-permute-start | bytes 786440 | tf_op jit(solution)/shard_map/ppermute | solution.py:15
  18.1 8.5 %collective-permute-start.9 = (s32[256]{0:T(256)S(1)}, s32[256]{0:T(256)S(1)}, u32[]{:S(2)}, u32[]{:S(2)}) collective-permute-start(s32[256]{0:T(256)S(1)} %collective-permute-done.6), channel_id=1, source_target_pairs={{0,2},{2,4},{4,6},{6,8},{8,10},{10,12},{12,14},{14,16},{16,18},{18... | collective-permute-start | bytes 3080 | tf_op jit(solution)/shard_map/ppermute | solution.py:15
  26.6 5.7 %collective-permute-start.12 = (s32[256]{0:T(256)S(1)}, s32[256]{0:T(256)S(1)}, u32[]{:S(2)}, u32[]{:S(2)}) collective-permute-start(s32[256]{0:T(256)S(1)} %collective-permute-done.9), channel_id=1, source_target_pairs={{0,2},{2,4},{4,6},{6,8},{8,10},{10,12},{12,14},{14,16},{16,18},{18... | collective-permute-start | bytes 3080 | tf_op jit(solution)/shard_map/ppermute | solution.py:15
  27.1 19.8 %copy-start.57 = (s32[256]{0:T(256)S(1)}, s32[256]{0:T(256)}, u32[]{:S(2)}) copy-start(s32[256]{0:T(256)} %param.7) | copy-start | bytes 3076
  27.1 20.8 %collective-permute-start.1 = (bf16[256,512]{1,0:T(8,128)(2,1)S(1)}, bf16[256,512]{1,0:T(8,128)(2,1)}, u32[]{:S(2)}, u32[]{:S(2)}) collective-permute-start(bf16[256,512]{1,0:T(8,128)(2,1)S(1)} %convolution_convert_fusion), channel_id=1, source_target_pairs={{0,26},{2,28},{4,30},{6,0},{8,2},{10,4},{12,6},{14,8},{16,10},{18,... | collective-permute-start | bytes 786440 | tf_op jit(solution)/shard_map/ppermute | solution.py:15
  32.3 8.8 %collective-permute-start.15 = (s32[256]{0:T(256)S(1)}, s32[256]{0:T(256)S(1)}, u32[]{:S(2)}, u32[]{:S(2)}) collective-permute-start(s32[256]{0:T(256)S(1)} %collective-permute-done.12), channel_id=1, source_target_pairs={{0,2},{2,4},{4,6},{6,8},{8,10},{10,12},{12,14},{14,16},{16,18},{18... | collective-permute-start | bytes 3080 | tf_op jit(solution)/shard_map/ppermute | solution.py:15
  41.1 5.7 %collective-permute-start.18 = (s32[256]{0:T(256)S(1)}, s32[256]{0:T(256)S(1)}, u32[]{:S(2)}, u32[]{:S(2)}) collective-permute-start(s32[256]{0:T(256)S(1)} %collective-permute-done.15), channel_id=1, source_target_pairs={{0,2},{2,4},{4,6},{6,8},{8,10},{10,12},{12,14},{14,16},{16,18},{18... | collective-permute-start | bytes 3080 | tf_op jit(solution)/shard_map/ppermute | solution.py:15
  41.9 11.5 %copy-start.26 = (bf16[256,512]{0,1:T(8,128)(2,1)}, bf16[256,512]{0,1:T(8,128)(2,1)S(1)}, u32[]{:S(2)}) copy-start(bf16[256,512]{0,1:T(8,128)(2,1)S(1)} %copy.50) | copy-start | bytes 786436
  47.8 14.3 %copy-start.21 = (pred[256,256]{1,0:T(8,128)(4,1)}, pred[256,256]{1,0:T(8,128)(4,1)S(1)}, u32[]{:S(2)}) copy-start(pred[256,256]{1,0:T(8,128)(4,1)S(1)} %get-tuple-element.79) | copy-start | bytes 196612
  51.5 10.6 %copy-start.32 = (f32[8,256]{1,0:T(8,128)}, f32[8,256]{1,0:T(8,128)S(1)}, u32[]{:S(2)}) copy-start(f32[8,256]{1,0:T(8,128)S(1)} %get-tuple-element.20) | copy-start | bytes 24580
  51.5 8.8 %collective-permute-start.4 = (bf16[256,512]{1,0:T(8,128)(2,1)}, bf16[256,512]{1,0:T(8,128)(2,1)}, u32[]{:S(2)}, u32[]{:S(2)}) collective-permute-start(bf16[256,512]{1,0:T(8,128)(2,1)} %collective-permute-done.1), channel_id=1, source_target_pairs={{0,2},{2,4},{4,6},{6,8},{8,10},{10,12},{12,14},{14,16},{16,18},{18... | collective-permute-start | bytes 786440 | tf_op jit(solution)/shard_map/ppermute | solution.py:15
  51.5 14.7 %collective-permute-start.22 = (bf16[8,256]{1,0:T(8,128)(2,1)S(1)}, bf16[8,256]{1,0:T(8,128)(2,1)S(1)}, u32[]{:S(2)}, u32[]{:S(2)}) collective-permute-start(bf16[8,256]{1,0:T(8,128)(2,1)S(1)} %fusion.150), channel_id=1, source_target_pairs={{0,2},{2,4},{4,6},{6,8},{8,10},{10,12},{12,14},{14,16},{16,18},{18... | collective-permute-start | bytes 12296 | tf_op jit(solution)/shard_map/ppermute | solution.py:15
  53.4 11.1 %collective-permute-start.5 = (bf16[256,512]{1,0:T(8,128)(2,1)}, bf16[256,512]{1,0:T(8,128)(2,1)}, u32[]{:S(2)}, u32[]{:S(2)}) collective-permute-start(bf16[256,512]{1,0:T(8,128)(2,1)} %collective-permute-done.2), channel_id=1, source_target_pairs={{0,2},{2,4},{4,6},{6,8},{8,10},{10,12},{12,14},{14,16},{16,18},{18... | collective-permute-start | bytes 786440 | tf_op jit(solution)/shard_map/ppermute | solution.py:15
  64.4 8.8 %collective-permute-start.7 = (bf16[256,512]{1,0:T(8,128)(2,1)}, bf16[256,512]{1,0:T(8,128)(2,1)}, u32[]{:S(2)}, u32[]{:S(2)}) collective-permute-start(bf16[256,512]{1,0:T(8,128)(2,1)} %collective-permute-done.4), channel_id=1, source_target_pairs={{0,2},{2,4},{4,6},{6,8},{8,10},{10,12},{12,14},{14,16},{16,18},{18... | collective-permute-start | bytes 786440 | tf_op jit(solution)/shard_map/ppermute | solution.py:15
  66.2 9.8 %collective-permute-start.8 = (bf16[256,512]{1,0:T(8,128)(2,1)}, bf16[256,512]{1,0:T(8,128)(2,1)}, u32[]{:S(2)}, u32[]{:S(2)}) collective-permute-start(bf16[256,512]{1,0:T(8,128)(2,1)} %collective-permute-done.5), channel_id=1, source_target_pairs={{0,2},{2,4},{4,6},{6,8},{8,10},{10,12},{12,14},{14,16},{16,18},{18... | collective-permute-start | bytes 786440 | tf_op jit(solution)/shard_map/ppermute | solution.py:15
  66.2 15.1 %copy-start.51 = (bf16[8,256]{1,0:T(8,128)(2,1)}, bf16[8,256]{1,0:T(8,128)(2,1)S(1)}, u32[]{:S(2)}) copy-start(bf16[8,256]{1,0:T(8,128)(2,1)S(1)} %collective-permute-done.22) | copy-start | bytes 12292
  73.2 8.8 %collective-permute-start.10 = (bf16[256,512]{1,0:T(8,128)(2,1)}, bf16[256,512]{1,0:T(8,128)(2,1)}, u32[]{:S(2)}, u32[]{:S(2)}) collective-permute-start(bf16[256,512]{1,0:T(8,128)(2,1)} %collective-permute-done.7), channel_id=1, source_target_pairs={{0,2},{2,4},{4,6},{6,8},{8,10},{10,12},{12,14},{14,16},{16,18},{18... | collective-permute-start | bytes 786440 | tf_op jit(solution)/shard_map/ppermute | solution.py:15
  77.8 8.8 %collective-permute-start.11 = (bf16[256,512]{1,0:T(8,128)(2,1)}, bf16[256,512]{1,0:T(8,128)(2,1)}, u32[]{:S(2)}, u32[]{:S(2)}) collective-permute-start(bf16[256,512]{1,0:T(8,128)(2,1)} %collective-permute-done.8), channel_id=1, source_target_pairs={{0,2},{2,4},{4,6},{6,8},{8,10},{10,12},{12,14},{14,16},{16,18},{18... | collective-permute-start | bytes 786440 | tf_op jit(solution)/shard_map/ppermute | solution.py:15
  82.0 10.0 %collective-permute-start.13 = (bf16[256,512]{1,0:T(8,128)(2,1)}, bf16[256,512]{1,0:T(8,128)(2,1)}, u32[]{:S(2)}, u32[]{:S(2)}) collective-permute-start(bf16[256,512]{1,0:T(8,128)(2,1)} %collective-permute-done.10), channel_id=1, source_target_pairs={{0,2},{2,4},{4,6},{6,8},{8,10},{10,12},{12,14},{14,16},{16,18},{18... | collective-permute-start | bytes 786440 | tf_op jit(solution)/shard_map/ppermute | solution.py:15
  88.4 8.8 %collective-permute-start.14 = (bf16[256,512]{1,0:T(8,128)(2,1)}, bf16[256,512]{1,0:T(8,128)(2,1)}, u32[]{:S(2)}, u32[]{:S(2)}) collective-permute-start(bf16[256,512]{1,0:T(8,128)(2,1)} %collective-permute-done.11), channel_id=1, source_target_pairs={{0,2},{2,4},{4,6},{6,8},{8,10},{10,12},{12,14},{14,16},{16,18},{18... | collective-permute-start | bytes 786440 | tf_op jit(solution)/shard_map/ppermute | solution.py:15
  92.0 10.6 %collective-permute-start.16 = (bf16[256,512]{1,0:T(8,128)(2,1)}, bf16[256,512]{1,0:T(8,128)(2,1)}, u32[]{:S(2)}, u32[]{:S(2)}) collective-permute-start(bf16[256,512]{1,0:T(8,128)(2,1)} %collective-permute-done.13), channel_id=1, source_target_pairs={{0,2},{2,4},{4,6},{6,8},{8,10},{10,12},{12,14},{14,16},{16,18},{18... | collective-permute-start | bytes 786440 | tf_op jit(solution)/shard_map/ppermute | solution.py:15
  99.0 8.8 %collective-permute-start.17 = (bf16[256,512]{1,0:T(8,128)(2,1)}, bf16[256,512]{1,0:T(8,128)(2,1)}, u32[]{:S(2)}, u32[]{:S(2)}) collective-permute-start(bf16[256,512]{1,0:T(8,128)(2,1)} %collective-permute-done.14), channel_id=1, source_target_pairs={{0,2},{2,4},{4,6},{6,8},{8,10},{10,12},{12,14},{14,16},{16,18},{18... | collective-permute-start | bytes 786440 | tf_op jit(solution)/shard_map/ppermute | solution.py:15
  102.6 10.5 %collective-permute-start.19 = (bf16[256,512]{1,0:T(8,128)(2,1)}, bf16[256,512]{1,0:T(8,128)(2,1)}, u32[]{:S(2)}, u32[]{:S(2)}) collective-permute-start(bf16[256,512]{1,0:T(8,128)(2,1)} %collective-permute-done.16), channel_id=1, source_target_pairs={{0,2},{2,4},{4,6},{6,8},{8,10},{10,12},{12,14},{14,16},{16,18},{18... | collective-permute-start | bytes 786440 | tf_op jit(solution)/shard_map/ppermute | solution.py:15
  109.6 20.9 %collective-permute-start.20 = (bf16[256,512]{1,0:T(8,128)(2,1)}, bf16[256,512]{1,0:T(8,128)(2,1)}, u32[]{:S(2)}, u32[]{:S(2)}) collective-permute-start(bf16[256,512]{1,0:T(8,128)(2,1)} %collective-permute-done.17), channel_id=1, source_target_pairs={{0,2},{2,4},{4,6},{6,8},{8,10},{10,12},{12,14},{14,16},{16,18},{18... | collective-permute-start | bytes 786440 | tf_op jit(solution)/shard_map/ppermute | solution.py:15
  115.0 7.7 %copy-start.33 = (f32[8,256]{1,0:T(8,128)S(1)}, f32[8,256]{1,0:T(8,128)}, u32[]{:S(2)}) copy-start(f32[8,256]{1,0:T(8,128)} %copy-done.32) | copy-start | bytes 24580
  115.0 8.0 %copy-start.11 = (pred[256,256]{1,0:T(8,128)(4,1)S(1)}, pred[256,256]{1,0:T(8,128)(4,1)}, u32[]{:S(2)}) copy-start(pred[256,256]{1,0:T(8,128)(4,1)} %get-tuple-element.74) | copy-start | bytes 196612
  120.1 8.5 %copy-start.52 = (bf16[8,256]{1,0:T(8,128)(2,1)S(1)}, bf16[8,256]{1,0:T(8,128)(2,1)}, u32[]{:S(2)}) copy-start(bf16[8,256]{1,0:T(8,128)(2,1)} %copy-done.51) | copy-start | bytes 12292
  120.1 9.1 %copy-start.40 = (f32[8,256]{1,0:T(8,128)S(1)}, f32[8,256]{1,0:T(8,128)}, u32[]{:S(2)}) copy-start(f32[8,256]{1,0:T(8,128)} %broadcast_maximum_fusion) | copy-start | bytes 24580
  122.7 6.0 %collective-permute-start.34 = (bf16[8,256]{1,0:T(8,128)(2,1)S(1)}, bf16[8,256]{1,0:T(8,128)(2,1)S(1)}, u32[]{:S(2)}, u32[]{:S(2)}) collective-permute-start(bf16[8,256]{1,0:T(8,128)(2,1)S(1)} %get-tuple-element.69), channel_id=1, source_target_pairs={{0,2},{2,4},{4,6},{6,8},{8,10},{10,12},{12,14},{14,16},{16,18},{18... | collective-permute-start | bytes 12296 | tf_op jit(solution)/shard_map/ppermute | solution.py:15
  129.3 5.9 %collective-permute-start.24 = (bf16[8,256]{1,0:T(8,128)(2,1)}, bf16[8,256]{1,0:T(8,128)(2,1)S(1)}, u32[]{:S(2)}, u32[]{:S(2)}) collective-permute-start(bf16[8,256]{1,0:T(8,128)(2,1)} %get-tuple-element.68), channel_id=1, source_target_pairs={{0,2},{2,4},{4,6},{6,8},{8,10},{10,12},{12,14},{14,16},{16,18},{18... | collective-permute-start | bytes 12296 | tf_op jit(solution)/shard_map/ppermute | solution.py:15
  130.5 38.8 %collective-permute-start.21 = (bf16[256,512]{0,1:T(8,128)(2,1)}, bf16[256,512]{0,1:T(8,128)(2,1)}, u32[]{:S(2)}, u32[]{:S(2)}) collective-permute-start(bf16[256,512]{0,1:T(8,128)(2,1)} %bitcast.40), channel_id=1, source_target_pairs={{0,2},{2,4},{4,6},{6,8},{8,10},{10,12},{12,14},{14,16},{16,18},{18... | collective-permute-start | bytes 786440 | tf_op jit(solution)/shard_map/ppermute | solution.py:15
  132.3 7.0 %collective-permute-start.35 = (bf16[8,256]{1,0:T(8,128)(2,1)S(1)}, bf16[8,256]{1,0:T(8,128)(2,1)S(1)}, u32[]{:S(2)}, u32[]{:S(2)}) collective-permute-start(bf16[8,256]{1,0:T(8,128)(2,1)S(1)} %copy-done.56), channel_id=1, source_target_pairs={{0,2},{2,4},{4,6},{6,8},{8,10},{10,12},{12,14},{14,16},{16,18},{18... | collective-permute-start | bytes 12296 | tf_op jit(solution)/shard_map/ppermute | solution.py:15
  135.9 9.2 %copy-start.55 = (f32[8,256]{1,0:T(8,128)S(1)}, f32[8,256]{1,0:T(8,128)}, u32[]{:S(2)}) copy-start(f32[8,256]{1,0:T(8,128)} %get-tuple-element.26) | copy-start | bytes 24580
  135.9 9.2 %copy-start.2 = (f32[8,256,256]{2,1,0:T(8,128)S(1)}, f32[8,256,256]{2,1,0:T(8,128)}, u32[]{:S(2)}) copy-start(f32[8,256,256]{2,1,0:T(8,128)} %get-tuple-element.85) | copy-start | bytes 6291460
  135.9 9.2 %copy-start.9 = (pred[256,256]{1,0:T(8,128)(4,1)S(1)}, pred[256,256]{1,0:T(8,128)(4,1)}, u32[]{:S(2)}) copy-start(pred[256,256]{1,0:T(8,128)(4,1)} %get-tuple-element.75) | copy-start | bytes 196612
  135.9 9.2 %copy-start.28 = (f32[8,256]{1,0:T(8,128)S(1)}, f32[8,256]{1,0:T(8,128)}, u32[]{:S(2)}) copy-start(f32[8,256]{1,0:T(8,128)} %get-tuple-element.53) | copy-start | bytes 24580
  139.3 5.8 %collective-permute-start.26 = (bf16[8,256]{1,0:T(8,128)(2,1)S(1)}, bf16[8,256]{1,0:T(8,128)(2,1)S(1)}, u32[]{:S(2)}, u32[]{:S(2)}) collective-permute-start(bf16[8,256]{1,0:T(8,128)(2,1)S(1)} %get-tuple-element.66), channel_id=1, source_target_pairs={{0,2},{2,4},{4,6},{6,8},{8,10},{10,12},{12,14},{14,16},{16,18},{18... | collective-permute-start | bytes 12296 | tf_op jit(solution)/shard_map/ppermute | solution.py:15
  139.9 6.5 %collective-permute-start.36 = (bf16[8,256]{1,0:T(8,128)(2,1)S(1)}, bf16[8,256]{1,0:T(8,128)(2,1)S(1)}, u32[]{:S(2)}, u32[]{:S(2)}) collective-permute-start(bf16[8,256]{1,0:T(8,128)(2,1)S(1)} %get-tuple-element.65), channel_id=1, source_target_pairs={{0,2},{2,4},{4,6},{6,8},{8,10},{10,12},{12,14},{14,16},{16,18},{18... | collective-permute-start | bytes 12296 | tf_op jit(solution)/shard_map/ppermute | solution.py:15
  146.4 5.8 %collective-permute-start.28 = (bf16[8,256]{1,0:T(8,128)(2,1)S(1)}, bf16[8,256]{1,0:T(8,128)(2,1)S(1)}, u32[]{:S(2)}, u32[]{:S(2)}) collective-permute-start(bf16[8,256]{1,0:T(8,128)(2,1)S(1)} %get-tuple-element.64), channel_id=1, source_target_pairs={{0,2},{2,4},{4,6},{6,8},{8,10},{10,12},{12,14},{14,16},{16,18},{18... | collective-permute-start | bytes 12296 | tf_op jit(solution)/shard_map/ppermute | solution.py:15
  146.9 6.5 %collective-permute-start.37 = (bf16[8,256]{1,0:T(8,128)(2,1)S(1)}, bf16[8,256]{1,0:T(8,128)(2,1)S(1)}, u32[]{:S(2)}, u32[]{:S(2)}) collective-permute-start(bf16[8,256]{1,0:T(8,128)(2,1)S(1)} %get-tuple-element.63), channel_id=1, source_target_pairs={{0,2},{2,4},{4,6},{6,8},{8,10},{10,12},{12,14},{14,16},{16,18},{18... | collective-permute-start | bytes 12296 | tf_op jit(solution)/shard_map/ppermute | solution.py:15
  153.5 5.8 %collective-permute-start.30 = (bf16[8,256]{1,0:T(8,128)(2,1)S(1)}, bf16[8,256]{1,0:T(8,128)(2,1)S(1)}, u32[]{:S(2)}, u32[]{:S(2)}) collective-permute-start(bf16[8,256]{1,0:T(8,128)(2,1)S(1)} %get-tuple-element.62), channel_id=1, source_target_pairs={{0,2},{2,4},{4,6},{6,8},{8,10},{10,12},{12,14},{14,16},{16,18},{18... | collective-permute-start | bytes 12296 | tf_op jit(solution)/shard_map/ppermute | solution.py:15
  154.0 6.5 %collective-permute-start.38 = (bf16[8,256]{1,0:T(8,128)(2,1)S(1)}, bf16[8,256]{1,0:T(8,128)(2,1)S(1)}, u32[]{:S(2)}, u32[]{:S(2)}) collective-permute-start(bf16[8,256]{1,0:T(8,128)(2,1)S(1)} %get-tuple-element.61), channel_id=1, source_target_pairs={{0,2},{2,4},{4,6},{6,8},{8,10},{10,12},{12,14},{14,16},{16,18},{18... | collective-permute-start | bytes 12296 | tf_op jit(solution)/shard_map/ppermute | solution.py:15
  160.6 7.3 %copy-start.7 = (f32[8,256,256]{2,1,0:T(8,128)S(1)}, f32[8,256,256]{2,1,0:T(8,128)}, u32[]{:S(2)}) copy-start(f32[8,256,256]{2,1,0:T(8,128)} %get-tuple-element.80) | copy-start | bytes 6291460
  160.6 7.3 %copy-start.23 = (pred[256,256]{1,0:T(8,128)(4,1)S(1)}, pred[256,256]{1,0:T(8,128)(4,1)}, u32[]{:S(2)}) copy-start(pred[256,256]{1,0:T(8,128)(4,1)} %copy-done.21) | copy-start | bytes 196612
  160.7 7.3 %copy-start.24 = (bf16[256,512]{0,1:T(8,128)(2,1)S(1)}, bf16[256,512]{0,1:T(8,128)(2,1)}, u32[]{:S(2)}) copy-start(bf16[256,512]{0,1:T(8,128)(2,1)} %copy.52) | copy-start | bytes 786436
  160.7 5.8 %collective-permute-start.32 = (bf16[8,256]{1,0:T(8,128)(2,1)S(1)}, bf16[8,256]{1,0:T(8,128)(2,1)S(1)}, u32[]{:S(2)}, u32[]{:S(2)}) collective-permute-start(bf16[8,256]{1,0:T(8,128)(2,1)S(1)} %get-tuple-element.60), channel_id=1, source_target_pairs={{0,2},{2,4},{4,6},{6,8},{8,10},{10,12},{12,14},{14,16},{16,18},{18... | collective-permute-start | bytes 12296 | tf_op jit(solution)/shard_map/ppermute | solution.py:15
  161.2 6.5 %collective-permute-start.39 = (bf16[8,256]{1,0:T(8,128)(2,1)S(1)}, bf16[8,256]{1,0:T(8,128)(2,1)S(1)}, u32[]{:S(2)}, u32[]{:S(2)}) collective-permute-start(bf16[8,256]{1,0:T(8,128)(2,1)S(1)} %get-tuple-element.59), channel_id=1, source_target_pairs={{0,2},{2,4},{4,6},{6,8},{8,10},{10,12},{12,14},{14,16},{16,18},{18... | collective-permute-start | bytes 12296 | tf_op jit(solution)/shard_map/ppermute | solution.py:15
  167.8 47.8 %collective-permute-start.40 = (bf16[8,256]{1,0:T(8,128)(2,1)S(1)}, bf16[8,256]{1,0:T(8,128)(2,1)S(1)}, u32[]{:S(2)}, u32[]{:S(2)}) collective-permute-start(bf16[8,256]{1,0:T(8,128)(2,1)S(1)} %get-tuple-element.57), channel_id=1, source_target_pairs={{0,26},{2,28},{4,30},{6,0},{8,2},{10,4},{12,6},{14,8},{16,10},{18,... | collective-permute-start | bytes 12296 | tf_op jit(solution)/shard_map/ppermute | solution.py:15
  170.7 8.8 %collective-permute-start.23 = (bf16[256,512]{0,1:T(8,128)(2,1)S(1)}, bf16[256,512]{0,1:T(8,128)(2,1)S(1)}, u32[]{:S(2)}, u32[]{:S(2)}) collective-permute-start(bf16[256,512]{0,1:T(8,128)(2,1)S(1)} %fusion.112), channel_id=1, source_target_pairs={{0,2},{2,4},{4,6},{6,8},{8,10},{10,12},{12,14},{14,16},{16,18},{18... | collective-permute-start | bytes 786440 | tf_op jit(solution)/shard_map/ppermute | solution.py:15
  171.0 8.6 %copy-start.17 = (bf16[256,512]{0,1:T(8,128)(2,1)S(1)}, bf16[256,512]{0,1:T(8,128)(2,1)}, u32[]{:S(2)}) copy-start(bf16[256,512]{0,1:T(8,128)(2,1)} %copy.58) | copy-start | bytes 786436
  179.5 8.5 %collective-permute-start.25 = (bf16[256,512]{0,1:T(8,128)(2,1)S(1)}, bf16[256,512]{0,1:T(8,128)(2,1)S(1)}, u32[]{:S(2)}, u32[]{:S(2)}) collective-permute-start(bf16[256,512]{0,1:T(8,128)(2,1)S(1)} %fusion.111), channel_id=1, source_target_pairs={{0,2},{2,4},{4,6},{6,8},{8,10},{10,12},{12,14},{14,16},{16,18},{18... | collective-permute-start | bytes 786440 | tf_op jit(solution)/shard_map/ppermute | solution.py:15
  179.6 8.6 %copy-start.18 = (bf16[256,512]{0,1:T(8,128)(2,1)S(1)}, bf16[256,512]{0,1:T(8,128)(2,1)}, u32[]{:S(2)}) copy-start(bf16[256,512]{0,1:T(8,128)(2,1)} %copy.60) | copy-start | bytes 786436
  188.1 8.6 %collective-permute-start.27 = (bf16[256,512]{0,1:T(8,128)(2,1)S(1)}, bf16[256,512]{0,1:T(8,128)(2,1)S(1)}, u32[]{:S(2)}, u32[]{:S(2)}) collective-permute-start(bf16[256,512]{0,1:T(8,128)(2,1)S(1)} %fusion.110), channel_id=1, source_target_pairs={{0,2},{2,4},{4,6},{6,8},{8,10},{10,12},{12,14},{14,16},{16,18},{18... | collective-permute-start | bytes 786440 | tf_op jit(solution)/shard_map/ppermute | solution.py:15
  188.2 8.7 %copy-start.19 = (bf16[256,512]{0,1:T(8,128)(2,1)S(1)}, bf16[256,512]{0,1:T(8,128)(2,1)}, u32[]{:S(2)}) copy-start(bf16[256,512]{0,1:T(8,128)(2,1)} %copy.62) | copy-start | bytes 786436
  196.8 8.5 %collective-permute-start.29 = (bf16[256,512]{0,1:T(8,128)(2,1)S(1)}, bf16[256,512]{0,1:T(8,128)(2,1)S(1)}, u32[]{:S(2)}, u32[]{:S(2)}) collective-permute-start(bf16[256,512]{0,1:T(8,128)(2,1)S(1)} %fusion.109), channel_id=1, source_target_pairs={{0,2},{2,4},{4,6},{6,8},{8,10},{10,12},{12,14},{14,16},{16,18},{18... | collective-permute-start | bytes 786440 | tf_op jit(solution)/shard_map/ppermute | solution.py:15
  205.4 8.7 %copy-start.25 = (bf16[256,512]{0,1:T(8,128)(2,1)S(1)}, bf16[256,512]{0,1:T(8,128)(2,1)}, u32[]{:S(2)}) copy-start(bf16[256,512]{0,1:T(8,128)(2,1)} %copy.64) | copy-start | bytes 786436
  205.4 8.5 %collective-permute-start.31 = (bf16[256,512]{0,1:T(8,128)(2,1)S(1)}, bf16[256,512]{0,1:T(8,128)(2,1)S(1)}, u32[]{:S(2)}, u32[]{:S(2)}) collective-permute-start(bf16[256,512]{0,1:T(8,128)(2,1)S(1)} %fusion.108), channel_id=1, source_target_pairs={{0,2},{2,4},{4,6},{6,8},{8,10},{10,12},{12,14},{14,16},{16,18},{18... | collective-permute-start | bytes 786440 | tf_op jit(solution)/shard_map/ppermute | solution.py:15
  214.1 5.8 %collective-permute-start.33 = (bf16[256,512]{0,1:T(8,128)(2,1)S(1)}, bf16[256,512]{0,1:T(8,128)(2,1)S(1)}, u32[]{:S(2)}, u32[]{:S(2)}) collective-permute-start(bf16[256,512]{0,1:T(8,128)(2,1)S(1)} %fusion.107), channel_id=1, source_target_pairs={{0,26},{2,28},{4,30},{6,0},{8,2},{10,4},{12,6},{14,8},{16,10},{18,... | collective-permute-start | bytes 786440 | tf_op jit(solution)/shard_map/ppermute | solution.py:15
  (35 other events, 188.4 us)
where the time goes:
time: 222 us; the launch traced here: 221 us
  waiting for transfers between devices  112 us (50%)
  matrix products  33.2 us (15%)
  local copies, waits for them, and re-layouts  27.1 us (12%)
  other arithmetic  19.3 us (9%)
  blocking collectives  17.3 us (8%)
  starting transfers between devices  10.5 us (5%)
    ppermute x41, waiting for transfers between devices, shifted(): lax.ppermute(x, axis, [(i, (i + by) % length) for i in range(length)])  112 us
    ppermute x14, local copies, waits for them, and re-layouts, shifted(): lax.ppermute(x, axis, [(i, (i + by) % length) for i in range(length)])  24.4 us
    dot_general x7, matrix products, tile_scores(): jnp.einsum('the,uhe->htu', queries, key_block, preferred_element_type=jnp...  22.8 us
    reduce_sum x7, other arithmetic, video_update(): totals = totals * factor + jnp.sum(weights, axis=1)  12.1 us
    ppermute x41, starting transfers between devices, shifted(): lax.ppermute(x, axis, [(i, (i + by) % length) for i in range(length)])  10.5 us
    all_gather x1, blocking collectives, local(): lax.all_gather(audio_frames, 'head', axis=1, tiled=True)  8.8 us
    all_gather x1, blocking collectives, local(): lax.all_gather(video_frames, 'head', axis=1, tiled=True)  8.51 us
    dot_general x7, matrix products, video_update(): jnp.einsum('htu,the->uhe', weights.astype(jnp.bfloat16), values.reshape(v...  5.68 us
  transfers between devices with their start and end apart: 41, of which 25 were waited for; matrix products, arithmetic and copies ran while one was open for 35% of the time, Pallas kernels for 0%

commit v1 on v0

v1 whole, which is shorter than its diff:
```python
import functools

import jax
import jax.numpy as jnp
from jax import lax
from jax.experimental import pallas as pl
from jax.experimental.pallas import tpu as pltpu
from jax.sharding import PartitionSpec as P

HEAD = 64
RADIUS = 3
GROUP = 4
NEG = -1e30
ID_ROWS = 16

VMEM = pl.BlockSpec(memory_space=pltpu.VMEM)


def place():
    return lax.rem(lax.axis_index("tm"), GROUP)


def call(kernel, outs, scratch=(), flops=0, moved=0, exps=0, name=None):
    return pl.pallas_call(
        kernel,
        out_shape=outs,
        scratch_shapes=scratch,
        compiler_params=pltpu.CompilerParams(vmem_limit_bytes=48 * 2**20),
        cost_estimate=pl.CostEstimate(flops=flops, bytes_accessed=moved, transcendentals=exps),
        name=name,
    )


def split_kernel(audio, video, ids, *packs):
    rows, width = audio.shape[0], packs[0].shape[1]
    mine = place()
    id_rows = (ids[...] + 1).astype(jnp.float32).astype(jnp.bfloat16)
    for k in range(GROUP):
        columns = pl.ds(pl.multiple_of((mine ^ k) * width, width), width)
        packs[k][:rows] = audio[:, columns]
        packs[k][rows : 2 * rows] = video[:, columns]
        packs[k][2 * rows :] = id_rows


def project_kernel(scale, own, other, weight, *refs):
    *pieces, full = refs
    half, width = own.shape[1], pieces[0].shape[1]
    side = lax.axis_index("head")
    mine = place()
    first = weight[pl.ds(pl.multiple_of(side * half, half), half), :]
    second = weight[pl.ds(pl.multiple_of((1 - side) * half, half), half), :]
    total = jnp.dot(own[...], first, preferred_element_type=jnp.float32)
    total += jnp.dot(other[...], second, preferred_element_type=jnp.float32)
    rounded = total.astype(jnp.bfloat16)
    full[...] = rounded * jnp.bfloat16(scale) if scale != 1.0 else rounded
    for k in range(GROUP):
        columns = pl.ds(pl.multiple_of((mine ^ k) * width, width), width)
        pieces[k][...] = full[:, columns]


def halo_kernel(*refs):
    pieces, (up, down) = refs[:GROUP], refs[GROUP:]
    rows = pieces[0].shape[0]
    mine = place()
    for k in range(GROUP):
        block = mine ^ k

        @pl.when(block >= GROUP - RADIUS)
        def _():
            up[pl.ds(pl.multiple_of((block - (GROUP - RADIUS)) * rows, 16), rows)] = pieces[k][...]

        @pl.when(block < RADIUS)
        def _():
            down[pl.ds(pl.multiple_of(block * rows, 16), rows)] = pieces[k][...]


def join_kernel(*refs):
    pieces, out = refs[:GROUP], refs[GROUP]
    width = pieces[0].shape[1]
    mine = place()
    for k in range(GROUP):
        out[:, pl.ds(pl.multiple_of((mine ^ k) * width, width), width)] = pieces[k][...]


def attend_kernel(side, *refs):
    refs = list(refs)
    take = lambda count: [refs.pop(0) for _ in range(count)]
    asking = take(GROUP)
    keys, (keys_below, keys_above) = take(GROUP), take(2)
    packs, (packs_below, packs_above) = take(GROUP), take(2)
    outs = take(GROUP)
    ask_all, key_all, value_all, id_lanes, id_column, out_all = refs
    rows, width = asking[0].shape
    window = (2 * RADIUS + 1) * rows
    mine = place()
    pack_rows = packs[0].shape[0]

    def put_pack(pack, at, block):
        value_all[pl.ds(pl.multiple_of(block * rows, rows), rows)] = pack[
            at + side * rows : at + (side + 1) * rows
        ]
        lanes = pack[at + 2 * rows : at + 2 * rows + ID_ROWS].astype(jnp.float32)
        for half in range(rows // width):
            id_lanes[:, pl.ds(pl.multiple_of(block * rows + half * width, width), width)] = (
                jnp.broadcast_to(lanes[half : half + 1], (8, width))
            )
        return lanes

    for k in range(GROUP):
        block = mine ^ k
        at = pl.ds(pl.multiple_of(block * rows, rows), rows)
        ask_all[at] = asking[k][...]
        key_all[pl.ds(pl.multiple_of((block + RADIUS) * rows, rows), rows)] = keys[k][...]
        lanes = put_pack(packs[k], 0, block + RADIUS)
        for half in range(rows // width):
            column = jnp.transpose(jnp.broadcast_to(lanes[half : half + 1], (width, width)))
            id_column[pl.ds(pl.multiple_of(block * rows + half * width, width), width)] = column
    key_all[: RADIUS * rows] = keys_below[...]
    key_all[(RADIUS + GROUP) * rows :] = keys_above[...]
    for i in range(RADIUS):
        put_pack(packs_below, i * pack_rows, i)
        put_pack(packs_above, i * pack_rows, RADIUS + GROUP + i)

    lane = lax.broadcasted_iota(jnp.int32, (rows, width), 1)

    def one(block, _):
        start = pl.multiple_of(block * rows, rows)
        at, near = pl.ds(start, rows), pl.ds(start, window)
        allowed = id_column[at, :1] == id_lanes[:1, near]
        ask, key, value = ask_all[at], key_all[near], value_all[near]
        results = []
        for h in range(width // HEAD):
            mine_lanes = lane // HEAD == h
            only = jnp.where(mine_lanes, ask, jnp.zeros_like(ask))
            scores = lax.dot_general(
                only, key, (((1,), (1,)), ((), ())), preferred_element_type=jnp.float32
            )
            scores = jnp.where(allowed, scores, NEG)
            weights = jnp.exp(scores - jnp.max(scores, axis=1, keepdims=True))
            total = jnp.sum(weights, axis=1, keepdims=True)
            mixed = jnp.dot(weights.astype(jnp.bfloat16), value, preferred_element_type=jnp.float32)
            results.append(mixed / total)
        out = results[0]
        for h in range(1, width // HEAD):
            out = jnp.where(lane // HEAD == h, results[h], out)
        out_all[at] = out.astype(out_all.dtype)
        return _

    lax.fori_loop(0, GROUP, one, 0)
    for k in range(GROUP):
        outs[k][...] = out_all[pl.ds(pl.multiple_of((mine ^ k) * rows, rows), rows)]


def local(audio_frames, video_frames, recording, audio_query, video_key):
    rows, half = audio_frames.shape
    width = half // GROUP
    length = lax.axis_size("tm")
    bf16 = jnp.bfloat16
    pack_rows = 2 * rows + ID_ROWS
    shape = jax.ShapeDtypeStruct

    def swapped(x):
        return lax.ppermute(x, "head", [(0, 1), (1, 0)])

    def traded(pieces):
        pairs = lambda k: [(i, i ^ k) for i in range(length)]
        return [pieces[0]] + [lax.ppermute(pieces[k], "tm", pairs(k)) for k in range(1, GROUP)]

    def halo(pieces):
        size = pieces[0].shape[0]
        edge = shape((RADIUS * size, width), bf16)
        up, down = call(
            halo_kernel, [edge, edge], moved=10 * size * width * 2, name="halo"
        )(*pieces)
        below = lax.ppermute(up, "tm", [(i, i + GROUP) for i in range(length - GROUP)])
        above = lax.ppermute(down, "tm", [(i + GROUP, i) for i in range(length - GROUP)])
        return below, above

    def project(own, other, weight, scale):
        return call(
            functools.partial(project_kernel, scale),
            [shape((rows, width), bf16)] * GROUP,
            [pltpu.VMEM((rows, half), bf16)],
            flops=4 * rows * half * half,
            moved=weight.size * 2 + 3 * rows * half * 2,
            name="project",
        )(own, other, weight)

    def attend(side, asking, keys, key_halo, packs, pack_halo):
        window = (2 * RADIUS + 1) * rows
        reach = (2 * RADIUS + GROUP) * rows
        return call(
            functools.partial(attend_kernel, side),
            [shape((rows, width), bf16)] * GROUP,
            [
                pltpu.VMEM((GROUP * rows, width), bf16),
                pltpu.VMEM((reach, width), bf16),
                pltpu.VMEM((reach, width), bf16),
                pltpu.VMEM((8, reach), jnp.float32),
                pltpu.VMEM((GROUP * rows, width), jnp.float32),
                pltpu.VMEM((GROUP * rows, width), bf16),
            ],
            flops=8 * GROUP * rows * window * width * 4,
            moved=4 * reach * width * 2,
            exps=2 * GROUP * rows * window,
            name="attend",
        )(*asking, *keys, *key_halo, *packs, *pack_halo)

    def join(pieces):
        return call(
            join_kernel, shape((rows, half), bf16), moved=2 * rows * half * 2, name="join"
        )(*traded(pieces))

    other_audio = swapped(audio_frames)
    other_video = swapped(video_frames)
    id_rows = jnp.pad(recording.reshape(rows // width, width), ((0, ID_ROWS - rows // width), (0, 0)))
    packs = call(
        split_kernel,
        [shape((pack_rows, width), bf16)] * GROUP,
        moved=4 * rows * half * 2,
        name="split",
    )(audio_frames, video_frames, id_rows)
    packs = traded(packs)
    pack_halo = halo(packs)
    queries = traded(project(audio_frames, other_audio, audio_query, HEAD**-0.5))
    query_halo = halo(queries)
    key_rows = traded(project(video_frames, other_video, video_key, 1.0))
    key_halo = halo(key_rows)
    video_pieces = attend(0, key_rows, queries, query_halo, packs, pack_halo)
    audio_pieces = attend(1, queries, key_rows, key_halo, packs, pack_halo)
    video_attended = join(video_pieces)
    audio_attended = join(audio_pieces)
    return (audio_attended, video_attended)


def solution(mesh):
    return jax.shard_map(
        local,
        mesh=mesh,
        in_specs=(P("tm", "head"), P("tm", "head"), P("tm"), P(None, "head"), P(None, "head")),
        out_specs=(P("tm", "head"), P("tm", "head")),
        check_vma=False,
    )
```

time: 222 us -> 72.6 us (0.33)
  the two profiles are of different devices: /device:TPU:0 before, /device:TPU:9 now
where the time goes in v1:
time: 72.6 us; the launch traced here: 72.2 us
  starting transfers between devices  31.5 us (43%)
  Pallas kernels  20.9 us (29%)
  waiting for transfers between devices  16.4 us (23%)
  local copies, waits for them, and re-layouts  2.59 us (4%)
  between operations  0.84 us (1%)
    ppermute x15, waiting for transfers between devices, traded(): lax.ppermute(pieces[k], 'tm', pairs(k))  16.4 us
    pallas_call x2, Pallas kernels, attend(): call(functools.partial(attend_kernel, side), [shape((rows, width), bf16)]...  16.2 us
    ppermute x15, starting transfers between devices, traded(): lax.ppermute(pieces[k], 'tm', pairs(k))  13.9 us
    ppermute x3, starting transfers between devices, halo(): lax.ppermute(up, 'tm', [(i, i + GROUP) for i in range(length - GROUP)])  9.7 us
    ppermute x3, starting transfers between devices, halo(): lax.ppermute(down, 'tm', [(i + GROUP, i) for i in range(length - GROUP)])  6.32 us
    pallas_call x2, Pallas kernels, project(): call(functools.partial(project_kernel, scale), [shape((rows, width), bf16...  1.97 us
    unnamed x8, local copies, waits for them, and re-layouts  1.9 us
    ppermute x2, starting transfers between devices, swapped(): return lax.ppermute(x, 'head', [(0, 1), (1, 0)])  1.53 us
  transfers between devices with their start and end apart: 23, of which 8 were waited for; matrix products, arithmetic and copies ran while one was open for 1% of the time, Pallas kernels for 28%

profile of v1, /device:TPU:9, one launch (start us, length us, event | category | flops | bytes accessed | tf_op | source)
XLA Modules:
  0.0 72.2 jit_solution(12092562991849993460)
XLA Ops:
  0.6 0.0 copy-start
  0.6 1.3 %collective-permute-start = (bf16[256,512]{1,0:T(8,128)(2,1)}, bf16[256,512]{1,0:T(8,128)(2,1)S(1)}, u32[]{:S(2)}, u32[]{:S(2)}) collective-permute-start(bf16[256,512]{1,0:T(8,128)(2,1)} %audio.1), channel_id=1, source_target_pairs={{0,1},{1,0},{2,3},{3,2},{4,5},{5,4},{6,7},{7,6},{8,9},{9,8},{10,11... | collective-permute-start | bytes 786440 | tf_op jit(solution)/shard_map/ppermute | solution.py:163
  1.9 0.7 pad.4.ids
  2.6 0.0 copy-start.2
  2.6 0.9 %copy-done.2 = bf16[256,512]{1,0:T(8,128)(2,1)S(1)} copy-done((bf16[256,512]{1,0:T(8,128)(2,1)S(1)}, bf16[256,512]{1,0:T(8,128)(2,1)}, u32[]{:S(2)}) %copy-start.2) | copy-done | bytes 262168
  3.6 1.0 %split.1 = (bf16[528,128]{1,0:T(8,128)(2,1)S(1)}, bf16[528,128]{1,0:T(8,128)(2,1)S(1)}, bf16[528,128]{1,0:T(8,128)(2,1)S(1)}, bf16[528,128]{1,0:T(8,128)(2,1)S(1)}) custom-call(bf16[256,512]{1,0:T(8,128)(2,1)S(1)} %copy-done.2, bf16[256,512]{1,0:T(8,128)(2,1)} %video.1, s32[16,128]{1,0:T(8,128)S(1)} %pad.4.ids), custom_call_target="tpu_custom_call" | custom-call | bytes 1048576 | tf_op jit(solution)/shard_map/split/pallas_call | solution.py:217
  4.6 1.0 %collective-permute-start.10 = (bf16[528,128]{1,0:T(8,128)(2,1)S(1)}, bf16[528,128]{1,0:T(8,128)(2,1)S(1)}, u32[]{:S(2)}, u32[]{:S(2)}) collective-permute-start(bf16[528,128]{1,0:T(8,128)(2,1)S(1)} %get-tuple-element.39), channel_id=1, source_target_pairs={{0,2},{2,0},{4,6},{6,4},{8,10},{10,8},{12,14},{14,12},{16,18},{18,... | collective-permute-start | bytes 405512 | tf_op jit(solution)/shard_map/ppermute | solution.py:167
  5.6 1.2 %collective-permute-start.11 = (bf16[528,128]{1,0:T(8,128)(2,1)S(1)}, bf16[528,128]{1,0:T(8,128)(2,1)S(1)}, u32[]{:S(2)}, u32[]{:S(2)}) collective-permute-start(bf16[528,128]{1,0:T(8,128)(2,1)S(1)} %get-tuple-element.40), channel_id=1, source_target_pairs={{0,4},{2,6},{4,0},{6,2},{8,12},{10,14},{12,8},{14,10},{16,20},{18,... | collective-permute-start | bytes 405512 | tf_op jit(solution)/shard_map/ppermute | solution.py:167
  6.9 0.5 collective-permute-start.12
  7.4 0.2 collective-permute-start.4
  7.6 0.0 collective-permute-done.10.refs_1_.refs_11_
  7.6 3.2 %collective-permute-done.11.refs_2_.refs_12_ = bf16[528,128]{1,0:T(8,128)(2,1)S(1)} collective-permute-done((bf16[528,128]{1,0:T(8,128)(2,1)S(1)}, bf16[528,128]{1,0:T(8,128)(2,1)S(1)}, u32[]{:S(2)}, u32[]{:S(2)}) %collective-permute-start.11) | collective-permute-done | bytes 135200 | tf_op jit(solution)/shard_map/ppermute | solution.py:167
  10.8 3.4 %collective-permute-done.12.refs_3_.refs_13_ = bf16[528,128]{1,0:T(8,128)(2,1)S(1)} collective-permute-done((bf16[528,128]{1,0:T(8,128)(2,1)S(1)}, bf16[528,128]{1,0:T(8,128)(2,1)S(1)}, u32[]{:S(2)}, u32[]{:S(2)}) %collective-permute-start.12) | collective-permute-done | bytes 135200 | tf_op jit(solution)/shard_map/ppermute | solution.py:167
  14.2 0.1 halo.4
  14.3 3.3 %collective-permute-start.13 = (bf16[1584,128]{1,0:T(8,128)(2,1)S(1)}, bf16[1584,128]{1,0:T(8,128)(2,1)S(1)}, u32[]{:S(2)}, u32[]{:S(2)}) collective-permute-start(bf16[1584,128]{1,0:T(8,128)(2,1)S(1)} %get-tuple-element.42), channel_id=1, source_target_pairs={{0,8},{2,10},{4,12},{6,14},{8,16},{10,18},{12,20},{14,22},{16,24},... | collective-permute-start | bytes 1216520 | tf_op jit(solution)/shard_map/ppermute | solution.py:175
  17.6 2.1 %collective-permute-start.14 = (bf16[1584,128]{1,0:T(8,128)(2,1)S(1)}, bf16[1584,128]{1,0:T(8,128)(2,1)S(1)}, u32[]{:S(2)}, u32[]{:S(2)}) collective-permute-start(bf16[1584,128]{1,0:T(8,128)(2,1)S(1)} %get-tuple-element.43), channel_id=1, source_target_pairs={{8,0},{10,2},{12,4},{14,6},{16,8},{18,10},{20,12},{22,14},{24,16},... | collective-permute-start | bytes 1216520 | tf_op jit(solution)/shard_map/ppermute | solution.py:176
  19.7 0.0 collective-permute-done.other
  19.7 0.0 copy-done
  19.7 0.0 copy-start.3
  19.7 0.9 %copy-done.3 = bf16[256,512]{1,0:T(8,128)(2,1)S(1)} copy-done((bf16[256,512]{1,0:T(8,128)(2,1)S(1)}, bf16[256,512]{1,0:T(8,128)(2,1)}, u32[]{:S(2)}) %copy-start.3) | copy-done | bytes 262168
  20.7 0.5 project.2
  21.2 0.6 collective-permute-start.1
  21.8 1.2 %collective-permute-start.2 = (bf16[256,128]{1,0:T(8,128)(2,1)S(1)}, bf16[256,128]{1,0:T(8,128)(2,1)S(1)}, u32[]{:S(2)}, u32[]{:S(2)}) collective-permute-start(bf16[256,128]{1,0:T(8,128)(2,1)S(1)} %get-tuple-element.30), channel_id=1, source_target_pairs={{0,4},{2,6},{4,0},{6,2},{8,12},{10,14},{12,8},{14,10},{16,20},{18,... | collective-permute-start | bytes 196616 | tf_op jit(solution)/shard_map/ppermute | solution.py:167
  23.0 0.0 collective-permute-done.4.other
  23.0 0.5 collective-permute-start.3
  23.5 0.0 copy-done.1
  23.5 1.5 %project.3 = (bf16[256,128]{1,0:T(8,128)(2,1)S(1)}, bf16[256,128]{1,0:T(8,128)(2,1)S(1)}, bf16[256,128]{1,0:T(8,128)(2,1)S(1)}, bf16[256,128]{1,0:T(8,128)(2,1)S(1)}) custom-call(bf16[256,512]{1,0:T(8,128)(2,1)} %video.1, bf16[256,512]{1,0:T(8,128)(2,1)S(1)} %collective-permute-done.4.other, bf16[1024,512]{1,0:T(8,128)(2,1)S(1)} %copy-done.1), custom_call_target="tpu_custom_call" | custom-call | flops 268435456 | bytes 1835008 | tf_op jit(solution)/shard_map/project/pallas_call | solution.py:180
  24.9 0.0 collective-permute-done.1.refs_1_.refs_5_
  25.0 0.2 collective-permute-start.5
  25.2 0.2 collective-permute-done.2.refs_2_.refs_6_
  25.4 1.9 %collective-permute-done.3.refs_3_.refs_7_ = bf16[256,128]{1,0:T(8,128)(2,1)S(1)} collective-permute-done((bf16[256,128]{1,0:T(8,128)(2,1)S(1)}, bf16[256,128]{1,0:T(8,128)(2,1)S(1)}, u32[]{:S(2)}, u32[]{:S(2)}) %collective-permute-start.3) | collective-permute-done | bytes 65568 | tf_op jit(solution)/shard_map/ppermute | solution.py:167
  27.3 0.1 halo.5
  27.4 3.2 %collective-permute-start.18 = (bf16[768,128]{1,0:T(8,128)(2,1)S(1)}, bf16[768,128]{1,0:T(8,128)(2,1)S(1)}, u32[]{:S(2)}, u32[]{:S(2)}) collective-permute-start(bf16[768,128]{1,0:T(8,128)(2,1)S(1)} %get-tuple-element.48), channel_id=1, source_target_pairs={{0,8},{2,10},{4,12},{6,14},{8,16},{10,18},{12,20},{14,22},{16,24},... | collective-permute-start | bytes 589832 | tf_op jit(solution)/shard_map/ppermute | solution.py:175
  30.6 2.1 %collective-permute-start.19 = (bf16[768,128]{1,0:T(8,128)(2,1)S(1)}, bf16[768,128]{1,0:T(8,128)(2,1)S(1)}, u32[]{:S(2)}, u32[]{:S(2)}) collective-permute-start(bf16[768,128]{1,0:T(8,128)(2,1)S(1)} %get-tuple-element.49), channel_id=1, source_target_pairs={{8,0},{10,2},{12,4},{14,6},{16,8},{18,10},{20,12},{22,14},{24,16},... | collective-permute-start | bytes 589832 | tf_op jit(solution)/shard_map/ppermute | solution.py:176
  32.7 0.0 collective-permute-done.5.refs_1_.refs_5_
  32.7 1.2 %collective-permute-start.6 = (bf16[256,128]{1,0:T(8,128)(2,1)S(1)}, bf16[256,128]{1,0:T(8,128)(2,1)S(1)}, u32[]{:S(2)}, u32[]{:S(2)}) collective-permute-start(bf16[256,128]{1,0:T(8,128)(2,1)S(1)} %get-tuple-element.34), channel_id=1, source_target_pairs={{0,4},{2,6},{4,0},{6,2},{8,12},{10,14},{12,8},{14,10},{16,20},{18,... | collective-permute-start | bytes 196616 | tf_op jit(solution)/shard_map/ppermute | solution.py:167
  34.0 2.2 %collective-permute-done.6.refs_2_.refs_6_ = bf16[256,128]{1,0:T(8,128)(2,1)S(1)} collective-permute-done((bf16[256,128]{1,0:T(8,128)(2,1)S(1)}, bf16[256,128]{1,0:T(8,128)(2,1)S(1)}, u32[]{:S(2)}, u32[]{:S(2)}) %collective-permute-start.6) | collective-permute-done | bytes 65568 | tf_op jit(solution)/shard_map/ppermute | solution.py:167
  36.2 2.4 %collective-permute-start.7 = (bf16[256,128]{1,0:T(8,128)(2,1)S(1)}, bf16[256,128]{1,0:T(8,128)(2,1)S(1)}, u32[]{:S(2)}, u32[]{:S(2)}) collective-permute-start(bf16[256,128]{1,0:T(8,128)(2,1)S(1)} %get-tuple-element.35), channel_id=1, source_target_pairs={{0,6},{2,4},{4,2},{6,0},{8,14},{10,12},{12,10},{14,8},{16,22},{18,... | collective-permute-start | bytes 196616 | tf_op jit(solution)/shard_map/ppermute | solution.py:167
  38.6 2.8 %collective-permute-done.7.refs_3_.refs_7_ = bf16[256,128]{1,0:T(8,128)(2,1)S(1)} collective-permute-done((bf16[256,128]{1,0:T(8,128)(2,1)S(1)}, bf16[256,128]{1,0:T(8,128)(2,1)S(1)}, u32[]{:S(2)}, u32[]{:S(2)}) %collective-permute-start.7) | collective-permute-done | bytes 65568 | tf_op jit(solution)/shard_map/ppermute | solution.py:167
  41.5 0.1 halo.3
  41.5 3.2 %collective-permute-start.8 = (bf16[768,128]{1,0:T(8,128)(2,1)S(1)}, bf16[768,128]{1,0:T(8,128)(2,1)S(1)}, u32[]{:S(2)}, u32[]{:S(2)}) collective-permute-start(bf16[768,128]{1,0:T(8,128)(2,1)S(1)} %get-tuple-element.36), channel_id=1, source_target_pairs={{0,8},{2,10},{4,12},{6,14},{8,16},{10,18},{12,20},{14,22},{16,24},... | collective-permute-start | bytes 589832 | tf_op jit(solution)/shard_map/ppermute | solution.py:175
  44.7 0.0 collective-permute-done.18.refs_8_
  44.7 2.1 %collective-permute-start.9 = (bf16[768,128]{1,0:T(8,128)(2,1)S(1)}, bf16[768,128]{1,0:T(8,128)(2,1)S(1)}, u32[]{:S(2)}, u32[]{:S(2)}) collective-permute-start(bf16[768,128]{1,0:T(8,128)(2,1)S(1)} %get-tuple-element.37), channel_id=1, source_target_pairs={{8,0},{10,2},{12,4},{14,6},{16,8},{18,10},{20,12},{22,14},{24,16},... | collective-permute-start | bytes 589832 | tf_op jit(solution)/shard_map/ppermute | solution.py:176
  46.8 0.0 collective-permute-done.19.refs_9_
  46.8 0.0 collective-permute-done.13.refs_14_
  46.9 0.0 collective-permute-done.14.refs_15_
  46.9 8.1 %attend.3 = (bf16[256,128]{1,0:T(8,128)(2,1)S(1)}, bf16[256,128]{1,0:T(8,128)(2,1)S(1)}, bf16[256,128]{1,0:T(8,128)(2,1)S(1)}, bf16[256,128]{1,0:T(8,128)(2,1)S(1)}) custom-call(bf16[256,128]{1,0:T(8,128)(2,1)S(1)} %get-tuple-element.32.refs_0_.refs_4_, bf16[256,128]{1,0:T(8,128)(2,1)S(1)} %collective-permute-done.5.refs_1_.refs_5_, ...), custom_call_target="tpu_custom_call" | custom-call | flops 7516192768 | bytes 2621440 | tf_op jit(solution)/shard_map/attend/pallas_call | solution.py:192
  55.0 1.1 %collective-permute-start.20 = (bf16[256,128]{1,0:T(8,128)(2,1)S(1)}, bf16[256,128]{1,0:T(8,128)(2,1)S(1)}, u32[]{:S(2)}, u32[]{:S(2)}) collective-permute-start(bf16[256,128]{1,0:T(8,128)(2,1)S(1)} %get-tuple-element.51), channel_id=1, source_target_pairs={{0,2},{2,0},{4,6},{6,4},{8,10},{10,8},{12,14},{14,12},{16,18},{18,... | collective-permute-start | bytes 196616 | tf_op jit(solution)/shard_map/ppermute | solution.py:167
  56.1 0.5 collective-permute-start.21
  56.6 1.2 %collective-permute-start.22 = (bf16[256,128]{1,0:T(8,128)(2,1)S(1)}, bf16[256,128]{1,0:T(8,128)(2,1)S(1)}, u32[]{:S(2)}, u32[]{:S(2)}) collective-permute-start(bf16[256,128]{1,0:T(8,128)(2,1)S(1)} %get-tuple-element.53), channel_id=1, source_target_pairs={{0,6},{2,4},{4,2},{6,0},{8,14},{10,12},{12,10},{14,8},{16,22},{18,... | collective-permute-start | bytes 196616 | tf_op jit(solution)/shard_map/ppermute | solution.py:167
  57.8 0.0 collective-permute-done.8.refs_8_
  57.8 0.0 collective-permute-done.9.refs_9_
  57.8 8.1 %attend.2 = (bf16[256,128]{1,0:T(8,128)(2,1)S(1)}, bf16[256,128]{1,0:T(8,128)(2,1)S(1)}, bf16[256,128]{1,0:T(8,128)(2,1)S(1)}, bf16[256,128]{1,0:T(8,128)(2,1)S(1)}) custom-call(bf16[256,128]{1,0:T(8,128)(2,1)S(1)} %get-tuple-element.28.refs_0_.refs_4_, bf16[256,128]{1,0:T(8,128)(2,1)S(1)} %collective-permute-done.1.refs_1_.refs_5_, ...), custom_call_target="tpu_custom_call" | custom-call | flops 7516192768 | bytes 2621440 | tf_op jit(solution)/shard_map/attend/pallas_call | solution.py:192
  65.9 0.2 collective-permute-start.15
  66.2 0.5 collective-permute-start.16
  66.7 0.0 collective-permute-done.20.refs_1_
  66.7 1.5 %collective-permute-start.17 = (bf16[256,128]{1,0:T(8,128)(2,1)S(1)}, bf16[256,128]{1,0:T(8,128)(2,1)S(1)}, u32[]{:S(2)}, u32[]{:S(2)}) collective-permute-start(bf16[256,128]{1,0:T(8,128)(2,1)S(1)} %get-tuple-element.47), channel_id=1, source_target_pairs={{0,6},{2,4},{4,2},{6,0},{8,14},{10,12},{12,10},{14,8},{16,22},{18,... | collective-permute-start | bytes 196616 | tf_op jit(solution)/shard_map/ppermute | solution.py:167
  68.1 0.0 collective-permute-done.21.refs_2_
  68.1 0.0 collective-permute-done.22.refs_3_
  68.1 0.8 %join.3 = bf16[256,512]{1,0:T(8,128)(2,1)} custom-call(bf16[256,128]{1,0:T(8,128)(2,1)S(1)} %get-tuple-element.50.refs_0_, bf16[256,128]{1,0:T(8,128)(2,1)S(1)} %collective-permute-done.20.refs_1_, bf16[256,128]{1,0:T(8,128)(2,1)S(1)} %collective-permute-done.21.refs_2_, bf16[256,128]{1,0:T(8,128)(2,1)S(1)} %collective-permute-done.22.refs_3_), custom_call_target="tpu_custom_call" | custom-call | bytes 524288 | tf_op jit(solution)/shard_map/join/pallas_call | solution.py:210
  68.9 0.0 collective-permute-done.15.refs_1_
  68.9 0.4 collective-permute-done.16.refs_2_
  69.3 2.2 %collective-permute-done.17.refs_3_ = bf16[256,128]{1,0:T(8,128)(2,1)S(1)} collective-permute-done((bf16[256,128]{1,0:T(8,128)(2,1)S(1)}, bf16[256,128]{1,0:T(8,128)(2,1)S(1)}, u32[]{:S(2)}, u32[]{:S(2)}) %collective-permute-start.17) | collective-permute-done | bytes 65568 | tf_op jit(solution)/shard_map/ppermute | solution.py:167
  71.5 0.8 %join.2 = bf16[256,512]{1,0:T(8,128)(2,1)} custom-call(bf16[256,128]{1,0:T(8,128)(2,1)S(1)} %get-tuple-element.44.refs_0_, bf16[256,128]{1,0:T(8,128)(2,1)S(1)} %collective-permute-done.15.refs_1_, bf16[256,128]{1,0:T(8,128)(2,1)S(1)} %collective-permute-done.16.refs_2_, bf16[256,128]{1,0:T(8,128)(2,1)S(1)} %collective-permute-done.17.refs_3_), custom_call_target="tpu_custom_call" | custom-call | bytes 524288 | tf_op jit(solution)/shard_map/join/pallas_call | solution.py:210
  (1 shorter events, 0.0 us)
Async XLA Ops:
  0.6 19.1 %copy-start = (bf16[1024,512]{1,0:T(8,128)(2,1)S(1)}, bf16[1024,512]{1,0:T(8,128)(2,1)}, u32[]{:S(2)}) copy-start(bf16[1024,512]{1,0:T(8,128)(2,1)} %weight.2) | copy-start | bytes 3145732
  0.6 19.1 %collective-permute-start = (bf16[256,512]{1,0:T(8,128)(2,1)}, bf16[256,512]{1,0:T(8,128)(2,1)S(1)}, u32[]{:S(2)}, u32[]{:S(2)}) collective-permute-start(bf16[256,512]{1,0:T(8,128)(2,1)} %audio.1), channel_id=1, source_target_pairs={{0,1},{1,0},{2,3},{3,2},{4,5},{5,4},{6,7},{7,6},{8,9},{9,8},{10,11... | collective-permute-start | bytes 786440 | tf_op jit(solution)/shard_map/ppermute | solution.py:163
  2.6 0.9 %copy-start.2 = (bf16[256,512]{1,0:T(8,128)(2,1)S(1)}, bf16[256,512]{1,0:T(8,128)(2,1)}, u32[]{:S(2)}) copy-start(bf16[256,512]{1,0:T(8,128)(2,1)} %audio.1) | copy-start | bytes 786436
  4.6 3.0 %collective-permute-start.10 = (bf16[528,128]{1,0:T(8,128)(2,1)S(1)}, bf16[528,128]{1,0:T(8,128)(2,1)S(1)}, u32[]{:S(2)}, u32[]{:S(2)}) collective-permute-start(bf16[528,128]{1,0:T(8,128)(2,1)S(1)} %get-tuple-element.39), channel_id=1, source_target_pairs={{0,2},{2,0},{4,6},{6,4},{8,10},{10,8},{12,14},{14,12},{16,18},{18,... | collective-permute-start | bytes 405512 | tf_op jit(solution)/shard_map/ppermute | solution.py:167
  5.6 5.2 %collective-permute-start.11 = (bf16[528,128]{1,0:T(8,128)(2,1)S(1)}, bf16[528,128]{1,0:T(8,128)(2,1)S(1)}, u32[]{:S(2)}, u32[]{:S(2)}) collective-permute-start(bf16[528,128]{1,0:T(8,128)(2,1)S(1)} %get-tuple-element.40), channel_id=1, source_target_pairs={{0,4},{2,6},{4,0},{6,2},{8,12},{10,14},{12,8},{14,10},{16,20},{18,... | collective-permute-start | bytes 405512 | tf_op jit(solution)/shard_map/ppermute | solution.py:167
  6.9 7.3 %collective-permute-start.12 = (bf16[528,128]{1,0:T(8,128)(2,1)S(1)}, bf16[528,128]{1,0:T(8,128)(2,1)S(1)}, u32[]{:S(2)}, u32[]{:S(2)}) collective-permute-start(bf16[528,128]{1,0:T(8,128)(2,1)S(1)} %get-tuple-element.41), channel_id=1, source_target_pairs={{0,6},{2,4},{4,2},{6,0},{8,14},{10,12},{12,10},{14,8},{16,22},{18,... | collective-permute-start | bytes 405512 | tf_op jit(solution)/shard_map/ppermute | solution.py:167
  7.4 15.6 %collective-permute-start.4 = (bf16[256,512]{1,0:T(8,128)(2,1)}, bf16[256,512]{1,0:T(8,128)(2,1)S(1)}, u32[]{:S(2)}, u32[]{:S(2)}) collective-permute-start(bf16[256,512]{1,0:T(8,128)(2,1)} %video.1), channel_id=1, source_target_pairs={{0,1},{1,0},{2,3},{3,2},{4,5},{5,4},{6,7},{7,6},{8,9},{9,8},{10,11... | collective-permute-start | bytes 786440 | tf_op jit(solution)/shard_map/ppermute | solution.py:163
  14.2 9.3 %copy-start.1 = (bf16[1024,512]{1,0:T(8,128)(2,1)S(1)}, bf16[1024,512]{1,0:T(8,128)(2,1)}, u32[]{:S(2)}) copy-start(bf16[1024,512]{1,0:T(8,128)(2,1)} %weight.3) | copy-start | bytes 3145732
  14.3 32.6 %collective-permute-start.13 = (bf16[1584,128]{1,0:T(8,128)(2,1)S(1)}, bf16[1584,128]{1,0:T(8,128)(2,1)S(1)}, u32[]{:S(2)}, u32[]{:S(2)}) collective-permute-start(bf16[1584,128]{1,0:T(8,128)(2,1)S(1)} %get-tuple-element.42), channel_id=1, source_target_pairs={{0,8},{2,10},{4,12},{6,14},{8,16},{10,18},{12,20},{14,22},{16,24},... | collective-permute-start | bytes 1216520 | tf_op jit(solution)/shard_map/ppermute | solution.py:175
  17.6 29.2 %collective-permute-start.14 = (bf16[1584,128]{1,0:T(8,128)(2,1)S(1)}, bf16[1584,128]{1,0:T(8,128)(2,1)S(1)}, u32[]{:S(2)}, u32[]{:S(2)}) collective-permute-start(bf16[1584,128]{1,0:T(8,128)(2,1)S(1)} %get-tuple-element.43), channel_id=1, source_target_pairs={{8,0},{10,2},{12,4},{14,6},{16,8},{18,10},{20,12},{22,14},{24,16},... | collective-permute-start | bytes 1216520 | tf_op jit(solution)/shard_map/ppermute | solution.py:176
  19.7 1.0 %copy-start.3 = (bf16[256,512]{1,0:T(8,128)(2,1)S(1)}, bf16[256,512]{1,0:T(8,128)(2,1)}, u32[]{:S(2)}) copy-start(bf16[256,512]{1,0:T(8,128)(2,1)} %audio.1) | copy-start | bytes 786436
  21.2 3.7 %collective-permute-start.1 = (bf16[256,128]{1,0:T(8,128)(2,1)S(1)}, bf16[256,128]{1,0:T(8,128)(2,1)S(1)}, u32[]{:S(2)}, u32[]{:S(2)}) collective-permute-start(bf16[256,128]{1,0:T(8,128)(2,1)S(1)} %get-tuple-element.29), channel_id=1, source_target_pairs={{0,2},{2,0},{4,6},{6,4},{8,10},{10,8},{12,14},{14,12},{16,18},{18,... | collective-permute-start | bytes 196616 | tf_op jit(solution)/shard_map/ppermute | solution.py:167
  21.8 3.7 %collective-permute-start.2 = (bf16[256,128]{1,0:T(8,128)(2,1)S(1)}, bf16[256,128]{1,0:T(8,128)(2,1)S(1)}, u32[]{:S(2)}, u32[]{:S(2)}) collective-permute-start(bf16[256,128]{1,0:T(8,128)(2,1)S(1)} %get-tuple-element.30), channel_id=1, source_target_pairs={{0,4},{2,6},{4,0},{6,2},{8,12},{10,14},{12,8},{14,10},{16,20},{18,... | collective-permute-start | bytes 196616 | tf_op jit(solution)/shard_map/ppermute | solution.py:167
  23.0 4.3 %collective-permute-start.3 = (bf16[256,128]{1,0:T(8,128)(2,1)S(1)}, bf16[256,128]{1,0:T(8,128)(2,1)S(1)}, u32[]{:S(2)}, u32[]{:S(2)}) collective-permute-start(bf16[256,128]{1,0:T(8,128)(2,1)S(1)} %get-tuple-element.31), channel_id=1, source_target_pairs={{0,6},{2,4},{4,2},{6,0},{8,14},{10,12},{12,10},{14,8},{16,22},{18,... | collective-permute-start | bytes 196616 | tf_op jit(solution)/shard_map/ppermute | solution.py:167
  25.0 7.8 %collective-permute-start.5 = (bf16[256,128]{1,0:T(8,128)(2,1)S(1)}, bf16[256,128]{1,0:T(8,128)(2,1)S(1)}, u32[]{:S(2)}, u32[]{:S(2)}) collective-permute-start(bf16[256,128]{1,0:T(8,128)(2,1)S(1)} %get-tuple-element.33), channel_id=1, source_target_pairs={{0,2},{2,0},{4,6},{6,4},{8,10},{10,8},{12,14},{14,12},{16,18},{18,... | collective-permute-start | bytes 196616 | tf_op jit(solution)/shard_map/ppermute | solution.py:167
  27.4 17.3 %collective-permute-start.18 = (bf16[768,128]{1,0:T(8,128)(2,1)S(1)}, bf16[768,128]{1,0:T(8,128)(2,1)S(1)}, u32[]{:S(2)}, u32[]{:S(2)}) collective-permute-start(bf16[768,128]{1,0:T(8,128)(2,1)S(1)} %get-tuple-element.48), channel_id=1, source_target_pairs={{0,8},{2,10},{4,12},{6,14},{8,16},{10,18},{12,20},{14,22},{16,24},... | collective-permute-start | bytes 589832 | tf_op jit(solution)/shard_map/ppermute | solution.py:175
  30.6 16.2 %collective-permute-start.19 = (bf16[768,128]{1,0:T(8,128)(2,1)S(1)}, bf16[768,128]{1,0:T(8,128)(2,1)S(1)}, u32[]{:S(2)}, u32[]{:S(2)}) collective-permute-start(bf16[768,128]{1,0:T(8,128)(2,1)S(1)} %get-tuple-element.49), channel_id=1, source_target_pairs={{8,0},{10,2},{12,4},{14,6},{16,8},{18,10},{20,12},{22,14},{24,16},... | collective-permute-start | bytes 589832 | tf_op jit(solution)/shard_map/ppermute | solution.py:176
  32.7 3.5 %collective-permute-start.6 = (bf16[256,128]{1,0:T(8,128)(2,1)S(1)}, bf16[256,128]{1,0:T(8,128)(2,1)S(1)}, u32[]{:S(2)}, u32[]{:S(2)}) collective-permute-start(bf16[256,128]{1,0:T(8,128)(2,1)S(1)} %get-tuple-element.34), channel_id=1, source_target_pairs={{0,4},{2,6},{4,0},{6,2},{8,12},{10,14},{12,8},{14,10},{16,20},{18,... | collective-permute-start | bytes 196616 | tf_op jit(solution)/shard_map/ppermute | solution.py:167
  36.2 5.3 %collective-permute-start.7 = (bf16[256,128]{1,0:T(8,128)(2,1)S(1)}, bf16[256,128]{1,0:T(8,128)(2,1)S(1)}, u32[]{:S(2)}, u32[]{:S(2)}) collective-permute-start(bf16[256,128]{1,0:T(8,128)(2,1)S(1)} %get-tuple-element.35), channel_id=1, source_target_pairs={{0,6},{2,4},{4,2},{6,0},{8,14},{10,12},{12,10},{14,8},{16,22},{18,... | collective-permute-start | bytes 196616 | tf_op jit(solution)/shard_map/ppermute | solution.py:167
  41.5 16.3 %collective-permute-start.8 = (bf16[768,128]{1,0:T(8,128)(2,1)S(1)}, bf16[768,128]{1,0:T(8,128)(2,1)S(1)}, u32[]{:S(2)}, u32[]{:S(2)}) collective-permute-start(bf16[768,128]{1,0:T(8,128)(2,1)S(1)} %get-tuple-element.36), channel_id=1, source_target_pairs={{0,8},{2,10},{4,12},{6,14},{8,16},{10,18},{12,20},{14,22},{16,24},... | collective-permute-start | bytes 589832 | tf_op jit(solution)/shard_map/ppermute | solution.py:175
  44.7 13.1 %collective-permute-start.9 = (bf16[768,128]{1,0:T(8,128)(2,1)S(1)}, bf16[768,128]{1,0:T(8,128)(2,1)S(1)}, u32[]{:S(2)}, u32[]{:S(2)}) collective-permute-start(bf16[768,128]{1,0:T(8,128)(2,1)S(1)} %get-tuple-element.37), channel_id=1, source_target_pairs={{8,0},{10,2},{12,4},{14,6},{16,8},{18,10},{20,12},{22,14},{24,16},... | collective-permute-start | bytes 589832 | tf_op jit(solution)/shard_map/ppermute | solution.py:176
  55.0 11.7 %collective-permute-start.20 = (bf16[256,128]{1,0:T(8,128)(2,1)S(1)}, bf16[256,128]{1,0:T(8,128)(2,1)S(1)}, u32[]{:S(2)}, u32[]{:S(2)}) collective-permute-start(bf16[256,128]{1,0:T(8,128)(2,1)S(1)} %get-tuple-element.51), channel_id=1, source_target_pairs={{0,2},{2,0},{4,6},{6,4},{8,10},{10,8},{12,14},{14,12},{16,18},{18,... | collective-permute-start | bytes 196616 | tf_op jit(solution)/shard_map/ppermute | solution.py:167
  56.1 12.0 %collective-permute-start.21 = (bf16[256,128]{1,0:T(8,128)(2,1)S(1)}, bf16[256,128]{1,0:T(8,128)(2,1)S(1)}, u32[]{:S(2)}, u32[]{:S(2)}) collective-permute-start(bf16[256,128]{1,0:T(8,128)(2,1)S(1)} %get-tuple-element.52), channel_id=1, source_target_pairs={{0,4},{2,6},{4,0},{6,2},{8,12},{10,14},{12,8},{14,10},{16,20},{18,... | collective-permute-start | bytes 196616 | tf_op jit(solution)/shard_map/ppermute | solution.py:167
  56.6 11.5 %collective-permute-start.22 = (bf16[256,128]{1,0:T(8,128)(2,1)S(1)}, bf16[256,128]{1,0:T(8,128)(2,1)S(1)}, u32[]{:S(2)}, u32[]{:S(2)}) collective-permute-start(bf16[256,128]{1,0:T(8,128)(2,1)S(1)} %get-tuple-element.53), channel_id=1, source_target_pairs={{0,6},{2,4},{4,2},{6,0},{8,14},{10,12},{12,10},{14,8},{16,22},{18,... | collective-permute-start | bytes 196616 | tf_op jit(solution)/shard_map/ppermute | solution.py:167
  65.9 3.0 %collective-permute-start.15 = (bf16[256,128]{1,0:T(8,128)(2,1)S(1)}, bf16[256,128]{1,0:T(8,128)(2,1)S(1)}, u32[]{:S(2)}, u32[]{:S(2)}) collective-permute-start(bf16[256,128]{1,0:T(8,128)(2,1)S(1)} %get-tuple-element.45), channel_id=1, source_target_pairs={{0,2},{2,0},{4,6},{6,4},{8,10},{10,8},{12,14},{14,12},{16,18},{18,... | collective-permute-start | bytes 196616 | tf_op jit(solution)/shard_map/ppermute | solution.py:167
  66.2 3.1 %collective-permute-start.16 = (bf16[256,128]{1,0:T(8,128)(2,1)S(1)}, bf16[256,128]{1,0:T(8,128)(2,1)S(1)}, u32[]{:S(2)}, u32[]{:S(2)}) collective-permute-start(bf16[256,128]{1,0:T(8,128)(2,1)S(1)} %get-tuple-element.46), channel_id=1, source_target_pairs={{0,4},{2,6},{4,0},{6,2},{8,12},{10,14},{12,8},{14,10},{16,20},{18,... | collective-permute-start | bytes 196616 | tf_op jit(solution)/shard_map/ppermute | solution.py:167
  66.7 4.8 %collective-permute-start.17 = (bf16[256,128]{1,0:T(8,128)(2,1)S(1)}, bf16[256,128]{1,0:T(8,128)(2,1)S(1)}, u32[]{:S(2)}, u32[]{:S(2)}) collective-permute-start(bf16[256,128]{1,0:T(8,128)(2,1)S(1)} %get-tuple-element.47), channel_id=1, source_target_pairs={{0,6},{2,4},{4,2},{6,0},{8,14},{10,12},{12,10},{14,8},{16,22},{18,... | collective-permute-start | bytes 196616 | tf_op jit(solution)/shard_map/ppermute | solution.py:167

commit v2 on v1

v2 whole, which is shorter than its diff:
```python
import functools

import jax
import jax.numpy as jnp
from jax import lax
from jax.experimental import pallas as pl
from jax.experimental.pallas import tpu as pltpu
from jax.sharding import PartitionSpec as P

HEAD = 64
RADIUS = 3
GROUP = 4
NEG = -1e30
ID_ROWS = 16

VMEM = pl.BlockSpec(memory_space=pltpu.VMEM)
ANY = pl.BlockSpec(memory_space=pl.ANY)


def place():
    return lax.rem(lax.axis_index("tm"), GROUP)


def plane():
    return lax.axis_index("tm") // GROUP


def call(kernel, outs, scratch=(), ins=None, flops=0, moved=0, exps=0, name=None):
    return pl.pallas_call(
        kernel,
        out_shape=outs,
        **({"in_specs": ins} if ins else {}),
        scratch_shapes=scratch,
        compiler_params=pltpu.CompilerParams(vmem_limit_bytes=48 * 2**20),
        cost_estimate=pl.CostEstimate(flops=flops, bytes_accessed=moved, transcendentals=exps),
        name=name,
    )


def project_kernel(scale, has_ids, *refs):
    own, other, weight = refs[:3]
    packs, (full, id_rows) = refs[-GROUP - 2 : -2], refs[-2:]
    (rows, half), width = own.shape, packs[0].shape[1]
    side = lax.axis_index("head")
    mine = place()
    first = weight[pl.ds(pl.multiple_of(side * half, half), half), :]
    second = weight[pl.ds(pl.multiple_of((1 - side) * half, half), half), :]
    total = jnp.dot(own[...], first, preferred_element_type=jnp.float32)
    total += jnp.dot(other[...], second, preferred_element_type=jnp.float32)
    rounded = total.astype(jnp.bfloat16)
    full[...] = rounded * jnp.bfloat16(scale) if scale != 1.0 else rounded
    if has_ids:
        ids = refs[3]
        id_rows[...] = jnp.zeros_like(id_rows)
        id_rows[: ids.shape[0]] = (ids[...] + 1).astype(jnp.float32)
    for k in range(GROUP):
        columns = pl.ds(pl.multiple_of((mine ^ k) * width, width), width)
        packs[k][:rows] = own[:, columns]
        packs[k][rows : 2 * rows] = full[:, columns]
        if has_ids:
            packs[k][2 * rows :] = id_rows[...].astype(jnp.bfloat16)


def halo_kernel(has_ids, *refs):
    pieces, (first, second) = refs[:GROUP], refs[-2:]
    rows = pieces[0].shape[0]
    mine = place()
    odd = lax.rem(plane(), 2)
    for k in range(GROUP):
        block = mine ^ k
        for out, skip in ((first, (GROUP - RADIUS) * (1 - odd)), (second, (GROUP - RADIUS) * odd)):
            spot = block - skip

            @pl.when((spot >= 0) & (spot < RADIUS))
            def _():
                out[pl.ds(pl.multiple_of(spot * rows, 16), rows)] = pieces[k][...]

    if has_ids:
        last = lax.axis_size("tm") // GROUP - 1

        @pl.when((plane() == 0) | (plane() == last))
        def _():
            for i in range(RADIUS):
                at = (i + 1) * rows - ID_ROWS
                second[at : at + ID_ROWS] = jnp.zeros((ID_ROWS, second.shape[1]), second.dtype)


def join_kernel(*refs):
    pieces, out = refs[:GROUP], refs[GROUP]
    width = pieces[0].shape[1]
    mine = place()
    for k in range(GROUP):
        out[:, pl.ds(pl.multiple_of((mine ^ k) * width, width), width)] = pieces[k][...]


def attend_kernel(shared, skipped, *refs):
    refs = list(refs)
    take = lambda count: [refs.pop(0) for _ in range(count)]
    asking, sources, source_edges = take(GROUP), take(GROUP), take(2)
    id_packs, id_edges = (sources, source_edges) if shared else (take(GROUP), take(2))
    take(skipped)
    outs = take(GROUP)
    ask_all, key_all, value_all, id_lanes, id_column, out_all = refs
    rows, width = outs[0].shape
    window = (2 * RADIUS + 1) * rows
    mine = place()
    source_rows, id_pack_rows = sources[0].shape[0], id_packs[0].shape[0]

    def block_at(block):
        return pl.ds(pl.multiple_of(block * rows, rows), rows)

    def put(source, at, ids, ids_at, block):
        value_all[block_at(block)] = source[at : at + rows]
        key_all[block_at(block)] = source[at + rows : at + 2 * rows]
        ids_at += 2 * rows
        lanes = ids[ids_at : ids_at + ID_ROWS].astype(jnp.float32)
        for part in range(rows // width):
            id_lanes[:, pl.ds(pl.multiple_of(block * rows + part * width, width), width)] = (
                jnp.broadcast_to(lanes[part : part + 1], (8, width))
            )
        return lanes

    for k in range(GROUP):
        block = mine ^ k
        ask_all[block_at(block)] = asking[k][rows : 2 * rows]
        lanes = put(sources[k], 0, id_packs[k], 0, block + RADIUS)
        for part in range(rows // width):
            column = jnp.transpose(jnp.broadcast_to(lanes[part : part + 1], (width, width)))
            id_column[pl.ds(pl.multiple_of(block * rows + part * width, width), width)] = column
    odd = lax.rem(plane(), 2)
    for edge in range(2):
        spot = (RADIUS + GROUP) * (odd if edge else 1 - odd)
        for i in range(RADIUS):
            put(source_edges[edge], i * source_rows, id_edges[edge], i * id_pack_rows, spot + i)

    lane = lax.broadcasted_iota(jnp.int32, (rows, width), 1)

    def one(block, _):
        start = pl.multiple_of(block * rows, rows)
        at, near = pl.ds(start, rows), pl.ds(start, window)
        allowed = id_column[at, :1] == id_lanes[:1, near]
        ask, key, value = ask_all[at], key_all[near], value_all[near]
        results = []
        for h in range(width // HEAD):
            only = jnp.where(lane // HEAD == h, ask, jnp.zeros_like(ask))
            scores = lax.dot_general(
                only, key, (((1,), (1,)), ((), ())), preferred_element_type=jnp.float32
            )
            scores = jnp.where(allowed, scores, NEG)
            weights = jnp.exp(scores - jnp.max(scores, axis=1, keepdims=True))
            total = jnp.sum(weights, axis=1, keepdims=True)
            mixed = jnp.dot(weights.astype(jnp.bfloat16), value, preferred_element_type=jnp.float32)
            results.append(mixed / total)
        out = results[0]
        for h in range(1, width // HEAD):
            out = jnp.where(lane // HEAD == h, results[h], out)
        out_all[at] = out.astype(out_all.dtype)
        return _

    lax.fori_loop(0, GROUP, one, 0)
    for k in range(GROUP):
        outs[k][...] = out_all[block_at(mine ^ k)]


def local(audio_frames, video_frames, recording, audio_query, video_key):
    rows, half = audio_frames.shape
    width = half // GROUP
    length = lax.axis_size("tm")
    bf16 = jnp.bfloat16
    shape = jax.ShapeDtypeStruct

    def swapped(x):
        return lax.ppermute(x, "head", [(0, 1), (1, 0)])

    def traded(pieces):
        pairs = lambda k: [(i, i ^ k) for i in range(length)]
        return [pieces[0]] + [lax.ppermute(pieces[k], "tm", pairs(k)) for k in range(1, GROUP)]

    def halo(pieces, has_ids, after=()):
        size = pieces[0].shape[0]
        edge = shape((RADIUS * size, width), bf16)
        sent = call(
            functools.partial(halo_kernel, has_ids),
            [edge, edge],
            ins=[VMEM] * GROUP + [ANY] * len(after),
            moved=10 * size * width * 2,
            name="halo",
        )(*pieces, *after)

        def partner(i, second):
            spot, inside = divmod(i, GROUP)
            spot = ((spot + second) ^ 1) - second
            return min(max(spot, 0), length // GROUP - 1) * GROUP + inside

        return [
            lax.ppermute(sent[s], "tm", [(i, partner(i, s)) for i in range(length)])
            for s in range(2)
        ]

    def project(own, other, weight, scale, *ids):
        pack = shape((2 * rows + (ID_ROWS if ids else 0), width), bf16)
        return call(
            functools.partial(project_kernel, scale, bool(ids)),
            [pack] * GROUP,
            [pltpu.VMEM((rows, half), bf16), pltpu.VMEM((ID_ROWS, width), jnp.float32)],
            flops=4 * rows * half * half,
            moved=weight.size * 2 + 3 * rows * half * 2,
            name="project",
        )(own, other, weight, *ids)

    def attend(asking, *sources, after=()):
        window = (2 * RADIUS + 1) * rows
        reach = (2 * RADIUS + GROUP) * rows
        return call(
            functools.partial(attend_kernel, len(sources) == GROUP + 2, len(after)),
            [shape((rows, width), bf16)] * GROUP,
            [
                pltpu.VMEM((GROUP * rows, width), bf16),
                pltpu.VMEM((reach, width), bf16),
                pltpu.VMEM((reach, width), bf16),
                pltpu.VMEM((8, reach), jnp.float32),
                pltpu.VMEM((GROUP * rows, width), jnp.float32),
                pltpu.VMEM((GROUP * rows, width), bf16),
            ],
            flops=8 * GROUP * rows * window * width * 4,
            moved=4 * reach * width * 2,
            exps=2 * GROUP * rows * window,
            ins=[VMEM] * (GROUP + len(sources)) + [ANY] * len(after),
            name="attend",
        )(*asking, *sources, *after)

    def join(pieces):
        return call(
            join_kernel, shape((rows, half), bf16), moved=2 * rows * half * 2, name="join"
        )(*traded(pieces))

    assert length % (2 * GROUP) == 0
    ids = recording.reshape(rows // width, width)
    other_audio = swapped(audio_frames)
    other_video = swapped(video_frames)
    audio_packs = project(audio_frames, other_audio, audio_query, HEAD**-0.5, ids)
    audio_packs = traded(audio_packs)
    video_packs = project(video_frames, other_video, video_key, 1.0)
    audio_edges = halo(audio_packs, True, [video_packs[0]])
    video_packs = traded(video_packs)
    video_edges = halo(video_packs, False)
    video_pieces = attend(video_packs, *audio_packs, *audio_edges)
    audio_pieces = attend(
        audio_packs, *video_packs, *video_edges, *audio_packs, *audio_edges, after=video_pieces[:1]
    )
    video_attended = join(video_pieces)
    audio_attended = join(audio_pieces)
    return (audio_attended, video_attended)


def solution(mesh):
    return jax.shard_map(
        local,
        mesh=mesh,
        in_specs=(P("tm", "head"), P("tm", "head"), P("tm"), P(None, "head"), P(None, "head")),
        out_specs=(P("tm", "head"), P("tm", "head")),
        check_vma=False,
    )
```

time: 72.6 us -> 65.2 us (0.90)
  starting transfers between devices: 31.5 us -> 19.8 us
  waiting for transfers between devices: 16.4 us -> 21.7 us
  Pallas kernels: 20.9 us -> 19 us
    ppermute x6 -> x4, starting transfers between devices: 16 us -> 6.54 us  [halo(): lax.ppermute(sent[s], 'tm', [(i, partner(i, s)) for i in range(length)])]
    ppermute x2, waiting for transfers between devices: 0.01 us -> 5.92 us  [swapped(): return lax.ppermute(x, 'head', [(0, 1), (1, 0)])]
    ppermute x15 -> x12, starting transfers between devices: 13.9 us -> 11.7 us  [traded(): lax.ppermute(pieces[k], 'tm', pairs(k))]
    pallas_call x8 -> x6, Pallas kernels: 19.4 us -> 17.5 us  [the longest x2 16.3 us: attend(): call(functools.partial(attend_kernel, len(sources) == GROUP + 2, len(afte...]
    ppermute x15 -> x12, waiting for transfers between devices: 16.4 us -> 15.4 us  [traded(): lax.ppermute(pieces[k], 'tm', pairs(k))]
    unnamed x8 -> x10, local copies, waits for them, and re-layouts: 1.9 us -> 2.86 us
  transfers between devices with their start and end apart: 23 -> 18, of which waited for: 8 -> 8; matrix products, arithmetic and copies ran while one was open for 1% -> 0% of each run, Pallas kernels for 28% -> 28%
where the time goes in v2:
time: 65.2 us; the launch traced here: 64.1 us
  waiting for transfers between devices  21.7 us (33%)
  starting transfers between devices  19.8 us (30%)
  Pallas kernels  19 us (29%)
  local copies, waits for them, and re-layouts  2.86 us (4%)
  between operations  0.77 us (1%)
    pallas_call x2, Pallas kernels, attend(): call(functools.partial(attend_kernel, len(sources) == GROUP + 2, len(afte...  16.3 us
    ppermute x12, waiting for transfers between devices, traded(): lax.ppermute(pieces[k], 'tm', pairs(k))  15.4 us
    ppermute x12, starting transfers between devices, traded(): lax.ppermute(pieces[k], 'tm', pairs(k))  11.7 us
    ppermute x4, starting transfers between devices, halo(): lax.ppermute(sent[s], 'tm', [(i, partner(i, s)) for i in range(length)])  6.54 us
    ppermute x2, waiting for transfers between devices, swapped(): return lax.ppermute(x, 'head', [(0, 1), (1, 0)])  5.92 us
    unnamed x10, local copies, waits for them, and re-layouts  2.86 us
    ppermute x2, starting transfers between devices, swapped(): return lax.ppermute(x, 'head', [(0, 1), (1, 0)])  1.53 us
    pallas_call x2, Pallas kernels, join(): call(join_kernel, shape((rows, half), bf16), moved=2 * rows * half * 2, n...  1.53 us
  transfers between devices with their start and end apart: 18, of which 8 were waited for; matrix products, arithmetic and copies ran while one was open for 0% of the time, Pallas kernels for 28%

profile of v2, /device:TPU:9, one launch (start us, length us, event | category | flops | bytes accessed | tf_op | source)
XLA Modules:
  0.0 64.1 jit_solution(9660549834342566482)
XLA Ops:
  0.6 0.0 copy-start
  0.6 1.3 %collective-permute-start = (bf16[256,512]{1,0:T(8,128)(2,1)}, bf16[256,512]{1,0:T(8,128)(2,1)S(1)}, u32[]{:S(2)}, u32[]{:S(2)}) collective-permute-start(bf16[256,512]{1,0:T(8,128)(2,1)} %refs_0_.2), channel_id=1, source_target_pairs={{0,1},{1,0},{2,3},{3,2},{4,5},{5,4},{6,7},{7,6},{8,9},{9,8},{10,11... | collective-permute-start | bytes 786440 | tf_op jit(solution)/shard_map/ppermute | solution.py:173
  1.9 0.2 collective-permute-start.4
  2.2 5.9 %collective-permute-done.refs_1_ = bf16[256,512]{1,0:T(8,128)(2,1)S(1)} collective-permute-done((bf16[256,512]{1,0:T(8,128)(2,1)}, bf16[256,512]{1,0:T(8,128)(2,1)S(1)}, u32[]{:S(2)}, u32[]{:S(2)}) %collective-permute-start) | collective-permute-done | bytes 262176 | tf_op jit(solution)/shard_map/ppermute | solution.py:173
  8.1 0.0 copy-start.1
  8.1 1.2 %copy-done.1 = bf16[1024,512]{1,0:T(8,128)(2,1)S(1)} copy-done((bf16[1024,512]{1,0:T(8,128)(2,1)S(1)}, bf16[1024,512]{1,0:T(8,128)(2,1)}, u32[]{:S(2)}) %copy-start.1) | copy-done | bytes 1048600
  9.3 0.0 copy-start.2
  9.3 0.9 %copy-done.2 = bf16[256,512]{1,0:T(8,128)(2,1)S(1)} copy-done((bf16[256,512]{1,0:T(8,128)(2,1)S(1)}, bf16[256,512]{1,0:T(8,128)(2,1)}, u32[]{:S(2)}) %copy-start.2) | copy-done | bytes 262168
  10.3 0.0 copy-start.4
  10.3 0.7 %copy-done.4 = s32[256]{0:T(256)S(1)} copy-done((s32[256]{0:T(256)S(1)}, s32[256]{0:T(256)}, u32[]{:S(2)}) %copy-start.4) | copy-done | bytes 1048
  10.9 0.0 copy-start.3
  10.9 0.5 project.2
  11.5 2.8 %collective-permute-start.1 = (bf16[528,128]{1,0:T(8,128)(2,1)S(1)}, bf16[528,128]{1,0:T(8,128)(2,1)S(1)}, u32[]{:S(2)}, u32[]{:S(2)}) collective-permute-start(bf16[528,128]{1,0:T(8,128)(2,1)S(1)} %get-tuple-element.23), channel_id=1, source_target_pairs={{0,2},{2,0},{4,6},{6,4},{8,10},{10,8},{12,14},{14,12},{16,18},{18,... | collective-permute-start | bytes 405512 | tf_op jit(solution)/shard_map/ppermute | solution.py:177
  14.2 1.2 %collective-permute-start.2 = (bf16[528,128]{1,0:T(8,128)(2,1)S(1)}, bf16[528,128]{1,0:T(8,128)(2,1)S(1)}, u32[]{:S(2)}, u32[]{:S(2)}) collective-permute-start(bf16[528,128]{1,0:T(8,128)(2,1)S(1)} %get-tuple-element.24), channel_id=1, source_target_pairs={{0,4},{2,6},{4,0},{6,2},{8,12},{10,14},{12,8},{14,10},{16,20},{18,... | collective-permute-start | bytes 405512 | tf_op jit(solution)/shard_map/ppermute | solution.py:177
  15.5 0.5 collective-permute-start.3
  15.9 0.0 collective-permute-done.4.refs_1_
  15.9 0.0 copy-done
  15.9 0.0 copy-done.3
  15.9 0.5 project.3
  16.5 0.0 collective-permute-done.1.refs_1_.refs_5_.refs_11_
  16.5 2.9 %collective-permute-done.2.refs_2_.refs_6_.refs_12_ = bf16[528,128]{1,0:T(8,128)(2,1)S(1)} collective-permute-done((bf16[528,128]{1,0:T(8,128)(2,1)S(1)}, bf16[528,128]{1,0:T(8,128)(2,1)S(1)}, u32[]{:S(2)}, u32[]{:S(2)}) %collective-permute-start.2) | collective-permute-done | bytes 135200 | tf_op jit(solution)/shard_map/ppermute | solution.py:177
  19.4 3.1 %collective-permute-done.3.refs_3_.refs_7_.refs_13_ = bf16[528,128]{1,0:T(8,128)(2,1)S(1)} collective-permute-done((bf16[528,128]{1,0:T(8,128)(2,1)S(1)}, bf16[528,128]{1,0:T(8,128)(2,1)S(1)}, u32[]{:S(2)}, u32[]{:S(2)}) %collective-permute-start.3) | collective-permute-done | bytes 135200 | tf_op jit(solution)/shard_map/ppermute | solution.py:177
  22.4 0.1 halo.3
  22.6 0.1 collective-permute-start.10
  22.6 4.5 %collective-permute-start.11 = (bf16[1584,128]{1,0:T(8,128)(2,1)S(1)}, bf16[1584,128]{1,0:T(8,128)(2,1)S(1)}, u32[]{:S(2)}, u32[]{:S(2)}) collective-permute-start(bf16[1584,128]{1,0:T(8,128)(2,1)S(1)} %get-tuple-element.33), channel_id=1, source_target_pairs={{0,0},{2,2},{4,4},{6,6},{8,16},{10,18},{12,20},{14,22},{16,8},{18,... | collective-permute-start | bytes 1216520 | tf_op jit(solution)/shard_map/ppermute | solution.py:196
  27.1 0.9 %collective-permute-start.5 = (bf16[512,128]{1,0:T(8,128)(2,1)S(1)}, bf16[512,128]{1,0:T(8,128)(2,1)S(1)}, u32[]{:S(2)}, u32[]{:S(2)}) collective-permute-start(bf16[512,128]{1,0:T(8,128)(2,1)S(1)} %get-tuple-element.27), channel_id=1, source_target_pairs={{0,2},{2,0},{4,6},{6,4},{8,10},{10,8},{12,14},{14,12},{16,18},{18,... | collective-permute-start | bytes 393224 | tf_op jit(solution)/shard_map/ppermute | solution.py:177
  28.0 1.2 %collective-permute-start.6 = (bf16[512,128]{1,0:T(8,128)(2,1)S(1)}, bf16[512,128]{1,0:T(8,128)(2,1)S(1)}, u32[]{:S(2)}, u32[]{:S(2)}) collective-permute-start(bf16[512,128]{1,0:T(8,128)(2,1)S(1)} %get-tuple-element.28), channel_id=1, source_target_pairs={{0,4},{2,6},{4,0},{6,2},{8,12},{10,14},{12,8},{14,10},{16,20},{18,... | collective-permute-start | bytes 393224 | tf_op jit(solution)/shard_map/ppermute | solution.py:177
  29.2 0.5 collective-permute-start.7
  29.7 0.0 collective-permute-done.5.refs_1_.refs_5_
  29.7 3.4 %collective-permute-done.6.refs_2_.refs_6_ = bf16[512,128]{1,0:T(8,128)(2,1)S(1)} collective-permute-done((bf16[512,128]{1,0:T(8,128)(2,1)S(1)}, bf16[512,128]{1,0:T(8,128)(2,1)S(1)}, u32[]{:S(2)}, u32[]{:S(2)}) %collective-permute-start.6) | collective-permute-done | bytes 131104 | tf_op jit(solution)/shard_map/ppermute | solution.py:177
  33.1 3.3 %collective-permute-done.7.refs_3_.refs_7_ = bf16[512,128]{1,0:T(8,128)(2,1)S(1)} collective-permute-done((bf16[512,128]{1,0:T(8,128)(2,1)S(1)}, bf16[512,128]{1,0:T(8,128)(2,1)S(1)}, u32[]{:S(2)}, u32[]{:S(2)}) %collective-permute-start.7) | collective-permute-done | bytes 131104 | tf_op jit(solution)/shard_map/ppermute | solution.py:177
  36.3 0.1 halo.2
  36.4 0.1 collective-permute-start.8
  36.5 1.9 %collective-permute-start.9 = (bf16[1536,128]{1,0:T(8,128)(2,1)S(1)}, bf16[1536,128]{1,0:T(8,128)(2,1)S(1)}, u32[]{:S(2)}, u32[]{:S(2)}) collective-permute-start(bf16[1536,128]{1,0:T(8,128)(2,1)S(1)} %get-tuple-element.31), channel_id=1, source_target_pairs={{0,0},{2,2},{4,4},{6,6},{8,16},{10,18},{12,20},{14,22},{16,8},{18,... | collective-permute-start | bytes 1179656 | tf_op jit(solution)/shard_map/ppermute | solution.py:196
  38.4 0.0 collective-permute-done.10.refs_8_.refs_14_
  38.4 0.0 collective-permute-done.11.refs_9_.refs_15_
  38.4 8.2 %attend.2 = (bf16[256,128]{1,0:T(8,128)(2,1)S(1)}, bf16[256,128]{1,0:T(8,128)(2,1)S(1)}, bf16[256,128]{1,0:T(8,128)(2,1)S(1)}, bf16[256,128]{1,0:T(8,128)(2,1)S(1)}) custom-call(bf16[512,128]{1,0:T(8,128)(2,1)S(1)} %get-tuple-element.26.refs_0_.refs_4_, bf16[512,128]{1,0:T(8,128)(2,1)S(1)} %collective-permute-done.5.refs_1_.refs_5_, ...), custom_call_target="tpu_custom_call" | custom-call | flops 7516192768 | bytes 2621440 | tf_op jit(solution)/shard_map/attend/pallas_call | solution.py:214
  46.6 0.1 collective-permute-start.15
  46.7 1.3 %collective-permute-start.16 = (bf16[256,128]{1,0:T(8,128)(2,1)S(1)}, bf16[256,128]{1,0:T(8,128)(2,1)S(1)}, u32[]{:S(2)}, u32[]{:S(2)}) collective-permute-start(bf16[256,128]{1,0:T(8,128)(2,1)S(1)} %get-tuple-element.40), channel_id=1, source_target_pairs={{0,4},{2,6},{4,0},{6,2},{8,12},{10,14},{12,8},{14,10},{16,20},{18,... | collective-permute-start | bytes 196616 | tf_op jit(solution)/shard_map/ppermute | solution.py:177
  48.0 0.8 %collective-permute-start.17 = (bf16[256,128]{1,0:T(8,128)(2,1)S(1)}, bf16[256,128]{1,0:T(8,128)(2,1)S(1)}, u32[]{:S(2)}, u32[]{:S(2)}) collective-permute-start(bf16[256,128]{1,0:T(8,128)(2,1)S(1)} %get-tuple-element.41), channel_id=1, source_target_pairs={{0,6},{2,4},{4,2},{6,0},{8,14},{10,12},{12,10},{14,8},{16,22},{18,... | collective-permute-start | bytes 196616 | tf_op jit(solution)/shard_map/ppermute | solution.py:177
  48.8 0.0 collective-permute-done.8.refs_8_
  48.8 0.4 collective-permute-done.9.refs_9_
  49.2 8.1 %attend.3 = (bf16[256,128]{1,0:T(8,128)(2,1)S(1)}, bf16[256,128]{1,0:T(8,128)(2,1)S(1)}, bf16[256,128]{1,0:T(8,128)(2,1)S(1)}, bf16[256,128]{1,0:T(8,128)(2,1)S(1)}) custom-call(bf16[528,128]{1,0:T(8,128)(2,1)S(1)} %get-tuple-element.22.refs_0_.refs_4_.refs_10_, bf16[528,128]{1,0:T(8,128)(2,1)S(1)} %collective-permute-done.1.refs_1_.refs_5_.refs_11_, ...), custom_call_target="tpu_custom_call" | custom-call | flops 7516192768 | bytes 2621440 | tf_op jit(solution)/shard_map/attend/pallas_call | solution.py:214
  57.3 0.8 %collective-permute-start.12 = (bf16[256,128]{1,0:T(8,128)(2,1)S(1)}, bf16[256,128]{1,0:T(8,128)(2,1)S(1)}, u32[]{:S(2)}, u32[]{:S(2)}) collective-permute-start(bf16[256,128]{1,0:T(8,128)(2,1)S(1)} %get-tuple-element.36), channel_id=1, source_target_pairs={{0,2},{2,0},{4,6},{6,4},{8,10},{10,8},{12,14},{14,12},{16,18},{18,... | collective-permute-start | bytes 196616 | tf_op jit(solution)/shard_map/ppermute | solution.py:177
  58.1 1.2 %collective-permute-start.13 = (bf16[256,128]{1,0:T(8,128)(2,1)S(1)}, bf16[256,128]{1,0:T(8,128)(2,1)S(1)}, u32[]{:S(2)}, u32[]{:S(2)}) collective-permute-start(bf16[256,128]{1,0:T(8,128)(2,1)S(1)} %get-tuple-element.37), channel_id=1, source_target_pairs={{0,4},{2,6},{4,0},{6,2},{8,12},{10,14},{12,8},{14,10},{16,20},{18,... | collective-permute-start | bytes 196616 | tf_op jit(solution)/shard_map/ppermute | solution.py:177
  59.3 0.0 collective-permute-done.15.refs_1_
  59.3 0.5 collective-permute-start.14
  59.8 0.0 collective-permute-done.16.refs_2_
  59.8 0.0 collective-permute-done.17.refs_3_
  59.8 0.8 %join.3 = bf16[256,512]{1,0:T(8,128)(2,1)} custom-call(bf16[256,128]{1,0:T(8,128)(2,1)S(1)} %get-tuple-element.34.refs_16_.refs_0_, bf16[256,128]{1,0:T(8,128)(2,1)S(1)} %collective-permute-done.15.refs_1_, bf16[256,128]{1,0:T(8,128)(2,1)S(1)} %collective-permute-done.16.refs_2_, bf16[256,128]{1,0:T(8,128)(2,1)S(1)} %collective-permute-done.17.refs_3_), custom_call_target="tpu_custom_call" | custom-call | bytes 524288 | tf_op jit(solution)/shard_map/join/pallas_call | solution.py:233
  60.6 0.0 collective-permute-done.12.refs_1_
  60.6 1.2 %collective-permute-done.13.refs_2_ = bf16[256,128]{1,0:T(8,128)(2,1)S(1)} collective-permute-done((bf16[256,128]{1,0:T(8,128)(2,1)S(1)}, bf16[256,128]{1,0:T(8,128)(2,1)S(1)}, u32[]{:S(2)}, u32[]{:S(2)}) %collective-permute-start.13) | collective-permute-done | bytes 65568 | tf_op jit(solution)/shard_map/ppermute | solution.py:177
  61.8 1.6 %collective-permute-done.14.refs_3_ = bf16[256,128]{1,0:T(8,128)(2,1)S(1)} collective-permute-done((bf16[256,128]{1,0:T(8,128)(2,1)S(1)}, bf16[256,128]{1,0:T(8,128)(2,1)S(1)}, u32[]{:S(2)}, u32[]{:S(2)}) %collective-permute-start.14) | collective-permute-done | bytes 65568 | tf_op jit(solution)/shard_map/ppermute | solution.py:177
  63.4 0.8 %join.2 = bf16[256,512]{1,0:T(8,128)(2,1)} custom-call(bf16[256,128]{1,0:T(8,128)(2,1)S(1)} %get-tuple-element.35.refs_0_, bf16[256,128]{1,0:T(8,128)(2,1)S(1)} %collective-permute-done.12.refs_1_, bf16[256,128]{1,0:T(8,128)(2,1)S(1)} %collective-permute-done.13.refs_2_, bf16[256,128]{1,0:T(8,128)(2,1)S(1)} %collective-permute-done.14.refs_3_), custom_call_target="tpu_custom_call" | custom-call | bytes 524288 | tf_op jit(solution)/shard_map/join/pallas_call | solution.py:233
Async XLA Ops:
  0.6 15.3 %copy-start = (bf16[1024,512]{1,0:T(8,128)(2,1)S(1)}, bf16[1024,512]{1,0:T(8,128)(2,1)}, u32[]{:S(2)}) copy-start(bf16[1024,512]{1,0:T(8,128)(2,1)} %refs_2_.3) | copy-start | bytes 3145732
  0.6 7.5 %collective-permute-start = (bf16[256,512]{1,0:T(8,128)(2,1)}, bf16[256,512]{1,0:T(8,128)(2,1)S(1)}, u32[]{:S(2)}, u32[]{:S(2)}) collective-permute-start(bf16[256,512]{1,0:T(8,128)(2,1)} %refs_0_.2), channel_id=1, source_target_pairs={{0,1},{1,0},{2,3},{3,2},{4,5},{5,4},{6,7},{7,6},{8,9},{9,8},{10,11... | collective-permute-start | bytes 786440 | tf_op jit(solution)/shard_map/ppermute | solution.py:173
  1.9 14.0 %collective-permute-start.4 = (bf16[256,512]{1,0:T(8,128)(2,1)}, bf16[256,512]{1,0:T(8,128)(2,1)S(1)}, u32[]{:S(2)}, u32[]{:S(2)}) collective-permute-start(bf16[256,512]{1,0:T(8,128)(2,1)} %refs_0_.3), channel_id=1, source_target_pairs={{0,1},{1,0},{2,3},{3,2},{4,5},{5,4},{6,7},{7,6},{8,9},{9,8},{10,11... | collective-permute-start | bytes 786440 | tf_op jit(solution)/shard_map/ppermute | solution.py:173
  8.1 1.2 %copy-start.1 = (bf16[1024,512]{1,0:T(8,128)(2,1)S(1)}, bf16[1024,512]{1,0:T(8,128)(2,1)}, u32[]{:S(2)}) copy-start(bf16[1024,512]{1,0:T(8,128)(2,1)} %refs_2_.2) | copy-start | bytes 3145732
  9.3 0.9 %copy-start.2 = (bf16[256,512]{1,0:T(8,128)(2,1)S(1)}, bf16[256,512]{1,0:T(8,128)(2,1)}, u32[]{:S(2)}) copy-start(bf16[256,512]{1,0:T(8,128)(2,1)} %refs_0_.2) | copy-start | bytes 786436
  10.3 0.7 %copy-start.4 = (s32[256]{0:T(256)S(1)}, s32[256]{0:T(256)}, u32[]{:S(2)}) copy-start(s32[256]{0:T(256)} %param.7) | copy-start | bytes 3076
  10.9 5.0 %copy-start.3 = (bf16[256,512]{1,0:T(8,128)(2,1)S(1)}, bf16[256,512]{1,0:T(8,128)(2,1)}, u32[]{:S(2)}) copy-start(bf16[256,512]{1,0:T(8,128)(2,1)} %refs_0_.3) | copy-start | bytes 786436
  11.5 5.0 %collective-permute-start.1 = (bf16[528,128]{1,0:T(8,128)(2,1)S(1)}, bf16[528,128]{1,0:T(8,128)(2,1)S(1)}, u32[]{:S(2)}, u32[]{:S(2)}) collective-permute-start(bf16[528,128]{1,0:T(8,128)(2,1)S(1)} %get-tuple-element.23), channel_id=1, source_target_pairs={{0,2},{2,0},{4,6},{6,4},{8,10},{10,8},{12,14},{14,12},{16,18},{18,... | collective-permute-start | bytes 405512 | tf_op jit(solution)/shard_map/ppermute | solution.py:177
  14.2 5.2 %collective-permute-start.2 = (bf16[528,128]{1,0:T(8,128)(2,1)S(1)}, bf16[528,128]{1,0:T(8,128)(2,1)S(1)}, u32[]{:S(2)}, u32[]{:S(2)}) collective-permute-start(bf16[528,128]{1,0:T(8,128)(2,1)S(1)} %get-tuple-element.24), channel_id=1, source_target_pairs={{0,4},{2,6},{4,0},{6,2},{8,12},{10,14},{12,8},{14,10},{16,20},{18,... | collective-permute-start | bytes 405512 | tf_op jit(solution)/shard_map/ppermute | solution.py:177
  15.5 7.0 %collective-permute-start.3 = (bf16[528,128]{1,0:T(8,128)(2,1)S(1)}, bf16[528,128]{1,0:T(8,128)(2,1)S(1)}, u32[]{:S(2)}, u32[]{:S(2)}) collective-permute-start(bf16[528,128]{1,0:T(8,128)(2,1)S(1)} %get-tuple-element.25), channel_id=1, source_target_pairs={{0,6},{2,4},{4,2},{6,0},{8,14},{10,12},{12,10},{14,8},{16,22},{18,... | collective-permute-start | bytes 405512 | tf_op jit(solution)/shard_map/ppermute | solution.py:177
  22.6 15.9 %collective-permute-start.10 = (bf16[1584,128]{1,0:T(8,128)(2,1)S(1)}, bf16[1584,128]{1,0:T(8,128)(2,1)S(1)}, u32[]{:S(2)}, u32[]{:S(2)}) collective-permute-start(bf16[1584,128]{1,0:T(8,128)(2,1)S(1)} %get-tuple-element.32), channel_id=1, source_target_pairs={{0,8},{2,10},{4,12},{6,14},{8,0},{10,2},{12,4},{14,6},{16,24},{18,... | collective-permute-start | bytes 1216520 | tf_op jit(solution)/shard_map/ppermute | solution.py:196
  22.6 15.8 %collective-permute-start.11 = (bf16[1584,128]{1,0:T(8,128)(2,1)S(1)}, bf16[1584,128]{1,0:T(8,128)(2,1)S(1)}, u32[]{:S(2)}, u32[]{:S(2)}) collective-permute-start(bf16[1584,128]{1,0:T(8,128)(2,1)S(1)} %get-tuple-element.33), channel_id=1, source_target_pairs={{0,0},{2,2},{4,4},{6,6},{8,16},{10,18},{12,20},{14,22},{16,8},{18,... | collective-permute-start | bytes 1216520 | tf_op jit(solution)/shard_map/ppermute | solution.py:196
  27.1 2.6 %collective-permute-start.5 = (bf16[512,128]{1,0:T(8,128)(2,1)S(1)}, bf16[512,128]{1,0:T(8,128)(2,1)S(1)}, u32[]{:S(2)}, u32[]{:S(2)}) collective-permute-start(bf16[512,128]{1,0:T(8,128)(2,1)S(1)} %get-tuple-element.27), channel_id=1, source_target_pairs={{0,2},{2,0},{4,6},{6,4},{8,10},{10,8},{12,14},{14,12},{16,18},{18,... | collective-permute-start | bytes 393224 | tf_op jit(solution)/shard_map/ppermute | solution.py:177
  28.0 5.1 %collective-permute-start.6 = (bf16[512,128]{1,0:T(8,128)(2,1)S(1)}, bf16[512,128]{1,0:T(8,128)(2,1)S(1)}, u32[]{:S(2)}, u32[]{:S(2)}) collective-permute-start(bf16[512,128]{1,0:T(8,128)(2,1)S(1)} %get-tuple-element.28), channel_id=1, source_target_pairs={{0,4},{2,6},{4,0},{6,2},{8,12},{10,14},{12,8},{14,10},{16,20},{18,... | collective-permute-start | bytes 393224 | tf_op jit(solution)/shard_map/ppermute | solution.py:177
  29.2 7.1 %collective-permute-start.7 = (bf16[512,128]{1,0:T(8,128)(2,1)S(1)}, bf16[512,128]{1,0:T(8,128)(2,1)S(1)}, u32[]{:S(2)}, u32[]{:S(2)}) collective-permute-start(bf16[512,128]{1,0:T(8,128)(2,1)S(1)} %get-tuple-element.29), channel_id=1, source_target_pairs={{0,6},{2,4},{4,2},{6,0},{8,14},{10,12},{12,10},{14,8},{16,22},{18,... | collective-permute-start | bytes 393224 | tf_op jit(solution)/shard_map/ppermute | solution.py:177
  36.4 12.4 %collective-permute-start.8 = (bf16[1536,128]{1,0:T(8,128)(2,1)S(1)}, bf16[1536,128]{1,0:T(8,128)(2,1)S(1)}, u32[]{:S(2)}, u32[]{:S(2)}) collective-permute-start(bf16[1536,128]{1,0:T(8,128)(2,1)S(1)} %get-tuple-element.30), channel_id=1, source_target_pairs={{0,8},{2,10},{4,12},{6,14},{8,0},{10,2},{12,4},{14,6},{16,24},{18,... | collective-permute-start | bytes 1179656 | tf_op jit(solution)/shard_map/ppermute | solution.py:196
  36.5 12.7 %collective-permute-start.9 = (bf16[1536,128]{1,0:T(8,128)(2,1)S(1)}, bf16[1536,128]{1,0:T(8,128)(2,1)S(1)}, u32[]{:S(2)}, u32[]{:S(2)}) collective-permute-start(bf16[1536,128]{1,0:T(8,128)(2,1)S(1)} %get-tuple-element.31), channel_id=1, source_target_pairs={{0,0},{2,2},{4,4},{6,6},{8,16},{10,18},{12,20},{14,22},{16,8},{18,... | collective-permute-start | bytes 1179656 | tf_op jit(solution)/shard_map/ppermute | solution.py:196
  46.6 12.7 %collective-permute-start.15 = (bf16[256,128]{1,0:T(8,128)(2,1)S(1)}, bf16[256,128]{1,0:T(8,128)(2,1)S(1)}, u32[]{:S(2)}, u32[]{:S(2)}) collective-permute-start(bf16[256,128]{1,0:T(8,128)(2,1)S(1)} %get-tuple-element.39), channel_id=1, source_target_pairs={{0,2},{2,0},{4,6},{6,4},{8,10},{10,8},{12,14},{14,12},{16,18},{18,... | collective-permute-start | bytes 196616 | tf_op jit(solution)/shard_map/ppermute | solution.py:177
  46.7 13.1 %collective-permute-start.16 = (bf16[256,128]{1,0:T(8,128)(2,1)S(1)}, bf16[256,128]{1,0:T(8,128)(2,1)S(1)}, u32[]{:S(2)}, u32[]{:S(2)}) collective-permute-start(bf16[256,128]{1,0:T(8,128)(2,1)S(1)} %get-tuple-element.40), channel_id=1, source_target_pairs={{0,4},{2,6},{4,0},{6,2},{8,12},{10,14},{12,8},{14,10},{16,20},{18,... | collective-permute-start | bytes 196616 | tf_op jit(solution)/shard_map/ppermute | solution.py:177
  48.0 11.8 %collective-permute-start.17 = (bf16[256,128]{1,0:T(8,128)(2,1)S(1)}, bf16[256,128]{1,0:T(8,128)(2,1)S(1)}, u32[]{:S(2)}, u32[]{:S(2)}) collective-permute-start(bf16[256,128]{1,0:T(8,128)(2,1)S(1)} %get-tuple-element.41), channel_id=1, source_target_pairs={{0,6},{2,4},{4,2},{6,0},{8,14},{10,12},{12,10},{14,8},{16,22},{18,... | collective-permute-start | bytes 196616 | tf_op jit(solution)/shard_map/ppermute | solution.py:177
  57.3 3.3 %collective-permute-start.12 = (bf16[256,128]{1,0:T(8,128)(2,1)S(1)}, bf16[256,128]{1,0:T(8,128)(2,1)S(1)}, u32[]{:S(2)}, u32[]{:S(2)}) collective-permute-start(bf16[256,128]{1,0:T(8,128)(2,1)S(1)} %get-tuple-element.36), channel_id=1, source_target_pairs={{0,2},{2,0},{4,6},{6,4},{8,10},{10,8},{12,14},{14,12},{16,18},{18,... | collective-permute-start | bytes 196616 | tf_op jit(solution)/shard_map/ppermute | solution.py:177
  58.1 3.7 %collective-permute-start.13 = (bf16[256,128]{1,0:T(8,128)(2,1)S(1)}, bf16[256,128]{1,0:T(8,128)(2,1)S(1)}, u32[]{:S(2)}, u32[]{:S(2)}) collective-permute-start(bf16[256,128]{1,0:T(8,128)(2,1)S(1)} %get-tuple-element.37), channel_id=1, source_target_pairs={{0,4},{2,6},{4,0},{6,2},{8,12},{10,14},{12,8},{14,10},{16,20},{18,... | collective-permute-start | bytes 196616 | tf_op jit(solution)/shard_map/ppermute | solution.py:177
  59.3 4.0 %collective-permute-start.14 = (bf16[256,128]{1,0:T(8,128)(2,1)S(1)}, bf16[256,128]{1,0:T(8,128)(2,1)S(1)}, u32[]{:S(2)}, u32[]{:S(2)}) collective-permute-start(bf16[256,128]{1,0:T(8,128)(2,1)S(1)} %get-tuple-element.38), channel_id=1, source_target_pairs={{0,6},{2,4},{4,2},{6,0},{8,14},{10,12},{12,10},{14,8},{16,22},{18,... | collective-permute-start | bytes 196616 | tf_op jit(solution)/shard_map/ppermute | solution.py:177

commit v3 on v2

v3 whole, which is shorter than its diff:
```python
import functools

import jax
import jax.numpy as jnp
from jax import lax
from jax.experimental import pallas as pl
from jax.experimental.pallas import tpu as pltpu
from jax.sharding import PartitionSpec as P

HEAD = 64
RADIUS = 3
GROUP = 4
NEG = -1e30
ID_ROWS = 16

VMEM = pl.BlockSpec(memory_space=pltpu.VMEM)
ANY = pl.BlockSpec(memory_space=pl.ANY)
HBM = pl.BlockSpec(memory_space=pltpu.HBM)


def place():
    return lax.rem(lax.axis_index("tm"), GROUP)


def plane():
    return lax.axis_index("tm") // GROUP


def call(kernel, outs, scratch=(), ins=None, flops=0, moved=0, exps=0, name=None, room=48):
    return pl.pallas_call(
        kernel,
        out_shape=outs,
        **({"in_specs": ins} if ins else {}),
        scratch_shapes=scratch,
        compiler_params=pltpu.CompilerParams(vmem_limit_bytes=room * 2**20),
        cost_estimate=pl.CostEstimate(flops=flops, bytes_accessed=moved, transcendentals=exps),
        name=name,
    )


def prepare_kernel(audio, video, query, key, ids, *refs):
    sent, sums, turned, seconds, id_rows = refs[0], refs[1:3], refs[3:5], refs[5:7], refs[7]
    own, firsts, ids_in, ids_wide, sems = refs[8], refs[9:11], refs[11], refs[12], refs[13]
    half = audio.shape[1]
    rows, width = audio.shape[0], turned[0].shape[1]
    side = lax.axis_index("head")
    mine = place()
    copies = []

    def fetch(source, target):
        copies.append(pltpu.make_async_copy(source, target, sems.at[len(copies)]))
        copies[-1].start()
        return copies[-1]

    streams = (own, sent)
    loads = [fetch(audio, own), fetch(video, sent)]
    ours = pl.ds(pl.multiple_of(side * half, half), half)
    theirs = pl.ds(pl.multiple_of((1 - side) * half, half), half)
    weights = [fetch(w.at[ours], f) for w, f in zip((query, key), firsts)]
    others = [fetch(w.at[theirs], f) for w, f in zip((query, key), seconds)]
    others.append(fetch(ids, ids_in))
    for i in range(2):
        loads[i].wait()
        for k in range(GROUP):
            columns = pl.ds(pl.multiple_of((mine ^ k) * width, width), width)
            for at in range(0, rows, width):
                square = streams[i][at : at + width, columns]
                turned[i][k * rows + at : k * rows + at + width] = jnp.transpose(square)
    for i in range(2):
        weights[i].wait()
        sums[i][...] = jnp.dot(
            streams[i][...], firsts[i][...], preferred_element_type=jnp.float32
        )
    for copy in others:
        copy.wait()
    ids_wide[...] = jnp.zeros_like(ids_wide)
    ids_wide[: ids_in.shape[0]] = (ids_in[...] + 1).astype(jnp.float32)
    id_rows[...] = ids_wide[...].astype(id_rows.dtype)


def project_kernel(scale, has_ids, *refs):
    turned, part, other, weight = refs[:4]
    packs, full = refs[-GROUP - 1 : -1], refs[-1]
    rows, width = other.shape[0], packs[0].shape[1]
    mine = place()
    total = part[...] + jnp.dot(other[...], weight[...], preferred_element_type=jnp.float32)
    rounded = total.astype(jnp.bfloat16)
    full[...] = rounded * jnp.bfloat16(scale) if scale != 1.0 else rounded
    for k in range(GROUP):
        columns = pl.ds(pl.multiple_of((mine ^ k) * width, width), width)
        packs[k][:rows] = turned[k * rows : (k + 1) * rows]
        packs[k][rows : 2 * rows] = full[:, columns]
        if has_ids:
            packs[k][2 * rows :] = refs[4][...]


def halo_kernel(has_ids, *refs):
    pieces, (first, second) = refs[:GROUP], refs[-2:]
    rows = pieces[0].shape[0]
    mine = place()
    odd = lax.rem(plane(), 2)
    for k in range(GROUP):
        block = mine ^ k
        for out, skip in ((first, (GROUP - RADIUS) * (1 - odd)), (second, (GROUP - RADIUS) * odd)):
            spot = block - skip

            @pl.when((spot >= 0) & (spot < RADIUS))
            def _():
                out[pl.ds(pl.multiple_of(spot * rows, 16), rows)] = pieces[k][...]

    if has_ids:
        last = lax.axis_size("tm") // GROUP - 1

        @pl.when((plane() == 0) | (plane() == last))
        def _():
            for i in range(RADIUS):
                at = (i + 1) * rows - ID_ROWS
                second[at : at + ID_ROWS] = jnp.zeros((ID_ROWS, second.shape[1]), second.dtype)


def join_kernel(*refs):
    pieces, out = refs[:GROUP], refs[GROUP]
    width = pieces[0].shape[1]
    mine = place()
    for k in range(GROUP):
        out[:, pl.ds(pl.multiple_of((mine ^ k) * width, width), width)] = pieces[k][...]


def attend_kernel(first, *refs):
    refs = list(refs)
    take = lambda count: [refs.pop(0) for _ in range(count)]
    asking, sources, edges, (marks,) = take(GROUP), take(GROUP), take(2), take(1) if not first else (None,)
    outs, (marks_out,) = take(GROUP), take(1) if first else (None,)
    ask_all, key_all, value_all, out_all = refs
    rows, width = outs[0].shape
    window = (2 * RADIUS + 1) * rows
    reach = key_all.shape[0]
    mine = place()
    source_rows = sources[0].shape[0]
    bf16 = jnp.bfloat16

    def block_at(block):
        return pl.ds(pl.multiple_of(block * rows, rows), rows)

    def put(source, at, block):
        key_all[block_at(block), :width] = source[at + rows : at + 2 * rows]
        if first:
            lanes = source[at + 2 * rows : at + 2 * rows + ID_ROWS].astype(jnp.float32)
        for part in range(0, rows, width):
            spot = pl.ds(pl.multiple_of(block * rows + part, width), width)
            value_all[:, spot] = source[at + part : at + part + width]
            if first:
                ids = lanes[part // width : part // width + 1]
                column = jnp.transpose(jnp.broadcast_to(ids, (width, width)))
                lane = lax.broadcasted_iota(jnp.int32, (width, width), 1)
                mark = jnp.where(column == lane.astype(jnp.float32), 1.0, 0.0).astype(bf16)
                key_all[spot, width:] = mark
                marks_out[spot] = mark

    for k in range(GROUP):
        ask_all[block_at(mine ^ k)] = asking[k][rows : 2 * rows]
        put(sources[k], 0, (mine ^ k) + RADIUS)
    odd = lax.rem(plane(), 2)
    for edge in range(2):
        spot = (RADIUS + GROUP) * (odd if edge else 1 - odd)
        for i in range(RADIUS):
            put(edges[edge], i * source_rows, spot + i)
    if not first:
        key_all[:, width:] = marks[...]

    lane = lax.broadcasted_iota(jnp.int32, (rows, width), 1)

    def one(block, _):
        near = pl.ds(pl.multiple_of(block * rows, rows), window)
        ask = ask_all[block_at(block)]
        forbid = (key_all[block_at(block + RADIUS), width:] - bf16(1.0)) * bf16(-NEG)
        results = []
        for h in range(width // HEAD):
            only = jnp.where(lane // HEAD == h, ask, jnp.zeros_like(ask))
            scores = lax.dot_general(
                key_all[near, :],
                jnp.concatenate([only, forbid], axis=1),
                (((1,), (1,)), ((), ())),
                preferred_element_type=jnp.float32,
            )
            weights = jnp.exp(scores - jnp.max(scores, axis=0, keepdims=True))
            total = jnp.sum(weights, axis=0, keepdims=True)
            mixed = jnp.dot(
                value_all[h * HEAD : (h + 1) * HEAD, near],
                weights.astype(bf16),
                preferred_element_type=jnp.float32,
            )
            results.append(mixed / total)
        out_all[block_at(block)] = jnp.transpose(jnp.concatenate(results, axis=0)).astype(bf16)
        return _

    lax.fori_loop(0, GROUP, one, 0)
    for k in range(GROUP):
        outs[k][...] = out_all[block_at(mine ^ k)]


def local(audio_frames, video_frames, recording, audio_query, video_key):
    rows, half = audio_frames.shape
    width = half // GROUP
    length = lax.axis_size("tm")
    bf16 = jnp.bfloat16
    shape = jax.ShapeDtypeStruct

    def swapped(x):
        return lax.ppermute(x, "head", [(0, 1), (1, 0)])

    def traded(pieces):
        pairs = lambda k: [(i, i ^ k) for i in range(length)]
        return [pieces[0]] + [lax.ppermute(pieces[k], "tm", pairs(k)) for k in range(1, GROUP)]

    def halo(pieces, has_ids, after=()):
        size = pieces[0].shape[0]
        edge = shape((RADIUS * size, width), bf16)
        sent = call(
            functools.partial(halo_kernel, has_ids),
            [edge, edge],
            ins=[VMEM] * GROUP + [ANY] * len(after),
            moved=10 * size * width * 2,
            name="halo",
        )(*pieces, *after)

        def partner(i, second):
            spot, inside = divmod(i, GROUP)
            spot = ((spot + second) ^ 1) - second
            return min(max(spot, 0), length // GROUP - 1) * GROUP + inside

        return [
            lax.ppermute(sent[s], "tm", [(i, partner(i, s)) for i in range(length)])
            for s in range(2)
        ]

    def project(turned, part, other, weight, scale, *ids):
        pack = shape((2 * rows + (ID_ROWS if ids else 0), width), bf16)
        return call(
            functools.partial(project_kernel, scale, bool(ids)),
            [pack] * GROUP,
            [pltpu.VMEM((rows, half), bf16)],
            flops=2 * rows * half * half,
            moved=weight.size * 2 + 3 * rows * half * 2,
            name="project",
        )(turned, part, other, weight, *ids)

    def attend(asking, sources, edges, *marks):
        window = (2 * RADIUS + 1) * rows
        reach = (2 * RADIUS + GROUP) * rows
        outs = [shape((rows, width), bf16)] * GROUP
        return call(
            functools.partial(attend_kernel, not marks),
            outs if marks else outs + [shape((reach, width), bf16)],
            [
                pltpu.VMEM((GROUP * rows, width), bf16),
                pltpu.VMEM((reach, 2 * width), bf16),
                pltpu.VMEM((width, reach), bf16),
                pltpu.VMEM((GROUP * rows, width), bf16),
            ],
            flops=8 * GROUP * rows * window * width * 4,
            moved=4 * reach * width * 2,
            exps=2 * GROUP * rows * window,
            name="attend",
        )(*asking, *sources, *edges, *marks)

    def join(pieces):
        return call(
            join_kernel, shape((rows, half), bf16), moved=2 * rows * half * 2, name="join"
        )(*traded(pieces))

    assert length % (2 * GROUP) == 0
    other_audio = swapped(audio_frames)
    part = shape((rows, half), jnp.float32)
    turned = shape((GROUP * rows, width), bf16)
    square = shape((half, half), bf16)
    given = (audio_frames, video_frames, audio_query, video_key, recording.reshape(rows // width, width))
    video_copy, query_part, key_part, audio_turned, video_turned, query_rest, key_rest, ids = call(
        prepare_kernel,
        [shape((rows, half), bf16), part, part, turned, turned, square, square]
        + [shape((ID_ROWS, width), bf16)],
        [pltpu.VMEM((rows, half), bf16)]
        + [pltpu.VMEM((half, half), bf16)] * 2
        + [pltpu.VMEM((rows // width, width), jnp.int32), pltpu.VMEM((ID_ROWS, width), jnp.float32)]
        + [pltpu.SemaphoreType.DMA((7,))],
        ins=[HBM] * 5,
        flops=4 * rows * half * half,
        moved=16 * half * half,
        name="prepare",
    )(*(pltpu.with_memory_space_constraint(x, pltpu.HBM) for x in given))
    other_video = swapped(video_copy)
    audio_packs = traded(
        project(audio_turned, query_part, other_audio, query_rest, HEAD**-0.5, ids)
    )
    video_packs = traded(project(video_turned, key_part, other_video, key_rest, 1.0))
    audio_edges = halo(audio_packs, True, [video_packs[1]])
    video_edges = halo(video_packs, False)
    *video_pieces, marks = attend(video_packs, audio_packs, audio_edges)
    audio_pieces = attend(audio_packs, video_packs, video_edges, marks)
    video_attended = join(video_pieces)
    audio_attended = join(audio_pieces)
    return (audio_attended, video_attended)


def solution(mesh):
    return jax.shard_map(
        local,
        mesh=mesh,
        in_specs=(P("tm", "head"), P("tm", "head"), P("tm"), P(None, "head"), P(None, "head")),
        out_specs=(P("tm", "head"), P("tm", "head")),
        check_vma=False,
    )
```

time: 65.2 us -> 64.6 us (level)
  the two profiles are of different devices: /device:TPU:9 before, /device:TPU:0 now
where the time goes in v3:
time: 64.6 us; the launch traced here: 64.4 us
  Pallas kernels  23.9 us (37%)
  waiting for transfers between devices  21 us (33%)
  starting transfers between devices  18.7 us (29%)
  between operations  0.77 us (1%)
    pallas_call x2, Pallas kernels, attend(): call(functools.partial(attend_kernel, not marks), outs if marks else outs...  19.5 us
    ppermute x12, waiting for transfers between devices, traded(): lax.ppermute(pieces[k], 'tm', pairs(k))  13.5 us
    ppermute x12, starting transfers between devices, traded(): lax.ppermute(pieces[k], 'tm', pairs(k))  8.12 us
    ppermute x4, starting transfers between devices, halo(): lax.ppermute(sent[s], 'tm', [(i, partner(i, s)) for i in range(length)])  7.51 us
    ppermute x2, waiting for transfers between devices, swapped(): return lax.ppermute(x, 'head', [(0, 1), (1, 0)])  7.5 us
    ppermute x2, starting transfers between devices, swapped(): return lax.ppermute(x, 'head', [(0, 1), (1, 0)])  3.1 us
    pallas_call x1, Pallas kernels, local(): call(prepare_kernel, [shape((rows, half), bf16), part, part, turned, turn...  1.91 us
    pallas_call x2, Pallas kernels, join(): call(join_kernel, shape((rows, half), bf16), moved=2 * rows * half * 2, n...  1.54 us
  transfers between devices with their start and end apart: 18, of which 9 were waited for; matrix products, arithmetic and copies ran while one was open for 0% of the time, Pallas kernels for 36%

profile of v3, /device:TPU:0, one launch (start us, length us, event | category | flops | bytes accessed | tf_op | source)
XLA Modules:
  0.0 64.4 jit_solution(7805474291744506254)
XLA Ops:
  0.6 3.0 %collective-permute-start = (bf16[256,512]{1,0:T(8,128)(2,1)}, bf16[256,512]{1,0:T(8,128)(2,1)S(1)}, u32[]{:S(2)}, u32[]{:S(2)}) collective-permute-start(bf16[256,512]{1,0:T(8,128)(2,1)} %audio.1), channel_id=1, source_target_pairs={{0,1},{1,0},{2,3},{3,2},{4,5},{5,4},{6,7},{7,6},{8,9},{9,8},{10,11... | collective-permute-start | bytes 786440 | tf_op jit(solution)/shard_map/ppermute | solution.py:210
  3.7 1.9 %prepare.1 = (bf16[256,512]{1,0:T(8,128)(2,1)S(1)}, f32[256,512]{1,0:T(8,128)S(1)}, f32[256,512]{1,0:T(8,128)S(1)}, bf16[1024,128]{1,0:T(8,128)(2,1)S(1)}, bf16[...) custom-call(bf16[256,512]{1,0:T(8,128)(2,1)} %audio.1, ...), custom_call_target="tpu_custom_call" | custom-call | flops 268435456 | bytes 4194304 | tf_op jit(solution)/shard_map/prepare/pallas_call | solution.py:278
  5.6 0.1 collective-permute-start.4
  5.7 5.3 %collective-permute-done.refs_2_ = bf16[256,512]{1,0:T(8,128)(2,1)S(1)} collective-permute-done((bf16[256,512]{1,0:T(8,128)(2,1)}, bf16[256,512]{1,0:T(8,128)(2,1)S(1)}, u32[]{:S(2)}, u32[]{:S(2)}) %collective-permute-start) | collective-permute-done | bytes 262176 | tf_op jit(solution)/shard_map/ppermute | solution.py:210
  11.0 0.4 project.2
  11.4 0.1 collective-permute-start.1
  11.5 2.1 %collective-permute-start.2 = (bf16[528,128]{1,0:T(8,128)(2,1)S(1)}, bf16[528,128]{1,0:T(8,128)(2,1)S(1)}, u32[]{:S(2)}, u32[]{:S(2)}) collective-permute-start(bf16[528,128]{1,0:T(8,128)(2,1)S(1)} %get-tuple-element.37), channel_id=1, source_target_pairs={{0,4},{2,6},{4,0},{6,2},{8,12},{10,14},{12,8},{14,10},{16,20},{18,... | collective-permute-start | bytes 405512 | tf_op jit(solution)/shard_map/ppermute | solution.py:214
  13.6 0.1 collective-permute-start.3
  13.6 2.1 %collective-permute-done.4.refs_2_ = bf16[256,512]{1,0:T(8,128)(2,1)S(1)} collective-permute-done((bf16[256,512]{1,0:T(8,128)(2,1)S(1)}, bf16[256,512]{1,0:T(8,128)(2,1)S(1)}, u32[]{:S(2)}, u32[]{:S(2)}) %collective-permute-start.4) | collective-permute-done | bytes 262176 | tf_op jit(solution)/shard_map/ppermute | solution.py:210
  15.8 0.4 project.3
  16.2 0.1 collective-permute-start.5
  16.3 1.3 %collective-permute-done.5.refs_1_.refs_4_.refs_5_ = bf16[512,128]{1,0:T(8,128)(2,1)S(1)} collective-permute-done((bf16[512,128]{1,0:T(8,128)(2,1)S(1)}, bf16[512,128]{1,0:T(8,128)(2,1)S(1)}, u32[]{:S(2)}, u32[]{:S(2)}) %collective-permute-start.5) | collective-permute-done | bytes 131104 | tf_op jit(solution)/shard_map/ppermute | solution.py:214
  17.6 0.0 collective-permute-done.1.refs_1_.refs_5_
  17.6 0.4 collective-permute-done.2.refs_2_.refs_6_
  18.0 2.4 %collective-permute-done.3.refs_3_.refs_7_ = bf16[528,128]{1,0:T(8,128)(2,1)S(1)} collective-permute-done((bf16[528,128]{1,0:T(8,128)(2,1)S(1)}, bf16[528,128]{1,0:T(8,128)(2,1)S(1)}, u32[]{:S(2)}, u32[]{:S(2)}) %collective-permute-start.3) | collective-permute-done | bytes 135200 | tf_op jit(solution)/shard_map/ppermute | solution.py:214
  20.4 0.1 halo.3
  20.5 1.7 %collective-permute-start.10 = (bf16[1584,128]{1,0:T(8,128)(2,1)S(1)}, bf16[1584,128]{1,0:T(8,128)(2,1)S(1)}, u32[]{:S(2)}, u32[]{:S(2)}) collective-permute-start(bf16[1584,128]{1,0:T(8,128)(2,1)S(1)} %get-tuple-element.49), channel_id=1, source_target_pairs={{0,8},{2,10},{4,12},{6,14},{8,0},{10,2},{12,4},{14,6},{16,24},{18,... | collective-permute-start | bytes 1216520 | tf_op jit(solution)/shard_map/ppermute | solution.py:233
  22.2 0.7 %collective-permute-start.11 = (bf16[1584,128]{1,0:T(8,128)(2,1)S(1)}, bf16[1584,128]{1,0:T(8,128)(2,1)S(1)}, u32[]{:S(2)}, u32[]{:S(2)}) collective-permute-start(bf16[1584,128]{1,0:T(8,128)(2,1)S(1)} %get-tuple-element.50), channel_id=1, source_target_pairs={{0,0},{2,2},{4,4},{6,6},{8,16},{10,18},{12,20},{14,22},{16,8},{18,... | collective-permute-start | bytes 1216520 | tf_op jit(solution)/shard_map/ppermute | solution.py:233
  22.9 1.6 %collective-permute-start.6 = (bf16[512,128]{1,0:T(8,128)(2,1)S(1)}, bf16[512,128]{1,0:T(8,128)(2,1)S(1)}, u32[]{:S(2)}, u32[]{:S(2)}) collective-permute-start(bf16[512,128]{1,0:T(8,128)(2,1)S(1)} %get-tuple-element.45), channel_id=1, source_target_pairs={{0,4},{2,6},{4,0},{6,2},{8,12},{10,14},{12,8},{14,10},{16,20},{18,... | collective-permute-start | bytes 393224 | tf_op jit(solution)/shard_map/ppermute | solution.py:214
  24.4 0.0 collective-permute-start.7
  24.5 4.8 %collective-permute-done.6.refs_2_.refs_6_ = bf16[512,128]{1,0:T(8,128)(2,1)S(1)} collective-permute-done((bf16[512,128]{1,0:T(8,128)(2,1)S(1)}, bf16[512,128]{1,0:T(8,128)(2,1)S(1)}, u32[]{:S(2)}, u32[]{:S(2)}) %collective-permute-start.6) | collective-permute-done | bytes 131104 | tf_op jit(solution)/shard_map/ppermute | solution.py:214
  29.3 1.0 %collective-permute-done.7.refs_3_.refs_7_ = bf16[512,128]{1,0:T(8,128)(2,1)S(1)} collective-permute-done((bf16[512,128]{1,0:T(8,128)(2,1)S(1)}, bf16[512,128]{1,0:T(8,128)(2,1)S(1)}, u32[]{:S(2)}, u32[]{:S(2)}) %collective-permute-start.7) | collective-permute-done | bytes 131104 | tf_op jit(solution)/shard_map/ppermute | solution.py:214
  30.2 0.1 halo.2
  30.3 4.4 %collective-permute-start.8 = (bf16[1536,128]{1,0:T(8,128)(2,1)S(1)}, bf16[1536,128]{1,0:T(8,128)(2,1)S(1)}, u32[]{:S(2)}, u32[]{:S(2)}) collective-permute-start(bf16[1536,128]{1,0:T(8,128)(2,1)S(1)} %get-tuple-element.47), channel_id=1, source_target_pairs={{0,8},{2,10},{4,12},{6,14},{8,0},{10,2},{12,4},{14,6},{16,24},{18,... | collective-permute-start | bytes 1179656 | tf_op jit(solution)/shard_map/ppermute | solution.py:233
  34.8 0.7 %collective-permute-start.9 = (bf16[1536,128]{1,0:T(8,128)(2,1)S(1)}, bf16[1536,128]{1,0:T(8,128)(2,1)S(1)}, u32[]{:S(2)}, u32[]{:S(2)}) collective-permute-start(bf16[1536,128]{1,0:T(8,128)(2,1)S(1)} %get-tuple-element.48), channel_id=1, source_target_pairs={{0,0},{2,2},{4,4},{6,6},{8,16},{10,18},{12,20},{14,22},{16,8},{18,... | collective-permute-start | bytes 1179656 | tf_op jit(solution)/shard_map/ppermute | solution.py:233
  35.4 0.0 collective-permute-done.10.refs_8_
  35.5 0.0 collective-permute-done.11.refs_9_
  35.5 9.9 %attend.2 = (bf16[256,128]{1,0:T(8,128)(2,1)S(1)}, bf16[256,128]{1,0:T(8,128)(2,1)S(1)}, bf16[256,128]{1,0:T(8,128)(2,1)S(1)}, bf16[256,128]{1,0:T(8,128)(2,1)S(1)}, bf16[2560,128]{1,0:T(8,128)(2,1)S(1)}) custom-call(bf16[512,128]{1,0:T(8,128)(2,1)S(1)} %get-tuple-element.43.refs_0_.refs_4_, ...), custom_call_target="tpu_custom_call" | custom-call | flops 7516192768 | bytes 2621440 | tf_op jit(solution)/shard_map/attend/pallas_call | solution.py:252
  45.3 0.5 collective-permute-start.15
  45.9 1.5 %collective-permute-start.16 = (bf16[256,128]{1,0:T(8,128)(2,1)S(1)}, bf16[256,128]{1,0:T(8,128)(2,1)S(1)}, u32[]{:S(2)}, u32[]{:S(2)}) collective-permute-start(bf16[256,128]{1,0:T(8,128)(2,1)S(1)} %get-tuple-element.58), channel_id=1, source_target_pairs={{0,4},{2,6},{4,0},{6,2},{8,12},{10,14},{12,8},{14,10},{16,20},{18,... | collective-permute-start | bytes 196616 | tf_op jit(solution)/shard_map/ppermute | solution.py:214
  47.4 0.0 collective-permute-start.17
  47.4 0.0 collective-permute-done.8.refs_8_
  47.4 0.0 collective-permute-done.9.refs_9_
  47.4 9.7 %attend.3 = (bf16[256,128]{1,0:T(8,128)(2,1)S(1)}, bf16[256,128]{1,0:T(8,128)(2,1)S(1)}, bf16[256,128]{1,0:T(8,128)(2,1)S(1)}, bf16[256,128]{1,0:T(8,128)(2,1)S(1)}) custom-call(bf16[528,128]{1,0:T(8,128)(2,1)S(1)} %get-tuple-element.35.refs_0_.refs_4_, bf16[528,128]{1,0:T(8,128)(2,1)S(1)} %collective-permute-done.1.refs_1_.refs_5_, ...), custom_call_target="tpu_custom_call" | custom-call | flops 7516192768 | bytes 2621440 | tf_op jit(solution)/shard_map/attend/pallas_call | solution.py:252
  57.1 0.7 %collective-permute-start.12 = (bf16[256,128]{1,0:T(8,128)(2,1)S(1)}, bf16[256,128]{1,0:T(8,128)(2,1)S(1)}, u32[]{:S(2)}, u32[]{:S(2)}) collective-permute-start(bf16[256,128]{1,0:T(8,128)(2,1)S(1)} %get-tuple-element.53), channel_id=1, source_target_pairs={{0,2},{2,0},{4,6},{6,4},{8,10},{10,8},{12,14},{14,12},{16,18},{18,... | collective-permute-start | bytes 196616 | tf_op jit(solution)/shard_map/ppermute | solution.py:214
  57.8 1.5 %collective-permute-start.13 = (bf16[256,128]{1,0:T(8,128)(2,1)S(1)}, bf16[256,128]{1,0:T(8,128)(2,1)S(1)}, u32[]{:S(2)}, u32[]{:S(2)}) collective-permute-start(bf16[256,128]{1,0:T(8,128)(2,1)S(1)} %get-tuple-element.54), channel_id=1, source_target_pairs={{0,4},{2,6},{4,0},{6,2},{8,12},{10,14},{12,8},{14,10},{16,20},{18,... | collective-permute-start | bytes 196616 | tf_op jit(solution)/shard_map/ppermute | solution.py:214
  59.3 0.0 collective-permute-done.15.refs_1_
  59.3 0.0 collective-permute-start.14
  59.3 0.0 collective-permute-done.16.refs_2_
  59.3 0.0 collective-permute-done.17.refs_3_
  59.3 0.8 %join.3 = bf16[256,512]{1,0:T(8,128)(2,1)} custom-call(bf16[256,128]{1,0:T(8,128)(2,1)S(1)} %get-tuple-element.56.refs_0_, bf16[256,128]{1,0:T(8,128)(2,1)S(1)} %collective-permute-done.15.refs_1_, bf16[256,128]{1,0:T(8,128)(2,1)S(1)} %collective-permute-done.16.refs_2_, bf16[256,128]{1,0:T(8,128)(2,1)S(1)} %collective-permute-done.17.refs_3_), custom_call_target="tpu_custom_call" | custom-call | bytes 524288 | tf_op jit(solution)/shard_map/join/pallas_call | solution.py:268
  60.1 0.0 collective-permute-done.12.refs_1_
  60.1 2.0 %collective-permute-done.13.refs_2_ = bf16[256,128]{1,0:T(8,128)(2,1)S(1)} collective-permute-done((bf16[256,128]{1,0:T(8,128)(2,1)S(1)}, bf16[256,128]{1,0:T(8,128)(2,1)S(1)}, u32[]{:S(2)}, u32[]{:S(2)}) %collective-permute-start.13) | collective-permute-done | bytes 65568 | tf_op jit(solution)/shard_map/ppermute | solution.py:214
  62.0 1.6 %collective-permute-done.14.refs_3_ = bf16[256,128]{1,0:T(8,128)(2,1)S(1)} collective-permute-done((bf16[256,128]{1,0:T(8,128)(2,1)S(1)}, bf16[256,128]{1,0:T(8,128)(2,1)S(1)}, u32[]{:S(2)}, u32[]{:S(2)}) %collective-permute-start.14) | collective-permute-done | bytes 65568 | tf_op jit(solution)/shard_map/ppermute | solution.py:214
  63.6 0.8 %join.2 = bf16[256,512]{1,0:T(8,128)(2,1)} custom-call(bf16[256,128]{1,0:T(8,128)(2,1)S(1)} %get-tuple-element.52.refs_0_, bf16[256,128]{1,0:T(8,128)(2,1)S(1)} %collective-permute-done.12.refs_1_, bf16[256,128]{1,0:T(8,128)(2,1)S(1)} %collective-permute-done.13.refs_2_, bf16[256,128]{1,0:T(8,128)(2,1)S(1)} %collective-permute-done.14.refs_3_), custom_call_target="tpu_custom_call" | custom-call | bytes 524288 | tf_op jit(solution)/shard_map/join/pallas_call | solution.py:268
Async XLA Ops:
  0.6 10.4 %collective-permute-start = (bf16[256,512]{1,0:T(8,128)(2,1)}, bf16[256,512]{1,0:T(8,128)(2,1)S(1)}, u32[]{:S(2)}, u32[]{:S(2)}) collective-permute-start(bf16[256,512]{1,0:T(8,128)(2,1)} %audio.1), channel_id=1, source_target_pairs={{0,1},{1,0},{2,3},{3,2},{4,5},{5,4},{6,7},{7,6},{8,9},{9,8},{10,11... | collective-permute-start | bytes 786440 | tf_op jit(solution)/shard_map/ppermute | solution.py:210
  5.6 10.2 %collective-permute-start.4 = (bf16[256,512]{1,0:T(8,128)(2,1)S(1)}, bf16[256,512]{1,0:T(8,128)(2,1)S(1)}, u32[]{:S(2)}, u32[]{:S(2)}) collective-permute-start(bf16[256,512]{1,0:T(8,128)(2,1)S(1)} %get-tuple-element.41), channel_id=1, source_target_pairs={{0,1},{1,0},{2,3},{3,2},{4,5},{5,4},{6,7},{7,6},{8,9},{9,8},{10,11... | collective-permute-start | bytes 786440 | tf_op jit(solution)/shard_map/ppermute | solution.py:210
  11.4 6.2 %collective-permute-start.1 = (bf16[528,128]{1,0:T(8,128)(2,1)S(1)}, bf16[528,128]{1,0:T(8,128)(2,1)S(1)}, u32[]{:S(2)}, u32[]{:S(2)}) collective-permute-start(bf16[528,128]{1,0:T(8,128)(2,1)S(1)} %get-tuple-element.36), channel_id=1, source_target_pairs={{0,2},{2,0},{4,6},{6,4},{8,10},{10,8},{12,14},{14,12},{16,18},{18,... | collective-permute-start | bytes 405512 | tf_op jit(solution)/shard_map/ppermute | solution.py:214
  11.5 6.5 %collective-permute-start.2 = (bf16[528,128]{1,0:T(8,128)(2,1)S(1)}, bf16[528,128]{1,0:T(8,128)(2,1)S(1)}, u32[]{:S(2)}, u32[]{:S(2)}) collective-permute-start(bf16[528,128]{1,0:T(8,128)(2,1)S(1)} %get-tuple-element.37), channel_id=1, source_target_pairs={{0,4},{2,6},{4,0},{6,2},{8,12},{10,14},{12,8},{14,10},{16,20},{18,... | collective-permute-start | bytes 405512 | tf_op jit(solution)/shard_map/ppermute | solution.py:214
  13.6 6.8 %collective-permute-start.3 = (bf16[528,128]{1,0:T(8,128)(2,1)S(1)}, bf16[528,128]{1,0:T(8,128)(2,1)S(1)}, u32[]{:S(2)}, u32[]{:S(2)}) collective-permute-start(bf16[528,128]{1,0:T(8,128)(2,1)S(1)} %get-tuple-element.38), channel_id=1, source_target_pairs={{0,6},{2,4},{4,2},{6,0},{8,14},{10,12},{12,10},{14,8},{16,22},{18,... | collective-permute-start | bytes 405512 | tf_op jit(solution)/shard_map/ppermute | solution.py:214
  16.2 1.4 %collective-permute-start.5 = (bf16[512,128]{1,0:T(8,128)(2,1)S(1)}, bf16[512,128]{1,0:T(8,128)(2,1)S(1)}, u32[]{:S(2)}, u32[]{:S(2)}) collective-permute-start(bf16[512,128]{1,0:T(8,128)(2,1)S(1)} %get-tuple-element.44), channel_id=1, source_target_pairs={{0,2},{2,0},{4,6},{6,4},{8,10},{10,8},{12,14},{14,12},{16,18},{18,... | collective-permute-start | bytes 393224 | tf_op jit(solution)/shard_map/ppermute | solution.py:214
  20.5 15.0 %collective-permute-start.10 = (bf16[1584,128]{1,0:T(8,128)(2,1)S(1)}, bf16[1584,128]{1,0:T(8,128)(2,1)S(1)}, u32[]{:S(2)}, u32[]{:S(2)}) collective-permute-start(bf16[1584,128]{1,0:T(8,128)(2,1)S(1)} %get-tuple-element.49), channel_id=1, source_target_pairs={{0,8},{2,10},{4,12},{6,14},{8,0},{10,2},{12,4},{14,6},{16,24},{18,... | collective-permute-start | bytes 1216520 | tf_op jit(solution)/shard_map/ppermute | solution.py:233
  22.2 13.3 %collective-permute-start.11 = (bf16[1584,128]{1,0:T(8,128)(2,1)S(1)}, bf16[1584,128]{1,0:T(8,128)(2,1)S(1)}, u32[]{:S(2)}, u32[]{:S(2)}) collective-permute-start(bf16[1584,128]{1,0:T(8,128)(2,1)S(1)} %get-tuple-element.50), channel_id=1, source_target_pairs={{0,0},{2,2},{4,4},{6,6},{8,16},{10,18},{12,20},{14,22},{16,8},{18,... | collective-permute-start | bytes 1216520 | tf_op jit(solution)/shard_map/ppermute | solution.py:233
  22.9 6.4 %collective-permute-start.6 = (bf16[512,128]{1,0:T(8,128)(2,1)S(1)}, bf16[512,128]{1,0:T(8,128)(2,1)S(1)}, u32[]{:S(2)}, u32[]{:S(2)}) collective-permute-start(bf16[512,128]{1,0:T(8,128)(2,1)S(1)} %get-tuple-element.45), channel_id=1, source_target_pairs={{0,4},{2,6},{4,0},{6,2},{8,12},{10,14},{12,8},{14,10},{16,20},{18,... | collective-permute-start | bytes 393224 | tf_op jit(solution)/shard_map/ppermute | solution.py:214
  24.4 5.8 %collective-permute-start.7 = (bf16[512,128]{1,0:T(8,128)(2,1)S(1)}, bf16[512,128]{1,0:T(8,128)(2,1)S(1)}, u32[]{:S(2)}, u32[]{:S(2)}) collective-permute-start(bf16[512,128]{1,0:T(8,128)(2,1)S(1)} %get-tuple-element.46), channel_id=1, source_target_pairs={{0,6},{2,4},{4,2},{6,0},{8,14},{10,12},{12,10},{14,8},{16,22},{18,... | collective-permute-start | bytes 393224 | tf_op jit(solution)/shard_map/ppermute | solution.py:214
  30.3 17.1 %collective-permute-start.8 = (bf16[1536,128]{1,0:T(8,128)(2,1)S(1)}, bf16[1536,128]{1,0:T(8,128)(2,1)S(1)}, u32[]{:S(2)}, u32[]{:S(2)}) collective-permute-start(bf16[1536,128]{1,0:T(8,128)(2,1)S(1)} %get-tuple-element.47), channel_id=1, source_target_pairs={{0,8},{2,10},{4,12},{6,14},{8,0},{10,2},{12,4},{14,6},{16,24},{18,... | collective-permute-start | bytes 1179656 | tf_op jit(solution)/shard_map/ppermute | solution.py:233
  34.8 12.6 %collective-permute-start.9 = (bf16[1536,128]{1,0:T(8,128)(2,1)S(1)}, bf16[1536,128]{1,0:T(8,128)(2,1)S(1)}, u32[]{:S(2)}, u32[]{:S(2)}) collective-permute-start(bf16[1536,128]{1,0:T(8,128)(2,1)S(1)} %get-tuple-element.48), channel_id=1, source_target_pairs={{0,0},{2,2},{4,4},{6,6},{8,16},{10,18},{12,20},{14,22},{16,8},{18,... | collective-permute-start | bytes 1179656 | tf_op jit(solution)/shard_map/ppermute | solution.py:233
  45.3 13.9 %collective-permute-start.15 = (bf16[256,128]{1,0:T(8,128)(2,1)S(1)}, bf16[256,128]{1,0:T(8,128)(2,1)S(1)}, u32[]{:S(2)}, u32[]{:S(2)}) collective-permute-start(bf16[256,128]{1,0:T(8,128)(2,1)S(1)} %get-tuple-element.57), channel_id=1, source_target_pairs={{0,2},{2,0},{4,6},{6,4},{8,10},{10,8},{12,14},{14,12},{16,18},{18,... | collective-permute-start | bytes 196616 | tf_op jit(solution)/shard_map/ppermute | solution.py:214
  45.9 13.4 %collective-permute-start.16 = (bf16[256,128]{1,0:T(8,128)(2,1)S(1)}, bf16[256,128]{1,0:T(8,128)(2,1)S(1)}, u32[]{:S(2)}, u32[]{:S(2)}) collective-permute-start(bf16[256,128]{1,0:T(8,128)(2,1)S(1)} %get-tuple-element.58), channel_id=1, source_target_pairs={{0,4},{2,6},{4,0},{6,2},{8,12},{10,14},{12,8},{14,10},{16,20},{18,... | collective-permute-start | bytes 196616 | tf_op jit(solution)/shard_map/ppermute | solution.py:214
  47.4 11.9 %collective-permute-start.17 = (bf16[256,128]{1,0:T(8,128)(2,1)S(1)}, bf16[256,128]{1,0:T(8,128)(2,1)S(1)}, u32[]{:S(2)}, u32[]{:S(2)}) collective-permute-start(bf16[256,128]{1,0:T(8,128)(2,1)S(1)} %get-tuple-element.59), channel_id=1, source_target_pairs={{0,6},{2,4},{4,2},{6,0},{8,14},{10,12},{12,10},{14,8},{16,22},{18,... | collective-permute-start | bytes 196616 | tf_op jit(solution)/shard_map/ppermute | solution.py:214
  57.1 3.0 %collective-permute-start.12 = (bf16[256,128]{1,0:T(8,128)(2,1)S(1)}, bf16[256,128]{1,0:T(8,128)(2,1)S(1)}, u32[]{:S(2)}, u32[]{:S(2)}) collective-permute-start(bf16[256,128]{1,0:T(8,128)(2,1)S(1)} %get-tuple-element.53), channel_id=1, source_target_pairs={{0,2},{2,0},{4,6},{6,4},{8,10},{10,8},{12,14},{14,12},{16,18},{18,... | collective-permute-start | bytes 196616 | tf_op jit(solution)/shard_map/ppermute | solution.py:214
  57.8 4.3 %collective-permute-start.13 = (bf16[256,128]{1,0:T(8,128)(2,1)S(1)}, bf16[256,128]{1,0:T(8,128)(2,1)S(1)}, u32[]{:S(2)}, u32[]{:S(2)}) collective-permute-start(bf16[256,128]{1,0:T(8,128)(2,1)S(1)} %get-tuple-element.54), channel_id=1, source_target_pairs={{0,4},{2,6},{4,0},{6,2},{8,12},{10,14},{12,8},{14,10},{16,20},{18,... | collective-permute-start | bytes 196616 | tf_op jit(solution)/shard_map/ppermute | solution.py:214
  59.3 4.4 %collective-permute-start.14 = (bf16[256,128]{1,0:T(8,128)(2,1)S(1)}, bf16[256,128]{1,0:T(8,128)(2,1)S(1)}, u32[]{:S(2)}, u32[]{:S(2)}) collective-permute-start(bf16[256,128]{1,0:T(8,128)(2,1)S(1)} %get-tuple-element.55), channel_id=1, source_target_pairs={{0,6},{2,4},{4,2},{6,0},{8,14},{10,12},{12,10},{14,8},{16,22},{18,... | collective-permute-start | bytes 196616 | tf_op jit(solution)/shard_map/ppermute | solution.py:214

commit v4 on v3

v4 whole, which is shorter than its diff:
```python
import functools

import jax
import jax.numpy as jnp
from jax import lax
from jax.experimental import pallas as pl
from jax.experimental.pallas import tpu as pltpu
from jax.sharding import PartitionSpec as P

HEAD = 64
RADIUS = 3
GROUP = 4
NEG = -1e30
ID_ROWS = 16

VMEM = pl.BlockSpec(memory_space=pltpu.VMEM)
ANY = pl.BlockSpec(memory_space=pl.ANY)
HBM = pl.BlockSpec(memory_space=pltpu.HBM)


def plane():
    return lax.axis_index("tm") // GROUP


def call(kernel, outs, scratch=(), ins=None, flops=0, moved=0, exps=0, name=None):
    return pl.pallas_call(
        kernel,
        out_shape=outs,
        **({"in_specs": ins} if ins else {}),
        scratch_shapes=scratch,
        compiler_params=pltpu.CompilerParams(vmem_limit_bytes=48 * 2**20),
        cost_estimate=pl.CostEstimate(flops=flops, bytes_accessed=moved, transcendentals=exps),
        name=name,
    )


def prepare_kernel(audio, video, query, key, ids, *refs):
    sent, sums, seconds, packs = refs[0], refs[1:3], refs[3:5], refs[5]
    own, firsts, ids_in, ids_wide, sems = refs[6], refs[7:9], refs[9], refs[10], refs[11]
    rows, half = audio.shape
    width = packs.shape[2]
    side = lax.axis_index("head")
    copies = []

    def fetch(source, target):
        copies.append(pltpu.make_async_copy(source, target, sems.at[len(copies)]))
        copies[-1].start()
        return copies[-1]

    streams = (own, sent)
    loads = [fetch(audio, own), fetch(video, sent)]
    ours = pl.ds(pl.multiple_of(side * half, half), half)
    theirs = pl.ds(pl.multiple_of((1 - side) * half, half), half)
    weights = [fetch(w.at[ours], f) for w, f in zip((query, key), firsts)]
    others = [fetch(w.at[theirs], f) for w, f in zip((query, key), seconds)]
    others.append(fetch(ids, ids_in))
    for i in range(2):
        loads[i].wait()
        for k in range(GROUP):
            for at in range(0, rows, width):
                square = streams[i][at : at + width, k * width : (k + 1) * width]
                packs[k, i * rows + at : i * rows + at + width] = jnp.transpose(square)
    for i in range(2):
        weights[i].wait()
        sums[i][...] = jnp.dot(
            streams[i][...], firsts[i][...], preferred_element_type=jnp.float32
        )
    for copy in others:
        copy.wait()
    ids_wide[...] = jnp.zeros_like(ids_wide)
    ids_wide[: ids_in.shape[0]] = (ids_in[...] + 1).astype(jnp.float32)
    for k in range(GROUP):
        packs[k, 2 * rows :] = ids_wide[...].astype(packs.dtype)


def project_kernel(scale, part, other, weight, *refs):
    out = refs[-1]
    total = part[...] + jnp.dot(other[...], weight[...], preferred_element_type=jnp.float32)
    rounded = total.astype(jnp.bfloat16)
    rounded = rounded * jnp.bfloat16(scale) if scale != 1.0 else rounded
    rows, width = other.shape[0], out.shape[2]
    before = refs[0] if len(refs) == 2 else None
    for k in range(GROUP):
        if before is None:
            out[k] = rounded[:, k * width : (k + 1) * width]
        else:
            out[k, :rows] = before[k]
            out[k, rows:] = rounded[:, k * width : (k + 1) * width]


def halo_kernel(has_ids, pieces, first, second):
    odd = lax.rem(plane(), 2)
    first[...] = pieces[pl.ds((GROUP - RADIUS) * (1 - odd), RADIUS)]
    second[...] = pieces[pl.ds((GROUP - RADIUS) * odd, RADIUS)]
    if has_ids:
        last = lax.axis_size("tm") // GROUP - 1

        @pl.when((plane() == 0) | (plane() == last))
        def _():
            second[:, second.shape[1] - ID_ROWS :] = jnp.zeros(
                (RADIUS, ID_ROWS, second.shape[2]), second.dtype
            )


def join_kernel(pieces, *outs):
    width = pieces.shape[2]
    rows = outs[0].shape[0]
    for i, out in enumerate(outs):
        for k in range(GROUP):
            out[:, k * width : (k + 1) * width] = pieces[k, i * rows : (i + 1) * rows]


def mark(pack, rows, width, put):
    lanes = pack[2 * rows :].astype(jnp.float32)
    lane = lax.broadcasted_iota(jnp.int32, (width, width), 1).astype(jnp.float32)
    for at in range(0, rows, width):
        ids = lanes[at // width : at // width + 1]
        column = jnp.transpose(jnp.broadcast_to(ids, (width, width)))
        put(at, jnp.where(column == lane, 1.0, 0.0).astype(jnp.bfloat16))


def fold(parts, combine):
    parts = list(parts)
    while len(parts) > 1:
        pairs = [combine(a, b) for a, b in zip(parts[::2], parts[1::2])]
        parts = pairs + ([parts[-1]] if len(parts) % 2 else [])
    x = parts[0]
    while x.shape[0] > 8:
        middle = x.shape[0] // 2
        x = combine(x[:middle], x[middle:])
    return x


def chunk_scores(ask, key_at, count):
    return [
        lax.dot_general(
            key_at(c), ask, (((1,), (1,)), ((), ())), preferred_element_type=jnp.float32
        )
        for c in range(count)
    ]


def peak_of(scores):
    return jnp.max(fold(scores, jnp.maximum), axis=0, keepdims=True)


def weigh(scores, peak, value_at):
    weights = [jnp.exp(s - peak) for s in scores]
    total = jnp.sum(fold(weights, jnp.add), axis=0, keepdims=True)
    mixed = sum(
        jnp.dot(value_at(c), w.astype(jnp.bfloat16), preferred_element_type=jnp.float32)
        for c, w in enumerate(weights)
    )
    return total, mixed


def asks(block, width, forbid):
    lane = lax.broadcasted_iota(jnp.int32, block.shape, 1)
    return [
        jnp.concatenate([jnp.where(lane // HEAD == h, block, jnp.zeros_like(block)), forbid], axis=1)
        for h in range(width // HEAD)
    ]


def plane_kernel(values, projected, peaks, totals, sums, forbids, keys, turned):
    rows = forbids.shape[1]
    width = values.shape[2]
    for b in range(GROUP):
        at = slice(b * rows, (b + 1) * rows)

        def put(spot, marks):
            for i in range(2):
                keys[i, b * rows + spot : b * rows + spot + width, width:] = marks
            forbids[b, spot : spot + width] = (marks - jnp.bfloat16(1.0)) * jnp.bfloat16(-NEG)

        mark(values[b], rows, width, put)
        for i in range(2):
            keys[i, at, :width] = projected[b, (1 - i) * rows : (2 - i) * rows]
            for spot in range(0, rows, width):
                turned[i, :, b * rows + spot : b * rows + spot + width] = values[
                    b, (1 - i) * rows + spot : (1 - i) * rows + spot + width
                ]

    def one(b, _):
        for i in range(2):
            block = projected[b, i * rows : (i + 1) * rows]
            for h, ask in enumerate(asks(block, width, forbids[b])):
                scores = chunk_scores(ask, lambda c: keys[i, c * rows : (c + 1) * rows], GROUP)
                peak = peak_of(scores)
                lanes = slice(h * HEAD, (h + 1) * HEAD)
                total, mixed = weigh(
                    scores, peak, lambda c: turned[i, lanes, c * rows : (c + 1) * rows]
                )
                peaks[i, b, h : h + 1] = peak
                totals[i, b, h : h + 1] = total
                sums[i, b, lanes] = mixed
        return _

    lax.fori_loop(0, GROUP, one, 0)


def edge_kernel(projected, peaks, totals, sums, forbids, *refs):
    value_edges, projected_edges, out, keys, turned = refs[:2], refs[2:4], refs[4], refs[5], refs[6]
    rows = forbids.shape[1]
    width = projected.shape[2]
    odd = lax.rem(plane(), 2)
    for edge in range(2):
        base = RADIUS * (odd if edge else 1 - odd)
        for j in range(RADIUS):

            def spot_at(at, size):
                return pl.ds(pl.multiple_of((base + j) * rows + at, size), size)

            def put(at, marks):
                for i in range(2):
                    keys[i, spot_at(at, width), width:] = marks

            mark(value_edges[edge][j], rows, width, put)
            for i in range(2):
                keys[i, spot_at(0, rows), :width] = projected_edges[edge][
                    j, (1 - i) * rows : (2 - i) * rows
                ]
                for at in range(0, rows, width):
                    turned[i, :, spot_at(at, width)] = value_edges[edge][
                        j, (1 - i) * rows + at : (1 - i) * rows + at + width
                    ]

    def one(b, _):
        def near(c):
            return pl.ds(pl.multiple_of((b + c) * rows, rows), rows)

        for i in range(2):
            block = projected[b, i * rows : (i + 1) * rows]
            results = []
            for h, ask in enumerate(asks(block, width, forbids[b])):
                scores = chunk_scores(ask, lambda c: keys[i, near(c)], RADIUS)
                old = peaks[i, b, h : h + 1]
                peak = jnp.maximum(old, peak_of(scores))
                lanes = slice(h * HEAD, (h + 1) * HEAD)
                total, mixed = weigh(scores, peak, lambda c: turned[i, lanes, near(c)])
                factor = jnp.exp(old - peak)
                total += totals[i, b, h : h + 1] * factor
                results.append((mixed + sums[i, b, lanes] * factor) / total)
            out[b, i * rows : (i + 1) * rows] = jnp.transpose(
                jnp.concatenate(results, axis=0)
            ).astype(out.dtype)
        return _

    lax.fori_loop(0, GROUP, one, 0)


def local(audio_frames, video_frames, recording, audio_query, video_key):
    rows, half = audio_frames.shape
    width = half // GROUP
    heads = width // HEAD
    length = lax.axis_size("tm")
    bf16, f32 = jnp.bfloat16, jnp.float32
    shape = jax.ShapeDtypeStruct
    assert length % (2 * GROUP) == 0

    def swapped(x):
        return lax.ppermute(x, "head", [(0, 1), (1, 0)])

    def traded(pieces):
        groups = [list(range(i, i + GROUP)) for i in range(0, length, GROUP)]
        return lax.all_to_all(pieces, "tm", 0, 0, axis_index_groups=groups)

    def halo(pieces, has_ids, after=()):
        size = pieces.shape[1]
        edge = shape((RADIUS, size, width), bf16)

        def kernel(pieces, *refs):
            halo_kernel(has_ids, pieces, *refs[-2:])

        sent = call(
            kernel,
            [edge, edge],
            ins=[VMEM] + [ANY] * len(after),
            moved=10 * size * width * 2,
            name="halo",
        )(pieces, *after)

        def partner(i, second):
            spot, inside = divmod(i, GROUP)
            spot = ((spot + second) ^ 1) - second
            return min(max(spot, 0), length // GROUP - 1) * GROUP + inside

        return [
            lax.ppermute(sent[s], "tm", [(i, partner(i, s)) for i in range(length)])
            for s in range(2)
        ]

    def project(part, other, weight, scale, *before):
        return call(
            functools.partial(project_kernel, scale),
            shape((GROUP, (1 + len(before)) * rows, width), bf16),
            flops=2 * rows * half * half,
            moved=half * half * 2 + 4 * rows * half * 2,
            name="project",
        )(part, other, weight, *before)

    other_audio = swapped(audio_frames)
    part = shape((rows, half), f32)
    square = shape((half, half), bf16)
    given = (audio_frames, video_frames, audio_query, video_key, recording.reshape(rows // width, width))
    video_copy, query_part, key_part, query_rest, key_rest, values = call(
        prepare_kernel,
        [shape((rows, half), bf16), part, part, square, square]
        + [shape((GROUP, 2 * rows + ID_ROWS, width), bf16)],
        [pltpu.VMEM((rows, half), bf16)]
        + [pltpu.VMEM((half, half), bf16)] * 2
        + [pltpu.VMEM((rows // width, width), jnp.int32), pltpu.VMEM((ID_ROWS, width), f32)]
        + [pltpu.SemaphoreType.DMA((7,))],
        ins=[HBM] * 5,
        flops=4 * rows * half * half,
        moved=16 * half * half,
        name="prepare",
    )(*(pltpu.with_memory_space_constraint(x, pltpu.HBM) for x in given))
    other_video = swapped(video_copy)
    values = traded(values)
    value_edges = halo(values, True)
    queries = project(query_part, other_audio, query_rest, HEAD**-0.5)
    projected = traded(project(key_part, other_video, key_rest, 1.0, queries))
    projected_edges = halo(projected, False)

    stat = shape((2, GROUP, heads, rows), f32)
    sums = shape((2, GROUP, width, rows), f32)
    inside, around = GROUP * rows, 2 * RADIUS * rows
    state = call(
        plane_kernel,
        [stat, stat, sums, shape((GROUP, rows, width), bf16)],
        [pltpu.VMEM((2, inside, 2 * width), bf16), pltpu.VMEM((2, width, inside), bf16)],
        flops=16 * GROUP * rows * inside * width,
        moved=8 * inside * width * 2,
        exps=4 * GROUP * rows * inside,
        name="plane",
    )(values, projected)
    pieces = call(
        edge_kernel,
        shape((GROUP, 2 * rows, width), bf16),
        [pltpu.VMEM((2, around, 2 * width), bf16), pltpu.VMEM((2, width, around), bf16)],
        flops=16 * GROUP * rows * RADIUS * rows * width,
        moved=8 * around * width * 2,
        exps=4 * GROUP * rows * RADIUS * rows,
        name="edge",
    )(projected, *state, *value_edges, *projected_edges)
    out = shape((rows, half), bf16)
    return tuple(
        call(join_kernel, [out, out], moved=4 * rows * half * 2, name="join")(traded(pieces))
    )


def solution(mesh):
    return jax.shard_map(
        local,
        mesh=mesh,
        in_specs=(P("tm", "head"), P("tm", "head"), P("tm"), P(None, "head"), P(None, "head")),
        out_specs=(P("tm", "head"), P("tm", "head")),
        check_vma=False,
    )
```

time: 64.6 us -> 71.7 us (1.11)
  the two profiles are of different devices: /device:TPU:0 before, /device:TPU:9 now
where the time goes in v4:
time: 71.7 us; the launch traced here: 71 us
  Pallas kernels  24.4 us (34%)
  starting transfers between devices  19.2 us (27%)
  waiting for transfers between devices  15.1 us (21%)
  blocking collectives  11.6 us (16%)
  between operations  0.74 us (1%)
    ppermute x2, waiting for transfers between devices, swapped(): return lax.ppermute(x, 'head', [(0, 1), (1, 0)])  11.7 us
    all_to_all x1, blocking collectives, traded(): return lax.all_to_all(pieces, 'tm', 0, 0, axis_index_groups=groups)  11.6 us
    pallas_call x1, Pallas kernels, local(): call(plane_kernel, [stat, stat, sums, shape((GROUP, rows, width), bf16)],...  10 us
    pallas_call x1, Pallas kernels, local(): call(edge_kernel, shape((GROUP, 2 * rows, width), bf16), [pltpu.VMEM((2,...  9.31 us
    ppermute x4, starting transfers between devices, halo(): lax.ppermute(sent[s], 'tm', [(i, partner(i, s)) for i in range(length)])  9.09 us
    all_to_all x2, starting transfers between devices, traded(): return lax.all_to_all(pieces, 'tm', 0, 0, axis_index_groups=groups)  8.57 us
    all_to_all x2, waiting for transfers between devices, traded(): return lax.all_to_all(pieces, 'tm', 0, 0, axis_index_groups=groups)  3.36 us
    pallas_call x1, Pallas kernels, local(): call(prepare_kernel, [shape((rows, half), bf16), part, part, square, squa...  2.68 us
  transfers between devices with their start and end apart: 8, of which 3 were waited for; matrix products, arithmetic and copies ran while one was open for 0% of the time, Pallas kernels for 16%

profile of v4, /device:TPU:9, one launch (start us, length us, event | category | flops | bytes accessed | tf_op | source)
XLA Modules:
  0.0 71.0 jit_solution(11150536673436940395)
XLA Ops:
  0.6 2.7 %prepare.1 = (bf16[256,512]{1,0:T(8,128)(2,1)S(1)}, f32[256,512]{1,0:T(8,128)S(1)}, f32[256,512]{1,0:T(8,128)S(1)}, bf16[512,512]{1,0:T(8,128)(2,1)S(1)}, bf16[5...) custom-call(bf16[256,512]{1,0:T(8,128)(2,1)} %audio.1, bf16[256,512]{1,0:T(8,128)(2,1)} %video.1, ...), custom_call_target="tpu_custom_call" | custom-call | flops 268435456 | bytes 4194304 | tf_op jit(solution)/shard_map/prepare/pallas_call | solution.py:306
  3.3 0.0 copy-start
  3.3 4.3 %all-to-all-start.1 = ((bf16[4,528,128]{2,1,0:T(8,128)(2,1)}), bf16[4,528,128]{2,1,0:T(8,128)(2,1)S(1)}, u32[]{:S(2)}, u32[]{:S(2)}) async-start(bf16[4,528,128]{2,1,0:T(8,128)(2,1)} %get-tuple-element.21), calls=%async_computation.1 | async-start | bytes 1081344 | tf_op jit(solution)/shard_map/all_to_all | solution.py:266
  7.6 0.0 copy-done
  7.6 1.3 %collective-permute-start.1 = (bf16[256,512]{1,0:T(8,128)(2,1)S(1)}, bf16[256,512]{1,0:T(8,128)(2,1)S(1)}, u32[]{:S(2)}, u32[]{:S(2)}) collective-permute-start(bf16[256,512]{1,0:T(8,128)(2,1)S(1)} %copy-done), channel_id=1, source_target_pairs={{0,1},{1,0},{2,3},{3,2},{4,5},{5,4},{6,7},{7,6},{8,9},{9,8},{10,11... | collective-permute-start | bytes 786440 | tf_op jit(solution)/shard_map/ppermute | solution.py:262
  8.9 0.2 collective-permute-start
  9.1 6.4 %collective-permute-done.1.other = bf16[256,512]{1,0:T(8,128)(2,1)S(1)} collective-permute-done((bf16[256,512]{1,0:T(8,128)(2,1)S(1)}, bf16[256,512]{1,0:T(8,128)(2,1)S(1)}, u32[]{:S(2)}, u32[]{:S(2)}) %collective-permute-start.1) | collective-permute-done | bytes 262176 | tf_op jit(solution)/shard_map/ppermute | solution.py:262
  15.5 0.3 project.2.refs_0_
  15.8 5.3 %collective-permute-done.other = bf16[256,512]{1,0:T(8,128)(2,1)S(1)} collective-permute-done((bf16[256,512]{1,0:T(8,128)(2,1)S(1)}, bf16[256,512]{1,0:T(8,128)(2,1)S(1)}, u32[]{:S(2)}, u32[]{:S(2)}) %collective-permute-start) | collective-permute-done | bytes 262176 | tf_op jit(solution)/shard_map/ppermute | solution.py:262
  21.1 1.1 %project.3 = bf16[4,512,128]{2,1,0:T(8,128)(2,1)} custom-call(f32[256,512]{1,0:T(8,128)S(1)} %get-tuple-element.16.part, bf16[256,512]{1,0:T(8,128)(2,1)S(1)} %collective-permute-done.other, bf16[512,512]{1,0:T(8,128)(2,1)S(1)} %get-tuple-element.18.weight, bf16[4,256,128]{2,1,0:T(8,128)(2,1)S(1)} %project.2.refs_0_), custom_call_target="tpu_custom_call" | custom-call | flops 134217728 | bytes 1572864 | tf_op jit(solution)/shard_map/project/pallas_call | solution.py:294
  22.2 0.0 all-to-all-done.1.values.pieces
  22.2 4.3 %all-to-all-start = ((bf16[4,512,128]{2,1,0:T(8,128)(2,1)}), bf16[4,512,128]{2,1,0:T(8,128)(2,1)S(1)}, u32[]{:S(2)}, u32[]{:S(2)}) async-start(bf16[4,512,128]{2,1,0:T(8,128)(2,1)} %project.3), calls=%async_computation | async-start | bytes 1048576 | tf_op jit(solution)/shard_map/all_to_all | solution.py:266
  26.5 0.1 halo.2
  26.6 0.1 collective-permute-start.2
  26.6 4.5 %collective-permute-start.3 = (bf16[3,528,128]{2,1,0:T(8,128)(2,1)S(1)}, bf16[3,528,128]{2,1,0:T(8,128)(2,1)S(1)}, u32[]{:S(2)}, u32[]{:S(2)}) collective-permute-start(bf16[3,528,128]{2,1,0:T(8,128)(2,1)S(1)} %get-tuple-element.27), channel_id=1, source_target_pairs={{0,0},{2,2},{4,4},{6,6},{8,16},{10,18},{12,20},{14,22},{16,8},{18,... | collective-permute-start | bytes 1216520 | tf_op jit(solution)/shard_map/ppermute | solution.py:289
  31.1 3.4 %all-to-all-done.projected.pieces = bf16[4,512,128]{2,1,0:T(8,128)(2,1)S(1)} async-done(((bf16[4,512,128]{2,1,0:T(8,128)(2,1)}), bf16[4,512,128]{2,1,0:T(8,128)(2,1)S(1)}, u32[]{:S(2)}, u32[]{:S(2)}) %all-to-all-start) | async-done | bytes 524320 | tf_op jit(solution)/shard_map/all_to_all | solution.py:266
  34.5 0.1 halo.3
  34.5 0.1 collective-permute-start.4
  34.6 4.5 %collective-permute-start.5 = (bf16[3,512,128]{2,1,0:T(8,128)(2,1)S(1)}, bf16[3,512,128]{2,1,0:T(8,128)(2,1)S(1)}, u32[]{:S(2)}, u32[]{:S(2)}) collective-permute-start(bf16[3,512,128]{2,1,0:T(8,128)(2,1)S(1)} %get-tuple-element.29), channel_id=1, source_target_pairs={{0,0},{2,2},{4,4},{6,6},{8,16},{10,18},{12,20},{14,22},{16,8},{18,... | collective-permute-start | bytes 1179656 | tf_op jit(solution)/shard_map/ppermute | solution.py:289
  39.1 10.0 %plane.1 = (f32[2,4,2,256]{3,2,1,0:T(2,128)S(1)}, f32[2,4,2,256]{3,2,1,0:T(2,128)S(1)}, f32[2,4,128,256]{3,2,1,0:T(8,128)S(1)}, bf16[4,256,128]{2,1,0:T(8,128)(2,1)S(1)}) custom-call(bf16[4,528,128]{2,1,0:T(8,128)(2,1)S(1)} %all-to-all-done.1.values.pieces, bf16[4,512,128]{2,1,0:T(8,128)(2,1)S(1)} %all-to-all-done.projected.pieces), custom_call_target="tpu_custom_call" | custom-call | flops 2147483648 | bytes 2097152 | tf_op jit(solution)/shard_map/plane/pallas_call | solution.py:329
  49.1 0.0 collective-permute-done.2.refs_0_
  49.1 0.0 collective-permute-done.3.refs_1_
  49.1 0.0 collective-permute-done.4.refs_2_
  49.2 0.0 collective-permute-done.5.refs_3_
  49.2 9.3 %edge.1 = bf16[4,512,128]{2,1,0:T(8,128)(2,1)S(1)} custom-call(bf16[4,512,128]{2,1,0:T(8,128)(2,1)S(1)} %all-to-all-done.projected.pieces, f32[2,4,2,256]{3,2,1,0:T(2,128)S(1)} %get-tuple-element.22.peaks, f32[2,4,2,256]{3,2,1,0:T(2,128)S(1)} %get-tuple-element.23.totals, f32[2,4,128,256]{3,2,1,0:T(8,128)S(1)} %get-tuple-element.24.sums, ...), custom_call_target="tpu_custom_call" | custom-call | flops 1610612736 | bytes 3145728 | tf_op jit(solution)/shard_map/edge/pallas_call | solution.py:338
  58.5 11.6 %all_to_all.15.pieces = bf16[4,512,128]{2,1,0:T(8,128)(2,1)S(1)} all-to-all(bf16[4,512,128]{2,1,0:T(8,128)(2,1)S(1)} %edge.1), channel_id=1, replica_groups={{0,2,4,6},{8,10,12,14},{16,18,20,22},{24,26,28,30},{1,3,5,7},{9,11,13,1..., dimensions={0} | all-to-all | bytes 1048576 | tf_op jit(solution)/shard_map/all_to_all | solution.py:266
  70.1 0.9 %join.1 = (bf16[256,512]{1,0:T(8,128)(2,1)}, bf16[256,512]{1,0:T(8,128)(2,1)}) custom-call(bf16[4,512,128]{2,1,0:T(8,128)(2,1)S(1)} %all_to_all.15.pieces), custom_call_target="tpu_custom_call" | custom-call | bytes 1048576 | tf_op jit(solution)/shard_map/join/pallas_call | solution.py:349
Async XLA Ops:
  3.3 4.3 %copy-start = (bf16[256,512]{1,0:T(8,128)(2,1)S(1)}, bf16[256,512]{1,0:T(8,128)(2,1)}, u32[]{:S(2)}) copy-start(bf16[256,512]{1,0:T(8,128)(2,1)} %audio.1) | copy-start | bytes 786436
  3.3 18.9 %all-to-all-start.1 = ((bf16[4,528,128]{2,1,0:T(8,128)(2,1)}), bf16[4,528,128]{2,1,0:T(8,128)(2,1)S(1)}, u32[]{:S(2)}, u32[]{:S(2)}) async-start(bf16[4,528,128]{2,1,0:T(8,128)(2,1)} %get-tuple-element.21), calls=%async_computation.1 | async-start | bytes 1081344 | tf_op jit(solution)/shard_map/all_to_all | solution.py:266
  7.6 7.9 %collective-permute-start.1 = (bf16[256,512]{1,0:T(8,128)(2,1)S(1)}, bf16[256,512]{1,0:T(8,128)(2,1)S(1)}, u32[]{:S(2)}, u32[]{:S(2)}) collective-permute-start(bf16[256,512]{1,0:T(8,128)(2,1)S(1)} %copy-done), channel_id=1, source_target_pairs={{0,1},{1,0},{2,3},{3,2},{4,5},{5,4},{6,7},{7,6},{8,9},{9,8},{10,11... | collective-permute-start | bytes 786440 | tf_op jit(solution)/shard_map/ppermute | solution.py:262
  8.9 12.2 %collective-permute-start = (bf16[256,512]{1,0:T(8,128)(2,1)S(1)}, bf16[256,512]{1,0:T(8,128)(2,1)S(1)}, u32[]{:S(2)}, u32[]{:S(2)}) collective-permute-start(bf16[256,512]{1,0:T(8,128)(2,1)S(1)} %get-tuple-element.17), channel_id=1, source_target_pairs={{0,1},{1,0},{2,3},{3,2},{4,5},{5,4},{6,7},{7,6},{8,9},{9,8},{10,11... | collective-permute-start | bytes 786440 | tf_op jit(solution)/shard_map/ppermute | solution.py:262
  22.2 12.3 %all-to-all-start = ((bf16[4,512,128]{2,1,0:T(8,128)(2,1)}), bf16[4,512,128]{2,1,0:T(8,128)(2,1)S(1)}, u32[]{:S(2)}, u32[]{:S(2)}) async-start(bf16[4,512,128]{2,1,0:T(8,128)(2,1)} %project.3), calls=%async_computation | async-start | bytes 1048576 | tf_op jit(solution)/shard_map/all_to_all | solution.py:266
  26.6 22.6 %collective-permute-start.2 = (bf16[3,528,128]{2,1,0:T(8,128)(2,1)S(1)}, bf16[3,528,128]{2,1,0:T(8,128)(2,1)S(1)}, u32[]{:S(2)}, u32[]{:S(2)}) collective-permute-start(bf16[3,528,128]{2,1,0:T(8,128)(2,1)S(1)} %get-tuple-element.26), channel_id=1, source_target_pairs={{0,8},{2,10},{4,12},{6,14},{8,0},{10,2},{12,4},{14,6},{16,24},{18,... | collective-permute-start | bytes 1216520 | tf_op jit(solution)/shard_map/ppermute | solution.py:289
  26.6 22.5 %collective-permute-start.3 = (bf16[3,528,128]{2,1,0:T(8,128)(2,1)S(1)}, bf16[3,528,128]{2,1,0:T(8,128)(2,1)S(1)}, u32[]{:S(2)}, u32[]{:S(2)}) collective-permute-start(bf16[3,528,128]{2,1,0:T(8,128)(2,1)S(1)} %get-tuple-element.27), channel_id=1, source_target_pairs={{0,0},{2,2},{4,4},{6,6},{8,16},{10,18},{12,20},{14,22},{16,8},{18,... | collective-permute-start | bytes 1216520 | tf_op jit(solution)/shard_map/ppermute | solution.py:289
  34.5 14.6 %collective-permute-start.4 = (bf16[3,512,128]{2,1,0:T(8,128)(2,1)S(1)}, bf16[3,512,128]{2,1,0:T(8,128)(2,1)S(1)}, u32[]{:S(2)}, u32[]{:S(2)}) collective-permute-start(bf16[3,512,128]{2,1,0:T(8,128)(2,1)S(1)} %get-tuple-element.28), channel_id=1, source_target_pairs={{0,8},{2,10},{4,12},{6,14},{8,0},{10,2},{12,4},{14,6},{16,24},{18,... | collective-permute-start | bytes 1179656 | tf_op jit(solution)/shard_map/ppermute | solution.py:289
  34.6 14.5 %collective-permute-start.5 = (bf16[3,512,128]{2,1,0:T(8,128)(2,1)S(1)}, bf16[3,512,128]{2,1,0:T(8,128)(2,1)S(1)}, u32[]{:S(2)}, u32[]{:S(2)}) collective-permute-start(bf16[3,512,128]{2,1,0:T(8,128)(2,1)S(1)} %get-tuple-element.29), channel_id=1, source_target_pairs={{0,0},{2,2},{4,4},{6,6},{8,16},{10,18},{12,20},{14,22},{16,8},{18,... | collective-permute-start | bytes 1179656 | tf_op jit(solution)/shard_map/ppermute | solution.py:289

commit v5 on v2

v5 whole, which is shorter than its diff:
```python
import functools

import jax
import jax.numpy as jnp
from jax import lax
from jax.experimental import pallas as pl
from jax.experimental.pallas import tpu as pltpu
from jax.sharding import PartitionSpec as P

HEAD = 64
RADIUS = 3
GROUP = 4
NEG = -1e30
ID_ROWS = 16

VMEM = pl.BlockSpec(memory_space=pltpu.VMEM)
ANY = pl.BlockSpec(memory_space=pl.ANY)
HBM = pl.BlockSpec(memory_space=pltpu.HBM)


def place():
    return lax.rem(lax.axis_index("tm"), GROUP)


def plane():
    return lax.axis_index("tm") // GROUP


def call(kernel, outs, scratch=(), ins=None, flops=0, moved=0, exps=0, name=None):
    return pl.pallas_call(
        kernel,
        out_shape=outs,
        **({"in_specs": ins} if ins else {}),
        scratch_shapes=scratch,
        compiler_params=pltpu.CompilerParams(vmem_limit_bytes=48 * 2**20),
        cost_estimate=pl.CostEstimate(flops=flops, bytes_accessed=moved, transcendentals=exps),
        name=name,
    )


def prepare_kernel(audio, video, query, key, ids, *refs):
    sums, seconds, packs = refs[:2], refs[2:4], refs[4 : 4 + GROUP]
    streams, firsts, ids_in, ids_wide, sems = refs[8:10], refs[10:12], refs[12], refs[13], refs[14]
    rows, half = audio.shape
    width = packs[0].shape[1]
    side = lax.axis_index("head")
    mine = place()
    copies = []

    def fetch(source, target):
        copies.append(pltpu.make_async_copy(source, target, sems.at[len(copies)]))
        copies[-1].start()
        return copies[-1]

    pieces = []
    for k in range(GROUP):
        columns = pl.ds(pl.multiple_of((mine ^ k) * width, width), width)
        for i, stream in enumerate((audio, video)):
            pieces.append(fetch(stream.at[:, columns], packs[k].at[i * rows : (i + 1) * rows]))
    pieces.append(fetch(ids, ids_in))
    ours = pl.ds(pl.multiple_of(side * half, half), half)
    theirs = pl.ds(pl.multiple_of((1 - side) * half, half), half)
    loads = [fetch(x, s) for x, s in zip((audio, video), streams)]
    loads += [fetch(w.at[ours], f) for w, f in zip((query, key), firsts)]
    others = [fetch(w.at[theirs], f) for w, f in zip((query, key), seconds)]
    for copy in pieces:
        copy.wait()
    ids_wide[...] = jnp.zeros_like(ids_wide)
    ids_wide[: ids_in.shape[0]] = (ids_in[...] + 1).astype(jnp.float32)
    for k in range(GROUP):
        packs[k][2 * rows :] = ids_wide[...].astype(packs[k].dtype)
    for copy in loads:
        copy.wait()
    for i in range(2):
        sums[i][...] = jnp.dot(
            streams[i][...], firsts[i][...], preferred_element_type=jnp.float32
        )
    for copy in others:
        copy.wait()


def project_kernel(scales, *refs):
    parts, others, weights, packs, full = refs[:2], refs[2:4], refs[4:6], refs[7 : 7 + GROUP], refs[-1]
    rows, width = others[0].shape[0], packs[0].shape[1]
    mine = place()
    for i in range(2):
        total = parts[i][...] + jnp.dot(
            others[i][...], weights[i][...], preferred_element_type=jnp.float32
        )
        full[i] = total.astype(jnp.bfloat16) * jnp.bfloat16(scales[i])
        for k in range(GROUP):
            columns = pl.ds(pl.multiple_of((mine ^ k) * width, width), width)
            packs[k][i * rows : (i + 1) * rows] = full[i, :, columns]


def halo_kernel(has_ids, *refs):
    pieces, (first, second) = refs[:GROUP], refs[-2:]
    mine = place()
    odd = lax.rem(plane(), 2)
    for k in range(GROUP):
        block = mine ^ k
        for out, skip in ((first, (GROUP - RADIUS) * (1 - odd)), (second, (GROUP - RADIUS) * odd)):
            spot = block - skip

            @pl.when((spot >= 0) & (spot < RADIUS))
            def _():
                out[spot] = pieces[k][...]

    if has_ids:
        last = lax.axis_size("tm") // GROUP - 1

        @pl.when((plane() == 0) | (plane() == last))
        def _():
            second[:, second.shape[1] - ID_ROWS :] = jnp.zeros(
                (RADIUS, ID_ROWS, second.shape[2]), second.dtype
            )


def join_kernel(*refs):
    pieces, out = refs[:GROUP], refs[GROUP]
    width = pieces[0].shape[1]
    mine = place()
    for k in range(GROUP):
        out[:, pl.ds(pl.multiple_of((mine ^ k) * width, width), width)] = pieces[k][...]


def mark(lanes, width, put):
    lanes = lanes.astype(jnp.float32)
    lane = lax.broadcasted_iota(jnp.int32, (width, width), 1).astype(jnp.float32)
    for part in range(2):
        column = jnp.transpose(jnp.broadcast_to(lanes[part : part + 1], (width, width)))
        put(part * width, jnp.where(column == lane, 1.0, 0.0).astype(jnp.bfloat16))


def stacked_ask(block, forbid):
    head = lax.broadcasted_iota(jnp.int32, block.shape, 1) // HEAD
    return jnp.concatenate(
        [
            jnp.concatenate([jnp.where(head == h, block, jnp.zeros_like(block)), forbid], axis=1)
            for h in range(block.shape[1] // HEAD)
        ],
        axis=0,
    )


def by_head(stacked, rows):
    out = stacked[:rows]
    head = lax.broadcasted_iota(jnp.int32, out.shape, 1) // HEAD
    for h in range(1, stacked.shape[0] // rows):
        out = jnp.where(head == h, stacked[h * rows : (h + 1) * rows], out)
    return out


def attend(ask, old, key_at, value_at, count):
    scores = [
        lax.dot_general(
            ask, key_at(c), (((1,), (1,)), ((), ())), preferred_element_type=jnp.float32
        )
        for c in range(count)
    ]
    top = scores[0]
    for s in scores[1:]:
        top = jnp.maximum(top, s)
    peak = jnp.max(top, axis=1, keepdims=True)
    if old is not None:
        peak = jnp.maximum(peak, old)
    mixed = None
    for c, s in enumerate(scores):
        part = jnp.dot(
            jnp.exp(s - peak).astype(jnp.bfloat16), value_at(c), preferred_element_type=jnp.float32
        )
        mixed = part if mixed is None else mixed + part
    return peak, mixed


def plane_kernel(*refs):
    values, projected = refs[:GROUP], refs[GROUP : 2 * GROUP]
    peaks, totals, sums, forbids, asked, keys, beside = refs[2 * GROUP :]
    rows, width = projected[0].shape[0] // 2, projected[0].shape[1]
    mine = place()
    beside[:, :, width:] = jnp.ones((2, GROUP * rows, width), beside.dtype)
    for k in range(GROUP):
        b = mine ^ k

        def spot(at, size):
            return pl.ds(pl.multiple_of(b * rows + at, size), size)

        def put(at, marks):
            for i in range(2):
                keys[i, spot(at, width), width:] = marks
            forbids[b, at : at + width] = (marks - jnp.bfloat16(1.0)) * jnp.bfloat16(-NEG)

        mark(values[k][2 * rows :], width, put)
        for i in range(2):
            keys[i, spot(0, rows), :width] = projected[k][(1 - i) * rows : (2 - i) * rows]
            beside[i, spot(0, rows), :width] = values[k][(1 - i) * rows : (2 - i) * rows]
            asked[i, b] = projected[k][i * rows : (i + 1) * rows]

    def one(b, _):
        for i in range(2):
            peak, mixed = attend(
                stacked_ask(asked[i, b], forbids[b]),
                None,
                lambda c: keys[i, c * rows : (c + 1) * rows],
                lambda c: beside[i, c * rows : (c + 1) * rows],
                GROUP,
            )
            peaks[i, b] = by_head(jnp.broadcast_to(peak, (peak.shape[0], width)), rows)
            sums[i, b] = by_head(mixed[:, :width], rows)
            totals[i, b] = by_head(mixed[:, width:], rows)
        return _

    lax.fori_loop(0, GROUP, one, 0)


def edge_kernel(side, peaks, totals, sums, forbids, asked, *refs):
    value_edges, projected_edges = refs[:2], refs[2:4]
    outs, (keys, beside, whole) = refs[-GROUP - 3 : -3], refs[-3:]
    rows, width = forbids.shape[1:]
    mine = place()
    odd = lax.rem(plane(), 2)
    beside[:, width:] = jnp.ones((beside.shape[0], width), beside.dtype)
    theirs = slice((1 - side) * rows, (2 - side) * rows)
    for edge in range(2):
        base = RADIUS * (odd if edge else 1 - odd)
        for j in range(RADIUS):

            def spot(at, size):
                return pl.ds(pl.multiple_of((base + j) * rows + at, size), size)

            def put(at, marks):
                keys[spot(at, width), width:] = marks

            mark(value_edges[edge][j, 2 * rows :], width, put)
            keys[spot(0, rows), :width] = projected_edges[edge][j, theirs]
            beside[spot(0, rows), :width] = value_edges[edge][j, theirs]

    def one(b, _):
        def near(c):
            return pl.ds(pl.multiple_of((b + c) * rows, rows), rows)

        old = peaks[side, b]
        peak, mixed = attend(
            stacked_ask(asked[side, b], forbids[b]),
            jnp.concatenate([old[:, h : h + 1] for h in range(0, width, HEAD)], axis=0),
            lambda c: keys[near(c)],
            lambda c: beside[near(c)],
            RADIUS,
        )
        factor = jnp.exp(old - by_head(jnp.broadcast_to(peak, (peak.shape[0], width)), rows))
        total = by_head(mixed[:, width:], rows) + totals[side, b] * factor
        mean = (by_head(mixed[:, :width], rows) + sums[side, b] * factor) / total
        whole[b] = mean.astype(whole.dtype)
        return _

    lax.fori_loop(0, GROUP, one, 0)
    for k in range(GROUP):
        outs[k][...] = whole[mine ^ k]


def local(audio_frames, video_frames, recording, audio_query, video_key):
    rows, half = audio_frames.shape
    width = half // GROUP
    length = lax.axis_size("tm")
    bf16, f32 = jnp.bfloat16, jnp.float32
    shape = jax.ShapeDtypeStruct
    assert length % (2 * GROUP) == 0

    def swapped(x):
        return lax.ppermute(x, "head", [(0, 1), (1, 0)])

    def traded(pieces):
        pairs = lambda k: [(i, i ^ k) for i in range(length)]
        return [pieces[0]] + [lax.ppermute(pieces[k], "tm", pairs(k)) for k in range(1, GROUP)]

    def halo(pieces, has_ids):
        size = pieces[0].shape[0]
        edge = shape((RADIUS, size, width), bf16)
        sent = call(
            functools.partial(halo_kernel, has_ids),
            [edge, edge],
            moved=10 * size * width * 2,
            name="halo",
        )(*pieces)

        def partner(i, second):
            spot, inside = divmod(i, GROUP)
            spot = ((spot + second) ^ 1) - second
            return min(max(spot, 0), length // GROUP - 1) * GROUP + inside

        return sent, [
            lax.ppermute(sent[s], "tm", [(i, partner(i, s)) for i in range(length)])
            for s in range(2)
        ]

    other_audio = swapped(audio_frames)
    other_video = swapped(video_frames)
    part = shape((rows, half), f32)
    square = shape((half, half), bf16)
    given = (audio_frames, video_frames, audio_query, video_key, recording.reshape(rows // width, width))
    query_part, key_part, query_rest, key_rest, *values = call(
        prepare_kernel,
        [part, part, square, square] + [shape((2 * rows + ID_ROWS, width), bf16)] * GROUP,
        [pltpu.VMEM((rows, half), bf16)] * 2
        + [pltpu.VMEM((half, half), bf16)] * 2
        + [pltpu.VMEM((rows // width, width), jnp.int32), pltpu.VMEM((ID_ROWS, width), f32)]
        + [pltpu.SemaphoreType.DMA((2 * GROUP + 7,))],
        ins=[HBM] * 5,
        flops=4 * rows * half * half,
        moved=16 * half * half,
        name="prepare",
    )(*(pltpu.with_memory_space_constraint(x, pltpu.HBM) for x in given))
    values = traded(values)
    sent, value_edges = halo(values, True)
    projected = call(
        functools.partial(project_kernel, (HEAD**-0.5, 1.0)),
        [shape((2 * rows, width), bf16)] * GROUP,
        [pltpu.VMEM((2, rows, half), bf16)],
        ins=[VMEM] * 6 + [ANY],
        flops=4 * rows * half * half,
        moved=4 * half * half + 8 * rows * half * 2,
        name="project",
    )(query_part, key_part, other_audio, other_video, query_rest, key_rest, sent[0])
    projected = traded(projected)
    _, projected_edges = halo(projected, False)

    stat = shape((2, GROUP, rows, width), f32)
    held = shape((GROUP, rows, width), bf16)
    inside, around = GROUP * rows, 2 * RADIUS * rows
    state = call(
        plane_kernel,
        [stat, stat, stat, held, shape((2, GROUP, rows, width), bf16)],
        [pltpu.VMEM((2, inside, 2 * width), bf16)] * 2,
        flops=96 * GROUP * rows * inside * width,
        moved=8 * inside * width * 2,
        exps=4 * GROUP * rows * inside,
        name="plane",
    )(*values, *projected)

    def edge(side, *after):
        return call(
            functools.partial(edge_kernel, side),
            [shape((rows, width), bf16)] * GROUP,
            [pltpu.VMEM((around, 2 * width), bf16)] * 2 + [pltpu.VMEM((GROUP, rows, width), bf16)],
            ins=[VMEM] * 9 + [ANY] * len(after),
            flops=48 * GROUP * rows * RADIUS * rows * width,
            moved=8 * around * width * 2,
            exps=2 * GROUP * rows * RADIUS * rows,
            name="edge",
        )(*state, *value_edges, *projected_edges, *after)

    def join(pieces):
        return call(
            join_kernel, shape((rows, half), bf16), moved=2 * rows * half * 2, name="join"
        )(*traded(pieces))

    video_pieces = edge(1)
    audio_pieces = edge(0, video_pieces[0])
    video_attended = join(video_pieces)
    audio_attended = join(audio_pieces)
    return (audio_attended, video_attended)


def solution(mesh):
    return jax.shard_map(
        local,
        mesh=mesh,
        in_specs=(P("tm", "head"), P("tm", "head"), P("tm"), P(None, "head"), P(None, "head")),
        out_specs=(P("tm", "head"), P("tm", "head")),
        check_vma=False,
    )
```

time: 65.2 us -> 63.5 us (0.974); the launches traced: 64.1 us -> 63.2 us
  Pallas kernels: 19 us -> 25.2 us
  waiting for transfers between devices: 21.7 us -> 16.1 us
  local copies, waits for them, and re-layouts: 2.86 us -> 0 us
  starting transfers between devices: 19.8 us -> 21 us
    pallas_call x6 -> x7, Pallas kernels: 17.5 us -> 23.7 us  [the longest x2 12.7 us: edge(): call(functools.partial(edge_kernel, side), [shape((rows, width), bf16)] *...]
    ppermute x2, waiting for transfers between devices: 5.92 us -> 0.01 us  [swapped(): return lax.ppermute(x, 'head', [(0, 1), (1, 0)])]
    unnamed x10 -> x0, local copies, waits for them, and re-layouts: 2.86 us -> none
    ppermute x4, waiting for transfers between devices: 0.38 us -> 2.89 us  [halo(): lax.ppermute(sent[s], 'tm', [(i, partner(i, s)) for i in range(length)])]
    ppermute x4, starting transfers between devices: 6.54 us -> 9.03 us  [halo(): lax.ppermute(sent[s], 'tm', [(i, partner(i, s)) for i in range(length)])]
    ppermute x12, waiting for transfers between devices: 15.4 us -> 13.2 us  [traded(): lax.ppermute(pieces[k], 'tm', pairs(k))]
    ppermute x12, starting transfers between devices: 11.7 us -> 10.5 us  [traded(): lax.ppermute(pieces[k], 'tm', pairs(k))]
  transfers between devices with their start and end apart: 18 -> 18, of which waited for: 8 -> 7; matrix products, arithmetic and copies ran while one was open for 0% -> 0% of each run, Pallas kernels for 28% -> 28%
where the time goes in v5:
time: 63.5 us; the launch traced here: 63.2 us
  Pallas kernels  25.2 us (40%)
  starting transfers between devices  21 us (33%)
  waiting for transfers between devices  16.1 us (25%)
  between operations  0.78 us (1%)
    ppermute x12, waiting for transfers between devices, traded(): lax.ppermute(pieces[k], 'tm', pairs(k))  13.2 us
    pallas_call x2, Pallas kernels, edge(): call(functools.partial(edge_kernel, side), [shape((rows, width), bf16)] *...  12.7 us
    ppermute x12, starting transfers between devices, traded(): lax.ppermute(pieces[k], 'tm', pairs(k))  10.5 us
    ppermute x4, starting transfers between devices, halo(): lax.ppermute(sent[s], 'tm', [(i, partner(i, s)) for i in range(length)])  9.03 us
    pallas_call x1, Pallas kernels, local(): call(plane_kernel, [stat, stat, stat, held, shape((2, GROUP, rows, width)...  8.08 us
    ppermute x4, waiting for transfers between devices, halo(): lax.ppermute(sent[s], 'tm', [(i, partner(i, s)) for i in range(length)])  2.89 us
    pallas_call x1, Pallas kernels, local(): call(prepare_kernel, [part, part, square, square] + [shape((2 * rows + ID...  2.22 us
    ppermute x2, starting transfers between devices, swapped(): return lax.ppermute(x, 'head', [(0, 1), (1, 0)])  1.53 us
  transfers between devices with their start and end apart: 18, of which 7 were waited for; matrix products, arithmetic and copies ran while one was open for 0% of the time, Pallas kernels for 28%

profile of v5, /device:TPU:9, one launch (start us, length us, event | category | flops | bytes accessed | tf_op | source)
XLA Modules:
  0.0 63.2 jit_solution(8833250049580370810)
XLA Ops:
  0.6 1.3 %collective-permute-start.3 = (bf16[256,512]{1,0:T(8,128)(2,1)}, bf16[256,512]{1,0:T(8,128)(2,1)S(1)}, u32[]{:S(2)}, u32[]{:S(2)}) collective-permute-start(bf16[256,512]{1,0:T(8,128)(2,1)} %audio.1), channel_id=1, source_target_pairs={{0,1},{1,0},{2,3},{3,2},{4,5},{5,4},{6,7},{7,6},{8,9},{9,8},{10,11... | collective-permute-start | bytes 786440 | tf_op jit(solution)/shard_map/ppermute | solution.py:270
  1.9 0.2 collective-permute-start.4
  2.2 2.2 %prepare.1 = (f32[256,512]{1,0:T(8,128)S(1)}, f32[256,512]{1,0:T(8,128)S(1)}, bf16[512,512]{1,0:T(8,128)(2,1)S(1)}, bf16[512,512]{1,0:T(8,128)(2,1)S(1)}, bf16[5...) custom-call(bf16[256,512]{1,0:T(8,128)(2,1)} %audio.1, ...), custom_call_target="tpu_custom_call" | custom-call | flops 268435456 | bytes 4194304 | tf_op jit(solution)/shard_map/prepare/pallas_call | solution.py:301
  4.4 1.3 %collective-permute-start = (bf16[528,128]{1,0:T(8,128)(2,1)S(1)}, bf16[528,128]{1,0:T(8,128)(2,1)S(1)}, u32[]{:S(2)}, u32[]{:S(2)}) collective-permute-start(bf16[528,128]{1,0:T(8,128)(2,1)S(1)} %get-tuple-element.32), channel_id=1, source_target_pairs={{0,2},{2,0},{4,6},{6,4},{8,10},{10,8},{12,14},{14,12},{16,18},{18,... | collective-permute-start | bytes 405512 | tf_op jit(solution)/shard_map/ppermute | solution.py:274
  5.7 1.2 %collective-permute-start.1 = (bf16[528,128]{1,0:T(8,128)(2,1)S(1)}, bf16[528,128]{1,0:T(8,128)(2,1)S(1)}, u32[]{:S(2)}, u32[]{:S(2)}) collective-permute-start(bf16[528,128]{1,0:T(8,128)(2,1)S(1)} %get-tuple-element.33), channel_id=1, source_target_pairs={{0,4},{2,6},{4,0},{6,2},{8,12},{10,14},{12,8},{14,10},{16,20},{18,... | collective-permute-start | bytes 405512 | tf_op jit(solution)/shard_map/ppermute | solution.py:274
  6.9 0.5 collective-permute-start.2
  7.4 0.0 collective-permute-done.refs_1_
  7.4 3.5 %collective-permute-done.1.refs_2_ = bf16[528,128]{1,0:T(8,128)(2,1)S(1)} collective-permute-done((bf16[528,128]{1,0:T(8,128)(2,1)S(1)}, bf16[528,128]{1,0:T(8,128)(2,1)S(1)}, u32[]{:S(2)}, u32[]{:S(2)}) %collective-permute-start.1) | collective-permute-done | bytes 135200 | tf_op jit(solution)/shard_map/ppermute | solution.py:274
  10.9 3.4 %collective-permute-done.2.refs_3_ = bf16[528,128]{1,0:T(8,128)(2,1)S(1)} collective-permute-done((bf16[528,128]{1,0:T(8,128)(2,1)S(1)}, bf16[528,128]{1,0:T(8,128)(2,1)S(1)}, u32[]{:S(2)}, u32[]{:S(2)}) %collective-permute-start.2) | collective-permute-done | bytes 135200 | tf_op jit(solution)/shard_map/ppermute | solution.py:274
  14.2 0.1 halo.2
  14.3 0.0 collective-permute-done.3.refs_2_
  14.3 0.0 collective-permute-done.4.refs_3_
  14.3 0.6 project.1
  14.9 1.0 %collective-permute-start.5 = (bf16[512,128]{1,0:T(8,128)(2,1)S(1)}, bf16[512,128]{1,0:T(8,128)(2,1)S(1)}, u32[]{:S(2)}, u32[]{:S(2)}) collective-permute-start(bf16[512,128]{1,0:T(8,128)(2,1)S(1)} %get-tuple-element.41), channel_id=1, source_target_pairs={{0,2},{2,0},{4,6},{6,4},{8,10},{10,8},{12,14},{14,12},{16,18},{18,... | collective-permute-start | bytes 393224 | tf_op jit(solution)/shard_map/ppermute | solution.py:274
  15.9 1.2 %collective-permute-start.6 = (bf16[512,128]{1,0:T(8,128)(2,1)S(1)}, bf16[512,128]{1,0:T(8,128)(2,1)S(1)}, u32[]{:S(2)}, u32[]{:S(2)}) collective-permute-start(bf16[512,128]{1,0:T(8,128)(2,1)S(1)} %get-tuple-element.42), channel_id=1, source_target_pairs={{0,4},{2,6},{4,0},{6,2},{8,12},{10,14},{12,8},{14,10},{16,20},{18,... | collective-permute-start | bytes 393224 | tf_op jit(solution)/shard_map/ppermute | solution.py:274
  17.1 0.5 collective-permute-start.7
  17.6 0.0 collective-permute-start.8
  17.6 4.5 %collective-permute-start.9 = (bf16[3,528,128]{2,1,0:T(8,128)(2,1)S(1)}, bf16[3,528,128]{2,1,0:T(8,128)(2,1)S(1)}, u32[]{:S(2)}, u32[]{:S(2)}) collective-permute-start(bf16[3,528,128]{2,1,0:T(8,128)(2,1)S(1)} %get-tuple-element.49), channel_id=1, source_target_pairs={{0,0},{2,2},{4,4},{6,6},{8,16},{10,18},{12,20},{14,22},{16,8},{18,... | collective-permute-start | bytes 1216520 | tf_op jit(solution)/shard_map/ppermute | solution.py:292
  22.1 0.0 collective-permute-done.5.refs_5_.refs_1_
  22.1 0.0 collective-permute-done.6.refs_6_.refs_2_
  22.1 2.1 %collective-permute-done.7.refs_7_.refs_3_ = bf16[512,128]{1,0:T(8,128)(2,1)S(1)} collective-permute-done((bf16[512,128]{1,0:T(8,128)(2,1)S(1)}, bf16[512,128]{1,0:T(8,128)(2,1)S(1)}, u32[]{:S(2)}, u32[]{:S(2)}) %collective-permute-start.7) | collective-permute-done | bytes 131104 | tf_op jit(solution)/shard_map/ppermute | solution.py:274
  24.2 0.1 halo.3
  24.3 0.1 collective-permute-start.10
  24.4 4.5 %collective-permute-start.11 = (bf16[3,512,128]{2,1,0:T(8,128)(2,1)S(1)}, bf16[3,512,128]{2,1,0:T(8,128)(2,1)S(1)}, u32[]{:S(2)}, u32[]{:S(2)}) collective-permute-start(bf16[3,512,128]{2,1,0:T(8,128)(2,1)S(1)} %get-tuple-element.51), channel_id=1, source_target_pairs={{0,0},{2,2},{4,4},{6,6},{8,16},{10,18},{12,20},{14,22},{16,8},{18,... | collective-permute-start | bytes 1179656 | tf_op jit(solution)/shard_map/ppermute | solution.py:292
  28.9 8.1 %plane.1 = (f32[2,4,256,128]{3,2,1,0:T(8,128)S(1)}, f32[2,4,256,128]{3,2,1,0:T(8,128)S(1)}, f32[2,4,256,128]{3,2,1,0:T(8,128)S(1)}, bf16[4,256,128]{2,1,0:T(8,128)(2,1)S(1)}, bf16[2,4,256,128]{3,2,1,0:T(8,128)(2,1)S(1)}) custom-call(bf16[528,128]{1,0:T(8,128)(2,1)S(1)} %get-tuple-element.31.refs_0_, bf16[528,128]{1,0:T(8,128)(2,1)S(1)} %collective-permute-done.refs_1_, ...), custom_call_target="tpu_custom_call" | custom-call | flops 12884901888 | bytes 2097152 | tf_op jit(solution)/shard_map/plane/pallas_call | solution.py:330
  36.9 0.0 collective-permute-done.8.refs_0_
  37.0 0.0 collective-permute-done.9.refs_1_
  37.0 0.0 collective-permute-done.10.refs_2_
  37.0 2.9 %collective-permute-done.11.refs_3_ = bf16[3,512,128]{2,1,0:T(8,128)(2,1)S(1)} collective-permute-done((bf16[3,512,128]{2,1,0:T(8,128)(2,1)S(1)}, bf16[3,512,128]{2,1,0:T(8,128)(2,1)S(1)}, u32[]{:S(2)}, u32[]{:S(2)}) %collective-permute-start.11) | collective-permute-done | bytes 393248 | tf_op jit(solution)/shard_map/ppermute | solution.py:292
  39.9 6.3 %edge.2 = (bf16[256,128]{1,0:T(8,128)(2,1)S(1)}, bf16[256,128]{1,0:T(8,128)(2,1)S(1)}, bf16[256,128]{1,0:T(8,128)(2,1)S(1)}, bf16[256,128]{1,0:T(8,128)(2,1)S(1)}) custom-call(f32[2,4,256,128]{3,2,1,0:T(8,128)S(1)} %get-tuple-element.44.peaks, f32[2,4,256,128]{3,2,1,0:T(8,128)S(1)} %get-tuple-element.45.totals, ...), custom_call_target="tpu_custom_call" | custom-call | flops 4831838208 | bytes 3145728 | tf_op jit(solution)/shard_map/edge/pallas_call | solution.py:341
  46.2 1.0 %collective-permute-start.15 = (bf16[256,128]{1,0:T(8,128)(2,1)S(1)}, bf16[256,128]{1,0:T(8,128)(2,1)S(1)}, u32[]{:S(2)}, u32[]{:S(2)}) collective-permute-start(bf16[256,128]{1,0:T(8,128)(2,1)S(1)} %get-tuple-element.57), channel_id=1, source_target_pairs={{0,2},{2,0},{4,6},{6,4},{8,10},{10,8},{12,14},{14,12},{16,18},{18,... | collective-permute-start | bytes 196616 | tf_op jit(solution)/shard_map/ppermute | solution.py:274
  47.2 6.3 %edge.3 = (bf16[256,128]{1,0:T(8,128)(2,1)S(1)}, bf16[256,128]{1,0:T(8,128)(2,1)S(1)}, bf16[256,128]{1,0:T(8,128)(2,1)S(1)}, bf16[256,128]{1,0:T(8,128)(2,1)S(1)}) custom-call(f32[2,4,256,128]{3,2,1,0:T(8,128)S(1)} %get-tuple-element.44.peaks, f32[2,4,256,128]{3,2,1,0:T(8,128)S(1)} %get-tuple-element.45.totals, ...), custom_call_target="tpu_custom_call" | custom-call | flops 4831838208 | bytes 3145728 | tf_op jit(solution)/shard_map/edge/pallas_call | solution.py:341
  53.6 0.1 collective-permute-start.12
  53.7 1.3 %collective-permute-start.16 = (bf16[256,128]{1,0:T(8,128)(2,1)S(1)}, bf16[256,128]{1,0:T(8,128)(2,1)S(1)}, u32[]{:S(2)}, u32[]{:S(2)}) collective-permute-start(bf16[256,128]{1,0:T(8,128)(2,1)S(1)} %get-tuple-element.58), channel_id=1, source_target_pairs={{0,4},{2,6},{4,0},{6,2},{8,12},{10,14},{12,8},{14,10},{16,20},{18,... | collective-permute-start | bytes 196616 | tf_op jit(solution)/shard_map/ppermute | solution.py:274
  54.9 0.8 %collective-permute-start.17 = (bf16[256,128]{1,0:T(8,128)(2,1)S(1)}, bf16[256,128]{1,0:T(8,128)(2,1)S(1)}, u32[]{:S(2)}, u32[]{:S(2)}) collective-permute-start(bf16[256,128]{1,0:T(8,128)(2,1)S(1)} %get-tuple-element.59), channel_id=1, source_target_pairs={{0,6},{2,4},{4,2},{6,0},{8,14},{10,12},{12,10},{14,8},{16,22},{18,... | collective-permute-start | bytes 196616 | tf_op jit(solution)/shard_map/ppermute | solution.py:274
  55.8 1.2 %collective-permute-start.13 = (bf16[256,128]{1,0:T(8,128)(2,1)S(1)}, bf16[256,128]{1,0:T(8,128)(2,1)S(1)}, u32[]{:S(2)}, u32[]{:S(2)}) collective-permute-start(bf16[256,128]{1,0:T(8,128)(2,1)S(1)} %get-tuple-element.55), channel_id=1, source_target_pairs={{0,4},{2,6},{4,0},{6,2},{8,12},{10,14},{12,8},{14,10},{16,20},{18,... | collective-permute-start | bytes 196616 | tf_op jit(solution)/shard_map/ppermute | solution.py:274
  57.0 0.0 collective-permute-done.15.refs_1_
  57.0 0.3 collective-permute-start.14
  57.3 0.0 collective-permute-done.16.refs_2_
  57.3 2.3 %collective-permute-done.17.refs_3_ = bf16[256,128]{1,0:T(8,128)(2,1)S(1)} collective-permute-done((bf16[256,128]{1,0:T(8,128)(2,1)S(1)}, bf16[256,128]{1,0:T(8,128)(2,1)S(1)}, u32[]{:S(2)}, u32[]{:S(2)}) %collective-permute-start.17) | collective-permute-done | bytes 65568 | tf_op jit(solution)/shard_map/ppermute | solution.py:274
  59.6 0.8 %join.3 = bf16[256,512]{1,0:T(8,128)(2,1)} custom-call(bf16[256,128]{1,0:T(8,128)(2,1)S(1)} %get-tuple-element.52.refs_4_.refs_0_, bf16[256,128]{1,0:T(8,128)(2,1)S(1)} %collective-permute-done.15.refs_1_, bf16[256,128]{1,0:T(8,128)(2,1)S(1)} %collective-permute-done.16.refs_2_, bf16[256,128]{1,0:T(8,128)(2,1)S(1)} %collective-permute-done.17.refs_3_), custom_call_target="tpu_custom_call" | custom-call | bytes 524288 | tf_op jit(solution)/shard_map/join/pallas_call | solution.py:353
  60.4 0.0 collective-permute-done.12.refs_1_
  60.4 0.6 %collective-permute-done.13.refs_2_ = bf16[256,128]{1,0:T(8,128)(2,1)S(1)} collective-permute-done((bf16[256,128]{1,0:T(8,128)(2,1)S(1)}, bf16[256,128]{1,0:T(8,128)(2,1)S(1)}, u32[]{:S(2)}, u32[]{:S(2)}) %collective-permute-start.13) | collective-permute-done | bytes 65568 | tf_op jit(solution)/shard_map/ppermute | solution.py:274
  61.0 1.4 %collective-permute-done.14.refs_3_ = bf16[256,128]{1,0:T(8,128)(2,1)S(1)} collective-permute-done((bf16[256,128]{1,0:T(8,128)(2,1)S(1)}, bf16[256,128]{1,0:T(8,128)(2,1)S(1)}, u32[]{:S(2)}, u32[]{:S(2)}) %collective-permute-start.14) | collective-permute-done | bytes 65568 | tf_op jit(solution)/shard_map/ppermute | solution.py:274
  62.4 0.8 %join.2 = bf16[256,512]{1,0:T(8,128)(2,1)} custom-call(bf16[256,128]{1,0:T(8,128)(2,1)S(1)} %get-tuple-element.53.refs_0_, bf16[256,128]{1,0:T(8,128)(2,1)S(1)} %collective-permute-done.12.refs_1_, bf16[256,128]{1,0:T(8,128)(2,1)S(1)} %collective-permute-done.13.refs_2_, bf16[256,128]{1,0:T(8,128)(2,1)S(1)} %collective-permute-done.14.refs_3_), custom_call_target="tpu_custom_call" | custom-call | bytes 524288 | tf_op jit(solution)/shard_map/join/pallas_call | solution.py:353
Async XLA Ops:
  0.6 13.7 %collective-permute-start.3 = (bf16[256,512]{1,0:T(8,128)(2,1)}, bf16[256,512]{1,0:T(8,128)(2,1)S(1)}, u32[]{:S(2)}, u32[]{:S(2)}) collective-permute-start(bf16[256,512]{1,0:T(8,128)(2,1)} %audio.1), channel_id=1, source_target_pairs={{0,1},{1,0},{2,3},{3,2},{4,5},{5,4},{6,7},{7,6},{8,9},{9,8},{10,11... | collective-permute-start | bytes 786440 | tf_op jit(solution)/shard_map/ppermute | solution.py:270
  1.9 12.4 %collective-permute-start.4 = (bf16[256,512]{1,0:T(8,128)(2,1)}, bf16[256,512]{1,0:T(8,128)(2,1)S(1)}, u32[]{:S(2)}, u32[]{:S(2)}) collective-permute-start(bf16[256,512]{1,0:T(8,128)(2,1)} %video.1), channel_id=1, source_target_pairs={{0,1},{1,0},{2,3},{3,2},{4,5},{5,4},{6,7},{7,6},{8,9},{9,8},{10,11... | collective-permute-start | bytes 786440 | tf_op jit(solution)/shard_map/ppermute | solution.py:270
  4.4 3.0 %collective-permute-start = (bf16[528,128]{1,0:T(8,128)(2,1)S(1)}, bf16[528,128]{1,0:T(8,128)(2,1)S(1)}, u32[]{:S(2)}, u32[]{:S(2)}) collective-permute-start(bf16[528,128]{1,0:T(8,128)(2,1)S(1)} %get-tuple-element.32), channel_id=1, source_target_pairs={{0,2},{2,0},{4,6},{6,4},{8,10},{10,8},{12,14},{14,12},{16,18},{18,... | collective-permute-start | bytes 405512 | tf_op jit(solution)/shard_map/ppermute | solution.py:274
  5.7 5.2 %collective-permute-start.1 = (bf16[528,128]{1,0:T(8,128)(2,1)S(1)}, bf16[528,128]{1,0:T(8,128)(2,1)S(1)}, u32[]{:S(2)}, u32[]{:S(2)}) collective-permute-start(bf16[528,128]{1,0:T(8,128)(2,1)S(1)} %get-tuple-element.33), channel_id=1, source_target_pairs={{0,4},{2,6},{4,0},{6,2},{8,12},{10,14},{12,8},{14,10},{16,20},{18,... | collective-permute-start | bytes 405512 | tf_op jit(solution)/shard_map/ppermute | solution.py:274
  6.9 7.3 %collective-permute-start.2 = (bf16[528,128]{1,0:T(8,128)(2,1)S(1)}, bf16[528,128]{1,0:T(8,128)(2,1)S(1)}, u32[]{:S(2)}, u32[]{:S(2)}) collective-permute-start(bf16[528,128]{1,0:T(8,128)(2,1)S(1)} %get-tuple-element.34), channel_id=1, source_target_pairs={{0,6},{2,4},{4,2},{6,0},{8,14},{10,12},{12,10},{14,8},{16,22},{18,... | collective-permute-start | bytes 405512 | tf_op jit(solution)/shard_map/ppermute | solution.py:274
  14.9 7.2 %collective-permute-start.5 = (bf16[512,128]{1,0:T(8,128)(2,1)S(1)}, bf16[512,128]{1,0:T(8,128)(2,1)S(1)}, u32[]{:S(2)}, u32[]{:S(2)}) collective-permute-start(bf16[512,128]{1,0:T(8,128)(2,1)S(1)} %get-tuple-element.41), channel_id=1, source_target_pairs={{0,2},{2,0},{4,6},{6,4},{8,10},{10,8},{12,14},{14,12},{16,18},{18,... | collective-permute-start | bytes 393224 | tf_op jit(solution)/shard_map/ppermute | solution.py:274
  15.9 6.2 %collective-permute-start.6 = (bf16[512,128]{1,0:T(8,128)(2,1)S(1)}, bf16[512,128]{1,0:T(8,128)(2,1)S(1)}, u32[]{:S(2)}, u32[]{:S(2)}) collective-permute-start(bf16[512,128]{1,0:T(8,128)(2,1)S(1)} %get-tuple-element.42), channel_id=1, source_target_pairs={{0,4},{2,6},{4,0},{6,2},{8,12},{10,14},{12,8},{14,10},{16,20},{18,... | collective-permute-start | bytes 393224 | tf_op jit(solution)/shard_map/ppermute | solution.py:274
  17.1 7.1 %collective-permute-start.7 = (bf16[512,128]{1,0:T(8,128)(2,1)S(1)}, bf16[512,128]{1,0:T(8,128)(2,1)S(1)}, u32[]{:S(2)}, u32[]{:S(2)}) collective-permute-start(bf16[512,128]{1,0:T(8,128)(2,1)S(1)} %get-tuple-element.43), channel_id=1, source_target_pairs={{0,6},{2,4},{4,2},{6,0},{8,14},{10,12},{12,10},{14,8},{16,22},{18,... | collective-permute-start | bytes 393224 | tf_op jit(solution)/shard_map/ppermute | solution.py:274
  17.6 19.4 %collective-permute-start.8 = (bf16[3,528,128]{2,1,0:T(8,128)(2,1)S(1)}, bf16[3,528,128]{2,1,0:T(8,128)(2,1)S(1)}, u32[]{:S(2)}, u32[]{:S(2)}) collective-permute-start(bf16[3,528,128]{2,1,0:T(8,128)(2,1)S(1)} %get-tuple-element.39.refs_6_), channel_id=1, source_target_pairs={{0,8},{2,10},{4,12},{6,14},{8,0},{10,2},{12,4},{14,6},{16,24},{18,... | collective-permute-start | bytes 1216520 | tf_op jit(solution)/shard_map/ppermute | solution.py:292
  17.6 19.4 %collective-permute-start.9 = (bf16[3,528,128]{2,1,0:T(8,128)(2,1)S(1)}, bf16[3,528,128]{2,1,0:T(8,128)(2,1)S(1)}, u32[]{:S(2)}, u32[]{:S(2)}) collective-permute-start(bf16[3,528,128]{2,1,0:T(8,128)(2,1)S(1)} %get-tuple-element.49), channel_id=1, source_target_pairs={{0,0},{2,2},{4,4},{6,6},{8,16},{10,18},{12,20},{14,22},{16,8},{18,... | collective-permute-start | bytes 1216520 | tf_op jit(solution)/shard_map/ppermute | solution.py:292
  24.3 12.7 %collective-permute-start.10 = (bf16[3,512,128]{2,1,0:T(8,128)(2,1)S(1)}, bf16[3,512,128]{2,1,0:T(8,128)(2,1)S(1)}, u32[]{:S(2)}, u32[]{:S(2)}) collective-permute-start(bf16[3,512,128]{2,1,0:T(8,128)(2,1)S(1)} %get-tuple-element.50), channel_id=1, source_target_pairs={{0,8},{2,10},{4,12},{6,14},{8,0},{10,2},{12,4},{14,6},{16,24},{18,... | collective-permute-start | bytes 1179656 | tf_op jit(solution)/shard_map/ppermute | solution.py:292
  24.4 15.5 %collective-permute-start.11 = (bf16[3,512,128]{2,1,0:T(8,128)(2,1)S(1)}, bf16[3,512,128]{2,1,0:T(8,128)(2,1)S(1)}, u32[]{:S(2)}, u32[]{:S(2)}) collective-permute-start(bf16[3,512,128]{2,1,0:T(8,128)(2,1)S(1)} %get-tuple-element.51), channel_id=1, source_target_pairs={{0,0},{2,2},{4,4},{6,6},{8,16},{10,18},{12,20},{14,22},{16,8},{18,... | collective-permute-start | bytes 1179656 | tf_op jit(solution)/shard_map/ppermute | solution.py:292
  46.2 10.8 %collective-permute-start.15 = (bf16[256,128]{1,0:T(8,128)(2,1)S(1)}, bf16[256,128]{1,0:T(8,128)(2,1)S(1)}, u32[]{:S(2)}, u32[]{:S(2)}) collective-permute-start(bf16[256,128]{1,0:T(8,128)(2,1)S(1)} %get-tuple-element.57), channel_id=1, source_target_pairs={{0,2},{2,0},{4,6},{6,4},{8,10},{10,8},{12,14},{14,12},{16,18},{18,... | collective-permute-start | bytes 196616 | tf_op jit(solution)/shard_map/ppermute | solution.py:274
  53.6 6.8 %collective-permute-start.12 = (bf16[256,128]{1,0:T(8,128)(2,1)S(1)}, bf16[256,128]{1,0:T(8,128)(2,1)S(1)}, u32[]{:S(2)}, u32[]{:S(2)}) collective-permute-start(bf16[256,128]{1,0:T(8,128)(2,1)S(1)} %get-tuple-element.54), channel_id=1, source_target_pairs={{0,2},{2,0},{4,6},{6,4},{8,10},{10,8},{12,14},{14,12},{16,18},{18,... | collective-permute-start | bytes 196616 | tf_op jit(solution)/shard_map/ppermute | solution.py:274
  53.7 3.7 %collective-permute-start.16 = (bf16[256,128]{1,0:T(8,128)(2,1)S(1)}, bf16[256,128]{1,0:T(8,128)(2,1)S(1)}, u32[]{:S(2)}, u32[]{:S(2)}) collective-permute-start(bf16[256,128]{1,0:T(8,128)(2,1)S(1)} %get-tuple-element.58), channel_id=1, source_target_pairs={{0,4},{2,6},{4,0},{6,2},{8,12},{10,14},{12,8},{14,10},{16,20},{18,... | collective-permute-start | bytes 196616 | tf_op jit(solution)/shard_map/ppermute | solution.py:274
  54.9 4.7 %collective-permute-start.17 = (bf16[256,128]{1,0:T(8,128)(2,1)S(1)}, bf16[256,128]{1,0:T(8,128)(2,1)S(1)}, u32[]{:S(2)}, u32[]{:S(2)}) collective-permute-start(bf16[256,128]{1,0:T(8,128)(2,1)S(1)} %get-tuple-element.59), channel_id=1, source_target_pairs={{0,6},{2,4},{4,2},{6,0},{8,14},{10,12},{12,10},{14,8},{16,22},{18,... | collective-permute-start | bytes 196616 | tf_op jit(solution)/shard_map/ppermute | solution.py:274
  55.8 5.2 %collective-permute-start.13 = (bf16[256,128]{1,0:T(8,128)(2,1)S(1)}, bf16[256,128]{1,0:T(8,128)(2,1)S(1)}, u32[]{:S(2)}, u32[]{:S(2)}) collective-permute-start(bf16[256,128]{1,0:T(8,128)(2,1)S(1)} %get-tuple-element.55), channel_id=1, source_target_pairs={{0,4},{2,6},{4,0},{6,2},{8,12},{10,14},{12,8},{14,10},{16,20},{18,... | collective-permute-start | bytes 196616 | tf_op jit(solution)/shard_map/ppermute | solution.py:274
  57.0 5.4 %collective-permute-start.14 = (bf16[256,128]{1,0:T(8,128)(2,1)S(1)}, bf16[256,128]{1,0:T(8,128)(2,1)S(1)}, u32[]{:S(2)}, u32[]{:S(2)}) collective-permute-start(bf16[256,128]{1,0:T(8,128)(2,1)S(1)} %get-tuple-element.56), channel_id=1, source_target_pairs={{0,6},{2,4},{4,2},{6,0},{8,14},{10,12},{12,10},{14,8},{16,22},{18,... | collective-permute-start | bytes 196616 | tf_op jit(solution)/shard_map/ppermute | solution.py:274

commit v6 on v5

v6 whole, which is shorter than its diff:
```python
import functools

import jax
import jax.numpy as jnp
from jax import lax
from jax.experimental import pallas as pl
from jax.experimental.pallas import tpu as pltpu
from jax.sharding import PartitionSpec as P

HEAD = 64
RADIUS = 3
GROUP = 4
NEG = -1e30
ID_ROWS = 16
STAT_ROWS = 16

VMEM = pl.BlockSpec(memory_space=pltpu.VMEM)
ANY = pl.BlockSpec(memory_space=pl.ANY)
HBM = pl.BlockSpec(memory_space=pltpu.HBM)


def place():
    return lax.rem(lax.axis_index("tm"), GROUP)


def plane():
    return lax.axis_index("tm") // GROUP


def call(kernel, outs, scratch=(), ins=None, flops=0, moved=0, exps=0, name=None):
    return pl.pallas_call(
        kernel,
        out_shape=outs,
        **({"in_specs": ins} if ins else {}),
        scratch_shapes=scratch,
        compiler_params=pltpu.CompilerParams(vmem_limit_bytes=32 * 2**20),
        cost_estimate=pl.CostEstimate(flops=flops, bytes_accessed=moved, transcendentals=exps),
        name=name,
    )


def prepare_kernel(audio, video, query, key, ids, *refs):
    sums, seconds, columns, streams, id_rows = refs[:2], refs[2:4], refs[4:6], refs[6:8], refs[8]
    firsts, ids_in, ids_wide, sems = refs[9:11], refs[11], refs[12], refs[13]
    half = audio.shape[1]
    width = id_rows.shape[1]
    side = lax.axis_index("head")
    mine = place()
    copies = []

    def fetch(source, target):
        copies.append(pltpu.make_async_copy(source, target, sems.at[len(copies)]))
        copies[-1].start()
        return copies[-1]

    ours = pl.ds(pl.multiple_of(side * half, half), half)
    theirs = pl.ds(pl.multiple_of((1 - side) * half, half), half)
    for i, stream in enumerate((audio, video)):
        fetch(stream, streams[i])
    for i, weight in enumerate((query, key)):
        fetch(weight.at[ours], firsts[i])
    fetch(ids, ids_in)
    for i, stream in enumerate((audio, video)):
        for k in range(GROUP):
            at = pl.ds(pl.multiple_of((mine ^ k) * width, width), width)
            fetch(stream.at[:, at], columns[i].at[k])
    for i, weight in enumerate((query, key)):
        fetch(weight.at[theirs], seconds[i])
    for copy in copies[:5]:
        copy.wait()
    for i in range(2):
        sums[i][...] = jnp.dot(
            streams[i][...], firsts[i][...], preferred_element_type=jnp.float32
        )
    ids_wide[...] = jnp.zeros_like(ids_wide)
    ids_wide[: ids_in.shape[0]] = (ids_in[...] + 1).astype(jnp.float32)
    id_rows[...] = ids_wide[...].astype(id_rows.dtype)
    for copy in copies[5:]:
        copy.wait()


def project_kernel(scale, first, part, other, weight, columns, *refs):
    if first:
        ids, passed, *packs, relay, full = refs
        relay[...] = passed[...]
    else:
        *packs, full = refs
    rows, width = other.shape[0], columns.shape[2]
    mine = place()
    total = part[...] + jnp.dot(other[...], weight[...], preferred_element_type=jnp.float32)
    full[...] = total.astype(jnp.bfloat16) * jnp.bfloat16(scale)
    for k in range(GROUP):
        packs[k][:rows] = columns[k]
        at = pl.ds(pl.multiple_of((mine ^ k) * width, width), width)
        packs[k][rows : 2 * rows] = full[:, at]
        if first:
            packs[k][2 * rows :] = ids[...]


def halo_kernel(*refs):
    pieces, (first, second) = refs[:GROUP], refs[-2:]
    mine = place()
    odd = lax.rem(plane(), 2)
    for k in range(GROUP):
        block = mine ^ k
        for out, skip in ((first, (GROUP - RADIUS) * (1 - odd)), (second, (GROUP - RADIUS) * odd)):
            spot = block - skip

            @pl.when((spot >= 0) & (spot < RADIUS))
            def _():
                out[spot] = pieces[k][...]

    last = lax.axis_size("tm") // GROUP - 1

    @pl.when((plane() == 0) | (plane() == last))
    def _():
        second[:, second.shape[1] - ID_ROWS :] = jnp.zeros(
            (RADIUS, ID_ROWS, second.shape[2]), second.dtype
        )


def join_kernel(*refs):
    pieces, out = refs[:GROUP], refs[GROUP]
    width = pieces[0].shape[1]
    mine = place()
    for k in range(GROUP):
        out[:, pl.ds(pl.multiple_of((mine ^ k) * width, width), width)] = pieces[k][...]


def mark(lanes, put):
    lanes = lanes.astype(jnp.float32)
    width = lanes.shape[1]
    row = lax.broadcasted_iota(jnp.int32, (width, width), 0).astype(jnp.float32)
    for part in range(2):
        turned = jnp.where(row == lanes[part : part + 1], 1.0, 0.0).astype(jnp.bfloat16)
        put(part * width, jnp.transpose(turned))


def forbid(marks):
    return (marks - jnp.bfloat16(1.0)) * jnp.bfloat16(-NEG)


def stacked_ask(block, marks):
    head = lax.broadcasted_iota(jnp.int32, block.shape, 1) // HEAD
    beside = forbid(marks)
    return jnp.concatenate(
        [
            jnp.concatenate([jnp.where(head == h, block, jnp.zeros_like(block)), beside], axis=1)
            for h in range(block.shape[1] // HEAD)
        ],
        axis=0,
    )


def by_head(stacked, rows):
    out = stacked[:rows]
    head = lax.broadcasted_iota(jnp.int32, out.shape, 1) // HEAD
    for h in range(1, stacked.shape[0] // rows):
        out = jnp.where(head == h, stacked[h * rows : (h + 1) * rows], out)
    return out


def attend(ask, old, keys, values):
    scores = [
        lax.dot_general(ask, key, (((1,), (1,)), ((), ())), preferred_element_type=jnp.float32)
        for key in keys
    ]
    top = scores[0]
    for s in scores[1:]:
        top = jnp.maximum(top, s)
    middle = top.shape[1] // 2
    top = jnp.maximum(top[:, :middle], top[:, middle:])
    if old is not None:
        top = jnp.maximum(top, old)
    peak = jnp.max(top, axis=1, keepdims=True)
    mixed = None
    for s, value in zip(scores, values):
        part = jnp.dot(
            jnp.exp(s - peak).astype(jnp.bfloat16), value, preferred_element_type=jnp.float32
        )
        mixed = part if mixed is None else mixed + part
    return peak, mixed


def plane_kernel(*refs):
    audio, video = refs[:GROUP], refs[GROUP : 2 * GROUP]
    peaks, sums, keys, beside = refs[2 * GROUP :]
    rows, width = video[0].shape[0] // 2, video[0].shape[1]
    mine = place()
    beside[:, :, width:] = jnp.ones((2, GROUP * rows, width), beside.dtype)
    for k in range(GROUP):
        b = mine ^ k

        def spot(at, size):
            return pl.ds(pl.multiple_of(b * rows + at, size), size)

        def put(at, marks):
            for i in range(2):
                keys[i, spot(at, width), width:] = marks

        mark(audio[k][2 * rows :], put)
        for i, pack in enumerate((video[k], audio[k])):
            keys[i, spot(0, rows), :width] = pack[rows : 2 * rows]
            beside[i, spot(0, rows), :width] = pack[:rows]

    def one(b, _):
        at = pl.ds(pl.multiple_of(b * rows, rows), rows)
        blocks = [slice(c * rows, (c + 1) * rows) for c in range(GROUP)]
        for i in range(2):
            peak, sums[i, b] = attend(
                stacked_ask(keys[1 - i, at, :width], keys[i, at, width:]),
                None,
                [keys[i, c] for c in blocks],
                [beside[i, c] for c in blocks],
            )
            peaks[i, b] = jnp.broadcast_to(peak, (peak.shape[0], width))
        return _

    lax.fori_loop(0, GROUP, one, 0)


def lend_kernel(edge_a, edge_b, plane_keys, plane_beside, first, second, keys, results):
    rows, width = keys.shape[0] // (2 * RADIUS), keys.shape[1] // 2
    odd = lax.rem(plane(), 2)
    for edge, base in ((edge_a, RADIUS * (1 - odd)), (edge_b, RADIUS * odd)):
        for j in range(RADIUS):

            def spot(at, size):
                return pl.ds(pl.multiple_of((base + j) * rows + at, size), size)

            def put(at, marks):
                keys[spot(at, width), width:] = marks

            mark(edge[j, 2 * rows :], put)
            keys[spot(0, rows), :width] = edge[j, rows : 2 * rows]
    lane = lax.broadcasted_iota(jnp.int32, (rows, width), 1)
    for e in range(2 * RADIUS):
        below, j = e < RADIUS, e % RADIUS
        blocks = range(0, j + 1) if below else range(j + 1, GROUP)
        blocks = [slice(c * rows, (c + 1) * rows) for c in blocks]
        at = slice(e * rows, (e + 1) * rows)
        peak, mixed = attend(
            stacked_ask(keys[at, :width], keys[at, width:]),
            None,
            [plane_keys[0, c] for c in blocks],
            [plane_beside[0, c] for c in blocks],
        )
        mean = by_head(mixed[:, :width], rows) / by_head(mixed[:, width:], rows)
        results[e // RADIUS, j, :rows] = mean.astype(results.dtype)
        logs = peak + jnp.log(mixed[:, width:])
        high = logs.astype(jnp.bfloat16)
        rest = logs - high.astype(jnp.float32)
        middle = rest.astype(jnp.bfloat16)
        low = (rest - middle.astype(jnp.float32)).astype(jnp.bfloat16)
        picked = jnp.zeros((rows, width), jnp.bfloat16)
        for h in range(width // HEAD):
            for n, piece in enumerate((high, middle, low)):
                picked = jnp.where(lane == 8 * h + n, piece[h * rows : (h + 1) * rows], picked)
        for part in range(rows // width):
            turned = jnp.transpose(picked[part * width : (part + 1) * width])
            at = rows + part * STAT_ROWS
            results[e // RADIUS, j, at : at + STAT_ROWS] = turned[:STAT_ROWS]
    first[...] = results[1 - odd]
    second[...] = results[odd]


def edge_kernel(edge_a, edge_b, keys, plane_keys, peaks, sums, *refs):
    outs, (beside, whole) = refs[-GROUP - 2 : -2], refs[-2:]
    rows, width = outs[0].shape
    mine = place()
    odd = lax.rem(plane(), 2)
    beside[:, width:] = jnp.ones((beside.shape[0], width), beside.dtype)
    for edge, base in ((edge_a, RADIUS * (1 - odd)), (edge_b, RADIUS * odd)):
        for j in range(RADIUS):
            beside[pl.ds(pl.multiple_of((base + j) * rows, rows), rows), :width] = edge[j, :rows]

    def one(b, _):
        at = pl.ds(pl.multiple_of(b * rows, rows), rows)
        near = [
            pl.ds(pl.multiple_of((b + c) * rows, rows), rows) for c in range(RADIUS)
        ]
        old = peaks[1, b]
        peak, mixed = attend(
            stacked_ask(plane_keys[0, at, :width], plane_keys[0, at, width:]),
            old,
            [keys[c] for c in near],
            [beside[c] for c in near],
        )
        factor = jnp.exp(old - peak)
        mixed += sums[1, b] * jnp.concatenate([factor, factor], axis=1)
        mean = by_head(mixed[:, :width], rows) / by_head(mixed[:, width:], rows)
        whole[b] = mean.astype(whole.dtype)
        return _

    lax.fori_loop(0, GROUP, one, 0)
    for k in range(GROUP):
        outs[k][...] = whole[mine ^ k]


def merge_kernel(back_a, back_b, peaks, sums, *refs):
    outs, (backs, whole) = refs[-GROUP - 2 : -2], refs[-2:]
    rows, width = outs[0].shape
    mine = place()
    odd = lax.rem(plane(), 2)
    backs[1 - odd] = back_a[...]
    backs[odd] = back_b[...]
    lane = lax.broadcasted_iota(jnp.int32, (width, width), 1)

    def logs(side, j):
        squares = []
        for part in range(rows // width):
            at = rows + part * STAT_ROWS
            stats = backs[side, j, at : at + STAT_ROWS].astype(jnp.float32)
            heads = [
                stats[8 * h : 8 * h + 1] + stats[8 * h + 1 : 8 * h + 2] + stats[8 * h + 2 : 8 * h + 3]
                for h in range(width // HEAD)
            ]
            turned = jnp.transpose(
                jnp.concatenate([jnp.broadcast_to(x, (HEAD, width)) for x in heads], axis=0)
            )
            squares.append(turned)
        return jnp.concatenate(squares, axis=0)

    for b in range(GROUP):
        theirs = []
        if b < RADIUS:
            theirs.append((0, b))
        if b >= GROUP - RADIUS:
            theirs.append((1, b - (GROUP - RADIUS)))
        theirs = [(logs(*t), backs[t[0], t[1], :rows].astype(jnp.float32)) for t in theirs]
        old = by_head(peaks[0, b], rows)
        top = old
        for log, _ in theirs:
            top = jnp.maximum(top, log)
        factor = jnp.exp(old - top)
        value = by_head(sums[0, b, :, :width], rows) * factor
        total = by_head(sums[0, b, :, width:], rows) * factor
        for log, mean in theirs:
            weight = jnp.exp(log - top)
            value += weight * mean
            total += weight
        whole[b] = (value / total).astype(whole.dtype)
    for k in range(GROUP):
        outs[k][...] = whole[mine ^ k]


def local(audio_frames, video_frames, recording, audio_query, video_key):
    rows, half = audio_frames.shape
    width = half // GROUP
    heads = width // HEAD
    length = lax.axis_size("tm")
    bf16, f32 = jnp.bfloat16, jnp.float32
    shape = jax.ShapeDtypeStruct
    assert length % (2 * GROUP) == 0

    def swapped(x):
        return lax.ppermute(x, "head", [(0, 1), (1, 0)])

    def traded(pieces):
        pairs = lambda k: [(i, i ^ k) for i in range(length)]
        return [pieces[0]] + [lax.ppermute(pieces[k], "tm", pairs(k)) for k in range(1, GROUP)]

    def partner(i, second):
        spot, inside = divmod(i, GROUP)
        spot = ((spot + second) ^ 1) - second
        return min(max(spot, 0), length // GROUP - 1) * GROUP + inside

    def crossed(sent):
        return [
            lax.ppermute(sent[s], "tm", [(i, partner(i, s)) for i in range(length)])
            for s in range(2)
        ]

    part = shape((rows, half), f32)
    square = shape((half, half), bf16)
    columns = shape((GROUP, rows, width), bf16)
    stream = shape((rows, half), bf16)
    given = (audio_frames, video_frames, audio_query, video_key, recording.reshape(rows // width, width))
    other_audio = swapped(audio_frames)
    query_part, key_part, query_rest, key_rest, audio_columns, video_columns, _, video_copy, ids = call(
        prepare_kernel,
        [part, part, square, square, columns, columns, stream, stream]
        + [shape((ID_ROWS, width), bf16)],
        [pltpu.VMEM((half, half), bf16)] * 2
        + [pltpu.VMEM((rows // width, width), jnp.int32), pltpu.VMEM((ID_ROWS, width), f32)]
        + [pltpu.SemaphoreType.DMA((7 + 2 * GROUP,))],
        ins=[HBM] * 5,
        flops=4 * rows * half * half,
        moved=16 * half * half,
        name="prepare",
    )(*(pltpu.with_memory_space_constraint(x, pltpu.HBM) for x in given))

    def project(scale, pack_rows, *operands):
        first = len(operands) > 4
        return call(
            functools.partial(project_kernel, scale, first),
            [shape((pack_rows, width), bf16)] * GROUP + ([stream] if first else []),
            [pltpu.VMEM((rows, half), bf16)],
            flops=2 * rows * half * half,
            moved=2 * half * half + 6 * rows * half * 2,
            name="project",
        )(*operands)

    *audio, relay = project(
        HEAD**-0.5,
        2 * rows + ID_ROWS,
        query_part,
        other_audio,
        query_rest,
        audio_columns,
        ids,
        video_copy,
    )
    other_video = swapped(relay)
    audio = traded(audio)
    video = traded(project(1.0, 2 * rows, key_part, other_video, key_rest, video_columns))
    edge = shape((RADIUS, 2 * rows + ID_ROWS, width), bf16)
    edges = crossed(
        call(halo_kernel, [edge, edge], moved=20 * rows * width * 2, name="halo")(*audio)
    )

    inside, around = GROUP * rows, 2 * RADIUS * rows
    asked = shape((2, inside, 2 * width), bf16)
    peaks, sums, plane_keys, plane_beside = call(
        plane_kernel,
        [shape((2, GROUP, heads * rows, n * width), f32) for n in (1, 2)] + [asked, asked],
        flops=32 * GROUP * rows * inside * width,
        moved=8 * inside * width * 2,
        exps=4 * GROUP * rows * inside,
        name="plane",
    )(*audio, *video)
    back = shape((RADIUS, rows + rows // width * STAT_ROWS, width), bf16)
    lent_a, lent_b, keys = call(
        lend_kernel,
        [back, back, shape((around, 2 * width), bf16)],
        [pltpu.VMEM((2,) + back.shape, bf16)],
        flops=48 * RADIUS * GROUP * rows * rows * width,
        moved=8 * around * width * 2,
        exps=2 * RADIUS * GROUP * rows * rows,
        name="lend",
    )(*edges, plane_keys, plane_beside)
    backs = crossed([lent_a, lent_b])

    pieces = [shape((rows, width), bf16)] * GROUP
    video_pieces = call(
        edge_kernel,
        pieces,
        [pltpu.VMEM((around, 2 * width), bf16), pltpu.VMEM((GROUP, rows, width), bf16)],
        flops=48 * RADIUS * GROUP * rows * rows * width,
        moved=8 * around * width * 2,
        exps=2 * RADIUS * GROUP * rows * rows,
        name="edge",
    )(*edges, keys, plane_keys, peaks, sums)
    audio_pieces = call(
        merge_kernel,
        pieces,
        [pltpu.VMEM((2,) + back.shape, bf16), pltpu.VMEM((GROUP, rows, width), bf16)],
        moved=16 * inside * width,
        exps=4 * inside * width,
        ins=[VMEM] * 4 + [ANY],
        name="merge",
    )(*backs, peaks, sums, video_pieces[0])

    def join(pieces):
        return call(
            join_kernel, shape((rows, half), bf16), moved=2 * rows * half * 2, name="join"
        )(*traded(pieces))

    video_attended = join(video_pieces)
    audio_attended = join(audio_pieces)
    return (audio_attended, video_attended)


def solution(mesh):
    return jax.shard_map(
        local,
        mesh=mesh,
        in_specs=(P("tm", "head"), P("tm", "head"), P("tm"), P(None, "head"), P(None, "head")),
        out_specs=(P("tm", "head"), P("tm", "head")),
        check_vma=False,
    )
```

time: 63.5 us -> 56.5 us (0.89)
  waiting for transfers between devices: 16.1 us -> 10.1 us
  Pallas kernels: 25.2 us -> 21.6 us
  starting transfers between devices: 21 us -> 23.9 us
    ppermute x12, waiting for transfers between devices: 13.2 us -> 5.08 us  [traded(): lax.ppermute(pieces[k], 'tm', pairs(k))]
    ppermute x2, waiting for transfers between devices: 0.01 us -> 4.99 us  [swapped(): return lax.ppermute(x, 'head', [(0, 1), (1, 0)])]
    pallas_call x7 -> x8, Pallas kernels: 23.7 us -> 20.1 us  [the longest x1 8.44 us: local(): call(plane_kernel, [shape((2, GROUP, heads * rows, n * width), f32) for n...]
    ppermute x4, waiting for transfers between devices: 2.89 us -> 0.01 us  [crossed(): lax.ppermute(sent[s], 'tm', [(i, partner(i, s)) for i in range(length)])]
    ppermute x12, starting transfers between devices: 10.5 us -> 12.2 us  [traded(): lax.ppermute(pieces[k], 'tm', pairs(k))]
    ppermute x2, starting transfers between devices: 1.53 us -> 2.61 us  [swapped(): return lax.ppermute(x, 'head', [(0, 1), (1, 0)])]
  transfers between devices with their start and end apart: 18 -> 18, of which waited for: 7 -> 7; matrix products, arithmetic and copies ran while one was open for 0% -> 0% of each run, Pallas kernels for 28% -> 31%
where the time goes in v6:
time: 56.5 us; the launch traced here: 56.3 us
  starting transfers between devices  23.9 us (42%)
  Pallas kernels  21.6 us (38%)
  waiting for transfers between devices  10.1 us (18%)
  between operations  0.75 us (1%)
    ppermute x12, starting transfers between devices, traded(): lax.ppermute(pieces[k], 'tm', pairs(k))  12.2 us
    ppermute x4, starting transfers between devices, crossed(): lax.ppermute(sent[s], 'tm', [(i, partner(i, s)) for i in range(length)])  9.08 us
    pallas_call x1, Pallas kernels, local(): call(plane_kernel, [shape((2, GROUP, heads * rows, n * width), f32) for n...  8.44 us
    ppermute x12, waiting for transfers between devices, traded(): lax.ppermute(pieces[k], 'tm', pairs(k))  5.08 us
    ppermute x2, waiting for transfers between devices, swapped(): return lax.ppermute(x, 'head', [(0, 1), (1, 0)])  4.99 us
    pallas_call x1, Pallas kernels, local(): call(edge_kernel, pieces, [pltpu.VMEM((around, 2 * width), bf16), pltpu.V...  4.54 us
    pallas_call x1, Pallas kernels, local(): call(lend_kernel, [back, back, shape((around, 2 * width), bf16)], [pltpu....  2.99 us
    pallas_call x1, Pallas kernels, local(): call(prepare_kernel, [part, part, square, square, columns, columns, strea...  2.69 us
  transfers between devices with their start and end apart: 18, of which 7 were waited for; matrix products, arithmetic and copies ran while one was open for 0% of the time, Pallas kernels for 31%

profile of v6, /device:TPU:9, one launch (start us, length us, event | category | flops | bytes accessed | tf_op | source)
XLA Modules:
  0.0 56.3 jit_solution(6882340464608366718)
XLA Ops:
  0.6 1.3 %collective-permute-start = (bf16[256,512]{1,0:T(8,128)(2,1)}, bf16[256,512]{1,0:T(8,128)(2,1)S(1)}, u32[]{:S(2)}, u32[]{:S(2)}) collective-permute-start(bf16[256,512]{1,0:T(8,128)(2,1)} %audio.1), channel_id=1, source_target_pairs={{0,1},{1,0},{2,3},{3,2},{4,5},{5,4},{6,7},{7,6},{8,9},{9,8},{10,11... | collective-permute-start | bytes 786440 | tf_op jit(solution)/shard_map/ppermute | solution.py:357
  1.9 2.7 %prepare.1 = (f32[256,512]{1,0:T(8,128)S(1)}, f32[256,512]{1,0:T(8,128)S(1)}, bf16[512,512]{1,0:T(8,128)(2,1)S(1)}, bf16[512,512]{1,0:T(8,128)(2,1)S(1)}, bf16[4...) custom-call(bf16[256,512]{1,0:T(8,128)(2,1)} %audio.1, ...), custom_call_target="tpu_custom_call" | custom-call | flops 268435456 | bytes 4194304 | tf_op jit(solution)/shard_map/prepare/pallas_call | solution.py:380
  4.6 3.4 %collective-permute-done.other = bf16[256,512]{1,0:T(8,128)(2,1)S(1)} collective-permute-done((bf16[256,512]{1,0:T(8,128)(2,1)}, bf16[256,512]{1,0:T(8,128)(2,1)S(1)}, u32[]{:S(2)}, u32[]{:S(2)}) %collective-permute-start) | collective-permute-done | bytes 262176 | tf_op jit(solution)/shard_map/ppermute | solution.py:357
  8.1 0.4 project.2
  8.5 1.3 %collective-permute-start.6 = (bf16[256,512]{1,0:T(8,128)(2,1)S(1)}, bf16[256,512]{1,0:T(8,128)(2,1)S(1)}, u32[]{:S(2)}, u32[]{:S(2)}) collective-permute-start(bf16[256,512]{1,0:T(8,128)(2,1)S(1)} %get-tuple-element.48), channel_id=1, source_target_pairs={{0,1},{1,0},{2,3},{3,2},{4,5},{5,4},{6,7},{7,6},{8,9},{9,8},{10,11... | collective-permute-start | bytes 786440 | tf_op jit(solution)/shard_map/ppermute | solution.py:357
  9.8 1.8 %collective-permute-start.1 = (bf16[528,128]{1,0:T(8,128)(2,1)S(1)}, bf16[528,128]{1,0:T(8,128)(2,1)S(1)}, u32[]{:S(2)}, u32[]{:S(2)}) collective-permute-start(bf16[528,128]{1,0:T(8,128)(2,1)S(1)} %get-tuple-element.42), channel_id=1, source_target_pairs={{0,2},{2,0},{4,6},{6,4},{8,10},{10,8},{12,14},{14,12},{16,18},{18,... | collective-permute-start | bytes 405512 | tf_op jit(solution)/shard_map/ppermute | solution.py:361
  11.6 1.2 %collective-permute-start.2 = (bf16[528,128]{1,0:T(8,128)(2,1)S(1)}, bf16[528,128]{1,0:T(8,128)(2,1)S(1)}, u32[]{:S(2)}, u32[]{:S(2)}) collective-permute-start(bf16[528,128]{1,0:T(8,128)(2,1)S(1)} %get-tuple-element.43), channel_id=1, source_target_pairs={{0,4},{2,6},{4,0},{6,2},{8,12},{10,14},{12,8},{14,10},{16,20},{18,... | collective-permute-start | bytes 405512 | tf_op jit(solution)/shard_map/ppermute | solution.py:361
  12.8 0.4 collective-permute-start.3
  13.2 1.6 %collective-permute-done.6.other = bf16[256,512]{1,0:T(8,128)(2,1)S(1)} collective-permute-done((bf16[256,512]{1,0:T(8,128)(2,1)S(1)}, bf16[256,512]{1,0:T(8,128)(2,1)S(1)}, u32[]{:S(2)}, u32[]{:S(2)}) %collective-permute-start.6) | collective-permute-done | bytes 262176 | tf_op jit(solution)/shard_map/ppermute | solution.py:357
  14.8 0.4 project.3
  15.2 2.5 %collective-permute-start.7 = (bf16[512,128]{1,0:T(8,128)(2,1)S(1)}, bf16[512,128]{1,0:T(8,128)(2,1)S(1)}, u32[]{:S(2)}, u32[]{:S(2)}) collective-permute-start(bf16[512,128]{1,0:T(8,128)(2,1)S(1)} %get-tuple-element.52), channel_id=1, source_target_pairs={{0,2},{2,0},{4,6},{6,4},{8,10},{10,8},{12,14},{14,12},{16,18},{18,... | collective-permute-start | bytes 393224 | tf_op jit(solution)/shard_map/ppermute | solution.py:361
  17.7 1.2 %collective-permute-start.8 = (bf16[512,128]{1,0:T(8,128)(2,1)S(1)}, bf16[512,128]{1,0:T(8,128)(2,1)S(1)}, u32[]{:S(2)}, u32[]{:S(2)}) collective-permute-start(bf16[512,128]{1,0:T(8,128)(2,1)S(1)} %get-tuple-element.53), channel_id=1, source_target_pairs={{0,4},{2,6},{4,0},{6,2},{8,12},{10,14},{12,8},{14,10},{16,20},{18,... | collective-permute-start | bytes 393224 | tf_op jit(solution)/shard_map/ppermute | solution.py:361
  19.0 0.0 collective-permute-done.1.refs_1_
  19.0 0.5 collective-permute-start.9
  19.4 0.0 collective-permute-done.2.refs_2_
  19.4 0.4 collective-permute-done.3.refs_3_
  19.8 0.1 halo.1
  19.9 0.2 collective-permute-start.4
  20.1 4.3 %collective-permute-start.5 = (bf16[3,528,128]{2,1,0:T(8,128)(2,1)S(1)}, bf16[3,528,128]{2,1,0:T(8,128)(2,1)S(1)}, u32[]{:S(2)}, u32[]{:S(2)}) collective-permute-start(bf16[3,528,128]{2,1,0:T(8,128)(2,1)S(1)} %get-tuple-element.46), channel_id=1, source_target_pairs={{0,0},{2,2},{4,4},{6,6},{8,16},{10,18},{12,20},{14,22},{16,8},{18,... | collective-permute-start | bytes 1216520 | tf_op jit(solution)/shard_map/ppermute | solution.py:370
  24.5 0.0 collective-permute-done.7.refs_5_
  24.5 0.0 collective-permute-done.8.refs_6_
  24.5 1.6 %collective-permute-done.9.refs_7_ = bf16[512,128]{1,0:T(8,128)(2,1)S(1)} collective-permute-done((bf16[512,128]{1,0:T(8,128)(2,1)S(1)}, bf16[512,128]{1,0:T(8,128)(2,1)S(1)}, u32[]{:S(2)}, u32[]{:S(2)}) %collective-permute-start.9) | collective-permute-done | bytes 131104 | tf_op jit(solution)/shard_map/ppermute | solution.py:361
  26.1 8.4 %plane.1 = (f32[2,4,512,128]{3,2,1,0:T(8,128)S(1)}, f32[2,4,512,256]{3,2,1,0:T(8,128)S(1)}, bf16[2,1024,256]{2,1,0:T(8,128)(2,1)S(1)}, bf16[2,1024,256]{2,1,0:T(8,128)(2,1)S(1)}) custom-call(bf16[528,128]{1,0:T(8,128)(2,1)S(1)} %get-tuple-element.41.refs_0_, bf16[528,128]{1,0:T(8,128)(2,1)S(1)} %collective-permute-done.1.refs_1_, ...), custom_call_target="tpu_custom_call" | custom-call | flops 4294967296 | bytes 2097152 | tf_op jit(solution)/shard_map/plane/pallas_call | solution.py:424
  34.5 0.0 collective-permute-done.4.edge_a
  34.5 0.0 collective-permute-done.5.edge_b
  34.5 3.0 %lend.1 = (bf16[3,288,128]{2,1,0:T(8,128)(2,1)S(1)}, bf16[3,288,128]{2,1,0:T(8,128)(2,1)S(1)}, bf16[1536,256]{1,0:T(8,128)(2,1)S(1)}) custom-call(bf16[3,528,128]{2,1,0:T(8,128)(2,1)S(1)} %collective-permute-done.4.edge_a, bf16[3,528,128]{2,1,0:T(8,128)(2,1)S(1)} %collective-permute-done.5.edge_b, bf16[2,1024,256]{2,1,0:T(8,128)(2,1)S(1)} %get-tuple-element.55.plane_keys, ...), custom_call_target="tpu_custom_call" | custom-call | flops 4831838208 | bytes 3145728 | tf_op jit(solution)/shard_map/lend/pallas_call | solution.py:433
  37.5 0.3 collective-permute-start.10
  37.9 4.2 %collective-permute-start.11 = (bf16[3,288,128]{2,1,0:T(8,128)(2,1)S(1)}, bf16[3,288,128]{2,1,0:T(8,128)(2,1)S(1)}, u32[]{:S(2)}, u32[]{:S(2)}) collective-permute-start(bf16[3,288,128]{2,1,0:T(8,128)(2,1)S(1)} %get-tuple-element.58), channel_id=1, source_target_pairs={{0,0},{2,2},{4,4},{6,6},{8,16},{10,18},{12,20},{14,22},{16,8},{18,... | collective-permute-start | bytes 663560 | tf_op jit(solution)/shard_map/ppermute | solution.py:370
  42.1 4.5 %edge.1 = (bf16[256,128]{1,0:T(8,128)(2,1)S(1)}, bf16[256,128]{1,0:T(8,128)(2,1)S(1)}, bf16[256,128]{1,0:T(8,128)(2,1)S(1)}, bf16[256,128]{1,0:T(8,128)(2,1)S(1)}) custom-call(bf16[3,528,128]{2,1,0:T(8,128)(2,1)S(1)} %collective-permute-done.4.edge_a, bf16[3,528,128]{2,1,0:T(8,128)(2,1)S(1)} %collective-permute-done.5.edge_b, ...), custom_call_target="tpu_custom_call" | custom-call | flops 4831838208 | bytes 3145728 | tf_op jit(solution)/shard_map/edge/pallas_call | solution.py:445
  46.6 0.6 %collective-permute-start.15 = (bf16[256,128]{1,0:T(8,128)(2,1)S(1)}, bf16[256,128]{1,0:T(8,128)(2,1)S(1)}, u32[]{:S(2)}, u32[]{:S(2)}) collective-permute-start(bf16[256,128]{1,0:T(8,128)(2,1)S(1)} %get-tuple-element.67), channel_id=1, source_target_pairs={{0,2},{2,0},{4,6},{6,4},{8,10},{10,8},{12,14},{14,12},{16,18},{18,... | collective-permute-start | bytes 196616 | tf_op jit(solution)/shard_map/ppermute | solution.py:361
  47.2 1.2 %collective-permute-start.16 = (bf16[256,128]{1,0:T(8,128)(2,1)S(1)}, bf16[256,128]{1,0:T(8,128)(2,1)S(1)}, u32[]{:S(2)}, u32[]{:S(2)}) collective-permute-start(bf16[256,128]{1,0:T(8,128)(2,1)S(1)} %get-tuple-element.68), channel_id=1, source_target_pairs={{0,4},{2,6},{4,0},{6,2},{8,12},{10,14},{12,8},{14,10},{16,20},{18,... | collective-permute-start | bytes 196616 | tf_op jit(solution)/shard_map/ppermute | solution.py:361
  48.4 0.5 collective-permute-start.17
  48.9 0.0 collective-permute-done.10.back_a
  48.9 0.0 collective-permute-done.11.back_b
  48.9 0.5 merge.1
  49.4 0.2 collective-permute-start.12
  49.7 1.2 %collective-permute-start.13 = (bf16[256,128]{1,0:T(8,128)(2,1)S(1)}, bf16[256,128]{1,0:T(8,128)(2,1)S(1)}, u32[]{:S(2)}, u32[]{:S(2)}) collective-permute-start(bf16[256,128]{1,0:T(8,128)(2,1)S(1)} %get-tuple-element.65), channel_id=1, source_target_pairs={{0,4},{2,6},{4,0},{6,2},{8,12},{10,14},{12,8},{14,10},{16,20},{18,... | collective-permute-start | bytes 196616 | tf_op jit(solution)/shard_map/ppermute | solution.py:361
  50.9 0.0 collective-permute-done.15.refs_1_
  50.9 0.7 %collective-permute-start.14 = (bf16[256,128]{1,0:T(8,128)(2,1)S(1)}, bf16[256,128]{1,0:T(8,128)(2,1)S(1)}, u32[]{:S(2)}, u32[]{:S(2)}) collective-permute-start(bf16[256,128]{1,0:T(8,128)(2,1)S(1)} %get-tuple-element.66), channel_id=1, source_target_pairs={{0,6},{2,4},{4,2},{6,0},{8,14},{10,12},{12,10},{14,8},{16,22},{18,... | collective-permute-start | bytes 196616 | tf_op jit(solution)/shard_map/ppermute | solution.py:361
  51.7 0.0 collective-permute-done.16.refs_2_
  51.7 1.1 %collective-permute-done.17.refs_3_ = bf16[256,128]{1,0:T(8,128)(2,1)S(1)} collective-permute-done((bf16[256,128]{1,0:T(8,128)(2,1)S(1)}, bf16[256,128]{1,0:T(8,128)(2,1)S(1)}, u32[]{:S(2)}, u32[]{:S(2)}) %collective-permute-start.17) | collective-permute-done | bytes 65568 | tf_op jit(solution)/shard_map/ppermute | solution.py:361
  52.8 0.8 %join.3 = bf16[256,512]{1,0:T(8,128)(2,1)} custom-call(bf16[256,128]{1,0:T(8,128)(2,1)S(1)} %get-tuple-element.62.refs_0_, bf16[256,128]{1,0:T(8,128)(2,1)S(1)} %collective-permute-done.15.refs_1_, bf16[256,128]{1,0:T(8,128)(2,1)S(1)} %collective-permute-done.16.refs_2_, bf16[256,128]{1,0:T(8,128)(2,1)S(1)} %collective-permute-done.17.refs_3_), custom_call_target="tpu_custom_call" | custom-call | bytes 524288 | tf_op jit(solution)/shard_map/join/pallas_call | solution.py:465
  53.6 0.0 collective-permute-done.12.refs_1_
  53.6 0.1 collective-permute-done.13.refs_2_
  53.7 1.9 %collective-permute-done.14.refs_3_ = bf16[256,128]{1,0:T(8,128)(2,1)S(1)} collective-permute-done((bf16[256,128]{1,0:T(8,128)(2,1)S(1)}, bf16[256,128]{1,0:T(8,128)(2,1)S(1)}, u32[]{:S(2)}, u32[]{:S(2)}) %collective-permute-start.14) | collective-permute-done | bytes 65568 | tf_op jit(solution)/shard_map/ppermute | solution.py:361
  55.5 0.8 %join.2 = bf16[256,512]{1,0:T(8,128)(2,1)} custom-call(bf16[256,128]{1,0:T(8,128)(2,1)S(1)} %get-tuple-element.63.refs_0_, bf16[256,128]{1,0:T(8,128)(2,1)S(1)} %collective-permute-done.12.refs_1_, bf16[256,128]{1,0:T(8,128)(2,1)S(1)} %collective-permute-done.13.refs_2_, bf16[256,128]{1,0:T(8,128)(2,1)S(1)} %collective-permute-done.14.refs_3_), custom_call_target="tpu_custom_call" | custom-call | bytes 524288 | tf_op jit(solution)/shard_map/join/pallas_call | solution.py:465
Async XLA Ops:
  0.6 7.5 %collective-permute-start = (bf16[256,512]{1,0:T(8,128)(2,1)}, bf16[256,512]{1,0:T(8,128)(2,1)S(1)}, u32[]{:S(2)}, u32[]{:S(2)}) collective-permute-start(bf16[256,512]{1,0:T(8,128)(2,1)} %audio.1), channel_id=1, source_target_pairs={{0,1},{1,0},{2,3},{3,2},{4,5},{5,4},{6,7},{7,6},{8,9},{9,8},{10,11... | collective-permute-start | bytes 786440 | tf_op jit(solution)/shard_map/ppermute | solution.py:357
  8.5 6.3 %collective-permute-start.6 = (bf16[256,512]{1,0:T(8,128)(2,1)S(1)}, bf16[256,512]{1,0:T(8,128)(2,1)S(1)}, u32[]{:S(2)}, u32[]{:S(2)}) collective-permute-start(bf16[256,512]{1,0:T(8,128)(2,1)S(1)} %get-tuple-element.48), channel_id=1, source_target_pairs={{0,1},{1,0},{2,3},{3,2},{4,5},{5,4},{6,7},{7,6},{8,9},{9,8},{10,11... | collective-permute-start | bytes 786440 | tf_op jit(solution)/shard_map/ppermute | solution.py:357
  9.8 9.2 %collective-permute-start.1 = (bf16[528,128]{1,0:T(8,128)(2,1)S(1)}, bf16[528,128]{1,0:T(8,128)(2,1)S(1)}, u32[]{:S(2)}, u32[]{:S(2)}) collective-permute-start(bf16[528,128]{1,0:T(8,128)(2,1)S(1)} %get-tuple-element.42), channel_id=1, source_target_pairs={{0,2},{2,0},{4,6},{6,4},{8,10},{10,8},{12,14},{14,12},{16,18},{18,... | collective-permute-start | bytes 405512 | tf_op jit(solution)/shard_map/ppermute | solution.py:361
  11.6 7.8 %collective-permute-start.2 = (bf16[528,128]{1,0:T(8,128)(2,1)S(1)}, bf16[528,128]{1,0:T(8,128)(2,1)S(1)}, u32[]{:S(2)}, u32[]{:S(2)}) collective-permute-start(bf16[528,128]{1,0:T(8,128)(2,1)S(1)} %get-tuple-element.43), channel_id=1, source_target_pairs={{0,4},{2,6},{4,0},{6,2},{8,12},{10,14},{12,8},{14,10},{16,20},{18,... | collective-permute-start | bytes 405512 | tf_op jit(solution)/shard_map/ppermute | solution.py:361
  12.8 7.0 %collective-permute-start.3 = (bf16[528,128]{1,0:T(8,128)(2,1)S(1)}, bf16[528,128]{1,0:T(8,128)(2,1)S(1)}, u32[]{:S(2)}, u32[]{:S(2)}) collective-permute-start(bf16[528,128]{1,0:T(8,128)(2,1)S(1)} %get-tuple-element.44), channel_id=1, source_target_pairs={{0,6},{2,4},{4,2},{6,0},{8,14},{10,12},{12,10},{14,8},{16,22},{18,... | collective-permute-start | bytes 405512 | tf_op jit(solution)/shard_map/ppermute | solution.py:361
  15.2 9.3 %collective-permute-start.7 = (bf16[512,128]{1,0:T(8,128)(2,1)S(1)}, bf16[512,128]{1,0:T(8,128)(2,1)S(1)}, u32[]{:S(2)}, u32[]{:S(2)}) collective-permute-start(bf16[512,128]{1,0:T(8,128)(2,1)S(1)} %get-tuple-element.52), channel_id=1, source_target_pairs={{0,2},{2,0},{4,6},{6,4},{8,10},{10,8},{12,14},{14,12},{16,18},{18,... | collective-permute-start | bytes 393224 | tf_op jit(solution)/shard_map/ppermute | solution.py:361
  17.7 6.8 %collective-permute-start.8 = (bf16[512,128]{1,0:T(8,128)(2,1)S(1)}, bf16[512,128]{1,0:T(8,128)(2,1)S(1)}, u32[]{:S(2)}, u32[]{:S(2)}) collective-permute-start(bf16[512,128]{1,0:T(8,128)(2,1)S(1)} %get-tuple-element.53), channel_id=1, source_target_pairs={{0,4},{2,6},{4,0},{6,2},{8,12},{10,14},{12,8},{14,10},{16,20},{18,... | collective-permute-start | bytes 393224 | tf_op jit(solution)/shard_map/ppermute | solution.py:361
  19.0 7.1 %collective-permute-start.9 = (bf16[512,128]{1,0:T(8,128)(2,1)S(1)}, bf16[512,128]{1,0:T(8,128)(2,1)S(1)}, u32[]{:S(2)}, u32[]{:S(2)}) collective-permute-start(bf16[512,128]{1,0:T(8,128)(2,1)S(1)} %get-tuple-element.54), channel_id=1, source_target_pairs={{0,6},{2,4},{4,2},{6,0},{8,14},{10,12},{12,10},{14,8},{16,22},{18,... | collective-permute-start | bytes 393224 | tf_op jit(solution)/shard_map/ppermute | solution.py:361
  19.9 14.6 %collective-permute-start.4 = (bf16[3,528,128]{2,1,0:T(8,128)(2,1)S(1)}, bf16[3,528,128]{2,1,0:T(8,128)(2,1)S(1)}, u32[]{:S(2)}, u32[]{:S(2)}) collective-permute-start(bf16[3,528,128]{2,1,0:T(8,128)(2,1)S(1)} %get-tuple-element.45), channel_id=1, source_target_pairs={{0,8},{2,10},{4,12},{6,14},{8,0},{10,2},{12,4},{14,6},{16,24},{18,... | collective-permute-start | bytes 1216520 | tf_op jit(solution)/shard_map/ppermute | solution.py:370
  20.1 14.4 %collective-permute-start.5 = (bf16[3,528,128]{2,1,0:T(8,128)(2,1)S(1)}, bf16[3,528,128]{2,1,0:T(8,128)(2,1)S(1)}, u32[]{:S(2)}, u32[]{:S(2)}) collective-permute-start(bf16[3,528,128]{2,1,0:T(8,128)(2,1)S(1)} %get-tuple-element.46), channel_id=1, source_target_pairs={{0,0},{2,2},{4,4},{6,6},{8,16},{10,18},{12,20},{14,22},{16,8},{18,... | collective-permute-start | bytes 1216520 | tf_op jit(solution)/shard_map/ppermute | solution.py:370
  37.5 11.4 %collective-permute-start.10 = (bf16[3,288,128]{2,1,0:T(8,128)(2,1)S(1)}, bf16[3,288,128]{2,1,0:T(8,128)(2,1)S(1)}, u32[]{:S(2)}, u32[]{:S(2)}) collective-permute-start(bf16[3,288,128]{2,1,0:T(8,128)(2,1)S(1)} %get-tuple-element.57), channel_id=1, source_target_pairs={{0,8},{2,10},{4,12},{6,14},{8,0},{10,2},{12,4},{14,6},{16,24},{18,... | collective-permute-start | bytes 663560 | tf_op jit(solution)/shard_map/ppermute | solution.py:370
  37.9 11.0 %collective-permute-start.11 = (bf16[3,288,128]{2,1,0:T(8,128)(2,1)S(1)}, bf16[3,288,128]{2,1,0:T(8,128)(2,1)S(1)}, u32[]{:S(2)}, u32[]{:S(2)}) collective-permute-start(bf16[3,288,128]{2,1,0:T(8,128)(2,1)S(1)} %get-tuple-element.58), channel_id=1, source_target_pairs={{0,0},{2,2},{4,4},{6,6},{8,16},{10,18},{12,20},{14,22},{16,8},{18,... | collective-permute-start | bytes 663560 | tf_op jit(solution)/shard_map/ppermute | solution.py:370
  46.6 4.3 %collective-permute-start.15 = (bf16[256,128]{1,0:T(8,128)(2,1)S(1)}, bf16[256,128]{1,0:T(8,128)(2,1)S(1)}, u32[]{:S(2)}, u32[]{:S(2)}) collective-permute-start(bf16[256,128]{1,0:T(8,128)(2,1)S(1)} %get-tuple-element.67), channel_id=1, source_target_pairs={{0,2},{2,0},{4,6},{6,4},{8,10},{10,8},{12,14},{14,12},{16,18},{18,... | collective-permute-start | bytes 196616 | tf_op jit(solution)/shard_map/ppermute | solution.py:361
  47.2 4.5 %collective-permute-start.16 = (bf16[256,128]{1,0:T(8,128)(2,1)S(1)}, bf16[256,128]{1,0:T(8,128)(2,1)S(1)}, u32[]{:S(2)}, u32[]{:S(2)}) collective-permute-start(bf16[256,128]{1,0:T(8,128)(2,1)S(1)} %get-tuple-element.68), channel_id=1, source_target_pairs={{0,4},{2,6},{4,0},{6,2},{8,12},{10,14},{12,8},{14,10},{16,20},{18,... | collective-permute-start | bytes 196616 | tf_op jit(solution)/shard_map/ppermute | solution.py:361
  48.4 4.4 %collective-permute-start.17 = (bf16[256,128]{1,0:T(8,128)(2,1)S(1)}, bf16[256,128]{1,0:T(8,128)(2,1)S(1)}, u32[]{:S(2)}, u32[]{:S(2)}) collective-permute-start(bf16[256,128]{1,0:T(8,128)(2,1)S(1)} %get-tuple-element.69), channel_id=1, source_target_pairs={{0,6},{2,4},{4,2},{6,0},{8,14},{10,12},{12,10},{14,8},{16,22},{18,... | collective-permute-start | bytes 196616 | tf_op jit(solution)/shard_map/ppermute | solution.py:361
  49.4 4.1 %collective-permute-start.12 = (bf16[256,128]{1,0:T(8,128)(2,1)S(1)}, bf16[256,128]{1,0:T(8,128)(2,1)S(1)}, u32[]{:S(2)}, u32[]{:S(2)}) collective-permute-start(bf16[256,128]{1,0:T(8,128)(2,1)S(1)} %get-tuple-element.64), channel_id=1, source_target_pairs={{0,2},{2,0},{4,6},{6,4},{8,10},{10,8},{12,14},{14,12},{16,18},{18,... | collective-permute-start | bytes 196616 | tf_op jit(solution)/shard_map/ppermute | solution.py:361
  49.7 4.0 %collective-permute-start.13 = (bf16[256,128]{1,0:T(8,128)(2,1)S(1)}, bf16[256,128]{1,0:T(8,128)(2,1)S(1)}, u32[]{:S(2)}, u32[]{:S(2)}) collective-permute-start(bf16[256,128]{1,0:T(8,128)(2,1)S(1)} %get-tuple-element.65), channel_id=1, source_target_pairs={{0,4},{2,6},{4,0},{6,2},{8,12},{10,14},{12,8},{14,10},{16,20},{18,... | collective-permute-start | bytes 196616 | tf_op jit(solution)/shard_map/ppermute | solution.py:361
  50.9 4.6 %collective-permute-start.14 = (bf16[256,128]{1,0:T(8,128)(2,1)S(1)}, bf16[256,128]{1,0:T(8,128)(2,1)S(1)}, u32[]{:S(2)}, u32[]{:S(2)}) collective-permute-start(bf16[256,128]{1,0:T(8,128)(2,1)S(1)} %get-tuple-element.66), channel_id=1, source_target_pairs={{0,6},{2,4},{4,2},{6,0},{8,14},{10,12},{12,10},{14,8},{16,22},{18,... | collective-permute-start | bytes 196616 | tf_op jit(solution)/shard_map/ppermute | solution.py:361

commit v7 on v6

v7 whole, which is shorter than its diff:
```python
import functools

import jax
import jax.numpy as jnp
from jax import lax
from jax.experimental import pallas as pl
from jax.experimental.pallas import tpu as pltpu
from jax.sharding import PartitionSpec as P

HEAD = 64
RADIUS = 3
GROUP = 4
NEG = -1e30
ID_ROWS = 16
STAT_ROWS = 16

VMEM = pl.BlockSpec(memory_space=pltpu.VMEM)
ANY = pl.BlockSpec(memory_space=pl.ANY)
HBM = pl.BlockSpec(memory_space=pltpu.HBM)


def place():
    return lax.rem(lax.axis_index("tm"), GROUP)


def plane():
    return lax.axis_index("tm") // GROUP


def call(kernel, outs, scratch=(), ins=None, flops=0, moved=0, exps=0, name=None):
    return pl.pallas_call(
        kernel,
        out_shape=outs,
        **({"in_specs": ins} if ins else {}),
        scratch_shapes=scratch,
        compiler_params=pltpu.CompilerParams(vmem_limit_bytes=32 * 2**20),
        cost_estimate=pl.CostEstimate(flops=flops, bytes_accessed=moved, transcendentals=exps),
        name=name,
    )


def prepare_kernel(audio, video, query, key, ids, *refs):
    sums, seconds, sent, packs = refs[:2], refs[2:4], refs[4], refs[5 : 5 + GROUP]
    own, firsts, ids_in, ids_wide, sems = refs[9], refs[10:12], refs[12], refs[13], refs[14]
    rows, half = audio.shape
    width = packs[0].shape[1]
    side = lax.axis_index("head")
    mine = place()
    copies = []

    def fetch(source, target):
        copies.append(pltpu.make_async_copy(source, target, sems.at[len(copies)]))
        copies[-1].start()

    ours = pl.ds(pl.multiple_of(side * half, half), half)
    theirs = pl.ds(pl.multiple_of((1 - side) * half, half), half)
    fetch(ids, ids_in)
    fetch(audio, own)
    fetch(video, sent)
    for i, weight in enumerate((query, key)):
        fetch(weight.at[ours], firsts[i])
    for i, stream in enumerate((audio, video)):
        for k in range(GROUP):
            at = pl.ds(pl.multiple_of((mine ^ k) * width, width), width)
            fetch(stream.at[:, at], packs[k].at[i * rows : (i + 1) * rows])
    for i, weight in enumerate((query, key)):
        fetch(weight.at[theirs], seconds[i])
    for copy in copies[:5]:
        copy.wait()
    for i, stream in enumerate((own, sent)):
        sums[i][...] = jnp.dot(stream[...], firsts[i][...], preferred_element_type=jnp.float32)
    ids_wide[...] = jnp.zeros_like(ids_wide)
    ids_wide[: ids_in.shape[0]] = (ids_in[...] + 1).astype(jnp.float32)
    for k in range(GROUP):
        packs[k][2 * rows :] = ids_wide[...].astype(packs[k].dtype)
    for copy in copies[5:]:
        copy.wait()


def project_kernel(scale, part, other, weight, *refs):
    pieces, full = refs[-GROUP - 1 : -1], refs[-1]
    width = pieces[0].shape[1]
    mine = place()
    total = part[...] + jnp.dot(other[...], weight[...], preferred_element_type=jnp.float32)
    full[...] = total.astype(jnp.bfloat16) * jnp.bfloat16(scale)
    for k in range(GROUP):
        pieces[k][...] = full[:, pl.ds(pl.multiple_of((mine ^ k) * width, width), width)]


def halo_kernel(*refs):
    values, queries, (first, second) = refs[:GROUP], refs[GROUP : 2 * GROUP], refs[-2:]
    rows = queries[0].shape[0]
    mine = place()
    odd = lax.rem(plane(), 2)
    for k in range(GROUP):
        block = mine ^ k
        for out, skip in ((first, (GROUP - RADIUS) * (1 - odd)), (second, (GROUP - RADIUS) * odd)):
            spot = block - skip

            @pl.when((spot >= 0) & (spot < RADIUS))
            def _():
                out[spot, :rows] = values[k][:rows]
                out[spot, rows : 2 * rows] = queries[k][...]
                out[spot, 2 * rows :] = values[k][2 * rows :]

    last = lax.axis_size("tm") // GROUP - 1

    @pl.when((plane() == 0) | (plane() == last))
    def _():
        second[:, second.shape[1] - ID_ROWS :] = jnp.zeros(
            (RADIUS, ID_ROWS, second.shape[2]), second.dtype
        )


def join_kernel(*refs):
    pieces, out = refs[:GROUP], refs[GROUP]
    width = pieces[0].shape[1]
    mine = place()
    for k in range(GROUP):
        out[:, pl.ds(pl.multiple_of((mine ^ k) * width, width), width)] = pieces[k][...]


def marks_turned(lanes):
    lanes = lanes.astype(jnp.float32)
    width = lanes.shape[1]
    row = lax.broadcasted_iota(jnp.int32, (width, width), 0).astype(jnp.float32)
    return [
        jnp.where(row == lanes[part : part + 1], 1.0, 0.0).astype(jnp.bfloat16) for part in range(2)
    ]


def stacked_ask(block, turned):
    head = lax.broadcasted_iota(jnp.int32, block.shape, 1) // HEAD
    marks = jnp.concatenate([jnp.transpose(x) for x in turned], axis=0)
    beside = (marks - jnp.bfloat16(1.0)) * jnp.bfloat16(-NEG)
    return jnp.concatenate(
        [
            jnp.concatenate([jnp.where(head == h, block, jnp.zeros_like(block)), beside], axis=1)
            for h in range(block.shape[1] // HEAD)
        ],
        axis=0,
    )


def by_head(stacked, rows):
    out = stacked[:rows]
    head = lax.broadcasted_iota(jnp.int32, out.shape, 1) // HEAD
    for h in range(1, stacked.shape[0] // rows):
        out = jnp.where(head == h, stacked[h * rows : (h + 1) * rows], out)
    return out


def product(a, b):
    return jnp.dot(a, b, preferred_element_type=jnp.float32)


def attend(scores, old, values):
    width = values.shape[1] // 2
    top = old
    for at in range(0, scores.shape[1], width):
        part = scores[:, at : at + width]
        top = part if top is None else jnp.maximum(top, part)
    peak = jnp.max(top, axis=1, keepdims=True)
    return peak, product(jnp.exp(scores - peak).astype(jnp.bfloat16), values)


def plane_kernel(*refs):
    packs, queries, keys = refs[:GROUP], refs[GROUP : 2 * GROUP], refs[2 * GROUP : 3 * GROUP]
    peaks, sums, turned, beside, asks = refs[3 * GROUP :]
    rows, width = keys[0].shape
    mine = place()
    beside[:, :, width:] = jnp.ones((2, GROUP * rows, width), beside.dtype)
    for k in range(GROUP):
        b = mine ^ k

        def spot(at, size):
            return pl.ds(pl.multiple_of(b * rows + at, size), size)

        marks = marks_turned(packs[k][2 * rows :])
        for i, (ask, key) in enumerate(((queries, keys), (keys, queries))):
            asks[i, b] = stacked_ask(ask[k][...], marks)
            beside[i, spot(0, rows), :width] = packs[k][(1 - i) * rows : (2 - i) * rows]
            for part, x in enumerate(marks):
                at = spot(part * width, width)
                turned[i, :width, at] = jnp.transpose(key[k][part * width : (part + 1) * width])
                turned[i, width:, at] = x

    def one(b, _):
        scores = [product(asks[i, b], turned[i]) for i in range(2)]
        for i in range(2):
            peak, sums[i, b] = attend(scores[i], None, beside[i])
            peaks[i, b] = jnp.broadcast_to(peak, (peak.shape[0], width))
        return _

    lax.fori_loop(0, GROUP, one, 0)


def lend_kernel(edge_a, edge_b, plane_turned, plane_beside, first, second, turned, ordered, results):
    rows, width = (ordered.shape[2] - ID_ROWS) // 2, ordered.shape[3]
    odd = lax.rem(plane(), 2)
    ordered[1 - odd] = edge_a[...]
    ordered[odd] = edge_b[...]
    lane = lax.broadcasted_iota(jnp.int32, (rows, width), 1)
    for e in range(2 * RADIUS):
        side, j = e // RADIUS, e % RADIUS
        marks = marks_turned(ordered[side, j, 2 * rows :])
        query = ordered[side, j, rows : 2 * rows]
        for part, x in enumerate(marks):
            at = slice(e * rows + part * width, e * rows + (part + 1) * width)
            turned[:width, at] = jnp.transpose(query[part * width : (part + 1) * width])
            turned[width:, at] = x
        blocks = slice((j + 1) * rows, GROUP * rows) if side else slice(0, (j + 1) * rows)
        scores = product(stacked_ask(query, marks), plane_turned[0, :, blocks])
        peak, mixed = attend(scores, None, plane_beside[0, blocks])
        mean = by_head(mixed[:, :width], rows) / by_head(mixed[:, width:], rows)
        results[side, j, :rows] = mean.astype(results.dtype)
        logs = peak + jnp.log(mixed[:, width:])
        high = logs.astype(jnp.bfloat16)
        rest = logs - high.astype(jnp.float32)
        middle = rest.astype(jnp.bfloat16)
        low = (rest - middle.astype(jnp.float32)).astype(jnp.bfloat16)
        picked = jnp.zeros((rows, width), jnp.bfloat16)
        for h in range(width // HEAD):
            for n, piece in enumerate((high, middle, low)):
                picked = jnp.where(lane == 8 * h + n, piece[h * rows : (h + 1) * rows], picked)
        for part in range(rows // width):
            stats = jnp.transpose(picked[part * width : (part + 1) * width])
            at = rows + part * STAT_ROWS
            results[side, j, at : at + STAT_ROWS] = stats[:STAT_ROWS]
    first[...] = results[1 - odd]
    second[...] = results[odd]


def edge_kernel(edge_a, edge_b, turned, asks, peaks, sums, *refs):
    outs, (beside, whole) = refs[-GROUP - 2 : -2], refs[-2:]
    rows, width = outs[0].shape
    mine = place()
    odd = lax.rem(plane(), 2)
    beside[:, width:] = jnp.ones((beside.shape[0], width), beside.dtype)
    for edge, base in ((edge_a, RADIUS * (1 - odd)), (edge_b, RADIUS * odd)):
        for j in range(RADIUS):
            beside[pl.ds(pl.multiple_of((base + j) * rows, rows), rows), :width] = edge[j, :rows]
    near = [slice(b * rows, (b + RADIUS) * rows) for b in range(GROUP)]
    scores = product(asks[1, 0], turned[:, near[0]])
    for b in range(GROUP):
        following = product(asks[1, b + 1], turned[:, near[b + 1]]) if b + 1 < GROUP else None
        old = peaks[1, b]
        peak, mixed = attend(scores, old, beside[near[b]])
        factor = jnp.exp(old - peak)
        mixed += sums[1, b] * jnp.concatenate([factor, factor], axis=1)
        mean = by_head(mixed[:, :width], rows) / by_head(mixed[:, width:], rows)
        whole[b] = mean.astype(whole.dtype)
        scores = following
    for k in range(GROUP):
        outs[k][...] = whole[mine ^ k]


def merge_kernel(back_a, back_b, peaks, sums, *refs):
    outs, (backs, whole) = refs[-GROUP - 2 : -2], refs[-2:]
    rows, width = outs[0].shape
    mine = place()
    odd = lax.rem(plane(), 2)
    backs[1 - odd] = back_a[...]
    backs[odd] = back_b[...]
    lane = lax.broadcasted_iota(jnp.int32, (width, width), 1)

    def logs(side, j):
        squares = []
        for part in range(rows // width):
            at = rows + part * STAT_ROWS
            stats = backs[side, j, at : at + STAT_ROWS].astype(jnp.float32)
            heads = [
                stats[8 * h : 8 * h + 1] + stats[8 * h + 1 : 8 * h + 2] + stats[8 * h + 2 : 8 * h + 3]
                for h in range(width // HEAD)
            ]
            turned = jnp.transpose(
                jnp.concatenate([jnp.broadcast_to(x, (HEAD, width)) for x in heads], axis=0)
            )
            squares.append(turned)
        return jnp.concatenate(squares, axis=0)

    for b in range(GROUP):
        theirs = []
        if b < RADIUS:
            theirs.append((0, b))
        if b >= GROUP - RADIUS:
            theirs.append((1, b - (GROUP - RADIUS)))
        theirs = [(logs(*t), backs[t[0], t[1], :rows].astype(jnp.float32)) for t in theirs]
        old = by_head(peaks[0, b], rows)
        top = old
        for log, _ in theirs:
            top = jnp.maximum(top, log)
        factor = jnp.exp(old - top)
        value = by_head(sums[0, b, :, :width], rows) * factor
        total = by_head(sums[0, b, :, width:], rows) * factor
        for log, mean in theirs:
            weight = jnp.exp(log - top)
            value += weight * mean
            total += weight
        whole[b] = (value / total).astype(whole.dtype)
    for k in range(GROUP):
        outs[k][...] = whole[mine ^ k]


def local(audio_frames, video_frames, recording, audio_query, video_key):
    rows, half = audio_frames.shape
    width = half // GROUP
    heads = width // HEAD
    length = lax.axis_size("tm")
    bf16, f32 = jnp.bfloat16, jnp.float32
    shape = jax.ShapeDtypeStruct
    assert length % (2 * GROUP) == 0

    def swapped(x):
        return lax.ppermute(x, "head", [(0, 1), (1, 0)])

    def traded(pieces):
        pairs = lambda k: [(i, i ^ k) for i in range(length)]
        return [pieces[0]] + [lax.ppermute(pieces[k], "tm", pairs(k)) for k in range(1, GROUP)]

    def partner(i, second):
        spot, inside = divmod(i, GROUP)
        spot = ((spot + second) ^ 1) - second
        return min(max(spot, 0), length // GROUP - 1) * GROUP + inside

    def crossed(sent):
        return [
            lax.ppermute(sent[s], "tm", [(i, partner(i, s)) for i in range(length)])
            for s in range(2)
        ]

    part = shape((rows, half), f32)
    square = shape((half, half), bf16)
    stream = shape((rows, half), bf16)
    piece = shape((rows, width), bf16)
    given = (audio_frames, video_frames, audio_query, video_key, recording.reshape(rows // width, width))
    other_audio = swapped(audio_frames)
    query_part, key_part, query_rest, key_rest, video_copy, *packs = call(
        prepare_kernel,
        [part, part, square, square, stream] + [shape((2 * rows + ID_ROWS, width), bf16)] * GROUP,
        [pltpu.VMEM((rows, half), bf16)]
        + [pltpu.VMEM((half, half), bf16)] * 2
        + [pltpu.VMEM((rows // width, width), jnp.int32), pltpu.VMEM((ID_ROWS, width), f32)]
        + [pltpu.SemaphoreType.DMA((7 + 2 * GROUP,))],
        ins=[HBM] * 5,
        flops=4 * rows * half * half,
        moved=16 * half * half,
        name="prepare",
    )(*(pltpu.with_memory_space_constraint(x, pltpu.HBM) for x in given))

    def project(scale, *operands):
        return call(
            functools.partial(project_kernel, scale),
            [piece] * GROUP,
            [pltpu.VMEM((rows, half), bf16)],
            ins=[VMEM] * 3 + [ANY] * (len(operands) - 3),
            flops=2 * rows * half * half,
            moved=2 * half * half + 6 * rows * half * 2,
            name="project",
        )(*operands)

    packs = traded(packs)
    other_video = swapped(video_copy)
    queries = project(HEAD**-0.5, query_part, other_audio, query_rest, *packs[1:])
    queries = traded(queries)
    keys = project(1.0, key_part, other_video, key_rest)
    edge = shape((RADIUS, 2 * rows + ID_ROWS, width), bf16)
    edges = crossed(
        call(
            halo_kernel,
            [edge, edge],
            ins=[VMEM] * (2 * GROUP) + [ANY],
            moved=20 * rows * width * 2,
            name="halo",
        )(*packs, *queries, keys[0])
    )
    keys = traded(keys)

    inside, around = GROUP * rows, 2 * RADIUS * rows
    peaks, sums, plane_turned, plane_beside, asks = call(
        plane_kernel,
        [shape((2, GROUP, heads * rows, n * width), f32) for n in (1, 2)]
        + [shape((2, 2 * width, inside), bf16), shape((2, inside, 2 * width), bf16)]
        + [shape((2, GROUP, heads * rows, 2 * width), bf16)],
        flops=32 * GROUP * rows * inside * width,
        moved=8 * inside * width * 2,
        exps=4 * GROUP * rows * inside,
        name="plane",
    )(*packs, *queries, *keys)
    back = shape((RADIUS, rows + rows // width * STAT_ROWS, width), bf16)
    lent_a, lent_b, edge_turned = call(
        lend_kernel,
        [back, back, shape((2 * width, around), bf16)],
        [pltpu.VMEM((2,) + edge.shape, bf16), pltpu.VMEM((2,) + back.shape, bf16)],
        flops=48 * RADIUS * GROUP * rows * rows * width,
        moved=8 * around * width * 2,
        exps=2 * RADIUS * GROUP * rows * rows,
        name="lend",
    )(*edges, plane_turned, plane_beside)
    backs = crossed([lent_a, lent_b])

    video_pieces = call(
        edge_kernel,
        [piece] * GROUP,
        [pltpu.VMEM((around, 2 * width), bf16), pltpu.VMEM((GROUP, rows, width), bf16)],
        flops=48 * RADIUS * GROUP * rows * rows * width,
        moved=8 * around * width * 2,
        exps=2 * RADIUS * GROUP * rows * rows,
        name="edge",
    )(*edges, edge_turned, asks, peaks, sums)
    audio_pieces = call(
        merge_kernel,
        [piece] * GROUP,
        [pltpu.VMEM((2,) + back.shape, bf16), pltpu.VMEM((GROUP, rows, width), bf16)],
        moved=16 * inside * width,
        exps=4 * inside * width,
        ins=[VMEM] * 4 + [ANY],
        name="merge",
    )(*backs, peaks, sums, video_pieces[0])

    def join(pieces):
        return call(
            join_kernel, shape((rows, half), bf16), moved=2 * rows * half * 2, name="join"
        )(*traded(pieces))

    video_attended = join(video_pieces)
    audio_attended = join(audio_pieces)
    return (audio_attended, video_attended)


def solution(mesh):
    return jax.shard_map(
        local,
        mesh=mesh,
        in_specs=(P("tm", "head"), P("tm", "head"), P("tm"), P(None, "head"), P(None, "head")),
        out_specs=(P("tm", "head"), P("tm", "head")),
        check_vma=False,
    )
```

time: 56.5 us -> 54.2 us (0.959)
  Pallas kernels: 21.6 us -> 17.8 us
  waiting for transfers between devices: 10.1 us -> 13 us
  starting transfers between devices: 23.9 us -> 22.4 us
    ppermute x12 -> x15, waiting for transfers between devices: 5.08 us -> 11.3 us  [traded(): lax.ppermute(pieces[k], 'tm', pairs(k))]
    ppermute x2, waiting for transfers between devices: 4.99 us -> 0.01 us  [swapped(): return lax.ppermute(x, 'head', [(0, 1), (1, 0)])]
    pallas_call x7, Pallas kernels: 11.6 us -> 8.97 us  [the longest x1 3.06 us: local(): call(lend_kernel, [back, back, shape((2 * width, around), bf16)], [pltpu....]
    ppermute x4, waiting for transfers between devices: 0.01 us -> 1.72 us  [crossed(): lax.ppermute(sent[s], 'tm', [(i, partner(i, s)) for i in range(length)])]
    ppermute x4, starting transfers between devices: 9.08 us -> 7.66 us  [crossed(): lax.ppermute(sent[s], 'tm', [(i, partner(i, s)) for i in range(length)])]
    pallas_call x1, Pallas kernels: 8.44 us -> 7.3 us  [local(): call(plane_kernel, [shape((2, GROUP, heads * rows, n * width), f32) for n...]
    ppermute x2, starting transfers between devices: 2.61 us -> 1.6 us  [swapped(): return lax.ppermute(x, 'head', [(0, 1), (1, 0)])]
    ppermute x12 -> x15, starting transfers between devices: 12.2 us -> 13.2 us  [traded(): lax.ppermute(pieces[k], 'tm', pairs(k))]
  transfers between devices with their start and end apart: 18 -> 21, of which waited for: 7 -> 7; matrix products, arithmetic and copies ran while one was open for 0% -> 0% of each run, Pallas kernels for 31% -> 26%
where the time goes in v7:
time: 54.2 us; the launch traced here: 54 us
  starting transfers between devices  22.4 us (41%)
  Pallas kernels  17.8 us (33%)
  waiting for transfers between devices  13 us (24%)
  between operations  0.78 us (1%)
    ppermute x15, starting transfers between devices, traded(): lax.ppermute(pieces[k], 'tm', pairs(k))  13.2 us
    ppermute x15, waiting for transfers between devices, traded(): lax.ppermute(pieces[k], 'tm', pairs(k))  11.3 us
    ppermute x4, starting transfers between devices, crossed(): lax.ppermute(sent[s], 'tm', [(i, partner(i, s)) for i in range(length)])  7.66 us
    pallas_call x1, Pallas kernels, local(): call(plane_kernel, [shape((2, GROUP, heads * rows, n * width), f32) for n...  7.3 us
    pallas_call x1, Pallas kernels, local(): call(lend_kernel, [back, back, shape((2 * width, around), bf16)], [pltpu....  3.06 us
    pallas_call x1, Pallas kernels, local(): call(edge_kernel, [piece] * GROUP, [pltpu.VMEM((around, 2 * width), bf16)...  2.53 us
    pallas_call x1, Pallas kernels, local(): call(prepare_kernel, [part, part, square, square, stream] + [shape((2 * r...  1.99 us
    ppermute x4, waiting for transfers between devices, crossed(): lax.ppermute(sent[s], 'tm', [(i, partner(i, s)) for i in range(length)])  1.72 us
  transfers between devices with their start and end apart: 21, of which 7 were waited for; matrix products, arithmetic and copies ran while one was open for 0% of the time, Pallas kernels for 26%

profile of v7, /device:TPU:9, one launch (start us, length us, event | category | flops | bytes accessed | tf_op | source)
XLA Modules:
  0.0 54.0 jit_solution(16146413367658548195)
XLA Ops:
  0.6 1.3 %collective-permute-start.3 = (bf16[256,512]{1,0:T(8,128)(2,1)}, bf16[256,512]{1,0:T(8,128)(2,1)S(1)}, u32[]{:S(2)}, u32[]{:S(2)}) collective-permute-start(bf16[256,512]{1,0:T(8,128)(2,1)} %audio.1), channel_id=1, source_target_pairs={{0,1},{1,0},{2,3},{3,2},{4,5},{5,4},{6,7},{7,6},{8,9},{9,8},{10,11... | collective-permute-start | bytes 786440 | tf_op jit(solution)/shard_map/ppermute | solution.py:315
  1.9 2.0 %prepare.1 = (f32[256,512]{1,0:T(8,128)S(1)}, f32[256,512]{1,0:T(8,128)S(1)}, bf16[512,512]{1,0:T(8,128)(2,1)S(1)}, bf16[512,512]{1,0:T(8,128)(2,1)S(1)}, bf16[2...) custom-call(bf16[256,512]{1,0:T(8,128)(2,1)} %audio.1, ...), custom_call_target="tpu_custom_call" | custom-call | flops 268435456 | bytes 4194304 | tf_op jit(solution)/shard_map/prepare/pallas_call | solution.py:338
  3.9 0.3 collective-permute-start.7
  4.2 1.2 %collective-permute-start = (bf16[528,128]{1,0:T(8,128)(2,1)S(1)}, bf16[528,128]{1,0:T(8,128)(2,1)S(1)}, u32[]{:S(2)}, u32[]{:S(2)}) collective-permute-start(bf16[528,128]{1,0:T(8,128)(2,1)S(1)} %get-tuple-element.38), channel_id=1, source_target_pairs={{0,2},{2,0},{4,6},{6,4},{8,10},{10,8},{12,14},{14,12},{16,18},{18,... | collective-permute-start | bytes 405512 | tf_op jit(solution)/shard_map/ppermute | solution.py:319
  5.5 1.2 %collective-permute-start.1 = (bf16[528,128]{1,0:T(8,128)(2,1)S(1)}, bf16[528,128]{1,0:T(8,128)(2,1)S(1)}, u32[]{:S(2)}, u32[]{:S(2)}) collective-permute-start(bf16[528,128]{1,0:T(8,128)(2,1)S(1)} %get-tuple-element.39), channel_id=1, source_target_pairs={{0,4},{2,6},{4,0},{6,2},{8,12},{10,14},{12,8},{14,10},{16,20},{18,... | collective-permute-start | bytes 405512 | tf_op jit(solution)/shard_map/ppermute | solution.py:319
  6.7 0.4 collective-permute-start.2
  7.1 0.0 collective-permute-done.refs_0_.refs_1_
  7.1 3.6 %collective-permute-done.1.refs_1_.refs_2_ = bf16[528,128]{1,0:T(8,128)(2,1)S(1)} collective-permute-done((bf16[528,128]{1,0:T(8,128)(2,1)S(1)}, bf16[528,128]{1,0:T(8,128)(2,1)S(1)}, u32[]{:S(2)}, u32[]{:S(2)}) %collective-permute-start.1) | collective-permute-done | bytes 135200 | tf_op jit(solution)/shard_map/ppermute | solution.py:319
  10.7 3.3 %collective-permute-done.2.refs_2_.refs_3_ = bf16[528,128]{1,0:T(8,128)(2,1)S(1)} collective-permute-done((bf16[528,128]{1,0:T(8,128)(2,1)S(1)}, bf16[528,128]{1,0:T(8,128)(2,1)S(1)}, u32[]{:S(2)}, u32[]{:S(2)}) %collective-permute-start.2) | collective-permute-done | bytes 135200 | tf_op jit(solution)/shard_map/ppermute | solution.py:319
  14.0 0.0 collective-permute-done.3.other
  14.0 0.4 project.2
  14.4 0.1 collective-permute-start.4
  14.4 1.3 %collective-permute-start.5 = (bf16[256,128]{1,0:T(8,128)(2,1)S(1)}, bf16[256,128]{1,0:T(8,128)(2,1)S(1)}, u32[]{:S(2)}, u32[]{:S(2)}) collective-permute-start(bf16[256,128]{1,0:T(8,128)(2,1)S(1)} %get-tuple-element.45), channel_id=1, source_target_pairs={{0,4},{2,6},{4,0},{6,2},{8,12},{10,14},{12,8},{14,10},{16,20},{18,... | collective-permute-start | bytes 196616 | tf_op jit(solution)/shard_map/ppermute | solution.py:319
  15.7 0.8 %collective-permute-start.6 = (bf16[256,128]{1,0:T(8,128)(2,1)S(1)}, bf16[256,128]{1,0:T(8,128)(2,1)S(1)}, u32[]{:S(2)}, u32[]{:S(2)}) collective-permute-start(bf16[256,128]{1,0:T(8,128)(2,1)S(1)} %get-tuple-element.46), channel_id=1, source_target_pairs={{0,6},{2,4},{4,2},{6,0},{8,14},{10,12},{12,10},{14,8},{16,22},{18,... | collective-permute-start | bytes 196616 | tf_op jit(solution)/shard_map/ppermute | solution.py:319
  16.6 0.0 collective-permute-done.7.other
  16.6 0.4 project.3
  16.9 0.1 collective-permute-start.10
  17.0 1.3 %collective-permute-start.11 = (bf16[256,128]{1,0:T(8,128)(2,1)S(1)}, bf16[256,128]{1,0:T(8,128)(2,1)S(1)}, u32[]{:S(2)}, u32[]{:S(2)}) collective-permute-start(bf16[256,128]{1,0:T(8,128)(2,1)S(1)} %get-tuple-element.54), channel_id=1, source_target_pairs={{0,4},{2,6},{4,0},{6,2},{8,12},{10,14},{12,8},{14,10},{16,20},{18,... | collective-permute-start | bytes 196616 | tf_op jit(solution)/shard_map/ppermute | solution.py:319
  18.3 0.0 collective-permute-done.4.refs_5_
  18.3 0.8 %collective-permute-start.12 = (bf16[256,128]{1,0:T(8,128)(2,1)S(1)}, bf16[256,128]{1,0:T(8,128)(2,1)S(1)}, u32[]{:S(2)}, u32[]{:S(2)}) collective-permute-start(bf16[256,128]{1,0:T(8,128)(2,1)S(1)} %get-tuple-element.55), channel_id=1, source_target_pairs={{0,6},{2,4},{4,2},{6,0},{8,14},{10,12},{12,10},{14,8},{16,22},{18,... | collective-permute-start | bytes 196616 | tf_op jit(solution)/shard_map/ppermute | solution.py:319
  19.2 0.0 collective-permute-done.5.refs_6_
  19.2 1.2 %collective-permute-done.6.refs_7_ = bf16[256,128]{1,0:T(8,128)(2,1)S(1)} collective-permute-done((bf16[256,128]{1,0:T(8,128)(2,1)S(1)}, bf16[256,128]{1,0:T(8,128)(2,1)S(1)}, u32[]{:S(2)}, u32[]{:S(2)}) %collective-permute-start.6) | collective-permute-done | bytes 65568 | tf_op jit(solution)/shard_map/ppermute | solution.py:319
  20.4 0.1 halo.1
  20.5 0.2 collective-permute-start.8
  20.7 4.3 %collective-permute-start.9 = (bf16[3,528,128]{2,1,0:T(8,128)(2,1)S(1)}, bf16[3,528,128]{2,1,0:T(8,128)(2,1)S(1)}, u32[]{:S(2)}, u32[]{:S(2)}) collective-permute-start(bf16[3,528,128]{2,1,0:T(8,128)(2,1)S(1)} %get-tuple-element.52), channel_id=1, source_target_pairs={{0,0},{2,2},{4,4},{6,6},{8,16},{10,18},{12,20},{14,22},{16,8},{18,... | collective-permute-start | bytes 1216520 | tf_op jit(solution)/shard_map/ppermute | solution.py:328
  25.0 0.0 collective-permute-done.10.refs_9_
  25.0 0.0 collective-permute-done.11.refs_10_
  25.1 0.0 collective-permute-done.12.refs_11_
  25.1 7.3 %plane.1 = (f32[2,4,512,128]{3,2,1,0:T(8,128)S(1)}, f32[2,4,512,256]{3,2,1,0:T(8,128)S(1)}, bf16[2,256,1024]{2,1,0:T(8,128)(2,1)S(1)}, bf16[2,1024,256]{2,1,0:T(8,128)(2,1)S(1)}, bf16[2,4,512,256]{3,2,1,0:T(8,128)(2,1)S(1)}) custom-call(bf16[528,128]{1,0:T(8,128)(2,1)S(1)} %get-tuple-element.37.refs_0_, ...), custom_call_target="tpu_custom_call" | custom-call | flops 4294967296 | bytes 2097152 | tf_op jit(solution)/shard_map/plane/pallas_call | solution.py:380
  32.4 0.0 collective-permute-done.8.edge_a
  32.4 1.7 %collective-permute-done.9.edge_b = bf16[3,528,128]{2,1,0:T(8,128)(2,1)S(1)} collective-permute-done((bf16[3,528,128]{2,1,0:T(8,128)(2,1)S(1)}, bf16[3,528,128]{2,1,0:T(8,128)(2,1)S(1)}, u32[]{:S(2)}, u32[]{:S(2)}) %collective-permute-start.9) | collective-permute-done | bytes 405536 | tf_op jit(solution)/shard_map/ppermute | solution.py:328
  34.1 3.1 %lend.1 = (bf16[3,288,128]{2,1,0:T(8,128)(2,1)S(1)}, bf16[3,288,128]{2,1,0:T(8,128)(2,1)S(1)}, bf16[256,1536]{1,0:T(8,128)(2,1)S(1)}) custom-call(bf16[3,528,128]{2,1,0:T(8,128)(2,1)S(1)} %collective-permute-done.8.edge_a, bf16[3,528,128]{2,1,0:T(8,128)(2,1)S(1)} %collective-permute-done.9.edge_b, bf16[2,256,1024]{2,1,0:T(8,128)(2,1)S(1)} %get-tuple-element.56.plane_turned, ...), custom_call_target="tpu_custom_call" | custom-call | flops 4831838208 | bytes 3145728 | tf_op jit(solution)/shard_map/lend/pallas_call | solution.py:391
  37.2 0.0 collective-permute-start.13
  37.2 3.1 %collective-permute-start.14 = (bf16[3,288,128]{2,1,0:T(8,128)(2,1)S(1)}, bf16[3,288,128]{2,1,0:T(8,128)(2,1)S(1)}, u32[]{:S(2)}, u32[]{:S(2)}) collective-permute-start(bf16[3,288,128]{2,1,0:T(8,128)(2,1)S(1)} %get-tuple-element.59), channel_id=1, source_target_pairs={{0,0},{2,2},{4,4},{6,6},{8,16},{10,18},{12,20},{14,22},{16,8},{18,... | collective-permute-start | bytes 663560 | tf_op jit(solution)/shard_map/ppermute | solution.py:328
  40.3 2.5 %edge.1 = (bf16[256,128]{1,0:T(8,128)(2,1)S(1)}, bf16[256,128]{1,0:T(8,128)(2,1)S(1)}, bf16[256,128]{1,0:T(8,128)(2,1)S(1)}, bf16[256,128]{1,0:T(8,128)(2,1)S(1)}) custom-call(bf16[3,528,128]{2,1,0:T(8,128)(2,1)S(1)} %collective-permute-done.8.edge_a, bf16[3,528,128]{2,1,0:T(8,128)(2,1)S(1)} %collective-permute-done.9.edge_b, ...), custom_call_target="tpu_custom_call" | custom-call | flops 4831838208 | bytes 3145728 | tf_op jit(solution)/shard_map/edge/pallas_call | solution.py:402
  42.8 1.9 %collective-permute-start.18 = (bf16[256,128]{1,0:T(8,128)(2,1)S(1)}, bf16[256,128]{1,0:T(8,128)(2,1)S(1)}, u32[]{:S(2)}, u32[]{:S(2)}) collective-permute-start(bf16[256,128]{1,0:T(8,128)(2,1)S(1)} %get-tuple-element.69), channel_id=1, source_target_pairs={{0,2},{2,0},{4,6},{6,4},{8,10},{10,8},{12,14},{14,12},{16,18},{18,... | collective-permute-start | bytes 196616 | tf_op jit(solution)/shard_map/ppermute | solution.py:319
  44.7 1.0 %collective-permute-start.19 = (bf16[256,128]{1,0:T(8,128)(2,1)S(1)}, bf16[256,128]{1,0:T(8,128)(2,1)S(1)}, u32[]{:S(2)}, u32[]{:S(2)}) collective-permute-start(bf16[256,128]{1,0:T(8,128)(2,1)S(1)} %get-tuple-element.70), channel_id=1, source_target_pairs={{0,4},{2,6},{4,0},{6,2},{8,12},{10,14},{12,8},{14,10},{16,20},{18,... | collective-permute-start | bytes 196616 | tf_op jit(solution)/shard_map/ppermute | solution.py:319
  45.7 0.7 %collective-permute-start.20 = (bf16[256,128]{1,0:T(8,128)(2,1)S(1)}, bf16[256,128]{1,0:T(8,128)(2,1)S(1)}, u32[]{:S(2)}, u32[]{:S(2)}) collective-permute-start(bf16[256,128]{1,0:T(8,128)(2,1)S(1)} %get-tuple-element.71), channel_id=1, source_target_pairs={{0,6},{2,4},{4,2},{6,0},{8,14},{10,12},{12,10},{14,8},{16,22},{18,... | collective-permute-start | bytes 196616 | tf_op jit(solution)/shard_map/ppermute | solution.py:319
  46.4 0.0 collective-permute-done.13.back_a
  46.5 0.0 collective-permute-done.14.back_b
  46.5 0.5 %merge.1 = (bf16[256,128]{1,0:T(8,128)(2,1)S(1)}, bf16[256,128]{1,0:T(8,128)(2,1)S(1)}, bf16[256,128]{1,0:T(8,128)(2,1)S(1)}, bf16[256,128]{1,0:T(8,128)(2,1)S(1)}) custom-call(bf16[3,288,128]{2,1,0:T(8,128)(2,1)S(1)} %collective-permute-done.13.back_a, bf16[3,288,128]{2,1,0:T(8,128)(2,1)S(1)} %collective-permute-done.14.back_b, ...), custom_call_target="tpu_custom_call" | custom-call | bytes 2097152 | tf_op jit(solution)/shard_map/merge/pallas_call | solution.py:411
  47.0 0.5 collective-permute-start.15
  47.5 1.7 %collective-permute-start.16 = (bf16[256,128]{1,0:T(8,128)(2,1)S(1)}, bf16[256,128]{1,0:T(8,128)(2,1)S(1)}, u32[]{:S(2)}, u32[]{:S(2)}) collective-permute-start(bf16[256,128]{1,0:T(8,128)(2,1)S(1)} %get-tuple-element.67), channel_id=1, source_target_pairs={{0,4},{2,6},{4,0},{6,2},{8,12},{10,14},{12,8},{14,10},{16,20},{18,... | collective-permute-start | bytes 196616 | tf_op jit(solution)/shard_map/ppermute | solution.py:319
  49.2 0.0 collective-permute-done.18.refs_1_
  49.2 0.0 collective-permute-start.17
  49.3 0.0 collective-permute-done.19.refs_2_
  49.3 0.8 %collective-permute-done.20.refs_3_ = bf16[256,128]{1,0:T(8,128)(2,1)S(1)} collective-permute-done((bf16[256,128]{1,0:T(8,128)(2,1)S(1)}, bf16[256,128]{1,0:T(8,128)(2,1)S(1)}, u32[]{:S(2)}, u32[]{:S(2)}) %collective-permute-start.20) | collective-permute-done | bytes 65568 | tf_op jit(solution)/shard_map/ppermute | solution.py:319
  50.0 0.8 %join.3 = bf16[256,512]{1,0:T(8,128)(2,1)} custom-call(bf16[256,128]{1,0:T(8,128)(2,1)S(1)} %get-tuple-element.64.refs_0_, bf16[256,128]{1,0:T(8,128)(2,1)S(1)} %collective-permute-done.18.refs_1_, bf16[256,128]{1,0:T(8,128)(2,1)S(1)} %collective-permute-done.19.refs_2_, bf16[256,128]{1,0:T(8,128)(2,1)S(1)} %collective-permute-done.20.refs_3_), custom_call_target="tpu_custom_call" | custom-call | bytes 524288 | tf_op jit(solution)/shard_map/join/pallas_call | solution.py:422
  50.8 0.0 collective-permute-done.15.refs_1_
  50.8 0.7 %collective-permute-done.16.refs_2_ = bf16[256,128]{1,0:T(8,128)(2,1)S(1)} collective-permute-done((bf16[256,128]{1,0:T(8,128)(2,1)S(1)}, bf16[256,128]{1,0:T(8,128)(2,1)S(1)}, u32[]{:S(2)}, u32[]{:S(2)}) %collective-permute-start.16) | collective-permute-done | bytes 65568 | tf_op jit(solution)/shard_map/ppermute | solution.py:319
  51.5 1.8 %collective-permute-done.17.refs_3_ = bf16[256,128]{1,0:T(8,128)(2,1)S(1)} collective-permute-done((bf16[256,128]{1,0:T(8,128)(2,1)S(1)}, bf16[256,128]{1,0:T(8,128)(2,1)S(1)}, u32[]{:S(2)}, u32[]{:S(2)}) %collective-permute-start.17) | collective-permute-done | bytes 65568 | tf_op jit(solution)/shard_map/ppermute | solution.py:319
  53.3 0.8 %join.2 = bf16[256,512]{1,0:T(8,128)(2,1)} custom-call(bf16[256,128]{1,0:T(8,128)(2,1)S(1)} %get-tuple-element.65.refs_0_, bf16[256,128]{1,0:T(8,128)(2,1)S(1)} %collective-permute-done.15.refs_1_, bf16[256,128]{1,0:T(8,128)(2,1)S(1)} %collective-permute-done.16.refs_2_, bf16[256,128]{1,0:T(8,128)(2,1)S(1)} %collective-permute-done.17.refs_3_), custom_call_target="tpu_custom_call" | custom-call | bytes 524288 | tf_op jit(solution)/shard_map/join/pallas_call | solution.py:422
Async XLA Ops:
  0.6 13.3 %collective-permute-start.3 = (bf16[256,512]{1,0:T(8,128)(2,1)}, bf16[256,512]{1,0:T(8,128)(2,1)S(1)}, u32[]{:S(2)}, u32[]{:S(2)}) collective-permute-start(bf16[256,512]{1,0:T(8,128)(2,1)} %audio.1), channel_id=1, source_target_pairs={{0,1},{1,0},{2,3},{3,2},{4,5},{5,4},{6,7},{7,6},{8,9},{9,8},{10,11... | collective-permute-start | bytes 786440 | tf_op jit(solution)/shard_map/ppermute | solution.py:315
  3.9 12.6 %collective-permute-start.7 = (bf16[256,512]{1,0:T(8,128)(2,1)S(1)}, bf16[256,512]{1,0:T(8,128)(2,1)S(1)}, u32[]{:S(2)}, u32[]{:S(2)}) collective-permute-start(bf16[256,512]{1,0:T(8,128)(2,1)S(1)} %get-tuple-element.48), channel_id=1, source_target_pairs={{0,1},{1,0},{2,3},{3,2},{4,5},{5,4},{6,7},{7,6},{8,9},{9,8},{10,11... | collective-permute-start | bytes 786440 | tf_op jit(solution)/shard_map/ppermute | solution.py:315
  4.2 2.9 %collective-permute-start = (bf16[528,128]{1,0:T(8,128)(2,1)S(1)}, bf16[528,128]{1,0:T(8,128)(2,1)S(1)}, u32[]{:S(2)}, u32[]{:S(2)}) collective-permute-start(bf16[528,128]{1,0:T(8,128)(2,1)S(1)} %get-tuple-element.38), channel_id=1, source_target_pairs={{0,2},{2,0},{4,6},{6,4},{8,10},{10,8},{12,14},{14,12},{16,18},{18,... | collective-permute-start | bytes 405512 | tf_op jit(solution)/shard_map/ppermute | solution.py:319
  5.5 5.2 %collective-permute-start.1 = (bf16[528,128]{1,0:T(8,128)(2,1)S(1)}, bf16[528,128]{1,0:T(8,128)(2,1)S(1)}, u32[]{:S(2)}, u32[]{:S(2)}) collective-permute-start(bf16[528,128]{1,0:T(8,128)(2,1)S(1)} %get-tuple-element.39), channel_id=1, source_target_pairs={{0,4},{2,6},{4,0},{6,2},{8,12},{10,14},{12,8},{14,10},{16,20},{18,... | collective-permute-start | bytes 405512 | tf_op jit(solution)/shard_map/ppermute | solution.py:319
  6.7 7.3 %collective-permute-start.2 = (bf16[528,128]{1,0:T(8,128)(2,1)S(1)}, bf16[528,128]{1,0:T(8,128)(2,1)S(1)}, u32[]{:S(2)}, u32[]{:S(2)}) collective-permute-start(bf16[528,128]{1,0:T(8,128)(2,1)S(1)} %get-tuple-element.40), channel_id=1, source_target_pairs={{0,6},{2,4},{4,2},{6,0},{8,14},{10,12},{12,10},{14,8},{16,22},{18,... | collective-permute-start | bytes 405512 | tf_op jit(solution)/shard_map/ppermute | solution.py:319
  14.4 4.0 %collective-permute-start.4 = (bf16[256,128]{1,0:T(8,128)(2,1)S(1)}, bf16[256,128]{1,0:T(8,128)(2,1)S(1)}, u32[]{:S(2)}, u32[]{:S(2)}) collective-permute-start(bf16[256,128]{1,0:T(8,128)(2,1)S(1)} %get-tuple-element.44), channel_id=1, source_target_pairs={{0,2},{2,0},{4,6},{6,4},{8,10},{10,8},{12,14},{14,12},{16,18},{18,... | collective-permute-start | bytes 196616 | tf_op jit(solution)/shard_map/ppermute | solution.py:319
  14.4 4.7 %collective-permute-start.5 = (bf16[256,128]{1,0:T(8,128)(2,1)S(1)}, bf16[256,128]{1,0:T(8,128)(2,1)S(1)}, u32[]{:S(2)}, u32[]{:S(2)}) collective-permute-start(bf16[256,128]{1,0:T(8,128)(2,1)S(1)} %get-tuple-element.45), channel_id=1, source_target_pairs={{0,4},{2,6},{4,0},{6,2},{8,12},{10,14},{12,8},{14,10},{16,20},{18,... | collective-permute-start | bytes 196616 | tf_op jit(solution)/shard_map/ppermute | solution.py:319
  15.7 4.7 %collective-permute-start.6 = (bf16[256,128]{1,0:T(8,128)(2,1)S(1)}, bf16[256,128]{1,0:T(8,128)(2,1)S(1)}, u32[]{:S(2)}, u32[]{:S(2)}) collective-permute-start(bf16[256,128]{1,0:T(8,128)(2,1)S(1)} %get-tuple-element.46), channel_id=1, source_target_pairs={{0,6},{2,4},{4,2},{6,0},{8,14},{10,12},{12,10},{14,8},{16,22},{18,... | collective-permute-start | bytes 196616 | tf_op jit(solution)/shard_map/ppermute | solution.py:319
  16.9 8.1 %collective-permute-start.10 = (bf16[256,128]{1,0:T(8,128)(2,1)S(1)}, bf16[256,128]{1,0:T(8,128)(2,1)S(1)}, u32[]{:S(2)}, u32[]{:S(2)}) collective-permute-start(bf16[256,128]{1,0:T(8,128)(2,1)S(1)} %get-tuple-element.53), channel_id=1, source_target_pairs={{0,2},{2,0},{4,6},{6,4},{8,10},{10,8},{12,14},{14,12},{16,18},{18,... | collective-permute-start | bytes 196616 | tf_op jit(solution)/shard_map/ppermute | solution.py:319
  17.0 8.0 %collective-permute-start.11 = (bf16[256,128]{1,0:T(8,128)(2,1)S(1)}, bf16[256,128]{1,0:T(8,128)(2,1)S(1)}, u32[]{:S(2)}, u32[]{:S(2)}) collective-permute-start(bf16[256,128]{1,0:T(8,128)(2,1)S(1)} %get-tuple-element.54), channel_id=1, source_target_pairs={{0,4},{2,6},{4,0},{6,2},{8,12},{10,14},{12,8},{14,10},{16,20},{18,... | collective-permute-start | bytes 196616 | tf_op jit(solution)/shard_map/ppermute | solution.py:319
  18.3 6.7 %collective-permute-start.12 = (bf16[256,128]{1,0:T(8,128)(2,1)S(1)}, bf16[256,128]{1,0:T(8,128)(2,1)S(1)}, u32[]{:S(2)}, u32[]{:S(2)}) collective-permute-start(bf16[256,128]{1,0:T(8,128)(2,1)S(1)} %get-tuple-element.55), channel_id=1, source_target_pairs={{0,6},{2,4},{4,2},{6,0},{8,14},{10,12},{12,10},{14,8},{16,22},{18,... | collective-permute-start | bytes 196616 | tf_op jit(solution)/shard_map/ppermute | solution.py:319
  20.5 11.9 %collective-permute-start.8 = (bf16[3,528,128]{2,1,0:T(8,128)(2,1)S(1)}, bf16[3,528,128]{2,1,0:T(8,128)(2,1)S(1)}, u32[]{:S(2)}, u32[]{:S(2)}) collective-permute-start(bf16[3,528,128]{2,1,0:T(8,128)(2,1)S(1)} %get-tuple-element.51), channel_id=1, source_target_pairs={{0,8},{2,10},{4,12},{6,14},{8,0},{10,2},{12,4},{14,6},{16,24},{18,... | collective-permute-start | bytes 1216520 | tf_op jit(solution)/shard_map/ppermute | solution.py:328
  20.7 13.4 %collective-permute-start.9 = (bf16[3,528,128]{2,1,0:T(8,128)(2,1)S(1)}, bf16[3,528,128]{2,1,0:T(8,128)(2,1)S(1)}, u32[]{:S(2)}, u32[]{:S(2)}) collective-permute-start(bf16[3,528,128]{2,1,0:T(8,128)(2,1)S(1)} %get-tuple-element.52), channel_id=1, source_target_pairs={{0,0},{2,2},{4,4},{6,6},{8,16},{10,18},{12,20},{14,22},{16,8},{18,... | collective-permute-start | bytes 1216520 | tf_op jit(solution)/shard_map/ppermute | solution.py:328
  37.2 9.3 %collective-permute-start.13 = (bf16[3,288,128]{2,1,0:T(8,128)(2,1)S(1)}, bf16[3,288,128]{2,1,0:T(8,128)(2,1)S(1)}, u32[]{:S(2)}, u32[]{:S(2)}) collective-permute-start(bf16[3,288,128]{2,1,0:T(8,128)(2,1)S(1)} %get-tuple-element.58), channel_id=1, source_target_pairs={{0,8},{2,10},{4,12},{6,14},{8,0},{10,2},{12,4},{14,6},{16,24},{18,... | collective-permute-start | bytes 663560 | tf_op jit(solution)/shard_map/ppermute | solution.py:328
  37.2 9.3 %collective-permute-start.14 = (bf16[3,288,128]{2,1,0:T(8,128)(2,1)S(1)}, bf16[3,288,128]{2,1,0:T(8,128)(2,1)S(1)}, u32[]{:S(2)}, u32[]{:S(2)}) collective-permute-start(bf16[3,288,128]{2,1,0:T(8,128)(2,1)S(1)} %get-tuple-element.59), channel_id=1, source_target_pairs={{0,0},{2,2},{4,4},{6,6},{8,16},{10,18},{12,20},{14,22},{16,8},{18,... | collective-permute-start | bytes 663560 | tf_op jit(solution)/shard_map/ppermute | solution.py:328
  42.8 6.4 %collective-permute-start.18 = (bf16[256,128]{1,0:T(8,128)(2,1)S(1)}, bf16[256,128]{1,0:T(8,128)(2,1)S(1)}, u32[]{:S(2)}, u32[]{:S(2)}) collective-permute-start(bf16[256,128]{1,0:T(8,128)(2,1)S(1)} %get-tuple-element.69), channel_id=1, source_target_pairs={{0,2},{2,0},{4,6},{6,4},{8,10},{10,8},{12,14},{14,12},{16,18},{18,... | collective-permute-start | bytes 196616 | tf_op jit(solution)/shard_map/ppermute | solution.py:319
  44.7 4.5 %collective-permute-start.19 = (bf16[256,128]{1,0:T(8,128)(2,1)S(1)}, bf16[256,128]{1,0:T(8,128)(2,1)S(1)}, u32[]{:S(2)}, u32[]{:S(2)}) collective-permute-start(bf16[256,128]{1,0:T(8,128)(2,1)S(1)} %get-tuple-element.70), channel_id=1, source_target_pairs={{0,4},{2,6},{4,0},{6,2},{8,12},{10,14},{12,8},{14,10},{16,20},{18,... | collective-permute-start | bytes 196616 | tf_op jit(solution)/shard_map/ppermute | solution.py:319
  45.7 4.3 %collective-permute-start.20 = (bf16[256,128]{1,0:T(8,128)(2,1)S(1)}, bf16[256,128]{1,0:T(8,128)(2,1)S(1)}, u32[]{:S(2)}, u32[]{:S(2)}) collective-permute-start(bf16[256,128]{1,0:T(8,128)(2,1)S(1)} %get-tuple-element.71), channel_id=1, source_target_pairs={{0,6},{2,4},{4,2},{6,0},{8,14},{10,12},{12,10},{14,8},{16,22},{18,... | collective-permute-start | bytes 196616 | tf_op jit(solution)/shard_map/ppermute | solution.py:319
  47.0 3.8 %collective-permute-start.15 = (bf16[256,128]{1,0:T(8,128)(2,1)S(1)}, bf16[256,128]{1,0:T(8,128)(2,1)S(1)}, u32[]{:S(2)}, u32[]{:S(2)}) collective-permute-start(bf16[256,128]{1,0:T(8,128)(2,1)S(1)} %get-tuple-element.66), channel_id=1, source_target_pairs={{0,2},{2,0},{4,6},{6,4},{8,10},{10,8},{12,14},{14,12},{16,18},{18,... | collective-permute-start | bytes 196616 | tf_op jit(solution)/shard_map/ppermute | solution.py:319
  47.5 4.0 %collective-permute-start.16 = (bf16[256,128]{1,0:T(8,128)(2,1)S(1)}, bf16[256,128]{1,0:T(8,128)(2,1)S(1)}, u32[]{:S(2)}, u32[]{:S(2)}) collective-permute-start(bf16[256,128]{1,0:T(8,128)(2,1)S(1)} %get-tuple-element.67), channel_id=1, source_target_pairs={{0,4},{2,6},{4,0},{6,2},{8,12},{10,14},{12,8},{14,10},{16,20},{18,... | collective-permute-start | bytes 196616 | tf_op jit(solution)/shard_map/ppermute | solution.py:319
  49.2 4.0 %collective-permute-start.17 = (bf16[256,128]{1,0:T(8,128)(2,1)S(1)}, bf16[256,128]{1,0:T(8,128)(2,1)S(1)}, u32[]{:S(2)}, u32[]{:S(2)}) collective-permute-start(bf16[256,128]{1,0:T(8,128)(2,1)S(1)} %get-tuple-element.68), channel_id=1, source_target_pairs={{0,6},{2,4},{4,2},{6,0},{8,14},{10,12},{12,10},{14,8},{16,22},{18,... | collective-permute-start | bytes 196616 | tf_op jit(solution)/shard_map/ppermute | solution.py:319

commit v8 on v7

--- a/solution.py
+++ b/solution.py
@@ -27,11 +27,12 @@
     return lax.axis_index("tm") // GROUP
 
 
-def call(kernel, outs, scratch=(), ins=None, flops=0, moved=0, exps=0, name=None):
+def call(kernel, outs, scratch=(), ins=None, outs_in=None, flops=0, moved=0, exps=0, name=None):
     return pl.pallas_call(
         kernel,
         out_shape=outs,
         **({"in_specs": ins} if ins else {}),
+        **({"out_specs": outs_in} if outs_in else {}),
         scratch_shapes=scratch,
         compiler_params=pltpu.CompilerParams(vmem_limit_bytes=32 * 2**20),
         cost_estimate=pl.CostEstimate(flops=flops, bytes_accessed=moved, transcendentals=exps),
@@ -39,41 +40,56 @@
     )
 
 
-def prepare_kernel(audio, video, query, key, ids, *refs):
-    sums, seconds, sent, packs = refs[:2], refs[2:4], refs[4], refs[5 : 5 + GROUP]
-    own, firsts, ids_in, ids_wide, sems = refs[9], refs[10:12], refs[12], refs[13], refs[14]
-    rows, half = audio.shape
-    width = packs[0].shape[1]
-    side = lax.axis_index("head")
-    mine = place()
+def product(a, b):
+    return jnp.dot(a, b, preferred_element_type=jnp.float32)
+
+
+def fetcher(sems):
     copies = []
 
     def fetch(source, target):
         copies.append(pltpu.make_async_copy(source, target, sems.at[len(copies)]))
         copies[-1].start()
 
+    return copies, fetch
+
+
+def split_kernel(audio, video, ids, *refs):
+    packs, (ids_in, ids_wide, sems) = refs[:GROUP], refs[GROUP:]
+    rows, width = audio.shape[0], packs[0].shape[1]
+    mine = place()
+    copies, fetch = fetcher(sems)
+    fetch(ids, ids_in)
+    for k in range(GROUP):
+        at = pl.ds(pl.multiple_of((mine ^ k) * width, width), width)
+        for i, stream in enumerate((audio, video)):
+            fetch(stream.at[:, at], packs[k].at[i * rows : (i + 1) * rows])
+    copies[0].wait()
+    ids_wide[...] = jnp.zeros_like(ids_wide)
+    ids_wide[: ids_in.shape[0]] = (ids_in[...] + 1).astype(jnp.float32)
+    for k in range(GROUP):
+        packs[k][2 * rows :] = ids_wide[...].astype(packs[k].dtype)
+    for copy in copies[1:]:
+        copy.wait()
+
+
+def prepare_kernel(audio, video, query, key, *refs):
+    sums, seconds, streams, firsts, sems = refs[-9:-7], refs[-7:-5], refs[-5:-3], refs[-3:-1], refs[-1]
+    half = audio.shape[1]
+    side = lax.axis_index("head")
     ours = pl.ds(pl.multiple_of(side * half, half), half)
     theirs = pl.ds(pl.multiple_of((1 - side) * half, half), half)
-    fetch(ids, ids_in)
-    fetch(audio, own)
-    fetch(video, sent)
-    for i, weight in enumerate((query, key)):
+    copies, fetch = fetcher(sems)
+    for i, (stream, weight) in enumerate(((audio, query), (video, key))):
+        fetch(stream, streams[i])
         fetch(weight.at[ours], firsts[i])
-    for i, stream in enumerate((audio, video)):
-        for k in range(GROUP):
-            at = pl.ds(pl.multiple_of((mine ^ k) * width, width), width)
-            fetch(stream.at[:, at], packs[k].at[i * rows : (i + 1) * rows])
     for i, weight in enumerate((query, key)):
         fetch(weight.at[theirs], seconds[i])
-    for copy in copies[:5]:
-        copy.wait()
-    for i, stream in enumerate((own, sent)):
-        sums[i][...] = jnp.dot(stream[...], firsts[i][...], preferred_element_type=jnp.float32)
-    ids_wide[...] = jnp.zeros_like(ids_wide)
-    ids_wide[: ids_in.shape[0]] = (ids_in[...] + 1).astype(jnp.float32)
-    for k in range(GROUP):
-        packs[k][2 * rows :] = ids_wide[...].astype(packs[k].dtype)
-    for copy in copies[5:]:
+    for i in range(2):
+        copies[2 * i].wait()
+        copies[2 * i + 1].wait()
+        sums[i][...] = product(streams[i][...], firsts[i][...])
+    for copy in copies[4:]:
         copy.wait()
 
 
@@ -81,7 +97,7 @@
     pieces, full = refs[-GROUP - 1 : -1], refs[-1]
     width = pieces[0].shape[1]
     mine = place()
-    total = part[...] + jnp.dot(other[...], weight[...], preferred_element_type=jnp.float32)
+    total = part[...] + product(other[...], weight[...])
     full[...] = total.astype(jnp.bfloat16) * jnp.bfloat16(scale)
     for k in range(GROUP):
         pieces[k][...] = full[:, pl.ds(pl.multiple_of((mine ^ k) * width, width), width)]
@@ -113,11 +129,14 @@
 
 
 def join_kernel(*refs):
-    pieces, out = refs[:GROUP], refs[GROUP]
+    pieces, out, sems = refs[:GROUP], refs[GROUP], refs[GROUP + 1]
     width = pieces[0].shape[1]
     mine = place()
-    for k in range(GROUP):
-        out[:, pl.ds(pl.multiple_of((mine ^ k) * width, width), width)] = pieces[k][...]
+    copies, fetch = fetcher(sems)
+    for k in range(GROUP):
+        fetch(pieces[k], out.at[:, pl.ds(pl.multiple_of((mine ^ k) * width, width), width)])
+    for copy in copies:
+        copy.wait()
 
 
 def marks_turned(lanes):
@@ -150,10 +169,6 @@
     return out
 
 
-def product(a, b):
-    return jnp.dot(a, b, preferred_element_type=jnp.float32)
-
-
 def attend(scores, old, values):
     width = values.shape[1] // 2
     top = old
@@ -185,14 +200,14 @@
                 turned[i, :width, at] = jnp.transpose(key[k][part * width : (part + 1) * width])
                 turned[i, width:, at] = x
 
-    def one(b, _):
-        scores = [product(asks[i, b], turned[i]) for i in range(2)]
-        for i in range(2):
-            peak, sums[i, b] = attend(scores[i], None, beside[i])
-            peaks[i, b] = jnp.broadcast_to(peak, (peak.shape[0], width))
-        return _
-
-    lax.fori_loop(0, GROUP, one, 0)
+    units = [(i, b) for b in range(GROUP) for i in range(2)]
+    ahead = product(asks[units[0]], turned[0])
+    for n, (i, b) in enumerate(units):
+        scores = ahead
+        if n + 1 < len(units):
+            ahead = product(asks[units[n + 1]], turned[units[n + 1][0]])
+        peak, sums[i, b] = attend(scores, None, beside[i])
+        peaks[i, b] = jnp.broadcast_to(peak, (peak.shape[0], width))
 
 
 def lend_kernel(edge_a, edge_b, plane_turned, plane_beside, first, second, turned, ordered, results):
@@ -201,7 +216,10 @@
     ordered[1 - odd] = edge_a[...]
     ordered[odd] = edge_b[...]
     lane = lax.broadcasted_iota(jnp.int32, (rows, width), 1)
-    for e in range(2 * RADIUS):
+    blocks = [slice(0, (j + 1) * rows) for j in range(RADIUS)]
+    blocks += [slice((j + 1) * rows, GROUP * rows) for j in range(RADIUS)]
+
+    def scores_of(e):
         side, j = e // RADIUS, e % RADIUS
         marks = marks_turned(ordered[side, j, 2 * rows :])
         query = ordered[side, j, rows : 2 * rows]
@@ -209,9 +227,15 @@
             at = slice(e * rows + part * width, e * rows + (part + 1) * width)
             turned[:width, at] = jnp.transpose(query[part * width : (part + 1) * width])
             turned[width:, at] = x
-        blocks = slice((j + 1) * rows, GROUP * rows) if side else slice(0, (j + 1) * rows)
-        scores = product(stacked_ask(query, marks), plane_turned[0, :, blocks])
-        peak, mixed = attend(scores, None, plane_beside[0, blocks])
+        return product(stacked_ask(query, marks), plane_turned[0, :, blocks[e]])
+
+    ahead = scores_of(0)
+    for e in range(2 * RADIUS):
+        side, j = e // RADIUS, e % RADIUS
+        scores = ahead
+        if e + 1 < 2 * RADIUS:
+            ahead = scores_of(e + 1)
+        peak, mixed = attend(scores, None, plane_beside[0, blocks[e]])
         mean = by_head(mixed[:, :width], rows) / by_head(mixed[:, width:], rows)
         results[side, j, :rows] = mean.astype(results.dtype)
         logs = peak + jnp.log(mixed[:, width:])
@@ -331,22 +355,34 @@
 
     part = shape((rows, half), f32)
     square = shape((half, half), bf16)
-    stream = shape((rows, half), bf16)
     piece = shape((rows, width), bf16)
     given = (audio_frames, video_frames, audio_query, video_key, recording.reshape(rows // width, width))
+    audio_in, video_in, query_in, key_in, ids_in = (
+        pltpu.with_memory_space_constraint(x, pltpu.HBM) for x in given
+    )
     other_audio = swapped(audio_frames)
-    query_part, key_part, query_rest, key_rest, video_copy, *packs = call(
+    other_video = swapped(video_frames)
+    packs = call(
+        split_kernel,
+        [shape((2 * rows + ID_ROWS, width), bf16)] * GROUP,
+        [pltpu.VMEM((rows // width, width), jnp.int32), pltpu.VMEM((ID_ROWS, width), f32)]
+        + [pltpu.SemaphoreType.DMA((1 + 2 * GROUP,))],
+        ins=[HBM] * 3,
+        moved=8 * rows * half,
+        name="split",
+    )(audio_in, video_in, ids_in)
+    packs = traded(packs)
+    query_part, key_part, query_rest, key_rest = call(
         prepare_kernel,
-        [part, part, square, square, stream] + [shape((2 * rows + ID_ROWS, width), bf16)] * GROUP,
-        [pltpu.VMEM((rows, half), bf16)]
+        [part, part, square, square],
+        [pltpu.VMEM((rows, half), bf16)] * 2
         + [pltpu.VMEM((half, half), bf16)] * 2
-        + [pltpu.VMEM((rows // width, width), jnp.int32), pltpu.VMEM((ID_ROWS, width), f32)]
-        + [pltpu.SemaphoreType.DMA((7 + 2 * GROUP,))],
-        ins=[HBM] * 5,
+        + [pltpu.SemaphoreType.DMA((6,))],
+        ins=[HBM] * 4 + [ANY],
         flops=4 * rows * half * half,
         moved=16 * half * half,
         name="prepare",
-    )(*(pltpu.with_memory_space_constraint(x, pltpu.HBM) for x in given))
+    )(audio_in, video_in, query_in, key_in, packs[1])
 
     def project(scale, *operands):
         return call(
@@ -359,8 +395,6 @@
             name="project",
         )(*operands)
 
-    packs = traded(packs)
-    other_video = swapped(video_copy)
     queries = project(HEAD**-0.5, query_part, other_audio, query_rest, *packs[1:])
     queries = traded(queries)
     keys = project(1.0, key_part, other_video, key_rest)
@@ -420,7 +454,12 @@
 
     def join(pieces):
         return call(
-            join_kernel, shape((rows, half), bf16), moved=2 * rows * half * 2, name="join"
+            join_kernel,
+            shape((rows, half), bf16),
+            [pltpu.SemaphoreType.DMA((GROUP,))],
+            outs_in=HBM,
+            moved=2 * rows * half * 2,
+            name="join",
         )(*traded(pieces))
 
     video_attended = join(video_pieces)

time: 54.2 us -> 53.3 us (0.983)
  waiting for transfers between devices: 13 us -> 11.7 us
    ppermute x15, waiting for transfers between devices: 11.3 us -> 9.4 us  [traded(): lax.ppermute(pieces[k], 'tm', pairs(k))]
    pallas_call x3 -> x4, Pallas kernels: 3.52 us -> 4.4 us  [the longest x1 1.78 us: local(): call(prepare_kernel, [part, part, square, square], [pltpu.VMEM((rows, hal...]
  transfers between devices with their start and end apart: 21 -> 21, of which waited for: 7 -> 7; matrix products, arithmetic and copies ran while one was open for 0% -> 0% of each run, Pallas kernels for 26% -> 27%
where the time goes in v8:
time: 53.3 us; the launch traced here: 53.1 us
  starting transfers between devices  22.6 us (42%)
  Pallas kernels  17.9 us (34%)
  waiting for transfers between devices  11.7 us (22%)
  between operations  0.96 us (2%)
    ppermute x15, starting transfers between devices, traded(): lax.ppermute(pieces[k], 'tm', pairs(k))  13.2 us
    ppermute x15, waiting for transfers between devices, traded(): lax.ppermute(pieces[k], 'tm', pairs(k))  9.4 us
    ppermute x4, starting transfers between devices, crossed(): lax.ppermute(sent[s], 'tm', [(i, partner(i, s)) for i in range(length)])  7.83 us
    pallas_call x1, Pallas kernels, local(): call(plane_kernel, [shape((2, GROUP, heads * rows, n * width), f32) for n...  6.76 us
    pallas_call x1, Pallas kernels, local(): call(lend_kernel, [back, back, shape((2 * width, around), bf16)], [pltpu....  2.78 us
    pallas_call x1, Pallas kernels, local(): call(edge_kernel, [piece] * GROUP, [pltpu.VMEM((around, 2 * width), bf16)...  2.53 us
    ppermute x4, waiting for transfers between devices, crossed(): lax.ppermute(sent[s], 'tm', [(i, partner(i, s)) for i in range(length)])  2.25 us
    pallas_call x1, Pallas kernels, local(): call(prepare_kernel, [part, part, square, square], [pltpu.VMEM((rows, hal...  1.78 us
  transfers between devices with their start and end apart: 21, of which 7 were waited for; matrix products, arithmetic and copies ran while one was open for 0% of the time, Pallas kernels for 27%

profile of v8, /device:TPU:9, one launch (start us, length us, event | category | flops | bytes accessed | tf_op | source)
XLA Modules:
  0.0 53.1 jit_solution(12813740531695645620)
XLA Ops:
  0.6 1.3 %collective-permute-start.3 = (bf16[256,512]{1,0:T(8,128)(2,1)}, bf16[256,512]{1,0:T(8,128)(2,1)S(1)}, u32[]{:S(2)}, u32[]{:S(2)}) collective-permute-start(bf16[256,512]{1,0:T(8,128)(2,1)} %audio.3), channel_id=1, source_target_pairs={{0,1},{1,0},{2,3},{3,2},{4,5},{5,4},{6,7},{7,6},{8,9},{9,8},{10,11... | collective-permute-start | bytes 786440 | tf_op jit(solution)/shard_map/ppermute | solution.py:339
  1.9 0.2 collective-permute-start.7
  2.2 1.2 %split.1 = (bf16[528,128]{1,0:T(8,128)(2,1)S(1)}, bf16[528,128]{1,0:T(8,128)(2,1)S(1)}, bf16[528,128]{1,0:T(8,128)(2,1)S(1)}, bf16[528,128]{1,0:T(8,128)(2,1)S(1)}) custom-call(bf16[256,512]{1,0:T(8,128)(2,1)} %audio.3, bf16[256,512]{1,0:T(8,128)(2,1)} %video.3, s32[2,128]{1,0:T(2,128)} %bitcast.1), custom_call_target="tpu_custom_call" | custom-call | bytes 1048576 | tf_op jit(solution)/shard_map/split/pallas_call | solution.py:365
  3.3 1.3 %collective-permute-start = (bf16[528,128]{1,0:T(8,128)(2,1)S(1)}, bf16[528,128]{1,0:T(8,128)(2,1)S(1)}, u32[]{:S(2)}, u32[]{:S(2)}) collective-permute-start(bf16[528,128]{1,0:T(8,128)(2,1)S(1)} %get-tuple-element.37), channel_id=1, source_target_pairs={{0,2},{2,0},{4,6},{6,4},{8,10},{10,8},{12,14},{14,12},{16,18},{18,... | collective-permute-start | bytes 405512 | tf_op jit(solution)/shard_map/ppermute | solution.py:343
  4.6 1.2 %collective-permute-start.1 = (bf16[528,128]{1,0:T(8,128)(2,1)S(1)}, bf16[528,128]{1,0:T(8,128)(2,1)S(1)}, u32[]{:S(2)}, u32[]{:S(2)}) collective-permute-start(bf16[528,128]{1,0:T(8,128)(2,1)S(1)} %get-tuple-element.38), channel_id=1, source_target_pairs={{0,4},{2,6},{4,0},{6,2},{8,12},{10,14},{12,8},{14,10},{16,20},{18,... | collective-permute-start | bytes 405512 | tf_op jit(solution)/shard_map/ppermute | solution.py:343
  5.9 0.5 collective-permute-start.2
  6.3 0.0 collective-permute-done.refs_0_.refs_1_
  6.3 1.8 %prepare.1 = (f32[256,512]{1,0:T(8,128)S(1)}, f32[256,512]{1,0:T(8,128)S(1)}, bf16[512,512]{1,0:T(8,128)(2,1)S(1)}, bf16[512,512]{1,0:T(8,128)(2,1)S(1)}) custom-call(bf16[256,512]{1,0:T(8,128)(2,1)} %audio.3, bf16[256,512]{1,0:T(8,128)(2,1)} %video.3, bf16[1024,512]{1,0:T(8,128)(2,1)} %query.1, bf16[1024,512]{1,0:T(8,128)(2,1)} %key.1, ...), custom_call_target="tpu_custom_call" | custom-call | flops 268435456 | bytes 4194304 | tf_op jit(solution)/shard_map/prepare/pallas_call | solution.py:375
  8.1 1.7 %collective-permute-done.1.refs_1_.refs_2_ = bf16[528,128]{1,0:T(8,128)(2,1)S(1)} collective-permute-done((bf16[528,128]{1,0:T(8,128)(2,1)S(1)}, bf16[528,128]{1,0:T(8,128)(2,1)S(1)}, u32[]{:S(2)}, u32[]{:S(2)}) %collective-permute-start.1) | collective-permute-done | bytes 135200 | tf_op jit(solution)/shard_map/ppermute | solution.py:343
  9.8 3.4 %collective-permute-done.2.refs_2_.refs_3_ = bf16[528,128]{1,0:T(8,128)(2,1)S(1)} collective-permute-done((bf16[528,128]{1,0:T(8,128)(2,1)S(1)}, bf16[528,128]{1,0:T(8,128)(2,1)S(1)}, u32[]{:S(2)}, u32[]{:S(2)}) %collective-permute-start.2) | collective-permute-done | bytes 135200 | tf_op jit(solution)/shard_map/ppermute | solution.py:343
  13.2 0.0 collective-permute-done.3.other
  13.2 0.4 project.2
  13.5 0.1 collective-permute-start.4
  13.6 1.3 %collective-permute-start.5 = (bf16[256,128]{1,0:T(8,128)(2,1)S(1)}, bf16[256,128]{1,0:T(8,128)(2,1)S(1)}, u32[]{:S(2)}, u32[]{:S(2)}) collective-permute-start(bf16[256,128]{1,0:T(8,128)(2,1)S(1)} %get-tuple-element.44), channel_id=1, source_target_pairs={{0,4},{2,6},{4,0},{6,2},{8,12},{10,14},{12,8},{14,10},{16,20},{18,... | collective-permute-start | bytes 196616 | tf_op jit(solution)/shard_map/ppermute | solution.py:343
  14.9 0.8 %collective-permute-start.6 = (bf16[256,128]{1,0:T(8,128)(2,1)S(1)}, bf16[256,128]{1,0:T(8,128)(2,1)S(1)}, u32[]{:S(2)}, u32[]{:S(2)}) collective-permute-start(bf16[256,128]{1,0:T(8,128)(2,1)S(1)} %get-tuple-element.45), channel_id=1, source_target_pairs={{0,6},{2,4},{4,2},{6,0},{8,14},{10,12},{12,10},{14,8},{16,22},{18,... | collective-permute-start | bytes 196616 | tf_op jit(solution)/shard_map/ppermute | solution.py:343
  15.7 0.0 collective-permute-done.7.other
  15.8 0.4 project.3
  16.1 0.1 collective-permute-start.10
  16.2 1.3 %collective-permute-start.11 = (bf16[256,128]{1,0:T(8,128)(2,1)S(1)}, bf16[256,128]{1,0:T(8,128)(2,1)S(1)}, u32[]{:S(2)}, u32[]{:S(2)}) collective-permute-start(bf16[256,128]{1,0:T(8,128)(2,1)S(1)} %get-tuple-element.52), channel_id=1, source_target_pairs={{0,4},{2,6},{4,0},{6,2},{8,12},{10,14},{12,8},{14,10},{16,20},{18,... | collective-permute-start | bytes 196616 | tf_op jit(solution)/shard_map/ppermute | solution.py:343
  17.5 0.0 collective-permute-done.4.refs_5_
  17.5 0.8 %collective-permute-start.12 = (bf16[256,128]{1,0:T(8,128)(2,1)S(1)}, bf16[256,128]{1,0:T(8,128)(2,1)S(1)}, u32[]{:S(2)}, u32[]{:S(2)}) collective-permute-start(bf16[256,128]{1,0:T(8,128)(2,1)S(1)} %get-tuple-element.53), channel_id=1, source_target_pairs={{0,6},{2,4},{4,2},{6,0},{8,14},{10,12},{12,10},{14,8},{16,22},{18,... | collective-permute-start | bytes 196616 | tf_op jit(solution)/shard_map/ppermute | solution.py:343
  18.3 0.0 collective-permute-done.5.refs_6_
  18.4 1.2 %collective-permute-done.6.refs_7_ = bf16[256,128]{1,0:T(8,128)(2,1)S(1)} collective-permute-done((bf16[256,128]{1,0:T(8,128)(2,1)S(1)}, bf16[256,128]{1,0:T(8,128)(2,1)S(1)}, u32[]{:S(2)}, u32[]{:S(2)}) %collective-permute-start.6) | collective-permute-done | bytes 65568 | tf_op jit(solution)/shard_map/ppermute | solution.py:343
  19.6 0.1 halo.1
  19.7 0.2 collective-permute-start.8
  19.9 4.3 %collective-permute-start.9 = (bf16[3,528,128]{2,1,0:T(8,128)(2,1)S(1)}, bf16[3,528,128]{2,1,0:T(8,128)(2,1)S(1)}, u32[]{:S(2)}, u32[]{:S(2)}) collective-permute-start(bf16[3,528,128]{2,1,0:T(8,128)(2,1)S(1)} %get-tuple-element.50), channel_id=1, source_target_pairs={{0,0},{2,2},{4,4},{6,6},{8,16},{10,18},{12,20},{14,22},{16,8},{18,... | collective-permute-start | bytes 1216520 | tf_op jit(solution)/shard_map/ppermute | solution.py:352
  24.2 0.0 collective-permute-done.10.refs_9_
  24.2 0.0 collective-permute-done.11.refs_10_
  24.2 0.0 collective-permute-done.12.refs_11_
  24.3 6.8 %plane.1 = (f32[2,4,512,128]{3,2,1,0:T(8,128)S(1)}, f32[2,4,512,256]{3,2,1,0:T(8,128)S(1)}, bf16[2,256,1024]{2,1,0:T(8,128)(2,1)S(1)}, bf16[2,1024,256]{2,1,0:T(8,128)(2,1)S(1)}, bf16[2,4,512,256]{3,2,1,0:T(8,128)(2,1)S(1)}) custom-call(bf16[528,128]{1,0:T(8,128)(2,1)S(1)} %get-tuple-element.36.refs_0_, ...), custom_call_target="tpu_custom_call" | custom-call | flops 4294967296 | bytes 2097152 | tf_op jit(solution)/shard_map/plane/pallas_call | solution.py:414
  31.0 0.0 collective-permute-done.8.edge_a
  31.0 2.2 %collective-permute-done.9.edge_b = bf16[3,528,128]{2,1,0:T(8,128)(2,1)S(1)} collective-permute-done((bf16[3,528,128]{2,1,0:T(8,128)(2,1)S(1)}, bf16[3,528,128]{2,1,0:T(8,128)(2,1)S(1)}, u32[]{:S(2)}, u32[]{:S(2)}) %collective-permute-start.9) | collective-permute-done | bytes 405536 | tf_op jit(solution)/shard_map/ppermute | solution.py:352
  33.3 2.8 %lend.1 = (bf16[3,288,128]{2,1,0:T(8,128)(2,1)S(1)}, bf16[3,288,128]{2,1,0:T(8,128)(2,1)S(1)}, bf16[256,1536]{1,0:T(8,128)(2,1)S(1)}) custom-call(bf16[3,528,128]{2,1,0:T(8,128)(2,1)S(1)} %collective-permute-done.8.edge_a, bf16[3,528,128]{2,1,0:T(8,128)(2,1)S(1)} %collective-permute-done.9.edge_b, bf16[2,256,1024]{2,1,0:T(8,128)(2,1)S(1)} %get-tuple-element.54.plane_turned, ...), custom_call_target="tpu_custom_call" | custom-call | flops 4831838208 | bytes 3145728 | tf_op jit(solution)/shard_map/lend/pallas_call | solution.py:425
  36.1 0.0 collective-permute-start.13
  36.1 3.2 %collective-permute-start.14 = (bf16[3,288,128]{2,1,0:T(8,128)(2,1)S(1)}, bf16[3,288,128]{2,1,0:T(8,128)(2,1)S(1)}, u32[]{:S(2)}, u32[]{:S(2)}) collective-permute-start(bf16[3,288,128]{2,1,0:T(8,128)(2,1)S(1)} %get-tuple-element.57), channel_id=1, source_target_pairs={{0,0},{2,2},{4,4},{6,6},{8,16},{10,18},{12,20},{14,22},{16,8},{18,... | collective-permute-start | bytes 663560 | tf_op jit(solution)/shard_map/ppermute | solution.py:352
  39.4 2.5 %edge.1 = (bf16[256,128]{1,0:T(8,128)(2,1)S(1)}, bf16[256,128]{1,0:T(8,128)(2,1)S(1)}, bf16[256,128]{1,0:T(8,128)(2,1)S(1)}, bf16[256,128]{1,0:T(8,128)(2,1)S(1)}) custom-call(bf16[3,528,128]{2,1,0:T(8,128)(2,1)S(1)} %collective-permute-done.8.edge_a, bf16[3,528,128]{2,1,0:T(8,128)(2,1)S(1)} %collective-permute-done.9.edge_b, ...), custom_call_target="tpu_custom_call" | custom-call | flops 4831838208 | bytes 3145728 | tf_op jit(solution)/shard_map/edge/pallas_call | solution.py:436
  41.9 1.9 %collective-permute-start.18 = (bf16[256,128]{1,0:T(8,128)(2,1)S(1)}, bf16[256,128]{1,0:T(8,128)(2,1)S(1)}, u32[]{:S(2)}, u32[]{:S(2)}) collective-permute-start(bf16[256,128]{1,0:T(8,128)(2,1)S(1)} %get-tuple-element.67), channel_id=1, source_target_pairs={{0,2},{2,0},{4,6},{6,4},{8,10},{10,8},{12,14},{14,12},{16,18},{18,... | collective-permute-start | bytes 196616 | tf_op jit(solution)/shard_map/ppermute | solution.py:343
  43.8 1.0 %collective-permute-start.19 = (bf16[256,128]{1,0:T(8,128)(2,1)S(1)}, bf16[256,128]{1,0:T(8,128)(2,1)S(1)}, u32[]{:S(2)}, u32[]{:S(2)}) collective-permute-start(bf16[256,128]{1,0:T(8,128)(2,1)S(1)} %get-tuple-element.68), channel_id=1, source_target_pairs={{0,4},{2,6},{4,0},{6,2},{8,12},{10,14},{12,8},{14,10},{16,20},{18,... | collective-permute-start | bytes 196616 | tf_op jit(solution)/shard_map/ppermute | solution.py:343
  44.8 0.7 %collective-permute-start.20 = (bf16[256,128]{1,0:T(8,128)(2,1)S(1)}, bf16[256,128]{1,0:T(8,128)(2,1)S(1)}, u32[]{:S(2)}, u32[]{:S(2)}) collective-permute-start(bf16[256,128]{1,0:T(8,128)(2,1)S(1)} %get-tuple-element.69), channel_id=1, source_target_pairs={{0,6},{2,4},{4,2},{6,0},{8,14},{10,12},{12,10},{14,8},{16,22},{18,... | collective-permute-start | bytes 196616 | tf_op jit(solution)/shard_map/ppermute | solution.py:343
  45.5 0.0 collective-permute-done.13.back_a
  45.5 0.0 collective-permute-done.14.back_b
  45.5 0.5 %merge.1 = (bf16[256,128]{1,0:T(8,128)(2,1)S(1)}, bf16[256,128]{1,0:T(8,128)(2,1)S(1)}, bf16[256,128]{1,0:T(8,128)(2,1)S(1)}, bf16[256,128]{1,0:T(8,128)(2,1)S(1)}) custom-call(bf16[3,288,128]{2,1,0:T(8,128)(2,1)S(1)} %collective-permute-done.13.back_a, bf16[3,288,128]{2,1,0:T(8,128)(2,1)S(1)} %collective-permute-done.14.back_b, ...), custom_call_target="tpu_custom_call" | custom-call | bytes 2097152 | tf_op jit(solution)/shard_map/merge/pallas_call | solution.py:445
  46.1 0.4 collective-permute-start.15
  46.5 1.7 %collective-permute-start.16 = (bf16[256,128]{1,0:T(8,128)(2,1)S(1)}, bf16[256,128]{1,0:T(8,128)(2,1)S(1)}, u32[]{:S(2)}, u32[]{:S(2)}) collective-permute-start(bf16[256,128]{1,0:T(8,128)(2,1)S(1)} %get-tuple-element.65), channel_id=1, source_target_pairs={{0,4},{2,6},{4,0},{6,2},{8,12},{10,14},{12,8},{14,10},{16,20},{18,... | collective-permute-start | bytes 196616 | tf_op jit(solution)/shard_map/ppermute | solution.py:343
  48.1 0.0 collective-permute-done.18.refs_1_
  48.1 0.1 collective-permute-start.17
  48.3 0.0 collective-permute-done.19.refs_2_
  48.3 0.8 %collective-permute-done.20.refs_3_ = bf16[256,128]{1,0:T(8,128)(2,1)S(1)} collective-permute-done((bf16[256,128]{1,0:T(8,128)(2,1)S(1)}, bf16[256,128]{1,0:T(8,128)(2,1)S(1)}, u32[]{:S(2)}, u32[]{:S(2)}) %collective-permute-start.20) | collective-permute-done | bytes 65568 | tf_op jit(solution)/shard_map/ppermute | solution.py:343
  49.1 0.7 %join.3 = bf16[256,512]{1,0:T(8,128)(2,1)} custom-call(bf16[256,128]{1,0:T(8,128)(2,1)S(1)} %get-tuple-element.62.refs_0_, bf16[256,128]{1,0:T(8,128)(2,1)S(1)} %collective-permute-done.18.refs_1_, bf16[256,128]{1,0:T(8,128)(2,1)S(1)} %collective-permute-done.19.refs_2_, bf16[256,128]{1,0:T(8,128)(2,1)S(1)} %collective-permute-done.20.refs_3_), custom_call_target="tpu_custom_call" | custom-call | bytes 524288 | tf_op jit(solution)/shard_map/join/pallas_call | solution.py:456
  49.9 0.0 collective-permute-done.15.refs_1_
  49.9 0.5 %collective-permute-done.16.refs_2_ = bf16[256,128]{1,0:T(8,128)(2,1)S(1)} collective-permute-done((bf16[256,128]{1,0:T(8,128)(2,1)S(1)}, bf16[256,128]{1,0:T(8,128)(2,1)S(1)}, u32[]{:S(2)}, u32[]{:S(2)}) %collective-permute-start.16) | collective-permute-done | bytes 65568 | tf_op jit(solution)/shard_map/ppermute | solution.py:343
  50.4 1.8 %collective-permute-done.17.refs_3_ = bf16[256,128]{1,0:T(8,128)(2,1)S(1)} collective-permute-done((bf16[256,128]{1,0:T(8,128)(2,1)S(1)}, bf16[256,128]{1,0:T(8,128)(2,1)S(1)}, u32[]{:S(2)}, u32[]{:S(2)}) %collective-permute-start.17) | collective-permute-done | bytes 65568 | tf_op jit(solution)/shard_map/ppermute | solution.py:343
  52.2 0.7 %join.2 = bf16[256,512]{1,0:T(8,128)(2,1)} custom-call(bf16[256,128]{1,0:T(8,128)(2,1)S(1)} %get-tuple-element.63.refs_0_, bf16[256,128]{1,0:T(8,128)(2,1)S(1)} %collective-permute-done.15.refs_1_, bf16[256,128]{1,0:T(8,128)(2,1)S(1)} %collective-permute-done.16.refs_2_, bf16[256,128]{1,0:T(8,128)(2,1)S(1)} %collective-permute-done.17.refs_3_), custom_call_target="tpu_custom_call" | custom-call | bytes 524288 | tf_op jit(solution)/shard_map/join/pallas_call | solution.py:456
Async XLA Ops:
  0.6 12.5 %collective-permute-start.3 = (bf16[256,512]{1,0:T(8,128)(2,1)}, bf16[256,512]{1,0:T(8,128)(2,1)S(1)}, u32[]{:S(2)}, u32[]{:S(2)}) collective-permute-start(bf16[256,512]{1,0:T(8,128)(2,1)} %audio.3), channel_id=1, source_target_pairs={{0,1},{1,0},{2,3},{3,2},{4,5},{5,4},{6,7},{7,6},{8,9},{9,8},{10,11... | collective-permute-start | bytes 786440 | tf_op jit(solution)/shard_map/ppermute | solution.py:339
  1.9 13.8 %collective-permute-start.7 = (bf16[256,512]{1,0:T(8,128)(2,1)}, bf16[256,512]{1,0:T(8,128)(2,1)S(1)}, u32[]{:S(2)}, u32[]{:S(2)}) collective-permute-start(bf16[256,512]{1,0:T(8,128)(2,1)} %video.3), channel_id=1, source_target_pairs={{0,1},{1,0},{2,3},{3,2},{4,5},{5,4},{6,7},{7,6},{8,9},{9,8},{10,11... | collective-permute-start | bytes 786440 | tf_op jit(solution)/shard_map/ppermute | solution.py:339
  3.3 3.0 %collective-permute-start = (bf16[528,128]{1,0:T(8,128)(2,1)S(1)}, bf16[528,128]{1,0:T(8,128)(2,1)S(1)}, u32[]{:S(2)}, u32[]{:S(2)}) collective-permute-start(bf16[528,128]{1,0:T(8,128)(2,1)S(1)} %get-tuple-element.37), channel_id=1, source_target_pairs={{0,2},{2,0},{4,6},{6,4},{8,10},{10,8},{12,14},{14,12},{16,18},{18,... | collective-permute-start | bytes 405512 | tf_op jit(solution)/shard_map/ppermute | solution.py:343
  4.6 5.2 %collective-permute-start.1 = (bf16[528,128]{1,0:T(8,128)(2,1)S(1)}, bf16[528,128]{1,0:T(8,128)(2,1)S(1)}, u32[]{:S(2)}, u32[]{:S(2)}) collective-permute-start(bf16[528,128]{1,0:T(8,128)(2,1)S(1)} %get-tuple-element.38), channel_id=1, source_target_pairs={{0,4},{2,6},{4,0},{6,2},{8,12},{10,14},{12,8},{14,10},{16,20},{18,... | collective-permute-start | bytes 405512 | tf_op jit(solution)/shard_map/ppermute | solution.py:343
  5.9 7.3 %collective-permute-start.2 = (bf16[528,128]{1,0:T(8,128)(2,1)S(1)}, bf16[528,128]{1,0:T(8,128)(2,1)S(1)}, u32[]{:S(2)}, u32[]{:S(2)}) collective-permute-start(bf16[528,128]{1,0:T(8,128)(2,1)S(1)} %get-tuple-element.39), channel_id=1, source_target_pairs={{0,6},{2,4},{4,2},{6,0},{8,14},{10,12},{12,10},{14,8},{16,22},{18,... | collective-permute-start | bytes 405512 | tf_op jit(solution)/shard_map/ppermute | solution.py:343
  13.5 4.0 %collective-permute-start.4 = (bf16[256,128]{1,0:T(8,128)(2,1)S(1)}, bf16[256,128]{1,0:T(8,128)(2,1)S(1)}, u32[]{:S(2)}, u32[]{:S(2)}) collective-permute-start(bf16[256,128]{1,0:T(8,128)(2,1)S(1)} %get-tuple-element.43), channel_id=1, source_target_pairs={{0,2},{2,0},{4,6},{6,4},{8,10},{10,8},{12,14},{14,12},{16,18},{18,... | collective-permute-start | bytes 196616 | tf_op jit(solution)/shard_map/ppermute | solution.py:343
  13.6 4.7 %collective-permute-start.5 = (bf16[256,128]{1,0:T(8,128)(2,1)S(1)}, bf16[256,128]{1,0:T(8,128)(2,1)S(1)}, u32[]{:S(2)}, u32[]{:S(2)}) collective-permute-start(bf16[256,128]{1,0:T(8,128)(2,1)S(1)} %get-tuple-element.44), channel_id=1, source_target_pairs={{0,4},{2,6},{4,0},{6,2},{8,12},{10,14},{12,8},{14,10},{16,20},{18,... | collective-permute-start | bytes 196616 | tf_op jit(solution)/shard_map/ppermute | solution.py:343
  14.9 4.7 %collective-permute-start.6 = (bf16[256,128]{1,0:T(8,128)(2,1)S(1)}, bf16[256,128]{1,0:T(8,128)(2,1)S(1)}, u32[]{:S(2)}, u32[]{:S(2)}) collective-permute-start(bf16[256,128]{1,0:T(8,128)(2,1)S(1)} %get-tuple-element.45), channel_id=1, source_target_pairs={{0,6},{2,4},{4,2},{6,0},{8,14},{10,12},{12,10},{14,8},{16,22},{18,... | collective-permute-start | bytes 196616 | tf_op jit(solution)/shard_map/ppermute | solution.py:343
  16.1 8.1 %collective-permute-start.10 = (bf16[256,128]{1,0:T(8,128)(2,1)S(1)}, bf16[256,128]{1,0:T(8,128)(2,1)S(1)}, u32[]{:S(2)}, u32[]{:S(2)}) collective-permute-start(bf16[256,128]{1,0:T(8,128)(2,1)S(1)} %get-tuple-element.51), channel_id=1, source_target_pairs={{0,2},{2,0},{4,6},{6,4},{8,10},{10,8},{12,14},{14,12},{16,18},{18,... | collective-permute-start | bytes 196616 | tf_op jit(solution)/shard_map/ppermute | solution.py:343
  16.2 8.0 %collective-permute-start.11 = (bf16[256,128]{1,0:T(8,128)(2,1)S(1)}, bf16[256,128]{1,0:T(8,128)(2,1)S(1)}, u32[]{:S(2)}, u32[]{:S(2)}) collective-permute-start(bf16[256,128]{1,0:T(8,128)(2,1)S(1)} %get-tuple-element.52), channel_id=1, source_target_pairs={{0,4},{2,6},{4,0},{6,2},{8,12},{10,14},{12,8},{14,10},{16,20},{18,... | collective-permute-start | bytes 196616 | tf_op jit(solution)/shard_map/ppermute | solution.py:343
  17.5 6.7 %collective-permute-start.12 = (bf16[256,128]{1,0:T(8,128)(2,1)S(1)}, bf16[256,128]{1,0:T(8,128)(2,1)S(1)}, u32[]{:S(2)}, u32[]{:S(2)}) collective-permute-start(bf16[256,128]{1,0:T(8,128)(2,1)S(1)} %get-tuple-element.53), channel_id=1, source_target_pairs={{0,6},{2,4},{4,2},{6,0},{8,14},{10,12},{12,10},{14,8},{16,22},{18,... | collective-permute-start | bytes 196616 | tf_op jit(solution)/shard_map/ppermute | solution.py:343
  19.7 11.4 %collective-permute-start.8 = (bf16[3,528,128]{2,1,0:T(8,128)(2,1)S(1)}, bf16[3,528,128]{2,1,0:T(8,128)(2,1)S(1)}, u32[]{:S(2)}, u32[]{:S(2)}) collective-permute-start(bf16[3,528,128]{2,1,0:T(8,128)(2,1)S(1)} %get-tuple-element.49), channel_id=1, source_target_pairs={{0,8},{2,10},{4,12},{6,14},{8,0},{10,2},{12,4},{14,6},{16,24},{18,... | collective-permute-start | bytes 1216520 | tf_op jit(solution)/shard_map/ppermute | solution.py:352
  19.9 13.4 %collective-permute-start.9 = (bf16[3,528,128]{2,1,0:T(8,128)(2,1)S(1)}, bf16[3,528,128]{2,1,0:T(8,128)(2,1)S(1)}, u32[]{:S(2)}, u32[]{:S(2)}) collective-permute-start(bf16[3,528,128]{2,1,0:T(8,128)(2,1)S(1)} %get-tuple-element.50), channel_id=1, source_target_pairs={{0,0},{2,2},{4,4},{6,6},{8,16},{10,18},{12,20},{14,22},{16,8},{18,... | collective-permute-start | bytes 1216520 | tf_op jit(solution)/shard_map/ppermute | solution.py:352
  36.1 9.5 %collective-permute-start.13 = (bf16[3,288,128]{2,1,0:T(8,128)(2,1)S(1)}, bf16[3,288,128]{2,1,0:T(8,128)(2,1)S(1)}, u32[]{:S(2)}, u32[]{:S(2)}) collective-permute-start(bf16[3,288,128]{2,1,0:T(8,128)(2,1)S(1)} %get-tuple-element.56), channel_id=1, source_target_pairs={{0,8},{2,10},{4,12},{6,14},{8,0},{10,2},{12,4},{14,6},{16,24},{18,... | collective-permute-start | bytes 663560 | tf_op jit(solution)/shard_map/ppermute | solution.py:352
  36.1 9.4 %collective-permute-start.14 = (bf16[3,288,128]{2,1,0:T(8,128)(2,1)S(1)}, bf16[3,288,128]{2,1,0:T(8,128)(2,1)S(1)}, u32[]{:S(2)}, u32[]{:S(2)}) collective-permute-start(bf16[3,288,128]{2,1,0:T(8,128)(2,1)S(1)} %get-tuple-element.57), channel_id=1, source_target_pairs={{0,0},{2,2},{4,4},{6,6},{8,16},{10,18},{12,20},{14,22},{16,8},{18,... | collective-permute-start | bytes 663560 | tf_op jit(solution)/shard_map/ppermute | solution.py:352
  41.9 6.3 %collective-permute-start.18 = (bf16[256,128]{1,0:T(8,128)(2,1)S(1)}, bf16[256,128]{1,0:T(8,128)(2,1)S(1)}, u32[]{:S(2)}, u32[]{:S(2)}) collective-permute-start(bf16[256,128]{1,0:T(8,128)(2,1)S(1)} %get-tuple-element.67), channel_id=1, source_target_pairs={{0,2},{2,0},{4,6},{6,4},{8,10},{10,8},{12,14},{14,12},{16,18},{18,... | collective-permute-start | bytes 196616 | tf_op jit(solution)/shard_map/ppermute | solution.py:343
  43.8 4.5 %collective-permute-start.19 = (bf16[256,128]{1,0:T(8,128)(2,1)S(1)}, bf16[256,128]{1,0:T(8,128)(2,1)S(1)}, u32[]{:S(2)}, u32[]{:S(2)}) collective-permute-start(bf16[256,128]{1,0:T(8,128)(2,1)S(1)} %get-tuple-element.68), channel_id=1, source_target_pairs={{0,4},{2,6},{4,0},{6,2},{8,12},{10,14},{12,8},{14,10},{16,20},{18,... | collective-permute-start | bytes 196616 | tf_op jit(solution)/shard_map/ppermute | solution.py:343
  44.8 4.3 %collective-permute-start.20 = (bf16[256,128]{1,0:T(8,128)(2,1)S(1)}, bf16[256,128]{1,0:T(8,128)(2,1)S(1)}, u32[]{:S(2)}, u32[]{:S(2)}) collective-permute-start(bf16[256,128]{1,0:T(8,128)(2,1)S(1)} %get-tuple-element.69), channel_id=1, source_target_pairs={{0,6},{2,4},{4,2},{6,0},{8,14},{10,12},{12,10},{14,8},{16,22},{18,... | collective-permute-start | bytes 196616 | tf_op jit(solution)/shard_map/ppermute | solution.py:343
  46.1 3.8 %collective-permute-start.15 = (bf16[256,128]{1,0:T(8,128)(2,1)S(1)}, bf16[256,128]{1,0:T(8,128)(2,1)S(1)}, u32[]{:S(2)}, u32[]{:S(2)}) collective-permute-start(bf16[256,128]{1,0:T(8,128)(2,1)S(1)} %get-tuple-element.64), channel_id=1, source_target_pairs={{0,2},{2,0},{4,6},{6,4},{8,10},{10,8},{12,14},{14,12},{16,18},{18,... | collective-permute-start | bytes 196616 | tf_op jit(solution)/shard_map/ppermute | solution.py:343
  46.5 3.9 %collective-permute-start.16 = (bf16[256,128]{1,0:T(8,128)(2,1)S(1)}, bf16[256,128]{1,0:T(8,128)(2,1)S(1)}, u32[]{:S(2)}, u32[]{:S(2)}) collective-permute-start(bf16[256,128]{1,0:T(8,128)(2,1)S(1)} %get-tuple-element.65), channel_id=1, source_target_pairs={{0,4},{2,6},{4,0},{6,2},{8,12},{10,14},{12,8},{14,10},{16,20},{18,... | collective-permute-start | bytes 196616 | tf_op jit(solution)/shard_map/ppermute | solution.py:343
  48.1 4.0 %collective-permute-start.17 = (bf16[256,128]{1,0:T(8,128)(2,1)S(1)}, bf16[256,128]{1,0:T(8,128)(2,1)S(1)}, u32[]{:S(2)}, u32[]{:S(2)}) collective-permute-start(bf16[256,128]{1,0:T(8,128)(2,1)S(1)} %get-tuple-element.66), channel_id=1, source_target_pairs={{0,6},{2,4},{4,2},{6,0},{8,14},{10,12},{12,10},{14,8},{16,22},{18,... | collective-permute-start | bytes 196616 | tf_op jit(solution)/shard_map/ppermute | solution.py:343

commit v9 on v8

--- a/solution.py
+++ b/solution.py
@@ -54,7 +54,7 @@
     return copies, fetch
 
 
-def split_kernel(audio, video, ids, *refs):
+def split_kernel(audio, ids, *refs):
     packs, (ids_in, ids_wide, sems) = refs[:GROUP], refs[GROUP:]
     rows, width = audio.shape[0], packs[0].shape[1]
     mine = place()
@@ -62,23 +62,23 @@
     fetch(ids, ids_in)
     for k in range(GROUP):
         at = pl.ds(pl.multiple_of((mine ^ k) * width, width), width)
-        for i, stream in enumerate((audio, video)):
-            fetch(stream.at[:, at], packs[k].at[i * rows : (i + 1) * rows])
+        fetch(audio.at[:, at], packs[k].at[:rows])
     copies[0].wait()
     ids_wide[...] = jnp.zeros_like(ids_wide)
     ids_wide[: ids_in.shape[0]] = (ids_in[...] + 1).astype(jnp.float32)
     for k in range(GROUP):
-        packs[k][2 * rows :] = ids_wide[...].astype(packs[k].dtype)
+        packs[k][rows:] = ids_wide[...].astype(packs[k].dtype)
     for copy in copies[1:]:
         copy.wait()
 
 
 def prepare_kernel(audio, video, query, key, *refs):
-    sums, seconds, streams, firsts, sems = refs[-9:-7], refs[-7:-5], refs[-5:-3], refs[-3:-1], refs[-1]
+    sums, seconds, sent, own, firsts, sems = refs[-9:-7], refs[-7:-5], refs[-5], refs[-4], refs[-3:-1], refs[-1]
     half = audio.shape[1]
     side = lax.axis_index("head")
     ours = pl.ds(pl.multiple_of(side * half, half), half)
     theirs = pl.ds(pl.multiple_of((1 - side) * half, half), half)
+    streams = (own, sent)
     copies, fetch = fetcher(sems)
     for i, (stream, weight) in enumerate(((audio, query), (video, key))):
         fetch(stream, streams[i])
@@ -93,14 +93,16 @@
         copy.wait()
 
 
-def project_kernel(scale, part, other, weight, *refs):
+def project_kernel(scale, stream, part, other, weight, *refs):
     pieces, full = refs[-GROUP - 1 : -1], refs[-1]
-    width = pieces[0].shape[1]
-    mine = place()
-    total = part[...] + product(other[...], weight[...])
-    full[...] = total.astype(jnp.bfloat16) * jnp.bfloat16(scale)
-    for k in range(GROUP):
-        pieces[k][...] = full[:, pl.ds(pl.multiple_of((mine ^ k) * width, width), width)]
+    rows, width = other.shape[0], pieces[0].shape[1]
+    mine = place()
+    full[...] = (part[...] + product(other[...], weight[...])).astype(jnp.bfloat16) * jnp.bfloat16(scale)
+    for k in range(GROUP):
+        at = pl.ds(pl.multiple_of((mine ^ k) * width, width), width)
+        if stream:
+            pieces[k][:rows] = refs[0][:, at]
+        pieces[k][stream * rows :] = full[:, at]
 
 
 def halo_kernel(*refs):
@@ -117,7 +119,7 @@
             def _():
                 out[spot, :rows] = values[k][:rows]
                 out[spot, rows : 2 * rows] = queries[k][...]
-                out[spot, 2 * rows :] = values[k][2 * rows :]
+                out[spot, 2 * rows :] = values[k][rows:]
 
     last = lax.axis_size("tm") // GROUP - 1
 
@@ -180,9 +182,9 @@
 
 
 def plane_kernel(*refs):
-    packs, queries, keys = refs[:GROUP], refs[GROUP : 2 * GROUP], refs[2 * GROUP : 3 * GROUP]
+    audio, queries, video = refs[:GROUP], refs[GROUP : 2 * GROUP], refs[2 * GROUP : 3 * GROUP]
     peaks, sums, turned, beside, asks = refs[3 * GROUP :]
-    rows, width = keys[0].shape
+    rows, width = queries[0].shape
     mine = place()
     beside[:, :, width:] = jnp.ones((2, GROUP * rows, width), beside.dtype)
     for k in range(GROUP):
@@ -191,13 +193,15 @@
         def spot(at, size):
             return pl.ds(pl.multiple_of(b * rows + at, size), size)
 
-        marks = marks_turned(packs[k][2 * rows :])
-        for i, (ask, key) in enumerate(((queries, keys), (keys, queries))):
-            asks[i, b] = stacked_ask(ask[k][...], marks)
-            beside[i, spot(0, rows), :width] = packs[k][(1 - i) * rows : (2 - i) * rows]
+        marks = marks_turned(audio[k][rows:])
+        projections = (queries[k][...], video[k][rows:])
+        for i in range(2):
+            key = projections[1 - i]
+            asks[i, b] = stacked_ask(projections[i], marks)
+            beside[i, spot(0, rows), :width] = (audio if i else video)[k][:rows]
             for part, x in enumerate(marks):
                 at = spot(part * width, width)
-                turned[i, :width, at] = jnp.transpose(key[k][part * width : (part + 1) * width])
+                turned[i, :width, at] = jnp.transpose(key[part * width : (part + 1) * width])
                 turned[i, width:, at] = x
 
     units = [(i, b) for b in range(GROUP) for i in range(2)]
@@ -364,18 +368,18 @@
     other_video = swapped(video_frames)
     packs = call(
         split_kernel,
-        [shape((2 * rows + ID_ROWS, width), bf16)] * GROUP,
+        [shape((rows + ID_ROWS, width), bf16)] * GROUP,
         [pltpu.VMEM((rows // width, width), jnp.int32), pltpu.VMEM((ID_ROWS, width), f32)]
-        + [pltpu.SemaphoreType.DMA((1 + 2 * GROUP,))],
-        ins=[HBM] * 3,
-        moved=8 * rows * half,
+        + [pltpu.SemaphoreType.DMA((1 + GROUP,))],
+        ins=[HBM] * 2,
+        moved=4 * rows * half,
         name="split",
-    )(audio_in, video_in, ids_in)
+    )(audio_in, ids_in)
     packs = traded(packs)
-    query_part, key_part, query_rest, key_rest = call(
+    query_part, key_part, query_rest, key_rest, video_copy = call(
         prepare_kernel,
-        [part, part, square, square],
-        [pltpu.VMEM((rows, half), bf16)] * 2
+        [part, part, square, square, shape((rows, half), bf16)],
+        [pltpu.VMEM((rows, half), bf16)]
         + [pltpu.VMEM((half, half), bf16)] * 2
         + [pltpu.SemaphoreType.DMA((6,))],
         ins=[HBM] * 4 + [ANY],
@@ -384,20 +388,20 @@
         name="prepare",
     )(audio_in, video_in, query_in, key_in, packs[1])
 
-    def project(scale, *operands):
+    def project(scale, *operands, stream=(), after=()):
         return call(
-            functools.partial(project_kernel, scale),
-            [piece] * GROUP,
+            functools.partial(project_kernel, scale, len(stream)),
+            [shape(((1 + len(stream)) * rows, width), bf16)] * GROUP,
             [pltpu.VMEM((rows, half), bf16)],
-            ins=[VMEM] * 3 + [ANY] * (len(operands) - 3),
+            ins=[VMEM] * (3 + len(stream)) + [ANY] * len(after),
             flops=2 * rows * half * half,
             moved=2 * half * half + 6 * rows * half * 2,
             name="project",
-        )(*operands)
-
-    queries = project(HEAD**-0.5, query_part, other_audio, query_rest, *packs[1:])
+        )(*operands, *stream, *after)
+
+    queries = project(HEAD**-0.5, query_part, other_audio, query_rest, after=packs[1:])
     queries = traded(queries)
-    keys = project(1.0, key_part, other_video, key_rest)
+    video = project(1.0, key_part, other_video, key_rest, stream=[video_copy], after=queries[1:])
     edge = shape((RADIUS, 2 * rows + ID_ROWS, width), bf16)
     edges = crossed(
         call(
@@ -406,9 +410,9 @@
             ins=[VMEM] * (2 * GROUP) + [ANY],
             moved=20 * rows * width * 2,
             name="halo",
-        )(*packs, *queries, keys[0])
+        )(*packs, *queries, video[0])
     )
-    keys = traded(keys)
+    video = traded(video)
 
     inside, around = GROUP * rows, 2 * RADIUS * rows
     peaks, sums, plane_turned, plane_beside, asks = call(
@@ -420,7 +424,7 @@
         moved=8 * inside * width * 2,
         exps=4 * GROUP * rows * inside,
         name="plane",
-    )(*packs, *queries, *keys)
+    )(*packs, *queries, *video)
     back = shape((RADIUS, rows + rows // width * STAT_ROWS, width), bf16)
     lent_a, lent_b, edge_turned = call(
         lend_kernel,

time: 53.3 us -> 53.3 us (level)
    ppermute x4, waiting for transfers between devices: 2.25 us -> 0.85 us  [crossed(): lax.ppermute(sent[s], 'tm', [(i, partner(i, s)) for i in range(length)])]
    ppermute x2, waiting for transfers between devices: 0.01 us -> 0.77 us  [swapped(): return lax.ppermute(x, 'head', [(0, 1), (1, 0)])]
    ppermute x4, starting transfers between devices: 7.83 us -> 8.41 us  [crossed(): lax.ppermute(sent[s], 'tm', [(i, partner(i, s)) for i in range(length)])]
  transfers between devices with their start and end apart: 21 -> 21, of which waited for: 7 -> 10; matrix products, arithmetic and copies ran while one was open for 0% -> 0% of each run, Pallas kernels for 27% -> 26%
where the time goes in v9:
time: 53.3 us; the launch traced here: 52.9 us
  starting transfers between devices  22.9 us (43%)
  Pallas kernels  17.7 us (33%)
  waiting for transfers between devices  11.3 us (21%)
  between operations  0.93 us (2%)
    ppermute x15, starting transfers between devices, traded(): lax.ppermute(pieces[k], 'tm', pairs(k))  13 us
    ppermute x15, waiting for transfers between devices, traded(): lax.ppermute(pieces[k], 'tm', pairs(k))  9.69 us
    ppermute x4, starting transfers between devices, crossed(): lax.ppermute(sent[s], 'tm', [(i, partner(i, s)) for i in range(length)])  8.41 us
    pallas_call x1, Pallas kernels, local(): call(plane_kernel, [shape((2, GROUP, heads * rows, n * width), f32) for n...  6.74 us
    pallas_call x1, Pallas kernels, local(): call(lend_kernel, [back, back, shape((2 * width, around), bf16)], [pltpu....  2.79 us
    pallas_call x1, Pallas kernels, local(): call(edge_kernel, [piece] * GROUP, [pltpu.VMEM((around, 2 * width), bf16)...  2.53 us
    pallas_call x1, Pallas kernels, local(): call(prepare_kernel, [part, part, square, square, shape((rows, half), bf1...  1.78 us
    ppermute x2, starting transfers between devices, swapped(): return lax.ppermute(x, 'head', [(0, 1), (1, 0)])  1.53 us
  transfers between devices with their start and end apart: 21, of which 10 were waited for; matrix products, arithmetic and copies ran while one was open for 0% of the time, Pallas kernels for 26%

profile of v9, /device:TPU:9, one launch (start us, length us, event | category | flops | bytes accessed | tf_op | source)
XLA Modules:
  0.0 52.9 jit_solution(4758159480101149317)
XLA Ops:
  0.6 1.3 %collective-permute-start.3 = (bf16[256,512]{1,0:T(8,128)(2,1)}, bf16[256,512]{1,0:T(8,128)(2,1)S(1)}, u32[]{:S(2)}, u32[]{:S(2)}) collective-permute-start(bf16[256,512]{1,0:T(8,128)(2,1)} %audio.3), channel_id=1, source_target_pairs={{0,1},{1,0},{2,3},{3,2},{4,5},{5,4},{6,7},{7,6},{8,9},{9,8},{10,11... | collective-permute-start | bytes 786440 | tf_op jit(solution)/shard_map/ppermute | solution.py:343
  1.9 0.2 collective-permute-start.7
  2.2 1.0 %split.1 = (bf16[272,128]{1,0:T(8,128)(2,1)S(1)}, bf16[272,128]{1,0:T(8,128)(2,1)S(1)}, bf16[272,128]{1,0:T(8,128)(2,1)S(1)}, bf16[272,128]{1,0:T(8,128)(2,1)S(1)}) custom-call(bf16[256,512]{1,0:T(8,128)(2,1)} %audio.3, s32[2,128]{1,0:T(2,128)} %bitcast.1), custom_call_target="tpu_custom_call" | custom-call | bytes 524288 | tf_op jit(solution)/shard_map/split/pallas_call | solution.py:369
  3.2 1.3 %collective-permute-start = (bf16[272,128]{1,0:T(8,128)(2,1)S(1)}, bf16[272,128]{1,0:T(8,128)(2,1)S(1)}, u32[]{:S(2)}, u32[]{:S(2)}) collective-permute-start(bf16[272,128]{1,0:T(8,128)(2,1)S(1)} %get-tuple-element.38), channel_id=1, source_target_pairs={{0,2},{2,0},{4,6},{6,4},{8,10},{10,8},{12,14},{14,12},{16,18},{18,... | collective-permute-start | bytes 208904 | tf_op jit(solution)/shard_map/ppermute | solution.py:347
  4.5 1.2 %collective-permute-start.1 = (bf16[272,128]{1,0:T(8,128)(2,1)S(1)}, bf16[272,128]{1,0:T(8,128)(2,1)S(1)}, u32[]{:S(2)}, u32[]{:S(2)}) collective-permute-start(bf16[272,128]{1,0:T(8,128)(2,1)S(1)} %get-tuple-element.39), channel_id=1, source_target_pairs={{0,4},{2,6},{4,0},{6,2},{8,12},{10,14},{12,8},{14,10},{16,20},{18,... | collective-permute-start | bytes 208904 | tf_op jit(solution)/shard_map/ppermute | solution.py:347
  5.7 0.5 collective-permute-start.2
  6.2 0.0 collective-permute-done.refs_0_.refs_1_
  6.2 1.8 %prepare.1 = (f32[256,512]{1,0:T(8,128)S(1)}, f32[256,512]{1,0:T(8,128)S(1)}, bf16[512,512]{1,0:T(8,128)(2,1)S(1)}, bf16[512,512]{1,0:T(8,128)(2,1)S(1)}, bf16[256,512]{1,0:T(8,128)(2,1)S(1)}) custom-call(bf16[256,512]{1,0:T(8,128)(2,1)} %audio.3, bf16[256,512]{1,0:T(8,128)(2,1)} %video.1, bf16[1024,512]{1,0:T(8,128)(2,1)} %query.1, bf16[1024,512]{1,0:T(8,128)(2,1)} %key.1, ...), custom_call_target="tpu_custom_call" | custom-call | flops 268435456 | bytes 4194304 | tf_op jit(solution)/shard_map/prepare/pallas_call | solution.py:379
  8.0 0.3 collective-permute-done.1.refs_1_.refs_2_
  8.2 1.9 %collective-permute-done.2.refs_2_.refs_3_ = bf16[272,128]{1,0:T(8,128)(2,1)S(1)} collective-permute-done((bf16[272,128]{1,0:T(8,128)(2,1)S(1)}, bf16[272,128]{1,0:T(8,128)(2,1)S(1)}, u32[]{:S(2)}, u32[]{:S(2)}) %collective-permute-start.2) | collective-permute-done | bytes 69664 | tf_op jit(solution)/shard_map/ppermute | solution.py:347
  10.2 0.0 collective-permute-done.3.other
  10.2 0.4 project.2
  10.6 0.7 %collective-permute-start.4 = (bf16[256,128]{1,0:T(8,128)(2,1)S(1)}, bf16[256,128]{1,0:T(8,128)(2,1)S(1)}, u32[]{:S(2)}, u32[]{:S(2)}) collective-permute-start(bf16[256,128]{1,0:T(8,128)(2,1)S(1)} %get-tuple-element.44), channel_id=1, source_target_pairs={{0,2},{2,0},{4,6},{6,4},{8,10},{10,8},{12,14},{14,12},{16,18},{18,... | collective-permute-start | bytes 196616 | tf_op jit(solution)/shard_map/ppermute | solution.py:347
  11.2 1.2 %collective-permute-start.5 = (bf16[256,128]{1,0:T(8,128)(2,1)S(1)}, bf16[256,128]{1,0:T(8,128)(2,1)S(1)}, u32[]{:S(2)}, u32[]{:S(2)}) collective-permute-start(bf16[256,128]{1,0:T(8,128)(2,1)S(1)} %get-tuple-element.45), channel_id=1, source_target_pairs={{0,4},{2,6},{4,0},{6,2},{8,12},{10,14},{12,8},{14,10},{16,20},{18,... | collective-permute-start | bytes 196616 | tf_op jit(solution)/shard_map/ppermute | solution.py:347
  12.5 0.5 collective-permute-start.6
  12.9 0.8 %collective-permute-done.7.other = bf16[256,512]{1,0:T(8,128)(2,1)S(1)} collective-permute-done((bf16[256,512]{1,0:T(8,128)(2,1)}, bf16[256,512]{1,0:T(8,128)(2,1)S(1)}, u32[]{:S(2)}, u32[]{:S(2)}) %collective-permute-start.7) | collective-permute-done | bytes 262176 | tf_op jit(solution)/shard_map/ppermute | solution.py:343
  13.7 0.0 collective-permute-done.4.refs_1_.refs_5_
  13.7 1.2 %collective-permute-done.5.refs_2_.refs_6_ = bf16[256,128]{1,0:T(8,128)(2,1)S(1)} collective-permute-done((bf16[256,128]{1,0:T(8,128)(2,1)S(1)}, bf16[256,128]{1,0:T(8,128)(2,1)S(1)}, u32[]{:S(2)}, u32[]{:S(2)}) %collective-permute-start.5) | collective-permute-done | bytes 65568 | tf_op jit(solution)/shard_map/ppermute | solution.py:347
  14.9 1.6 %collective-permute-done.6.refs_3_.refs_7_ = bf16[256,128]{1,0:T(8,128)(2,1)S(1)} collective-permute-done((bf16[256,128]{1,0:T(8,128)(2,1)S(1)}, bf16[256,128]{1,0:T(8,128)(2,1)S(1)}, u32[]{:S(2)}, u32[]{:S(2)}) %collective-permute-start.6) | collective-permute-done | bytes 65568 | tf_op jit(solution)/shard_map/ppermute | solution.py:347
  16.5 0.4 project.3
  16.9 0.4 collective-permute-start.10
  17.3 1.1 %collective-permute-start.11 = (bf16[512,128]{1,0:T(8,128)(2,1)S(1)}, bf16[512,128]{1,0:T(8,128)(2,1)S(1)}, u32[]{:S(2)}, u32[]{:S(2)}) collective-permute-start(bf16[512,128]{1,0:T(8,128)(2,1)S(1)} %get-tuple-element.54), channel_id=1, source_target_pairs={{0,4},{2,6},{4,0},{6,2},{8,12},{10,14},{12,8},{14,10},{16,20},{18,... | collective-permute-start | bytes 393224 | tf_op jit(solution)/shard_map/ppermute | solution.py:347
  18.4 0.7 %collective-permute-start.12 = (bf16[512,128]{1,0:T(8,128)(2,1)S(1)}, bf16[512,128]{1,0:T(8,128)(2,1)S(1)}, u32[]{:S(2)}, u32[]{:S(2)}) collective-permute-start(bf16[512,128]{1,0:T(8,128)(2,1)S(1)} %get-tuple-element.55), channel_id=1, source_target_pairs={{0,6},{2,4},{4,2},{6,0},{8,14},{10,12},{12,10},{14,8},{16,22},{18,... | collective-permute-start | bytes 393224 | tf_op jit(solution)/shard_map/ppermute | solution.py:347
  19.1 0.1 halo.1
  19.2 0.2 collective-permute-start.8
  19.5 4.3 %collective-permute-start.9 = (bf16[3,528,128]{2,1,0:T(8,128)(2,1)S(1)}, bf16[3,528,128]{2,1,0:T(8,128)(2,1)S(1)}, u32[]{:S(2)}, u32[]{:S(2)}) collective-permute-start(bf16[3,528,128]{2,1,0:T(8,128)(2,1)S(1)} %get-tuple-element.52), channel_id=1, source_target_pairs={{0,0},{2,2},{4,4},{6,6},{8,16},{10,18},{12,20},{14,22},{16,8},{18,... | collective-permute-start | bytes 1216520 | tf_op jit(solution)/shard_map/ppermute | solution.py:356
  23.8 0.0 collective-permute-done.10.refs_9_
  23.8 0.0 collective-permute-done.11.refs_10_
  23.8 1.8 %collective-permute-done.12.refs_11_ = bf16[512,128]{1,0:T(8,128)(2,1)S(1)} collective-permute-done((bf16[512,128]{1,0:T(8,128)(2,1)S(1)}, bf16[512,128]{1,0:T(8,128)(2,1)S(1)}, u32[]{:S(2)}, u32[]{:S(2)}) %collective-permute-start.12) | collective-permute-done | bytes 131104 | tf_op jit(solution)/shard_map/ppermute | solution.py:347
  25.7 6.7 %plane.1 = (f32[2,4,512,128]{3,2,1,0:T(8,128)S(1)}, f32[2,4,512,256]{3,2,1,0:T(8,128)S(1)}, bf16[2,256,1024]{2,1,0:T(8,128)(2,1)S(1)}, bf16[2,1024,256]{2,1,0:T(8,128)(2,1)S(1)}, bf16[2,4,512,256]{3,2,1,0:T(8,128)(2,1)S(1)}) custom-call(bf16[272,128]{1,0:T(8,128)(2,1)S(1)} %get-tuple-element.37.refs_0_, ...), custom_call_target="tpu_custom_call" | custom-call | flops 4294967296 | bytes 2097152 | tf_op jit(solution)/shard_map/plane/pallas_call | solution.py:418
  32.4 0.0 collective-permute-done.8.edge_a
  32.4 0.8 %collective-permute-done.9.edge_b = bf16[3,528,128]{2,1,0:T(8,128)(2,1)S(1)} collective-permute-done((bf16[3,528,128]{2,1,0:T(8,128)(2,1)S(1)}, bf16[3,528,128]{2,1,0:T(8,128)(2,1)S(1)}, u32[]{:S(2)}, u32[]{:S(2)}) %collective-permute-start.9) | collective-permute-done | bytes 405536 | tf_op jit(solution)/shard_map/ppermute | solution.py:356
  33.3 2.8 %lend.1 = (bf16[3,288,128]{2,1,0:T(8,128)(2,1)S(1)}, bf16[3,288,128]{2,1,0:T(8,128)(2,1)S(1)}, bf16[256,1536]{1,0:T(8,128)(2,1)S(1)}) custom-call(bf16[3,528,128]{2,1,0:T(8,128)(2,1)S(1)} %collective-permute-done.8.edge_a, bf16[3,528,128]{2,1,0:T(8,128)(2,1)S(1)} %collective-permute-done.9.edge_b, bf16[2,256,1024]{2,1,0:T(8,128)(2,1)S(1)} %get-tuple-element.56.plane_turned, ...), custom_call_target="tpu_custom_call" | custom-call | flops 4831838208 | bytes 3145728 | tf_op jit(solution)/shard_map/lend/pallas_call | solution.py:429
  36.0 0.0 collective-permute-start.13
  36.1 3.8 %collective-permute-start.14 = (bf16[3,288,128]{2,1,0:T(8,128)(2,1)S(1)}, bf16[3,288,128]{2,1,0:T(8,128)(2,1)S(1)}, u32[]{:S(2)}, u32[]{:S(2)}) collective-permute-start(bf16[3,288,128]{2,1,0:T(8,128)(2,1)S(1)} %get-tuple-element.59), channel_id=1, source_target_pairs={{0,0},{2,2},{4,4},{6,6},{8,16},{10,18},{12,20},{14,22},{16,8},{18,... | collective-permute-start | bytes 663560 | tf_op jit(solution)/shard_map/ppermute | solution.py:356
  39.9 2.5 %edge.1 = (bf16[256,128]{1,0:T(8,128)(2,1)S(1)}, bf16[256,128]{1,0:T(8,128)(2,1)S(1)}, bf16[256,128]{1,0:T(8,128)(2,1)S(1)}, bf16[256,128]{1,0:T(8,128)(2,1)S(1)}) custom-call(bf16[3,528,128]{2,1,0:T(8,128)(2,1)S(1)} %collective-permute-done.8.edge_a, bf16[3,528,128]{2,1,0:T(8,128)(2,1)S(1)} %collective-permute-done.9.edge_b, ...), custom_call_target="tpu_custom_call" | custom-call | flops 4831838208 | bytes 3145728 | tf_op jit(solution)/shard_map/edge/pallas_call | solution.py:440
  42.5 0.9 %collective-permute-start.18 = (bf16[256,128]{1,0:T(8,128)(2,1)S(1)}, bf16[256,128]{1,0:T(8,128)(2,1)S(1)}, u32[]{:S(2)}, u32[]{:S(2)}) collective-permute-start(bf16[256,128]{1,0:T(8,128)(2,1)S(1)} %get-tuple-element.69), channel_id=1, source_target_pairs={{0,2},{2,0},{4,6},{6,4},{8,10},{10,8},{12,14},{14,12},{16,18},{18,... | collective-permute-start | bytes 196616 | tf_op jit(solution)/shard_map/ppermute | solution.py:347
  43.4 1.2 %collective-permute-start.19 = (bf16[256,128]{1,0:T(8,128)(2,1)S(1)}, bf16[256,128]{1,0:T(8,128)(2,1)S(1)}, u32[]{:S(2)}, u32[]{:S(2)}) collective-permute-start(bf16[256,128]{1,0:T(8,128)(2,1)S(1)} %get-tuple-element.70), channel_id=1, source_target_pairs={{0,4},{2,6},{4,0},{6,2},{8,12},{10,14},{12,8},{14,10},{16,20},{18,... | collective-permute-start | bytes 196616 | tf_op jit(solution)/shard_map/ppermute | solution.py:347
  44.6 0.5 collective-permute-start.20
  45.1 0.0 collective-permute-done.13.back_a
  45.1 0.0 collective-permute-done.14.back_b
  45.1 0.5 %merge.1 = (bf16[256,128]{1,0:T(8,128)(2,1)S(1)}, bf16[256,128]{1,0:T(8,128)(2,1)S(1)}, bf16[256,128]{1,0:T(8,128)(2,1)S(1)}, bf16[256,128]{1,0:T(8,128)(2,1)S(1)}) custom-call(bf16[3,288,128]{2,1,0:T(8,128)(2,1)S(1)} %collective-permute-done.13.back_a, bf16[3,288,128]{2,1,0:T(8,128)(2,1)S(1)} %collective-permute-done.14.back_b, ...), custom_call_target="tpu_custom_call" | custom-call | bytes 2097152 | tf_op jit(solution)/shard_map/merge/pallas_call | solution.py:449
  45.7 1.1 %collective-permute-start.15 = (bf16[256,128]{1,0:T(8,128)(2,1)S(1)}, bf16[256,128]{1,0:T(8,128)(2,1)S(1)}, u32[]{:S(2)}, u32[]{:S(2)}) collective-permute-start(bf16[256,128]{1,0:T(8,128)(2,1)S(1)} %get-tuple-element.66), channel_id=1, source_target_pairs={{0,2},{2,0},{4,6},{6,4},{8,10},{10,8},{12,14},{14,12},{16,18},{18,... | collective-permute-start | bytes 196616 | tf_op jit(solution)/shard_map/ppermute | solution.py:347
  46.7 1.1 %collective-permute-start.16 = (bf16[256,128]{1,0:T(8,128)(2,1)S(1)}, bf16[256,128]{1,0:T(8,128)(2,1)S(1)}, u32[]{:S(2)}, u32[]{:S(2)}) collective-permute-start(bf16[256,128]{1,0:T(8,128)(2,1)S(1)} %get-tuple-element.67), channel_id=1, source_target_pairs={{0,4},{2,6},{4,0},{6,2},{8,12},{10,14},{12,8},{14,10},{16,20},{18,... | collective-permute-start | bytes 196616 | tf_op jit(solution)/shard_map/ppermute | solution.py:347
  47.8 0.0 collective-permute-done.18.refs_1_
  47.8 0.6 %collective-permute-start.17 = (bf16[256,128]{1,0:T(8,128)(2,1)S(1)}, bf16[256,128]{1,0:T(8,128)(2,1)S(1)}, u32[]{:S(2)}, u32[]{:S(2)}) collective-permute-start(bf16[256,128]{1,0:T(8,128)(2,1)S(1)} %get-tuple-element.68), channel_id=1, source_target_pairs={{0,6},{2,4},{4,2},{6,0},{8,14},{10,12},{12,10},{14,8},{16,22},{18,... | collective-permute-start | bytes 196616 | tf_op jit(solution)/shard_map/ppermute | solution.py:347
  48.4 0.0 collective-permute-done.19.refs_2_
  48.4 0.2 collective-permute-done.20.refs_3_
  48.6 0.7 %join.3 = bf16[256,512]{1,0:T(8,128)(2,1)} custom-call(bf16[256,128]{1,0:T(8,128)(2,1)S(1)} %get-tuple-element.64.refs_0_, bf16[256,128]{1,0:T(8,128)(2,1)S(1)} %collective-permute-done.18.refs_1_, bf16[256,128]{1,0:T(8,128)(2,1)S(1)} %collective-permute-done.19.refs_2_, bf16[256,128]{1,0:T(8,128)(2,1)S(1)} %collective-permute-done.20.refs_3_), custom_call_target="tpu_custom_call" | custom-call | bytes 524288 | tf_op jit(solution)/shard_map/join/pallas_call | solution.py:460
  49.4 0.0 collective-permute-done.15.refs_1_
  49.4 1.0 %collective-permute-done.16.refs_2_ = bf16[256,128]{1,0:T(8,128)(2,1)S(1)} collective-permute-done((bf16[256,128]{1,0:T(8,128)(2,1)S(1)}, bf16[256,128]{1,0:T(8,128)(2,1)S(1)}, u32[]{:S(2)}, u32[]{:S(2)}) %collective-permute-start.16) | collective-permute-done | bytes 65568 | tf_op jit(solution)/shard_map/ppermute | solution.py:347
  50.4 1.6 %collective-permute-done.17.refs_3_ = bf16[256,128]{1,0:T(8,128)(2,1)S(1)} collective-permute-done((bf16[256,128]{1,0:T(8,128)(2,1)S(1)}, bf16[256,128]{1,0:T(8,128)(2,1)S(1)}, u32[]{:S(2)}, u32[]{:S(2)}) %collective-permute-start.17) | collective-permute-done | bytes 65568 | tf_op jit(solution)/shard_map/ppermute | solution.py:347
  52.0 0.7 %join.2 = bf16[256,512]{1,0:T(8,128)(2,1)} custom-call(bf16[256,128]{1,0:T(8,128)(2,1)S(1)} %get-tuple-element.65.refs_0_, bf16[256,128]{1,0:T(8,128)(2,1)S(1)} %collective-permute-done.15.refs_1_, bf16[256,128]{1,0:T(8,128)(2,1)S(1)} %collective-permute-done.16.refs_2_, bf16[256,128]{1,0:T(8,128)(2,1)S(1)} %collective-permute-done.17.refs_3_), custom_call_target="tpu_custom_call" | custom-call | bytes 524288 | tf_op jit(solution)/shard_map/join/pallas_call | solution.py:460
Async XLA Ops:
  0.6 9.5 %collective-permute-start.3 = (bf16[256,512]{1,0:T(8,128)(2,1)}, bf16[256,512]{1,0:T(8,128)(2,1)S(1)}, u32[]{:S(2)}, u32[]{:S(2)}) collective-permute-start(bf16[256,512]{1,0:T(8,128)(2,1)} %audio.3), channel_id=1, source_target_pairs={{0,1},{1,0},{2,3},{3,2},{4,5},{5,4},{6,7},{7,6},{8,9},{9,8},{10,11... | collective-permute-start | bytes 786440 | tf_op jit(solution)/shard_map/ppermute | solution.py:343
  1.9 11.8 %collective-permute-start.7 = (bf16[256,512]{1,0:T(8,128)(2,1)}, bf16[256,512]{1,0:T(8,128)(2,1)S(1)}, u32[]{:S(2)}, u32[]{:S(2)}) collective-permute-start(bf16[256,512]{1,0:T(8,128)(2,1)} %video.1), channel_id=1, source_target_pairs={{0,1},{1,0},{2,3},{3,2},{4,5},{5,4},{6,7},{7,6},{8,9},{9,8},{10,11... | collective-permute-start | bytes 786440 | tf_op jit(solution)/shard_map/ppermute | solution.py:343
  3.2 3.0 %collective-permute-start = (bf16[272,128]{1,0:T(8,128)(2,1)S(1)}, bf16[272,128]{1,0:T(8,128)(2,1)S(1)}, u32[]{:S(2)}, u32[]{:S(2)}) collective-permute-start(bf16[272,128]{1,0:T(8,128)(2,1)S(1)} %get-tuple-element.38), channel_id=1, source_target_pairs={{0,2},{2,0},{4,6},{6,4},{8,10},{10,8},{12,14},{14,12},{16,18},{18,... | collective-permute-start | bytes 208904 | tf_op jit(solution)/shard_map/ppermute | solution.py:347
  4.5 3.8 %collective-permute-start.1 = (bf16[272,128]{1,0:T(8,128)(2,1)S(1)}, bf16[272,128]{1,0:T(8,128)(2,1)S(1)}, u32[]{:S(2)}, u32[]{:S(2)}) collective-permute-start(bf16[272,128]{1,0:T(8,128)(2,1)S(1)} %get-tuple-element.39), channel_id=1, source_target_pairs={{0,4},{2,6},{4,0},{6,2},{8,12},{10,14},{12,8},{14,10},{16,20},{18,... | collective-permute-start | bytes 208904 | tf_op jit(solution)/shard_map/ppermute | solution.py:347
  5.7 4.5 %collective-permute-start.2 = (bf16[272,128]{1,0:T(8,128)(2,1)S(1)}, bf16[272,128]{1,0:T(8,128)(2,1)S(1)}, u32[]{:S(2)}, u32[]{:S(2)}) collective-permute-start(bf16[272,128]{1,0:T(8,128)(2,1)S(1)} %get-tuple-element.40), channel_id=1, source_target_pairs={{0,6},{2,4},{4,2},{6,0},{8,14},{10,12},{12,10},{14,8},{16,22},{18,... | collective-permute-start | bytes 208904 | tf_op jit(solution)/shard_map/ppermute | solution.py:347
  10.6 3.1 %collective-permute-start.4 = (bf16[256,128]{1,0:T(8,128)(2,1)S(1)}, bf16[256,128]{1,0:T(8,128)(2,1)S(1)}, u32[]{:S(2)}, u32[]{:S(2)}) collective-permute-start(bf16[256,128]{1,0:T(8,128)(2,1)S(1)} %get-tuple-element.44), channel_id=1, source_target_pairs={{0,2},{2,0},{4,6},{6,4},{8,10},{10,8},{12,14},{14,12},{16,18},{18,... | collective-permute-start | bytes 196616 | tf_op jit(solution)/shard_map/ppermute | solution.py:347
  11.2 3.7 %collective-permute-start.5 = (bf16[256,128]{1,0:T(8,128)(2,1)S(1)}, bf16[256,128]{1,0:T(8,128)(2,1)S(1)}, u32[]{:S(2)}, u32[]{:S(2)}) collective-permute-start(bf16[256,128]{1,0:T(8,128)(2,1)S(1)} %get-tuple-element.45), channel_id=1, source_target_pairs={{0,4},{2,6},{4,0},{6,2},{8,12},{10,14},{12,8},{14,10},{16,20},{18,... | collective-permute-start | bytes 196616 | tf_op jit(solution)/shard_map/ppermute | solution.py:347
  12.5 4.0 %collective-permute-start.6 = (bf16[256,128]{1,0:T(8,128)(2,1)S(1)}, bf16[256,128]{1,0:T(8,128)(2,1)S(1)}, u32[]{:S(2)}, u32[]{:S(2)}) collective-permute-start(bf16[256,128]{1,0:T(8,128)(2,1)S(1)} %get-tuple-element.46), channel_id=1, source_target_pairs={{0,6},{2,4},{4,2},{6,0},{8,14},{10,12},{12,10},{14,8},{16,22},{18,... | collective-permute-start | bytes 196616 | tf_op jit(solution)/shard_map/ppermute | solution.py:347
  16.9 6.9 %collective-permute-start.10 = (bf16[512,128]{1,0:T(8,128)(2,1)S(1)}, bf16[512,128]{1,0:T(8,128)(2,1)S(1)}, u32[]{:S(2)}, u32[]{:S(2)}) collective-permute-start(bf16[512,128]{1,0:T(8,128)(2,1)S(1)} %get-tuple-element.53), channel_id=1, source_target_pairs={{0,2},{2,0},{4,6},{6,4},{8,10},{10,8},{12,14},{14,12},{16,18},{18,... | collective-permute-start | bytes 393224 | tf_op jit(solution)/shard_map/ppermute | solution.py:347
  17.3 6.5 %collective-permute-start.11 = (bf16[512,128]{1,0:T(8,128)(2,1)S(1)}, bf16[512,128]{1,0:T(8,128)(2,1)S(1)}, u32[]{:S(2)}, u32[]{:S(2)}) collective-permute-start(bf16[512,128]{1,0:T(8,128)(2,1)S(1)} %get-tuple-element.54), channel_id=1, source_target_pairs={{0,4},{2,6},{4,0},{6,2},{8,12},{10,14},{12,8},{14,10},{16,20},{18,... | collective-permute-start | bytes 393224 | tf_op jit(solution)/shard_map/ppermute | solution.py:347
  18.4 7.3 %collective-permute-start.12 = (bf16[512,128]{1,0:T(8,128)(2,1)S(1)}, bf16[512,128]{1,0:T(8,128)(2,1)S(1)}, u32[]{:S(2)}, u32[]{:S(2)}) collective-permute-start(bf16[512,128]{1,0:T(8,128)(2,1)S(1)} %get-tuple-element.55), channel_id=1, source_target_pairs={{0,6},{2,4},{4,2},{6,0},{8,14},{10,12},{12,10},{14,8},{16,22},{18,... | collective-permute-start | bytes 393224 | tf_op jit(solution)/shard_map/ppermute | solution.py:347
  19.2 13.2 %collective-permute-start.8 = (bf16[3,528,128]{2,1,0:T(8,128)(2,1)S(1)}, bf16[3,528,128]{2,1,0:T(8,128)(2,1)S(1)}, u32[]{:S(2)}, u32[]{:S(2)}) collective-permute-start(bf16[3,528,128]{2,1,0:T(8,128)(2,1)S(1)} %get-tuple-element.51), channel_id=1, source_target_pairs={{0,8},{2,10},{4,12},{6,14},{8,0},{10,2},{12,4},{14,6},{16,24},{18,... | collective-permute-start | bytes 1216520 | tf_op jit(solution)/shard_map/ppermute | solution.py:356
  19.5 13.8 %collective-permute-start.9 = (bf16[3,528,128]{2,1,0:T(8,128)(2,1)S(1)}, bf16[3,528,128]{2,1,0:T(8,128)(2,1)S(1)}, u32[]{:S(2)}, u32[]{:S(2)}) collective-permute-start(bf16[3,528,128]{2,1,0:T(8,128)(2,1)S(1)} %get-tuple-element.52), channel_id=1, source_target_pairs={{0,0},{2,2},{4,4},{6,6},{8,16},{10,18},{12,20},{14,22},{16,8},{18,... | collective-permute-start | bytes 1216520 | tf_op jit(solution)/shard_map/ppermute | solution.py:356
  36.0 9.1 %collective-permute-start.13 = (bf16[3,288,128]{2,1,0:T(8,128)(2,1)S(1)}, bf16[3,288,128]{2,1,0:T(8,128)(2,1)S(1)}, u32[]{:S(2)}, u32[]{:S(2)}) collective-permute-start(bf16[3,288,128]{2,1,0:T(8,128)(2,1)S(1)} %get-tuple-element.58), channel_id=1, source_target_pairs={{0,8},{2,10},{4,12},{6,14},{8,0},{10,2},{12,4},{14,6},{16,24},{18,... | collective-permute-start | bytes 663560 | tf_op jit(solution)/shard_map/ppermute | solution.py:356
  36.1 9.0 %collective-permute-start.14 = (bf16[3,288,128]{2,1,0:T(8,128)(2,1)S(1)}, bf16[3,288,128]{2,1,0:T(8,128)(2,1)S(1)}, u32[]{:S(2)}, u32[]{:S(2)}) collective-permute-start(bf16[3,288,128]{2,1,0:T(8,128)(2,1)S(1)} %get-tuple-element.59), channel_id=1, source_target_pairs={{0,0},{2,2},{4,4},{6,6},{8,16},{10,18},{12,20},{14,22},{16,8},{18,... | collective-permute-start | bytes 663560 | tf_op jit(solution)/shard_map/ppermute | solution.py:356
  42.5 5.3 %collective-permute-start.18 = (bf16[256,128]{1,0:T(8,128)(2,1)S(1)}, bf16[256,128]{1,0:T(8,128)(2,1)S(1)}, u32[]{:S(2)}, u32[]{:S(2)}) collective-permute-start(bf16[256,128]{1,0:T(8,128)(2,1)S(1)} %get-tuple-element.69), channel_id=1, source_target_pairs={{0,2},{2,0},{4,6},{6,4},{8,10},{10,8},{12,14},{14,12},{16,18},{18,... | collective-permute-start | bytes 196616 | tf_op jit(solution)/shard_map/ppermute | solution.py:347
  43.4 5.0 %collective-permute-start.19 = (bf16[256,128]{1,0:T(8,128)(2,1)S(1)}, bf16[256,128]{1,0:T(8,128)(2,1)S(1)}, u32[]{:S(2)}, u32[]{:S(2)}) collective-permute-start(bf16[256,128]{1,0:T(8,128)(2,1)S(1)} %get-tuple-element.70), channel_id=1, source_target_pairs={{0,4},{2,6},{4,0},{6,2},{8,12},{10,14},{12,8},{14,10},{16,20},{18,... | collective-permute-start | bytes 196616 | tf_op jit(solution)/shard_map/ppermute | solution.py:347
  44.6 4.0 %collective-permute-start.20 = (bf16[256,128]{1,0:T(8,128)(2,1)S(1)}, bf16[256,128]{1,0:T(8,128)(2,1)S(1)}, u32[]{:S(2)}, u32[]{:S(2)}) collective-permute-start(bf16[256,128]{1,0:T(8,128)(2,1)S(1)} %get-tuple-element.71), channel_id=1, source_target_pairs={{0,6},{2,4},{4,2},{6,0},{8,14},{10,12},{12,10},{14,8},{16,22},{18,... | collective-permute-start | bytes 196616 | tf_op jit(solution)/shard_map/ppermute | solution.py:347
  45.7 3.7 %collective-permute-start.15 = (bf16[256,128]{1,0:T(8,128)(2,1)S(1)}, bf16[256,128]{1,0:T(8,128)(2,1)S(1)}, u32[]{:S(2)}, u32[]{:S(2)}) collective-permute-start(bf16[256,128]{1,0:T(8,128)(2,1)S(1)} %get-tuple-element.66), channel_id=1, source_target_pairs={{0,2},{2,0},{4,6},{6,4},{8,10},{10,8},{12,14},{14,12},{16,18},{18,... | collective-permute-start | bytes 196616 | tf_op jit(solution)/shard_map/ppermute | solution.py:347
  46.7 3.7 %collective-permute-start.16 = (bf16[256,128]{1,0:T(8,128)(2,1)S(1)}, bf16[256,128]{1,0:T(8,128)(2,1)S(1)}, u32[]{:S(2)}, u32[]{:S(2)}) collective-permute-start(bf16[256,128]{1,0:T(8,128)(2,1)S(1)} %get-tuple-element.67), channel_id=1, source_target_pairs={{0,4},{2,6},{4,0},{6,2},{8,12},{10,14},{12,8},{14,10},{16,20},{18,... | collective-permute-start | bytes 196616 | tf_op jit(solution)/shard_map/ppermute | solution.py:347
  47.8 4.2 %collective-permute-start.17 = (bf16[256,128]{1,0:T(8,128)(2,1)S(1)}, bf16[256,128]{1,0:T(8,128)(2,1)S(1)}, u32[]{:S(2)}, u32[]{:S(2)}) collective-permute-start(bf16[256,128]{1,0:T(8,128)(2,1)S(1)} %get-tuple-element.68), channel_id=1, source_target_pairs={{0,6},{2,4},{4,2},{6,0},{8,14},{10,12},{12,10},{14,8},{16,22},{18,... | collective-permute-start | bytes 196616 | tf_op jit(solution)/shard_map/ppermute | solution.py:347

commit v10 on v9

--- a/solution.py
+++ b/solution.py
@@ -121,14 +121,6 @@
                 out[spot, rows : 2 * rows] = queries[k][...]
                 out[spot, 2 * rows :] = values[k][rows:]
 
-    last = lax.axis_size("tm") // GROUP - 1
-
-    @pl.when((plane() == 0) | (plane() == last))
-    def _():
-        second[:, second.shape[1] - ID_ROWS :] = jnp.zeros(
-            (RADIUS, ID_ROWS, second.shape[2]), second.dtype
-        )
-
 
 def join_kernel(*refs):
     pieces, out, sems = refs[:GROUP], refs[GROUP], refs[GROUP + 1]
@@ -214,34 +206,36 @@
         peaks[i, b] = jnp.broadcast_to(peak, (peak.shape[0], width))
 
 
-def lend_kernel(edge_a, edge_b, plane_turned, plane_beside, first, second, turned, ordered, results):
-    rows, width = (ordered.shape[2] - ID_ROWS) // 2, ordered.shape[3]
-    odd = lax.rem(plane(), 2)
-    ordered[1 - odd] = edge_a[...]
-    ordered[odd] = edge_b[...]
+def lend_kernel(second, edge, plane_turned, plane_beside, result, turned):
+    rows, width = (edge.shape[1] - ID_ROWS) // 2, edge.shape[2]
+    above = lax.rem(plane() + 1 + second, 2)
     lane = lax.broadcasted_iota(jnp.int32, (rows, width), 1)
-    blocks = [slice(0, (j + 1) * rows) for j in range(RADIUS)]
-    blocks += [slice((j + 1) * rows, GROUP * rows) for j in range(RADIUS)]
-
-    def scores_of(e):
-        side, j = e // RADIUS, e % RADIUS
-        marks = marks_turned(ordered[side, j, 2 * rows :])
-        query = ordered[side, j, rows : 2 * rows]
+
+    def place_of(n):
+        return n + above * (RADIUS - 1 - 2 * n), above * (GROUP - 1 - n)
+
+    def near(n):
+        return pl.ds(pl.multiple_of(place_of(n)[1] * rows, rows), (n + 1) * rows)
+
+    def scores_of(n):
+        j = place_of(n)[0]
+        marks = marks_turned(edge[j, 2 * rows :])
+        query = edge[j, rows : 2 * rows]
         for part, x in enumerate(marks):
-            at = slice(e * rows + part * width, e * rows + (part + 1) * width)
+            at = pl.ds(pl.multiple_of(j * rows + part * width, width), width)
             turned[:width, at] = jnp.transpose(query[part * width : (part + 1) * width])
             turned[width:, at] = x
-        return product(stacked_ask(query, marks), plane_turned[0, :, blocks[e]])
+        return product(stacked_ask(query, marks), plane_turned[0, :, near(n)])
 
     ahead = scores_of(0)
-    for e in range(2 * RADIUS):
-        side, j = e // RADIUS, e % RADIUS
+    for n in range(RADIUS):
+        j = place_of(n)[0]
         scores = ahead
-        if e + 1 < 2 * RADIUS:
-            ahead = scores_of(e + 1)
-        peak, mixed = attend(scores, None, plane_beside[0, blocks[e]])
+        if n + 1 < RADIUS:
+            ahead = scores_of(n + 1)
+        peak, mixed = attend(scores, None, plane_beside[0, near(n)])
         mean = by_head(mixed[:, :width], rows) / by_head(mixed[:, width:], rows)
-        results[side, j, :rows] = mean.astype(results.dtype)
+        result[j, :rows] = mean.astype(result.dtype)
         logs = peak + jnp.log(mixed[:, width:])
         high = logs.astype(jnp.bfloat16)
         rest = logs - high.astype(jnp.float32)
@@ -249,21 +243,21 @@
         low = (rest - middle.astype(jnp.float32)).astype(jnp.bfloat16)
         picked = jnp.zeros((rows, width), jnp.bfloat16)
         for h in range(width // HEAD):
-            for n, piece in enumerate((high, middle, low)):
-                picked = jnp.where(lane == 8 * h + n, piece[h * rows : (h + 1) * rows], picked)
+            for m, piece in enumerate((high, middle, low)):
+                picked = jnp.where(lane == 8 * h + m, piece[h * rows : (h + 1) * rows], picked)
         for part in range(rows // width):
             stats = jnp.transpose(picked[part * width : (part + 1) * width])
             at = rows + part * STAT_ROWS
-            results[side, j, at : at + STAT_ROWS] = stats[:STAT_ROWS]
-    first[...] = results[1 - odd]
-    second[...] = results[odd]
-
-
-def edge_kernel(edge_a, edge_b, turned, asks, peaks, sums, *refs):
-    outs, (beside, whole) = refs[-GROUP - 2 : -2], refs[-2:]
+            result[j, at : at + STAT_ROWS] = stats[:STAT_ROWS]
+
+
+def edge_kernel(edge_a, edge_b, turned_a, turned_b, asks, peaks, sums, *refs):
+    outs, (turned, beside, whole) = refs[-GROUP - 3 : -3], refs[-3:]
     rows, width = outs[0].shape
     mine = place()
     odd = lax.rem(plane(), 2)
+    for half, base in ((turned_a, RADIUS * (1 - odd)), (turned_b, RADIUS * odd)):
+        turned[:, pl.ds(pl.multiple_of(base * rows, rows), RADIUS * rows)] = half[...]
     beside[:, width:] = jnp.ones((beside.shape[0], width), beside.dtype)
     for edge, base in ((edge_a, RADIUS * (1 - odd)), (edge_b, RADIUS * odd)):
         for j in range(RADIUS):
@@ -290,7 +284,8 @@
     odd = lax.rem(plane(), 2)
     backs[1 - odd] = back_a[...]
     backs[odd] = back_b[...]
-    lane = lax.broadcasted_iota(jnp.int32, (width, width), 1)
+    last = lax.axis_size("tm") // GROUP - 1
+    absent = [jnp.where(plane() == end, NEG, 0.0) for end in (0, last)]
 
     def logs(side, j):
         squares = []
@@ -305,7 +300,7 @@
                 jnp.concatenate([jnp.broadcast_to(x, (HEAD, width)) for x in heads], axis=0)
             )
             squares.append(turned)
-        return jnp.concatenate(squares, axis=0)
+        return jnp.concatenate(squares, axis=0) + absent[side]
 
     for b in range(GROUP):
         theirs = []
@@ -346,16 +341,12 @@
         pairs = lambda k: [(i, i ^ k) for i in range(length)]
         return [pieces[0]] + [lax.ppermute(pieces[k], "tm", pairs(k)) for k in range(1, GROUP)]
 
-    def partner(i, second):
-        spot, inside = divmod(i, GROUP)
-        spot = ((spot + second) ^ 1) - second
-        return min(max(spot, 0), length // GROUP - 1) * GROUP + inside
-
-    def crossed(sent):
-        return [
-            lax.ppermute(sent[s], "tm", [(i, partner(i, s)) for i in range(length)])
-            for s in range(2)
-        ]
+    def crossed(sent, second):
+        planes = range(second, length // GROUP - second)
+        pairs = [(p, ((p + second) ^ 1) - second) for p in planes]
+        return lax.ppermute(
+            sent, "tm", [(p * GROUP + i, q * GROUP + i) for p, q in pairs for i in range(GROUP)]
+        )
 
     part = shape((rows, half), f32)
     square = shape((half, half), bf16)
@@ -403,15 +394,14 @@
     queries = traded(queries)
     video = project(1.0, key_part, other_video, key_rest, stream=[video_copy], after=queries[1:])
     edge = shape((RADIUS, 2 * rows + ID_ROWS, width), bf16)
-    edges = crossed(
-        call(
-            halo_kernel,
-            [edge, edge],
-            ins=[VMEM] * (2 * GROUP) + [ANY],
-            moved=20 * rows * width * 2,
-            name="halo",
-        )(*packs, *queries, video[0])
-    )
+    sent = call(
+        halo_kernel,
+        [edge, edge],
+        ins=[VMEM] * (2 * GROUP) + [ANY],
+        moved=20 * rows * width * 2,
+        name="halo",
+    )(*packs, *queries, video[0])
+    edges = [crossed(sent[i], i) for i in range(2)]
     video = traded(video)
 
     inside, around = GROUP * rows, 2 * RADIUS * rows
@@ -426,26 +416,29 @@
         name="plane",
     )(*packs, *queries, *video)
     back = shape((RADIUS, rows + rows // width * STAT_ROWS, width), bf16)
-    lent_a, lent_b, edge_turned = call(
-        lend_kernel,
-        [back, back, shape((2 * width, around), bf16)],
-        [pltpu.VMEM((2,) + edge.shape, bf16), pltpu.VMEM((2,) + back.shape, bf16)],
-        flops=48 * RADIUS * GROUP * rows * rows * width,
-        moved=8 * around * width * 2,
-        exps=2 * RADIUS * GROUP * rows * rows,
-        name="lend",
-    )(*edges, plane_turned, plane_beside)
-    backs = crossed([lent_a, lent_b])
+    backs, edge_turned = [], []
+    for i in range(2):
+        lent, edge_keys = call(
+            functools.partial(lend_kernel, i),
+            [back, shape((2 * width, RADIUS * rows), bf16)],
+            flops=24 * RADIUS * GROUP * rows * rows * width,
+            moved=4 * around * width * 2,
+            exps=RADIUS * GROUP * rows * rows,
+            name="lend",
+        )(edges[i], plane_turned, plane_beside)
+        backs.append(crossed(lent, i))
+        edge_turned.append(edge_keys)
 
     video_pieces = call(
         edge_kernel,
         [piece] * GROUP,
-        [pltpu.VMEM((around, 2 * width), bf16), pltpu.VMEM((GROUP, rows, width), bf16)],
+        [pltpu.VMEM((2 * width, around), bf16), pltpu.VMEM((around, 2 * width), bf16)]
+        + [pltpu.VMEM((GROUP, rows, width), bf16)],
         flops=48 * RADIUS * GROUP * rows * rows * width,
         moved=8 * around * width * 2,
         exps=2 * RADIUS * GROUP * rows * rows,
         name="edge",
-    )(*edges, edge_turned, asks, peaks, sums)
+    )(*edges, *edge_turned, asks, peaks, sums)
     audio_pieces = call(
         merge_kernel,
         [piece] * GROUP,

time: 53.3 us -> 54.7 us (1.026)
  the two profiles are of different devices: /device:TPU:9 before, /device:TPU:0 now
where the time goes in v10:
time: 54.7 us; the launch traced here: 54.5 us
  starting transfers between devices  24.4 us (45%)
  Pallas kernels  18 us (33%)
  waiting for transfers between devices  11.1 us (20%)
  between operations  0.94 us (2%)
    ppermute x4, starting transfers between devices, crossed(): lax.ppermute(sent, 'tm', [(p * GROUP + i, q * GROUP + i) for p, q in pair...  11.2 us
    ppermute x15, starting transfers between devices, traded(): lax.ppermute(pieces[k], 'tm', pairs(k))  10.2 us
    ppermute x15, waiting for transfers between devices, traded(): lax.ppermute(pieces[k], 'tm', pairs(k))  8.22 us
    pallas_call x1, Pallas kernels, local(): call(plane_kernel, [shape((2, GROUP, heads * rows, n * width), f32) for n...  6.63 us
    ppermute x2, starting transfers between devices, swapped(): return lax.ppermute(x, 'head', [(0, 1), (1, 0)])  3.11 us
    pallas_call x2, Pallas kernels, local(): call(functools.partial(lend_kernel, i), [back, shape((2 * width, RADIUS *...  3.1 us
    pallas_call x1, Pallas kernels, local(): call(edge_kernel, [piece] * GROUP, [pltpu.VMEM((2 * width, around), bf16)...  2.65 us
    ppermute x2, waiting for transfers between devices, swapped(): return lax.ppermute(x, 'head', [(0, 1), (1, 0)])  2.22 us
  transfers between devices with their start and end apart: 21, of which 11 were waited for; matrix products, arithmetic and copies ran while one was open for 0% of the time, Pallas kernels for 31%

profile of v10, /device:TPU:0, one launch (start us, length us, event | category | flops | bytes accessed | tf_op | source)
XLA Modules:
  0.0 54.5 jit_solution(11022674126968056416)
XLA Ops:
  0.6 3.0 %collective-permute-start.3 = (bf16[256,512]{1,0:T(8,128)(2,1)}, bf16[256,512]{1,0:T(8,128)(2,1)S(1)}, u32[]{:S(2)}, u32[]{:S(2)}) collective-permute-start(bf16[256,512]{1,0:T(8,128)(2,1)} %audio.3), channel_id=1, source_target_pairs={{0,1},{1,0},{2,3},{3,2},{4,5},{5,4},{6,7},{7,6},{8,9},{9,8},{10,11... | collective-permute-start | bytes 786440 | tf_op jit(solution)/shard_map/ppermute | solution.py:338
  3.7 0.1 collective-permute-start.7
  3.7 1.0 %split.1 = (bf16[272,128]{1,0:T(8,128)(2,1)S(1)}, bf16[272,128]{1,0:T(8,128)(2,1)S(1)}, bf16[272,128]{1,0:T(8,128)(2,1)S(1)}, bf16[272,128]{1,0:T(8,128)(2,1)S(1)}) custom-call(bf16[256,512]{1,0:T(8,128)(2,1)} %audio.3, s32[2,128]{1,0:T(2,128)} %bitcast.1), custom_call_target="tpu_custom_call" | custom-call | bytes 524288 | tf_op jit(solution)/shard_map/split/pallas_call | solution.py:360
  4.7 0.1 collective-permute-start
  4.8 2.0 %collective-permute-start.1 = (bf16[272,128]{1,0:T(8,128)(2,1)S(1)}, bf16[272,128]{1,0:T(8,128)(2,1)S(1)}, u32[]{:S(2)}, u32[]{:S(2)}) collective-permute-start(bf16[272,128]{1,0:T(8,128)(2,1)S(1)} %get-tuple-element.40), channel_id=1, source_target_pairs={{0,4},{2,6},{4,0},{6,2},{8,12},{10,14},{12,8},{14,10},{16,20},{18,... | collective-permute-start | bytes 208904 | tf_op jit(solution)/shard_map/ppermute | solution.py:342
  6.8 0.1 collective-permute-start.2
  6.9 0.0 collective-permute-done.refs_0_.refs_1_
  6.9 1.8 %prepare.1 = (f32[256,512]{1,0:T(8,128)S(1)}, f32[256,512]{1,0:T(8,128)S(1)}, bf16[512,512]{1,0:T(8,128)(2,1)S(1)}, bf16[512,512]{1,0:T(8,128)(2,1)S(1)}, bf16[256,512]{1,0:T(8,128)(2,1)S(1)}) custom-call(bf16[256,512]{1,0:T(8,128)(2,1)} %audio.3, bf16[256,512]{1,0:T(8,128)(2,1)} %video.1, bf16[1024,512]{1,0:T(8,128)(2,1)} %query.1, bf16[1024,512]{1,0:T(8,128)(2,1)} %key.1, ...), custom_call_target="tpu_custom_call" | custom-call | flops 268435456 | bytes 4194304 | tf_op jit(solution)/shard_map/prepare/pallas_call | solution.py:370
  8.7 0.9 %collective-permute-done.1.refs_1_.refs_2_ = bf16[272,128]{1,0:T(8,128)(2,1)S(1)} collective-permute-done((bf16[272,128]{1,0:T(8,128)(2,1)S(1)}, bf16[272,128]{1,0:T(8,128)(2,1)S(1)}, u32[]{:S(2)}, u32[]{:S(2)}) %collective-permute-start.1) | collective-permute-done | bytes 69664 | tf_op jit(solution)/shard_map/ppermute | solution.py:342
  9.6 1.4 %collective-permute-done.2.refs_2_.refs_3_ = bf16[272,128]{1,0:T(8,128)(2,1)S(1)} collective-permute-done((bf16[272,128]{1,0:T(8,128)(2,1)S(1)}, bf16[272,128]{1,0:T(8,128)(2,1)S(1)}, u32[]{:S(2)}, u32[]{:S(2)}) %collective-permute-start.2) | collective-permute-done | bytes 69664 | tf_op jit(solution)/shard_map/ppermute | solution.py:342
  10.9 0.1 collective-permute-done.3.other
  11.0 0.4 project.2
  11.4 0.5 collective-permute-start.4
  11.9 1.7 %collective-permute-start.5 = (bf16[256,128]{1,0:T(8,128)(2,1)S(1)}, bf16[256,128]{1,0:T(8,128)(2,1)S(1)}, u32[]{:S(2)}, u32[]{:S(2)}) collective-permute-start(bf16[256,128]{1,0:T(8,128)(2,1)S(1)} %get-tuple-element.46), channel_id=1, source_target_pairs={{0,4},{2,6},{4,0},{6,2},{8,12},{10,14},{12,8},{14,10},{16,20},{18,... | collective-permute-start | bytes 196616 | tf_op jit(solution)/shard_map/ppermute | solution.py:342
  13.6 0.1 collective-permute-start.6
  13.6 2.2 %collective-permute-done.7.other = bf16[256,512]{1,0:T(8,128)(2,1)S(1)} collective-permute-done((bf16[256,512]{1,0:T(8,128)(2,1)}, bf16[256,512]{1,0:T(8,128)(2,1)S(1)}, u32[]{:S(2)}, u32[]{:S(2)}) %collective-permute-start.7) | collective-permute-done | bytes 262176 | tf_op jit(solution)/shard_map/ppermute | solution.py:338
  15.8 0.0 collective-permute-done.4.refs_1_.refs_5_
  15.8 0.5 collective-permute-done.5.refs_2_.refs_6_
  16.3 1.4 %collective-permute-done.6.refs_3_.refs_7_ = bf16[256,128]{1,0:T(8,128)(2,1)S(1)} collective-permute-done((bf16[256,128]{1,0:T(8,128)(2,1)S(1)}, bf16[256,128]{1,0:T(8,128)(2,1)S(1)}, u32[]{:S(2)}, u32[]{:S(2)}) %collective-permute-start.6) | collective-permute-done | bytes 65568 | tf_op jit(solution)/shard_map/ppermute | solution.py:342
  17.6 0.4 project.3
  18.0 0.2 collective-permute-start.9
  18.3 1.5 %collective-permute-start.10 = (bf16[512,128]{1,0:T(8,128)(2,1)S(1)}, bf16[512,128]{1,0:T(8,128)(2,1)S(1)}, u32[]{:S(2)}, u32[]{:S(2)}) collective-permute-start(bf16[512,128]{1,0:T(8,128)(2,1)S(1)} %get-tuple-element.54), channel_id=1, source_target_pairs={{0,4},{2,6},{4,0},{6,2},{8,12},{10,14},{12,8},{14,10},{16,20},{18,... | collective-permute-start | bytes 393224 | tf_op jit(solution)/shard_map/ppermute | solution.py:342
  19.7 0.2 collective-permute-start.11
  20.0 0.1 halo.1
  20.0 0.7 %collective-permute-start.13 = (bf16[3,528,128]{2,1,0:T(8,128)(2,1)S(1)}, bf16[3,528,128]{2,1,0:T(8,128)(2,1)S(1)}, u32[]{:S(2)}, u32[]{:S(2)}) collective-permute-start(bf16[3,528,128]{2,1,0:T(8,128)(2,1)S(1)} %get-tuple-element.59), channel_id=1, source_target_pairs={{8,16},{10,18},{12,20},{14,22},{16,8},{18,10},{20,12},{22,14},{9,1... | collective-permute-start | bytes 1216520 | tf_op jit(solution)/shard_map/ppermute | solution.py:347
  20.7 4.4 %collective-permute-start.8 = (bf16[3,528,128]{2,1,0:T(8,128)(2,1)S(1)}, bf16[3,528,128]{2,1,0:T(8,128)(2,1)S(1)}, u32[]{:S(2)}, u32[]{:S(2)}) collective-permute-start(bf16[3,528,128]{2,1,0:T(8,128)(2,1)S(1)} %get-tuple-element.52), channel_id=1, source_target_pairs={{0,8},{2,10},{4,12},{6,14},{8,0},{10,2},{12,4},{14,6},{16,24},{18,... | collective-permute-start | bytes 1216520 | tf_op jit(solution)/shard_map/ppermute | solution.py:347
  25.2 0.0 collective-permute-done.9.refs_9_
  25.2 0.0 collective-permute-done.10.refs_10_
  25.2 1.1 %collective-permute-done.11.refs_11_ = bf16[512,128]{1,0:T(8,128)(2,1)S(1)} collective-permute-done((bf16[512,128]{1,0:T(8,128)(2,1)S(1)}, bf16[512,128]{1,0:T(8,128)(2,1)S(1)}, u32[]{:S(2)}, u32[]{:S(2)}) %collective-permute-start.11) | collective-permute-done | bytes 131104 | tf_op jit(solution)/shard_map/ppermute | solution.py:342
  26.2 6.6 %plane.1 = (f32[2,4,512,128]{3,2,1,0:T(8,128)S(1)}, f32[2,4,512,256]{3,2,1,0:T(8,128)S(1)}, bf16[2,256,1024]{2,1,0:T(8,128)(2,1)S(1)}, bf16[2,1024,256]{2,1,0:T(8,128)(2,1)S(1)}, bf16[2,4,512,256]{3,2,1,0:T(8,128)(2,1)S(1)}) custom-call(bf16[272,128]{1,0:T(8,128)(2,1)S(1)} %get-tuple-element.38.refs_0_, ...), custom_call_target="tpu_custom_call" | custom-call | flops 4294967296 | bytes 2097152 | tf_op jit(solution)/shard_map/plane/pallas_call | solution.py:408
  32.9 0.0 collective-permute-done.13.edge.edge_b
  32.9 1.6 %lend.3 = (bf16[3,288,128]{2,1,0:T(8,128)(2,1)S(1)}, bf16[256,768]{1,0:T(8,128)(2,1)S(1)}) custom-call(bf16[3,528,128]{2,1,0:T(8,128)(2,1)S(1)} %collective-permute-done.13.edge.edge_b, bf16[2,256,1024]{2,1,0:T(8,128)(2,1)S(1)} %get-tuple-element.56.plane_turned, bf16[2,1024,256]{2,1,0:T(8,128)(2,1)S(1)} %get-tuple-element.57.plane_beside), custom_call_target="tpu_custom_call" | custom-call | flops 2415919104 | bytes 1572864 | tf_op jit(solution)/shard_map/lend/pallas_call | solution.py:421
  34.5 0.8 %collective-permute-start.14 = (bf16[3,288,128]{2,1,0:T(8,128)(2,1)S(1)}, bf16[3,288,128]{2,1,0:T(8,128)(2,1)S(1)}, u32[]{:S(2)}, u32[]{:S(2)}) collective-permute-start(bf16[3,288,128]{2,1,0:T(8,128)(2,1)S(1)} %get-tuple-element.60), channel_id=1, source_target_pairs={{8,16},{10,18},{12,20},{14,22},{16,8},{18,10},{20,12},{22,14},{9,1... | collective-permute-start | bytes 663560 | tf_op jit(solution)/shard_map/ppermute | solution.py:347
  35.3 0.0 collective-permute-done.8.edge.edge_a
  35.3 1.5 %lend.2 = (bf16[3,288,128]{2,1,0:T(8,128)(2,1)S(1)}, bf16[256,768]{1,0:T(8,128)(2,1)S(1)}) custom-call(bf16[3,528,128]{2,1,0:T(8,128)(2,1)S(1)} %collective-permute-done.8.edge.edge_a, bf16[2,256,1024]{2,1,0:T(8,128)(2,1)S(1)} %get-tuple-element.56.plane_turned, bf16[2,1024,256]{2,1,0:T(8,128)(2,1)S(1)} %get-tuple-element.57.plane_beside), custom_call_target="tpu_custom_call" | custom-call | flops 2415919104 | bytes 1572864 | tf_op jit(solution)/shard_map/lend/pallas_call | solution.py:421
  36.9 5.2 %collective-permute-start.12 = (bf16[3,288,128]{2,1,0:T(8,128)(2,1)S(1)}, bf16[3,288,128]{2,1,0:T(8,128)(2,1)S(1)}, u32[]{:S(2)}, u32[]{:S(2)}) collective-permute-start(bf16[3,288,128]{2,1,0:T(8,128)(2,1)S(1)} %get-tuple-element.58), channel_id=1, source_target_pairs={{0,8},{2,10},{4,12},{6,14},{8,0},{10,2},{12,4},{14,6},{16,24},{18,... | collective-permute-start | bytes 663560 | tf_op jit(solution)/shard_map/ppermute | solution.py:347
  42.1 2.6 %edge.1 = (bf16[256,128]{1,0:T(8,128)(2,1)S(1)}, bf16[256,128]{1,0:T(8,128)(2,1)S(1)}, bf16[256,128]{1,0:T(8,128)(2,1)S(1)}, bf16[256,128]{1,0:T(8,128)(2,1)S(1)}) custom-call(bf16[3,528,128]{2,1,0:T(8,128)(2,1)S(1)} %collective-permute-done.8.edge.edge_a, bf16[3,528,128]{2,1,0:T(8,128)(2,1)S(1)} %collective-permute-done.13.edge.edge_b, ...), custom_call_target="tpu_custom_call" | custom-call | flops 4831838208 | bytes 3145728 | tf_op jit(solution)/shard_map/edge/pallas_call | solution.py:432
  44.7 0.1 collective-permute-start.18
  44.8 1.5 %collective-permute-start.19 = (bf16[256,128]{1,0:T(8,128)(2,1)S(1)}, bf16[256,128]{1,0:T(8,128)(2,1)S(1)}, u32[]{:S(2)}, u32[]{:S(2)}) collective-permute-start(bf16[256,128]{1,0:T(8,128)(2,1)S(1)} %get-tuple-element.72), channel_id=1, source_target_pairs={{0,4},{2,6},{4,0},{6,2},{8,12},{10,14},{12,8},{14,10},{16,20},{18,... | collective-permute-start | bytes 196616 | tf_op jit(solution)/shard_map/ppermute | solution.py:342
  46.3 0.3 collective-permute-start.20
  46.7 0.0 collective-permute-done.14.back_b
  46.7 0.6 %collective-permute-done.12.back_a = bf16[3,288,128]{2,1,0:T(8,128)(2,1)S(1)} collective-permute-done((bf16[3,288,128]{2,1,0:T(8,128)(2,1)S(1)}, bf16[3,288,128]{2,1,0:T(8,128)(2,1)S(1)}, u32[]{:S(2)}, u32[]{:S(2)}) %collective-permute-start.12) | collective-permute-done | bytes 221216 | tf_op jit(solution)/shard_map/ppermute | solution.py:347
  47.3 0.6 %merge.1 = (bf16[256,128]{1,0:T(8,128)(2,1)S(1)}, bf16[256,128]{1,0:T(8,128)(2,1)S(1)}, bf16[256,128]{1,0:T(8,128)(2,1)S(1)}, bf16[256,128]{1,0:T(8,128)(2,1)S(1)}) custom-call(bf16[3,288,128]{2,1,0:T(8,128)(2,1)S(1)} %collective-permute-done.12.back_a, bf16[3,288,128]{2,1,0:T(8,128)(2,1)S(1)} %collective-permute-done.14.back_b, ...), custom_call_target="tpu_custom_call" | custom-call | bytes 2097152 | tf_op jit(solution)/shard_map/merge/pallas_call | solution.py:442
  47.9 0.1 collective-permute-start.15
  47.9 1.4 %collective-permute-start.16 = (bf16[256,128]{1,0:T(8,128)(2,1)S(1)}, bf16[256,128]{1,0:T(8,128)(2,1)S(1)}, u32[]{:S(2)}, u32[]{:S(2)}) collective-permute-start(bf16[256,128]{1,0:T(8,128)(2,1)S(1)} %get-tuple-element.69), channel_id=1, source_target_pairs={{0,4},{2,6},{4,0},{6,2},{8,12},{10,14},{12,8},{14,10},{16,20},{18,... | collective-permute-start | bytes 196616 | tf_op jit(solution)/shard_map/ppermute | solution.py:342
  49.4 0.0 collective-permute-done.18.refs_1_
  49.4 0.4 collective-permute-start.17
  49.8 0.0 collective-permute-done.19.refs_2_
  49.8 0.6 %collective-permute-done.20.refs_3_ = bf16[256,128]{1,0:T(8,128)(2,1)S(1)} collective-permute-done((bf16[256,128]{1,0:T(8,128)(2,1)S(1)}, bf16[256,128]{1,0:T(8,128)(2,1)S(1)}, u32[]{:S(2)}, u32[]{:S(2)}) %collective-permute-start.20) | collective-permute-done | bytes 65568 | tf_op jit(solution)/shard_map/ppermute | solution.py:342
  50.4 0.7 %join.3 = bf16[256,512]{1,0:T(8,128)(2,1)} custom-call(bf16[256,128]{1,0:T(8,128)(2,1)S(1)} %get-tuple-element.66.refs_0_, bf16[256,128]{1,0:T(8,128)(2,1)S(1)} %collective-permute-done.18.refs_1_, bf16[256,128]{1,0:T(8,128)(2,1)S(1)} %collective-permute-done.19.refs_2_, bf16[256,128]{1,0:T(8,128)(2,1)S(1)} %collective-permute-done.20.refs_3_), custom_call_target="tpu_custom_call" | custom-call | bytes 524288 | tf_op jit(solution)/shard_map/join/pallas_call | solution.py:453
  51.1 0.0 collective-permute-done.15.refs_1_
  51.1 1.5 %collective-permute-done.16.refs_2_ = bf16[256,128]{1,0:T(8,128)(2,1)S(1)} collective-permute-done((bf16[256,128]{1,0:T(8,128)(2,1)S(1)}, bf16[256,128]{1,0:T(8,128)(2,1)S(1)}, u32[]{:S(2)}, u32[]{:S(2)}) %collective-permute-start.16) | collective-permute-done | bytes 65568 | tf_op jit(solution)/shard_map/ppermute | solution.py:342
  52.6 1.0 %collective-permute-done.17.refs_3_ = bf16[256,128]{1,0:T(8,128)(2,1)S(1)} collective-permute-done((bf16[256,128]{1,0:T(8,128)(2,1)S(1)}, bf16[256,128]{1,0:T(8,128)(2,1)S(1)}, u32[]{:S(2)}, u32[]{:S(2)}) %collective-permute-start.17) | collective-permute-done | bytes 65568 | tf_op jit(solution)/shard_map/ppermute | solution.py:342
  53.6 0.7 %join.2 = bf16[256,512]{1,0:T(8,128)(2,1)} custom-call(bf16[256,128]{1,0:T(8,128)(2,1)S(1)} %get-tuple-element.67.refs_0_, bf16[256,128]{1,0:T(8,128)(2,1)S(1)} %collective-permute-done.15.refs_1_, bf16[256,128]{1,0:T(8,128)(2,1)S(1)} %collective-permute-done.16.refs_2_, bf16[256,128]{1,0:T(8,128)(2,1)S(1)} %collective-permute-done.17.refs_3_), custom_call_target="tpu_custom_call" | custom-call | bytes 524288 | tf_op jit(solution)/shard_map/join/pallas_call | solution.py:453
Async XLA Ops:
  0.6 10.4 %collective-permute-start.3 = (bf16[256,512]{1,0:T(8,128)(2,1)}, bf16[256,512]{1,0:T(8,128)(2,1)S(1)}, u32[]{:S(2)}, u32[]{:S(2)}) collective-permute-start(bf16[256,512]{1,0:T(8,128)(2,1)} %audio.3), channel_id=1, source_target_pairs={{0,1},{1,0},{2,3},{3,2},{4,5},{5,4},{6,7},{7,6},{8,9},{9,8},{10,11... | collective-permute-start | bytes 786440 | tf_op jit(solution)/shard_map/ppermute | solution.py:338
  3.7 12.1 %collective-permute-start.7 = (bf16[256,512]{1,0:T(8,128)(2,1)}, bf16[256,512]{1,0:T(8,128)(2,1)S(1)}, u32[]{:S(2)}, u32[]{:S(2)}) collective-permute-start(bf16[256,512]{1,0:T(8,128)(2,1)} %video.1), channel_id=1, source_target_pairs={{0,1},{1,0},{2,3},{3,2},{4,5},{5,4},{6,7},{7,6},{8,9},{9,8},{10,11... | collective-permute-start | bytes 786440 | tf_op jit(solution)/shard_map/ppermute | solution.py:338
  4.7 2.1 %collective-permute-start = (bf16[272,128]{1,0:T(8,128)(2,1)S(1)}, bf16[272,128]{1,0:T(8,128)(2,1)S(1)}, u32[]{:S(2)}, u32[]{:S(2)}) collective-permute-start(bf16[272,128]{1,0:T(8,128)(2,1)S(1)} %get-tuple-element.39), channel_id=1, source_target_pairs={{0,2},{2,0},{4,6},{6,4},{8,10},{10,8},{12,14},{14,12},{16,18},{18,... | collective-permute-start | bytes 208904 | tf_op jit(solution)/shard_map/ppermute | solution.py:342
  4.8 4.8 %collective-permute-start.1 = (bf16[272,128]{1,0:T(8,128)(2,1)S(1)}, bf16[272,128]{1,0:T(8,128)(2,1)S(1)}, u32[]{:S(2)}, u32[]{:S(2)}) collective-permute-start(bf16[272,128]{1,0:T(8,128)(2,1)S(1)} %get-tuple-element.40), channel_id=1, source_target_pairs={{0,4},{2,6},{4,0},{6,2},{8,12},{10,14},{12,8},{14,10},{16,20},{18,... | collective-permute-start | bytes 208904 | tf_op jit(solution)/shard_map/ppermute | solution.py:342
  6.8 4.1 %collective-permute-start.2 = (bf16[272,128]{1,0:T(8,128)(2,1)S(1)}, bf16[272,128]{1,0:T(8,128)(2,1)S(1)}, u32[]{:S(2)}, u32[]{:S(2)}) collective-permute-start(bf16[272,128]{1,0:T(8,128)(2,1)S(1)} %get-tuple-element.41), channel_id=1, source_target_pairs={{0,6},{2,4},{4,2},{6,0},{8,14},{10,12},{12,10},{14,8},{16,22},{18,... | collective-permute-start | bytes 208904 | tf_op jit(solution)/shard_map/ppermute | solution.py:342
  11.4 4.4 %collective-permute-start.4 = (bf16[256,128]{1,0:T(8,128)(2,1)S(1)}, bf16[256,128]{1,0:T(8,128)(2,1)S(1)}, u32[]{:S(2)}, u32[]{:S(2)}) collective-permute-start(bf16[256,128]{1,0:T(8,128)(2,1)S(1)} %get-tuple-element.45), channel_id=1, source_target_pairs={{0,2},{2,0},{4,6},{6,4},{8,10},{10,8},{12,14},{14,12},{16,18},{18,... | collective-permute-start | bytes 196616 | tf_op jit(solution)/shard_map/ppermute | solution.py:342
  11.9 4.4 %collective-permute-start.5 = (bf16[256,128]{1,0:T(8,128)(2,1)S(1)}, bf16[256,128]{1,0:T(8,128)(2,1)S(1)}, u32[]{:S(2)}, u32[]{:S(2)}) collective-permute-start(bf16[256,128]{1,0:T(8,128)(2,1)S(1)} %get-tuple-element.46), channel_id=1, source_target_pairs={{0,4},{2,6},{4,0},{6,2},{8,12},{10,14},{12,8},{14,10},{16,20},{18,... | collective-permute-start | bytes 196616 | tf_op jit(solution)/shard_map/ppermute | solution.py:342
  13.6 4.0 %collective-permute-start.6 = (bf16[256,128]{1,0:T(8,128)(2,1)S(1)}, bf16[256,128]{1,0:T(8,128)(2,1)S(1)}, u32[]{:S(2)}, u32[]{:S(2)}) collective-permute-start(bf16[256,128]{1,0:T(8,128)(2,1)S(1)} %get-tuple-element.47), channel_id=1, source_target_pairs={{0,6},{2,4},{4,2},{6,0},{8,14},{10,12},{12,10},{14,8},{16,22},{18,... | collective-permute-start | bytes 196616 | tf_op jit(solution)/shard_map/ppermute | solution.py:342
  18.0 7.1 %collective-permute-start.9 = (bf16[512,128]{1,0:T(8,128)(2,1)S(1)}, bf16[512,128]{1,0:T(8,128)(2,1)S(1)}, u32[]{:S(2)}, u32[]{:S(2)}) collective-permute-start(bf16[512,128]{1,0:T(8,128)(2,1)S(1)} %get-tuple-element.53), channel_id=1, source_target_pairs={{0,2},{2,0},{4,6},{6,4},{8,10},{10,8},{12,14},{14,12},{16,18},{18,... | collective-permute-start | bytes 393224 | tf_op jit(solution)/shard_map/ppermute | solution.py:342
  18.3 6.9 %collective-permute-start.10 = (bf16[512,128]{1,0:T(8,128)(2,1)S(1)}, bf16[512,128]{1,0:T(8,128)(2,1)S(1)}, u32[]{:S(2)}, u32[]{:S(2)}) collective-permute-start(bf16[512,128]{1,0:T(8,128)(2,1)S(1)} %get-tuple-element.54), channel_id=1, source_target_pairs={{0,4},{2,6},{4,0},{6,2},{8,12},{10,14},{12,8},{14,10},{16,20},{18,... | collective-permute-start | bytes 393224 | tf_op jit(solution)/shard_map/ppermute | solution.py:342
  19.7 6.5 %collective-permute-start.11 = (bf16[512,128]{1,0:T(8,128)(2,1)S(1)}, bf16[512,128]{1,0:T(8,128)(2,1)S(1)}, u32[]{:S(2)}, u32[]{:S(2)}) collective-permute-start(bf16[512,128]{1,0:T(8,128)(2,1)S(1)} %get-tuple-element.55), channel_id=1, source_target_pairs={{0,6},{2,4},{4,2},{6,0},{8,14},{10,12},{12,10},{14,8},{16,22},{18,... | collective-permute-start | bytes 393224 | tf_op jit(solution)/shard_map/ppermute | solution.py:342
  20.0 12.8 %collective-permute-start.13 = (bf16[3,528,128]{2,1,0:T(8,128)(2,1)S(1)}, bf16[3,528,128]{2,1,0:T(8,128)(2,1)S(1)}, u32[]{:S(2)}, u32[]{:S(2)}) collective-permute-start(bf16[3,528,128]{2,1,0:T(8,128)(2,1)S(1)} %get-tuple-element.59), channel_id=1, source_target_pairs={{8,16},{10,18},{12,20},{14,22},{16,8},{18,10},{20,12},{22,14},{9,1... | collective-permute-start | bytes 1216520 | tf_op jit(solution)/shard_map/ppermute | solution.py:347
  20.7 14.6 %collective-permute-start.8 = (bf16[3,528,128]{2,1,0:T(8,128)(2,1)S(1)}, bf16[3,528,128]{2,1,0:T(8,128)(2,1)S(1)}, u32[]{:S(2)}, u32[]{:S(2)}) collective-permute-start(bf16[3,528,128]{2,1,0:T(8,128)(2,1)S(1)} %get-tuple-element.52), channel_id=1, source_target_pairs={{0,8},{2,10},{4,12},{6,14},{8,0},{10,2},{12,4},{14,6},{16,24},{18,... | collective-permute-start | bytes 1216520 | tf_op jit(solution)/shard_map/ppermute | solution.py:347
  34.5 12.2 %collective-permute-start.14 = (bf16[3,288,128]{2,1,0:T(8,128)(2,1)S(1)}, bf16[3,288,128]{2,1,0:T(8,128)(2,1)S(1)}, u32[]{:S(2)}, u32[]{:S(2)}) collective-permute-start(bf16[3,288,128]{2,1,0:T(8,128)(2,1)S(1)} %get-tuple-element.60), channel_id=1, source_target_pairs={{8,16},{10,18},{12,20},{14,22},{16,8},{18,10},{20,12},{22,14},{9,1... | collective-permute-start | bytes 663560 | tf_op jit(solution)/shard_map/ppermute | solution.py:347
  36.9 10.4 %collective-permute-start.12 = (bf16[3,288,128]{2,1,0:T(8,128)(2,1)S(1)}, bf16[3,288,128]{2,1,0:T(8,128)(2,1)S(1)}, u32[]{:S(2)}, u32[]{:S(2)}) collective-permute-start(bf16[3,288,128]{2,1,0:T(8,128)(2,1)S(1)} %get-tuple-element.58), channel_id=1, source_target_pairs={{0,8},{2,10},{4,12},{6,14},{8,0},{10,2},{12,4},{14,6},{16,24},{18,... | collective-permute-start | bytes 663560 | tf_op jit(solution)/shard_map/ppermute | solution.py:347
  44.7 4.6 %collective-permute-start.18 = (bf16[256,128]{1,0:T(8,128)(2,1)S(1)}, bf16[256,128]{1,0:T(8,128)(2,1)S(1)}, u32[]{:S(2)}, u32[]{:S(2)}) collective-permute-start(bf16[256,128]{1,0:T(8,128)(2,1)S(1)} %get-tuple-element.71), channel_id=1, source_target_pairs={{0,2},{2,0},{4,6},{6,4},{8,10},{10,8},{12,14},{14,12},{16,18},{18,... | collective-permute-start | bytes 196616 | tf_op jit(solution)/shard_map/ppermute | solution.py:342
  44.8 5.0 %collective-permute-start.19 = (bf16[256,128]{1,0:T(8,128)(2,1)S(1)}, bf16[256,128]{1,0:T(8,128)(2,1)S(1)}, u32[]{:S(2)}, u32[]{:S(2)}) collective-permute-start(bf16[256,128]{1,0:T(8,128)(2,1)S(1)} %get-tuple-element.72), channel_id=1, source_target_pairs={{0,4},{2,6},{4,0},{6,2},{8,12},{10,14},{12,8},{14,10},{16,20},{18,... | collective-permute-start | bytes 196616 | tf_op jit(solution)/shard_map/ppermute | solution.py:342
  46.3 4.0 %collective-permute-start.20 = (bf16[256,128]{1,0:T(8,128)(2,1)S(1)}, bf16[256,128]{1,0:T(8,128)(2,1)S(1)}, u32[]{:S(2)}, u32[]{:S(2)}) collective-permute-start(bf16[256,128]{1,0:T(8,128)(2,1)S(1)} %get-tuple-element.73), channel_id=1, source_target_pairs={{0,6},{2,4},{4,2},{6,0},{8,14},{10,12},{12,10},{14,8},{16,22},{18,... | collective-permute-start | bytes 196616 | tf_op jit(solution)/shard_map/ppermute | solution.py:342
  47.9 3.3 %collective-permute-start.15 = (bf16[256,128]{1,0:T(8,128)(2,1)S(1)}, bf16[256,128]{1,0:T(8,128)(2,1)S(1)}, u32[]{:S(2)}, u32[]{:S(2)}) collective-permute-start(bf16[256,128]{1,0:T(8,128)(2,1)S(1)} %get-tuple-element.68), channel_id=1, source_target_pairs={{0,2},{2,0},{4,6},{6,4},{8,10},{10,8},{12,14},{14,12},{16,18},{18,... | collective-permute-start | bytes 196616 | tf_op jit(solution)/shard_map/ppermute | solution.py:342
  47.9 4.6 %collective-permute-start.16 = (bf16[256,128]{1,0:T(8,128)(2,1)S(1)}, bf16[256,128]{1,0:T(8,128)(2,1)S(1)}, u32[]{:S(2)}, u32[]{:S(2)}) collective-permute-start(bf16[256,128]{1,0:T(8,128)(2,1)S(1)} %get-tuple-element.69), channel_id=1, source_target_pairs={{0,4},{2,6},{4,0},{6,2},{8,12},{10,14},{12,8},{14,10},{16,20},{18,... | collective-permute-start | bytes 196616 | tf_op jit(solution)/shard_map/ppermute | solution.py:342
  49.4 4.2 %collective-permute-start.17 = (bf16[256,128]{1,0:T(8,128)(2,1)S(1)}, bf16[256,128]{1,0:T(8,128)(2,1)S(1)}, u32[]{:S(2)}, u32[]{:S(2)}) collective-permute-start(bf16[256,128]{1,0:T(8,128)(2,1)S(1)} %get-tuple-element.70), channel_id=1, source_target_pairs={{0,6},{2,4},{4,2},{6,0},{8,14},{10,12},{12,10},{14,8},{16,22},{18,... | collective-permute-start | bytes 196616 | tf_op jit(solution)/shard_map/ppermute | solution.py:342

commit v11 on v8

--- a/solution.py
+++ b/solution.py
@@ -103,29 +103,21 @@
         pieces[k][...] = full[:, pl.ds(pl.multiple_of((mine ^ k) * width, width), width)]
 
 
-def halo_kernel(*refs):
-    values, queries, (first, second) = refs[:GROUP], refs[GROUP : 2 * GROUP], refs[-2:]
-    rows = queries[0].shape[0]
+def halo_kernel(ids_at, *refs):
+    pieces, id_packs, outs = refs[:GROUP], refs[GROUP : 2 * GROUP], refs[-2:]
+    rows = outs[0].shape[1] - (ID_ROWS if ids_at else 0)
     mine = place()
     odd = lax.rem(plane(), 2)
     for k in range(GROUP):
         block = mine ^ k
-        for out, skip in ((first, (GROUP - RADIUS) * (1 - odd)), (second, (GROUP - RADIUS) * odd)):
+        for out, skip in zip(outs, ((GROUP - RADIUS) * (1 - odd), (GROUP - RADIUS) * odd)):
             spot = block - skip
 
             @pl.when((spot >= 0) & (spot < RADIUS))
             def _():
-                out[spot, :rows] = values[k][:rows]
-                out[spot, rows : 2 * rows] = queries[k][...]
-                out[spot, 2 * rows :] = values[k][2 * rows :]
-
-    last = lax.axis_size("tm") // GROUP - 1
-
-    @pl.when((plane() == 0) | (plane() == last))
-    def _():
-        second[:, second.shape[1] - ID_ROWS :] = jnp.zeros(
-            (RADIUS, ID_ROWS, second.shape[2]), second.dtype
-        )
+                out[spot, :rows] = pieces[k][:rows]
+                if ids_at:
+                    out[spot, rows:] = id_packs[k][ids_at:]
 
 
 def join_kernel(*refs):
@@ -210,8 +202,8 @@
         peaks[i, b] = jnp.broadcast_to(peak, (peak.shape[0], width))
 
 
-def lend_kernel(edge_a, edge_b, plane_turned, plane_beside, first, second, turned, ordered, results):
-    rows, width = (ordered.shape[2] - ID_ROWS) // 2, ordered.shape[3]
+def lend_kernel(edge_b, edge_a, plane_turned, plane_beside, first, second, turned, ordered, results):
+    rows, width = ordered.shape[2] - ID_ROWS, ordered.shape[3]
     odd = lax.rem(plane(), 2)
     ordered[1 - odd] = edge_a[...]
     ordered[odd] = edge_b[...]
@@ -221,8 +213,8 @@
 
     def scores_of(e):
         side, j = e // RADIUS, e % RADIUS
-        marks = marks_turned(ordered[side, j, 2 * rows :])
-        query = ordered[side, j, rows : 2 * rows]
+        marks = marks_turned(ordered[side, j, rows:])
+        query = ordered[side, j, :rows]
         for part, x in enumerate(marks):
             at = slice(e * rows + part * width, e * rows + (part + 1) * width)
             turned[:width, at] = jnp.transpose(query[part * width : (part + 1) * width])
@@ -255,7 +247,7 @@
     second[...] = results[odd]
 
 
-def edge_kernel(edge_a, edge_b, turned, asks, peaks, sums, *refs):
+def edge_kernel(edge_b, edge_a, turned, asks, peaks, sums, *refs):
     outs, (beside, whole) = refs[-GROUP - 2 : -2], refs[-2:]
     rows, width = outs[0].shape
     mine = place()
@@ -263,7 +255,7 @@
     beside[:, width:] = jnp.ones((beside.shape[0], width), beside.dtype)
     for edge, base in ((edge_a, RADIUS * (1 - odd)), (edge_b, RADIUS * odd)):
         for j in range(RADIUS):
-            beside[pl.ds(pl.multiple_of((base + j) * rows, rows), rows), :width] = edge[j, :rows]
+            beside[pl.ds(pl.multiple_of((base + j) * rows, rows), rows), :width] = edge[j]
     near = [slice(b * rows, (b + RADIUS) * rows) for b in range(GROUP)]
     scores = product(asks[1, 0], turned[:, near[0]])
     for b in range(GROUP):
@@ -286,7 +278,8 @@
     odd = lax.rem(plane(), 2)
     backs[1 - odd] = back_a[...]
     backs[odd] = back_b[...]
-    lane = lax.broadcasted_iota(jnp.int32, (width, width), 1)
+    last = lax.axis_size("tm") // GROUP - 1
+    absent = [jnp.where(plane() == end, NEG, 0.0) for end in (0, last)]
 
     def logs(side, j):
         squares = []
@@ -301,7 +294,7 @@
                 jnp.concatenate([jnp.broadcast_to(x, (HEAD, width)) for x in heads], axis=0)
             )
             squares.append(turned)
-        return jnp.concatenate(squares, axis=0)
+        return jnp.concatenate(squares, axis=0) + absent[side]
 
     for b in range(GROUP):
         theirs = []
@@ -342,16 +335,12 @@
         pairs = lambda k: [(i, i ^ k) for i in range(length)]
         return [pieces[0]] + [lax.ppermute(pieces[k], "tm", pairs(k)) for k in range(1, GROUP)]
 
-    def partner(i, second):
-        spot, inside = divmod(i, GROUP)
-        spot = ((spot + second) ^ 1) - second
-        return min(max(spot, 0), length // GROUP - 1) * GROUP + inside
-
-    def crossed(sent):
-        return [
-            lax.ppermute(sent[s], "tm", [(i, partner(i, s)) for i in range(length)])
-            for s in range(2)
-        ]
+    def crossed(sent, second):
+        planes = range(second, length // GROUP - second)
+        pairs = [(p, ((p + second) ^ 1) - second) for p in planes]
+        return lax.ppermute(
+            sent, "tm", [(p * GROUP + i, q * GROUP + i) for p, q in pairs for i in range(GROUP)]
+        )
 
     part = shape((rows, half), f32)
     square = shape((half, half), bf16)
@@ -397,18 +386,22 @@
 
     queries = project(HEAD**-0.5, query_part, other_audio, query_rest, *packs[1:])
     queries = traded(queries)
-    keys = project(1.0, key_part, other_video, key_rest)
-    edge = shape((RADIUS, 2 * rows + ID_ROWS, width), bf16)
-    edges = crossed(
-        call(
-            halo_kernel,
+    keys = project(1.0, key_part, other_video, key_rest, *queries[1:])
+
+    def halo(pieces, id_packs, *after):
+        edge = shape((RADIUS, rows + (ID_ROWS if id_packs else 0), width), bf16)
+        sent = call(
+            functools.partial(halo_kernel, 2 * rows if id_packs else 0),
             [edge, edge],
-            ins=[VMEM] * (2 * GROUP) + [ANY],
-            moved=20 * rows * width * 2,
+            ins=[VMEM] * (GROUP + len(id_packs)) + [ANY] * len(after),
+            moved=10 * rows * width * 2,
             name="halo",
-        )(*packs, *queries, keys[0])
-    )
+        )(*pieces, *id_packs, *after)
+        return [crossed(sent[i], i) for i in range(2)]
+
+    query_edges = halo(queries, packs, keys[0])
     keys = traded(keys)
+    audio_edges = halo(packs, [], *keys[1:])
 
     inside, around = GROUP * rows, 2 * RADIUS * rows
     peaks, sums, plane_turned, plane_beside, asks = call(
@@ -425,13 +418,13 @@
     lent_a, lent_b, edge_turned = call(
         lend_kernel,
         [back, back, shape((2 * width, around), bf16)],
-        [pltpu.VMEM((2,) + edge.shape, bf16), pltpu.VMEM((2,) + back.shape, bf16)],
+        [pltpu.VMEM((2, RADIUS, rows + ID_ROWS, width), bf16), pltpu.VMEM((2,) + back.shape, bf16)],
         flops=48 * RADIUS * GROUP * rows * rows * width,
         moved=8 * around * width * 2,
         exps=2 * RADIUS * GROUP * rows * rows,
         name="lend",
-    )(*edges, plane_turned, plane_beside)
-    backs = crossed([lent_a, lent_b])
+    )(*query_edges[::-1], plane_turned, plane_beside)
+    backs = [crossed(x, i) for i, x in enumerate((lent_a, lent_b))]
 
     video_pieces = call(
         edge_kernel,
@@ -441,7 +434,7 @@
         moved=8 * around * width * 2,
         exps=2 * RADIUS * GROUP * rows * rows,
         name="edge",
-    )(*edges, edge_turned, asks, peaks, sums)
+    )(*audio_edges[::-1], edge_turned, asks, peaks, sums)
     audio_pieces = call(
         merge_kernel,
         [piece] * GROUP,

time: 53.3 us -> 56.5 us (1.060)
  starting transfers between devices: 22.6 us -> 26 us
    ppermute x4 -> x6, starting transfers between devices: 7.83 us -> 10.3 us  [crossed(): lax.ppermute(sent, 'tm', [(p * GROUP + i, q * GROUP + i) for p, q in pair...]
    ppermute x15, waiting for transfers between devices: 9.4 us -> 11.8 us  [traded(): lax.ppermute(pieces[k], 'tm', pairs(k))]
    ppermute x4 -> x6, waiting for transfers between devices: 2.25 us -> 0.02 us  [crossed(): lax.ppermute(sent, 'tm', [(p * GROUP + i, q * GROUP + i) for p, q in pair...]
    ppermute x15, starting transfers between devices: 13.2 us -> 14.1 us  [traded(): lax.ppermute(pieces[k], 'tm', pairs(k))]
  transfers between devices with their start and end apart: 21 -> 23, of which waited for: 7 -> 7; matrix products, arithmetic and copies ran while one was open for 0% -> 0% of each run, Pallas kernels for 27% -> 29%
where the time goes in v11:
time: 56.5 us; the launch traced here: 56.3 us
  starting transfers between devices  26 us (46%)
  Pallas kernels  17.6 us (31%)
  waiting for transfers between devices  11.8 us (21%)
  between operations  0.99 us (2%)
    ppermute x15, starting transfers between devices, traded(): lax.ppermute(pieces[k], 'tm', pairs(k))  14.1 us
    ppermute x15, waiting for transfers between devices, traded(): lax.ppermute(pieces[k], 'tm', pairs(k))  11.8 us
    ppermute x6, starting transfers between devices, crossed(): lax.ppermute(sent, 'tm', [(p * GROUP + i, q * GROUP + i) for p, q in pair...  10.3 us
    pallas_call x1, Pallas kernels, local(): call(plane_kernel, [shape((2, GROUP, heads * rows, n * width), f32) for n...  6.51 us
    pallas_call x1, Pallas kernels, local(): call(lend_kernel, [back, back, shape((2 * width, around), bf16)], [pltpu....  2.74 us
    pallas_call x1, Pallas kernels, local(): call(edge_kernel, [piece] * GROUP, [pltpu.VMEM((around, 2 * width), bf16)...  2.49 us
    pallas_call x1, Pallas kernels, local(): call(prepare_kernel, [part, part, square, square], [pltpu.VMEM((rows, hal...  1.78 us
    ppermute x2, starting transfers between devices, swapped(): return lax.ppermute(x, 'head', [(0, 1), (1, 0)])  1.53 us
  transfers between devices with their start and end apart: 23, of which 7 were waited for; matrix products, arithmetic and copies ran while one was open for 0% of the time, Pallas kernels for 29%

profile of v11, /device:TPU:9, one launch (start us, length us, event | category | flops | bytes accessed | tf_op | source)
XLA Modules:
  0.0 56.3 jit_solution(14211964588935366418)
XLA Ops:
  0.6 1.3 %collective-permute-start.1 = (bf16[256,512]{1,0:T(8,128)(2,1)}, bf16[256,512]{1,0:T(8,128)(2,1)S(1)}, u32[]{:S(2)}, u32[]{:S(2)}) collective-permute-start(bf16[256,512]{1,0:T(8,128)(2,1)} %audio.3), channel_id=1, source_target_pairs={{0,1},{1,0},{2,3},{3,2},{4,5},{5,4},{6,7},{7,6},{8,9},{9,8},{10,11... | collective-permute-start | bytes 786440 | tf_op jit(solution)/shard_map/ppermute | solution.py:332
  1.9 0.2 collective-permute-start.7
  2.2 1.2 %split.1 = (bf16[528,128]{1,0:T(8,128)(2,1)S(1)}, bf16[528,128]{1,0:T(8,128)(2,1)S(1)}, bf16[528,128]{1,0:T(8,128)(2,1)S(1)}, bf16[528,128]{1,0:T(8,128)(2,1)S(1)}) custom-call(bf16[256,512]{1,0:T(8,128)(2,1)} %audio.3, bf16[256,512]{1,0:T(8,128)(2,1)} %video.3, s32[2,128]{1,0:T(2,128)} %bitcast.1), custom_call_target="tpu_custom_call" | custom-call | bytes 1048576 | tf_op jit(solution)/shard_map/split/pallas_call | solution.py:354
  3.3 1.3 %collective-permute-start = (bf16[528,128]{1,0:T(8,128)(2,1)S(1)}, bf16[528,128]{1,0:T(8,128)(2,1)S(1)}, u32[]{:S(2)}, u32[]{:S(2)}) collective-permute-start(bf16[528,128]{1,0:T(8,128)(2,1)S(1)} %get-tuple-element.38), channel_id=1, source_target_pairs={{0,2},{2,0},{4,6},{6,4},{8,10},{10,8},{12,14},{14,12},{16,18},{18,... | collective-permute-start | bytes 405512 | tf_op jit(solution)/shard_map/ppermute | solution.py:336
  4.6 1.2 %collective-permute-start.2 = (bf16[528,128]{1,0:T(8,128)(2,1)S(1)}, bf16[528,128]{1,0:T(8,128)(2,1)S(1)}, u32[]{:S(2)}, u32[]{:S(2)}) collective-permute-start(bf16[528,128]{1,0:T(8,128)(2,1)S(1)} %get-tuple-element.41), channel_id=1, source_target_pairs={{0,4},{2,6},{4,0},{6,2},{8,12},{10,14},{12,8},{14,10},{16,20},{18,... | collective-permute-start | bytes 405512 | tf_op jit(solution)/shard_map/ppermute | solution.py:336
  5.9 0.5 collective-permute-start.3
  6.3 0.0 collective-permute-done.refs_0_.refs_5_.refs_1_
  6.3 1.8 %prepare.1 = (f32[256,512]{1,0:T(8,128)S(1)}, f32[256,512]{1,0:T(8,128)S(1)}, bf16[512,512]{1,0:T(8,128)(2,1)S(1)}, bf16[512,512]{1,0:T(8,128)(2,1)S(1)}) custom-call(bf16[256,512]{1,0:T(8,128)(2,1)} %audio.3, bf16[256,512]{1,0:T(8,128)(2,1)} %video.3, bf16[1024,512]{1,0:T(8,128)(2,1)} %query.1, bf16[1024,512]{1,0:T(8,128)(2,1)} %key.1, ...), custom_call_target="tpu_custom_call" | custom-call | flops 268435456 | bytes 4194304 | tf_op jit(solution)/shard_map/prepare/pallas_call | solution.py:364
  8.1 1.7 %collective-permute-done.2.refs_1_.refs_6_.refs_2_ = bf16[528,128]{1,0:T(8,128)(2,1)S(1)} collective-permute-done((bf16[528,128]{1,0:T(8,128)(2,1)S(1)}, bf16[528,128]{1,0:T(8,128)(2,1)S(1)}, u32[]{:S(2)}, u32[]{:S(2)}) %collective-permute-start.2) | collective-permute-done | bytes 135200 | tf_op jit(solution)/shard_map/ppermute | solution.py:336
  9.8 3.4 %collective-permute-done.3.refs_2_.refs_7_.refs_3_ = bf16[528,128]{1,0:T(8,128)(2,1)S(1)} collective-permute-done((bf16[528,128]{1,0:T(8,128)(2,1)S(1)}, bf16[528,128]{1,0:T(8,128)(2,1)S(1)}, u32[]{:S(2)}, u32[]{:S(2)}) %collective-permute-start.3) | collective-permute-done | bytes 135200 | tf_op jit(solution)/shard_map/ppermute | solution.py:336
  13.2 0.0 collective-permute-done.1.other
  13.2 0.4 project.2
  13.5 0.1 collective-permute-start.4
  13.6 1.3 %collective-permute-start.5 = (bf16[256,128]{1,0:T(8,128)(2,1)S(1)}, bf16[256,128]{1,0:T(8,128)(2,1)S(1)}, u32[]{:S(2)}, u32[]{:S(2)}) collective-permute-start(bf16[256,128]{1,0:T(8,128)(2,1)S(1)} %get-tuple-element.45), channel_id=1, source_target_pairs={{0,4},{2,6},{4,0},{6,2},{8,12},{10,14},{12,8},{14,10},{16,20},{18,... | collective-permute-start | bytes 196616 | tf_op jit(solution)/shard_map/ppermute | solution.py:336
  14.9 0.8 %collective-permute-start.6 = (bf16[256,128]{1,0:T(8,128)(2,1)S(1)}, bf16[256,128]{1,0:T(8,128)(2,1)S(1)}, u32[]{:S(2)}, u32[]{:S(2)}) collective-permute-start(bf16[256,128]{1,0:T(8,128)(2,1)S(1)} %get-tuple-element.46), channel_id=1, source_target_pairs={{0,6},{2,4},{4,2},{6,0},{8,14},{10,12},{12,10},{14,8},{16,22},{18,... | collective-permute-start | bytes 196616 | tf_op jit(solution)/shard_map/ppermute | solution.py:336
  15.7 0.0 collective-permute-done.7.other
  15.8 0.0 collective-permute-done.4.refs_0_.refs_1_.refs_5_
  15.8 1.0 %collective-permute-done.5.refs_1_.refs_2_.refs_6_ = bf16[256,128]{1,0:T(8,128)(2,1)S(1)} collective-permute-done((bf16[256,128]{1,0:T(8,128)(2,1)S(1)}, bf16[256,128]{1,0:T(8,128)(2,1)S(1)}, u32[]{:S(2)}, u32[]{:S(2)}) %collective-permute-start.5) | collective-permute-done | bytes 65568 | tf_op jit(solution)/shard_map/ppermute | solution.py:336
  16.8 2.8 %collective-permute-done.6.refs_2_.refs_3_.refs_7_ = bf16[256,128]{1,0:T(8,128)(2,1)S(1)} collective-permute-done((bf16[256,128]{1,0:T(8,128)(2,1)S(1)}, bf16[256,128]{1,0:T(8,128)(2,1)S(1)}, u32[]{:S(2)}, u32[]{:S(2)}) %collective-permute-start.6) | collective-permute-done | bytes 65568 | tf_op jit(solution)/shard_map/ppermute | solution.py:336
  19.6 0.4 project.3
  20.0 0.5 collective-permute-start.10
  20.4 0.4 collective-permute-start.11
  20.8 1.4 %collective-permute-start.12 = (bf16[256,128]{1,0:T(8,128)(2,1)S(1)}, bf16[256,128]{1,0:T(8,128)(2,1)S(1)}, u32[]{:S(2)}, u32[]{:S(2)}) collective-permute-start(bf16[256,128]{1,0:T(8,128)(2,1)S(1)} %get-tuple-element.55), channel_id=1, source_target_pairs={{0,6},{2,4},{4,2},{6,0},{8,14},{10,12},{12,10},{14,8},{16,22},{18,... | collective-permute-start | bytes 196616 | tf_op jit(solution)/shard_map/ppermute | solution.py:336
  22.2 0.1 halo.2
  22.2 3.2 %collective-permute-start.8 = (bf16[3,272,128]{2,1,0:T(8,128)(2,1)S(1)}, bf16[3,272,128]{2,1,0:T(8,128)(2,1)S(1)}, u32[]{:S(2)}, u32[]{:S(2)}) collective-permute-start(bf16[3,272,128]{2,1,0:T(8,128)(2,1)S(1)} %get-tuple-element.51), channel_id=1, source_target_pairs={{8,16},{10,18},{12,20},{14,22},{16,8},{18,10},{20,12},{22,14},{9,1... | collective-permute-start | bytes 626696 | tf_op jit(solution)/shard_map/ppermute | solution.py:341
  25.4 0.1 collective-permute-start.9
  25.5 0.0 collective-permute-done.10.refs_9_.refs_4_
  25.5 0.0 collective-permute-done.11.refs_10_.refs_5_
  25.5 0.1 collective-permute-done.12.refs_11_.refs_6_
  25.7 0.1 halo.3
  25.7 3.2 %collective-permute-start.15 = (bf16[3,256,128]{2,1,0:T(8,128)(2,1)S(1)}, bf16[3,256,128]{2,1,0:T(8,128)(2,1)S(1)}, u32[]{:S(2)}, u32[]{:S(2)}) collective-permute-start(bf16[3,256,128]{2,1,0:T(8,128)(2,1)S(1)} %get-tuple-element.62), channel_id=1, source_target_pairs={{8,16},{10,18},{12,20},{14,22},{16,8},{18,10},{20,12},{22,14},{9,1... | collective-permute-start | bytes 589832 | tf_op jit(solution)/shard_map/ppermute | solution.py:341
  29.0 0.1 collective-permute-start.16
  29.0 6.5 %plane.1 = (f32[2,4,512,128]{3,2,1,0:T(8,128)S(1)}, f32[2,4,512,256]{3,2,1,0:T(8,128)S(1)}, bf16[2,256,1024]{2,1,0:T(8,128)(2,1)S(1)}, bf16[2,1024,256]{2,1,0:T(8,128)(2,1)S(1)}, bf16[2,4,512,256]{3,2,1,0:T(8,128)(2,1)S(1)}) custom-call(bf16[528,128]{1,0:T(8,128)(2,1)S(1)} %get-tuple-element.47.refs_4_.refs_0_, ...), custom_call_target="tpu_custom_call" | custom-call | flops 4294967296 | bytes 2097152 | tf_op jit(solution)/shard_map/plane/pallas_call | solution.py:407
  35.5 0.0 collective-permute-done.8.edge_b
  35.6 0.0 collective-permute-done.9.edge_a
  35.6 2.7 %lend.1 = (bf16[3,288,128]{2,1,0:T(8,128)(2,1)S(1)}, bf16[3,288,128]{2,1,0:T(8,128)(2,1)S(1)}, bf16[256,1536]{1,0:T(8,128)(2,1)S(1)}) custom-call(bf16[3,272,128]{2,1,0:T(8,128)(2,1)S(1)} %collective-permute-done.8.edge_b, bf16[3,272,128]{2,1,0:T(8,128)(2,1)S(1)} %collective-permute-done.9.edge_a, bf16[2,256,1024]{2,1,0:T(8,128)(2,1)S(1)} %get-tuple-element.56.plane_turned, ...), custom_call_target="tpu_custom_call" | custom-call | flops 4831838208 | bytes 3145728 | tf_op jit(solution)/shard_map/lend/pallas_call | solution.py:418
  38.3 1.5 %collective-permute-start.13 = (bf16[3,288,128]{2,1,0:T(8,128)(2,1)S(1)}, bf16[3,288,128]{2,1,0:T(8,128)(2,1)S(1)}, u32[]{:S(2)}, u32[]{:S(2)}) collective-permute-start(bf16[3,288,128]{2,1,0:T(8,128)(2,1)S(1)} %get-tuple-element.58), channel_id=1, source_target_pairs={{0,8},{2,10},{4,12},{6,14},{8,0},{10,2},{12,4},{14,6},{16,24},{18,... | collective-permute-start | bytes 663560 | tf_op jit(solution)/shard_map/ppermute | solution.py:341
  39.8 2.2 %collective-permute-start.14 = (bf16[3,288,128]{2,1,0:T(8,128)(2,1)S(1)}, bf16[3,288,128]{2,1,0:T(8,128)(2,1)S(1)}, u32[]{:S(2)}, u32[]{:S(2)}) collective-permute-start(bf16[3,288,128]{2,1,0:T(8,128)(2,1)S(1)} %get-tuple-element.59), channel_id=1, source_target_pairs={{8,16},{10,18},{12,20},{14,22},{16,8},{18,10},{20,12},{22,14},{9,1... | collective-permute-start | bytes 663560 | tf_op jit(solution)/shard_map/ppermute | solution.py:341
  42.1 0.0 collective-permute-done.15.edge_b
  42.1 0.0 collective-permute-done.16.edge_a
  42.1 2.5 %edge.1 = (bf16[256,128]{1,0:T(8,128)(2,1)S(1)}, bf16[256,128]{1,0:T(8,128)(2,1)S(1)}, bf16[256,128]{1,0:T(8,128)(2,1)S(1)}, bf16[256,128]{1,0:T(8,128)(2,1)S(1)}) custom-call(bf16[3,256,128]{2,1,0:T(8,128)(2,1)S(1)} %collective-permute-done.15.edge_b, bf16[3,256,128]{2,1,0:T(8,128)(2,1)S(1)} %collective-permute-done.16.edge_a, ...), custom_call_target="tpu_custom_call" | custom-call | flops 4831838208 | bytes 3145728 | tf_op jit(solution)/shard_map/edge/pallas_call | solution.py:429
  44.6 1.5 %collective-permute-start.20 = (bf16[256,128]{1,0:T(8,128)(2,1)S(1)}, bf16[256,128]{1,0:T(8,128)(2,1)S(1)}, u32[]{:S(2)}, u32[]{:S(2)}) collective-permute-start(bf16[256,128]{1,0:T(8,128)(2,1)S(1)} %get-tuple-element.71), channel_id=1, source_target_pairs={{0,2},{2,0},{4,6},{6,4},{8,10},{10,8},{12,14},{14,12},{16,18},{18,... | collective-permute-start | bytes 196616 | tf_op jit(solution)/shard_map/ppermute | solution.py:336
  46.1 0.6 %collective-permute-start.21 = (bf16[256,128]{1,0:T(8,128)(2,1)S(1)}, bf16[256,128]{1,0:T(8,128)(2,1)S(1)}, u32[]{:S(2)}, u32[]{:S(2)}) collective-permute-start(bf16[256,128]{1,0:T(8,128)(2,1)S(1)} %get-tuple-element.72), channel_id=1, source_target_pairs={{0,4},{2,6},{4,0},{6,2},{8,12},{10,14},{12,8},{14,10},{16,20},{18,... | collective-permute-start | bytes 196616 | tf_op jit(solution)/shard_map/ppermute | solution.py:336
  46.7 1.1 %collective-permute-start.22 = (bf16[256,128]{1,0:T(8,128)(2,1)S(1)}, bf16[256,128]{1,0:T(8,128)(2,1)S(1)}, u32[]{:S(2)}, u32[]{:S(2)}) collective-permute-start(bf16[256,128]{1,0:T(8,128)(2,1)S(1)} %get-tuple-element.73), channel_id=1, source_target_pairs={{0,6},{2,4},{4,2},{6,0},{8,14},{10,12},{12,10},{14,8},{16,22},{18,... | collective-permute-start | bytes 196616 | tf_op jit(solution)/shard_map/ppermute | solution.py:336
  47.8 0.0 collective-permute-done.13.back_a
  47.8 0.0 collective-permute-done.14.back_b
  47.8 0.6 merge.1
  48.4 1.8 %collective-permute-start.17 = (bf16[256,128]{1,0:T(8,128)(2,1)S(1)}, bf16[256,128]{1,0:T(8,128)(2,1)S(1)}, u32[]{:S(2)}, u32[]{:S(2)}) collective-permute-start(bf16[256,128]{1,0:T(8,128)(2,1)S(1)} %get-tuple-element.68), channel_id=1, source_target_pairs={{0,2},{2,0},{4,6},{6,4},{8,10},{10,8},{12,14},{14,12},{16,18},{18,... | collective-permute-start | bytes 196616 | tf_op jit(solution)/shard_map/ppermute | solution.py:336
  50.2 0.5 collective-permute-start.18
  50.7 0.0 collective-permute-done.20.refs_1_
  50.7 1.2 %collective-permute-start.19 = (bf16[256,128]{1,0:T(8,128)(2,1)S(1)}, bf16[256,128]{1,0:T(8,128)(2,1)S(1)}, u32[]{:S(2)}, u32[]{:S(2)}) collective-permute-start(bf16[256,128]{1,0:T(8,128)(2,1)S(1)} %get-tuple-element.70), channel_id=1, source_target_pairs={{0,6},{2,4},{4,2},{6,0},{8,14},{10,12},{12,10},{14,8},{16,22},{18,... | collective-permute-start | bytes 196616 | tf_op jit(solution)/shard_map/ppermute | solution.py:336
  51.9 0.0 collective-permute-done.21.refs_2_
  51.9 0.0 collective-permute-done.22.refs_3_
  51.9 0.7 %join.3 = bf16[256,512]{1,0:T(8,128)(2,1)} custom-call(bf16[256,128]{1,0:T(8,128)(2,1)S(1)} %get-tuple-element.66.refs_0_, bf16[256,128]{1,0:T(8,128)(2,1)S(1)} %collective-permute-done.20.refs_1_, bf16[256,128]{1,0:T(8,128)(2,1)S(1)} %collective-permute-done.21.refs_2_, bf16[256,128]{1,0:T(8,128)(2,1)S(1)} %collective-permute-done.22.refs_3_), custom_call_target="tpu_custom_call" | custom-call | bytes 524288 | tf_op jit(solution)/shard_map/join/pallas_call | solution.py:449
  52.6 0.0 collective-permute-done.17.refs_1_
  52.6 1.2 %collective-permute-done.18.refs_2_ = bf16[256,128]{1,0:T(8,128)(2,1)S(1)} collective-permute-done((bf16[256,128]{1,0:T(8,128)(2,1)S(1)}, bf16[256,128]{1,0:T(8,128)(2,1)S(1)}, u32[]{:S(2)}, u32[]{:S(2)}) %collective-permute-start.18) | collective-permute-done | bytes 65568 | tf_op jit(solution)/shard_map/ppermute | solution.py:336
  53.8 1.6 %collective-permute-done.19.refs_3_ = bf16[256,128]{1,0:T(8,128)(2,1)S(1)} collective-permute-done((bf16[256,128]{1,0:T(8,128)(2,1)S(1)}, bf16[256,128]{1,0:T(8,128)(2,1)S(1)}, u32[]{:S(2)}, u32[]{:S(2)}) %collective-permute-start.19) | collective-permute-done | bytes 65568 | tf_op jit(solution)/shard_map/ppermute | solution.py:336
  55.4 0.7 %join.2 = bf16[256,512]{1,0:T(8,128)(2,1)} custom-call(bf16[256,128]{1,0:T(8,128)(2,1)S(1)} %get-tuple-element.67.refs_0_, bf16[256,128]{1,0:T(8,128)(2,1)S(1)} %collective-permute-done.17.refs_1_, bf16[256,128]{1,0:T(8,128)(2,1)S(1)} %collective-permute-done.18.refs_2_, bf16[256,128]{1,0:T(8,128)(2,1)S(1)} %collective-permute-done.19.refs_3_), custom_call_target="tpu_custom_call" | custom-call | bytes 524288 | tf_op jit(solution)/shard_map/join/pallas_call | solution.py:449
Async XLA Ops:
  0.6 12.5 %collective-permute-start.1 = (bf16[256,512]{1,0:T(8,128)(2,1)}, bf16[256,512]{1,0:T(8,128)(2,1)S(1)}, u32[]{:S(2)}, u32[]{:S(2)}) collective-permute-start(bf16[256,512]{1,0:T(8,128)(2,1)} %audio.3), channel_id=1, source_target_pairs={{0,1},{1,0},{2,3},{3,2},{4,5},{5,4},{6,7},{7,6},{8,9},{9,8},{10,11... | collective-permute-start | bytes 786440 | tf_op jit(solution)/shard_map/ppermute | solution.py:332
  1.9 13.8 %collective-permute-start.7 = (bf16[256,512]{1,0:T(8,128)(2,1)}, bf16[256,512]{1,0:T(8,128)(2,1)S(1)}, u32[]{:S(2)}, u32[]{:S(2)}) collective-permute-start(bf16[256,512]{1,0:T(8,128)(2,1)} %video.3), channel_id=1, source_target_pairs={{0,1},{1,0},{2,3},{3,2},{4,5},{5,4},{6,7},{7,6},{8,9},{9,8},{10,11... | collective-permute-start | bytes 786440 | tf_op jit(solution)/shard_map/ppermute | solution.py:332
  3.3 3.0 %collective-permute-start = (bf16[528,128]{1,0:T(8,128)(2,1)S(1)}, bf16[528,128]{1,0:T(8,128)(2,1)S(1)}, u32[]{:S(2)}, u32[]{:S(2)}) collective-permute-start(bf16[528,128]{1,0:T(8,128)(2,1)S(1)} %get-tuple-element.38), channel_id=1, source_target_pairs={{0,2},{2,0},{4,6},{6,4},{8,10},{10,8},{12,14},{14,12},{16,18},{18,... | collective-permute-start | bytes 405512 | tf_op jit(solution)/shard_map/ppermute | solution.py:336
  4.6 5.2 %collective-permute-start.2 = (bf16[528,128]{1,0:T(8,128)(2,1)S(1)}, bf16[528,128]{1,0:T(8,128)(2,1)S(1)}, u32[]{:S(2)}, u32[]{:S(2)}) collective-permute-start(bf16[528,128]{1,0:T(8,128)(2,1)S(1)} %get-tuple-element.41), channel_id=1, source_target_pairs={{0,4},{2,6},{4,0},{6,2},{8,12},{10,14},{12,8},{14,10},{16,20},{18,... | collective-permute-start | bytes 405512 | tf_op jit(solution)/shard_map/ppermute | solution.py:336
  5.9 7.3 %collective-permute-start.3 = (bf16[528,128]{1,0:T(8,128)(2,1)S(1)}, bf16[528,128]{1,0:T(8,128)(2,1)S(1)}, u32[]{:S(2)}, u32[]{:S(2)}) collective-permute-start(bf16[528,128]{1,0:T(8,128)(2,1)S(1)} %get-tuple-element.42), channel_id=1, source_target_pairs={{0,6},{2,4},{4,2},{6,0},{8,14},{10,12},{12,10},{14,8},{16,22},{18,... | collective-permute-start | bytes 405512 | tf_op jit(solution)/shard_map/ppermute | solution.py:336
  13.5 2.2 %collective-permute-start.4 = (bf16[256,128]{1,0:T(8,128)(2,1)S(1)}, bf16[256,128]{1,0:T(8,128)(2,1)S(1)}, u32[]{:S(2)}, u32[]{:S(2)}) collective-permute-start(bf16[256,128]{1,0:T(8,128)(2,1)S(1)} %get-tuple-element.44), channel_id=1, source_target_pairs={{0,2},{2,0},{4,6},{6,4},{8,10},{10,8},{12,14},{14,12},{16,18},{18,... | collective-permute-start | bytes 196616 | tf_op jit(solution)/shard_map/ppermute | solution.py:336
  13.6 3.2 %collective-permute-start.5 = (bf16[256,128]{1,0:T(8,128)(2,1)S(1)}, bf16[256,128]{1,0:T(8,128)(2,1)S(1)}, u32[]{:S(2)}, u32[]{:S(2)}) collective-permute-start(bf16[256,128]{1,0:T(8,128)(2,1)S(1)} %get-tuple-element.45), channel_id=1, source_target_pairs={{0,4},{2,6},{4,0},{6,2},{8,12},{10,14},{12,8},{14,10},{16,20},{18,... | collective-permute-start | bytes 196616 | tf_op jit(solution)/shard_map/ppermute | solution.py:336
  14.9 4.7 %collective-permute-start.6 = (bf16[256,128]{1,0:T(8,128)(2,1)S(1)}, bf16[256,128]{1,0:T(8,128)(2,1)S(1)}, u32[]{:S(2)}, u32[]{:S(2)}) collective-permute-start(bf16[256,128]{1,0:T(8,128)(2,1)S(1)} %get-tuple-element.46), channel_id=1, source_target_pairs={{0,6},{2,4},{4,2},{6,0},{8,14},{10,12},{12,10},{14,8},{16,22},{18,... | collective-permute-start | bytes 196616 | tf_op jit(solution)/shard_map/ppermute | solution.py:336
  20.0 5.6 %collective-permute-start.10 = (bf16[256,128]{1,0:T(8,128)(2,1)S(1)}, bf16[256,128]{1,0:T(8,128)(2,1)S(1)}, u32[]{:S(2)}, u32[]{:S(2)}) collective-permute-start(bf16[256,128]{1,0:T(8,128)(2,1)S(1)} %get-tuple-element.53), channel_id=1, source_target_pairs={{0,2},{2,0},{4,6},{6,4},{8,10},{10,8},{12,14},{14,12},{16,18},{18,... | collective-permute-start | bytes 196616 | tf_op jit(solution)/shard_map/ppermute | solution.py:336
  20.4 5.1 %collective-permute-start.11 = (bf16[256,128]{1,0:T(8,128)(2,1)S(1)}, bf16[256,128]{1,0:T(8,128)(2,1)S(1)}, u32[]{:S(2)}, u32[]{:S(2)}) collective-permute-start(bf16[256,128]{1,0:T(8,128)(2,1)S(1)} %get-tuple-element.54), channel_id=1, source_target_pairs={{0,4},{2,6},{4,0},{6,2},{8,12},{10,14},{12,8},{14,10},{16,20},{18,... | collective-permute-start | bytes 196616 | tf_op jit(solution)/shard_map/ppermute | solution.py:336
  20.8 4.9 %collective-permute-start.12 = (bf16[256,128]{1,0:T(8,128)(2,1)S(1)}, bf16[256,128]{1,0:T(8,128)(2,1)S(1)}, u32[]{:S(2)}, u32[]{:S(2)}) collective-permute-start(bf16[256,128]{1,0:T(8,128)(2,1)S(1)} %get-tuple-element.55), channel_id=1, source_target_pairs={{0,6},{2,4},{4,2},{6,0},{8,14},{10,12},{12,10},{14,8},{16,22},{18,... | collective-permute-start | bytes 196616 | tf_op jit(solution)/shard_map/ppermute | solution.py:336
  22.2 13.3 %collective-permute-start.8 = (bf16[3,272,128]{2,1,0:T(8,128)(2,1)S(1)}, bf16[3,272,128]{2,1,0:T(8,128)(2,1)S(1)}, u32[]{:S(2)}, u32[]{:S(2)}) collective-permute-start(bf16[3,272,128]{2,1,0:T(8,128)(2,1)S(1)} %get-tuple-element.51), channel_id=1, source_target_pairs={{8,16},{10,18},{12,20},{14,22},{16,8},{18,10},{20,12},{22,14},{9,1... | collective-permute-start | bytes 626696 | tf_op jit(solution)/shard_map/ppermute | solution.py:341
  25.4 10.1 %collective-permute-start.9 = (bf16[3,272,128]{2,1,0:T(8,128)(2,1)S(1)}, bf16[3,272,128]{2,1,0:T(8,128)(2,1)S(1)}, u32[]{:S(2)}, u32[]{:S(2)}) collective-permute-start(bf16[3,272,128]{2,1,0:T(8,128)(2,1)S(1)} %get-tuple-element.52), channel_id=1, source_target_pairs={{0,8},{2,10},{4,12},{6,14},{8,0},{10,2},{12,4},{14,6},{16,24},{18,... | collective-permute-start | bytes 626696 | tf_op jit(solution)/shard_map/ppermute | solution.py:341
  25.7 16.3 %collective-permute-start.15 = (bf16[3,256,128]{2,1,0:T(8,128)(2,1)S(1)}, bf16[3,256,128]{2,1,0:T(8,128)(2,1)S(1)}, u32[]{:S(2)}, u32[]{:S(2)}) collective-permute-start(bf16[3,256,128]{2,1,0:T(8,128)(2,1)S(1)} %get-tuple-element.62), channel_id=1, source_target_pairs={{8,16},{10,18},{12,20},{14,22},{16,8},{18,10},{20,12},{22,14},{9,1... | collective-permute-start | bytes 589832 | tf_op jit(solution)/shard_map/ppermute | solution.py:341
  29.0 13.1 %collective-permute-start.16 = (bf16[3,256,128]{2,1,0:T(8,128)(2,1)S(1)}, bf16[3,256,128]{2,1,0:T(8,128)(2,1)S(1)}, u32[]{:S(2)}, u32[]{:S(2)}) collective-permute-start(bf16[3,256,128]{2,1,0:T(8,128)(2,1)S(1)} %get-tuple-element.63), channel_id=1, source_target_pairs={{0,8},{2,10},{4,12},{6,14},{8,0},{10,2},{12,4},{14,6},{16,24},{18,... | collective-permute-start | bytes 589832 | tf_op jit(solution)/shard_map/ppermute | solution.py:341
  38.3 9.5 %collective-permute-start.13 = (bf16[3,288,128]{2,1,0:T(8,128)(2,1)S(1)}, bf16[3,288,128]{2,1,0:T(8,128)(2,1)S(1)}, u32[]{:S(2)}, u32[]{:S(2)}) collective-permute-start(bf16[3,288,128]{2,1,0:T(8,128)(2,1)S(1)} %get-tuple-element.58), channel_id=1, source_target_pairs={{0,8},{2,10},{4,12},{6,14},{8,0},{10,2},{12,4},{14,6},{16,24},{18,... | collective-permute-start | bytes 663560 | tf_op jit(solution)/shard_map/ppermute | solution.py:341
  39.8 8.0 %collective-permute-start.14 = (bf16[3,288,128]{2,1,0:T(8,128)(2,1)S(1)}, bf16[3,288,128]{2,1,0:T(8,128)(2,1)S(1)}, u32[]{:S(2)}, u32[]{:S(2)}) collective-permute-start(bf16[3,288,128]{2,1,0:T(8,128)(2,1)S(1)} %get-tuple-element.59), channel_id=1, source_target_pairs={{8,16},{10,18},{12,20},{14,22},{16,8},{18,10},{20,12},{22,14},{9,1... | collective-permute-start | bytes 663560 | tf_op jit(solution)/shard_map/ppermute | solution.py:341
  44.6 6.1 %collective-permute-start.20 = (bf16[256,128]{1,0:T(8,128)(2,1)S(1)}, bf16[256,128]{1,0:T(8,128)(2,1)S(1)}, u32[]{:S(2)}, u32[]{:S(2)}) collective-permute-start(bf16[256,128]{1,0:T(8,128)(2,1)S(1)} %get-tuple-element.71), channel_id=1, source_target_pairs={{0,2},{2,0},{4,6},{6,4},{8,10},{10,8},{12,14},{14,12},{16,18},{18,... | collective-permute-start | bytes 196616 | tf_op jit(solution)/shard_map/ppermute | solution.py:336
  46.1 5.8 %collective-permute-start.21 = (bf16[256,128]{1,0:T(8,128)(2,1)S(1)}, bf16[256,128]{1,0:T(8,128)(2,1)S(1)}, u32[]{:S(2)}, u32[]{:S(2)}) collective-permute-start(bf16[256,128]{1,0:T(8,128)(2,1)S(1)} %get-tuple-element.72), channel_id=1, source_target_pairs={{0,4},{2,6},{4,0},{6,2},{8,12},{10,14},{12,8},{14,10},{16,20},{18,... | collective-permute-start | bytes 196616 | tf_op jit(solution)/shard_map/ppermute | solution.py:336
  46.7 5.2 %collective-permute-start.22 = (bf16[256,128]{1,0:T(8,128)(2,1)S(1)}, bf16[256,128]{1,0:T(8,128)(2,1)S(1)}, u32[]{:S(2)}, u32[]{:S(2)}) collective-permute-start(bf16[256,128]{1,0:T(8,128)(2,1)S(1)} %get-tuple-element.73), channel_id=1, source_target_pairs={{0,6},{2,4},{4,2},{6,0},{8,14},{10,12},{12,10},{14,8},{16,22},{18,... | collective-permute-start | bytes 196616 | tf_op jit(solution)/shard_map/ppermute | solution.py:336
  48.4 4.2 %collective-permute-start.17 = (bf16[256,128]{1,0:T(8,128)(2,1)S(1)}, bf16[256,128]{1,0:T(8,128)(2,1)S(1)}, u32[]{:S(2)}, u32[]{:S(2)}) collective-permute-start(bf16[256,128]{1,0:T(8,128)(2,1)S(1)} %get-tuple-element.68), channel_id=1, source_target_pairs={{0,2},{2,0},{4,6},{6,4},{8,10},{10,8},{12,14},{14,12},{16,18},{18,... | collective-permute-start | bytes 196616 | tf_op jit(solution)/shard_map/ppermute | solution.py:336
  50.2 3.7 %collective-permute-start.18 = (bf16[256,128]{1,0:T(8,128)(2,1)S(1)}, bf16[256,128]{1,0:T(8,128)(2,1)S(1)}, u32[]{:S(2)}, u32[]{:S(2)}) collective-permute-start(bf16[256,128]{1,0:T(8,128)(2,1)S(1)} %get-tuple-element.69), channel_id=1, source_target_pairs={{0,4},{2,6},{4,0},{6,2},{8,12},{10,14},{12,8},{14,10},{16,20},{18,... | collective-permute-start | bytes 196616 | tf_op jit(solution)/shard_map/ppermute | solution.py:336
  50.7 4.7 %collective-permute-start.19 = (bf16[256,128]{1,0:T(8,128)(2,1)S(1)}, bf16[256,128]{1,0:T(8,128)(2,1)S(1)}, u32[]{:S(2)}, u32[]{:S(2)}) collective-permute-start(bf16[256,128]{1,0:T(8,128)(2,1)S(1)} %get-tuple-element.70), channel_id=1, source_target_pairs={{0,6},{2,4},{4,2},{6,0},{8,14},{10,12},{12,10},{14,8},{16,22},{18,... | collective-permute-start | bytes 196616 | tf_op jit(solution)/shard_map/ppermute | solution.py:336

commit v12 on v11

--- a/solution.py
+++ b/solution.py
@@ -54,7 +54,7 @@
     return copies, fetch
 
 
-def split_kernel(audio, video, ids, *refs):
+def split_kernel(audio, ids, *refs):
     packs, (ids_in, ids_wide, sems) = refs[:GROUP], refs[GROUP:]
     rows, width = audio.shape[0], packs[0].shape[1]
     mine = place()
@@ -62,23 +62,23 @@
     fetch(ids, ids_in)
     for k in range(GROUP):
         at = pl.ds(pl.multiple_of((mine ^ k) * width, width), width)
-        for i, stream in enumerate((audio, video)):
-            fetch(stream.at[:, at], packs[k].at[i * rows : (i + 1) * rows])
+        fetch(audio.at[:, at], packs[k].at[:rows])
     copies[0].wait()
     ids_wide[...] = jnp.zeros_like(ids_wide)
     ids_wide[: ids_in.shape[0]] = (ids_in[...] + 1).astype(jnp.float32)
     for k in range(GROUP):
-        packs[k][2 * rows :] = ids_wide[...].astype(packs[k].dtype)
+        packs[k][rows:] = ids_wide[...].astype(packs[k].dtype)
     for copy in copies[1:]:
         copy.wait()
 
 
 def prepare_kernel(audio, video, query, key, *refs):
-    sums, seconds, streams, firsts, sems = refs[-9:-7], refs[-7:-5], refs[-5:-3], refs[-3:-1], refs[-1]
+    sums, seconds, sent, own, firsts, sems = refs[-9:-7], refs[-7:-5], refs[-5], refs[-4], refs[-3:-1], refs[-1]
     half = audio.shape[1]
     side = lax.axis_index("head")
     ours = pl.ds(pl.multiple_of(side * half, half), half)
     theirs = pl.ds(pl.multiple_of((1 - side) * half, half), half)
+    streams = (own, sent)
     copies, fetch = fetcher(sems)
     for i, (stream, weight) in enumerate(((audio, query), (video, key))):
         fetch(stream, streams[i])
@@ -93,14 +93,16 @@
         copy.wait()
 
 
-def project_kernel(scale, part, other, weight, *refs):
+def project_kernel(scale, stream, part, other, weight, *refs):
     pieces, full = refs[-GROUP - 1 : -1], refs[-1]
-    width = pieces[0].shape[1]
-    mine = place()
-    total = part[...] + product(other[...], weight[...])
-    full[...] = total.astype(jnp.bfloat16) * jnp.bfloat16(scale)
-    for k in range(GROUP):
-        pieces[k][...] = full[:, pl.ds(pl.multiple_of((mine ^ k) * width, width), width)]
+    rows, width = other.shape[0], pieces[0].shape[1]
+    mine = place()
+    full[...] = (part[...] + product(other[...], weight[...])).astype(jnp.bfloat16) * jnp.bfloat16(scale)
+    for k in range(GROUP):
+        at = pl.ds(pl.multiple_of((mine ^ k) * width, width), width)
+        if stream:
+            pieces[k][:rows] = refs[0][:, at]
+        pieces[k][stream * rows :] = full[:, at]
 
 
 def halo_kernel(ids_at, *refs):
@@ -172,9 +174,9 @@
 
 
 def plane_kernel(*refs):
-    packs, queries, keys = refs[:GROUP], refs[GROUP : 2 * GROUP], refs[2 * GROUP : 3 * GROUP]
+    audio, queries, video = refs[:GROUP], refs[GROUP : 2 * GROUP], refs[2 * GROUP : 3 * GROUP]
     peaks, sums, turned, beside, asks = refs[3 * GROUP :]
-    rows, width = keys[0].shape
+    rows, width = queries[0].shape
     mine = place()
     beside[:, :, width:] = jnp.ones((2, GROUP * rows, width), beside.dtype)
     for k in range(GROUP):
@@ -183,13 +185,15 @@
         def spot(at, size):
             return pl.ds(pl.multiple_of(b * rows + at, size), size)
 
-        marks = marks_turned(packs[k][2 * rows :])
-        for i, (ask, key) in enumerate(((queries, keys), (keys, queries))):
-            asks[i, b] = stacked_ask(ask[k][...], marks)
-            beside[i, spot(0, rows), :width] = packs[k][(1 - i) * rows : (2 - i) * rows]
+        marks = marks_turned(audio[k][rows:])
+        projections = (queries[k][...], video[k][rows:])
+        for i in range(2):
+            key = projections[1 - i]
+            asks[i, b] = stacked_ask(projections[i], marks)
+            beside[i, spot(0, rows), :width] = (audio if i else video)[k][:rows]
             for part, x in enumerate(marks):
                 at = spot(part * width, width)
-                turned[i, :width, at] = jnp.transpose(key[k][part * width : (part + 1) * width])
+                turned[i, :width, at] = jnp.transpose(key[part * width : (part + 1) * width])
                 turned[i, width:, at] = x
 
     units = [(i, b) for b in range(GROUP) for i in range(2)]
@@ -353,18 +357,18 @@
     other_video = swapped(video_frames)
     packs = call(
         split_kernel,
-        [shape((2 * rows + ID_ROWS, width), bf16)] * GROUP,
+        [shape((rows + ID_ROWS, width), bf16)] * GROUP,
         [pltpu.VMEM((rows // width, width), jnp.int32), pltpu.VMEM((ID_ROWS, width), f32)]
-        + [pltpu.SemaphoreType.DMA((1 + 2 * GROUP,))],
-        ins=[HBM] * 3,
-        moved=8 * rows * half,
+        + [pltpu.SemaphoreType.DMA((1 + GROUP,))],
+        ins=[HBM] * 2,
+        moved=4 * rows * half,
         name="split",
-    )(audio_in, video_in, ids_in)
+    )(audio_in, ids_in)
     packs = traded(packs)
-    query_part, key_part, query_rest, key_rest = call(
+    query_part, key_part, query_rest, key_rest, video_copy = call(
         prepare_kernel,
-        [part, part, square, square],
-        [pltpu.VMEM((rows, half), bf16)] * 2
+        [part, part, square, square, shape((rows, half), bf16)],
+        [pltpu.VMEM((rows, half), bf16)]
         + [pltpu.VMEM((half, half), bf16)] * 2
         + [pltpu.SemaphoreType.DMA((6,))],
         ins=[HBM] * 4 + [ANY],
@@ -373,25 +377,21 @@
         name="prepare",
     )(audio_in, video_in, query_in, key_in, packs[1])
 
-    def project(scale, *operands):
+    def project(scale, *operands, stream=(), after=()):
         return call(
-            functools.partial(project_kernel, scale),
-            [piece] * GROUP,
+            functools.partial(project_kernel, scale, len(stream)),
+            [shape(((1 + len(stream)) * rows, width), bf16)] * GROUP,
             [pltpu.VMEM((rows, half), bf16)],
-            ins=[VMEM] * 3 + [ANY] * (len(operands) - 3),
+            ins=[VMEM] * (3 + len(stream)) + [ANY] * len(after),
             flops=2 * rows * half * half,
             moved=2 * half * half + 6 * rows * half * 2,
             name="project",
-        )(*operands)
-
-    queries = project(HEAD**-0.5, query_part, other_audio, query_rest, *packs[1:])
-    queries = traded(queries)
-    keys = project(1.0, key_part, other_video, key_rest, *queries[1:])
+        )(*operands, *stream, *after)
 
     def halo(pieces, id_packs, *after):
         edge = shape((RADIUS, rows + (ID_ROWS if id_packs else 0), width), bf16)
         sent = call(
-            functools.partial(halo_kernel, 2 * rows if id_packs else 0),
+            functools.partial(halo_kernel, rows if id_packs else 0),
             [edge, edge],
             ins=[VMEM] * (GROUP + len(id_packs)) + [ANY] * len(after),
             moved=10 * rows * width * 2,
@@ -399,9 +399,12 @@
         )(*pieces, *id_packs, *after)
         return [crossed(sent[i], i) for i in range(2)]
 
-    query_edges = halo(queries, packs, keys[0])
-    keys = traded(keys)
-    audio_edges = halo(packs, [], *keys[1:])
+    audio_edges = halo(packs, [])
+    queries = project(HEAD**-0.5, query_part, other_audio, query_rest, after=packs[1:])
+    queries = traded(queries)
+    video = project(1.0, key_part, other_video, key_rest, stream=[video_copy], after=queries[1:])
+    query_edges = halo(queries, packs, *audio_edges[::-1])
+    video = traded(video)
 
     inside, around = GROUP * rows, 2 * RADIUS * rows
     peaks, sums, plane_turned, plane_beside, asks = call(
@@ -413,7 +416,7 @@
         moved=8 * inside * width * 2,
         exps=4 * GROUP * rows * inside,
         name="plane",
-    )(*packs, *queries, *keys)
+    )(*packs, *queries, *video)
     back = shape((RADIUS, rows + rows // width * STAT_ROWS, width), bf16)
     lent_a, lent_b, edge_turned = call(
         lend_kernel,

time: 56.5 us -> 52.8 us (0.935)
  waiting for transfers between devices: 11.8 us -> 9.19 us
  starting transfers between devices: 26 us -> 25.3 us
    ppermute x15, waiting for transfers between devices: 11.8 us -> 5.98 us  [traded(): lax.ppermute(pieces[k], 'tm', pairs(k))]
    ppermute x6, waiting for transfers between devices: 0.02 us -> 3.2 us  [crossed(): lax.ppermute(sent, 'tm', [(p * GROUP + i, q * GROUP + i) for p, q in pair...]
    ppermute x15, starting transfers between devices: 14.1 us -> 13.6 us  [traded(): lax.ppermute(pieces[k], 'tm', pairs(k))]
  transfers between devices with their start and end apart: 23 -> 23, of which waited for: 7 -> 9; matrix products, arithmetic and copies ran while one was open for 0% -> 0% of each run, Pallas kernels for 29% -> 26%
where the time goes in v12:
time: 52.8 us; the launch traced here: 52.6 us
  starting transfers between devices  25.3 us (48%)
  Pallas kernels  17.1 us (32%)
  waiting for transfers between devices  9.19 us (17%)
  between operations  0.99 us (2%)
    ppermute x15, starting transfers between devices, traded(): lax.ppermute(pieces[k], 'tm', pairs(k))  13.6 us
    ppermute x6, starting transfers between devices, crossed(): lax.ppermute(sent, 'tm', [(p * GROUP + i, q * GROUP + i) for p, q in pair...  10.2 us
    pallas_call x1, Pallas kernels, local(): call(plane_kernel, [shape((2, GROUP, heads * rows, n * width), f32) for n...  6.29 us
    ppermute x15, waiting for transfers between devices, traded(): lax.ppermute(pieces[k], 'tm', pairs(k))  5.98 us
    ppermute x6, waiting for transfers between devices, crossed(): lax.ppermute(sent, 'tm', [(p * GROUP + i, q * GROUP + i) for p, q in pair...  3.2 us
    pallas_call x1, Pallas kernels, local(): call(lend_kernel, [back, back, shape((2 * width, around), bf16)], [pltpu....  2.68 us
    pallas_call x1, Pallas kernels, local(): call(edge_kernel, [piece] * GROUP, [pltpu.VMEM((around, 2 * width), bf16)...  2.49 us
    pallas_call x1, Pallas kernels, local(): call(prepare_kernel, [part, part, square, square, shape((rows, half), bf1...  1.78 us
  transfers between devices with their start and end apart: 23, of which 9 were waited for; matrix products, arithmetic and copies ran while one was open for 0% of the time, Pallas kernels for 26%

profile of v12, /device:TPU:9, one launch (start us, length us, event | category | flops | bytes accessed | tf_op | source)
XLA Modules:
  0.0 52.6 jit_solution(9979138562894133986)
XLA Ops:
  0.6 1.3 %collective-permute-start.1 = (bf16[256,512]{1,0:T(8,128)(2,1)}, bf16[256,512]{1,0:T(8,128)(2,1)S(1)}, u32[]{:S(2)}, u32[]{:S(2)}) collective-permute-start(bf16[256,512]{1,0:T(8,128)(2,1)} %audio.3), channel_id=1, source_target_pairs={{0,1},{1,0},{2,3},{3,2},{4,5},{5,4},{6,7},{7,6},{8,9},{9,8},{10,11... | collective-permute-start | bytes 786440 | tf_op jit(solution)/shard_map/ppermute | solution.py:336
  1.9 0.2 collective-permute-start.11
  2.2 1.0 %split.1 = (bf16[272,128]{1,0:T(8,128)(2,1)S(1)}, bf16[272,128]{1,0:T(8,128)(2,1)S(1)}, bf16[272,128]{1,0:T(8,128)(2,1)S(1)}, bf16[272,128]{1,0:T(8,128)(2,1)S(1)}) custom-call(bf16[256,512]{1,0:T(8,128)(2,1)} %audio.3, s32[2,128]{1,0:T(2,128)} %bitcast.1), custom_call_target="tpu_custom_call" | custom-call | bytes 524288 | tf_op jit(solution)/shard_map/split/pallas_call | solution.py:358
  3.2 1.3 %collective-permute-start = (bf16[272,128]{1,0:T(8,128)(2,1)S(1)}, bf16[272,128]{1,0:T(8,128)(2,1)S(1)}, u32[]{:S(2)}, u32[]{:S(2)}) collective-permute-start(bf16[272,128]{1,0:T(8,128)(2,1)S(1)} %get-tuple-element.39), channel_id=1, source_target_pairs={{0,2},{2,0},{4,6},{6,4},{8,10},{10,8},{12,14},{14,12},{16,18},{18,... | collective-permute-start | bytes 208904 | tf_op jit(solution)/shard_map/ppermute | solution.py:340
  4.5 1.2 %collective-permute-start.2 = (bf16[272,128]{1,0:T(8,128)(2,1)S(1)}, bf16[272,128]{1,0:T(8,128)(2,1)S(1)}, u32[]{:S(2)}, u32[]{:S(2)}) collective-permute-start(bf16[272,128]{1,0:T(8,128)(2,1)S(1)} %get-tuple-element.42), channel_id=1, source_target_pairs={{0,4},{2,6},{4,0},{6,2},{8,12},{10,14},{12,8},{14,10},{16,20},{18,... | collective-permute-start | bytes 208904 | tf_op jit(solution)/shard_map/ppermute | solution.py:340
  5.7 0.5 collective-permute-start.3
  6.2 0.0 collective-permute-done.refs_0_.refs_1_.refs_5_
  6.2 1.8 %prepare.1 = (f32[256,512]{1,0:T(8,128)S(1)}, f32[256,512]{1,0:T(8,128)S(1)}, bf16[512,512]{1,0:T(8,128)(2,1)S(1)}, bf16[512,512]{1,0:T(8,128)(2,1)S(1)}, bf16[256,512]{1,0:T(8,128)(2,1)S(1)}) custom-call(bf16[256,512]{1,0:T(8,128)(2,1)} %audio.3, bf16[256,512]{1,0:T(8,128)(2,1)} %video.1, bf16[1024,512]{1,0:T(8,128)(2,1)} %query.1, bf16[1024,512]{1,0:T(8,128)(2,1)} %key.1, ...), custom_call_target="tpu_custom_call" | custom-call | flops 268435456 | bytes 4194304 | tf_op jit(solution)/shard_map/prepare/pallas_call | solution.py:368
  8.0 0.3 collective-permute-done.2.refs_1_.refs_2_.refs_6_
  8.2 1.9 %collective-permute-done.3.refs_2_.refs_3_.refs_7_ = bf16[272,128]{1,0:T(8,128)(2,1)S(1)} collective-permute-done((bf16[272,128]{1,0:T(8,128)(2,1)S(1)}, bf16[272,128]{1,0:T(8,128)(2,1)S(1)}, u32[]{:S(2)}, u32[]{:S(2)}) %collective-permute-start.3) | collective-permute-done | bytes 69664 | tf_op jit(solution)/shard_map/ppermute | solution.py:340
  10.2 0.0 collective-permute-done.1.other
  10.2 0.4 project.2
  10.6 0.7 %collective-permute-start.4 = (bf16[256,128]{1,0:T(8,128)(2,1)S(1)}, bf16[256,128]{1,0:T(8,128)(2,1)S(1)}, u32[]{:S(2)}, u32[]{:S(2)}) collective-permute-start(bf16[256,128]{1,0:T(8,128)(2,1)S(1)} %get-tuple-element.45), channel_id=1, source_target_pairs={{0,2},{2,0},{4,6},{6,4},{8,10},{10,8},{12,14},{14,12},{16,18},{18,... | collective-permute-start | bytes 196616 | tf_op jit(solution)/shard_map/ppermute | solution.py:340
  11.2 1.2 %collective-permute-start.5 = (bf16[256,128]{1,0:T(8,128)(2,1)S(1)}, bf16[256,128]{1,0:T(8,128)(2,1)S(1)}, u32[]{:S(2)}, u32[]{:S(2)}) collective-permute-start(bf16[256,128]{1,0:T(8,128)(2,1)S(1)} %get-tuple-element.46), channel_id=1, source_target_pairs={{0,4},{2,6},{4,0},{6,2},{8,12},{10,14},{12,8},{14,10},{16,20},{18,... | collective-permute-start | bytes 196616 | tf_op jit(solution)/shard_map/ppermute | solution.py:340
  12.5 0.5 collective-permute-start.6
  12.9 0.1 halo.2
  13.0 3.2 %collective-permute-start.7 = (bf16[3,256,128]{2,1,0:T(8,128)(2,1)S(1)}, bf16[3,256,128]{2,1,0:T(8,128)(2,1)S(1)}, u32[]{:S(2)}, u32[]{:S(2)}) collective-permute-start(bf16[3,256,128]{2,1,0:T(8,128)(2,1)S(1)} %get-tuple-element.49), channel_id=1, source_target_pairs={{8,16},{10,18},{12,20},{14,22},{16,8},{18,10},{20,12},{22,14},{9,1... | collective-permute-start | bytes 589832 | tf_op jit(solution)/shard_map/ppermute | solution.py:345
  16.2 0.0 collective-permute-done.11.other
  16.2 0.1 collective-permute-start.8
  16.3 0.0 collective-permute-done.4.refs_1_.refs_5_
  16.3 0.0 collective-permute-done.5.refs_2_.refs_6_
  16.3 0.2 collective-permute-done.6.refs_3_.refs_7_
  16.5 0.4 project.3
  16.9 0.4 collective-permute-start.12
  17.3 1.1 %collective-permute-start.13 = (bf16[512,128]{1,0:T(8,128)(2,1)S(1)}, bf16[512,128]{1,0:T(8,128)(2,1)S(1)}, u32[]{:S(2)}, u32[]{:S(2)}) collective-permute-start(bf16[512,128]{1,0:T(8,128)(2,1)S(1)} %get-tuple-element.58), channel_id=1, source_target_pairs={{0,4},{2,6},{4,0},{6,2},{8,12},{10,14},{12,8},{14,10},{16,20},{18,... | collective-permute-start | bytes 393224 | tf_op jit(solution)/shard_map/ppermute | solution.py:340
  18.5 0.7 %collective-permute-start.14 = (bf16[512,128]{1,0:T(8,128)(2,1)S(1)}, bf16[512,128]{1,0:T(8,128)(2,1)S(1)}, u32[]{:S(2)}, u32[]{:S(2)}) collective-permute-start(bf16[512,128]{1,0:T(8,128)(2,1)S(1)} %get-tuple-element.59), channel_id=1, source_target_pairs={{0,6},{2,4},{4,2},{6,0},{8,14},{10,12},{12,10},{14,8},{16,22},{18,... | collective-permute-start | bytes 393224 | tf_op jit(solution)/shard_map/ppermute | solution.py:340
  19.1 2.1 %collective-permute-done.7.refs_8_.edge_b = bf16[3,256,128]{2,1,0:T(8,128)(2,1)S(1)} collective-permute-done((bf16[3,256,128]{2,1,0:T(8,128)(2,1)S(1)}, bf16[3,256,128]{2,1,0:T(8,128)(2,1)S(1)}, u32[]{:S(2)}, u32[]{:S(2)}) %collective-permute-start.7) | collective-permute-done | bytes 196640 | tf_op jit(solution)/shard_map/ppermute | solution.py:345
  21.2 1.1 %collective-permute-done.8.refs_9_.edge_a = bf16[3,256,128]{2,1,0:T(8,128)(2,1)S(1)} collective-permute-done((bf16[3,256,128]{2,1,0:T(8,128)(2,1)S(1)}, bf16[3,256,128]{2,1,0:T(8,128)(2,1)S(1)}, u32[]{:S(2)}, u32[]{:S(2)}) %collective-permute-start.8) | collective-permute-done | bytes 196640 | tf_op jit(solution)/shard_map/ppermute | solution.py:345
  22.3 0.1 halo.3
  22.4 2.1 %collective-permute-start.9 = (bf16[3,272,128]{2,1,0:T(8,128)(2,1)S(1)}, bf16[3,272,128]{2,1,0:T(8,128)(2,1)S(1)}, u32[]{:S(2)}, u32[]{:S(2)}) collective-permute-start(bf16[3,272,128]{2,1,0:T(8,128)(2,1)S(1)} %get-tuple-element.51), channel_id=1, source_target_pairs={{8,16},{10,18},{12,20},{14,22},{16,8},{18,10},{20,12},{22,14},{9,1... | collective-permute-start | bytes 626696 | tf_op jit(solution)/shard_map/ppermute | solution.py:345
  24.5 0.1 collective-permute-start.10
  24.6 0.0 collective-permute-done.12.refs_9_
  24.6 0.0 collective-permute-done.13.refs_10_
  24.6 0.7 %collective-permute-done.14.refs_11_ = bf16[512,128]{1,0:T(8,128)(2,1)S(1)} collective-permute-done((bf16[512,128]{1,0:T(8,128)(2,1)S(1)}, bf16[512,128]{1,0:T(8,128)(2,1)S(1)}, u32[]{:S(2)}, u32[]{:S(2)}) %collective-permute-start.14) | collective-permute-done | bytes 131104 | tf_op jit(solution)/shard_map/ppermute | solution.py:340
  25.4 6.3 %plane.1 = (f32[2,4,512,128]{3,2,1,0:T(8,128)S(1)}, f32[2,4,512,256]{3,2,1,0:T(8,128)S(1)}, bf16[2,256,1024]{2,1,0:T(8,128)(2,1)S(1)}, bf16[2,1024,256]{2,1,0:T(8,128)(2,1)S(1)}, bf16[2,4,512,256]{3,2,1,0:T(8,128)(2,1)S(1)}) custom-call(bf16[272,128]{1,0:T(8,128)(2,1)S(1)} %get-tuple-element.48.refs_0_.refs_4_, ...), custom_call_target="tpu_custom_call" | custom-call | flops 4294967296 | bytes 2097152 | tf_op jit(solution)/shard_map/plane/pallas_call | solution.py:410
  31.6 0.0 collective-permute-done.9.edge_b
  31.7 0.0 collective-permute-done.10.edge_a
  31.7 2.7 %lend.1 = (bf16[3,288,128]{2,1,0:T(8,128)(2,1)S(1)}, bf16[3,288,128]{2,1,0:T(8,128)(2,1)S(1)}, bf16[256,1536]{1,0:T(8,128)(2,1)S(1)}) custom-call(bf16[3,272,128]{2,1,0:T(8,128)(2,1)S(1)} %collective-permute-done.9.edge_b, bf16[3,272,128]{2,1,0:T(8,128)(2,1)S(1)} %collective-permute-done.10.edge_a, bf16[2,256,1024]{2,1,0:T(8,128)(2,1)S(1)} %get-tuple-element.60.plane_turned, ...), custom_call_target="tpu_custom_call" | custom-call | flops 4831838208 | bytes 3145728 | tf_op jit(solution)/shard_map/lend/pallas_call | solution.py:421
  34.3 1.7 %collective-permute-start.15 = (bf16[3,288,128]{2,1,0:T(8,128)(2,1)S(1)}, bf16[3,288,128]{2,1,0:T(8,128)(2,1)S(1)}, u32[]{:S(2)}, u32[]{:S(2)}) collective-permute-start(bf16[3,288,128]{2,1,0:T(8,128)(2,1)S(1)} %get-tuple-element.62), channel_id=1, source_target_pairs={{0,8},{2,10},{4,12},{6,14},{8,0},{10,2},{12,4},{14,6},{16,24},{18,... | collective-permute-start | bytes 663560 | tf_op jit(solution)/shard_map/ppermute | solution.py:345
  36.1 3.0 %collective-permute-start.16 = (bf16[3,288,128]{2,1,0:T(8,128)(2,1)S(1)}, bf16[3,288,128]{2,1,0:T(8,128)(2,1)S(1)}, u32[]{:S(2)}, u32[]{:S(2)}) collective-permute-start(bf16[3,288,128]{2,1,0:T(8,128)(2,1)S(1)} %get-tuple-element.63), channel_id=1, source_target_pairs={{8,16},{10,18},{12,20},{14,22},{16,8},{18,10},{20,12},{22,14},{9,1... | collective-permute-start | bytes 663560 | tf_op jit(solution)/shard_map/ppermute | solution.py:345
  39.1 2.5 %edge.1 = (bf16[256,128]{1,0:T(8,128)(2,1)S(1)}, bf16[256,128]{1,0:T(8,128)(2,1)S(1)}, bf16[256,128]{1,0:T(8,128)(2,1)S(1)}, bf16[256,128]{1,0:T(8,128)(2,1)S(1)}) custom-call(bf16[3,256,128]{2,1,0:T(8,128)(2,1)S(1)} %collective-permute-done.7.refs_8_.edge_b, bf16[3,256,128]{2,1,0:T(8,128)(2,1)S(1)} %collective-permute-done.8.refs_9_.edge_a, ...), custom_call_target="tpu_custom_call" | custom-call | flops 4831838208 | bytes 3145728 | tf_op jit(solution)/shard_map/edge/pallas_call | solution.py:432
  41.6 1.8 %collective-permute-start.20 = (bf16[256,128]{1,0:T(8,128)(2,1)S(1)}, bf16[256,128]{1,0:T(8,128)(2,1)S(1)}, u32[]{:S(2)}, u32[]{:S(2)}) collective-permute-start(bf16[256,128]{1,0:T(8,128)(2,1)S(1)} %get-tuple-element.73), channel_id=1, source_target_pairs={{0,2},{2,0},{4,6},{6,4},{8,10},{10,8},{12,14},{14,12},{16,18},{18,... | collective-permute-start | bytes 196616 | tf_op jit(solution)/shard_map/ppermute | solution.py:340
  43.4 1.2 %collective-permute-start.21 = (bf16[256,128]{1,0:T(8,128)(2,1)S(1)}, bf16[256,128]{1,0:T(8,128)(2,1)S(1)}, u32[]{:S(2)}, u32[]{:S(2)}) collective-permute-start(bf16[256,128]{1,0:T(8,128)(2,1)S(1)} %get-tuple-element.74), channel_id=1, source_target_pairs={{0,4},{2,6},{4,0},{6,2},{8,12},{10,14},{12,8},{14,10},{16,20},{18,... | collective-permute-start | bytes 196616 | tf_op jit(solution)/shard_map/ppermute | solution.py:340
  44.6 0.5 collective-permute-start.22
  45.1 0.0 collective-permute-done.15.back_a
  45.1 0.0 collective-permute-done.16.back_b
  45.1 0.6 %merge.1 = (bf16[256,128]{1,0:T(8,128)(2,1)S(1)}, bf16[256,128]{1,0:T(8,128)(2,1)S(1)}, bf16[256,128]{1,0:T(8,128)(2,1)S(1)}, bf16[256,128]{1,0:T(8,128)(2,1)S(1)}) custom-call(bf16[3,288,128]{2,1,0:T(8,128)(2,1)S(1)} %collective-permute-done.15.back_a, bf16[3,288,128]{2,1,0:T(8,128)(2,1)S(1)} %collective-permute-done.16.back_b, ...), custom_call_target="tpu_custom_call" | custom-call | bytes 2097152 | tf_op jit(solution)/shard_map/merge/pallas_call | solution.py:441
  45.7 0.7 %collective-permute-start.17 = (bf16[256,128]{1,0:T(8,128)(2,1)S(1)}, bf16[256,128]{1,0:T(8,128)(2,1)S(1)}, u32[]{:S(2)}, u32[]{:S(2)}) collective-permute-start(bf16[256,128]{1,0:T(8,128)(2,1)S(1)} %get-tuple-element.70), channel_id=1, source_target_pairs={{0,2},{2,0},{4,6},{6,4},{8,10},{10,8},{12,14},{14,12},{16,18},{18,... | collective-permute-start | bytes 196616 | tf_op jit(solution)/shard_map/ppermute | solution.py:340
  46.4 1.3 %collective-permute-start.18 = (bf16[256,128]{1,0:T(8,128)(2,1)S(1)}, bf16[256,128]{1,0:T(8,128)(2,1)S(1)}, u32[]{:S(2)}, u32[]{:S(2)}) collective-permute-start(bf16[256,128]{1,0:T(8,128)(2,1)S(1)} %get-tuple-element.71), channel_id=1, source_target_pairs={{0,4},{2,6},{4,0},{6,2},{8,12},{10,14},{12,8},{14,10},{16,20},{18,... | collective-permute-start | bytes 196616 | tf_op jit(solution)/shard_map/ppermute | solution.py:340
  47.7 0.0 collective-permute-done.20.refs_1_
  47.7 0.5 collective-permute-start.19
  48.1 0.0 collective-permute-done.21.refs_2_
  48.1 0.6 %collective-permute-done.22.refs_3_ = bf16[256,128]{1,0:T(8,128)(2,1)S(1)} collective-permute-done((bf16[256,128]{1,0:T(8,128)(2,1)S(1)}, bf16[256,128]{1,0:T(8,128)(2,1)S(1)}, u32[]{:S(2)}, u32[]{:S(2)}) %collective-permute-start.22) | collective-permute-done | bytes 65568 | tf_op jit(solution)/shard_map/ppermute | solution.py:340
  48.7 0.7 %join.3 = bf16[256,512]{1,0:T(8,128)(2,1)} custom-call(bf16[256,128]{1,0:T(8,128)(2,1)S(1)} %get-tuple-element.68.refs_0_, bf16[256,128]{1,0:T(8,128)(2,1)S(1)} %collective-permute-done.20.refs_1_, bf16[256,128]{1,0:T(8,128)(2,1)S(1)} %collective-permute-done.21.refs_2_, bf16[256,128]{1,0:T(8,128)(2,1)S(1)} %collective-permute-done.22.refs_3_), custom_call_target="tpu_custom_call" | custom-call | bytes 524288 | tf_op jit(solution)/shard_map/join/pallas_call | solution.py:452
  49.4 0.0 collective-permute-done.17.refs_1_
  49.4 0.7 %collective-permute-done.18.refs_2_ = bf16[256,128]{1,0:T(8,128)(2,1)S(1)} collective-permute-done((bf16[256,128]{1,0:T(8,128)(2,1)S(1)}, bf16[256,128]{1,0:T(8,128)(2,1)S(1)}, u32[]{:S(2)}, u32[]{:S(2)}) %collective-permute-start.18) | collective-permute-done | bytes 65568 | tf_op jit(solution)/shard_map/ppermute | solution.py:340
  50.1 1.6 %collective-permute-done.19.refs_3_ = bf16[256,128]{1,0:T(8,128)(2,1)S(1)} collective-permute-done((bf16[256,128]{1,0:T(8,128)(2,1)S(1)}, bf16[256,128]{1,0:T(8,128)(2,1)S(1)}, u32[]{:S(2)}, u32[]{:S(2)}) %collective-permute-start.19) | collective-permute-done | bytes 65568 | tf_op jit(solution)/shard_map/ppermute | solution.py:340
  51.7 0.7 %join.2 = bf16[256,512]{1,0:T(8,128)(2,1)} custom-call(bf16[256,128]{1,0:T(8,128)(2,1)S(1)} %get-tuple-element.69.refs_0_, bf16[256,128]{1,0:T(8,128)(2,1)S(1)} %collective-permute-done.17.refs_1_, bf16[256,128]{1,0:T(8,128)(2,1)S(1)} %collective-permute-done.18.refs_2_, bf16[256,128]{1,0:T(8,128)(2,1)S(1)} %collective-permute-done.19.refs_3_), custom_call_target="tpu_custom_call" | custom-call | bytes 524288 | tf_op jit(solution)/shard_map/join/pallas_call | solution.py:452
Async XLA Ops:
  0.6 9.5 %collective-permute-start.1 = (bf16[256,512]{1,0:T(8,128)(2,1)}, bf16[256,512]{1,0:T(8,128)(2,1)S(1)}, u32[]{:S(2)}, u32[]{:S(2)}) collective-permute-start(bf16[256,512]{1,0:T(8,128)(2,1)} %audio.3), channel_id=1, source_target_pairs={{0,1},{1,0},{2,3},{3,2},{4,5},{5,4},{6,7},{7,6},{8,9},{9,8},{10,11... | collective-permute-start | bytes 786440 | tf_op jit(solution)/shard_map/ppermute | solution.py:336
  1.9 14.3 %collective-permute-start.11 = (bf16[256,512]{1,0:T(8,128)(2,1)}, bf16[256,512]{1,0:T(8,128)(2,1)S(1)}, u32[]{:S(2)}, u32[]{:S(2)}) collective-permute-start(bf16[256,512]{1,0:T(8,128)(2,1)} %video.1), channel_id=1, source_target_pairs={{0,1},{1,0},{2,3},{3,2},{4,5},{5,4},{6,7},{7,6},{8,9},{9,8},{10,11... | collective-permute-start | bytes 786440 | tf_op jit(solution)/shard_map/ppermute | solution.py:336
  3.2 3.0 %collective-permute-start = (bf16[272,128]{1,0:T(8,128)(2,1)S(1)}, bf16[272,128]{1,0:T(8,128)(2,1)S(1)}, u32[]{:S(2)}, u32[]{:S(2)}) collective-permute-start(bf16[272,128]{1,0:T(8,128)(2,1)S(1)} %get-tuple-element.39), channel_id=1, source_target_pairs={{0,2},{2,0},{4,6},{6,4},{8,10},{10,8},{12,14},{14,12},{16,18},{18,... | collective-permute-start | bytes 208904 | tf_op jit(solution)/shard_map/ppermute | solution.py:340
  4.5 3.8 %collective-permute-start.2 = (bf16[272,128]{1,0:T(8,128)(2,1)S(1)}, bf16[272,128]{1,0:T(8,128)(2,1)S(1)}, u32[]{:S(2)}, u32[]{:S(2)}) collective-permute-start(bf16[272,128]{1,0:T(8,128)(2,1)S(1)} %get-tuple-element.42), channel_id=1, source_target_pairs={{0,4},{2,6},{4,0},{6,2},{8,12},{10,14},{12,8},{14,10},{16,20},{18,... | collective-permute-start | bytes 208904 | tf_op jit(solution)/shard_map/ppermute | solution.py:340
  5.7 4.5 %collective-permute-start.3 = (bf16[272,128]{1,0:T(8,128)(2,1)S(1)}, bf16[272,128]{1,0:T(8,128)(2,1)S(1)}, u32[]{:S(2)}, u32[]{:S(2)}) collective-permute-start(bf16[272,128]{1,0:T(8,128)(2,1)S(1)} %get-tuple-element.43), channel_id=1, source_target_pairs={{0,6},{2,4},{4,2},{6,0},{8,14},{10,12},{12,10},{14,8},{16,22},{18,... | collective-permute-start | bytes 208904 | tf_op jit(solution)/shard_map/ppermute | solution.py:340
  10.6 5.7 %collective-permute-start.4 = (bf16[256,128]{1,0:T(8,128)(2,1)S(1)}, bf16[256,128]{1,0:T(8,128)(2,1)S(1)}, u32[]{:S(2)}, u32[]{:S(2)}) collective-permute-start(bf16[256,128]{1,0:T(8,128)(2,1)S(1)} %get-tuple-element.45), channel_id=1, source_target_pairs={{0,2},{2,0},{4,6},{6,4},{8,10},{10,8},{12,14},{14,12},{16,18},{18,... | collective-permute-start | bytes 196616 | tf_op jit(solution)/shard_map/ppermute | solution.py:340
  11.2 5.1 %collective-permute-start.5 = (bf16[256,128]{1,0:T(8,128)(2,1)S(1)}, bf16[256,128]{1,0:T(8,128)(2,1)S(1)}, u32[]{:S(2)}, u32[]{:S(2)}) collective-permute-start(bf16[256,128]{1,0:T(8,128)(2,1)S(1)} %get-tuple-element.46), channel_id=1, source_target_pairs={{0,4},{2,6},{4,0},{6,2},{8,12},{10,14},{12,8},{14,10},{16,20},{18,... | collective-permute-start | bytes 196616 | tf_op jit(solution)/shard_map/ppermute | solution.py:340
  12.5 4.0 %collective-permute-start.6 = (bf16[256,128]{1,0:T(8,128)(2,1)S(1)}, bf16[256,128]{1,0:T(8,128)(2,1)S(1)}, u32[]{:S(2)}, u32[]{:S(2)}) collective-permute-start(bf16[256,128]{1,0:T(8,128)(2,1)S(1)} %get-tuple-element.47), channel_id=1, source_target_pairs={{0,6},{2,4},{4,2},{6,0},{8,14},{10,12},{12,10},{14,8},{16,22},{18,... | collective-permute-start | bytes 196616 | tf_op jit(solution)/shard_map/ppermute | solution.py:340
  13.0 8.3 %collective-permute-start.7 = (bf16[3,256,128]{2,1,0:T(8,128)(2,1)S(1)}, bf16[3,256,128]{2,1,0:T(8,128)(2,1)S(1)}, u32[]{:S(2)}, u32[]{:S(2)}) collective-permute-start(bf16[3,256,128]{2,1,0:T(8,128)(2,1)S(1)} %get-tuple-element.49), channel_id=1, source_target_pairs={{8,16},{10,18},{12,20},{14,22},{16,8},{18,10},{20,12},{22,14},{9,1... | collective-permute-start | bytes 589832 | tf_op jit(solution)/shard_map/ppermute | solution.py:345
  16.2 6.1 %collective-permute-start.8 = (bf16[3,256,128]{2,1,0:T(8,128)(2,1)S(1)}, bf16[3,256,128]{2,1,0:T(8,128)(2,1)S(1)}, u32[]{:S(2)}, u32[]{:S(2)}) collective-permute-start(bf16[3,256,128]{2,1,0:T(8,128)(2,1)S(1)} %get-tuple-element.50), channel_id=1, source_target_pairs={{0,8},{2,10},{4,12},{6,14},{8,0},{10,2},{12,4},{14,6},{16,24},{18,... | collective-permute-start | bytes 589832 | tf_op jit(solution)/shard_map/ppermute | solution.py:345
  16.9 7.7 %collective-permute-start.12 = (bf16[512,128]{1,0:T(8,128)(2,1)S(1)}, bf16[512,128]{1,0:T(8,128)(2,1)S(1)}, u32[]{:S(2)}, u32[]{:S(2)}) collective-permute-start(bf16[512,128]{1,0:T(8,128)(2,1)S(1)} %get-tuple-element.57), channel_id=1, source_target_pairs={{0,2},{2,0},{4,6},{6,4},{8,10},{10,8},{12,14},{14,12},{16,18},{18,... | collective-permute-start | bytes 393224 | tf_op jit(solution)/shard_map/ppermute | solution.py:340
  17.3 7.3 %collective-permute-start.13 = (bf16[512,128]{1,0:T(8,128)(2,1)S(1)}, bf16[512,128]{1,0:T(8,128)(2,1)S(1)}, u32[]{:S(2)}, u32[]{:S(2)}) collective-permute-start(bf16[512,128]{1,0:T(8,128)(2,1)S(1)} %get-tuple-element.58), channel_id=1, source_target_pairs={{0,4},{2,6},{4,0},{6,2},{8,12},{10,14},{12,8},{14,10},{16,20},{18,... | collective-permute-start | bytes 393224 | tf_op jit(solution)/shard_map/ppermute | solution.py:340
  18.5 6.9 %collective-permute-start.14 = (bf16[512,128]{1,0:T(8,128)(2,1)S(1)}, bf16[512,128]{1,0:T(8,128)(2,1)S(1)}, u32[]{:S(2)}, u32[]{:S(2)}) collective-permute-start(bf16[512,128]{1,0:T(8,128)(2,1)S(1)} %get-tuple-element.59), channel_id=1, source_target_pairs={{0,6},{2,4},{4,2},{6,0},{8,14},{10,12},{12,10},{14,8},{16,22},{18,... | collective-permute-start | bytes 393224 | tf_op jit(solution)/shard_map/ppermute | solution.py:340
  22.4 9.3 %collective-permute-start.9 = (bf16[3,272,128]{2,1,0:T(8,128)(2,1)S(1)}, bf16[3,272,128]{2,1,0:T(8,128)(2,1)S(1)}, u32[]{:S(2)}, u32[]{:S(2)}) collective-permute-start(bf16[3,272,128]{2,1,0:T(8,128)(2,1)S(1)} %get-tuple-element.51), channel_id=1, source_target_pairs={{8,16},{10,18},{12,20},{14,22},{16,8},{18,10},{20,12},{22,14},{9,1... | collective-permute-start | bytes 626696 | tf_op jit(solution)/shard_map/ppermute | solution.py:345
  24.5 7.1 %collective-permute-start.10 = (bf16[3,272,128]{2,1,0:T(8,128)(2,1)S(1)}, bf16[3,272,128]{2,1,0:T(8,128)(2,1)S(1)}, u32[]{:S(2)}, u32[]{:S(2)}) collective-permute-start(bf16[3,272,128]{2,1,0:T(8,128)(2,1)S(1)} %get-tuple-element.52), channel_id=1, source_target_pairs={{0,8},{2,10},{4,12},{6,14},{8,0},{10,2},{12,4},{14,6},{16,24},{18,... | collective-permute-start | bytes 626696 | tf_op jit(solution)/shard_map/ppermute | solution.py:345
  34.3 10.8 %collective-permute-start.15 = (bf16[3,288,128]{2,1,0:T(8,128)(2,1)S(1)}, bf16[3,288,128]{2,1,0:T(8,128)(2,1)S(1)}, u32[]{:S(2)}, u32[]{:S(2)}) collective-permute-start(bf16[3,288,128]{2,1,0:T(8,128)(2,1)S(1)} %get-tuple-element.62), channel_id=1, source_target_pairs={{0,8},{2,10},{4,12},{6,14},{8,0},{10,2},{12,4},{14,6},{16,24},{18,... | collective-permute-start | bytes 663560 | tf_op jit(solution)/shard_map/ppermute | solution.py:345
  36.1 9.1 %collective-permute-start.16 = (bf16[3,288,128]{2,1,0:T(8,128)(2,1)S(1)}, bf16[3,288,128]{2,1,0:T(8,128)(2,1)S(1)}, u32[]{:S(2)}, u32[]{:S(2)}) collective-permute-start(bf16[3,288,128]{2,1,0:T(8,128)(2,1)S(1)} %get-tuple-element.63), channel_id=1, source_target_pairs={{8,16},{10,18},{12,20},{14,22},{16,8},{18,10},{20,12},{22,14},{9,1... | collective-permute-start | bytes 663560 | tf_op jit(solution)/shard_map/ppermute | solution.py:345
  41.6 6.1 %collective-permute-start.20 = (bf16[256,128]{1,0:T(8,128)(2,1)S(1)}, bf16[256,128]{1,0:T(8,128)(2,1)S(1)}, u32[]{:S(2)}, u32[]{:S(2)}) collective-permute-start(bf16[256,128]{1,0:T(8,128)(2,1)S(1)} %get-tuple-element.73), channel_id=1, source_target_pairs={{0,2},{2,0},{4,6},{6,4},{8,10},{10,8},{12,14},{14,12},{16,18},{18,... | collective-permute-start | bytes 196616 | tf_op jit(solution)/shard_map/ppermute | solution.py:340
  43.4 4.7 %collective-permute-start.21 = (bf16[256,128]{1,0:T(8,128)(2,1)S(1)}, bf16[256,128]{1,0:T(8,128)(2,1)S(1)}, u32[]{:S(2)}, u32[]{:S(2)}) collective-permute-start(bf16[256,128]{1,0:T(8,128)(2,1)S(1)} %get-tuple-element.74), channel_id=1, source_target_pairs={{0,4},{2,6},{4,0},{6,2},{8,12},{10,14},{12,8},{14,10},{16,20},{18,... | collective-permute-start | bytes 196616 | tf_op jit(solution)/shard_map/ppermute | solution.py:340
  44.6 4.0 %collective-permute-start.22 = (bf16[256,128]{1,0:T(8,128)(2,1)S(1)}, bf16[256,128]{1,0:T(8,128)(2,1)S(1)}, u32[]{:S(2)}, u32[]{:S(2)}) collective-permute-start(bf16[256,128]{1,0:T(8,128)(2,1)S(1)} %get-tuple-element.75), channel_id=1, source_target_pairs={{0,6},{2,4},{4,2},{6,0},{8,14},{10,12},{12,10},{14,8},{16,22},{18,... | collective-permute-start | bytes 196616 | tf_op jit(solution)/shard_map/ppermute | solution.py:340
  45.7 3.7 %collective-permute-start.17 = (bf16[256,128]{1,0:T(8,128)(2,1)S(1)}, bf16[256,128]{1,0:T(8,128)(2,1)S(1)}, u32[]{:S(2)}, u32[]{:S(2)}) collective-permute-start(bf16[256,128]{1,0:T(8,128)(2,1)S(1)} %get-tuple-element.70), channel_id=1, source_target_pairs={{0,2},{2,0},{4,6},{6,4},{8,10},{10,8},{12,14},{14,12},{16,18},{18,... | collective-permute-start | bytes 196616 | tf_op jit(solution)/shard_map/ppermute | solution.py:340
  46.4 3.7 %collective-permute-start.18 = (bf16[256,128]{1,0:T(8,128)(2,1)S(1)}, bf16[256,128]{1,0:T(8,128)(2,1)S(1)}, u32[]{:S(2)}, u32[]{:S(2)}) collective-permute-start(bf16[256,128]{1,0:T(8,128)(2,1)S(1)} %get-tuple-element.71), channel_id=1, source_target_pairs={{0,4},{2,6},{4,0},{6,2},{8,12},{10,14},{12,8},{14,10},{16,20},{18,... | collective-permute-start | bytes 196616 | tf_op jit(solution)/shard_map/ppermute | solution.py:340
  47.7 4.0 %collective-permute-start.19 = (bf16[256,128]{1,0:T(8,128)(2,1)S(1)}, bf16[256,128]{1,0:T(8,128)(2,1)S(1)}, u32[]{:S(2)}, u32[]{:S(2)}) collective-permute-start(bf16[256,128]{1,0:T(8,128)(2,1)S(1)} %get-tuple-element.72), channel_id=1, source_target_pairs={{0,6},{2,4},{4,2},{6,0},{8,14},{10,12},{12,10},{14,8},{16,22},{18,... | collective-permute-start | bytes 196616 | tf_op jit(solution)/shard_map/ppermute | solution.py:340

commit v13 on v12

--- a/solution.py
+++ b/solution.py
@@ -163,22 +163,24 @@
     return out
 
 
-def attend(scores, old, values):
-    width = values.shape[1] // 2
-    top = old
-    for at in range(0, scores.shape[1], width):
-        part = scores[:, at : at + width]
-        top = part if top is None else jnp.maximum(top, part)
+def attend(scores, values):
+    top = None
+    for s in scores:
+        for at in range(0, s.shape[1], values[0].shape[1] // 2):
+            part = s[:, at : at + values[0].shape[1] // 2]
+            top = part if top is None else jnp.maximum(top, part)
     peak = jnp.max(top, axis=1, keepdims=True)
-    return peak, product(jnp.exp(scores - peak).astype(jnp.bfloat16), values)
-
-
-def plane_kernel(*refs):
-    audio, queries, video = refs[:GROUP], refs[GROUP : 2 * GROUP], refs[2 * GROUP : 3 * GROUP]
-    peaks, sums, turned, beside, asks = refs[3 * GROUP :]
-    rows, width = queries[0].shape
-    mine = place()
-    beside[:, :, width:] = jnp.ones((2, GROUP * rows, width), beside.dtype)
+    mixed = None
+    for s, value in zip(scores, values):
+        part = product(jnp.exp(s - peak).astype(jnp.bfloat16), value)
+        mixed = part if mixed is None else mixed + part
+    return peak, mixed
+
+
+def set_up(audio, asked, keys, values, turned, beside, asks):
+    rows, width = asks.shape[1] // 2, asks.shape[2] // 2
+    mine = place()
+    beside[:, width:] = jnp.ones((GROUP * rows, width), beside.dtype)
     for k in range(GROUP):
         b = mine ^ k
 
@@ -186,24 +188,35 @@
             return pl.ds(pl.multiple_of(b * rows + at, size), size)
 
         marks = marks_turned(audio[k][rows:])
-        projections = (queries[k][...], video[k][rows:])
-        for i in range(2):
-            key = projections[1 - i]
-            asks[i, b] = stacked_ask(projections[i], marks)
-            beside[i, spot(0, rows), :width] = (audio if i else video)[k][:rows]
-            for part, x in enumerate(marks):
-                at = spot(part * width, width)
-                turned[i, :width, at] = jnp.transpose(key[part * width : (part + 1) * width])
-                turned[i, width:, at] = x
-
-    units = [(i, b) for b in range(GROUP) for i in range(2)]
-    ahead = product(asks[units[0]], turned[0])
-    for n, (i, b) in enumerate(units):
+        asks[b] = stacked_ask(asked(k), marks)
+        beside[spot(0, rows), :width] = values(k)
+        key = keys(k)
+        for part, x in enumerate(marks):
+            at = spot(part * width, width)
+            turned[:width, at] = jnp.transpose(key[part * width : (part + 1) * width])
+            turned[width:, at] = x
+
+
+def rows_kernel(*refs):
+    audio, queries, video = refs[:GROUP], refs[GROUP : 2 * GROUP], refs[2 * GROUP : 3 * GROUP]
+    peaks, sums, turned, beside, asks = refs[-5:]
+    rows, width = queries[0].shape
+    set_up(
+        audio,
+        lambda k: queries[k][...],
+        lambda k: video[k][rows:],
+        lambda k: video[k][:rows],
+        turned,
+        beside,
+        asks,
+    )
+    ahead = product(asks[0], turned[...])
+    for b in range(GROUP):
         scores = ahead
-        if n + 1 < len(units):
-            ahead = product(asks[units[n + 1]], turned[units[n + 1][0]])
-        peak, sums[i, b] = attend(scores, None, beside[i])
-        peaks[i, b] = jnp.broadcast_to(peak, (peak.shape[0], width))
+        if b + 1 < GROUP:
+            ahead = product(asks[b + 1], turned[...])
+        peak, sums[b] = attend([scores], [beside[...]])
+        peaks[b] = jnp.broadcast_to(peak, (peak.shape[0], width))
 
 
 def lend_kernel(edge_b, edge_a, plane_turned, plane_beside, first, second, turned, ordered, results):
@@ -223,7 +236,7 @@
             at = slice(e * rows + part * width, e * rows + (part + 1) * width)
             turned[:width, at] = jnp.transpose(query[part * width : (part + 1) * width])
             turned[width:, at] = x
-        return product(stacked_ask(query, marks), plane_turned[0, :, blocks[e]])
+        return product(stacked_ask(query, marks), plane_turned[:, blocks[e]])
 
     ahead = scores_of(0)
     for e in range(2 * RADIUS):
@@ -231,7 +244,7 @@
         scores = ahead
         if e + 1 < 2 * RADIUS:
             ahead = scores_of(e + 1)
-        peak, mixed = attend(scores, None, plane_beside[0, blocks[e]])
+        peak, mixed = attend([scores], [plane_beside[blocks[e]]])
         mean = by_head(mixed[:, :width], rows) / by_head(mixed[:, width:], rows)
         results[side, j, :rows] = mean.astype(results.dtype)
         logs = peak + jnp.log(mixed[:, width:])
@@ -251,26 +264,40 @@
     second[...] = results[odd]
 
 
-def edge_kernel(edge_b, edge_a, turned, asks, peaks, sums, *refs):
-    outs, (beside, whole) = refs[-GROUP - 2 : -2], refs[-2:]
+def columns_kernel(*refs):
+    audio, queries, video = refs[:GROUP], refs[GROUP : 2 * GROUP], refs[2 * GROUP : 3 * GROUP]
+    (edge_b, edge_a, edge_turned), outs = refs[3 * GROUP : 3 * GROUP + 3], refs[-GROUP - 5 : -5]
+    edge_beside, turned, beside, asks, whole = refs[-5:]
     rows, width = outs[0].shape
     mine = place()
     odd = lax.rem(plane(), 2)
-    beside[:, width:] = jnp.ones((beside.shape[0], width), beside.dtype)
+    set_up(
+        audio,
+        lambda k: video[k][rows:],
+        lambda k: queries[k][...],
+        lambda k: audio[k][:rows],
+        turned,
+        beside,
+        asks,
+    )
+    edge_beside[:, width:] = jnp.ones((edge_beside.shape[0], width), beside.dtype)
     for edge, base in ((edge_a, RADIUS * (1 - odd)), (edge_b, RADIUS * odd)):
         for j in range(RADIUS):
-            beside[pl.ds(pl.multiple_of((base + j) * rows, rows), rows), :width] = edge[j]
+            at = pl.ds(pl.multiple_of((base + j) * rows, rows), rows)
+            edge_beside[at, :width] = edge[j]
     near = [slice(b * rows, (b + RADIUS) * rows) for b in range(GROUP)]
-    scores = product(asks[1, 0], turned[:, near[0]])
+
+    def scores_of(b):
+        return [product(asks[b], turned[...]), product(asks[b], edge_turned[:, near[b]])]
+
+    ahead = scores_of(0)
     for b in range(GROUP):
-        following = product(asks[1, b + 1], turned[:, near[b + 1]]) if b + 1 < GROUP else None
-        old = peaks[1, b]
-        peak, mixed = attend(scores, old, beside[near[b]])
-        factor = jnp.exp(old - peak)
-        mixed += sums[1, b] * jnp.concatenate([factor, factor], axis=1)
+        scores = ahead
+        if b + 1 < GROUP:
+            ahead = scores_of(b + 1)
+        _, mixed = attend(scores, [beside[...], edge_beside[near[b]]])
         mean = by_head(mixed[:, :width], rows) / by_head(mixed[:, width:], rows)
         whole[b] = mean.astype(whole.dtype)
-        scores = following
     for k in range(GROUP):
         outs[k][...] = whole[mine ^ k]
 
@@ -307,13 +334,13 @@
         if b >= GROUP - RADIUS:
             theirs.append((1, b - (GROUP - RADIUS)))
         theirs = [(logs(*t), backs[t[0], t[1], :rows].astype(jnp.float32)) for t in theirs]
-        old = by_head(peaks[0, b], rows)
+        old = by_head(peaks[b], rows)
         top = old
         for log, _ in theirs:
             top = jnp.maximum(top, log)
         factor = jnp.exp(old - top)
-        value = by_head(sums[0, b, :, :width], rows) * factor
-        total = by_head(sums[0, b, :, width:], rows) * factor
+        value = by_head(sums[b, :, :width], rows) * factor
+        total = by_head(sums[b, :, width:], rows) * factor
         for log, mean in theirs:
             weight = jnp.exp(log - top)
             value += weight * mean
@@ -403,19 +430,20 @@
     queries = project(HEAD**-0.5, query_part, other_audio, query_rest, after=packs[1:])
     queries = traded(queries)
     video = project(1.0, key_part, other_video, key_rest, stream=[video_copy], after=queries[1:])
-    query_edges = halo(queries, packs, *audio_edges[::-1])
+    query_edges = halo(queries, packs, video[0])
     video = traded(video)
 
     inside, around = GROUP * rows, 2 * RADIUS * rows
-    peaks, sums, plane_turned, plane_beside, asks = call(
-        plane_kernel,
-        [shape((2, GROUP, heads * rows, n * width), f32) for n in (1, 2)]
-        + [shape((2, 2 * width, inside), bf16), shape((2, inside, 2 * width), bf16)]
-        + [shape((2, GROUP, heads * rows, 2 * width), bf16)],
-        flops=32 * GROUP * rows * inside * width,
+    turned, beside = shape((2 * width, inside), bf16), shape((inside, 2 * width), bf16)
+    asks = shape((GROUP, heads * rows, 2 * width), bf16)
+    peaks, sums, plane_turned, plane_beside = call(
+        rows_kernel,
+        [shape((GROUP, heads * rows, n * width), f32) for n in (1, 2)] + [turned, beside],
+        [pltpu.VMEM(asks.shape, bf16)],
+        flops=16 * GROUP * rows * inside * width,
         moved=8 * inside * width * 2,
-        exps=4 * GROUP * rows * inside,
-        name="plane",
+        exps=2 * GROUP * rows * inside,
+        name="rows",
     )(*packs, *queries, *video)
     back = shape((RADIUS, rows + rows // width * STAT_ROWS, width), bf16)
     lent_a, lent_b, edge_turned = call(
@@ -430,14 +458,16 @@
     backs = [crossed(x, i) for i, x in enumerate((lent_a, lent_b))]
 
     video_pieces = call(
-        edge_kernel,
+        columns_kernel,
         [piece] * GROUP,
-        [pltpu.VMEM((around, 2 * width), bf16), pltpu.VMEM((GROUP, rows, width), bf16)],
-        flops=48 * RADIUS * GROUP * rows * rows * width,
+        [pltpu.VMEM((around, 2 * width), bf16)]
+        + [pltpu.VMEM(x.shape, bf16) for x in (turned, beside, asks)]
+        + [pltpu.VMEM((GROUP, rows, width), bf16)],
+        flops=112 * GROUP * rows * rows * width,
         moved=8 * around * width * 2,
-        exps=2 * RADIUS * GROUP * rows * rows,
-        name="edge",
-    )(*audio_edges[::-1], edge_turned, asks, peaks, sums)
+        exps=14 * GROUP * rows * rows,
+        name="columns",
+    )(*packs, *queries, *video, *audio_edges[::-1], edge_turned)
     audio_pieces = call(
         merge_kernel,
         [piece] * GROUP,

time: 52.8 us -> 51.5 us (0.975)
  starting transfers between devices: 25.3 us -> 24 us
    ppermute x6, waiting for transfers between devices: 3.2 us -> 0.02 us  [crossed(): lax.ppermute(sent, 'tm', [(p * GROUP + i, q * GROUP + i) for p, q in pair...]
    ppermute x15, waiting for transfers between devices: 5.98 us -> 8.87 us  [traded(): lax.ppermute(pieces[k], 'tm', pairs(k))]
    ppermute x15, starting transfers between devices: 13.6 us -> 12.3 us  [traded(): lax.ppermute(pieces[k], 'tm', pairs(k))]
    ppermute x2, waiting for transfers between devices: 0.01 us -> 0.77 us  [swapped(): return lax.ppermute(x, 'head', [(0, 1), (1, 0)])]
    pallas_call x2, Pallas kernels: 8.78 us -> 8.24 us  [the longest x1 4.92 us: local(): call(columns_kernel, [piece] * GROUP, [pltpu.VMEM((around, 2 * width), bf...]
  transfers between devices with their start and end apart: 23 -> 23, of which waited for: 9 -> 9; matrix products, arithmetic and copies ran while one was open for 0% -> 0% of each run, Pallas kernels for 26% -> 30%
where the time goes in v13:
time: 51.5 us; the launch traced here: 51.3 us
  starting transfers between devices  24 us (47%)
  Pallas kernels  16.7 us (32%)
  waiting for transfers between devices  9.66 us (19%)
  between operations  0.97 us (2%)
    ppermute x15, starting transfers between devices, traded(): lax.ppermute(pieces[k], 'tm', pairs(k))  12.3 us
    ppermute x6, starting transfers between devices, crossed(): lax.ppermute(sent, 'tm', [(p * GROUP + i, q * GROUP + i) for p, q in pair...  10.1 us
    ppermute x15, waiting for transfers between devices, traded(): lax.ppermute(pieces[k], 'tm', pairs(k))  8.87 us
    pallas_call x1, Pallas kernels, local(): call(columns_kernel, [piece] * GROUP, [pltpu.VMEM((around, 2 * width), bf...  4.92 us
    pallas_call x1, Pallas kernels, local(): call(rows_kernel, [shape((GROUP, heads * rows, n * width), f32) for n in...  3.32 us
    pallas_call x1, Pallas kernels, local(): call(lend_kernel, [back, back, shape((2 * width, around), bf16)], [pltpu....  2.75 us
    pallas_call x1, Pallas kernels, local(): call(prepare_kernel, [part, part, square, square, shape((rows, half), bf1...  1.78 us
    ppermute x2, starting transfers between devices, swapped(): return lax.ppermute(x, 'head', [(0, 1), (1, 0)])  1.53 us
  transfers between devices with their start and end apart: 23, of which 9 were waited for; matrix products, arithmetic and copies ran while one was open for 0% of the time, Pallas kernels for 30%

profile of v13, /device:TPU:9, one launch (start us, length us, event | category | flops | bytes accessed | tf_op | source)
XLA Modules:
  0.0 51.3 jit_solution(16999175047193164678)
XLA Ops:
  0.6 1.3 %collective-permute-start.1 = (bf16[256,512]{1,0:T(8,128)(2,1)}, bf16[256,512]{1,0:T(8,128)(2,1)S(1)}, u32[]{:S(2)}, u32[]{:S(2)}) collective-permute-start(bf16[256,512]{1,0:T(8,128)(2,1)} %audio.3), channel_id=1, source_target_pairs={{0,1},{1,0},{2,3},{3,2},{4,5},{5,4},{6,7},{7,6},{8,9},{9,8},{10,11... | collective-permute-start | bytes 786440 | tf_op jit(solution)/shard_map/ppermute | solution.py:363
  1.9 0.2 collective-permute-start.7
  2.2 1.0 %split.1 = (bf16[272,128]{1,0:T(8,128)(2,1)S(1)}, bf16[272,128]{1,0:T(8,128)(2,1)S(1)}, bf16[272,128]{1,0:T(8,128)(2,1)S(1)}, bf16[272,128]{1,0:T(8,128)(2,1)S(1)}) custom-call(bf16[256,512]{1,0:T(8,128)(2,1)} %audio.3, s32[2,128]{1,0:T(2,128)} %bitcast.1), custom_call_target="tpu_custom_call" | custom-call | bytes 524288 | tf_op jit(solution)/shard_map/split/pallas_call | solution.py:385
  3.2 1.3 %collective-permute-start = (bf16[272,128]{1,0:T(8,128)(2,1)S(1)}, bf16[272,128]{1,0:T(8,128)(2,1)S(1)}, u32[]{:S(2)}, u32[]{:S(2)}) collective-permute-start(bf16[272,128]{1,0:T(8,128)(2,1)S(1)} %get-tuple-element.38), channel_id=1, source_target_pairs={{0,2},{2,0},{4,6},{6,4},{8,10},{10,8},{12,14},{14,12},{16,18},{18,... | collective-permute-start | bytes 208904 | tf_op jit(solution)/shard_map/ppermute | solution.py:367
  4.5 1.2 %collective-permute-start.2 = (bf16[272,128]{1,0:T(8,128)(2,1)S(1)}, bf16[272,128]{1,0:T(8,128)(2,1)S(1)}, u32[]{:S(2)}, u32[]{:S(2)}) collective-permute-start(bf16[272,128]{1,0:T(8,128)(2,1)S(1)} %get-tuple-element.41), channel_id=1, source_target_pairs={{0,4},{2,6},{4,0},{6,2},{8,12},{10,14},{12,8},{14,10},{16,20},{18,... | collective-permute-start | bytes 208904 | tf_op jit(solution)/shard_map/ppermute | solution.py:367
  5.7 0.5 collective-permute-start.3
  6.2 0.0 collective-permute-done.refs_0_.refs_5_.refs_1_
  6.2 1.8 %prepare.1 = (f32[256,512]{1,0:T(8,128)S(1)}, f32[256,512]{1,0:T(8,128)S(1)}, bf16[512,512]{1,0:T(8,128)(2,1)S(1)}, bf16[512,512]{1,0:T(8,128)(2,1)S(1)}, bf16[256,512]{1,0:T(8,128)(2,1)S(1)}) custom-call(bf16[256,512]{1,0:T(8,128)(2,1)} %audio.3, bf16[256,512]{1,0:T(8,128)(2,1)} %video.1, bf16[1024,512]{1,0:T(8,128)(2,1)} %query.1, bf16[1024,512]{1,0:T(8,128)(2,1)} %key.1, ...), custom_call_target="tpu_custom_call" | custom-call | flops 268435456 | bytes 4194304 | tf_op jit(solution)/shard_map/prepare/pallas_call | solution.py:395
  8.0 0.3 collective-permute-done.2.refs_1_.refs_6_.refs_2_
  8.2 1.9 %collective-permute-done.3.refs_2_.refs_7_.refs_3_ = bf16[272,128]{1,0:T(8,128)(2,1)S(1)} collective-permute-done((bf16[272,128]{1,0:T(8,128)(2,1)S(1)}, bf16[272,128]{1,0:T(8,128)(2,1)S(1)}, u32[]{:S(2)}, u32[]{:S(2)}) %collective-permute-start.3) | collective-permute-done | bytes 69664 | tf_op jit(solution)/shard_map/ppermute | solution.py:367
  10.2 0.0 collective-permute-done.1.other
  10.2 0.4 project.2
  10.6 0.7 %collective-permute-start.4 = (bf16[256,128]{1,0:T(8,128)(2,1)S(1)}, bf16[256,128]{1,0:T(8,128)(2,1)S(1)}, u32[]{:S(2)}, u32[]{:S(2)}) collective-permute-start(bf16[256,128]{1,0:T(8,128)(2,1)S(1)} %get-tuple-element.44), channel_id=1, source_target_pairs={{0,2},{2,0},{4,6},{6,4},{8,10},{10,8},{12,14},{14,12},{16,18},{18,... | collective-permute-start | bytes 196616 | tf_op jit(solution)/shard_map/ppermute | solution.py:367
  11.2 1.2 %collective-permute-start.5 = (bf16[256,128]{1,0:T(8,128)(2,1)S(1)}, bf16[256,128]{1,0:T(8,128)(2,1)S(1)}, u32[]{:S(2)}, u32[]{:S(2)}) collective-permute-start(bf16[256,128]{1,0:T(8,128)(2,1)S(1)} %get-tuple-element.45), channel_id=1, source_target_pairs={{0,4},{2,6},{4,0},{6,2},{8,12},{10,14},{12,8},{14,10},{16,20},{18,... | collective-permute-start | bytes 196616 | tf_op jit(solution)/shard_map/ppermute | solution.py:367
  12.5 0.5 collective-permute-start.6
  12.9 0.8 %collective-permute-done.7.other = bf16[256,512]{1,0:T(8,128)(2,1)S(1)} collective-permute-done((bf16[256,512]{1,0:T(8,128)(2,1)}, bf16[256,512]{1,0:T(8,128)(2,1)S(1)}, u32[]{:S(2)}, u32[]{:S(2)}) %collective-permute-start.7) | collective-permute-done | bytes 262176 | tf_op jit(solution)/shard_map/ppermute | solution.py:363
  13.7 0.0 collective-permute-done.4.refs_1_.refs_5_
  13.7 1.2 %collective-permute-done.5.refs_2_.refs_6_ = bf16[256,128]{1,0:T(8,128)(2,1)S(1)} collective-permute-done((bf16[256,128]{1,0:T(8,128)(2,1)S(1)}, bf16[256,128]{1,0:T(8,128)(2,1)S(1)}, u32[]{:S(2)}, u32[]{:S(2)}) %collective-permute-start.5) | collective-permute-done | bytes 65568 | tf_op jit(solution)/shard_map/ppermute | solution.py:367
  14.9 1.6 %collective-permute-done.6.refs_3_.refs_7_ = bf16[256,128]{1,0:T(8,128)(2,1)S(1)} collective-permute-done((bf16[256,128]{1,0:T(8,128)(2,1)S(1)}, bf16[256,128]{1,0:T(8,128)(2,1)S(1)}, u32[]{:S(2)}, u32[]{:S(2)}) %collective-permute-start.6) | collective-permute-done | bytes 65568 | tf_op jit(solution)/shard_map/ppermute | solution.py:367
  16.5 0.4 project.3
  16.9 0.4 collective-permute-start.10
  17.3 1.1 %collective-permute-start.11 = (bf16[512,128]{1,0:T(8,128)(2,1)S(1)}, bf16[512,128]{1,0:T(8,128)(2,1)S(1)}, u32[]{:S(2)}, u32[]{:S(2)}) collective-permute-start(bf16[512,128]{1,0:T(8,128)(2,1)S(1)} %get-tuple-element.55), channel_id=1, source_target_pairs={{0,4},{2,6},{4,0},{6,2},{8,12},{10,14},{12,8},{14,10},{16,20},{18,... | collective-permute-start | bytes 393224 | tf_op jit(solution)/shard_map/ppermute | solution.py:367
  18.4 0.7 %collective-permute-start.12 = (bf16[512,128]{1,0:T(8,128)(2,1)S(1)}, bf16[512,128]{1,0:T(8,128)(2,1)S(1)}, u32[]{:S(2)}, u32[]{:S(2)}) collective-permute-start(bf16[512,128]{1,0:T(8,128)(2,1)S(1)} %get-tuple-element.56), channel_id=1, source_target_pairs={{0,6},{2,4},{4,2},{6,0},{8,14},{10,12},{12,10},{14,8},{16,22},{18,... | collective-permute-start | bytes 393224 | tf_op jit(solution)/shard_map/ppermute | solution.py:367
  19.1 0.1 halo.2
  19.2 3.2 %collective-permute-start.8 = (bf16[3,272,128]{2,1,0:T(8,128)(2,1)S(1)}, bf16[3,272,128]{2,1,0:T(8,128)(2,1)S(1)}, u32[]{:S(2)}, u32[]{:S(2)}) collective-permute-start(bf16[3,272,128]{2,1,0:T(8,128)(2,1)S(1)} %get-tuple-element.52), channel_id=1, source_target_pairs={{8,16},{10,18},{12,20},{14,22},{16,8},{18,10},{20,12},{22,14},{9,1... | collective-permute-start | bytes 626696 | tf_op jit(solution)/shard_map/ppermute | solution.py:372
  22.4 0.1 collective-permute-start.9
  22.5 0.1 halo.3
  22.6 0.0 collective-permute-done.10.refs_9_
  22.6 2.1 %collective-permute-start.15 = (bf16[3,256,128]{2,1,0:T(8,128)(2,1)S(1)}, bf16[3,256,128]{2,1,0:T(8,128)(2,1)S(1)}, u32[]{:S(2)}, u32[]{:S(2)}) collective-permute-start(bf16[3,256,128]{2,1,0:T(8,128)(2,1)S(1)} %get-tuple-element.63), channel_id=1, source_target_pairs={{8,16},{10,18},{12,20},{14,22},{16,8},{18,10},{20,12},{22,14},{9,1... | collective-permute-start | bytes 589832 | tf_op jit(solution)/shard_map/ppermute | solution.py:372
  24.7 0.0 collective-permute-done.11.refs_10_
  24.7 0.1 collective-permute-start.16
  24.8 0.9 %collective-permute-done.12.refs_11_ = bf16[512,128]{1,0:T(8,128)(2,1)S(1)} collective-permute-done((bf16[512,128]{1,0:T(8,128)(2,1)S(1)}, bf16[512,128]{1,0:T(8,128)(2,1)S(1)}, u32[]{:S(2)}, u32[]{:S(2)}) %collective-permute-start.12) | collective-permute-done | bytes 131104 | tf_op jit(solution)/shard_map/ppermute | solution.py:367
  25.7 3.3 %rows.1 = (f32[4,512,128]{2,1,0:T(8,128)S(1)}, f32[4,512,256]{2,1,0:T(8,128)S(1)}, bf16[256,1024]{1,0:T(8,128)(2,1)S(1)}, bf16[1024,256]{1,0:T(8,128)(2,1)S(1)}) custom-call(bf16[272,128]{1,0:T(8,128)(2,1)S(1)} %get-tuple-element.47.refs_4_.refs_0_, bf16[272,128]{1,0:T(8,128)(2,1)S(1)} %collective-permute-done.refs_0_.refs_5_.refs_1_, ...), custom_call_target="tpu_custom_call" | custom-call | flops 2147483648 | bytes 2097152 | tf_op jit(solution)/shard_map/rows/pallas_call | solution.py:439
  29.0 0.0 collective-permute-done.8.edge_b
  29.0 0.0 collective-permute-done.9.edge_a
  29.0 2.7 %lend.1 = (bf16[3,288,128]{2,1,0:T(8,128)(2,1)S(1)}, bf16[3,288,128]{2,1,0:T(8,128)(2,1)S(1)}, bf16[256,1536]{1,0:T(8,128)(2,1)S(1)}) custom-call(bf16[3,272,128]{2,1,0:T(8,128)(2,1)S(1)} %collective-permute-done.8.edge_b, bf16[3,272,128]{2,1,0:T(8,128)(2,1)S(1)} %collective-permute-done.9.edge_a, bf16[256,1024]{1,0:T(8,128)(2,1)S(1)} %get-tuple-element.57.plane_turned, ...), custom_call_target="tpu_custom_call" | custom-call | flops 4831838208 | bytes 3145728 | tf_op jit(solution)/shard_map/lend/pallas_call | solution.py:449
  31.8 0.6 %collective-permute-start.13 = (bf16[3,288,128]{2,1,0:T(8,128)(2,1)S(1)}, bf16[3,288,128]{2,1,0:T(8,128)(2,1)S(1)}, u32[]{:S(2)}, u32[]{:S(2)}) collective-permute-start(bf16[3,288,128]{2,1,0:T(8,128)(2,1)S(1)} %get-tuple-element.59), channel_id=1, source_target_pairs={{0,8},{2,10},{4,12},{6,14},{8,0},{10,2},{12,4},{14,6},{16,24},{18,... | collective-permute-start | bytes 663560 | tf_op jit(solution)/shard_map/ppermute | solution.py:372
  32.4 4.1 %collective-permute-start.14 = (bf16[3,288,128]{2,1,0:T(8,128)(2,1)S(1)}, bf16[3,288,128]{2,1,0:T(8,128)(2,1)S(1)}, u32[]{:S(2)}, u32[]{:S(2)}) collective-permute-start(bf16[3,288,128]{2,1,0:T(8,128)(2,1)S(1)} %get-tuple-element.60), channel_id=1, source_target_pairs={{8,16},{10,18},{12,20},{14,22},{16,8},{18,10},{20,12},{22,14},{9,1... | collective-permute-start | bytes 663560 | tf_op jit(solution)/shard_map/ppermute | solution.py:372
  36.5 0.0 collective-permute-done.15.refs_12_
  36.5 0.0 collective-permute-done.16.refs_13_
  36.5 4.9 %columns.1 = (bf16[256,128]{1,0:T(8,128)(2,1)S(1)}, bf16[256,128]{1,0:T(8,128)(2,1)S(1)}, bf16[256,128]{1,0:T(8,128)(2,1)S(1)}, bf16[256,128]{1,0:T(8,128)(2,1)S(1)}) custom-call(bf16[272,128]{1,0:T(8,128)(2,1)S(1)} %get-tuple-element.47.refs_4_.refs_0_, bf16[272,128]{1,0:T(8,128)(2,1)S(1)} %collective-permute-done.refs_0_.refs_5_.refs_1_, ...), custom_call_target="tpu_custom_call" | custom-call | flops 3758096384 | bytes 3145728 | tf_op jit(solution)/shard_map/columns/pallas_call | solution.py:460
  41.4 0.8 %collective-permute-start.20 = (bf16[256,128]{1,0:T(8,128)(2,1)S(1)}, bf16[256,128]{1,0:T(8,128)(2,1)S(1)}, u32[]{:S(2)}, u32[]{:S(2)}) collective-permute-start(bf16[256,128]{1,0:T(8,128)(2,1)S(1)} %get-tuple-element.71), channel_id=1, source_target_pairs={{0,2},{2,0},{4,6},{6,4},{8,10},{10,8},{12,14},{14,12},{16,18},{18,... | collective-permute-start | bytes 196616 | tf_op jit(solution)/shard_map/ppermute | solution.py:367
  42.2 1.1 %collective-permute-start.21 = (bf16[256,128]{1,0:T(8,128)(2,1)S(1)}, bf16[256,128]{1,0:T(8,128)(2,1)S(1)}, u32[]{:S(2)}, u32[]{:S(2)}) collective-permute-start(bf16[256,128]{1,0:T(8,128)(2,1)S(1)} %get-tuple-element.72), channel_id=1, source_target_pairs={{0,4},{2,6},{4,0},{6,2},{8,12},{10,14},{12,8},{14,10},{16,20},{18,... | collective-permute-start | bytes 196616 | tf_op jit(solution)/shard_map/ppermute | solution.py:367
  43.3 0.6 %collective-permute-start.22 = (bf16[256,128]{1,0:T(8,128)(2,1)S(1)}, bf16[256,128]{1,0:T(8,128)(2,1)S(1)}, u32[]{:S(2)}, u32[]{:S(2)}) collective-permute-start(bf16[256,128]{1,0:T(8,128)(2,1)S(1)} %get-tuple-element.73), channel_id=1, source_target_pairs={{0,6},{2,4},{4,2},{6,0},{8,14},{10,12},{12,10},{14,8},{16,22},{18,... | collective-permute-start | bytes 196616 | tf_op jit(solution)/shard_map/ppermute | solution.py:367
  43.9 0.0 collective-permute-done.13.back_a
  43.9 0.0 collective-permute-done.14.back_b
  43.9 0.5 %merge.1 = (bf16[256,128]{1,0:T(8,128)(2,1)S(1)}, bf16[256,128]{1,0:T(8,128)(2,1)S(1)}, bf16[256,128]{1,0:T(8,128)(2,1)S(1)}, bf16[256,128]{1,0:T(8,128)(2,1)S(1)}) custom-call(bf16[3,288,128]{2,1,0:T(8,128)(2,1)S(1)} %collective-permute-done.13.back_a, bf16[3,288,128]{2,1,0:T(8,128)(2,1)S(1)} %collective-permute-done.14.back_b, ...), custom_call_target="tpu_custom_call" | custom-call | bytes 2097152 | tf_op jit(solution)/shard_map/merge/pallas_call | solution.py:471
  44.5 0.2 collective-permute-start.17
  44.7 1.1 %collective-permute-start.18 = (bf16[256,128]{1,0:T(8,128)(2,1)S(1)}, bf16[256,128]{1,0:T(8,128)(2,1)S(1)}, u32[]{:S(2)}, u32[]{:S(2)}) collective-permute-start(bf16[256,128]{1,0:T(8,128)(2,1)S(1)} %get-tuple-element.69), channel_id=1, source_target_pairs={{0,4},{2,6},{4,0},{6,2},{8,12},{10,14},{12,8},{14,10},{16,20},{18,... | collective-permute-start | bytes 196616 | tf_op jit(solution)/shard_map/ppermute | solution.py:367
  45.8 0.0 collective-permute-done.20.refs_1_
  45.8 0.9 %collective-permute-start.19 = (bf16[256,128]{1,0:T(8,128)(2,1)S(1)}, bf16[256,128]{1,0:T(8,128)(2,1)S(1)}, u32[]{:S(2)}, u32[]{:S(2)}) collective-permute-start(bf16[256,128]{1,0:T(8,128)(2,1)S(1)} %get-tuple-element.70), channel_id=1, source_target_pairs={{0,6},{2,4},{4,2},{6,0},{8,14},{10,12},{12,10},{14,8},{16,22},{18,... | collective-permute-start | bytes 196616 | tf_op jit(solution)/shard_map/ppermute | solution.py:367
  46.7 0.0 collective-permute-done.21.refs_2_
  46.7 1.0 %collective-permute-done.22.refs_3_ = bf16[256,128]{1,0:T(8,128)(2,1)S(1)} collective-permute-done((bf16[256,128]{1,0:T(8,128)(2,1)S(1)}, bf16[256,128]{1,0:T(8,128)(2,1)S(1)}, u32[]{:S(2)}, u32[]{:S(2)}) %collective-permute-start.22) | collective-permute-done | bytes 65568 | tf_op jit(solution)/shard_map/ppermute | solution.py:367
  47.7 0.7 %join.3 = bf16[256,512]{1,0:T(8,128)(2,1)} custom-call(bf16[256,128]{1,0:T(8,128)(2,1)S(1)} %get-tuple-element.66.refs_0_, bf16[256,128]{1,0:T(8,128)(2,1)S(1)} %collective-permute-done.20.refs_1_, bf16[256,128]{1,0:T(8,128)(2,1)S(1)} %collective-permute-done.21.refs_2_, bf16[256,128]{1,0:T(8,128)(2,1)S(1)} %collective-permute-done.22.refs_3_), custom_call_target="tpu_custom_call" | custom-call | bytes 524288 | tf_op jit(solution)/shard_map/join/pallas_call | solution.py:482
  48.4 0.0 collective-permute-done.17.refs_1_
  48.4 0.2 collective-permute-done.18.refs_2_
  48.6 1.8 %collective-permute-done.19.refs_3_ = bf16[256,128]{1,0:T(8,128)(2,1)S(1)} collective-permute-done((bf16[256,128]{1,0:T(8,128)(2,1)S(1)}, bf16[256,128]{1,0:T(8,128)(2,1)S(1)}, u32[]{:S(2)}, u32[]{:S(2)}) %collective-permute-start.19) | collective-permute-done | bytes 65568 | tf_op jit(solution)/shard_map/ppermute | solution.py:367
  50.4 0.7 %join.2 = bf16[256,512]{1,0:T(8,128)(2,1)} custom-call(bf16[256,128]{1,0:T(8,128)(2,1)S(1)} %get-tuple-element.67.refs_0_, bf16[256,128]{1,0:T(8,128)(2,1)S(1)} %collective-permute-done.17.refs_1_, bf16[256,128]{1,0:T(8,128)(2,1)S(1)} %collective-permute-done.18.refs_2_, bf16[256,128]{1,0:T(8,128)(2,1)S(1)} %collective-permute-done.19.refs_3_), custom_call_target="tpu_custom_call" | custom-call | bytes 524288 | tf_op jit(solution)/shard_map/join/pallas_call | solution.py:482
Async XLA Ops:
  0.6 9.5 %collective-permute-start.1 = (bf16[256,512]{1,0:T(8,128)(2,1)}, bf16[256,512]{1,0:T(8,128)(2,1)S(1)}, u32[]{:S(2)}, u32[]{:S(2)}) collective-permute-start(bf16[256,512]{1,0:T(8,128)(2,1)} %audio.3), channel_id=1, source_target_pairs={{0,1},{1,0},{2,3},{3,2},{4,5},{5,4},{6,7},{7,6},{8,9},{9,8},{10,11... | collective-permute-start | bytes 786440 | tf_op jit(solution)/shard_map/ppermute | solution.py:363
  1.9 11.8 %collective-permute-start.7 = (bf16[256,512]{1,0:T(8,128)(2,1)}, bf16[256,512]{1,0:T(8,128)(2,1)S(1)}, u32[]{:S(2)}, u32[]{:S(2)}) collective-permute-start(bf16[256,512]{1,0:T(8,128)(2,1)} %video.1), channel_id=1, source_target_pairs={{0,1},{1,0},{2,3},{3,2},{4,5},{5,4},{6,7},{7,6},{8,9},{9,8},{10,11... | collective-permute-start | bytes 786440 | tf_op jit(solution)/shard_map/ppermute | solution.py:363
  3.2 3.0 %collective-permute-start = (bf16[272,128]{1,0:T(8,128)(2,1)S(1)}, bf16[272,128]{1,0:T(8,128)(2,1)S(1)}, u32[]{:S(2)}, u32[]{:S(2)}) collective-permute-start(bf16[272,128]{1,0:T(8,128)(2,1)S(1)} %get-tuple-element.38), channel_id=1, source_target_pairs={{0,2},{2,0},{4,6},{6,4},{8,10},{10,8},{12,14},{14,12},{16,18},{18,... | collective-permute-start | bytes 208904 | tf_op jit(solution)/shard_map/ppermute | solution.py:367
  4.5 3.8 %collective-permute-start.2 = (bf16[272,128]{1,0:T(8,128)(2,1)S(1)}, bf16[272,128]{1,0:T(8,128)(2,1)S(1)}, u32[]{:S(2)}, u32[]{:S(2)}) collective-permute-start(bf16[272,128]{1,0:T(8,128)(2,1)S(1)} %get-tuple-element.41), channel_id=1, source_target_pairs={{0,4},{2,6},{4,0},{6,2},{8,12},{10,14},{12,8},{14,10},{16,20},{18,... | collective-permute-start | bytes 208904 | tf_op jit(solution)/shard_map/ppermute | solution.py:367
  5.7 4.5 %collective-permute-start.3 = (bf16[272,128]{1,0:T(8,128)(2,1)S(1)}, bf16[272,128]{1,0:T(8,128)(2,1)S(1)}, u32[]{:S(2)}, u32[]{:S(2)}) collective-permute-start(bf16[272,128]{1,0:T(8,128)(2,1)S(1)} %get-tuple-element.42), channel_id=1, source_target_pairs={{0,6},{2,4},{4,2},{6,0},{8,14},{10,12},{12,10},{14,8},{16,22},{18,... | collective-permute-start | bytes 208904 | tf_op jit(solution)/shard_map/ppermute | solution.py:367
  10.6 3.1 %collective-permute-start.4 = (bf16[256,128]{1,0:T(8,128)(2,1)S(1)}, bf16[256,128]{1,0:T(8,128)(2,1)S(1)}, u32[]{:S(2)}, u32[]{:S(2)}) collective-permute-start(bf16[256,128]{1,0:T(8,128)(2,1)S(1)} %get-tuple-element.44), channel_id=1, source_target_pairs={{0,2},{2,0},{4,6},{6,4},{8,10},{10,8},{12,14},{14,12},{16,18},{18,... | collective-permute-start | bytes 196616 | tf_op jit(solution)/shard_map/ppermute | solution.py:367
  11.2 3.7 %collective-permute-start.5 = (bf16[256,128]{1,0:T(8,128)(2,1)S(1)}, bf16[256,128]{1,0:T(8,128)(2,1)S(1)}, u32[]{:S(2)}, u32[]{:S(2)}) collective-permute-start(bf16[256,128]{1,0:T(8,128)(2,1)S(1)} %get-tuple-element.45), channel_id=1, source_target_pairs={{0,4},{2,6},{4,0},{6,2},{8,12},{10,14},{12,8},{14,10},{16,20},{18,... | collective-permute-start | bytes 196616 | tf_op jit(solution)/shard_map/ppermute | solution.py:367
  12.5 4.0 %collective-permute-start.6 = (bf16[256,128]{1,0:T(8,128)(2,1)S(1)}, bf16[256,128]{1,0:T(8,128)(2,1)S(1)}, u32[]{:S(2)}, u32[]{:S(2)}) collective-permute-start(bf16[256,128]{1,0:T(8,128)(2,1)S(1)} %get-tuple-element.46), channel_id=1, source_target_pairs={{0,6},{2,4},{4,2},{6,0},{8,14},{10,12},{12,10},{14,8},{16,22},{18,... | collective-permute-start | bytes 196616 | tf_op jit(solution)/shard_map/ppermute | solution.py:367
  16.9 5.7 %collective-permute-start.10 = (bf16[512,128]{1,0:T(8,128)(2,1)S(1)}, bf16[512,128]{1,0:T(8,128)(2,1)S(1)}, u32[]{:S(2)}, u32[]{:S(2)}) collective-permute-start(bf16[512,128]{1,0:T(8,128)(2,1)S(1)} %get-tuple-element.54), channel_id=1, source_target_pairs={{0,2},{2,0},{4,6},{6,4},{8,10},{10,8},{12,14},{14,12},{16,18},{18,... | collective-permute-start | bytes 393224 | tf_op jit(solution)/shard_map/ppermute | solution.py:367
  17.3 7.3 %collective-permute-start.11 = (bf16[512,128]{1,0:T(8,128)(2,1)S(1)}, bf16[512,128]{1,0:T(8,128)(2,1)S(1)}, u32[]{:S(2)}, u32[]{:S(2)}) collective-permute-start(bf16[512,128]{1,0:T(8,128)(2,1)S(1)} %get-tuple-element.55), channel_id=1, source_target_pairs={{0,4},{2,6},{4,0},{6,2},{8,12},{10,14},{12,8},{14,10},{16,20},{18,... | collective-permute-start | bytes 393224 | tf_op jit(solution)/shard_map/ppermute | solution.py:367
  18.4 7.3 %collective-permute-start.12 = (bf16[512,128]{1,0:T(8,128)(2,1)S(1)}, bf16[512,128]{1,0:T(8,128)(2,1)S(1)}, u32[]{:S(2)}, u32[]{:S(2)}) collective-permute-start(bf16[512,128]{1,0:T(8,128)(2,1)S(1)} %get-tuple-element.56), channel_id=1, source_target_pairs={{0,6},{2,4},{4,2},{6,0},{8,14},{10,12},{12,10},{14,8},{16,22},{18,... | collective-permute-start | bytes 393224 | tf_op jit(solution)/shard_map/ppermute | solution.py:367
  19.2 9.8 %collective-permute-start.8 = (bf16[3,272,128]{2,1,0:T(8,128)(2,1)S(1)}, bf16[3,272,128]{2,1,0:T(8,128)(2,1)S(1)}, u32[]{:S(2)}, u32[]{:S(2)}) collective-permute-start(bf16[3,272,128]{2,1,0:T(8,128)(2,1)S(1)} %get-tuple-element.52), channel_id=1, source_target_pairs={{8,16},{10,18},{12,20},{14,22},{16,8},{18,10},{20,12},{22,14},{9,1... | collective-permute-start | bytes 626696 | tf_op jit(solution)/shard_map/ppermute | solution.py:372
  22.4 6.6 %collective-permute-start.9 = (bf16[3,272,128]{2,1,0:T(8,128)(2,1)S(1)}, bf16[3,272,128]{2,1,0:T(8,128)(2,1)S(1)}, u32[]{:S(2)}, u32[]{:S(2)}) collective-permute-start(bf16[3,272,128]{2,1,0:T(8,128)(2,1)S(1)} %get-tuple-element.53), channel_id=1, source_target_pairs={{0,8},{2,10},{4,12},{6,14},{8,0},{10,2},{12,4},{14,6},{16,24},{18,... | collective-permute-start | bytes 626696 | tf_op jit(solution)/shard_map/ppermute | solution.py:372
  22.6 13.9 %collective-permute-start.15 = (bf16[3,256,128]{2,1,0:T(8,128)(2,1)S(1)}, bf16[3,256,128]{2,1,0:T(8,128)(2,1)S(1)}, u32[]{:S(2)}, u32[]{:S(2)}) collective-permute-start(bf16[3,256,128]{2,1,0:T(8,128)(2,1)S(1)} %get-tuple-element.63), channel_id=1, source_target_pairs={{8,16},{10,18},{12,20},{14,22},{16,8},{18,10},{20,12},{22,14},{9,1... | collective-permute-start | bytes 589832 | tf_op jit(solution)/shard_map/ppermute | solution.py:372
  24.7 11.8 %collective-permute-start.16 = (bf16[3,256,128]{2,1,0:T(8,128)(2,1)S(1)}, bf16[3,256,128]{2,1,0:T(8,128)(2,1)S(1)}, u32[]{:S(2)}, u32[]{:S(2)}) collective-permute-start(bf16[3,256,128]{2,1,0:T(8,128)(2,1)S(1)} %get-tuple-element.64), channel_id=1, source_target_pairs={{0,8},{2,10},{4,12},{6,14},{8,0},{10,2},{12,4},{14,6},{16,24},{18,... | collective-permute-start | bytes 589832 | tf_op jit(solution)/shard_map/ppermute | solution.py:372
  31.8 12.2 %collective-permute-start.13 = (bf16[3,288,128]{2,1,0:T(8,128)(2,1)S(1)}, bf16[3,288,128]{2,1,0:T(8,128)(2,1)S(1)}, u32[]{:S(2)}, u32[]{:S(2)}) collective-permute-start(bf16[3,288,128]{2,1,0:T(8,128)(2,1)S(1)} %get-tuple-element.59), channel_id=1, source_target_pairs={{0,8},{2,10},{4,12},{6,14},{8,0},{10,2},{12,4},{14,6},{16,24},{18,... | collective-permute-start | bytes 663560 | tf_op jit(solution)/shard_map/ppermute | solution.py:372
  32.4 11.6 %collective-permute-start.14 = (bf16[3,288,128]{2,1,0:T(8,128)(2,1)S(1)}, bf16[3,288,128]{2,1,0:T(8,128)(2,1)S(1)}, u32[]{:S(2)}, u32[]{:S(2)}) collective-permute-start(bf16[3,288,128]{2,1,0:T(8,128)(2,1)S(1)} %get-tuple-element.60), channel_id=1, source_target_pairs={{8,16},{10,18},{12,20},{14,22},{16,8},{18,10},{20,12},{22,14},{9,1... | collective-permute-start | bytes 663560 | tf_op jit(solution)/shard_map/ppermute | solution.py:372
  41.4 4.4 %collective-permute-start.20 = (bf16[256,128]{1,0:T(8,128)(2,1)S(1)}, bf16[256,128]{1,0:T(8,128)(2,1)S(1)}, u32[]{:S(2)}, u32[]{:S(2)}) collective-permute-start(bf16[256,128]{1,0:T(8,128)(2,1)S(1)} %get-tuple-element.71), channel_id=1, source_target_pairs={{0,2},{2,0},{4,6},{6,4},{8,10},{10,8},{12,14},{14,12},{16,18},{18,... | collective-permute-start | bytes 196616 | tf_op jit(solution)/shard_map/ppermute | solution.py:367
  42.2 4.5 %collective-permute-start.21 = (bf16[256,128]{1,0:T(8,128)(2,1)S(1)}, bf16[256,128]{1,0:T(8,128)(2,1)S(1)}, u32[]{:S(2)}, u32[]{:S(2)}) collective-permute-start(bf16[256,128]{1,0:T(8,128)(2,1)S(1)} %get-tuple-element.72), channel_id=1, source_target_pairs={{0,4},{2,6},{4,0},{6,2},{8,12},{10,14},{12,8},{14,10},{16,20},{18,... | collective-permute-start | bytes 196616 | tf_op jit(solution)/shard_map/ppermute | solution.py:367
  43.3 4.4 %collective-permute-start.22 = (bf16[256,128]{1,0:T(8,128)(2,1)S(1)}, bf16[256,128]{1,0:T(8,128)(2,1)S(1)}, u32[]{:S(2)}, u32[]{:S(2)}) collective-permute-start(bf16[256,128]{1,0:T(8,128)(2,1)S(1)} %get-tuple-element.73), channel_id=1, source_target_pairs={{0,6},{2,4},{4,2},{6,0},{8,14},{10,12},{12,10},{14,8},{16,22},{18,... | collective-permute-start | bytes 196616 | tf_op jit(solution)/shard_map/ppermute | solution.py:367
  44.5 4.0 %collective-permute-start.17 = (bf16[256,128]{1,0:T(8,128)(2,1)S(1)}, bf16[256,128]{1,0:T(8,128)(2,1)S(1)}, u32[]{:S(2)}, u32[]{:S(2)}) collective-permute-start(bf16[256,128]{1,0:T(8,128)(2,1)S(1)} %get-tuple-element.68), channel_id=1, source_target_pairs={{0,2},{2,0},{4,6},{6,4},{8,10},{10,8},{12,14},{14,12},{16,18},{18,... | collective-permute-start | bytes 196616 | tf_op jit(solution)/shard_map/ppermute | solution.py:367
  44.7 3.9 %collective-permute-start.18 = (bf16[256,128]{1,0:T(8,128)(2,1)S(1)}, bf16[256,128]{1,0:T(8,128)(2,1)S(1)}, u32[]{:S(2)}, u32[]{:S(2)}) collective-permute-start(bf16[256,128]{1,0:T(8,128)(2,1)S(1)} %get-tuple-element.69), channel_id=1, source_target_pairs={{0,4},{2,6},{4,0},{6,2},{8,12},{10,14},{12,8},{14,10},{16,20},{18,... | collective-permute-start | bytes 196616 | tf_op jit(solution)/shard_map/ppermute | solution.py:367
  45.8 4.6 %collective-permute-start.19 = (bf16[256,128]{1,0:T(8,128)(2,1)S(1)}, bf16[256,128]{1,0:T(8,128)(2,1)S(1)}, u32[]{:S(2)}, u32[]{:S(2)}) collective-permute-start(bf16[256,128]{1,0:T(8,128)(2,1)S(1)} %get-tuple-element.70), channel_id=1, source_target_pairs={{0,6},{2,4},{4,2},{6,0},{8,14},{10,12},{12,10},{14,8},{16,22},{18,... | collective-permute-start | bytes 196616 | tf_op jit(solution)/shard_map/ppermute | solution.py:367

commit v14 on v13

--- a/solution.py
+++ b/solution.py
@@ -105,7 +105,7 @@
         pieces[k][stream * rows :] = full[:, at]
 
 
-def halo_kernel(ids_at, *refs):
+def halo_kernel(at, ids_at, *refs):
     pieces, id_packs, outs = refs[:GROUP], refs[GROUP : 2 * GROUP], refs[-2:]
     rows = outs[0].shape[1] - (ID_ROWS if ids_at else 0)
     mine = place()
@@ -117,7 +117,7 @@
 
             @pl.when((spot >= 0) & (spot < RADIUS))
             def _():
-                out[spot, :rows] = pieces[k][:rows]
+                out[spot, :rows] = pieces[k][at : at + rows]
                 if ids_at:
                     out[spot, rows:] = id_packs[k][ids_at:]
 
@@ -198,14 +198,14 @@
 
 
 def rows_kernel(*refs):
-    audio, queries, video = refs[:GROUP], refs[GROUP : 2 * GROUP], refs[2 * GROUP : 3 * GROUP]
+    audio, queries, keys = refs[:GROUP], refs[GROUP : 2 * GROUP], refs[2 * GROUP : 3 * GROUP]
     peaks, sums, turned, beside, asks = refs[-5:]
-    rows, width = queries[0].shape
+    rows, width = keys[0].shape
     set_up(
         audio,
-        lambda k: queries[k][...],
-        lambda k: video[k][rows:],
-        lambda k: video[k][:rows],
+        lambda k: queries[k][rows:],
+        lambda k: keys[k][...],
+        lambda k: queries[k][:rows],
         turned,
         beside,
         asks,
@@ -264,42 +264,49 @@
     second[...] = results[odd]
 
 
-def columns_kernel(*refs):
-    audio, queries, video = refs[:GROUP], refs[GROUP : 2 * GROUP], refs[2 * GROUP : 3 * GROUP]
-    (edge_b, edge_a, edge_turned), outs = refs[3 * GROUP : 3 * GROUP + 3], refs[-GROUP - 5 : -5]
-    edge_beside, turned, beside, asks, whole = refs[-5:]
+def columns_kernel(receivers, *refs):
+    refs = list(refs)
+    take = lambda count: [refs.pop(0) for _ in range(count)]
+    first = 0 not in receivers
+    if first:
+        audio, queries, keys, (edge_b, edge_a) = take(GROUP), take(GROUP), take(GROUP), take(2)
+    (edge_turned,) = take(1)
+    if not first:
+        shared, _ = take(4), take(1)
+    outs = take(len(receivers))
+    turned, beside, asks, edge_beside = take(4) if first else shared
     rows, width = outs[0].shape
     mine = place()
-    odd = lax.rem(plane(), 2)
-    set_up(
-        audio,
-        lambda k: video[k][rows:],
-        lambda k: queries[k][...],
-        lambda k: audio[k][:rows],
-        turned,
-        beside,
-        asks,
-    )
-    edge_beside[:, width:] = jnp.ones((edge_beside.shape[0], width), beside.dtype)
-    for edge, base in ((edge_a, RADIUS * (1 - odd)), (edge_b, RADIUS * odd)):
-        for j in range(RADIUS):
-            at = pl.ds(pl.multiple_of((base + j) * rows, rows), rows)
-            edge_beside[at, :width] = edge[j]
-    near = [slice(b * rows, (b + RADIUS) * rows) for b in range(GROUP)]
-
-    def scores_of(b):
-        return [product(asks[b], turned[...]), product(asks[b], edge_turned[:, near[b]])]
+    if first:
+        odd = lax.rem(plane(), 2)
+        set_up(
+            audio,
+            lambda k: keys[k][...],
+            lambda k: queries[k][rows:],
+            lambda k: audio[k][:rows],
+            turned,
+            beside,
+            asks,
+        )
+        edge_beside[:, width:] = jnp.ones((edge_beside.shape[0], width), beside.dtype)
+        for edge, base in ((edge_a, RADIUS * (1 - odd)), (edge_b, RADIUS * odd)):
+            for j in range(RADIUS):
+                at = pl.ds(pl.multiple_of((base + j) * rows, rows), rows)
+                edge_beside[at, :width] = edge[j]
+    near = [pl.ds(pl.multiple_of((mine ^ k) * rows, rows), RADIUS * rows) for k in receivers]
+
+    def scores_of(n):
+        ask = asks[mine ^ receivers[n]]
+        return [product(ask, turned[...]), product(ask, edge_turned[:, near[n]])]
 
     ahead = scores_of(0)
-    for b in range(GROUP):
+    for n in range(len(receivers)):
         scores = ahead
-        if b + 1 < GROUP:
-            ahead = scores_of(b + 1)
-        _, mixed = attend(scores, [beside[...], edge_beside[near[b]]])
+        if n + 1 < len(receivers):
+            ahead = scores_of(n + 1)
+        _, mixed = attend(scores, [beside[...], edge_beside[near[n]]])
         mean = by_head(mixed[:, :width], rows) / by_head(mixed[:, width:], rows)
-        whole[b] = mean.astype(whole.dtype)
-    for k in range(GROUP):
-        outs[k][...] = whole[mine ^ k]
+        outs[n][...] = mean.astype(outs[n].dtype)
 
 
 def merge_kernel(back_a, back_b, peaks, sums, *refs):
@@ -415,10 +422,10 @@
             name="project",
         )(*operands, *stream, *after)
 
-    def halo(pieces, id_packs, *after):
+    def halo(at, pieces, id_packs, *after):
         edge = shape((RADIUS, rows + (ID_ROWS if id_packs else 0), width), bf16)
         sent = call(
-            functools.partial(halo_kernel, rows if id_packs else 0),
+            functools.partial(halo_kernel, at, rows if id_packs else 0),
             [edge, edge],
             ins=[VMEM] * (GROUP + len(id_packs)) + [ANY] * len(after),
             moved=10 * rows * width * 2,
@@ -426,12 +433,13 @@
         )(*pieces, *id_packs, *after)
         return [crossed(sent[i], i) for i in range(2)]
 
-    audio_edges = halo(packs, [])
-    queries = project(HEAD**-0.5, query_part, other_audio, query_rest, after=packs[1:])
+    queries = project(
+        HEAD**-0.5, query_part, other_audio, query_rest, stream=[video_copy], after=packs[1:]
+    )
     queries = traded(queries)
-    video = project(1.0, key_part, other_video, key_rest, stream=[video_copy], after=queries[1:])
-    query_edges = halo(queries, packs, video[0])
-    video = traded(video)
+    keys = project(1.0, key_part, other_video, key_rest, after=())
+    query_edges = halo(rows, queries, packs, keys[0])
+    keys = traded(keys)
 
     inside, around = GROUP * rows, 2 * RADIUS * rows
     turned, beside = shape((2 * width, inside), bf16), shape((inside, 2 * width), bf16)
@@ -444,7 +452,8 @@
         moved=8 * inside * width * 2,
         exps=2 * GROUP * rows * inside,
         name="rows",
-    )(*packs, *queries, *video)
+    )(*packs, *queries, *keys)
+    audio_edges = halo(0, packs, [], peaks)
     back = shape((RADIUS, rows + rows // width * STAT_ROWS, width), bf16)
     lent_a, lent_b, edge_turned = call(
         lend_kernel,
@@ -457,17 +466,17 @@
     )(*query_edges[::-1], plane_turned, plane_beside)
     backs = [crossed(x, i) for i, x in enumerate((lent_a, lent_b))]
 
-    video_pieces = call(
-        columns_kernel,
-        [piece] * GROUP,
-        [pltpu.VMEM((around, 2 * width), bf16)]
-        + [pltpu.VMEM(x.shape, bf16) for x in (turned, beside, asks)]
-        + [pltpu.VMEM((GROUP, rows, width), bf16)],
-        flops=112 * GROUP * rows * rows * width,
-        moved=8 * around * width * 2,
-        exps=14 * GROUP * rows * rows,
+    half_columns = dict(
+        flops=56 * GROUP * rows * rows * width,
+        moved=4 * around * width * 2,
+        exps=7 * GROUP * rows * rows,
         name="columns",
-    )(*packs, *queries, *video, *audio_edges[::-1], edge_turned)
+    )
+    shared = [turned, beside, asks, shape((around, 2 * width), bf16)]
+    near, far = range(GROUP // 2), range(GROUP // 2, GROUP)
+    *far_pieces, turned, beside, asks, edge_beside = call(
+        functools.partial(columns_kernel, far), [piece] * len(far) + shared, **half_columns
+    )(*packs, *queries, *keys, *audio_edges[::-1], edge_turned)
     audio_pieces = call(
         merge_kernel,
         [piece] * GROUP,
@@ -476,7 +485,15 @@
         exps=4 * inside * width,
         ins=[VMEM] * 4 + [ANY],
         name="merge",
-    )(*backs, peaks, sums, video_pieces[0])
+    )(*backs, peaks, sums, far_pieces[0])
+    audio_pieces = traded(audio_pieces)
+    near_pieces = call(
+        functools.partial(columns_kernel, near),
+        [piece] * len(near),
+        ins=[VMEM] * 5 + [ANY],
+        **half_columns,
+    )(edge_turned, turned, beside, asks, edge_beside, audio_pieces[0])
+    video_pieces = traded([*near_pieces, *far_pieces])
 
     def join(pieces):
         return call(
@@ -486,7 +503,7 @@
             outs_in=HBM,
             moved=2 * rows * half * 2,
             name="join",
-        )(*traded(pieces))
+        )(*pieces)
 
     video_attended = join(video_pieces)
     audio_attended = join(audio_pieces)

time: 51.5 us -> 50.5 us (0.981)
  waiting for transfers between devices: 9.66 us -> 7.45 us
  starting transfers between devices: 24 us -> 25.2 us
    ppermute x15, waiting for transfers between devices: 8.87 us -> 5.61 us  [traded(): lax.ppermute(pieces[k], 'tm', pairs(k))]
    ppermute x15, starting transfers between devices: 12.3 us -> 14.5 us  [traded(): lax.ppermute(pieces[k], 'tm', pairs(k))]
    ppermute x6, waiting for transfers between devices: 0.02 us -> 1.07 us  [crossed(): lax.ppermute(sent, 'tm', [(p * GROUP + i, q * GROUP + i) for p, q in pair...]
    ppermute x6, starting transfers between devices: 10.1 us -> 9.22 us  [crossed(): lax.ppermute(sent, 'tm', [(p * GROUP + i, q * GROUP + i) for p, q in pair...]
    pallas_call x3 -> x4, Pallas kernels: 5.05 us -> 5.05 us  [the longest x1 2.65 us: local(): call(functools.partial(columns_kernel, far), [piece] * len(far) + shared,...]
  transfers between devices with their start and end apart: 23 -> 23, of which waited for: 9 -> 6; matrix products, arithmetic and copies ran while one was open for 0% -> 0% of each run, Pallas kernels for 30% -> 32%
where the time goes in v14:
time: 50.5 us; the launch traced here: 50.2 us
  starting transfers between devices  25.2 us (50%)
  Pallas kernels  16.6 us (33%)
  waiting for transfers between devices  7.45 us (15%)
  between operations  1.01 us (2%)
    ppermute x15, starting transfers between devices, traded(): lax.ppermute(pieces[k], 'tm', pairs(k))  14.5 us
    ppermute x6, starting transfers between devices, crossed(): lax.ppermute(sent, 'tm', [(p * GROUP + i, q * GROUP + i) for p, q in pair...  9.22 us
    ppermute x15, waiting for transfers between devices, traded(): lax.ppermute(pieces[k], 'tm', pairs(k))  5.61 us
    pallas_call x1, Pallas kernels, local(): call(rows_kernel, [shape((GROUP, heads * rows, n * width), f32) for n in...  3.27 us
    pallas_call x1, Pallas kernels, local(): call(lend_kernel, [back, back, shape((2 * width, around), bf16)], [pltpu....  2.72 us
    pallas_call x1, Pallas kernels, local(): call(functools.partial(columns_kernel, far), [piece] * len(far) + shared,...  2.65 us
    pallas_call x1, Pallas kernels, local(): call(functools.partial(columns_kernel, near), [piece] * len(near), ins=[V...  2.26 us
    pallas_call x1, Pallas kernels, local(): call(prepare_kernel, [part, part, square, square, shape((rows, half), bf1...  1.78 us
  transfers between devices with their start and end apart: 23, of which 6 were waited for; matrix products, arithmetic and copies ran while one was open for 0% of the time, Pallas kernels for 32%

profile of v14, /device:TPU:9, one launch (start us, length us, event | category | flops | bytes accessed | tf_op | source)
XLA Modules:
  0.0 50.2 jit_solution(9942673858827676442)
XLA Ops:
  0.6 1.3 %collective-permute-start.1 = (bf16[256,512]{1,0:T(8,128)(2,1)}, bf16[256,512]{1,0:T(8,128)(2,1)S(1)}, u32[]{:S(2)}, u32[]{:S(2)}) collective-permute-start(bf16[256,512]{1,0:T(8,128)(2,1)} %audio.3), channel_id=1, source_target_pairs={{0,1},{1,0},{2,3},{3,2},{4,5},{5,4},{6,7},{7,6},{8,9},{9,8},{10,11... | collective-permute-start | bytes 786440 | tf_op jit(solution)/shard_map/ppermute | solution.py:370
  1.9 0.2 collective-permute-start.7
  2.2 1.0 %split.1 = (bf16[272,128]{1,0:T(8,128)(2,1)S(1)}, bf16[272,128]{1,0:T(8,128)(2,1)S(1)}, bf16[272,128]{1,0:T(8,128)(2,1)S(1)}, bf16[272,128]{1,0:T(8,128)(2,1)S(1)}) custom-call(bf16[256,512]{1,0:T(8,128)(2,1)} %audio.3, s32[2,128]{1,0:T(2,128)} %bitcast.1), custom_call_target="tpu_custom_call" | custom-call | bytes 524288 | tf_op jit(solution)/shard_map/split/pallas_call | solution.py:392
  3.2 1.3 %collective-permute-start = (bf16[272,128]{1,0:T(8,128)(2,1)S(1)}, bf16[272,128]{1,0:T(8,128)(2,1)S(1)}, u32[]{:S(2)}, u32[]{:S(2)}) collective-permute-start(bf16[272,128]{1,0:T(8,128)(2,1)S(1)} %get-tuple-element.42), channel_id=1, source_target_pairs={{0,2},{2,0},{4,6},{6,4},{8,10},{10,8},{12,14},{14,12},{16,18},{18,... | collective-permute-start | bytes 208904 | tf_op jit(solution)/shard_map/ppermute | solution.py:374
  4.5 1.2 %collective-permute-start.2 = (bf16[272,128]{1,0:T(8,128)(2,1)S(1)}, bf16[272,128]{1,0:T(8,128)(2,1)S(1)}, u32[]{:S(2)}, u32[]{:S(2)}) collective-permute-start(bf16[272,128]{1,0:T(8,128)(2,1)S(1)} %get-tuple-element.46), channel_id=1, source_target_pairs={{0,4},{2,6},{4,0},{6,2},{8,12},{10,14},{12,8},{14,10},{16,20},{18,... | collective-permute-start | bytes 208904 | tf_op jit(solution)/shard_map/ppermute | solution.py:374
  5.7 0.5 collective-permute-start.3
  6.2 0.0 collective-permute-done.refs_0_.refs_1_.refs_5_
  6.2 1.8 %prepare.1 = (f32[256,512]{1,0:T(8,128)S(1)}, f32[256,512]{1,0:T(8,128)S(1)}, bf16[512,512]{1,0:T(8,128)(2,1)S(1)}, bf16[512,512]{1,0:T(8,128)(2,1)S(1)}, bf16[256,512]{1,0:T(8,128)(2,1)S(1)}) custom-call(bf16[256,512]{1,0:T(8,128)(2,1)} %audio.3, bf16[256,512]{1,0:T(8,128)(2,1)} %video.1, bf16[1024,512]{1,0:T(8,128)(2,1)} %query.1, bf16[1024,512]{1,0:T(8,128)(2,1)} %key.1, ...), custom_call_target="tpu_custom_call" | custom-call | flops 268435456 | bytes 4194304 | tf_op jit(solution)/shard_map/prepare/pallas_call | solution.py:402
  8.0 0.3 collective-permute-done.2.refs_2_.refs_6_
  8.2 1.9 %collective-permute-done.3.refs_3_.refs_7_ = bf16[272,128]{1,0:T(8,128)(2,1)S(1)} collective-permute-done((bf16[272,128]{1,0:T(8,128)(2,1)S(1)}, bf16[272,128]{1,0:T(8,128)(2,1)S(1)}, u32[]{:S(2)}, u32[]{:S(2)}) %collective-permute-start.3) | collective-permute-done | bytes 69664 | tf_op jit(solution)/shard_map/ppermute | solution.py:374
  10.2 0.0 collective-permute-done.1.other
  10.2 0.4 project.2
  10.6 0.7 %collective-permute-start.4 = (bf16[512,128]{1,0:T(8,128)(2,1)S(1)}, bf16[512,128]{1,0:T(8,128)(2,1)S(1)}, u32[]{:S(2)}, u32[]{:S(2)}) collective-permute-start(bf16[512,128]{1,0:T(8,128)(2,1)S(1)} %get-tuple-element.49), channel_id=1, source_target_pairs={{0,2},{2,0},{4,6},{6,4},{8,10},{10,8},{12,14},{14,12},{16,18},{18,... | collective-permute-start | bytes 393224 | tf_op jit(solution)/shard_map/ppermute | solution.py:374
  11.2 1.2 %collective-permute-start.5 = (bf16[512,128]{1,0:T(8,128)(2,1)S(1)}, bf16[512,128]{1,0:T(8,128)(2,1)S(1)}, u32[]{:S(2)}, u32[]{:S(2)}) collective-permute-start(bf16[512,128]{1,0:T(8,128)(2,1)S(1)} %get-tuple-element.50), channel_id=1, source_target_pairs={{0,4},{2,6},{4,0},{6,2},{8,12},{10,14},{12,8},{14,10},{16,20},{18,... | collective-permute-start | bytes 393224 | tf_op jit(solution)/shard_map/ppermute | solution.py:374
  12.5 0.5 collective-permute-start.6
  12.9 0.8 %collective-permute-done.7.other = bf16[256,512]{1,0:T(8,128)(2,1)S(1)} collective-permute-done((bf16[256,512]{1,0:T(8,128)(2,1)}, bf16[256,512]{1,0:T(8,128)(2,1)S(1)}, u32[]{:S(2)}, u32[]{:S(2)}) %collective-permute-start.7) | collective-permute-done | bytes 262176 | tf_op jit(solution)/shard_map/ppermute | solution.py:370
  13.7 0.4 project.3
  14.1 1.6 %collective-permute-start.10 = (bf16[256,128]{1,0:T(8,128)(2,1)S(1)}, bf16[256,128]{1,0:T(8,128)(2,1)S(1)}, u32[]{:S(2)}, u32[]{:S(2)}) collective-permute-start(bf16[256,128]{1,0:T(8,128)(2,1)S(1)} %get-tuple-element.58), channel_id=1, source_target_pairs={{0,2},{2,0},{4,6},{6,4},{8,10},{10,8},{12,14},{14,12},{16,18},{18,... | collective-permute-start | bytes 196616 | tf_op jit(solution)/shard_map/ppermute | solution.py:374
  15.7 1.2 %collective-permute-start.11 = (bf16[256,128]{1,0:T(8,128)(2,1)S(1)}, bf16[256,128]{1,0:T(8,128)(2,1)S(1)}, u32[]{:S(2)}, u32[]{:S(2)}) collective-permute-start(bf16[256,128]{1,0:T(8,128)(2,1)S(1)} %get-tuple-element.59), channel_id=1, source_target_pairs={{0,4},{2,6},{4,0},{6,2},{8,12},{10,14},{12,8},{14,10},{16,20},{18,... | collective-permute-start | bytes 196616 | tf_op jit(solution)/shard_map/ppermute | solution.py:374
  16.9 0.0 collective-permute-done.4.refs_1_.refs_5_
  16.9 0.5 collective-permute-start.12
  17.4 0.0 collective-permute-done.5.refs_2_.refs_6_
  17.4 2.3 %collective-permute-done.6.refs_3_.refs_7_ = bf16[512,128]{1,0:T(8,128)(2,1)S(1)} collective-permute-done((bf16[512,128]{1,0:T(8,128)(2,1)S(1)}, bf16[512,128]{1,0:T(8,128)(2,1)S(1)}, u32[]{:S(2)}, u32[]{:S(2)}) %collective-permute-start.6) | collective-permute-done | bytes 131104 | tf_op jit(solution)/shard_map/ppermute | solution.py:374
  19.7 0.1 halo.2
  19.8 3.2 %collective-permute-start.8 = (bf16[3,272,128]{2,1,0:T(8,128)(2,1)S(1)}, bf16[3,272,128]{2,1,0:T(8,128)(2,1)S(1)}, u32[]{:S(2)}, u32[]{:S(2)}) collective-permute-start(bf16[3,272,128]{2,1,0:T(8,128)(2,1)S(1)} %get-tuple-element.56), channel_id=1, source_target_pairs={{8,16},{10,18},{12,20},{14,22},{16,8},{18,10},{20,12},{22,14},{9,1... | collective-permute-start | bytes 626696 | tf_op jit(solution)/shard_map/ppermute | solution.py:379
  23.0 0.1 collective-permute-start.9
  23.1 0.0 collective-permute-done.10.refs_9_
  23.1 0.0 collective-permute-done.11.refs_10_
  23.1 0.0 collective-permute-done.12.refs_11_
  23.1 3.3 %rows.1 = (f32[4,512,128]{2,1,0:T(8,128)S(1)}, f32[4,512,256]{2,1,0:T(8,128)S(1)}, bf16[256,1024]{1,0:T(8,128)(2,1)S(1)}, bf16[1024,256]{1,0:T(8,128)(2,1)S(1)}) custom-call(bf16[272,128]{1,0:T(8,128)(2,1)S(1)} %get-tuple-element.52.refs_4_.refs_0_, bf16[272,128]{1,0:T(8,128)(2,1)S(1)} %collective-permute-done.refs_0_.refs_1_.refs_5_, ...), custom_call_target="tpu_custom_call" | custom-call | flops 2147483648 | bytes 2097152 | tf_op jit(solution)/shard_map/rows/pallas_call | solution.py:447
  26.4 0.1 halo.3
  26.5 2.2 %collective-permute-start.15 = (bf16[3,256,128]{2,1,0:T(8,128)(2,1)S(1)}, bf16[3,256,128]{2,1,0:T(8,128)(2,1)S(1)}, u32[]{:S(2)}, u32[]{:S(2)}) collective-permute-start(bf16[3,256,128]{2,1,0:T(8,128)(2,1)S(1)} %get-tuple-element.67), channel_id=1, source_target_pairs={{8,16},{10,18},{12,20},{14,22},{16,8},{18,10},{20,12},{22,14},{9,1... | collective-permute-start | bytes 589832 | tf_op jit(solution)/shard_map/ppermute | solution.py:379
  28.7 0.1 collective-permute-start.16
  28.7 0.0 collective-permute-done.8.edge_b
  28.7 1.1 %collective-permute-done.9.edge_a = bf16[3,272,128]{2,1,0:T(8,128)(2,1)S(1)} collective-permute-done((bf16[3,272,128]{2,1,0:T(8,128)(2,1)S(1)}, bf16[3,272,128]{2,1,0:T(8,128)(2,1)S(1)}, u32[]{:S(2)}, u32[]{:S(2)}) %collective-permute-start.9) | collective-permute-done | bytes 208928 | tf_op jit(solution)/shard_map/ppermute | solution.py:379
  29.8 2.7 %lend.1 = (bf16[3,288,128]{2,1,0:T(8,128)(2,1)S(1)}, bf16[3,288,128]{2,1,0:T(8,128)(2,1)S(1)}, bf16[256,1536]{1,0:T(8,128)(2,1)S(1)}) custom-call(bf16[3,272,128]{2,1,0:T(8,128)(2,1)S(1)} %collective-permute-done.8.edge_b, bf16[3,272,128]{2,1,0:T(8,128)(2,1)S(1)} %collective-permute-done.9.edge_a, bf16[256,1024]{1,0:T(8,128)(2,1)S(1)} %get-tuple-element.61.plane_turned, ...), custom_call_target="tpu_custom_call" | custom-call | flops 4831838208 | bytes 3145728 | tf_op jit(solution)/shard_map/lend/pallas_call | solution.py:458
  32.5 0.4 collective-permute-start.13
  33.0 3.3 %collective-permute-start.14 = (bf16[3,288,128]{2,1,0:T(8,128)(2,1)S(1)}, bf16[3,288,128]{2,1,0:T(8,128)(2,1)S(1)}, u32[]{:S(2)}, u32[]{:S(2)}) collective-permute-start(bf16[3,288,128]{2,1,0:T(8,128)(2,1)S(1)} %get-tuple-element.64), channel_id=1, source_target_pairs={{8,16},{10,18},{12,20},{14,22},{16,8},{18,10},{20,12},{22,14},{9,1... | collective-permute-start | bytes 663560 | tf_op jit(solution)/shard_map/ppermute | solution.py:379
  36.2 0.0 collective-permute-done.15.refs_12_
  36.2 0.0 collective-permute-done.16.refs_13_
  36.3 2.6 %columns.2 = (bf16[256,128]{1,0:T(8,128)(2,1)S(1)}, bf16[256,128]{1,0:T(8,128)(2,1)S(1)}, bf16[256,1024]{1,0:T(8,128)(2,1)S(1)}, bf16[1024,256]{1,0:T(8,128)(2,1...) custom-call(bf16[272,128]{1,0:T(8,128)(2,1)S(1)} %get-tuple-element.52.refs_4_.refs_0_, ...), custom_call_target="tpu_custom_call" | custom-call | flops 1879048192 | bytes 1572864 | tf_op jit(solution)/shard_map/columns/pallas_call | solution.py:477
  38.9 2.4 %collective-permute-start.22 = (bf16[256,128]{1,0:T(8,128)(2,1)S(1)}, bf16[256,128]{1,0:T(8,128)(2,1)S(1)}, u32[]{:S(2)}, u32[]{:S(2)}) collective-permute-start(bf16[256,128]{1,0:T(8,128)(2,1)S(1)} %get-tuple-element.81), channel_id=1, source_target_pairs={{0,6},{2,4},{4,2},{6,0},{8,14},{10,12},{12,10},{14,8},{16,22},{18,... | collective-permute-start | bytes 196616 | tf_op jit(solution)/shard_map/ppermute | solution.py:374
  41.3 0.2 collective-permute-start.21
  41.5 0.0 collective-permute-done.13.back_a
  41.5 0.0 collective-permute-done.14.back_b
  41.5 0.5 %merge.1 = (bf16[256,128]{1,0:T(8,128)(2,1)S(1)}, bf16[256,128]{1,0:T(8,128)(2,1)S(1)}, bf16[256,128]{1,0:T(8,128)(2,1)S(1)}, bf16[256,128]{1,0:T(8,128)(2,1)S(1)}) custom-call(bf16[3,288,128]{2,1,0:T(8,128)(2,1)S(1)} %collective-permute-done.13.back_a, bf16[3,288,128]{2,1,0:T(8,128)(2,1)S(1)} %collective-permute-done.14.back_b, ...), custom_call_target="tpu_custom_call" | custom-call | bytes 2097152 | tf_op jit(solution)/shard_map/merge/pallas_call | solution.py:480
  42.1 1.2 %collective-permute-start.17 = (bf16[256,128]{1,0:T(8,128)(2,1)S(1)}, bf16[256,128]{1,0:T(8,128)(2,1)S(1)}, u32[]{:S(2)}, u32[]{:S(2)}) collective-permute-start(bf16[256,128]{1,0:T(8,128)(2,1)S(1)} %get-tuple-element.72), channel_id=1, source_target_pairs={{0,2},{2,0},{4,6},{6,4},{8,10},{10,8},{12,14},{14,12},{16,18},{18,... | collective-permute-start | bytes 196616 | tf_op jit(solution)/shard_map/ppermute | solution.py:374
  43.3 1.2 %collective-permute-start.18 = (bf16[256,128]{1,0:T(8,128)(2,1)S(1)}, bf16[256,128]{1,0:T(8,128)(2,1)S(1)}, u32[]{:S(2)}, u32[]{:S(2)}) collective-permute-start(bf16[256,128]{1,0:T(8,128)(2,1)S(1)} %get-tuple-element.73), channel_id=1, source_target_pairs={{0,4},{2,6},{4,0},{6,2},{8,12},{10,14},{12,8},{14,10},{16,20},{18,... | collective-permute-start | bytes 196616 | tf_op jit(solution)/shard_map/ppermute | solution.py:374
  44.5 0.5 collective-permute-start.19
  45.0 2.3 %columns.3 = (bf16[256,128]{1,0:T(8,128)(2,1)S(1)}, bf16[256,128]{1,0:T(8,128)(2,1)S(1)}) custom-call(bf16[256,1536]{1,0:T(8,128)(2,1)S(1)} %get-tuple-element.69.refs_14_.refs_0_, bf16[256,1024]{1,0:T(8,128)(2,1)S(1)} %get-tuple-element.75.refs_1_, bf16[1024,256]{1,0:T(8,128)(2,1)S(1)} %get-tuple-element.76.refs_2_, ...), custom_call_target="tpu_custom_call" | custom-call | flops 1879048192 | bytes 1572864 | tf_op jit(solution)/shard_map/columns/pallas_call | solution.py:490
  47.3 0.0 collective-permute-done.17.refs_1_
  47.3 0.2 collective-permute-start.20
  47.5 0.0 collective-permute-done.18.refs_2_
  47.5 1.1 %collective-permute-done.19.refs_3_ = bf16[256,128]{1,0:T(8,128)(2,1)S(1)} collective-permute-done((bf16[256,128]{1,0:T(8,128)(2,1)S(1)}, bf16[256,128]{1,0:T(8,128)(2,1)S(1)}, u32[]{:S(2)}, u32[]{:S(2)}) %collective-permute-start.19) | collective-permute-done | bytes 65568 | tf_op jit(solution)/shard_map/ppermute | solution.py:374
  48.6 0.7 %join.2 = bf16[256,512]{1,0:T(8,128)(2,1)} custom-call(bf16[256,128]{1,0:T(8,128)(2,1)S(1)} %get-tuple-element.71.refs_0_.refs_5_, bf16[256,128]{1,0:T(8,128)(2,1)S(1)} %collective-permute-done.17.refs_1_, bf16[256,128]{1,0:T(8,128)(2,1)S(1)} %collective-permute-done.18.refs_2_, bf16[256,128]{1,0:T(8,128)(2,1)S(1)} %collective-permute-done.19.refs_3_), custom_call_target="tpu_custom_call" | custom-call | bytes 524288 | tf_op jit(solution)/shard_map/join/pallas_call | solution.py:499
  49.3 0.0 collective-permute-done.22.refs_3_
  49.3 0.0 collective-permute-done.21.refs_2_
  49.3 0.0 collective-permute-done.20.refs_1_
  49.3 0.7 %join.3 = bf16[256,512]{1,0:T(8,128)(2,1)} custom-call(bf16[256,128]{1,0:T(8,128)(2,1)S(1)} %get-tuple-element.79.refs_0_, bf16[256,128]{1,0:T(8,128)(2,1)S(1)} %collective-permute-done.20.refs_1_, bf16[256,128]{1,0:T(8,128)(2,1)S(1)} %collective-permute-done.21.refs_2_, bf16[256,128]{1,0:T(8,128)(2,1)S(1)} %collective-permute-done.22.refs_3_), custom_call_target="tpu_custom_call" | custom-call | bytes 524288 | tf_op jit(solution)/shard_map/join/pallas_call | solution.py:499
Async XLA Ops:
  0.6 9.5 %collective-permute-start.1 = (bf16[256,512]{1,0:T(8,128)(2,1)}, bf16[256,512]{1,0:T(8,128)(2,1)S(1)}, u32[]{:S(2)}, u32[]{:S(2)}) collective-permute-start(bf16[256,512]{1,0:T(8,128)(2,1)} %audio.3), channel_id=1, source_target_pairs={{0,1},{1,0},{2,3},{3,2},{4,5},{5,4},{6,7},{7,6},{8,9},{9,8},{10,11... | collective-permute-start | bytes 786440 | tf_op jit(solution)/shard_map/ppermute | solution.py:370
  1.9 11.8 %collective-permute-start.7 = (bf16[256,512]{1,0:T(8,128)(2,1)}, bf16[256,512]{1,0:T(8,128)(2,1)S(1)}, u32[]{:S(2)}, u32[]{:S(2)}) collective-permute-start(bf16[256,512]{1,0:T(8,128)(2,1)} %video.1), channel_id=1, source_target_pairs={{0,1},{1,0},{2,3},{3,2},{4,5},{5,4},{6,7},{7,6},{8,9},{9,8},{10,11... | collective-permute-start | bytes 786440 | tf_op jit(solution)/shard_map/ppermute | solution.py:370
  3.2 3.0 %collective-permute-start = (bf16[272,128]{1,0:T(8,128)(2,1)S(1)}, bf16[272,128]{1,0:T(8,128)(2,1)S(1)}, u32[]{:S(2)}, u32[]{:S(2)}) collective-permute-start(bf16[272,128]{1,0:T(8,128)(2,1)S(1)} %get-tuple-element.42), channel_id=1, source_target_pairs={{0,2},{2,0},{4,6},{6,4},{8,10},{10,8},{12,14},{14,12},{16,18},{18,... | collective-permute-start | bytes 208904 | tf_op jit(solution)/shard_map/ppermute | solution.py:374
  4.5 3.8 %collective-permute-start.2 = (bf16[272,128]{1,0:T(8,128)(2,1)S(1)}, bf16[272,128]{1,0:T(8,128)(2,1)S(1)}, u32[]{:S(2)}, u32[]{:S(2)}) collective-permute-start(bf16[272,128]{1,0:T(8,128)(2,1)S(1)} %get-tuple-element.46), channel_id=1, source_target_pairs={{0,4},{2,6},{4,0},{6,2},{8,12},{10,14},{12,8},{14,10},{16,20},{18,... | collective-permute-start | bytes 208904 | tf_op jit(solution)/shard_map/ppermute | solution.py:374
  5.7 4.5 %collective-permute-start.3 = (bf16[272,128]{1,0:T(8,128)(2,1)S(1)}, bf16[272,128]{1,0:T(8,128)(2,1)S(1)}, u32[]{:S(2)}, u32[]{:S(2)}) collective-permute-start(bf16[272,128]{1,0:T(8,128)(2,1)S(1)} %get-tuple-element.47), channel_id=1, source_target_pairs={{0,6},{2,4},{4,2},{6,0},{8,14},{10,12},{12,10},{14,8},{16,22},{18,... | collective-permute-start | bytes 208904 | tf_op jit(solution)/shard_map/ppermute | solution.py:374
  10.6 6.4 %collective-permute-start.4 = (bf16[512,128]{1,0:T(8,128)(2,1)S(1)}, bf16[512,128]{1,0:T(8,128)(2,1)S(1)}, u32[]{:S(2)}, u32[]{:S(2)}) collective-permute-start(bf16[512,128]{1,0:T(8,128)(2,1)S(1)} %get-tuple-element.49), channel_id=1, source_target_pairs={{0,2},{2,0},{4,6},{6,4},{8,10},{10,8},{12,14},{14,12},{16,18},{18,... | collective-permute-start | bytes 393224 | tf_op jit(solution)/shard_map/ppermute | solution.py:374
  11.2 6.2 %collective-permute-start.5 = (bf16[512,128]{1,0:T(8,128)(2,1)S(1)}, bf16[512,128]{1,0:T(8,128)(2,1)S(1)}, u32[]{:S(2)}, u32[]{:S(2)}) collective-permute-start(bf16[512,128]{1,0:T(8,128)(2,1)S(1)} %get-tuple-element.50), channel_id=1, source_target_pairs={{0,4},{2,6},{4,0},{6,2},{8,12},{10,14},{12,8},{14,10},{16,20},{18,... | collective-permute-start | bytes 393224 | tf_op jit(solution)/shard_map/ppermute | solution.py:374
  12.5 7.3 %collective-permute-start.6 = (bf16[512,128]{1,0:T(8,128)(2,1)S(1)}, bf16[512,128]{1,0:T(8,128)(2,1)S(1)}, u32[]{:S(2)}, u32[]{:S(2)}) collective-permute-start(bf16[512,128]{1,0:T(8,128)(2,1)S(1)} %get-tuple-element.51), channel_id=1, source_target_pairs={{0,6},{2,4},{4,2},{6,0},{8,14},{10,12},{12,10},{14,8},{16,22},{18,... | collective-permute-start | bytes 393224 | tf_op jit(solution)/shard_map/ppermute | solution.py:374
  14.1 9.0 %collective-permute-start.10 = (bf16[256,128]{1,0:T(8,128)(2,1)S(1)}, bf16[256,128]{1,0:T(8,128)(2,1)S(1)}, u32[]{:S(2)}, u32[]{:S(2)}) collective-permute-start(bf16[256,128]{1,0:T(8,128)(2,1)S(1)} %get-tuple-element.58), channel_id=1, source_target_pairs={{0,2},{2,0},{4,6},{6,4},{8,10},{10,8},{12,14},{14,12},{16,18},{18,... | collective-permute-start | bytes 196616 | tf_op jit(solution)/shard_map/ppermute | solution.py:374
  15.7 7.4 %collective-permute-start.11 = (bf16[256,128]{1,0:T(8,128)(2,1)S(1)}, bf16[256,128]{1,0:T(8,128)(2,1)S(1)}, u32[]{:S(2)}, u32[]{:S(2)}) collective-permute-start(bf16[256,128]{1,0:T(8,128)(2,1)S(1)} %get-tuple-element.59), channel_id=1, source_target_pairs={{0,4},{2,6},{4,0},{6,2},{8,12},{10,14},{12,8},{14,10},{16,20},{18,... | collective-permute-start | bytes 196616 | tf_op jit(solution)/shard_map/ppermute | solution.py:374
  16.9 6.2 %collective-permute-start.12 = (bf16[256,128]{1,0:T(8,128)(2,1)S(1)}, bf16[256,128]{1,0:T(8,128)(2,1)S(1)}, u32[]{:S(2)}, u32[]{:S(2)}) collective-permute-start(bf16[256,128]{1,0:T(8,128)(2,1)S(1)} %get-tuple-element.60), channel_id=1, source_target_pairs={{0,6},{2,4},{4,2},{6,0},{8,14},{10,12},{12,10},{14,8},{16,22},{18,... | collective-permute-start | bytes 196616 | tf_op jit(solution)/shard_map/ppermute | solution.py:374
  19.8 8.9 %collective-permute-start.8 = (bf16[3,272,128]{2,1,0:T(8,128)(2,1)S(1)}, bf16[3,272,128]{2,1,0:T(8,128)(2,1)S(1)}, u32[]{:S(2)}, u32[]{:S(2)}) collective-permute-start(bf16[3,272,128]{2,1,0:T(8,128)(2,1)S(1)} %get-tuple-element.56), channel_id=1, source_target_pairs={{8,16},{10,18},{12,20},{14,22},{16,8},{18,10},{20,12},{22,14},{9,1... | collective-permute-start | bytes 626696 | tf_op jit(solution)/shard_map/ppermute | solution.py:379
  23.0 6.8 %collective-permute-start.9 = (bf16[3,272,128]{2,1,0:T(8,128)(2,1)S(1)}, bf16[3,272,128]{2,1,0:T(8,128)(2,1)S(1)}, u32[]{:S(2)}, u32[]{:S(2)}) collective-permute-start(bf16[3,272,128]{2,1,0:T(8,128)(2,1)S(1)} %get-tuple-element.57), channel_id=1, source_target_pairs={{0,8},{2,10},{4,12},{6,14},{8,0},{10,2},{12,4},{14,6},{16,24},{18,... | collective-permute-start | bytes 626696 | tf_op jit(solution)/shard_map/ppermute | solution.py:379
  26.5 9.8 %collective-permute-start.15 = (bf16[3,256,128]{2,1,0:T(8,128)(2,1)S(1)}, bf16[3,256,128]{2,1,0:T(8,128)(2,1)S(1)}, u32[]{:S(2)}, u32[]{:S(2)}) collective-permute-start(bf16[3,256,128]{2,1,0:T(8,128)(2,1)S(1)} %get-tuple-element.67), channel_id=1, source_target_pairs={{8,16},{10,18},{12,20},{14,22},{16,8},{18,10},{20,12},{22,14},{9,1... | collective-permute-start | bytes 589832 | tf_op jit(solution)/shard_map/ppermute | solution.py:379
  28.7 7.6 %collective-permute-start.16 = (bf16[3,256,128]{2,1,0:T(8,128)(2,1)S(1)}, bf16[3,256,128]{2,1,0:T(8,128)(2,1)S(1)}, u32[]{:S(2)}, u32[]{:S(2)}) collective-permute-start(bf16[3,256,128]{2,1,0:T(8,128)(2,1)S(1)} %get-tuple-element.68), channel_id=1, source_target_pairs={{0,8},{2,10},{4,12},{6,14},{8,0},{10,2},{12,4},{14,6},{16,24},{18,... | collective-permute-start | bytes 589832 | tf_op jit(solution)/shard_map/ppermute | solution.py:379
  32.5 9.0 %collective-permute-start.13 = (bf16[3,288,128]{2,1,0:T(8,128)(2,1)S(1)}, bf16[3,288,128]{2,1,0:T(8,128)(2,1)S(1)}, u32[]{:S(2)}, u32[]{:S(2)}) collective-permute-start(bf16[3,288,128]{2,1,0:T(8,128)(2,1)S(1)} %get-tuple-element.63), channel_id=1, source_target_pairs={{0,8},{2,10},{4,12},{6,14},{8,0},{10,2},{12,4},{14,6},{16,24},{18,... | collective-permute-start | bytes 663560 | tf_op jit(solution)/shard_map/ppermute | solution.py:379
  33.0 8.6 %collective-permute-start.14 = (bf16[3,288,128]{2,1,0:T(8,128)(2,1)S(1)}, bf16[3,288,128]{2,1,0:T(8,128)(2,1)S(1)}, u32[]{:S(2)}, u32[]{:S(2)}) collective-permute-start(bf16[3,288,128]{2,1,0:T(8,128)(2,1)S(1)} %get-tuple-element.64), channel_id=1, source_target_pairs={{8,16},{10,18},{12,20},{14,22},{16,8},{18,10},{20,12},{22,14},{9,1... | collective-permute-start | bytes 663560 | tf_op jit(solution)/shard_map/ppermute | solution.py:379
  38.9 10.4 %collective-permute-start.22 = (bf16[256,128]{1,0:T(8,128)(2,1)S(1)}, bf16[256,128]{1,0:T(8,128)(2,1)S(1)}, u32[]{:S(2)}, u32[]{:S(2)}) collective-permute-start(bf16[256,128]{1,0:T(8,128)(2,1)S(1)} %get-tuple-element.81), channel_id=1, source_target_pairs={{0,6},{2,4},{4,2},{6,0},{8,14},{10,12},{12,10},{14,8},{16,22},{18,... | collective-permute-start | bytes 196616 | tf_op jit(solution)/shard_map/ppermute | solution.py:374
  41.3 8.0 %collective-permute-start.21 = (bf16[256,128]{1,0:T(8,128)(2,1)S(1)}, bf16[256,128]{1,0:T(8,128)(2,1)S(1)}, u32[]{:S(2)}, u32[]{:S(2)}) collective-permute-start(bf16[256,128]{1,0:T(8,128)(2,1)S(1)} %get-tuple-element.70.refs_0_), channel_id=1, source_target_pairs={{0,4},{2,6},{4,0},{6,2},{8,12},{10,14},{12,8},{14,10},{16,20},{18,... | collective-permute-start | bytes 196616 | tf_op jit(solution)/shard_map/ppermute | solution.py:374
  42.1 5.2 %collective-permute-start.17 = (bf16[256,128]{1,0:T(8,128)(2,1)S(1)}, bf16[256,128]{1,0:T(8,128)(2,1)S(1)}, u32[]{:S(2)}, u32[]{:S(2)}) collective-permute-start(bf16[256,128]{1,0:T(8,128)(2,1)S(1)} %get-tuple-element.72), channel_id=1, source_target_pairs={{0,2},{2,0},{4,6},{6,4},{8,10},{10,8},{12,14},{14,12},{16,18},{18,... | collective-permute-start | bytes 196616 | tf_op jit(solution)/shard_map/ppermute | solution.py:374
  43.3 4.2 %collective-permute-start.18 = (bf16[256,128]{1,0:T(8,128)(2,1)S(1)}, bf16[256,128]{1,0:T(8,128)(2,1)S(1)}, u32[]{:S(2)}, u32[]{:S(2)}) collective-permute-start(bf16[256,128]{1,0:T(8,128)(2,1)S(1)} %get-tuple-element.73), channel_id=1, source_target_pairs={{0,4},{2,6},{4,0},{6,2},{8,12},{10,14},{12,8},{14,10},{16,20},{18,... | collective-permute-start | bytes 196616 | tf_op jit(solution)/shard_map/ppermute | solution.py:374
  44.5 4.0 %collective-permute-start.19 = (bf16[256,128]{1,0:T(8,128)(2,1)S(1)}, bf16[256,128]{1,0:T(8,128)(2,1)S(1)}, u32[]{:S(2)}, u32[]{:S(2)}) collective-permute-start(bf16[256,128]{1,0:T(8,128)(2,1)S(1)} %get-tuple-element.74), channel_id=1, source_target_pairs={{0,6},{2,4},{4,2},{6,0},{8,14},{10,12},{12,10},{14,8},{16,22},{18,... | collective-permute-start | bytes 196616 | tf_op jit(solution)/shard_map/ppermute | solution.py:374
  47.3 2.1 %collective-permute-start.20 = (bf16[256,128]{1,0:T(8,128)(2,1)S(1)}, bf16[256,128]{1,0:T(8,128)(2,1)S(1)}, u32[]{:S(2)}, u32[]{:S(2)}) collective-permute-start(bf16[256,128]{1,0:T(8,128)(2,1)S(1)} %get-tuple-element.80), channel_id=1, source_target_pairs={{0,2},{2,0},{4,6},{6,4},{8,10},{10,8},{12,14},{14,12},{16,18},{18,... | collective-permute-start | bytes 196616 | tf_op jit(solution)/shard_map/ppermute | solution.py:374

commit v15 on v14

--- a/solution.py
+++ b/solution.py
@@ -54,7 +54,7 @@
     return copies, fetch
 
 
-def split_kernel(audio, ids, *refs):
+def split_kernel(audio, video, ids, *refs):
     packs, (ids_in, ids_wide, sems) = refs[:GROUP], refs[GROUP:]
     rows, width = audio.shape[0], packs[0].shape[1]
     mine = place()
@@ -62,23 +62,23 @@
     fetch(ids, ids_in)
     for k in range(GROUP):
         at = pl.ds(pl.multiple_of((mine ^ k) * width, width), width)
-        fetch(audio.at[:, at], packs[k].at[:rows])
+        for i, stream in enumerate((audio, video)):
+            fetch(stream.at[:, at], packs[k].at[i * rows : (i + 1) * rows])
     copies[0].wait()
     ids_wide[...] = jnp.zeros_like(ids_wide)
     ids_wide[: ids_in.shape[0]] = (ids_in[...] + 1).astype(jnp.float32)
     for k in range(GROUP):
-        packs[k][rows:] = ids_wide[...].astype(packs[k].dtype)
+        packs[k][2 * rows :] = ids_wide[...].astype(packs[k].dtype)
     for copy in copies[1:]:
         copy.wait()
 
 
 def prepare_kernel(audio, video, query, key, *refs):
-    sums, seconds, sent, own, firsts, sems = refs[-9:-7], refs[-7:-5], refs[-5], refs[-4], refs[-3:-1], refs[-1]
+    sums, seconds, streams, firsts, sems = refs[-9:-7], refs[-7:-5], refs[-5:-3], refs[-3:-1], refs[-1]
     half = audio.shape[1]
     side = lax.axis_index("head")
     ours = pl.ds(pl.multiple_of(side * half, half), half)
     theirs = pl.ds(pl.multiple_of((1 - side) * half, half), half)
-    streams = (own, sent)
     copies, fetch = fetcher(sems)
     for i, (stream, weight) in enumerate(((audio, query), (video, key))):
         fetch(stream, streams[i])
@@ -93,19 +93,16 @@
         copy.wait()
 
 
-def project_kernel(scale, stream, part, other, weight, *refs):
+def project_kernel(scale, part, other, weight, *refs):
     pieces, full = refs[-GROUP - 1 : -1], refs[-1]
-    rows, width = other.shape[0], pieces[0].shape[1]
+    width = pieces[0].shape[1]
     mine = place()
     full[...] = (part[...] + product(other[...], weight[...])).astype(jnp.bfloat16) * jnp.bfloat16(scale)
     for k in range(GROUP):
-        at = pl.ds(pl.multiple_of((mine ^ k) * width, width), width)
-        if stream:
-            pieces[k][:rows] = refs[0][:, at]
-        pieces[k][stream * rows :] = full[:, at]
-
-
-def halo_kernel(at, ids_at, *refs):
+        pieces[k][...] = full[:, pl.ds(pl.multiple_of((mine ^ k) * width, width), width)]
+
+
+def halo_kernel(ids_at, *refs):
     pieces, id_packs, outs = refs[:GROUP], refs[GROUP : 2 * GROUP], refs[-2:]
     rows = outs[0].shape[1] - (ID_ROWS if ids_at else 0)
     mine = place()
@@ -117,7 +114,7 @@
 
             @pl.when((spot >= 0) & (spot < RADIUS))
             def _():
-                out[spot, :rows] = pieces[k][at : at + rows]
+                out[spot, :rows] = pieces[k][:rows]
                 if ids_at:
                     out[spot, rows:] = id_packs[k][ids_at:]
 
@@ -177,7 +174,7 @@
     return peak, mixed
 
 
-def set_up(audio, asked, keys, values, turned, beside, asks):
+def set_up(packs, asked, keys, values, turned, beside, asks):
     rows, width = asks.shape[1] // 2, asks.shape[2] // 2
     mine = place()
     beside[:, width:] = jnp.ones((GROUP * rows, width), beside.dtype)
@@ -187,7 +184,7 @@
         def spot(at, size):
             return pl.ds(pl.multiple_of(b * rows + at, size), size)
 
-        marks = marks_turned(audio[k][rows:])
+        marks = marks_turned(packs[k][2 * rows :])
         asks[b] = stacked_ask(asked(k), marks)
         beside[spot(0, rows), :width] = values(k)
         key = keys(k)
@@ -198,14 +195,14 @@
 
 
 def rows_kernel(*refs):
-    audio, queries, keys = refs[:GROUP], refs[GROUP : 2 * GROUP], refs[2 * GROUP : 3 * GROUP]
+    packs, queries, keys = refs[:GROUP], refs[GROUP : 2 * GROUP], refs[2 * GROUP : 3 * GROUP]
     peaks, sums, turned, beside, asks = refs[-5:]
     rows, width = keys[0].shape
     set_up(
-        audio,
-        lambda k: queries[k][rows:],
+        packs,
+        lambda k: queries[k][...],
         lambda k: keys[k][...],
-        lambda k: queries[k][:rows],
+        lambda k: packs[k][rows : 2 * rows],
         turned,
         beside,
         asks,
@@ -269,7 +266,7 @@
     take = lambda count: [refs.pop(0) for _ in range(count)]
     first = 0 not in receivers
     if first:
-        audio, queries, keys, (edge_b, edge_a) = take(GROUP), take(GROUP), take(GROUP), take(2)
+        packs, queries, keys, (edge_b, edge_a) = take(GROUP), take(GROUP), take(GROUP), take(2)
     (edge_turned,) = take(1)
     if not first:
         shared, _ = take(4), take(1)
@@ -280,10 +277,10 @@
     if first:
         odd = lax.rem(plane(), 2)
         set_up(
-            audio,
+            packs,
             lambda k: keys[k][...],
-            lambda k: queries[k][rows:],
-            lambda k: audio[k][:rows],
+            lambda k: queries[k][...],
+            lambda k: packs[k][:rows],
             turned,
             beside,
             asks,
@@ -391,18 +388,18 @@
     other_video = swapped(video_frames)
     packs = call(
         split_kernel,
-        [shape((rows + ID_ROWS, width), bf16)] * GROUP,
+        [shape((2 * rows + ID_ROWS, width), bf16)] * GROUP,
         [pltpu.VMEM((rows // width, width), jnp.int32), pltpu.VMEM((ID_ROWS, width), f32)]
-        + [pltpu.SemaphoreType.DMA((1 + GROUP,))],
-        ins=[HBM] * 2,
-        moved=4 * rows * half,
+        + [pltpu.SemaphoreType.DMA((1 + 2 * GROUP,))],
+        ins=[HBM] * 3,
+        moved=8 * rows * half,
         name="split",
-    )(audio_in, ids_in)
+    )(audio_in, video_in, ids_in)
     packs = traded(packs)
-    query_part, key_part, query_rest, key_rest, video_copy = call(
+    query_part, key_part, query_rest, key_rest = call(
         prepare_kernel,
-        [part, part, square, square, shape((rows, half), bf16)],
-        [pltpu.VMEM((rows, half), bf16)]
+        [part, part, square, square],
+        [pltpu.VMEM((rows, half), bf16)] * 2
         + [pltpu.VMEM((half, half), bf16)] * 2
         + [pltpu.SemaphoreType.DMA((6,))],
         ins=[HBM] * 4 + [ANY],
@@ -411,21 +408,21 @@
         name="prepare",
     )(audio_in, video_in, query_in, key_in, packs[1])
 
-    def project(scale, *operands, stream=(), after=()):
+    def project(scale, *operands, after=()):
         return call(
-            functools.partial(project_kernel, scale, len(stream)),
-            [shape(((1 + len(stream)) * rows, width), bf16)] * GROUP,
+            functools.partial(project_kernel, scale),
+            [piece] * GROUP,
             [pltpu.VMEM((rows, half), bf16)],
-            ins=[VMEM] * (3 + len(stream)) + [ANY] * len(after),
+            ins=[VMEM] * 3 + [ANY] * len(after),
             flops=2 * rows * half * half,
             moved=2 * half * half + 6 * rows * half * 2,
             name="project",
-        )(*operands, *stream, *after)
-
-    def halo(at, pieces, id_packs, *after):
+        )(*operands, *after)
+
+    def halo(pieces, id_packs, *after):
         edge = shape((RADIUS, rows + (ID_ROWS if id_packs else 0), width), bf16)
         sent = call(
-            functools.partial(halo_kernel, at, rows if id_packs else 0),
+            functools.partial(halo_kernel, 2 * rows if id_packs else 0),
             [edge, edge],
             ins=[VMEM] * (GROUP + len(id_packs)) + [ANY] * len(after),
             moved=10 * rows * width * 2,
@@ -433,12 +430,9 @@
         )(*pieces, *id_packs, *after)
         return [crossed(sent[i], i) for i in range(2)]
 
-    queries = project(
-        HEAD**-0.5, query_part, other_audio, query_rest, stream=[video_copy], after=packs[1:]
-    )
-    queries = traded(queries)
+    queries = traded(project(HEAD**-0.5, query_part, other_audio, query_rest, after=packs[1:3]))
     keys = project(1.0, key_part, other_video, key_rest, after=())
-    query_edges = halo(rows, queries, packs, keys[0])
+    query_edges = halo(queries, packs, keys[0])
     keys = traded(keys)
 
     inside, around = GROUP * rows, 2 * RADIUS * rows
@@ -453,7 +447,7 @@
         exps=2 * GROUP * rows * inside,
         name="rows",
     )(*packs, *queries, *keys)
-    audio_edges = halo(0, packs, [], peaks)
+    audio_edges = halo(packs, [], peaks)
     back = shape((RADIUS, rows + rows // width * STAT_ROWS, width), bf16)
     lent_a, lent_b, edge_turned = call(
         lend_kernel,

time: 50.5 us -> 49.2 us (0.974)
  waiting for transfers between devices: 7.45 us -> 3.34 us
  starting transfers between devices: 25.2 us -> 28 us
    ppermute x15, waiting for transfers between devices: 5.61 us -> 2.89 us  [traded(): lax.ppermute(pieces[k], 'tm', pairs(k))]
    ppermute x15, starting transfers between devices: 14.5 us -> 16.2 us  [traded(): lax.ppermute(pieces[k], 'tm', pairs(k))]
    ppermute x6, waiting for transfers between devices: 1.07 us -> 0.02 us  [crossed(): lax.ppermute(sent, 'tm', [(p * GROUP + i, q * GROUP + i) for p, q in pair...]
    ppermute x6, starting transfers between devices: 9.22 us -> 10.3 us  [crossed(): lax.ppermute(sent, 'tm', [(p * GROUP + i, q * GROUP + i) for p, q in pair...]
  transfers between devices with their start and end apart: 23 -> 23, of which waited for: 6 -> 4; matrix products, arithmetic and copies ran while one was open for 0% -> 0% of each run, Pallas kernels for 32% -> 32%
where the time goes in v15:
time: 49.2 us; the launch traced here: 48.9 us
  starting transfers between devices  28 us (57%)
  Pallas kernels  16.6 us (34%)
  waiting for transfers between devices  3.34 us (7%)
  between operations  1.01 us (2%)
    ppermute x15, starting transfers between devices, traded(): lax.ppermute(pieces[k], 'tm', pairs(k))  16.2 us
    ppermute x6, starting transfers between devices, crossed(): lax.ppermute(sent, 'tm', [(p * GROUP + i, q * GROUP + i) for p, q in pair...  10.3 us
    pallas_call x1, Pallas kernels, local(): call(rows_kernel, [shape((GROUP, heads * rows, n * width), f32) for n in...  3.17 us
    ppermute x15, waiting for transfers between devices, traded(): lax.ppermute(pieces[k], 'tm', pairs(k))  2.89 us
    pallas_call x1, Pallas kernels, local(): call(functools.partial(columns_kernel, far), [piece] * len(far) + shared,...  2.65 us
    pallas_call x1, Pallas kernels, local(): call(lend_kernel, [back, back, shape((2 * width, around), bf16)], [pltpu....  2.62 us
    pallas_call x1, Pallas kernels, local(): call(functools.partial(columns_kernel, near), [piece] * len(near), ins=[V...  2.26 us
    pallas_call x1, Pallas kernels, local(): call(prepare_kernel, [part, part, square, square], [pltpu.VMEM((rows, hal...  1.78 us
  transfers between devices with their start and end apart: 23, of which 4 were waited for; matrix products, arithmetic and copies ran while one was open for 0% of the time, Pallas kernels for 32%

profile of v15, /device:TPU:9, one launch (start us, length us, event | category | flops | bytes accessed | tf_op | source)
XLA Modules:
  0.0 48.9 jit_solution(14073769148550068299)
XLA Ops:
  0.6 1.3 %collective-permute-start.1 = (bf16[256,512]{1,0:T(8,128)(2,1)}, bf16[256,512]{1,0:T(8,128)(2,1)S(1)}, u32[]{:S(2)}, u32[]{:S(2)}) collective-permute-start(bf16[256,512]{1,0:T(8,128)(2,1)} %audio.3), channel_id=1, source_target_pairs={{0,1},{1,0},{2,3},{3,2},{4,5},{5,4},{6,7},{7,6},{8,9},{9,8},{10,11... | collective-permute-start | bytes 786440 | tf_op jit(solution)/shard_map/ppermute | solution.py:367
  1.9 0.2 collective-permute-start.7
  2.2 1.2 %split.1 = (bf16[528,128]{1,0:T(8,128)(2,1)S(1)}, bf16[528,128]{1,0:T(8,128)(2,1)S(1)}, bf16[528,128]{1,0:T(8,128)(2,1)S(1)}, bf16[528,128]{1,0:T(8,128)(2,1)S(1)}) custom-call(bf16[256,512]{1,0:T(8,128)(2,1)} %audio.3, bf16[256,512]{1,0:T(8,128)(2,1)} %video.3, s32[2,128]{1,0:T(2,128)} %bitcast.1), custom_call_target="tpu_custom_call" | custom-call | bytes 1048576 | tf_op jit(solution)/shard_map/split/pallas_call | solution.py:389
  3.3 1.3 %collective-permute-start = (bf16[528,128]{1,0:T(8,128)(2,1)S(1)}, bf16[528,128]{1,0:T(8,128)(2,1)S(1)}, u32[]{:S(2)}, u32[]{:S(2)}) collective-permute-start(bf16[528,128]{1,0:T(8,128)(2,1)S(1)} %get-tuple-element.41), channel_id=1, source_target_pairs={{0,2},{2,0},{4,6},{6,4},{8,10},{10,8},{12,14},{14,12},{16,18},{18,... | collective-permute-start | bytes 405512 | tf_op jit(solution)/shard_map/ppermute | solution.py:371
  4.6 1.2 %collective-permute-start.2 = (bf16[528,128]{1,0:T(8,128)(2,1)S(1)}, bf16[528,128]{1,0:T(8,128)(2,1)S(1)}, u32[]{:S(2)}, u32[]{:S(2)}) collective-permute-start(bf16[528,128]{1,0:T(8,128)(2,1)S(1)} %get-tuple-element.44), channel_id=1, source_target_pairs={{0,4},{2,6},{4,0},{6,2},{8,12},{10,14},{12,8},{14,10},{16,20},{18,... | collective-permute-start | bytes 405512 | tf_op jit(solution)/shard_map/ppermute | solution.py:371
  5.9 0.5 collective-permute-start.6
  6.3 0.0 collective-permute-done.refs_0_.refs_5_.refs_1_
  6.3 1.8 %prepare.1 = (f32[256,512]{1,0:T(8,128)S(1)}, f32[256,512]{1,0:T(8,128)S(1)}, bf16[512,512]{1,0:T(8,128)(2,1)S(1)}, bf16[512,512]{1,0:T(8,128)(2,1)S(1)}) custom-call(bf16[256,512]{1,0:T(8,128)(2,1)} %audio.3, bf16[256,512]{1,0:T(8,128)(2,1)} %video.3, bf16[1024,512]{1,0:T(8,128)(2,1)} %query.1, bf16[1024,512]{1,0:T(8,128)(2,1)} %key.1, ...), custom_call_target="tpu_custom_call" | custom-call | flops 268435456 | bytes 4194304 | tf_op jit(solution)/shard_map/prepare/pallas_call | solution.py:399
  8.1 1.7 %collective-permute-done.2.refs_1_.refs_6_.refs_2_ = bf16[528,128]{1,0:T(8,128)(2,1)S(1)} collective-permute-done((bf16[528,128]{1,0:T(8,128)(2,1)S(1)}, bf16[528,128]{1,0:T(8,128)(2,1)S(1)}, u32[]{:S(2)}, u32[]{:S(2)}) %collective-permute-start.2) | collective-permute-done | bytes 135200 | tf_op jit(solution)/shard_map/ppermute | solution.py:371
  9.8 0.0 collective-permute-done.1.other
  9.8 0.4 project.2
  10.2 1.4 %collective-permute-start.3 = (bf16[256,128]{1,0:T(8,128)(2,1)S(1)}, bf16[256,128]{1,0:T(8,128)(2,1)S(1)}, u32[]{:S(2)}, u32[]{:S(2)}) collective-permute-start(bf16[256,128]{1,0:T(8,128)(2,1)S(1)} %get-tuple-element.46), channel_id=1, source_target_pairs={{0,2},{2,0},{4,6},{6,4},{8,10},{10,8},{12,14},{14,12},{16,18},{18,... | collective-permute-start | bytes 196616 | tf_op jit(solution)/shard_map/ppermute | solution.py:371
  11.6 1.2 %collective-permute-start.4 = (bf16[256,128]{1,0:T(8,128)(2,1)S(1)}, bf16[256,128]{1,0:T(8,128)(2,1)S(1)}, u32[]{:S(2)}, u32[]{:S(2)}) collective-permute-start(bf16[256,128]{1,0:T(8,128)(2,1)S(1)} %get-tuple-element.47), channel_id=1, source_target_pairs={{0,4},{2,6},{4,0},{6,2},{8,12},{10,14},{12,8},{14,10},{16,20},{18,... | collective-permute-start | bytes 196616 | tf_op jit(solution)/shard_map/ppermute | solution.py:371
  12.8 0.5 collective-permute-start.5
  13.3 0.4 collective-permute-done.7.other
  13.7 0.4 project.3
  14.1 1.6 %collective-permute-start.10 = (bf16[256,128]{1,0:T(8,128)(2,1)S(1)}, bf16[256,128]{1,0:T(8,128)(2,1)S(1)}, u32[]{:S(2)}, u32[]{:S(2)}) collective-permute-start(bf16[256,128]{1,0:T(8,128)(2,1)S(1)} %get-tuple-element.56), channel_id=1, source_target_pairs={{0,2},{2,0},{4,6},{6,4},{8,10},{10,8},{12,14},{14,12},{16,18},{18,... | collective-permute-start | bytes 196616 | tf_op jit(solution)/shard_map/ppermute | solution.py:371
  15.7 0.0 collective-permute-done.6.refs_7_.refs_3_
  15.7 1.2 %collective-permute-start.11 = (bf16[256,128]{1,0:T(8,128)(2,1)S(1)}, bf16[256,128]{1,0:T(8,128)(2,1)S(1)}, u32[]{:S(2)}, u32[]{:S(2)}) collective-permute-start(bf16[256,128]{1,0:T(8,128)(2,1)S(1)} %get-tuple-element.57), channel_id=1, source_target_pairs={{0,4},{2,6},{4,0},{6,2},{8,12},{10,14},{12,8},{14,10},{16,20},{18,... | collective-permute-start | bytes 196616 | tf_op jit(solution)/shard_map/ppermute | solution.py:371
  16.9 0.0 collective-permute-done.3.refs_1_.refs_5_
  16.9 0.5 collective-permute-start.12
  17.4 0.0 collective-permute-done.4.refs_2_.refs_6_
  17.4 0.0 collective-permute-done.5.refs_3_.refs_7_
  17.4 0.1 halo.2
  17.5 3.2 %collective-permute-start.8 = (bf16[3,272,128]{2,1,0:T(8,128)(2,1)S(1)}, bf16[3,272,128]{2,1,0:T(8,128)(2,1)S(1)}, u32[]{:S(2)}, u32[]{:S(2)}) collective-permute-start(bf16[3,272,128]{2,1,0:T(8,128)(2,1)S(1)} %get-tuple-element.54), channel_id=1, source_target_pairs={{8,16},{10,18},{12,20},{14,22},{16,8},{18,10},{20,12},{22,14},{9,1... | collective-permute-start | bytes 626696 | tf_op jit(solution)/shard_map/ppermute | solution.py:376
  20.7 0.1 collective-permute-start.9
  20.8 0.0 collective-permute-done.10.refs_9_
  20.8 0.0 collective-permute-done.11.refs_10_
  20.8 0.2 collective-permute-done.12.refs_11_
  21.0 3.2 %rows.1 = (f32[4,512,128]{2,1,0:T(8,128)S(1)}, f32[4,512,256]{2,1,0:T(8,128)S(1)}, bf16[256,1024]{1,0:T(8,128)(2,1)S(1)}, bf16[1024,256]{1,0:T(8,128)(2,1)S(1)}) custom-call(bf16[528,128]{1,0:T(8,128)(2,1)S(1)} %get-tuple-element.49.refs_4_.refs_0_, bf16[528,128]{1,0:T(8,128)(2,1)S(1)} %collective-permute-done.refs_0_.refs_5_.refs_1_, ...), custom_call_target="tpu_custom_call" | custom-call | flops 2147483648 | bytes 2097152 | tf_op jit(solution)/shard_map/rows/pallas_call | solution.py:441
  24.2 0.1 halo.3
  24.2 3.2 %collective-permute-start.15 = (bf16[3,256,128]{2,1,0:T(8,128)(2,1)S(1)}, bf16[3,256,128]{2,1,0:T(8,128)(2,1)S(1)}, u32[]{:S(2)}, u32[]{:S(2)}) collective-permute-start(bf16[3,256,128]{2,1,0:T(8,128)(2,1)S(1)} %get-tuple-element.65), channel_id=1, source_target_pairs={{8,16},{10,18},{12,20},{14,22},{16,8},{18,10},{20,12},{22,14},{9,1... | collective-permute-start | bytes 589832 | tf_op jit(solution)/shard_map/ppermute | solution.py:376
  27.5 0.1 collective-permute-start.16
  27.5 0.0 collective-permute-done.8.edge_b
  27.5 0.0 collective-permute-done.9.edge_a
  27.6 2.6 %lend.1 = (bf16[3,288,128]{2,1,0:T(8,128)(2,1)S(1)}, bf16[3,288,128]{2,1,0:T(8,128)(2,1)S(1)}, bf16[256,1536]{1,0:T(8,128)(2,1)S(1)}) custom-call(bf16[3,272,128]{2,1,0:T(8,128)(2,1)S(1)} %collective-permute-done.8.edge_b, bf16[3,272,128]{2,1,0:T(8,128)(2,1)S(1)} %collective-permute-done.9.edge_a, bf16[256,1024]{1,0:T(8,128)(2,1)S(1)} %get-tuple-element.59.plane_turned, ...), custom_call_target="tpu_custom_call" | custom-call | flops 4831838208 | bytes 3145728 | tf_op jit(solution)/shard_map/lend/pallas_call | solution.py:452
  30.2 1.5 %collective-permute-start.13 = (bf16[3,288,128]{2,1,0:T(8,128)(2,1)S(1)}, bf16[3,288,128]{2,1,0:T(8,128)(2,1)S(1)}, u32[]{:S(2)}, u32[]{:S(2)}) collective-permute-start(bf16[3,288,128]{2,1,0:T(8,128)(2,1)S(1)} %get-tuple-element.61), channel_id=1, source_target_pairs={{0,8},{2,10},{4,12},{6,14},{8,0},{10,2},{12,4},{14,6},{16,24},{18,... | collective-permute-start | bytes 663560 | tf_op jit(solution)/shard_map/ppermute | solution.py:376
  31.7 2.2 %collective-permute-start.14 = (bf16[3,288,128]{2,1,0:T(8,128)(2,1)S(1)}, bf16[3,288,128]{2,1,0:T(8,128)(2,1)S(1)}, u32[]{:S(2)}, u32[]{:S(2)}) collective-permute-start(bf16[3,288,128]{2,1,0:T(8,128)(2,1)S(1)} %get-tuple-element.62), channel_id=1, source_target_pairs={{8,16},{10,18},{12,20},{14,22},{16,8},{18,10},{20,12},{22,14},{9,1... | collective-permute-start | bytes 663560 | tf_op jit(solution)/shard_map/ppermute | solution.py:376
  33.9 0.0 collective-permute-done.15.refs_12_
  33.9 0.0 collective-permute-done.16.refs_13_
  33.9 2.6 %columns.2 = (bf16[256,128]{1,0:T(8,128)(2,1)S(1)}, bf16[256,128]{1,0:T(8,128)(2,1)S(1)}, bf16[256,1024]{1,0:T(8,128)(2,1)S(1)}, bf16[1024,256]{1,0:T(8,128)(2,1...) custom-call(bf16[528,128]{1,0:T(8,128)(2,1)S(1)} %get-tuple-element.49.refs_4_.refs_0_, ...), custom_call_target="tpu_custom_call" | custom-call | flops 1879048192 | bytes 1572864 | tf_op jit(solution)/shard_map/columns/pallas_call | solution.py:471
  36.6 3.0 %collective-permute-start.22 = (bf16[256,128]{1,0:T(8,128)(2,1)S(1)}, bf16[256,128]{1,0:T(8,128)(2,1)S(1)}, u32[]{:S(2)}, u32[]{:S(2)}) collective-permute-start(bf16[256,128]{1,0:T(8,128)(2,1)S(1)} %get-tuple-element.79), channel_id=1, source_target_pairs={{0,6},{2,4},{4,2},{6,0},{8,14},{10,12},{12,10},{14,8},{16,22},{18,... | collective-permute-start | bytes 196616 | tf_op jit(solution)/shard_map/ppermute | solution.py:371
  39.6 0.4 collective-permute-start.21
  40.0 0.0 collective-permute-done.13.back_a
  40.0 0.0 collective-permute-done.14.back_b
  40.0 0.6 %merge.1 = (bf16[256,128]{1,0:T(8,128)(2,1)S(1)}, bf16[256,128]{1,0:T(8,128)(2,1)S(1)}, bf16[256,128]{1,0:T(8,128)(2,1)S(1)}, bf16[256,128]{1,0:T(8,128)(2,1)S(1)}) custom-call(bf16[3,288,128]{2,1,0:T(8,128)(2,1)S(1)} %collective-permute-done.13.back_a, bf16[3,288,128]{2,1,0:T(8,128)(2,1)S(1)} %collective-permute-done.14.back_b, ...), custom_call_target="tpu_custom_call" | custom-call | bytes 2097152 | tf_op jit(solution)/shard_map/merge/pallas_call | solution.py:474
  40.6 1.4 %collective-permute-start.17 = (bf16[256,128]{1,0:T(8,128)(2,1)S(1)}, bf16[256,128]{1,0:T(8,128)(2,1)S(1)}, u32[]{:S(2)}, u32[]{:S(2)}) collective-permute-start(bf16[256,128]{1,0:T(8,128)(2,1)S(1)} %get-tuple-element.70), channel_id=1, source_target_pairs={{0,2},{2,0},{4,6},{6,4},{8,10},{10,8},{12,14},{14,12},{16,18},{18,... | collective-permute-start | bytes 196616 | tf_op jit(solution)/shard_map/ppermute | solution.py:371
  42.0 1.2 %collective-permute-start.18 = (bf16[256,128]{1,0:T(8,128)(2,1)S(1)}, bf16[256,128]{1,0:T(8,128)(2,1)S(1)}, u32[]{:S(2)}, u32[]{:S(2)}) collective-permute-start(bf16[256,128]{1,0:T(8,128)(2,1)S(1)} %get-tuple-element.71), channel_id=1, source_target_pairs={{0,4},{2,6},{4,0},{6,2},{8,12},{10,14},{12,8},{14,10},{16,20},{18,... | collective-permute-start | bytes 196616 | tf_op jit(solution)/shard_map/ppermute | solution.py:371
  43.2 0.5 %collective-permute-start.19 = (bf16[256,128]{1,0:T(8,128)(2,1)S(1)}, bf16[256,128]{1,0:T(8,128)(2,1)S(1)}, u32[]{:S(2)}, u32[]{:S(2)}) collective-permute-start(bf16[256,128]{1,0:T(8,128)(2,1)S(1)} %get-tuple-element.72), channel_id=1, source_target_pairs={{0,6},{2,4},{4,2},{6,0},{8,14},{10,12},{12,10},{14,8},{16,22},{18,... | collective-permute-start | bytes 196616 | tf_op jit(solution)/shard_map/ppermute | solution.py:371
  43.7 2.3 %columns.3 = (bf16[256,128]{1,0:T(8,128)(2,1)S(1)}, bf16[256,128]{1,0:T(8,128)(2,1)S(1)}) custom-call(bf16[256,1536]{1,0:T(8,128)(2,1)S(1)} %get-tuple-element.67.refs_14_.refs_0_, bf16[256,1024]{1,0:T(8,128)(2,1)S(1)} %get-tuple-element.73.refs_1_, bf16[1024,256]{1,0:T(8,128)(2,1)S(1)} %get-tuple-element.74.refs_2_, ...), custom_call_target="tpu_custom_call" | custom-call | flops 1879048192 | bytes 1572864 | tf_op jit(solution)/shard_map/columns/pallas_call | solution.py:484
  46.0 0.0 collective-permute-done.17.refs_1_
  46.0 0.2 collective-permute-start.20
  46.3 0.0 collective-permute-done.18.refs_2_
  46.3 1.0 %collective-permute-done.19.refs_3_ = bf16[256,128]{1,0:T(8,128)(2,1)S(1)} collective-permute-done((bf16[256,128]{1,0:T(8,128)(2,1)S(1)}, bf16[256,128]{1,0:T(8,128)(2,1)S(1)}, u32[]{:S(2)}, u32[]{:S(2)}) %collective-permute-start.19) | collective-permute-done | bytes 65568 | tf_op jit(solution)/shard_map/ppermute | solution.py:371
  47.3 0.7 %join.2 = bf16[256,512]{1,0:T(8,128)(2,1)} custom-call(bf16[256,128]{1,0:T(8,128)(2,1)S(1)} %get-tuple-element.69.refs_0_.refs_5_, bf16[256,128]{1,0:T(8,128)(2,1)S(1)} %collective-permute-done.17.refs_1_, bf16[256,128]{1,0:T(8,128)(2,1)S(1)} %collective-permute-done.18.refs_2_, bf16[256,128]{1,0:T(8,128)(2,1)S(1)} %collective-permute-done.19.refs_3_), custom_call_target="tpu_custom_call" | custom-call | bytes 524288 | tf_op jit(solution)/shard_map/join/pallas_call | solution.py:493
  48.0 0.0 collective-permute-done.22.refs_3_
  48.0 0.0 collective-permute-done.21.refs_2_
  48.0 0.0 collective-permute-done.20.refs_1_
  48.0 0.7 %join.3 = bf16[256,512]{1,0:T(8,128)(2,1)} custom-call(bf16[256,128]{1,0:T(8,128)(2,1)S(1)} %get-tuple-element.77.refs_0_, bf16[256,128]{1,0:T(8,128)(2,1)S(1)} %collective-permute-done.20.refs_1_, bf16[256,128]{1,0:T(8,128)(2,1)S(1)} %collective-permute-done.21.refs_2_, bf16[256,128]{1,0:T(8,128)(2,1)S(1)} %collective-permute-done.22.refs_3_), custom_call_target="tpu_custom_call" | custom-call | bytes 524288 | tf_op jit(solution)/shard_map/join/pallas_call | solution.py:493
Async XLA Ops:
  0.6 9.2 %collective-permute-start.1 = (bf16[256,512]{1,0:T(8,128)(2,1)}, bf16[256,512]{1,0:T(8,128)(2,1)S(1)}, u32[]{:S(2)}, u32[]{:S(2)}) collective-permute-start(bf16[256,512]{1,0:T(8,128)(2,1)} %audio.3), channel_id=1, source_target_pairs={{0,1},{1,0},{2,3},{3,2},{4,5},{5,4},{6,7},{7,6},{8,9},{9,8},{10,11... | collective-permute-start | bytes 786440 | tf_op jit(solution)/shard_map/ppermute | solution.py:367
  1.9 11.8 %collective-permute-start.7 = (bf16[256,512]{1,0:T(8,128)(2,1)}, bf16[256,512]{1,0:T(8,128)(2,1)S(1)}, u32[]{:S(2)}, u32[]{:S(2)}) collective-permute-start(bf16[256,512]{1,0:T(8,128)(2,1)} %video.3), channel_id=1, source_target_pairs={{0,1},{1,0},{2,3},{3,2},{4,5},{5,4},{6,7},{7,6},{8,9},{9,8},{10,11... | collective-permute-start | bytes 786440 | tf_op jit(solution)/shard_map/ppermute | solution.py:367
  3.3 3.0 %collective-permute-start = (bf16[528,128]{1,0:T(8,128)(2,1)S(1)}, bf16[528,128]{1,0:T(8,128)(2,1)S(1)}, u32[]{:S(2)}, u32[]{:S(2)}) collective-permute-start(bf16[528,128]{1,0:T(8,128)(2,1)S(1)} %get-tuple-element.41), channel_id=1, source_target_pairs={{0,2},{2,0},{4,6},{6,4},{8,10},{10,8},{12,14},{14,12},{16,18},{18,... | collective-permute-start | bytes 405512 | tf_op jit(solution)/shard_map/ppermute | solution.py:371
  4.6 5.2 %collective-permute-start.2 = (bf16[528,128]{1,0:T(8,128)(2,1)S(1)}, bf16[528,128]{1,0:T(8,128)(2,1)S(1)}, u32[]{:S(2)}, u32[]{:S(2)}) collective-permute-start(bf16[528,128]{1,0:T(8,128)(2,1)S(1)} %get-tuple-element.44), channel_id=1, source_target_pairs={{0,4},{2,6},{4,0},{6,2},{8,12},{10,14},{12,8},{14,10},{16,20},{18,... | collective-permute-start | bytes 405512 | tf_op jit(solution)/shard_map/ppermute | solution.py:371
  5.9 9.8 %collective-permute-start.6 = (bf16[528,128]{1,0:T(8,128)(2,1)S(1)}, bf16[528,128]{1,0:T(8,128)(2,1)S(1)}, u32[]{:S(2)}, u32[]{:S(2)}) collective-permute-start(bf16[528,128]{1,0:T(8,128)(2,1)S(1)} %get-tuple-element.50), channel_id=1, source_target_pairs={{0,6},{2,4},{4,2},{6,0},{8,14},{10,12},{12,10},{14,8},{16,22},{18,... | collective-permute-start | bytes 405512 | tf_op jit(solution)/shard_map/ppermute | solution.py:371
  10.2 6.7 %collective-permute-start.3 = (bf16[256,128]{1,0:T(8,128)(2,1)S(1)}, bf16[256,128]{1,0:T(8,128)(2,1)S(1)}, u32[]{:S(2)}, u32[]{:S(2)}) collective-permute-start(bf16[256,128]{1,0:T(8,128)(2,1)S(1)} %get-tuple-element.46), channel_id=1, source_target_pairs={{0,2},{2,0},{4,6},{6,4},{8,10},{10,8},{12,14},{14,12},{16,18},{18,... | collective-permute-start | bytes 196616 | tf_op jit(solution)/shard_map/ppermute | solution.py:371
  11.6 5.9 %collective-permute-start.4 = (bf16[256,128]{1,0:T(8,128)(2,1)S(1)}, bf16[256,128]{1,0:T(8,128)(2,1)S(1)}, u32[]{:S(2)}, u32[]{:S(2)}) collective-permute-start(bf16[256,128]{1,0:T(8,128)(2,1)S(1)} %get-tuple-element.47), channel_id=1, source_target_pairs={{0,4},{2,6},{4,0},{6,2},{8,12},{10,14},{12,8},{14,10},{16,20},{18,... | collective-permute-start | bytes 196616 | tf_op jit(solution)/shard_map/ppermute | solution.py:371
  12.8 4.6 %collective-permute-start.5 = (bf16[256,128]{1,0:T(8,128)(2,1)S(1)}, bf16[256,128]{1,0:T(8,128)(2,1)S(1)}, u32[]{:S(2)}, u32[]{:S(2)}) collective-permute-start(bf16[256,128]{1,0:T(8,128)(2,1)S(1)} %get-tuple-element.48), channel_id=1, source_target_pairs={{0,6},{2,4},{4,2},{6,0},{8,14},{10,12},{12,10},{14,8},{16,22},{18,... | collective-permute-start | bytes 196616 | tf_op jit(solution)/shard_map/ppermute | solution.py:371
  14.1 6.7 %collective-permute-start.10 = (bf16[256,128]{1,0:T(8,128)(2,1)S(1)}, bf16[256,128]{1,0:T(8,128)(2,1)S(1)}, u32[]{:S(2)}, u32[]{:S(2)}) collective-permute-start(bf16[256,128]{1,0:T(8,128)(2,1)S(1)} %get-tuple-element.56), channel_id=1, source_target_pairs={{0,2},{2,0},{4,6},{6,4},{8,10},{10,8},{12,14},{14,12},{16,18},{18,... | collective-permute-start | bytes 196616 | tf_op jit(solution)/shard_map/ppermute | solution.py:371
  15.7 5.1 %collective-permute-start.11 = (bf16[256,128]{1,0:T(8,128)(2,1)S(1)}, bf16[256,128]{1,0:T(8,128)(2,1)S(1)}, u32[]{:S(2)}, u32[]{:S(2)}) collective-permute-start(bf16[256,128]{1,0:T(8,128)(2,1)S(1)} %get-tuple-element.57), channel_id=1, source_target_pairs={{0,4},{2,6},{4,0},{6,2},{8,12},{10,14},{12,8},{14,10},{16,20},{18,... | collective-permute-start | bytes 196616 | tf_op jit(solution)/shard_map/ppermute | solution.py:371
  16.9 4.1 %collective-permute-start.12 = (bf16[256,128]{1,0:T(8,128)(2,1)S(1)}, bf16[256,128]{1,0:T(8,128)(2,1)S(1)}, u32[]{:S(2)}, u32[]{:S(2)}) collective-permute-start(bf16[256,128]{1,0:T(8,128)(2,1)S(1)} %get-tuple-element.58), channel_id=1, source_target_pairs={{0,6},{2,4},{4,2},{6,0},{8,14},{10,12},{12,10},{14,8},{16,22},{18,... | collective-permute-start | bytes 196616 | tf_op jit(solution)/shard_map/ppermute | solution.py:371
  17.5 10.0 %collective-permute-start.8 = (bf16[3,272,128]{2,1,0:T(8,128)(2,1)S(1)}, bf16[3,272,128]{2,1,0:T(8,128)(2,1)S(1)}, u32[]{:S(2)}, u32[]{:S(2)}) collective-permute-start(bf16[3,272,128]{2,1,0:T(8,128)(2,1)S(1)} %get-tuple-element.54), channel_id=1, source_target_pairs={{8,16},{10,18},{12,20},{14,22},{16,8},{18,10},{20,12},{22,14},{9,1... | collective-permute-start | bytes 626696 | tf_op jit(solution)/shard_map/ppermute | solution.py:376
  20.7 6.8 %collective-permute-start.9 = (bf16[3,272,128]{2,1,0:T(8,128)(2,1)S(1)}, bf16[3,272,128]{2,1,0:T(8,128)(2,1)S(1)}, u32[]{:S(2)}, u32[]{:S(2)}) collective-permute-start(bf16[3,272,128]{2,1,0:T(8,128)(2,1)S(1)} %get-tuple-element.55), channel_id=1, source_target_pairs={{0,8},{2,10},{4,12},{6,14},{8,0},{10,2},{12,4},{14,6},{16,24},{18,... | collective-permute-start | bytes 626696 | tf_op jit(solution)/shard_map/ppermute | solution.py:376
  24.2 9.7 %collective-permute-start.15 = (bf16[3,256,128]{2,1,0:T(8,128)(2,1)S(1)}, bf16[3,256,128]{2,1,0:T(8,128)(2,1)S(1)}, u32[]{:S(2)}, u32[]{:S(2)}) collective-permute-start(bf16[3,256,128]{2,1,0:T(8,128)(2,1)S(1)} %get-tuple-element.65), channel_id=1, source_target_pairs={{8,16},{10,18},{12,20},{14,22},{16,8},{18,10},{20,12},{22,14},{9,1... | collective-permute-start | bytes 589832 | tf_op jit(solution)/shard_map/ppermute | solution.py:376
  27.5 6.5 %collective-permute-start.16 = (bf16[3,256,128]{2,1,0:T(8,128)(2,1)S(1)}, bf16[3,256,128]{2,1,0:T(8,128)(2,1)S(1)}, u32[]{:S(2)}, u32[]{:S(2)}) collective-permute-start(bf16[3,256,128]{2,1,0:T(8,128)(2,1)S(1)} %get-tuple-element.66), channel_id=1, source_target_pairs={{0,8},{2,10},{4,12},{6,14},{8,0},{10,2},{12,4},{14,6},{16,24},{18,... | collective-permute-start | bytes 589832 | tf_op jit(solution)/shard_map/ppermute | solution.py:376
  30.2 9.8 %collective-permute-start.13 = (bf16[3,288,128]{2,1,0:T(8,128)(2,1)S(1)}, bf16[3,288,128]{2,1,0:T(8,128)(2,1)S(1)}, u32[]{:S(2)}, u32[]{:S(2)}) collective-permute-start(bf16[3,288,128]{2,1,0:T(8,128)(2,1)S(1)} %get-tuple-element.61), channel_id=1, source_target_pairs={{0,8},{2,10},{4,12},{6,14},{8,0},{10,2},{12,4},{14,6},{16,24},{18,... | collective-permute-start | bytes 663560 | tf_op jit(solution)/shard_map/ppermute | solution.py:376
  31.7 8.3 %collective-permute-start.14 = (bf16[3,288,128]{2,1,0:T(8,128)(2,1)S(1)}, bf16[3,288,128]{2,1,0:T(8,128)(2,1)S(1)}, u32[]{:S(2)}, u32[]{:S(2)}) collective-permute-start(bf16[3,288,128]{2,1,0:T(8,128)(2,1)S(1)} %get-tuple-element.62), channel_id=1, source_target_pairs={{8,16},{10,18},{12,20},{14,22},{16,8},{18,10},{20,12},{22,14},{9,1... | collective-permute-start | bytes 663560 | tf_op jit(solution)/shard_map/ppermute | solution.py:376
  36.6 11.4 %collective-permute-start.22 = (bf16[256,128]{1,0:T(8,128)(2,1)S(1)}, bf16[256,128]{1,0:T(8,128)(2,1)S(1)}, u32[]{:S(2)}, u32[]{:S(2)}) collective-permute-start(bf16[256,128]{1,0:T(8,128)(2,1)S(1)} %get-tuple-element.79), channel_id=1, source_target_pairs={{0,6},{2,4},{4,2},{6,0},{8,14},{10,12},{12,10},{14,8},{16,22},{18,... | collective-permute-start | bytes 196616 | tf_op jit(solution)/shard_map/ppermute | solution.py:371
  39.6 8.5 %collective-permute-start.21 = (bf16[256,128]{1,0:T(8,128)(2,1)S(1)}, bf16[256,128]{1,0:T(8,128)(2,1)S(1)}, u32[]{:S(2)}, u32[]{:S(2)}) collective-permute-start(bf16[256,128]{1,0:T(8,128)(2,1)S(1)} %get-tuple-element.68.refs_0_), channel_id=1, source_target_pairs={{0,4},{2,6},{4,0},{6,2},{8,12},{10,14},{12,8},{14,10},{16,20},{18,... | collective-permute-start | bytes 196616 | tf_op jit(solution)/shard_map/ppermute | solution.py:371
  40.6 5.4 %collective-permute-start.17 = (bf16[256,128]{1,0:T(8,128)(2,1)S(1)}, bf16[256,128]{1,0:T(8,128)(2,1)S(1)}, u32[]{:S(2)}, u32[]{:S(2)}) collective-permute-start(bf16[256,128]{1,0:T(8,128)(2,1)S(1)} %get-tuple-element.70), channel_id=1, source_target_pairs={{0,2},{2,0},{4,6},{6,4},{8,10},{10,8},{12,14},{14,12},{16,18},{18,... | collective-permute-start | bytes 196616 | tf_op jit(solution)/shard_map/ppermute | solution.py:371
  42.0 4.2 %collective-permute-start.18 = (bf16[256,128]{1,0:T(8,128)(2,1)S(1)}, bf16[256,128]{1,0:T(8,128)(2,1)S(1)}, u32[]{:S(2)}, u32[]{:S(2)}) collective-permute-start(bf16[256,128]{1,0:T(8,128)(2,1)S(1)} %get-tuple-element.71), channel_id=1, source_target_pairs={{0,4},{2,6},{4,0},{6,2},{8,12},{10,14},{12,8},{14,10},{16,20},{18,... | collective-permute-start | bytes 196616 | tf_op jit(solution)/shard_map/ppermute | solution.py:371
  43.2 4.1 %collective-permute-start.19 = (bf16[256,128]{1,0:T(8,128)(2,1)S(1)}, bf16[256,128]{1,0:T(8,128)(2,1)S(1)}, u32[]{:S(2)}, u32[]{:S(2)}) collective-permute-start(bf16[256,128]{1,0:T(8,128)(2,1)S(1)} %get-tuple-element.72), channel_id=1, source_target_pairs={{0,6},{2,4},{4,2},{6,0},{8,14},{10,12},{12,10},{14,8},{16,22},{18,... | collective-permute-start | bytes 196616 | tf_op jit(solution)/shard_map/ppermute | solution.py:371
  46.0 2.0 %collective-permute-start.20 = (bf16[256,128]{1,0:T(8,128)(2,1)S(1)}, bf16[256,128]{1,0:T(8,128)(2,1)S(1)}, u32[]{:S(2)}, u32[]{:S(2)}) collective-permute-start(bf16[256,128]{1,0:T(8,128)(2,1)S(1)} %get-tuple-element.78), channel_id=1, source_target_pairs={{0,2},{2,0},{4,6},{6,4},{8,10},{10,8},{12,14},{14,12},{16,18},{18,... | collective-permute-start | bytes 196616 | tf_op jit(solution)/shard_map/ppermute | solution.py:371

commit v16 on v15

--- a/solution.py
+++ b/solution.py
@@ -269,11 +269,17 @@
         packs, queries, keys, (edge_b, edge_a) = take(GROUP), take(GROUP), take(GROUP), take(2)
     (edge_turned,) = take(1)
     if not first:
-        shared, _ = take(4), take(1)
-    outs = take(len(receivers))
+        shared, received, _ = take(4), take(GROUP - 1), take(1)
+    outs = take(len(receivers) if first else 1)
     turned, beside, asks, edge_beside = take(4) if first else shared
-    rows, width = outs[0].shape
-    mine = place()
+    rows, width = beside.shape[0] // GROUP, beside.shape[1] // 2
+    mine = place()
+    if not first:
+        own, sems = refs
+        copies, fetch = fetcher(sems)
+        columns = [pl.ds(pl.multiple_of((mine ^ k) * width, width), width) for k in range(GROUP)]
+        for k in range(1, GROUP):
+            fetch(received[k - 1], outs[0].at[:, columns[k]])
     if first:
         odd = lax.rem(plane(), 2)
         set_up(
@@ -303,7 +309,11 @@
             ahead = scores_of(n + 1)
         _, mixed = attend(scores, [beside[...], edge_beside[near[n]]])
         mean = by_head(mixed[:, :width], rows) / by_head(mixed[:, width:], rows)
-        outs[n][...] = mean.astype(outs[n].dtype)
+        (outs[n] if first else own)[...] = mean.astype(outs[0].dtype)
+    if not first:
+        fetch(own, outs[0].at[:, columns[0]])
+        for copy in copies:
+            copy.wait()
 
 
 def merge_kernel(back_a, back_b, peaks, sums, *refs):
@@ -467,7 +477,7 @@
         name="columns",
     )
     shared = [turned, beside, asks, shape((around, 2 * width), bf16)]
-    near, far = range(GROUP // 2), range(GROUP // 2, GROUP)
+    far = range(1, GROUP)
     *far_pieces, turned, beside, asks, edge_beside = call(
         functools.partial(columns_kernel, far), [piece] * len(far) + shared, **half_columns
     )(*packs, *queries, *keys, *audio_edges[::-1], edge_turned)
@@ -481,13 +491,15 @@
         name="merge",
     )(*backs, peaks, sums, far_pieces[0])
     audio_pieces = traded(audio_pieces)
-    near_pieces = call(
-        functools.partial(columns_kernel, near),
-        [piece] * len(near),
-        ins=[VMEM] * 5 + [ANY],
+    video_pieces = traded([None, *far_pieces])[1:]
+    video_attended = call(
+        functools.partial(columns_kernel, range(1)),
+        shape((rows, half), bf16),
+        [pltpu.VMEM((rows, width), bf16), pltpu.SemaphoreType.DMA((GROUP,))],
+        ins=[VMEM] * (5 + GROUP - 1) + [ANY],
+        outs_in=HBM,
         **half_columns,
-    )(edge_turned, turned, beside, asks, edge_beside, audio_pieces[0])
-    video_pieces = traded([*near_pieces, *far_pieces])
+    )(edge_turned, turned, beside, asks, edge_beside, *video_pieces, audio_pieces[0])
 
     def join(pieces):
         return call(
@@ -499,7 +511,6 @@
             name="join",
         )(*pieces)
 
-    video_attended = join(video_pieces)
     audio_attended = join(audio_pieces)
     return (audio_attended, video_attended)
 

time: 49.2 us -> 49.6 us (level)
  Pallas kernels: 16.6 us -> 17.7 us
  waiting for transfers between devices: 3.34 us -> 2.32 us
    pallas_call x1, Pallas kernels: 2.65 us -> 3.91 us  [local(): call(functools.partial(columns_kernel, far), [piece] * len(far) + shared,...]
    ppermute x15, waiting for transfers between devices: 2.89 us -> 1.87 us  [traded(): lax.ppermute(pieces[k], 'tm', pairs(k))]
    pallas_call x2 -> x1, Pallas kernels: 1.47 us -> 0.74 us  [join(): call(join_kernel, shape((rows, half), bf16), [pltpu.SemaphoreType.DMA((GR...]
    pallas_call x1, Pallas kernels: 2.26 us -> 2.81 us  [local(): call(functools.partial(columns_kernel, range(1)), shape((rows, half), bf1...]
  transfers between devices with their start and end apart: 23 -> 23, of which waited for: 4 -> 3; matrix products, arithmetic and copies ran while one was open for 0% -> 0% of each run, Pallas kernels for 32% -> 34%
where the time goes in v16:
time: 49.6 us; the launch traced here: 49.4 us
  starting transfers between devices  28.4 us (57%)
  Pallas kernels  17.7 us (36%)
  waiting for transfers between devices  2.32 us (5%)
  between operations  1 us (2%)
    ppermute x15, starting transfers between devices, traded(): lax.ppermute(pieces[k], 'tm', pairs(k))  16.6 us
    ppermute x6, starting transfers between devices, crossed(): lax.ppermute(sent, 'tm', [(p * GROUP + i, q * GROUP + i) for p, q in pair...  10.3 us
    pallas_call x1, Pallas kernels, local(): call(functools.partial(columns_kernel, far), [piece] * len(far) + shared,...  3.91 us
    pallas_call x1, Pallas kernels, local(): call(rows_kernel, [shape((GROUP, heads * rows, n * width), f32) for n in...  3.17 us
    pallas_call x1, Pallas kernels, local(): call(functools.partial(columns_kernel, range(1)), shape((rows, half), bf1...  2.81 us
    pallas_call x1, Pallas kernels, local(): call(lend_kernel, [back, back, shape((2 * width, around), bf16)], [pltpu....  2.62 us
    ppermute x15, waiting for transfers between devices, traded(): lax.ppermute(pieces[k], 'tm', pairs(k))  1.87 us
    pallas_call x1, Pallas kernels, local(): call(prepare_kernel, [part, part, square, square], [pltpu.VMEM((rows, hal...  1.78 us
  transfers between devices with their start and end apart: 23, of which 3 were waited for; matrix products, arithmetic and copies ran while one was open for 0% of the time, Pallas kernels for 34%

profile of v16, /device:TPU:9, one launch (start us, length us, event | category | flops | bytes accessed | tf_op | source)
XLA Modules:
  0.0 49.4 jit_solution(16226404144146819707)
XLA Ops:
  0.6 1.3 %collective-permute-start.1 = (bf16[256,512]{1,0:T(8,128)(2,1)}, bf16[256,512]{1,0:T(8,128)(2,1)S(1)}, u32[]{:S(2)}, u32[]{:S(2)}) collective-permute-start(bf16[256,512]{1,0:T(8,128)(2,1)} %audio.3), channel_id=1, source_target_pairs={{0,1},{1,0},{2,3},{3,2},{4,5},{5,4},{6,7},{7,6},{8,9},{9,8},{10,11... | collective-permute-start | bytes 786440 | tf_op jit(solution)/shard_map/ppermute | solution.py:377
  1.9 0.2 collective-permute-start.7
  2.2 1.2 %split.1 = (bf16[528,128]{1,0:T(8,128)(2,1)S(1)}, bf16[528,128]{1,0:T(8,128)(2,1)S(1)}, bf16[528,128]{1,0:T(8,128)(2,1)S(1)}, bf16[528,128]{1,0:T(8,128)(2,1)S(1)}) custom-call(bf16[256,512]{1,0:T(8,128)(2,1)} %audio.3, bf16[256,512]{1,0:T(8,128)(2,1)} %video.3, s32[2,128]{1,0:T(2,128)} %bitcast.1), custom_call_target="tpu_custom_call" | custom-call | bytes 1048576 | tf_op jit(solution)/shard_map/split/pallas_call | solution.py:399
  3.3 1.3 %collective-permute-start = (bf16[528,128]{1,0:T(8,128)(2,1)S(1)}, bf16[528,128]{1,0:T(8,128)(2,1)S(1)}, u32[]{:S(2)}, u32[]{:S(2)}) collective-permute-start(bf16[528,128]{1,0:T(8,128)(2,1)S(1)} %get-tuple-element.40), channel_id=1, source_target_pairs={{0,2},{2,0},{4,6},{6,4},{8,10},{10,8},{12,14},{14,12},{16,18},{18,... | collective-permute-start | bytes 405512 | tf_op jit(solution)/shard_map/ppermute | solution.py:381
  4.6 1.2 %collective-permute-start.2 = (bf16[528,128]{1,0:T(8,128)(2,1)S(1)}, bf16[528,128]{1,0:T(8,128)(2,1)S(1)}, u32[]{:S(2)}, u32[]{:S(2)}) collective-permute-start(bf16[528,128]{1,0:T(8,128)(2,1)S(1)} %get-tuple-element.43), channel_id=1, source_target_pairs={{0,4},{2,6},{4,0},{6,2},{8,12},{10,14},{12,8},{14,10},{16,20},{18,... | collective-permute-start | bytes 405512 | tf_op jit(solution)/shard_map/ppermute | solution.py:381
  5.9 0.5 collective-permute-start.6
  6.3 0.0 collective-permute-done.refs_0_.refs_5_.refs_1_
  6.3 1.8 %prepare.1 = (f32[256,512]{1,0:T(8,128)S(1)}, f32[256,512]{1,0:T(8,128)S(1)}, bf16[512,512]{1,0:T(8,128)(2,1)S(1)}, bf16[512,512]{1,0:T(8,128)(2,1)S(1)}) custom-call(bf16[256,512]{1,0:T(8,128)(2,1)} %audio.3, bf16[256,512]{1,0:T(8,128)(2,1)} %video.3, bf16[1024,512]{1,0:T(8,128)(2,1)} %query.1, bf16[1024,512]{1,0:T(8,128)(2,1)} %key.1, ...), custom_call_target="tpu_custom_call" | custom-call | flops 268435456 | bytes 4194304 | tf_op jit(solution)/shard_map/prepare/pallas_call | solution.py:409
  8.1 1.7 %collective-permute-done.2.refs_1_.refs_6_.refs_2_ = bf16[528,128]{1,0:T(8,128)(2,1)S(1)} collective-permute-done((bf16[528,128]{1,0:T(8,128)(2,1)S(1)}, bf16[528,128]{1,0:T(8,128)(2,1)S(1)}, u32[]{:S(2)}, u32[]{:S(2)}) %collective-permute-start.2) | collective-permute-done | bytes 135200 | tf_op jit(solution)/shard_map/ppermute | solution.py:381
  9.8 0.0 collective-permute-done.1.other
  9.8 0.4 project.2
  10.2 1.4 %collective-permute-start.3 = (bf16[256,128]{1,0:T(8,128)(2,1)S(1)}, bf16[256,128]{1,0:T(8,128)(2,1)S(1)}, u32[]{:S(2)}, u32[]{:S(2)}) collective-permute-start(bf16[256,128]{1,0:T(8,128)(2,1)S(1)} %get-tuple-element.45), channel_id=1, source_target_pairs={{0,2},{2,0},{4,6},{6,4},{8,10},{10,8},{12,14},{14,12},{16,18},{18,... | collective-permute-start | bytes 196616 | tf_op jit(solution)/shard_map/ppermute | solution.py:381
  11.6 1.2 %collective-permute-start.4 = (bf16[256,128]{1,0:T(8,128)(2,1)S(1)}, bf16[256,128]{1,0:T(8,128)(2,1)S(1)}, u32[]{:S(2)}, u32[]{:S(2)}) collective-permute-start(bf16[256,128]{1,0:T(8,128)(2,1)S(1)} %get-tuple-element.46), channel_id=1, source_target_pairs={{0,4},{2,6},{4,0},{6,2},{8,12},{10,14},{12,8},{14,10},{16,20},{18,... | collective-permute-start | bytes 196616 | tf_op jit(solution)/shard_map/ppermute | solution.py:381
  12.8 0.5 collective-permute-start.5
  13.3 0.4 collective-permute-done.7.other
  13.7 0.4 project.3
  14.1 1.6 %collective-permute-start.10 = (bf16[256,128]{1,0:T(8,128)(2,1)S(1)}, bf16[256,128]{1,0:T(8,128)(2,1)S(1)}, u32[]{:S(2)}, u32[]{:S(2)}) collective-permute-start(bf16[256,128]{1,0:T(8,128)(2,1)S(1)} %get-tuple-element.55), channel_id=1, source_target_pairs={{0,2},{2,0},{4,6},{6,4},{8,10},{10,8},{12,14},{14,12},{16,18},{18,... | collective-permute-start | bytes 196616 | tf_op jit(solution)/shard_map/ppermute | solution.py:381
  15.7 0.0 collective-permute-done.6.refs_7_.refs_3_
  15.7 1.2 %collective-permute-start.11 = (bf16[256,128]{1,0:T(8,128)(2,1)S(1)}, bf16[256,128]{1,0:T(8,128)(2,1)S(1)}, u32[]{:S(2)}, u32[]{:S(2)}) collective-permute-start(bf16[256,128]{1,0:T(8,128)(2,1)S(1)} %get-tuple-element.56), channel_id=1, source_target_pairs={{0,4},{2,6},{4,0},{6,2},{8,12},{10,14},{12,8},{14,10},{16,20},{18,... | collective-permute-start | bytes 196616 | tf_op jit(solution)/shard_map/ppermute | solution.py:381
  16.9 0.0 collective-permute-done.3.refs_1_.refs_5_
  16.9 0.5 collective-permute-start.12
  17.4 0.0 collective-permute-done.4.refs_2_.refs_6_
  17.4 0.0 collective-permute-done.5.refs_3_.refs_7_
  17.4 0.1 halo.2
  17.5 3.2 %collective-permute-start.8 = (bf16[3,272,128]{2,1,0:T(8,128)(2,1)S(1)}, bf16[3,272,128]{2,1,0:T(8,128)(2,1)S(1)}, u32[]{:S(2)}, u32[]{:S(2)}) collective-permute-start(bf16[3,272,128]{2,1,0:T(8,128)(2,1)S(1)} %get-tuple-element.53), channel_id=1, source_target_pairs={{8,16},{10,18},{12,20},{14,22},{16,8},{18,10},{20,12},{22,14},{9,1... | collective-permute-start | bytes 626696 | tf_op jit(solution)/shard_map/ppermute | solution.py:386
  20.7 0.1 collective-permute-start.9
  20.8 0.0 collective-permute-done.10.refs_9_
  20.8 0.0 collective-permute-done.11.refs_10_
  20.8 0.2 collective-permute-done.12.refs_11_
  21.0 3.2 %rows.1 = (f32[4,512,128]{2,1,0:T(8,128)S(1)}, f32[4,512,256]{2,1,0:T(8,128)S(1)}, bf16[256,1024]{1,0:T(8,128)(2,1)S(1)}, bf16[1024,256]{1,0:T(8,128)(2,1)S(1)}) custom-call(bf16[528,128]{1,0:T(8,128)(2,1)S(1)} %get-tuple-element.48.refs_4_.refs_0_, bf16[528,128]{1,0:T(8,128)(2,1)S(1)} %collective-permute-done.refs_0_.refs_5_.refs_1_, ...), custom_call_target="tpu_custom_call" | custom-call | flops 2147483648 | bytes 2097152 | tf_op jit(solution)/shard_map/rows/pallas_call | solution.py:451
  24.2 0.1 halo.3
  24.2 3.2 %collective-permute-start.15 = (bf16[3,256,128]{2,1,0:T(8,128)(2,1)S(1)}, bf16[3,256,128]{2,1,0:T(8,128)(2,1)S(1)}, u32[]{:S(2)}, u32[]{:S(2)}) collective-permute-start(bf16[3,256,128]{2,1,0:T(8,128)(2,1)S(1)} %get-tuple-element.64), channel_id=1, source_target_pairs={{8,16},{10,18},{12,20},{14,22},{16,8},{18,10},{20,12},{22,14},{9,1... | collective-permute-start | bytes 589832 | tf_op jit(solution)/shard_map/ppermute | solution.py:386
  27.5 0.1 collective-permute-start.16
  27.5 0.0 collective-permute-done.8.edge_b
  27.5 0.0 collective-permute-done.9.edge_a
  27.6 2.6 %lend.1 = (bf16[3,288,128]{2,1,0:T(8,128)(2,1)S(1)}, bf16[3,288,128]{2,1,0:T(8,128)(2,1)S(1)}, bf16[256,1536]{1,0:T(8,128)(2,1)S(1)}) custom-call(bf16[3,272,128]{2,1,0:T(8,128)(2,1)S(1)} %collective-permute-done.8.edge_b, bf16[3,272,128]{2,1,0:T(8,128)(2,1)S(1)} %collective-permute-done.9.edge_a, bf16[256,1024]{1,0:T(8,128)(2,1)S(1)} %get-tuple-element.58.plane_turned, ...), custom_call_target="tpu_custom_call" | custom-call | flops 4831838208 | bytes 3145728 | tf_op jit(solution)/shard_map/lend/pallas_call | solution.py:462
  30.2 1.5 %collective-permute-start.13 = (bf16[3,288,128]{2,1,0:T(8,128)(2,1)S(1)}, bf16[3,288,128]{2,1,0:T(8,128)(2,1)S(1)}, u32[]{:S(2)}, u32[]{:S(2)}) collective-permute-start(bf16[3,288,128]{2,1,0:T(8,128)(2,1)S(1)} %get-tuple-element.60), channel_id=1, source_target_pairs={{0,8},{2,10},{4,12},{6,14},{8,0},{10,2},{12,4},{14,6},{16,24},{18,... | collective-permute-start | bytes 663560 | tf_op jit(solution)/shard_map/ppermute | solution.py:386
  31.7 2.2 %collective-permute-start.14 = (bf16[3,288,128]{2,1,0:T(8,128)(2,1)S(1)}, bf16[3,288,128]{2,1,0:T(8,128)(2,1)S(1)}, u32[]{:S(2)}, u32[]{:S(2)}) collective-permute-start(bf16[3,288,128]{2,1,0:T(8,128)(2,1)S(1)} %get-tuple-element.61), channel_id=1, source_target_pairs={{8,16},{10,18},{12,20},{14,22},{16,8},{18,10},{20,12},{22,14},{9,1... | collective-permute-start | bytes 663560 | tf_op jit(solution)/shard_map/ppermute | solution.py:386
  33.9 0.0 collective-permute-done.15.refs_12_
  33.9 0.0 collective-permute-done.16.refs_13_
  33.9 3.9 %columns.2 = (bf16[256,128]{1,0:T(8,128)(2,1)S(1)}, bf16[256,128]{1,0:T(8,128)(2,1)S(1)}, bf16[256,128]{1,0:T(8,128)(2,1)S(1)}, bf16[256,1024]{1,0:T(8,128)(2,1)...) custom-call(bf16[528,128]{1,0:T(8,128)(2,1)S(1)} %get-tuple-element.48.refs_4_., ...), custom_call_target="tpu_custom_call" | custom-call | flops 1879048192 | bytes 1572864 | tf_op jit(solution)/shard_map/columns/pallas_call | solution.py:481
  37.9 1.2 %collective-permute-start.21 = (bf16[256,128]{1,0:T(8,128)(2,1)S(1)}, bf16[256,128]{1,0:T(8,128)(2,1)S(1)}, u32[]{:S(2)}, u32[]{:S(2)}) collective-permute-start(bf16[256,128]{1,0:T(8,128)(2,1)S(1)} %get-tuple-element.76), channel_id=1, source_target_pairs={{0,4},{2,6},{4,0},{6,2},{8,12},{10,14},{12,8},{14,10},{16,20},{18,... | collective-permute-start | bytes 196616 | tf_op jit(solution)/shard_map/ppermute | solution.py:381
  39.1 2.5 %collective-permute-start.22 = (bf16[256,128]{1,0:T(8,128)(2,1)S(1)}, bf16[256,128]{1,0:T(8,128)(2,1)S(1)}, u32[]{:S(2)}, u32[]{:S(2)}) collective-permute-start(bf16[256,128]{1,0:T(8,128)(2,1)S(1)} %get-tuple-element.77), channel_id=1, source_target_pairs={{0,6},{2,4},{4,2},{6,0},{8,14},{10,12},{12,10},{14,8},{16,22},{18,... | collective-permute-start | bytes 196616 | tf_op jit(solution)/shard_map/ppermute | solution.py:381
  41.5 0.0 collective-permute-start.20
  41.6 0.0 collective-permute-done.13.back_a
  41.6 0.0 collective-permute-done.14.back_b
  41.6 0.6 %merge.1 = (bf16[256,128]{1,0:T(8,128)(2,1)S(1)}, bf16[256,128]{1,0:T(8,128)(2,1)S(1)}, bf16[256,128]{1,0:T(8,128)(2,1)S(1)}, bf16[256,128]{1,0:T(8,128)(2,1)S(1)}) custom-call(bf16[3,288,128]{2,1,0:T(8,128)(2,1)S(1)} %collective-permute-done.13.back_a, bf16[3,288,128]{2,1,0:T(8,128)(2,1)S(1)} %collective-permute-done.14.back_b, ...), custom_call_target="tpu_custom_call" | custom-call | bytes 2097152 | tf_op jit(solution)/shard_map/merge/pallas_call | solution.py:484
  42.2 0.6 %collective-permute-start.17 = (bf16[256,128]{1,0:T(8,128)(2,1)S(1)}, bf16[256,128]{1,0:T(8,128)(2,1)S(1)}, u32[]{:S(2)}, u32[]{:S(2)}) collective-permute-start(bf16[256,128]{1,0:T(8,128)(2,1)S(1)} %get-tuple-element.69), channel_id=1, source_target_pairs={{0,2},{2,0},{4,6},{6,4},{8,10},{10,8},{12,14},{14,12},{16,18},{18,... | collective-permute-start | bytes 196616 | tf_op jit(solution)/shard_map/ppermute | solution.py:381
  42.7 1.0 %collective-permute-start.18 = (bf16[256,128]{1,0:T(8,128)(2,1)S(1)}, bf16[256,128]{1,0:T(8,128)(2,1)S(1)}, u32[]{:S(2)}, u32[]{:S(2)}) collective-permute-start(bf16[256,128]{1,0:T(8,128)(2,1)S(1)} %get-tuple-element.70), channel_id=1, source_target_pairs={{0,4},{2,6},{4,0},{6,2},{8,12},{10,14},{12,8},{14,10},{16,20},{18,... | collective-permute-start | bytes 196616 | tf_op jit(solution)/shard_map/ppermute | solution.py:381
  43.8 0.0 collective-permute-done.21.refs_6_
  43.8 1.9 %collective-permute-start.19 = (bf16[256,128]{1,0:T(8,128)(2,1)S(1)}, bf16[256,128]{1,0:T(8,128)(2,1)S(1)}, u32[]{:S(2)}, u32[]{:S(2)}) collective-permute-start(bf16[256,128]{1,0:T(8,128)(2,1)S(1)} %get-tuple-element.71), channel_id=1, source_target_pairs={{0,6},{2,4},{4,2},{6,0},{8,14},{10,12},{12,10},{14,8},{16,22},{18,... | collective-permute-start | bytes 196616 | tf_op jit(solution)/shard_map/ppermute | solution.py:381
  45.6 0.0 collective-permute-done.22.refs_7_
  45.6 0.0 collective-permute-done.20.refs_5_
  45.7 2.8 %columns.3 = bf16[256,512]{1,0:T(8,128)(2,1)} custom-call(bf16[256,1536]{1,0:T(8,128)(2,1)S(1)} %get-tuple-element.66.refs_14_.refs_0_, bf16[256,1024]{1,0:T(8,128)(2,1)S(1)} %get-tuple-element.72.refs_1_, bf16[1024,256]{1,0:T(8,128)(2,1)S(1)} %get-tuple-element.73.refs_2_, bf16[4,512,256]{2,1,0:T(8,128)(2,1)S(1)} %get-tuple-element.74.refs_3_, ...), custom_call_target="tpu_custom_call" | custom-call | flops 1879048192 | bytes 1572864 | tf_op jit(solution)/shard_map/columns/pallas_call | solution.py:495
  48.5 0.0 collective-permute-done.17.refs_1_
  48.5 0.0 collective-permute-done.18.refs_2_
  48.5 0.0 collective-permute-done.19.refs_3_
  48.5 0.7 %join.1 = bf16[256,512]{1,0:T(8,128)(2,1)} custom-call(bf16[256,128]{1,0:T(8,128)(2,1)S(1)} %get-tuple-element.68.refs_0_.refs_8_, bf16[256,128]{1,0:T(8,128)(2,1)S(1)} %collective-permute-done.17.refs_1_, bf16[256,128]{1,0:T(8,128)(2,1)S(1)} %collective-permute-done.18.refs_2_, bf16[256,128]{1,0:T(8,128)(2,1)S(1)} %collective-permute-done.19.refs_3_), custom_call_target="tpu_custom_call" | custom-call | bytes 524288 | tf_op jit(solution)/shard_map/join/pallas_call | solution.py:505
Async XLA Ops:
  0.6 9.2 %collective-permute-start.1 = (bf16[256,512]{1,0:T(8,128)(2,1)}, bf16[256,512]{1,0:T(8,128)(2,1)S(1)}, u32[]{:S(2)}, u32[]{:S(2)}) collective-permute-start(bf16[256,512]{1,0:T(8,128)(2,1)} %audio.3), channel_id=1, source_target_pairs={{0,1},{1,0},{2,3},{3,2},{4,5},{5,4},{6,7},{7,6},{8,9},{9,8},{10,11... | collective-permute-start | bytes 786440 | tf_op jit(solution)/shard_map/ppermute | solution.py:377
  1.9 11.8 %collective-permute-start.7 = (bf16[256,512]{1,0:T(8,128)(2,1)}, bf16[256,512]{1,0:T(8,128)(2,1)S(1)}, u32[]{:S(2)}, u32[]{:S(2)}) collective-permute-start(bf16[256,512]{1,0:T(8,128)(2,1)} %video.3), channel_id=1, source_target_pairs={{0,1},{1,0},{2,3},{3,2},{4,5},{5,4},{6,7},{7,6},{8,9},{9,8},{10,11... | collective-permute-start | bytes 786440 | tf_op jit(solution)/shard_map/ppermute | solution.py:377
  3.3 3.0 %collective-permute-start = (bf16[528,128]{1,0:T(8,128)(2,1)S(1)}, bf16[528,128]{1,0:T(8,128)(2,1)S(1)}, u32[]{:S(2)}, u32[]{:S(2)}) collective-permute-start(bf16[528,128]{1,0:T(8,128)(2,1)S(1)} %get-tuple-element.40), channel_id=1, source_target_pairs={{0,2},{2,0},{4,6},{6,4},{8,10},{10,8},{12,14},{14,12},{16,18},{18,... | collective-permute-start | bytes 405512 | tf_op jit(solution)/shard_map/ppermute | solution.py:381
  4.6 5.2 %collective-permute-start.2 = (bf16[528,128]{1,0:T(8,128)(2,1)S(1)}, bf16[528,128]{1,0:T(8,128)(2,1)S(1)}, u32[]{:S(2)}, u32[]{:S(2)}) collective-permute-start(bf16[528,128]{1,0:T(8,128)(2,1)S(1)} %get-tuple-element.43), channel_id=1, source_target_pairs={{0,4},{2,6},{4,0},{6,2},{8,12},{10,14},{12,8},{14,10},{16,20},{18,... | collective-permute-start | bytes 405512 | tf_op jit(solution)/shard_map/ppermute | solution.py:381
  5.9 9.8 %collective-permute-start.6 = (bf16[528,128]{1,0:T(8,128)(2,1)S(1)}, bf16[528,128]{1,0:T(8,128)(2,1)S(1)}, u32[]{:S(2)}, u32[]{:S(2)}) collective-permute-start(bf16[528,128]{1,0:T(8,128)(2,1)S(1)} %get-tuple-element.49), channel_id=1, source_target_pairs={{0,6},{2,4},{4,2},{6,0},{8,14},{10,12},{12,10},{14,8},{16,22},{18,... | collective-permute-start | bytes 405512 | tf_op jit(solution)/shard_map/ppermute | solution.py:381
  10.2 6.7 %collective-permute-start.3 = (bf16[256,128]{1,0:T(8,128)(2,1)S(1)}, bf16[256,128]{1,0:T(8,128)(2,1)S(1)}, u32[]{:S(2)}, u32[]{:S(2)}) collective-permute-start(bf16[256,128]{1,0:T(8,128)(2,1)S(1)} %get-tuple-element.45), channel_id=1, source_target_pairs={{0,2},{2,0},{4,6},{6,4},{8,10},{10,8},{12,14},{14,12},{16,18},{18,... | collective-permute-start | bytes 196616 | tf_op jit(solution)/shard_map/ppermute | solution.py:381
  11.6 5.9 %collective-permute-start.4 = (bf16[256,128]{1,0:T(8,128)(2,1)S(1)}, bf16[256,128]{1,0:T(8,128)(2,1)S(1)}, u32[]{:S(2)}, u32[]{:S(2)}) collective-permute-start(bf16[256,128]{1,0:T(8,128)(2,1)S(1)} %get-tuple-element.46), channel_id=1, source_target_pairs={{0,4},{2,6},{4,0},{6,2},{8,12},{10,14},{12,8},{14,10},{16,20},{18,... | collective-permute-start | bytes 196616 | tf_op jit(solution)/shard_map/ppermute | solution.py:381
  12.8 4.6 %collective-permute-start.5 = (bf16[256,128]{1,0:T(8,128)(2,1)S(1)}, bf16[256,128]{1,0:T(8,128)(2,1)S(1)}, u32[]{:S(2)}, u32[]{:S(2)}) collective-permute-start(bf16[256,128]{1,0:T(8,128)(2,1)S(1)} %get-tuple-element.47), channel_id=1, source_target_pairs={{0,6},{2,4},{4,2},{6,0},{8,14},{10,12},{12,10},{14,8},{16,22},{18,... | collective-permute-start | bytes 196616 | tf_op jit(solution)/shard_map/ppermute | solution.py:381
  14.1 6.7 %collective-permute-start.10 = (bf16[256,128]{1,0:T(8,128)(2,1)S(1)}, bf16[256,128]{1,0:T(8,128)(2,1)S(1)}, u32[]{:S(2)}, u32[]{:S(2)}) collective-permute-start(bf16[256,128]{1,0:T(8,128)(2,1)S(1)} %get-tuple-element.55), channel_id=1, source_target_pairs={{0,2},{2,0},{4,6},{6,4},{8,10},{10,8},{12,14},{14,12},{16,18},{18,... | collective-permute-start | bytes 196616 | tf_op jit(solution)/shard_map/ppermute | solution.py:381
  15.7 5.1 %collective-permute-start.11 = (bf16[256,128]{1,0:T(8,128)(2,1)S(1)}, bf16[256,128]{1,0:T(8,128)(2,1)S(1)}, u32[]{:S(2)}, u32[]{:S(2)}) collective-permute-start(bf16[256,128]{1,0:T(8,128)(2,1)S(1)} %get-tuple-element.56), channel_id=1, source_target_pairs={{0,4},{2,6},{4,0},{6,2},{8,12},{10,14},{12,8},{14,10},{16,20},{18,... | collective-permute-start | bytes 196616 | tf_op jit(solution)/shard_map/ppermute | solution.py:381
  16.9 4.1 %collective-permute-start.12 = (bf16[256,128]{1,0:T(8,128)(2,1)S(1)}, bf16[256,128]{1,0:T(8,128)(2,1)S(1)}, u32[]{:S(2)}, u32[]{:S(2)}) collective-permute-start(bf16[256,128]{1,0:T(8,128)(2,1)S(1)} %get-tuple-element.57), channel_id=1, source_target_pairs={{0,6},{2,4},{4,2},{6,0},{8,14},{10,12},{12,10},{14,8},{16,22},{18,... | collective-permute-start | bytes 196616 | tf_op jit(solution)/shard_map/ppermute | solution.py:381
  17.5 10.0 %collective-permute-start.8 = (bf16[3,272,128]{2,1,0:T(8,128)(2,1)S(1)}, bf16[3,272,128]{2,1,0:T(8,128)(2,1)S(1)}, u32[]{:S(2)}, u32[]{:S(2)}) collective-permute-start(bf16[3,272,128]{2,1,0:T(8,128)(2,1)S(1)} %get-tuple-element.53), channel_id=1, source_target_pairs={{8,16},{10,18},{12,20},{14,22},{16,8},{18,10},{20,12},{22,14},{9,1... | collective-permute-start | bytes 626696 | tf_op jit(solution)/shard_map/ppermute | solution.py:386
  20.7 6.8 %collective-permute-start.9 = (bf16[3,272,128]{2,1,0:T(8,128)(2,1)S(1)}, bf16[3,272,128]{2,1,0:T(8,128)(2,1)S(1)}, u32[]{:S(2)}, u32[]{:S(2)}) collective-permute-start(bf16[3,272,128]{2,1,0:T(8,128)(2,1)S(1)} %get-tuple-element.54), channel_id=1, source_target_pairs={{0,8},{2,10},{4,12},{6,14},{8,0},{10,2},{12,4},{14,6},{16,24},{18,... | collective-permute-start | bytes 626696 | tf_op jit(solution)/shard_map/ppermute | solution.py:386
  24.2 9.7 %collective-permute-start.15 = (bf16[3,256,128]{2,1,0:T(8,128)(2,1)S(1)}, bf16[3,256,128]{2,1,0:T(8,128)(2,1)S(1)}, u32[]{:S(2)}, u32[]{:S(2)}) collective-permute-start(bf16[3,256,128]{2,1,0:T(8,128)(2,1)S(1)} %get-tuple-element.64), channel_id=1, source_target_pairs={{8,16},{10,18},{12,20},{14,22},{16,8},{18,10},{20,12},{22,14},{9,1... | collective-permute-start | bytes 589832 | tf_op jit(solution)/shard_map/ppermute | solution.py:386
  27.5 6.5 %collective-permute-start.16 = (bf16[3,256,128]{2,1,0:T(8,128)(2,1)S(1)}, bf16[3,256,128]{2,1,0:T(8,128)(2,1)S(1)}, u32[]{:S(2)}, u32[]{:S(2)}) collective-permute-start(bf16[3,256,128]{2,1,0:T(8,128)(2,1)S(1)} %get-tuple-element.65), channel_id=1, source_target_pairs={{0,8},{2,10},{4,12},{6,14},{8,0},{10,2},{12,4},{14,6},{16,24},{18,... | collective-permute-start | bytes 589832 | tf_op jit(solution)/shard_map/ppermute | solution.py:386
  30.2 11.4 %collective-permute-start.13 = (bf16[3,288,128]{2,1,0:T(8,128)(2,1)S(1)}, bf16[3,288,128]{2,1,0:T(8,128)(2,1)S(1)}, u32[]{:S(2)}, u32[]{:S(2)}) collective-permute-start(bf16[3,288,128]{2,1,0:T(8,128)(2,1)S(1)} %get-tuple-element.60), channel_id=1, source_target_pairs={{0,8},{2,10},{4,12},{6,14},{8,0},{10,2},{12,4},{14,6},{16,24},{18,... | collective-permute-start | bytes 663560 | tf_op jit(solution)/shard_map/ppermute | solution.py:386
  31.7 9.9 %collective-permute-start.14 = (bf16[3,288,128]{2,1,0:T(8,128)(2,1)S(1)}, bf16[3,288,128]{2,1,0:T(8,128)(2,1)S(1)}, u32[]{:S(2)}, u32[]{:S(2)}) collective-permute-start(bf16[3,288,128]{2,1,0:T(8,128)(2,1)S(1)} %get-tuple-element.61), channel_id=1, source_target_pairs={{8,16},{10,18},{12,20},{14,22},{16,8},{18,10},{20,12},{22,14},{9,1... | collective-permute-start | bytes 663560 | tf_op jit(solution)/shard_map/ppermute | solution.py:386
  37.9 5.9 %collective-permute-start.21 = (bf16[256,128]{1,0:T(8,128)(2,1)S(1)}, bf16[256,128]{1,0:T(8,128)(2,1)S(1)}, u32[]{:S(2)}, u32[]{:S(2)}) collective-permute-start(bf16[256,128]{1,0:T(8,128)(2,1)S(1)} %get-tuple-element.76), channel_id=1, source_target_pairs={{0,4},{2,6},{4,0},{6,2},{8,12},{10,14},{12,8},{14,10},{16,20},{18,... | collective-permute-start | bytes 196616 | tf_op jit(solution)/shard_map/ppermute | solution.py:381
  39.1 6.6 %collective-permute-start.22 = (bf16[256,128]{1,0:T(8,128)(2,1)S(1)}, bf16[256,128]{1,0:T(8,128)(2,1)S(1)}, u32[]{:S(2)}, u32[]{:S(2)}) collective-permute-start(bf16[256,128]{1,0:T(8,128)(2,1)S(1)} %get-tuple-element.77), channel_id=1, source_target_pairs={{0,6},{2,4},{4,2},{6,0},{8,14},{10,12},{12,10},{14,8},{16,22},{18,... | collective-permute-start | bytes 196616 | tf_op jit(solution)/shard_map/ppermute | solution.py:381
  41.5 4.1 %collective-permute-start.20 = (bf16[256,128]{1,0:T(8,128)(2,1)S(1)}, bf16[256,128]{1,0:T(8,128)(2,1)S(1)}, u32[]{:S(2)}, u32[]{:S(2)}) collective-permute-start(bf16[256,128]{1,0:T(8,128)(2,1)S(1)} %get-tuple-element.67.refs_0_), channel_id=1, source_target_pairs={{0,2},{2,0},{4,6},{6,4},{8,10},{10,8},{12,14},{14,12},{16,18},{18,... | collective-permute-start | bytes 196616 | tf_op jit(solution)/shard_map/ppermute | solution.py:381
  42.2 6.3 %collective-permute-start.17 = (bf16[256,128]{1,0:T(8,128)(2,1)S(1)}, bf16[256,128]{1,0:T(8,128)(2,1)S(1)}, u32[]{:S(2)}, u32[]{:S(2)}) collective-permute-start(bf16[256,128]{1,0:T(8,128)(2,1)S(1)} %get-tuple-element.69), channel_id=1, source_target_pairs={{0,2},{2,0},{4,6},{6,4},{8,10},{10,8},{12,14},{14,12},{16,18},{18,... | collective-permute-start | bytes 196616 | tf_op jit(solution)/shard_map/ppermute | solution.py:381
  42.7 5.8 %collective-permute-start.18 = (bf16[256,128]{1,0:T(8,128)(2,1)S(1)}, bf16[256,128]{1,0:T(8,128)(2,1)S(1)}, u32[]{:S(2)}, u32[]{:S(2)}) collective-permute-start(bf16[256,128]{1,0:T(8,128)(2,1)S(1)} %get-tuple-element.70), channel_id=1, source_target_pairs={{0,4},{2,6},{4,0},{6,2},{8,12},{10,14},{12,8},{14,10},{16,20},{18,... | collective-permute-start | bytes 196616 | tf_op jit(solution)/shard_map/ppermute | solution.py:381
  43.8 4.7 %collective-permute-start.19 = (bf16[256,128]{1,0:T(8,128)(2,1)S(1)}, bf16[256,128]{1,0:T(8,128)(2,1)S(1)}, u32[]{:S(2)}, u32[]{:S(2)}) collective-permute-start(bf16[256,128]{1,0:T(8,128)(2,1)S(1)} %get-tuple-element.71), channel_id=1, source_target_pairs={{0,6},{2,4},{4,2},{6,0},{8,14},{10,12},{12,10},{14,8},{16,22},{18,... | collective-permute-start | bytes 196616 | tf_op jit(solution)/shard_map/ppermute | solution.py:381

commit v17 on v15

--- a/solution.py
+++ b/solution.py
@@ -27,12 +27,13 @@
     return lax.axis_index("tm") // GROUP
 
 
-def call(kernel, outs, scratch=(), ins=None, outs_in=None, flops=0, moved=0, exps=0, name=None):
+def call(kernel, outs, scratch=(), ins=None, outs_in=None, aliases=None, flops=0, moved=0, exps=0, name=None):
     return pl.pallas_call(
         kernel,
         out_shape=outs,
         **({"in_specs": ins} if ins else {}),
         **({"out_specs": outs_in} if outs_in else {}),
+        input_output_aliases=aliases or {},
         scratch_shapes=scratch,
         compiler_params=pltpu.CompilerParams(vmem_limit_bytes=32 * 2**20),
         cost_estimate=pl.CostEstimate(flops=flops, bytes_accessed=moved, transcendentals=exps),
@@ -120,12 +121,13 @@
 
 
 def join_kernel(*refs):
-    pieces, out, sems = refs[:GROUP], refs[GROUP], refs[GROUP + 1]
-    width = pieces[0].shape[1]
+    audio, video, (_, audio_out, video_out, sems) = refs[:GROUP], refs[GROUP:-4], refs[-4:]
+    width = audio[0].shape[1]
     mine = place()
     copies, fetch = fetcher(sems)
-    for k in range(GROUP):
-        fetch(pieces[k], out.at[:, pl.ds(pl.multiple_of((mine ^ k) * width, width), width)])
+    for pieces, out in ((audio, audio_out), (video, video_out)):
+        for k, piece in enumerate(pieces):
+            fetch(piece, out.at[:, pl.ds(pl.multiple_of((mine ^ k) * width, width), width)])
     for copy in copies:
         copy.wait()
 
@@ -216,7 +218,7 @@
         peaks[b] = jnp.broadcast_to(peak, (peak.shape[0], width))
 
 
-def lend_kernel(edge_b, edge_a, plane_turned, plane_beside, first, second, turned, ordered, results):
+def lend_kernel(edge_b, edge_a, plane_turned, plane_beside, first, second, ordered, results):
     rows, width = ordered.shape[2] - ID_ROWS, ordered.shape[3]
     odd = lax.rem(plane(), 2)
     ordered[1 - odd] = edge_a[...]
@@ -229,10 +231,6 @@
         side, j = e // RADIUS, e % RADIUS
         marks = marks_turned(ordered[side, j, rows:])
         query = ordered[side, j, :rows]
-        for part, x in enumerate(marks):
-            at = slice(e * rows + part * width, e * rows + (part + 1) * width)
-            turned[:width, at] = jnp.transpose(query[part * width : (part + 1) * width])
-            turned[width:, at] = x
         return product(stacked_ask(query, marks), plane_turned[:, blocks[e]])
 
     ahead = scores_of(0)
@@ -266,12 +264,13 @@
     take = lambda count: [refs.pop(0) for _ in range(count)]
     first = 0 not in receivers
     if first:
-        packs, queries, keys, (edge_b, edge_a) = take(GROUP), take(GROUP), take(GROUP), take(2)
-    (edge_turned,) = take(1)
-    if not first:
-        shared, _ = take(4), take(1)
-    outs = take(len(receivers))
-    turned, beside, asks, edge_beside = take(4) if first else shared
+        packs, queries, keys = take(GROUP), take(GROUP), take(GROUP)
+        (ask_b, ask_a), (edge_b, edge_a) = take(2), take(2)
+        outs = take(len(receivers))
+        turned, beside, asks, edge_beside, edge_turned = take(5)
+    else:
+        turned, beside, asks, edge_beside, edge_turned = take(5)
+        received, _, outs, (whole,), (sems,) = take(len(receivers)), take(1), take(len(receivers)), take(1), take(1)
     rows, width = outs[0].shape
     mine = place()
     if first:
@@ -286,10 +285,24 @@
             asks,
         )
         edge_beside[:, width:] = jnp.ones((edge_beside.shape[0], width), beside.dtype)
-        for edge, base in ((edge_a, RADIUS * (1 - odd)), (edge_b, RADIUS * odd)):
+        for ask, edge, base in ((ask_a, edge_a, RADIUS * (1 - odd)), (ask_b, edge_b, RADIUS * odd)):
             for j in range(RADIUS):
-                at = pl.ds(pl.multiple_of((base + j) * rows, rows), rows)
-                edge_beside[at, :width] = edge[j]
+
+                def spot(at, size):
+                    return pl.ds(pl.multiple_of((base + j) * rows + at, size), size)
+
+                edge_beside[spot(0, rows), :width] = edge[j]
+                for part, x in enumerate(marks_turned(ask[j, rows:])):
+                    at = spot(part * width, width)
+                    edge_turned[:width, at] = jnp.transpose(
+                        ask[j, part * width : (part + 1) * width]
+                    )
+                    edge_turned[width:, at] = x
+    else:
+        copies, fetch = fetcher(sems)
+        for n, k in enumerate(range(GROUP - len(receivers), GROUP)):
+            at = pl.ds(pl.multiple_of((mine ^ k) * width, width), width)
+            fetch(received[n], whole.at[:, at])
     near = [pl.ds(pl.multiple_of((mine ^ k) * rows, rows), RADIUS * rows) for k in receivers]
 
     def scores_of(n):
@@ -304,6 +317,9 @@
         _, mixed = attend(scores, [beside[...], edge_beside[near[n]]])
         mean = by_head(mixed[:, :width], rows) / by_head(mixed[:, width:], rows)
         outs[n][...] = mean.astype(outs[n].dtype)
+    if not first:
+        for copy in copies:
+            copy.wait()
 
 
 def merge_kernel(back_a, back_b, peaks, sums, *refs):
@@ -368,7 +384,9 @@
 
     def traded(pieces):
         pairs = lambda k: [(i, i ^ k) for i in range(length)]
-        return [pieces[0]] + [lax.ppermute(pieces[k], "tm", pairs(k)) for k in range(1, GROUP)]
+        return [
+            lax.ppermute(x, "tm", pairs(k)) if k and x is not None else x for k, x in enumerate(pieces)
+        ]
 
     def crossed(sent, second):
         planes = range(second, length // GROUP - second)
@@ -449,9 +467,9 @@
     )(*packs, *queries, *keys)
     audio_edges = halo(packs, [], peaks)
     back = shape((RADIUS, rows + rows // width * STAT_ROWS, width), bf16)
-    lent_a, lent_b, edge_turned = call(
+    lent_a, lent_b = call(
         lend_kernel,
-        [back, back, shape((2 * width, around), bf16)],
+        [back, back],
         [pltpu.VMEM((2, RADIUS, rows + ID_ROWS, width), bf16), pltpu.VMEM((2,) + back.shape, bf16)],
         flops=48 * RADIUS * GROUP * rows * rows * width,
         moved=8 * around * width * 2,
@@ -466,11 +484,11 @@
         exps=7 * GROUP * rows * rows,
         name="columns",
     )
-    shared = [turned, beside, asks, shape((around, 2 * width), bf16)]
+    shared = [turned, beside, asks, shape((around, 2 * width), bf16), shape((2 * width, around), bf16)]
     near, far = range(GROUP // 2), range(GROUP // 2, GROUP)
-    *far_pieces, turned, beside, asks, edge_beside = call(
+    *far_pieces, turned, beside, asks, edge_beside, edge_turned = call(
         functools.partial(columns_kernel, far), [piece] * len(far) + shared, **half_columns
-    )(*packs, *queries, *keys, *audio_edges[::-1], edge_turned)
+    )(*packs, *queries, *keys, *query_edges[::-1], *audio_edges[::-1])
     audio_pieces = call(
         merge_kernel,
         [piece] * GROUP,
@@ -481,26 +499,27 @@
         name="merge",
     )(*backs, peaks, sums, far_pieces[0])
     audio_pieces = traded(audio_pieces)
-    near_pieces = call(
+    received = traded([None, None, *far_pieces])[2:]
+    whole = shape((rows, half), bf16)
+    *near_pieces, partial = call(
         functools.partial(columns_kernel, near),
-        [piece] * len(near),
-        ins=[VMEM] * 5 + [ANY],
+        [piece] * len(near) + [whole],
+        [pltpu.SemaphoreType.DMA((len(far),))],
+        ins=[VMEM] * (5 + len(far)) + [ANY],
+        outs_in=[VMEM] * len(near) + [HBM],
         **half_columns,
-    )(edge_turned, turned, beside, asks, edge_beside, audio_pieces[0])
-    video_pieces = traded([*near_pieces, *far_pieces])
-
-    def join(pieces):
-        return call(
-            join_kernel,
-            shape((rows, half), bf16),
-            [pltpu.SemaphoreType.DMA((GROUP,))],
-            outs_in=HBM,
-            moved=2 * rows * half * 2,
-            name="join",
-        )(*pieces)
-
-    video_attended = join(video_pieces)
-    audio_attended = join(audio_pieces)
+    )(turned, beside, asks, edge_beside, edge_turned, *received, audio_pieces[0])
+    near_pieces = traded(near_pieces)
+    audio_attended, video_attended = call(
+        join_kernel,
+        [whole, whole],
+        [pltpu.SemaphoreType.DMA((GROUP + len(near),))],
+        ins=[VMEM] * (GROUP + len(near)) + [HBM],
+        outs_in=[HBM, HBM],
+        aliases={GROUP + len(near): 1},
+        moved=4 * rows * half * 2,
+        name="join",
+    )(*audio_pieces, *near_pieces, partial)
     return (audio_attended, video_attended)
 
 

time: 49.2 us -> 49.5 us (level)
    pallas_call x4 -> x3, Pallas kernels: 6.35 us -> 5.9 us  [the longest x1 2.58 us: local(): call(functools.partial(columns_kernel, near), [piece] * len(near) + [whol...]
  transfers between devices with their start and end apart: 23 -> 23, of which waited for: 4 -> 6; matrix products, arithmetic and copies ran while one was open for 0% -> 0% of each run, Pallas kernels for 32% -> 32%
where the time goes in v17:
time: 49.5 us; the launch traced here: 49 us
  starting transfers between devices  28.1 us (57%)
  Pallas kernels  16.5 us (33%)
  waiting for transfers between devices  3.45 us (7%)
  between operations  0.97 us (2%)
    ppermute x15, starting transfers between devices, traded(): lax.ppermute(x, 'tm', pairs(k))  16.3 us
    ppermute x6, starting transfers between devices, crossed(): lax.ppermute(sent, 'tm', [(p * GROUP + i, q * GROUP + i) for p, q in pair...  10.3 us
    pallas_call x1, Pallas kernels, local(): call(rows_kernel, [shape((GROUP, heads * rows, n * width), f32) for n in...  3.35 us
    ppermute x15, waiting for transfers between devices, traded(): lax.ppermute(x, 'tm', pairs(k))  2.99 us
    pallas_call x1, Pallas kernels, local(): call(functools.partial(columns_kernel, far), [piece] * len(far) + shared,...  2.8 us
    pallas_call x1, Pallas kernels, local(): call(functools.partial(columns_kernel, near), [piece] * len(near) + [whol...  2.58 us
    pallas_call x1, Pallas kernels, local(): call(lend_kernel, [back, back], [pltpu.VMEM((2, RADIUS, rows + ID_ROWS, w...  2.53 us
    pallas_call x1, Pallas kernels, local(): call(prepare_kernel, [part, part, square, square], [pltpu.VMEM((rows, hal...  1.78 us
  transfers between devices with their start and end apart: 23, of which 6 were waited for; matrix products, arithmetic and copies ran while one was open for 0% of the time, Pallas kernels for 32%

profile of v17, /device:TPU:9, one launch (start us, length us, event | category | flops | bytes accessed | tf_op | source)
XLA Modules:
  0.0 49.0 jit_solution(15126857584039871712)
XLA Ops:
  0.6 1.3 %collective-permute-start.1 = (bf16[256,512]{1,0:T(8,128)(2,1)}, bf16[256,512]{1,0:T(8,128)(2,1)S(1)}, u32[]{:S(2)}, u32[]{:S(2)}) collective-permute-start(bf16[256,512]{1,0:T(8,128)(2,1)} %audio.3), channel_id=1, source_target_pairs={{0,1},{1,0},{2,3},{3,2},{4,5},{5,4},{6,7},{7,6},{8,9},{9,8},{10,11... | collective-permute-start | bytes 786440 | tf_op jit(solution)/shard_map/ppermute | solution.py:383
  1.9 0.2 collective-permute-start.7
  2.2 1.2 %split.1 = (bf16[528,128]{1,0:T(8,128)(2,1)S(1)}, bf16[528,128]{1,0:T(8,128)(2,1)S(1)}, bf16[528,128]{1,0:T(8,128)(2,1)S(1)}, bf16[528,128]{1,0:T(8,128)(2,1)S(1)}) custom-call(bf16[256,512]{1,0:T(8,128)(2,1)} %audio.3, bf16[256,512]{1,0:T(8,128)(2,1)} %video.3, s32[2,128]{1,0:T(2,128)} %bitcast.1), custom_call_target="tpu_custom_call" | custom-call | bytes 1048576 | tf_op jit(solution)/shard_map/split/pallas_call | solution.py:407
  3.3 1.3 %collective-permute-start = (bf16[528,128]{1,0:T(8,128)(2,1)S(1)}, bf16[528,128]{1,0:T(8,128)(2,1)S(1)}, u32[]{:S(2)}, u32[]{:S(2)}) collective-permute-start(bf16[528,128]{1,0:T(8,128)(2,1)S(1)} %get-tuple-element.42), channel_id=1, source_target_pairs={{0,2},{2,0},{4,6},{6,4},{8,10},{10,8},{12,14},{14,12},{16,18},{18,... | collective-permute-start | bytes 405512 | tf_op jit(solution)/shard_map/ppermute | solution.py:388
  4.6 1.2 %collective-permute-start.2 = (bf16[528,128]{1,0:T(8,128)(2,1)S(1)}, bf16[528,128]{1,0:T(8,128)(2,1)S(1)}, u32[]{:S(2)}, u32[]{:S(2)}) collective-permute-start(bf16[528,128]{1,0:T(8,128)(2,1)S(1)} %get-tuple-element.45), channel_id=1, source_target_pairs={{0,4},{2,6},{4,0},{6,2},{8,12},{10,14},{12,8},{14,10},{16,20},{18,... | collective-permute-start | bytes 405512 | tf_op jit(solution)/shard_map/ppermute | solution.py:388
  5.9 0.5 collective-permute-start.6
  6.3 0.0 collective-permute-done.refs_0_.refs_5_.refs_1_
  6.3 1.8 %prepare.1 = (f32[256,512]{1,0:T(8,128)S(1)}, f32[256,512]{1,0:T(8,128)S(1)}, bf16[512,512]{1,0:T(8,128)(2,1)S(1)}, bf16[512,512]{1,0:T(8,128)(2,1)S(1)}) custom-call(bf16[256,512]{1,0:T(8,128)(2,1)} %audio.3, bf16[256,512]{1,0:T(8,128)(2,1)} %video.3, bf16[1024,512]{1,0:T(8,128)(2,1)} %query.1, bf16[1024,512]{1,0:T(8,128)(2,1)} %key.1, ...), custom_call_target="tpu_custom_call" | custom-call | flops 268435456 | bytes 4194304 | tf_op jit(solution)/shard_map/prepare/pallas_call | solution.py:417
  8.1 1.7 %collective-permute-done.2.refs_1_.refs_6_.refs_2_ = bf16[528,128]{1,0:T(8,128)(2,1)S(1)} collective-permute-done((bf16[528,128]{1,0:T(8,128)(2,1)S(1)}, bf16[528,128]{1,0:T(8,128)(2,1)S(1)}, u32[]{:S(2)}, u32[]{:S(2)}) %collective-permute-start.2) | collective-permute-done | bytes 135200 | tf_op jit(solution)/shard_map/ppermute | solution.py:388
  9.8 0.0 collective-permute-done.1.other
  9.8 0.4 project.2
  10.2 1.4 %collective-permute-start.3 = (bf16[256,128]{1,0:T(8,128)(2,1)S(1)}, bf16[256,128]{1,0:T(8,128)(2,1)S(1)}, u32[]{:S(2)}, u32[]{:S(2)}) collective-permute-start(bf16[256,128]{1,0:T(8,128)(2,1)S(1)} %get-tuple-element.47), channel_id=1, source_target_pairs={{0,2},{2,0},{4,6},{6,4},{8,10},{10,8},{12,14},{14,12},{16,18},{18,... | collective-permute-start | bytes 196616 | tf_op jit(solution)/shard_map/ppermute | solution.py:388
  11.6 1.2 %collective-permute-start.4 = (bf16[256,128]{1,0:T(8,128)(2,1)S(1)}, bf16[256,128]{1,0:T(8,128)(2,1)S(1)}, u32[]{:S(2)}, u32[]{:S(2)}) collective-permute-start(bf16[256,128]{1,0:T(8,128)(2,1)S(1)} %get-tuple-element.48), channel_id=1, source_target_pairs={{0,4},{2,6},{4,0},{6,2},{8,12},{10,14},{12,8},{14,10},{16,20},{18,... | collective-permute-start | bytes 196616 | tf_op jit(solution)/shard_map/ppermute | solution.py:388
  12.8 0.5 collective-permute-start.5
  13.3 0.4 collective-permute-done.7.other
  13.7 0.4 project.3
  14.1 1.6 %collective-permute-start.10 = (bf16[256,128]{1,0:T(8,128)(2,1)S(1)}, bf16[256,128]{1,0:T(8,128)(2,1)S(1)}, u32[]{:S(2)}, u32[]{:S(2)}) collective-permute-start(bf16[256,128]{1,0:T(8,128)(2,1)S(1)} %get-tuple-element.57), channel_id=1, source_target_pairs={{0,2},{2,0},{4,6},{6,4},{8,10},{10,8},{12,14},{14,12},{16,18},{18,... | collective-permute-start | bytes 196616 | tf_op jit(solution)/shard_map/ppermute | solution.py:388
  15.7 0.0 collective-permute-done.6.refs_7_.refs_3_
  15.7 1.2 %collective-permute-start.11 = (bf16[256,128]{1,0:T(8,128)(2,1)S(1)}, bf16[256,128]{1,0:T(8,128)(2,1)S(1)}, u32[]{:S(2)}, u32[]{:S(2)}) collective-permute-start(bf16[256,128]{1,0:T(8,128)(2,1)S(1)} %get-tuple-element.58), channel_id=1, source_target_pairs={{0,4},{2,6},{4,0},{6,2},{8,12},{10,14},{12,8},{14,10},{16,20},{18,... | collective-permute-start | bytes 196616 | tf_op jit(solution)/shard_map/ppermute | solution.py:388
  16.9 0.0 collective-permute-done.3.refs_1_.refs_5_
  16.9 0.5 collective-permute-start.12
  17.4 0.0 collective-permute-done.4.refs_2_.refs_6_
  17.4 0.0 collective-permute-done.5.refs_3_.refs_7_
  17.4 0.1 halo.2
  17.5 3.2 %collective-permute-start.8 = (bf16[3,272,128]{2,1,0:T(8,128)(2,1)S(1)}, bf16[3,272,128]{2,1,0:T(8,128)(2,1)S(1)}, u32[]{:S(2)}, u32[]{:S(2)}) collective-permute-start(bf16[3,272,128]{2,1,0:T(8,128)(2,1)S(1)} %get-tuple-element.55), channel_id=1, source_target_pairs={{8,16},{10,18},{12,20},{14,22},{16,8},{18,10},{20,12},{22,14},{9,1... | collective-permute-start | bytes 626696 | tf_op jit(solution)/shard_map/ppermute | solution.py:394
  20.7 0.1 collective-permute-start.9
  20.8 0.0 collective-permute-done.10.refs_9_
  20.8 0.0 collective-permute-done.11.refs_10_
  20.8 0.2 collective-permute-done.12.refs_11_
  21.0 3.3 %rows.1 = (f32[4,512,128]{2,1,0:T(8,128)S(1)}, f32[4,512,256]{2,1,0:T(8,128)S(1)}, bf16[256,1024]{1,0:T(8,128)(2,1)S(1)}, bf16[1024,256]{1,0:T(8,128)(2,1)S(1)}) custom-call(bf16[528,128]{1,0:T(8,128)(2,1)S(1)} %get-tuple-element.50.refs_4_.refs_0_, bf16[528,128]{1,0:T(8,128)(2,1)S(1)} %collective-permute-done.refs_0_.refs_5_.refs_1_, ...), custom_call_target="tpu_custom_call" | custom-call | flops 2147483648 | bytes 2097152 | tf_op jit(solution)/shard_map/rows/pallas_call | solution.py:459
  24.3 0.1 halo.3
  24.4 3.2 %collective-permute-start.15 = (bf16[3,256,128]{2,1,0:T(8,128)(2,1)S(1)}, bf16[3,256,128]{2,1,0:T(8,128)(2,1)S(1)}, u32[]{:S(2)}, u32[]{:S(2)}) collective-permute-start(bf16[3,256,128]{2,1,0:T(8,128)(2,1)S(1)} %get-tuple-element.66), channel_id=1, source_target_pairs={{8,16},{10,18},{12,20},{14,22},{16,8},{18,10},{20,12},{22,14},{9,1... | collective-permute-start | bytes 589832 | tf_op jit(solution)/shard_map/ppermute | solution.py:394
  27.6 0.1 collective-permute-start.16
  27.7 0.0 collective-permute-done.8.edge_b.refs_12_
  27.7 0.0 collective-permute-done.9.edge_a.refs_13_
  27.7 2.5 %lend.1 = (bf16[3,288,128]{2,1,0:T(8,128)(2,1)S(1)}, bf16[3,288,128]{2,1,0:T(8,128)(2,1)S(1)}) custom-call(bf16[3,272,128]{2,1,0:T(8,128)(2,1)S(1)} %collective-permute-done.8.edge_b.refs_12_, bf16[3,272,128]{2,1,0:T(8,128)(2,1)S(1)} %collective-permute-done.9.edge_a.refs_13_, bf16[256,1024]{1,0:T(8,128)(2,1)S(1)} %get-tuple-element.60.plane_turned, ...), custom_call_target="tpu_custom_call" | custom-call | flops 4831838208 | bytes 3145728 | tf_op jit(solution)/shard_map/lend/pallas_call | solution.py:470
  30.3 1.5 %collective-permute-start.13 = (bf16[3,288,128]{2,1,0:T(8,128)(2,1)S(1)}, bf16[3,288,128]{2,1,0:T(8,128)(2,1)S(1)}, u32[]{:S(2)}, u32[]{:S(2)}) collective-permute-start(bf16[3,288,128]{2,1,0:T(8,128)(2,1)S(1)} %get-tuple-element.62), channel_id=1, source_target_pairs={{0,8},{2,10},{4,12},{6,14},{8,0},{10,2},{12,4},{14,6},{16,24},{18,... | collective-permute-start | bytes 663560 | tf_op jit(solution)/shard_map/ppermute | solution.py:394
  31.8 2.2 %collective-permute-start.14 = (bf16[3,288,128]{2,1,0:T(8,128)(2,1)S(1)}, bf16[3,288,128]{2,1,0:T(8,128)(2,1)S(1)}, u32[]{:S(2)}, u32[]{:S(2)}) collective-permute-start(bf16[3,288,128]{2,1,0:T(8,128)(2,1)S(1)} %get-tuple-element.63), channel_id=1, source_target_pairs={{8,16},{10,18},{12,20},{14,22},{16,8},{18,10},{20,12},{22,14},{9,1... | collective-permute-start | bytes 663560 | tf_op jit(solution)/shard_map/ppermute | solution.py:394
  34.0 0.0 collective-permute-done.15.refs_14_
  34.0 0.0 collective-permute-done.16.refs_15_
  34.0 2.8 %columns.2 = (bf16[256,128]{1,0:T(8,128)(2,1)S(1)}, bf16[256,128]{1,0:T(8,128)(2,1)S(1)}, bf16[256,1024]{1,0:T(8,128)(2,1)S(1)}, bf16[1024,256]{1,0:T(8,128)(2,1...) custom-call(bf16[528,128]{1,0:T(8,128)(2,1)S(1)} %get-tuple-element.50.refs_4_, ...), custom_call_target="tpu_custom_call" | custom-call | flops 1879048192 | bytes 1572864 | tf_op jit(solution)/shard_map/columns/pallas_call | solution.py:489
  36.8 3.1 %collective-permute-start.21 = (bf16[256,128]{1,0:T(8,128)(2,1)S(1)}, bf16[256,128]{1,0:T(8,128)(2,1)S(1)}, u32[]{:S(2)}, u32[]{:S(2)}) collective-permute-start(bf16[256,128]{1,0:T(8,128)(2,1)S(1)} %get-tuple-element.78), channel_id=1, source_target_pairs={{0,6},{2,4},{4,2},{6,0},{8,14},{10,12},{12,10},{14,8},{16,22},{18,... | collective-permute-start | bytes 196616 | tf_op jit(solution)/shard_map/ppermute | solution.py:388
  39.9 0.4 collective-permute-start.20
  40.3 0.0 collective-permute-done.13.back_a
  40.3 0.0 collective-permute-done.14.back_b
  40.3 0.6 %merge.1 = (bf16[256,128]{1,0:T(8,128)(2,1)S(1)}, bf16[256,128]{1,0:T(8,128)(2,1)S(1)}, bf16[256,128]{1,0:T(8,128)(2,1)S(1)}, bf16[256,128]{1,0:T(8,128)(2,1)S(1)}) custom-call(bf16[3,288,128]{2,1,0:T(8,128)(2,1)S(1)} %collective-permute-done.13.back_a, bf16[3,288,128]{2,1,0:T(8,128)(2,1)S(1)} %collective-permute-done.14.back_b, ...), custom_call_target="tpu_custom_call" | custom-call | bytes 2097152 | tf_op jit(solution)/shard_map/merge/pallas_call | solution.py:492
  40.9 1.2 %collective-permute-start.17 = (bf16[256,128]{1,0:T(8,128)(2,1)S(1)}, bf16[256,128]{1,0:T(8,128)(2,1)S(1)}, u32[]{:S(2)}, u32[]{:S(2)}) collective-permute-start(bf16[256,128]{1,0:T(8,128)(2,1)S(1)} %get-tuple-element.70), channel_id=1, source_target_pairs={{0,2},{2,0},{4,6},{6,4},{8,10},{10,8},{12,14},{14,12},{16,18},{18,... | collective-permute-start | bytes 196616 | tf_op jit(solution)/shard_map/ppermute | solution.py:388
  42.1 1.2 %collective-permute-start.18 = (bf16[256,128]{1,0:T(8,128)(2,1)S(1)}, bf16[256,128]{1,0:T(8,128)(2,1)S(1)}, u32[]{:S(2)}, u32[]{:S(2)}) collective-permute-start(bf16[256,128]{1,0:T(8,128)(2,1)S(1)} %get-tuple-element.71), channel_id=1, source_target_pairs={{0,4},{2,6},{4,0},{6,2},{8,12},{10,14},{12,8},{14,10},{16,20},{18,... | collective-permute-start | bytes 196616 | tf_op jit(solution)/shard_map/ppermute | solution.py:388
  43.3 0.5 %collective-permute-start.19 = (bf16[256,128]{1,0:T(8,128)(2,1)S(1)}, bf16[256,128]{1,0:T(8,128)(2,1)S(1)}, u32[]{:S(2)}, u32[]{:S(2)}) collective-permute-start(bf16[256,128]{1,0:T(8,128)(2,1)S(1)} %get-tuple-element.72), channel_id=1, source_target_pairs={{0,6},{2,4},{4,2},{6,0},{8,14},{10,12},{12,10},{14,8},{16,22},{18,... | collective-permute-start | bytes 196616 | tf_op jit(solution)/shard_map/ppermute | solution.py:388
  43.9 0.0 collective-permute-done.21.refs_6_
  43.9 0.2 collective-permute-done.20.refs_5_
  44.1 2.6 %columns.3 = (bf16[256,128]{1,0:T(8,128)(2,1)S(1)}, bf16[256,128]{1,0:T(8,128)(2,1)S(1)}, bf16[256,512]{1,0:T(8,128)(2,1)}) custom-call(bf16[256,1024]{1,0:T(8,128)(2,1)S(1)} %get-tuple-element.73.refs_0_, bf16[1024,256]{1,0:T(8,128)(2,1)S(1)} %get-tuple-element.74.refs_1_, bf16[4,512,256]{2,1,0:T(8,128)(2,1)S(1)} %get-tuple-element.75.refs_2_, ...), custom_call_target="tpu_custom_call" | custom-call | flops 1879048192 | bytes 1572864 | tf_op jit(solution)/shard_map/columns/pallas_call | solution.py:504
  46.7 0.5 collective-permute-start.22
  47.1 0.0 collective-permute-done.17.refs_1_
  47.1 0.0 collective-permute-done.18.refs_2_
  47.1 0.2 collective-permute-done.19.refs_3_
  47.4 0.7 %collective-permute-done.22.refs_5_ = bf16[256,128]{1,0:T(8,128)(2,1)S(1)} collective-permute-done((bf16[256,128]{1,0:T(8,128)(2,1)S(1)}, bf16[256,128]{1,0:T(8,128)(2,1)S(1)}, u32[]{:S(2)}, u32[]{:S(2)}) %collective-permute-start.22) | collective-permute-done | bytes 65568 | tf_op jit(solution)/shard_map/ppermute | solution.py:388
  48.0 0.8 %join.1 = (bf16[256,512]{1,0:T(8,128)(2,1)}, bf16[256,512]{1,0:T(8,128)(2,1)}) custom-call(bf16[256,128]{1,0:T(8,128)(2,1)S(1)} %get-tuple-element.69.refs_7_.refs_0_, bf16[256,128]{1,0:T(8,128)(2,1)S(1)} %collective-permute-done.17.refs_1_, bf16[256,128]{1,0:T(8,128)(2,1)S(1)} %collective-permute-done.18.refs_2_, ...), custom_call_target="tpu_custom_call", output_to_operand_aliasing={{1}: (6, {})} | custom-call | bytes 1048576 | tf_op jit(solution)/shard_map/join/pallas_call | solution.py:513
Async XLA Ops:
  0.6 9.2 %collective-permute-start.1 = (bf16[256,512]{1,0:T(8,128)(2,1)}, bf16[256,512]{1,0:T(8,128)(2,1)S(1)}, u32[]{:S(2)}, u32[]{:S(2)}) collective-permute-start(bf16[256,512]{1,0:T(8,128)(2,1)} %audio.3), channel_id=1, source_target_pairs={{0,1},{1,0},{2,3},{3,2},{4,5},{5,4},{6,7},{7,6},{8,9},{9,8},{10,11... | collective-permute-start | bytes 786440 | tf_op jit(solution)/shard_map/ppermute | solution.py:383
  1.9 11.8 %collective-permute-start.7 = (bf16[256,512]{1,0:T(8,128)(2,1)}, bf16[256,512]{1,0:T(8,128)(2,1)S(1)}, u32[]{:S(2)}, u32[]{:S(2)}) collective-permute-start(bf16[256,512]{1,0:T(8,128)(2,1)} %video.3), channel_id=1, source_target_pairs={{0,1},{1,0},{2,3},{3,2},{4,5},{5,4},{6,7},{7,6},{8,9},{9,8},{10,11... | collective-permute-start | bytes 786440 | tf_op jit(solution)/shard_map/ppermute | solution.py:383
  3.3 3.0 %collective-permute-start = (bf16[528,128]{1,0:T(8,128)(2,1)S(1)}, bf16[528,128]{1,0:T(8,128)(2,1)S(1)}, u32[]{:S(2)}, u32[]{:S(2)}) collective-permute-start(bf16[528,128]{1,0:T(8,128)(2,1)S(1)} %get-tuple-element.42), channel_id=1, source_target_pairs={{0,2},{2,0},{4,6},{6,4},{8,10},{10,8},{12,14},{14,12},{16,18},{18,... | collective-permute-start | bytes 405512 | tf_op jit(solution)/shard_map/ppermute | solution.py:388
  4.6 5.2 %collective-permute-start.2 = (bf16[528,128]{1,0:T(8,128)(2,1)S(1)}, bf16[528,128]{1,0:T(8,128)(2,1)S(1)}, u32[]{:S(2)}, u32[]{:S(2)}) collective-permute-start(bf16[528,128]{1,0:T(8,128)(2,1)S(1)} %get-tuple-element.45), channel_id=1, source_target_pairs={{0,4},{2,6},{4,0},{6,2},{8,12},{10,14},{12,8},{14,10},{16,20},{18,... | collective-permute-start | bytes 405512 | tf_op jit(solution)/shard_map/ppermute | solution.py:388
  5.9 9.8 %collective-permute-start.6 = (bf16[528,128]{1,0:T(8,128)(2,1)S(1)}, bf16[528,128]{1,0:T(8,128)(2,1)S(1)}, u32[]{:S(2)}, u32[]{:S(2)}) collective-permute-start(bf16[528,128]{1,0:T(8,128)(2,1)S(1)} %get-tuple-element.51), channel_id=1, source_target_pairs={{0,6},{2,4},{4,2},{6,0},{8,14},{10,12},{12,10},{14,8},{16,22},{18,... | collective-permute-start | bytes 405512 | tf_op jit(solution)/shard_map/ppermute | solution.py:388
  10.2 6.7 %collective-permute-start.3 = (bf16[256,128]{1,0:T(8,128)(2,1)S(1)}, bf16[256,128]{1,0:T(8,128)(2,1)S(1)}, u32[]{:S(2)}, u32[]{:S(2)}) collective-permute-start(bf16[256,128]{1,0:T(8,128)(2,1)S(1)} %get-tuple-element.47), channel_id=1, source_target_pairs={{0,2},{2,0},{4,6},{6,4},{8,10},{10,8},{12,14},{14,12},{16,18},{18,... | collective-permute-start | bytes 196616 | tf_op jit(solution)/shard_map/ppermute | solution.py:388
  11.6 5.9 %collective-permute-start.4 = (bf16[256,128]{1,0:T(8,128)(2,1)S(1)}, bf16[256,128]{1,0:T(8,128)(2,1)S(1)}, u32[]{:S(2)}, u32[]{:S(2)}) collective-permute-start(bf16[256,128]{1,0:T(8,128)(2,1)S(1)} %get-tuple-element.48), channel_id=1, source_target_pairs={{0,4},{2,6},{4,0},{6,2},{8,12},{10,14},{12,8},{14,10},{16,20},{18,... | collective-permute-start | bytes 196616 | tf_op jit(solution)/shard_map/ppermute | solution.py:388
  12.8 4.6 %collective-permute-start.5 = (bf16[256,128]{1,0:T(8,128)(2,1)S(1)}, bf16[256,128]{1,0:T(8,128)(2,1)S(1)}, u32[]{:S(2)}, u32[]{:S(2)}) collective-permute-start(bf16[256,128]{1,0:T(8,128)(2,1)S(1)} %get-tuple-element.49), channel_id=1, source_target_pairs={{0,6},{2,4},{4,2},{6,0},{8,14},{10,12},{12,10},{14,8},{16,22},{18,... | collective-permute-start | bytes 196616 | tf_op jit(solution)/shard_map/ppermute | solution.py:388
  14.1 6.7 %collective-permute-start.10 = (bf16[256,128]{1,0:T(8,128)(2,1)S(1)}, bf16[256,128]{1,0:T(8,128)(2,1)S(1)}, u32[]{:S(2)}, u32[]{:S(2)}) collective-permute-start(bf16[256,128]{1,0:T(8,128)(2,1)S(1)} %get-tuple-element.57), channel_id=1, source_target_pairs={{0,2},{2,0},{4,6},{6,4},{8,10},{10,8},{12,14},{14,12},{16,18},{18,... | collective-permute-start | bytes 196616 | tf_op jit(solution)/shard_map/ppermute | solution.py:388
  15.7 5.1 %collective-permute-start.11 = (bf16[256,128]{1,0:T(8,128)(2,1)S(1)}, bf16[256,128]{1,0:T(8,128)(2,1)S(1)}, u32[]{:S(2)}, u32[]{:S(2)}) collective-permute-start(bf16[256,128]{1,0:T(8,128)(2,1)S(1)} %get-tuple-element.58), channel_id=1, source_target_pairs={{0,4},{2,6},{4,0},{6,2},{8,12},{10,14},{12,8},{14,10},{16,20},{18,... | collective-permute-start | bytes 196616 | tf_op jit(solution)/shard_map/ppermute | solution.py:388
  16.9 4.1 %collective-permute-start.12 = (bf16[256,128]{1,0:T(8,128)(2,1)S(1)}, bf16[256,128]{1,0:T(8,128)(2,1)S(1)}, u32[]{:S(2)}, u32[]{:S(2)}) collective-permute-start(bf16[256,128]{1,0:T(8,128)(2,1)S(1)} %get-tuple-element.59), channel_id=1, source_target_pairs={{0,6},{2,4},{4,2},{6,0},{8,14},{10,12},{12,10},{14,8},{16,22},{18,... | collective-permute-start | bytes 196616 | tf_op jit(solution)/shard_map/ppermute | solution.py:388
  17.5 10.2 %collective-permute-start.8 = (bf16[3,272,128]{2,1,0:T(8,128)(2,1)S(1)}, bf16[3,272,128]{2,1,0:T(8,128)(2,1)S(1)}, u32[]{:S(2)}, u32[]{:S(2)}) collective-permute-start(bf16[3,272,128]{2,1,0:T(8,128)(2,1)S(1)} %get-tuple-element.55), channel_id=1, source_target_pairs={{8,16},{10,18},{12,20},{14,22},{16,8},{18,10},{20,12},{22,14},{9,1... | collective-permute-start | bytes 626696 | tf_op jit(solution)/shard_map/ppermute | solution.py:394
  20.7 7.0 %collective-permute-start.9 = (bf16[3,272,128]{2,1,0:T(8,128)(2,1)S(1)}, bf16[3,272,128]{2,1,0:T(8,128)(2,1)S(1)}, u32[]{:S(2)}, u32[]{:S(2)}) collective-permute-start(bf16[3,272,128]{2,1,0:T(8,128)(2,1)S(1)} %get-tuple-element.56), channel_id=1, source_target_pairs={{0,8},{2,10},{4,12},{6,14},{8,0},{10,2},{12,4},{14,6},{16,24},{18,... | collective-permute-start | bytes 626696 | tf_op jit(solution)/shard_map/ppermute | solution.py:394
  24.4 9.6 %collective-permute-start.15 = (bf16[3,256,128]{2,1,0:T(8,128)(2,1)S(1)}, bf16[3,256,128]{2,1,0:T(8,128)(2,1)S(1)}, u32[]{:S(2)}, u32[]{:S(2)}) collective-permute-start(bf16[3,256,128]{2,1,0:T(8,128)(2,1)S(1)} %get-tuple-element.66), channel_id=1, source_target_pairs={{8,16},{10,18},{12,20},{14,22},{16,8},{18,10},{20,12},{22,14},{9,1... | collective-permute-start | bytes 589832 | tf_op jit(solution)/shard_map/ppermute | solution.py:394
  27.6 6.4 %collective-permute-start.16 = (bf16[3,256,128]{2,1,0:T(8,128)(2,1)S(1)}, bf16[3,256,128]{2,1,0:T(8,128)(2,1)S(1)}, u32[]{:S(2)}, u32[]{:S(2)}) collective-permute-start(bf16[3,256,128]{2,1,0:T(8,128)(2,1)S(1)} %get-tuple-element.67), channel_id=1, source_target_pairs={{0,8},{2,10},{4,12},{6,14},{8,0},{10,2},{12,4},{14,6},{16,24},{18,... | collective-permute-start | bytes 589832 | tf_op jit(solution)/shard_map/ppermute | solution.py:394
  30.3 10.1 %collective-permute-start.13 = (bf16[3,288,128]{2,1,0:T(8,128)(2,1)S(1)}, bf16[3,288,128]{2,1,0:T(8,128)(2,1)S(1)}, u32[]{:S(2)}, u32[]{:S(2)}) collective-permute-start(bf16[3,288,128]{2,1,0:T(8,128)(2,1)S(1)} %get-tuple-element.62), channel_id=1, source_target_pairs={{0,8},{2,10},{4,12},{6,14},{8,0},{10,2},{12,4},{14,6},{16,24},{18,... | collective-permute-start | bytes 663560 | tf_op jit(solution)/shard_map/ppermute | solution.py:394
  31.8 8.6 %collective-permute-start.14 = (bf16[3,288,128]{2,1,0:T(8,128)(2,1)S(1)}, bf16[3,288,128]{2,1,0:T(8,128)(2,1)S(1)}, u32[]{:S(2)}, u32[]{:S(2)}) collective-permute-start(bf16[3,288,128]{2,1,0:T(8,128)(2,1)S(1)} %get-tuple-element.63), channel_id=1, source_target_pairs={{8,16},{10,18},{12,20},{14,22},{16,8},{18,10},{20,12},{22,14},{9,1... | collective-permute-start | bytes 663560 | tf_op jit(solution)/shard_map/ppermute | solution.py:394
  36.8 7.0 %collective-permute-start.21 = (bf16[256,128]{1,0:T(8,128)(2,1)S(1)}, bf16[256,128]{1,0:T(8,128)(2,1)S(1)}, u32[]{:S(2)}, u32[]{:S(2)}) collective-permute-start(bf16[256,128]{1,0:T(8,128)(2,1)S(1)} %get-tuple-element.78), channel_id=1, source_target_pairs={{0,6},{2,4},{4,2},{6,0},{8,14},{10,12},{12,10},{14,8},{16,22},{18,... | collective-permute-start | bytes 196616 | tf_op jit(solution)/shard_map/ppermute | solution.py:388
  39.9 4.2 %collective-permute-start.20 = (bf16[256,128]{1,0:T(8,128)(2,1)S(1)}, bf16[256,128]{1,0:T(8,128)(2,1)S(1)}, u32[]{:S(2)}, u32[]{:S(2)}) collective-permute-start(bf16[256,128]{1,0:T(8,128)(2,1)S(1)} %get-tuple-element.68.refs_0_), channel_id=1, source_target_pairs={{0,4},{2,6},{4,0},{6,2},{8,12},{10,14},{12,8},{14,10},{16,20},{18,... | collective-permute-start | bytes 196616 | tf_op jit(solution)/shard_map/ppermute | solution.py:388
  40.9 6.2 %collective-permute-start.17 = (bf16[256,128]{1,0:T(8,128)(2,1)S(1)}, bf16[256,128]{1,0:T(8,128)(2,1)S(1)}, u32[]{:S(2)}, u32[]{:S(2)}) collective-permute-start(bf16[256,128]{1,0:T(8,128)(2,1)S(1)} %get-tuple-element.70), channel_id=1, source_target_pairs={{0,2},{2,0},{4,6},{6,4},{8,10},{10,8},{12,14},{14,12},{16,18},{18,... | collective-permute-start | bytes 196616 | tf_op jit(solution)/shard_map/ppermute | solution.py:388
  42.1 5.0 %collective-permute-start.18 = (bf16[256,128]{1,0:T(8,128)(2,1)S(1)}, bf16[256,128]{1,0:T(8,128)(2,1)S(1)}, u32[]{:S(2)}, u32[]{:S(2)}) collective-permute-start(bf16[256,128]{1,0:T(8,128)(2,1)S(1)} %get-tuple-element.71), channel_id=1, source_target_pairs={{0,4},{2,6},{4,0},{6,2},{8,12},{10,14},{12,8},{14,10},{16,20},{18,... | collective-permute-start | bytes 196616 | tf_op jit(solution)/shard_map/ppermute | solution.py:388
  43.3 4.1 %collective-permute-start.19 = (bf16[256,128]{1,0:T(8,128)(2,1)S(1)}, bf16[256,128]{1,0:T(8,128)(2,1)S(1)}, u32[]{:S(2)}, u32[]{:S(2)}) collective-permute-start(bf16[256,128]{1,0:T(8,128)(2,1)S(1)} %get-tuple-element.72), channel_id=1, source_target_pairs={{0,6},{2,4},{4,2},{6,0},{8,14},{10,12},{12,10},{14,8},{16,22},{18,... | collective-permute-start | bytes 196616 | tf_op jit(solution)/shard_map/ppermute | solution.py:388
  46.7 1.4 %collective-permute-start.22 = (bf16[256,128]{1,0:T(8,128)(2,1)S(1)}, bf16[256,128]{1,0:T(8,128)(2,1)S(1)}, u32[]{:S(2)}, u32[]{:S(2)}) collective-permute-start(bf16[256,128]{1,0:T(8,128)(2,1)S(1)} %get-tuple-element.80), channel_id=1, source_target_pairs={{0,2},{2,0},{4,6},{6,4},{8,10},{10,8},{12,14},{14,12},{16,18},{18,... | collective-permute-start | bytes 196616 | tf_op jit(solution)/shard_map/ppermute | solution.py:388

commit v18 on v15

--- a/solution.py
+++ b/solution.py
@@ -21,6 +21,14 @@
 
 def place():
     return lax.rem(lax.axis_index("tm"), GROUP)
+
+
+def receiver(mine, k):
+    return lax.rem(mine + k, GROUP)
+
+
+def sender(mine, k):
+    return lax.rem(mine + GROUP - k, GROUP)
 
 
 def plane():
@@ -61,7 +69,7 @@
     copies, fetch = fetcher(sems)
     fetch(ids, ids_in)
     for k in range(GROUP):
-        at = pl.ds(pl.multiple_of((mine ^ k) * width, width), width)
+        at = pl.ds(pl.multiple_of(receiver(mine, k) * width, width), width)
         for i, stream in enumerate((audio, video)):
             fetch(stream.at[:, at], packs[k].at[i * rows : (i + 1) * rows])
     copies[0].wait()
@@ -99,7 +107,7 @@
     mine = place()
     full[...] = (part[...] + product(other[...], weight[...])).astype(jnp.bfloat16) * jnp.bfloat16(scale)
     for k in range(GROUP):
-        pieces[k][...] = full[:, pl.ds(pl.multiple_of((mine ^ k) * width, width), width)]
+        pieces[k][...] = full[:, pl.ds(pl.multiple_of(receiver(mine, k) * width, width), width)]
 
 
 def halo_kernel(ids_at, *refs):
@@ -108,7 +116,7 @@
     mine = place()
     odd = lax.rem(plane(), 2)
     for k in range(GROUP):
-        block = mine ^ k
+        block = sender(mine, k)
         for out, skip in zip(outs, ((GROUP - RADIUS) * (1 - odd), (GROUP - RADIUS) * odd)):
             spot = block - skip
 
@@ -125,7 +133,7 @@
     mine = place()
     copies, fetch = fetcher(sems)
     for k in range(GROUP):
-        fetch(pieces[k], out.at[:, pl.ds(pl.multiple_of((mine ^ k) * width, width), width)])
+        fetch(pieces[k], out.at[:, pl.ds(pl.multiple_of(sender(mine, k) * width, width), width)])
     for copy in copies:
         copy.wait()
 
@@ -179,7 +187,7 @@
     mine = place()
     beside[:, width:] = jnp.ones((GROUP * rows, width), beside.dtype)
     for k in range(GROUP):
-        b = mine ^ k
+        b = sender(mine, k)
 
         def spot(at, size):
             return pl.ds(pl.multiple_of(b * rows + at, size), size)
@@ -290,10 +298,10 @@
             for j in range(RADIUS):
                 at = pl.ds(pl.multiple_of((base + j) * rows, rows), rows)
                 edge_beside[at, :width] = edge[j]
-    near = [pl.ds(pl.multiple_of((mine ^ k) * rows, rows), RADIUS * rows) for k in receivers]
+    near = [pl.ds(pl.multiple_of(receiver(mine, k) * rows, rows), RADIUS * rows) for k in receivers]
 
     def scores_of(n):
-        ask = asks[mine ^ receivers[n]]
+        ask = asks[receiver(mine, receivers[n])]
         return [product(ask, turned[...]), product(ask, edge_turned[:, near[n]])]
 
     ahead = scores_of(0)
@@ -351,7 +359,7 @@
             total += weight
         whole[b] = (value / total).astype(whole.dtype)
     for k in range(GROUP):
-        outs[k][...] = whole[mine ^ k]
+        outs[k][...] = whole[receiver(mine, k)]
 
 
 def local(audio_frames, video_frames, recording, audio_query, video_key):
@@ -367,7 +375,7 @@
         return lax.ppermute(x, "head", [(0, 1), (1, 0)])
 
     def traded(pieces):
-        pairs = lambda k: [(i, i ^ k) for i in range(length)]
+        pairs = lambda k: [(i, i - i % GROUP + (i + k) % GROUP) for i in range(length)]
         return [pieces[0]] + [lax.ppermute(pieces[k], "tm", pairs(k)) for k in range(1, GROUP)]
 
     def crossed(sent, second):

time: 49.2 us -> 51.3 us (1.043)
  the two profiles are of different devices: /device:TPU:9 before, /device:TPU:8 now
where the time goes in v18:
time: 51.3 us; the launch traced here: 51.1 us
  starting transfers between devices  26 us (51%)
  Pallas kernels  16.7 us (33%)
  waiting for transfers between devices  7.3 us (14%)
  between operations  1.03 us (2%)
    ppermute x15, starting transfers between devices, traded(): lax.ppermute(pieces[k], 'tm', pairs(k))  12.8 us
    ppermute x6, starting transfers between devices, crossed(): lax.ppermute(sent, 'tm', [(p * GROUP + i, q * GROUP + i) for p, q in pair...  11.2 us
    ppermute x15, waiting for transfers between devices, traded(): lax.ppermute(pieces[k], 'tm', pairs(k))  5.23 us
    pallas_call x1, Pallas kernels, local(): call(rows_kernel, [shape((GROUP, heads * rows, n * width), f32) for n in...  3.22 us
    pallas_call x1, Pallas kernels, local(): call(functools.partial(columns_kernel, far), [piece] * len(far) + shared,...  2.74 us
    pallas_call x1, Pallas kernels, local(): call(lend_kernel, [back, back, shape((2 * width, around), bf16)], [pltpu....  2.62 us
    pallas_call x1, Pallas kernels, local(): call(functools.partial(columns_kernel, near), [piece] * len(near), ins=[V...  2.26 us
    ppermute x2, starting transfers between devices, swapped(): return lax.ppermute(x, 'head', [(0, 1), (1, 0)])  2.09 us
  transfers between devices with their start and end apart: 23, of which 5 were waited for; matrix products, arithmetic and copies ran while one was open for 0% of the time, Pallas kernels for 31%

profile of v18, /device:TPU:8, one launch (start us, length us, event | category | flops | bytes accessed | tf_op | source)
XLA Modules:
  0.0 51.1 jit_solution(17718688248652882087)
XLA Ops:
  0.6 1.6 %collective-permute-start.1 = (bf16[256,512]{1,0:T(8,128)(2,1)}, bf16[256,512]{1,0:T(8,128)(2,1)S(1)}, u32[]{:S(2)}, u32[]{:S(2)}) collective-permute-start(bf16[256,512]{1,0:T(8,128)(2,1)} %audio.3), channel_id=1, source_target_pairs={{0,1},{1,0},{2,3},{3,2},{4,5},{5,4},{6,7},{7,6},{8,9},{9,8},{10,11... | collective-permute-start | bytes 786440 | tf_op jit(solution)/shard_map/ppermute | solution.py:375
  2.2 0.5 collective-permute-start.7
  2.7 1.2 %split.1 = (bf16[528,128]{1,0:T(8,128)(2,1)S(1)}, bf16[528,128]{1,0:T(8,128)(2,1)S(1)}, bf16[528,128]{1,0:T(8,128)(2,1)S(1)}, bf16[528,128]{1,0:T(8,128)(2,1)S(1)}) custom-call(bf16[256,512]{1,0:T(8,128)(2,1)} %audio.3, bf16[256,512]{1,0:T(8,128)(2,1)} %video.3, s32[2,128]{1,0:T(2,128)} %bitcast.1), custom_call_target="tpu_custom_call" | custom-call | bytes 1048576 | tf_op jit(solution)/shard_map/split/pallas_call | solution.py:397
  3.9 0.1 collective-permute-start
  4.0 1.6 %collective-permute-start.2 = (bf16[528,128]{1,0:T(8,128)(2,1)S(1)}, bf16[528,128]{1,0:T(8,128)(2,1)S(1)}, u32[]{:S(2)}, u32[]{:S(2)}) collective-permute-start(bf16[528,128]{1,0:T(8,128)(2,1)S(1)} %get-tuple-element.44), channel_id=1, source_target_pairs={{0,4},{2,6},{4,0},{6,2},{8,12},{10,14},{12,8},{14,10},{16,20},{18,... | collective-permute-start | bytes 405512 | tf_op jit(solution)/shard_map/ppermute | solution.py:379
  5.5 1.4 %collective-permute-start.6 = (bf16[528,128]{1,0:T(8,128)(2,1)S(1)}, bf16[528,128]{1,0:T(8,128)(2,1)S(1)}, u32[]{:S(2)}, u32[]{:S(2)}) collective-permute-start(bf16[528,128]{1,0:T(8,128)(2,1)S(1)} %get-tuple-element.50), channel_id=1, source_target_pairs={{0,6},{2,0},{4,2},{6,4},{8,14},{10,8},{12,10},{14,12},{16,22},{18,... | collective-permute-start | bytes 405512 | tf_op jit(solution)/shard_map/ppermute | solution.py:379
  6.9 2.3 %collective-permute-done.refs_0_.refs_5_.refs_1_ = bf16[528,128]{1,0:T(8,128)(2,1)S(1)} collective-permute-done((bf16[528,128]{1,0:T(8,128)(2,1)S(1)}, bf16[528,128]{1,0:T(8,128)(2,1)S(1)}, u32[]{:S(2)}, u32[]{:S(2)}) %collective-permute-start) | collective-permute-done | bytes 135200 | tf_op jit(solution)/shard_map/ppermute | solution.py:379
  9.2 1.8 %prepare.1 = (f32[256,512]{1,0:T(8,128)S(1)}, f32[256,512]{1,0:T(8,128)S(1)}, bf16[512,512]{1,0:T(8,128)(2,1)S(1)}, bf16[512,512]{1,0:T(8,128)(2,1)S(1)}) custom-call(bf16[256,512]{1,0:T(8,128)(2,1)} %audio.3, bf16[256,512]{1,0:T(8,128)(2,1)} %video.3, bf16[1024,512]{1,0:T(8,128)(2,1)} %query.1, bf16[1024,512]{1,0:T(8,128)(2,1)} %key.1, ...), custom_call_target="tpu_custom_call" | custom-call | flops 268435456 | bytes 4194304 | tf_op jit(solution)/shard_map/prepare/pallas_call | solution.py:407
  11.0 0.0 collective-permute-done.2.refs_1_.refs_6_.refs_2_
  11.0 0.0 collective-permute-done.1.other
  11.0 0.4 project.2
  11.4 1.3 %collective-permute-start.3 = (bf16[256,128]{1,0:T(8,128)(2,1)S(1)}, bf16[256,128]{1,0:T(8,128)(2,1)S(1)}, u32[]{:S(2)}, u32[]{:S(2)}) collective-permute-start(bf16[256,128]{1,0:T(8,128)(2,1)S(1)} %get-tuple-element.46), channel_id=1, source_target_pairs={{0,2},{2,4},{4,6},{6,0},{8,10},{10,12},{12,14},{14,8},{16,18},{18,... | collective-permute-start | bytes 196616 | tf_op jit(solution)/shard_map/ppermute | solution.py:379
  12.7 1.5 %collective-permute-start.4 = (bf16[256,128]{1,0:T(8,128)(2,1)S(1)}, bf16[256,128]{1,0:T(8,128)(2,1)S(1)}, u32[]{:S(2)}, u32[]{:S(2)}) collective-permute-start(bf16[256,128]{1,0:T(8,128)(2,1)S(1)} %get-tuple-element.47), channel_id=1, source_target_pairs={{0,4},{2,6},{4,0},{6,2},{8,12},{10,14},{12,8},{14,10},{16,20},{18,... | collective-permute-start | bytes 196616 | tf_op jit(solution)/shard_map/ppermute | solution.py:379
  14.1 0.3 collective-permute-start.5
  14.4 0.1 collective-permute-done.7.other
  14.6 0.4 project.3
  14.9 0.1 collective-permute-start.10
  15.1 0.0 collective-permute-done.6.refs_7_.refs_3_
  15.1 1.5 %collective-permute-start.11 = (bf16[256,128]{1,0:T(8,128)(2,1)S(1)}, bf16[256,128]{1,0:T(8,128)(2,1)S(1)}, u32[]{:S(2)}, u32[]{:S(2)}) collective-permute-start(bf16[256,128]{1,0:T(8,128)(2,1)S(1)} %get-tuple-element.57), channel_id=1, source_target_pairs={{0,4},{2,6},{4,0},{6,2},{8,12},{10,14},{12,8},{14,10},{16,20},{18,... | collective-permute-start | bytes 196616 | tf_op jit(solution)/shard_map/ppermute | solution.py:379
  16.6 0.0 collective-permute-done.3.refs_1_.refs_5_
  16.6 1.4 %collective-permute-start.12 = (bf16[256,128]{1,0:T(8,128)(2,1)S(1)}, bf16[256,128]{1,0:T(8,128)(2,1)S(1)}, u32[]{:S(2)}, u32[]{:S(2)}) collective-permute-start(bf16[256,128]{1,0:T(8,128)(2,1)S(1)} %get-tuple-element.58), channel_id=1, source_target_pairs={{0,6},{2,0},{4,2},{6,4},{8,14},{10,8},{12,10},{14,12},{16,22},{18,... | collective-permute-start | bytes 196616 | tf_op jit(solution)/shard_map/ppermute | solution.py:379
  18.0 0.0 collective-permute-done.4.refs_2_.refs_6_
  18.0 0.0 collective-permute-done.5.refs_3_.refs_7_
  18.0 0.1 halo.2
  18.0 3.5 %collective-permute-start.8 = (bf16[3,272,128]{2,1,0:T(8,128)(2,1)S(1)}, bf16[3,272,128]{2,1,0:T(8,128)(2,1)S(1)}, u32[]{:S(2)}, u32[]{:S(2)}) collective-permute-start(bf16[3,272,128]{2,1,0:T(8,128)(2,1)S(1)} %get-tuple-element.54), channel_id=1, source_target_pairs={{8,16},{10,18},{12,20},{14,22},{16,8},{18,10},{20,12},{22,14},{9,1... | collective-permute-start | bytes 626696 | tf_op jit(solution)/shard_map/ppermute | solution.py:384
  21.5 0.1 collective-permute-start.9
  21.6 0.0 collective-permute-done.10.refs_9_
  21.6 0.0 collective-permute-done.11.refs_10_
  21.6 0.0 collective-permute-done.12.refs_11_
  21.6 3.2 %rows.1 = (f32[4,512,128]{2,1,0:T(8,128)S(1)}, f32[4,512,256]{2,1,0:T(8,128)S(1)}, bf16[256,1024]{1,0:T(8,128)(2,1)S(1)}, bf16[1024,256]{1,0:T(8,128)(2,1)S(1)}) custom-call(bf16[528,128]{1,0:T(8,128)(2,1)S(1)} %get-tuple-element.49.refs_4_.refs_0_, bf16[528,128]{1,0:T(8,128)(2,1)S(1)} %collective-permute-done.refs_0_.refs_5_.refs_1_, ...), custom_call_target="tpu_custom_call" | custom-call | flops 2147483648 | bytes 2097152 | tf_op jit(solution)/shard_map/rows/pallas_call | solution.py:449
  24.9 0.1 halo.3
  25.0 2.4 %collective-permute-start.15 = (bf16[3,256,128]{2,1,0:T(8,128)(2,1)S(1)}, bf16[3,256,128]{2,1,0:T(8,128)(2,1)S(1)}, u32[]{:S(2)}, u32[]{:S(2)}) collective-permute-start(bf16[3,256,128]{2,1,0:T(8,128)(2,1)S(1)} %get-tuple-element.65), channel_id=1, source_target_pairs={{8,16},{10,18},{12,20},{14,22},{16,8},{18,10},{20,12},{22,14},{9,1... | collective-permute-start | bytes 589832 | tf_op jit(solution)/shard_map/ppermute | solution.py:384
  27.3 0.4 collective-permute-start.16
  27.7 0.0 collective-permute-done.8.edge_b
  27.7 0.4 collective-permute-done.9.edge_a
  28.1 2.6 %lend.1 = (bf16[3,288,128]{2,1,0:T(8,128)(2,1)S(1)}, bf16[3,288,128]{2,1,0:T(8,128)(2,1)S(1)}, bf16[256,1536]{1,0:T(8,128)(2,1)S(1)}) custom-call(bf16[3,272,128]{2,1,0:T(8,128)(2,1)S(1)} %collective-permute-done.8.edge_b, bf16[3,272,128]{2,1,0:T(8,128)(2,1)S(1)} %collective-permute-done.9.edge_a, bf16[256,1024]{1,0:T(8,128)(2,1)S(1)} %get-tuple-element.59.plane_turned, ...), custom_call_target="tpu_custom_call" | custom-call | flops 4831838208 | bytes 3145728 | tf_op jit(solution)/shard_map/lend/pallas_call | solution.py:460
  30.7 1.4 %collective-permute-start.13 = (bf16[3,288,128]{2,1,0:T(8,128)(2,1)S(1)}, bf16[3,288,128]{2,1,0:T(8,128)(2,1)S(1)}, u32[]{:S(2)}, u32[]{:S(2)}) collective-permute-start(bf16[3,288,128]{2,1,0:T(8,128)(2,1)S(1)} %get-tuple-element.61), channel_id=1, source_target_pairs={{0,8},{2,10},{4,12},{6,14},{8,0},{10,2},{12,4},{14,6},{16,24},{18,... | collective-permute-start | bytes 663560 | tf_op jit(solution)/shard_map/ppermute | solution.py:384
  32.1 3.4 %collective-permute-start.14 = (bf16[3,288,128]{2,1,0:T(8,128)(2,1)S(1)}, bf16[3,288,128]{2,1,0:T(8,128)(2,1)S(1)}, u32[]{:S(2)}, u32[]{:S(2)}) collective-permute-start(bf16[3,288,128]{2,1,0:T(8,128)(2,1)S(1)} %get-tuple-element.62), channel_id=1, source_target_pairs={{8,16},{10,18},{12,20},{14,22},{16,8},{18,10},{20,12},{22,14},{9,1... | collective-permute-start | bytes 663560 | tf_op jit(solution)/shard_map/ppermute | solution.py:384
  35.6 0.0 collective-permute-done.15.refs_12_
  35.6 0.0 collective-permute-done.16.refs_13_
  35.6 2.7 %columns.2 = (bf16[256,128]{1,0:T(8,128)(2,1)S(1)}, bf16[256,128]{1,0:T(8,128)(2,1)S(1)}, bf16[256,1024]{1,0:T(8,128)(2,1)S(1)}, bf16[1024,256]{1,0:T(8,128)(2,1...) custom-call(bf16[528,128]{1,0:T(8,128)(2,1)S(1)} %get-tuple-element.49.refs_4_.refs_0_, ...), custom_call_target="tpu_custom_call" | custom-call | flops 1879048192 | bytes 1572864 | tf_op jit(solution)/shard_map/columns/pallas_call | solution.py:479
  38.3 0.1 collective-permute-start.22
  38.4 0.6 %collective-permute-start.21 = (bf16[256,128]{1,0:T(8,128)(2,1)S(1)}, bf16[256,128]{1,0:T(8,128)(2,1)S(1)}, u32[]{:S(2)}, u32[]{:S(2)}) collective-permute-start(bf16[256,128]{1,0:T(8,128)(2,1)S(1)} %get-tuple-element.68.refs_0_), channel_id=1, source_target_pairs={{0,4},{2,6},{4,0},{6,2},{8,12},{10,14},{12,8},{14,10},{16,20},{18,... | collective-permute-start | bytes 196616 | tf_op jit(solution)/shard_map/ppermute | solution.py:379
  39.0 0.0 collective-permute-done.13.back_a
  39.0 1.5 %collective-permute-done.14.back_b = bf16[3,288,128]{2,1,0:T(8,128)(2,1)S(1)} collective-permute-done((bf16[3,288,128]{2,1,0:T(8,128)(2,1)S(1)}, bf16[3,288,128]{2,1,0:T(8,128)(2,1)S(1)}, u32[]{:S(2)}, u32[]{:S(2)}) %collective-permute-start.14) | collective-permute-done | bytes 221216 | tf_op jit(solution)/shard_map/ppermute | solution.py:384
  40.6 0.6 %merge.1 = (bf16[256,128]{1,0:T(8,128)(2,1)S(1)}, bf16[256,128]{1,0:T(8,128)(2,1)S(1)}, bf16[256,128]{1,0:T(8,128)(2,1)S(1)}, bf16[256,128]{1,0:T(8,128)(2,1)S(1)}) custom-call(bf16[3,288,128]{2,1,0:T(8,128)(2,1)S(1)} %collective-permute-done.13.back_a, bf16[3,288,128]{2,1,0:T(8,128)(2,1)S(1)} %collective-permute-done.14.back_b, ...), custom_call_target="tpu_custom_call" | custom-call | bytes 2097152 | tf_op jit(solution)/shard_map/merge/pallas_call | solution.py:482
  41.1 0.1 collective-permute-start.17
  41.2 1.6 %collective-permute-start.18 = (bf16[256,128]{1,0:T(8,128)(2,1)S(1)}, bf16[256,128]{1,0:T(8,128)(2,1)S(1)}, u32[]{:S(2)}, u32[]{:S(2)}) collective-permute-start(bf16[256,128]{1,0:T(8,128)(2,1)S(1)} %get-tuple-element.71), channel_id=1, source_target_pairs={{0,4},{2,6},{4,0},{6,2},{8,12},{10,14},{12,8},{14,10},{16,20},{18,... | collective-permute-start | bytes 196616 | tf_op jit(solution)/shard_map/ppermute | solution.py:379
  42.8 1.4 %collective-permute-start.19 = (bf16[256,128]{1,0:T(8,128)(2,1)S(1)}, bf16[256,128]{1,0:T(8,128)(2,1)S(1)}, u32[]{:S(2)}, u32[]{:S(2)}) collective-permute-start(bf16[256,128]{1,0:T(8,128)(2,1)S(1)} %get-tuple-element.72), channel_id=1, source_target_pairs={{0,6},{2,0},{4,2},{6,4},{8,14},{10,8},{12,10},{14,12},{16,22},{18,... | collective-permute-start | bytes 196616 | tf_op jit(solution)/shard_map/ppermute | solution.py:379
  44.2 2.3 %columns.3 = (bf16[256,128]{1,0:T(8,128)(2,1)S(1)}, bf16[256,128]{1,0:T(8,128)(2,1)S(1)}) custom-call(bf16[256,1536]{1,0:T(8,128)(2,1)S(1)} %get-tuple-element.67.refs_14_.refs_0_, bf16[256,1024]{1,0:T(8,128)(2,1)S(1)} %get-tuple-element.73.refs_1_, bf16[1024,256]{1,0:T(8,128)(2,1)S(1)} %get-tuple-element.74.refs_2_, ...), custom_call_target="tpu_custom_call" | custom-call | flops 1879048192 | bytes 1572864 | tf_op jit(solution)/shard_map/columns/pallas_call | solution.py:492
  46.4 0.0 collective-permute-done.17.refs_1_
  46.4 0.1 collective-permute-start.20
  46.5 0.0 collective-permute-done.18.refs_2_
  46.5 0.0 collective-permute-done.19.refs_3_
  46.5 0.7 %join.2 = bf16[256,512]{1,0:T(8,128)(2,1)} custom-call(bf16[256,128]{1,0:T(8,128)(2,1)S(1)} %get-tuple-element.69.refs_0_.refs_5_, bf16[256,128]{1,0:T(8,128)(2,1)S(1)} %collective-permute-done.17.refs_1_, bf16[256,128]{1,0:T(8,128)(2,1)S(1)} %collective-permute-done.18.refs_2_, bf16[256,128]{1,0:T(8,128)(2,1)S(1)} %collective-permute-done.19.refs_3_), custom_call_target="tpu_custom_call" | custom-call | bytes 524288 | tf_op jit(solution)/shard_map/join/pallas_call | solution.py:501
  47.3 0.0 collective-permute-done.22.refs_3_
  47.3 0.0 collective-permute-done.21.refs_2_
  47.3 2.9 %collective-permute-done.20.refs_1_ = bf16[256,128]{1,0:T(8,128)(2,1)S(1)} collective-permute-done((bf16[256,128]{1,0:T(8,128)(2,1)S(1)}, bf16[256,128]{1,0:T(8,128)(2,1)S(1)}, u32[]{:S(2)}, u32[]{:S(2)}) %collective-permute-start.20) | collective-permute-done | bytes 65568 | tf_op jit(solution)/shard_map/ppermute | solution.py:379
  50.2 0.7 %join.3 = bf16[256,512]{1,0:T(8,128)(2,1)} custom-call(bf16[256,128]{1,0:T(8,128)(2,1)S(1)} %get-tuple-element.77.refs_0_, bf16[256,128]{1,0:T(8,128)(2,1)S(1)} %collective-permute-done.20.refs_1_, bf16[256,128]{1,0:T(8,128)(2,1)S(1)} %collective-permute-done.21.refs_2_, bf16[256,128]{1,0:T(8,128)(2,1)S(1)} %collective-permute-done.22.refs_3_), custom_call_target="tpu_custom_call" | custom-call | bytes 524288 | tf_op jit(solution)/shard_map/join/pallas_call | solution.py:501
Async XLA Ops:
  0.6 10.4 %collective-permute-start.1 = (bf16[256,512]{1,0:T(8,128)(2,1)}, bf16[256,512]{1,0:T(8,128)(2,1)S(1)}, u32[]{:S(2)}, u32[]{:S(2)}) collective-permute-start(bf16[256,512]{1,0:T(8,128)(2,1)} %audio.3), channel_id=1, source_target_pairs={{0,1},{1,0},{2,3},{3,2},{4,5},{5,4},{6,7},{7,6},{8,9},{9,8},{10,11... | collective-permute-start | bytes 786440 | tf_op jit(solution)/shard_map/ppermute | solution.py:375
  2.2 12.4 %collective-permute-start.7 = (bf16[256,512]{1,0:T(8,128)(2,1)}, bf16[256,512]{1,0:T(8,128)(2,1)S(1)}, u32[]{:S(2)}, u32[]{:S(2)}) collective-permute-start(bf16[256,512]{1,0:T(8,128)(2,1)} %video.3), channel_id=1, source_target_pairs={{0,1},{1,0},{2,3},{3,2},{4,5},{5,4},{6,7},{7,6},{8,9},{9,8},{10,11... | collective-permute-start | bytes 786440 | tf_op jit(solution)/shard_map/ppermute | solution.py:375
  3.9 5.3 %collective-permute-start = (bf16[528,128]{1,0:T(8,128)(2,1)S(1)}, bf16[528,128]{1,0:T(8,128)(2,1)S(1)}, u32[]{:S(2)}, u32[]{:S(2)}) collective-permute-start(bf16[528,128]{1,0:T(8,128)(2,1)S(1)} %get-tuple-element.41), channel_id=1, source_target_pairs={{0,2},{2,4},{4,6},{6,0},{8,10},{10,12},{12,14},{14,8},{16,18},{18,... | collective-permute-start | bytes 405512 | tf_op jit(solution)/shard_map/ppermute | solution.py:379
  4.0 7.1 %collective-permute-start.2 = (bf16[528,128]{1,0:T(8,128)(2,1)S(1)}, bf16[528,128]{1,0:T(8,128)(2,1)S(1)}, u32[]{:S(2)}, u32[]{:S(2)}) collective-permute-start(bf16[528,128]{1,0:T(8,128)(2,1)S(1)} %get-tuple-element.44), channel_id=1, source_target_pairs={{0,4},{2,6},{4,0},{6,2},{8,12},{10,14},{12,8},{14,10},{16,20},{18,... | collective-permute-start | bytes 405512 | tf_op jit(solution)/shard_map/ppermute | solution.py:379
  5.5 9.6 %collective-permute-start.6 = (bf16[528,128]{1,0:T(8,128)(2,1)S(1)}, bf16[528,128]{1,0:T(8,128)(2,1)S(1)}, u32[]{:S(2)}, u32[]{:S(2)}) collective-permute-start(bf16[528,128]{1,0:T(8,128)(2,1)S(1)} %get-tuple-element.50), channel_id=1, source_target_pairs={{0,6},{2,0},{4,2},{6,4},{8,14},{10,8},{12,10},{14,12},{16,22},{18,... | collective-permute-start | bytes 405512 | tf_op jit(solution)/shard_map/ppermute | solution.py:379
  11.4 5.2 %collective-permute-start.3 = (bf16[256,128]{1,0:T(8,128)(2,1)S(1)}, bf16[256,128]{1,0:T(8,128)(2,1)S(1)}, u32[]{:S(2)}, u32[]{:S(2)}) collective-permute-start(bf16[256,128]{1,0:T(8,128)(2,1)S(1)} %get-tuple-element.46), channel_id=1, source_target_pairs={{0,2},{2,4},{4,6},{6,0},{8,10},{10,12},{12,14},{14,8},{16,18},{18,... | collective-permute-start | bytes 196616 | tf_op jit(solution)/shard_map/ppermute | solution.py:379
  12.7 5.3 %collective-permute-start.4 = (bf16[256,128]{1,0:T(8,128)(2,1)S(1)}, bf16[256,128]{1,0:T(8,128)(2,1)S(1)}, u32[]{:S(2)}, u32[]{:S(2)}) collective-permute-start(bf16[256,128]{1,0:T(8,128)(2,1)S(1)} %get-tuple-element.47), channel_id=1, source_target_pairs={{0,4},{2,6},{4,0},{6,2},{8,12},{10,14},{12,8},{14,10},{16,20},{18,... | collective-permute-start | bytes 196616 | tf_op jit(solution)/shard_map/ppermute | solution.py:379
  14.1 3.8 %collective-permute-start.5 = (bf16[256,128]{1,0:T(8,128)(2,1)S(1)}, bf16[256,128]{1,0:T(8,128)(2,1)S(1)}, u32[]{:S(2)}, u32[]{:S(2)}) collective-permute-start(bf16[256,128]{1,0:T(8,128)(2,1)S(1)} %get-tuple-element.48), channel_id=1, source_target_pairs={{0,6},{2,0},{4,2},{6,4},{8,14},{10,8},{12,10},{14,12},{16,22},{18,... | collective-permute-start | bytes 196616 | tf_op jit(solution)/shard_map/ppermute | solution.py:379
  14.9 6.7 %collective-permute-start.10 = (bf16[256,128]{1,0:T(8,128)(2,1)S(1)}, bf16[256,128]{1,0:T(8,128)(2,1)S(1)}, u32[]{:S(2)}, u32[]{:S(2)}) collective-permute-start(bf16[256,128]{1,0:T(8,128)(2,1)S(1)} %get-tuple-element.56), channel_id=1, source_target_pairs={{0,2},{2,4},{4,6},{6,0},{8,10},{10,12},{12,14},{14,8},{16,18},{18,... | collective-permute-start | bytes 196616 | tf_op jit(solution)/shard_map/ppermute | solution.py:379
  15.1 6.5 %collective-permute-start.11 = (bf16[256,128]{1,0:T(8,128)(2,1)S(1)}, bf16[256,128]{1,0:T(8,128)(2,1)S(1)}, u32[]{:S(2)}, u32[]{:S(2)}) collective-permute-start(bf16[256,128]{1,0:T(8,128)(2,1)S(1)} %get-tuple-element.57), channel_id=1, source_target_pairs={{0,4},{2,6},{4,0},{6,2},{8,12},{10,14},{12,8},{14,10},{16,20},{18,... | collective-permute-start | bytes 196616 | tf_op jit(solution)/shard_map/ppermute | solution.py:379
  16.6 5.1 %collective-permute-start.12 = (bf16[256,128]{1,0:T(8,128)(2,1)S(1)}, bf16[256,128]{1,0:T(8,128)(2,1)S(1)}, u32[]{:S(2)}, u32[]{:S(2)}) collective-permute-start(bf16[256,128]{1,0:T(8,128)(2,1)S(1)} %get-tuple-element.58), channel_id=1, source_target_pairs={{0,6},{2,0},{4,2},{6,4},{8,14},{10,8},{12,10},{14,12},{16,22},{18,... | collective-permute-start | bytes 196616 | tf_op jit(solution)/shard_map/ppermute | solution.py:379
  18.0 9.7 %collective-permute-start.8 = (bf16[3,272,128]{2,1,0:T(8,128)(2,1)S(1)}, bf16[3,272,128]{2,1,0:T(8,128)(2,1)S(1)}, u32[]{:S(2)}, u32[]{:S(2)}) collective-permute-start(bf16[3,272,128]{2,1,0:T(8,128)(2,1)S(1)} %get-tuple-element.54), channel_id=1, source_target_pairs={{8,16},{10,18},{12,20},{14,22},{16,8},{18,10},{20,12},{22,14},{9,1... | collective-permute-start | bytes 626696 | tf_op jit(solution)/shard_map/ppermute | solution.py:384
  21.5 6.5 %collective-permute-start.9 = (bf16[3,272,128]{2,1,0:T(8,128)(2,1)S(1)}, bf16[3,272,128]{2,1,0:T(8,128)(2,1)S(1)}, u32[]{:S(2)}, u32[]{:S(2)}) collective-permute-start(bf16[3,272,128]{2,1,0:T(8,128)(2,1)S(1)} %get-tuple-element.55), channel_id=1, source_target_pairs={{0,8},{2,10},{4,12},{6,14},{8,0},{10,2},{12,4},{14,6},{16,24},{18,... | collective-permute-start | bytes 626696 | tf_op jit(solution)/shard_map/ppermute | solution.py:384
  25.0 10.6 %collective-permute-start.15 = (bf16[3,256,128]{2,1,0:T(8,128)(2,1)S(1)}, bf16[3,256,128]{2,1,0:T(8,128)(2,1)S(1)}, u32[]{:S(2)}, u32[]{:S(2)}) collective-permute-start(bf16[3,256,128]{2,1,0:T(8,128)(2,1)S(1)} %get-tuple-element.65), channel_id=1, source_target_pairs={{8,16},{10,18},{12,20},{14,22},{16,8},{18,10},{20,12},{22,14},{9,1... | collective-permute-start | bytes 589832 | tf_op jit(solution)/shard_map/ppermute | solution.py:384
  27.3 8.2 %collective-permute-start.16 = (bf16[3,256,128]{2,1,0:T(8,128)(2,1)S(1)}, bf16[3,256,128]{2,1,0:T(8,128)(2,1)S(1)}, u32[]{:S(2)}, u32[]{:S(2)}) collective-permute-start(bf16[3,256,128]{2,1,0:T(8,128)(2,1)S(1)} %get-tuple-element.66), channel_id=1, source_target_pairs={{0,8},{2,10},{4,12},{6,14},{8,0},{10,2},{12,4},{14,6},{16,24},{18,... | collective-permute-start | bytes 589832 | tf_op jit(solution)/shard_map/ppermute | solution.py:384
  30.7 8.3 %collective-permute-start.13 = (bf16[3,288,128]{2,1,0:T(8,128)(2,1)S(1)}, bf16[3,288,128]{2,1,0:T(8,128)(2,1)S(1)}, u32[]{:S(2)}, u32[]{:S(2)}) collective-permute-start(bf16[3,288,128]{2,1,0:T(8,128)(2,1)S(1)} %get-tuple-element.61), channel_id=1, source_target_pairs={{0,8},{2,10},{4,12},{6,14},{8,0},{10,2},{12,4},{14,6},{16,24},{18,... | collective-permute-start | bytes 663560 | tf_op jit(solution)/shard_map/ppermute | solution.py:384
  32.1 8.5 %collective-permute-start.14 = (bf16[3,288,128]{2,1,0:T(8,128)(2,1)S(1)}, bf16[3,288,128]{2,1,0:T(8,128)(2,1)S(1)}, u32[]{:S(2)}, u32[]{:S(2)}) collective-permute-start(bf16[3,288,128]{2,1,0:T(8,128)(2,1)S(1)} %get-tuple-element.62), channel_id=1, source_target_pairs={{8,16},{10,18},{12,20},{14,22},{16,8},{18,10},{20,12},{22,14},{9,1... | collective-permute-start | bytes 663560 | tf_op jit(solution)/shard_map/ppermute | solution.py:384
  38.3 9.0 %collective-permute-start.22 = (bf16[256,128]{1,0:T(8,128)(2,1)S(1)}, bf16[256,128]{1,0:T(8,128)(2,1)S(1)}, u32[]{:S(2)}, u32[]{:S(2)}) collective-permute-start(bf16[256,128]{1,0:T(8,128)(2,1)S(1)} %get-tuple-element.79), channel_id=1, source_target_pairs={{0,6},{2,0},{4,2},{6,4},{8,14},{10,8},{12,10},{14,12},{16,22},{18,... | collective-permute-start | bytes 196616 | tf_op jit(solution)/shard_map/ppermute | solution.py:379
  38.4 8.9 %collective-permute-start.21 = (bf16[256,128]{1,0:T(8,128)(2,1)S(1)}, bf16[256,128]{1,0:T(8,128)(2,1)S(1)}, u32[]{:S(2)}, u32[]{:S(2)}) collective-permute-start(bf16[256,128]{1,0:T(8,128)(2,1)S(1)} %get-tuple-element.68.refs_0_), channel_id=1, source_target_pairs={{0,4},{2,6},{4,0},{6,2},{8,12},{10,14},{12,8},{14,10},{16,20},{18,... | collective-permute-start | bytes 196616 | tf_op jit(solution)/shard_map/ppermute | solution.py:379
  41.1 5.3 %collective-permute-start.17 = (bf16[256,128]{1,0:T(8,128)(2,1)S(1)}, bf16[256,128]{1,0:T(8,128)(2,1)S(1)}, u32[]{:S(2)}, u32[]{:S(2)}) collective-permute-start(bf16[256,128]{1,0:T(8,128)(2,1)S(1)} %get-tuple-element.70), channel_id=1, source_target_pairs={{0,2},{2,4},{4,6},{6,0},{8,10},{10,12},{12,14},{14,8},{16,18},{18,... | collective-permute-start | bytes 196616 | tf_op jit(solution)/shard_map/ppermute | solution.py:379
  41.2 5.3 %collective-permute-start.18 = (bf16[256,128]{1,0:T(8,128)(2,1)S(1)}, bf16[256,128]{1,0:T(8,128)(2,1)S(1)}, u32[]{:S(2)}, u32[]{:S(2)}) collective-permute-start(bf16[256,128]{1,0:T(8,128)(2,1)S(1)} %get-tuple-element.71), channel_id=1, source_target_pairs={{0,4},{2,6},{4,0},{6,2},{8,12},{10,14},{12,8},{14,10},{16,20},{18,... | collective-permute-start | bytes 196616 | tf_op jit(solution)/shard_map/ppermute | solution.py:379
  42.8 3.7 %collective-permute-start.19 = (bf16[256,128]{1,0:T(8,128)(2,1)S(1)}, bf16[256,128]{1,0:T(8,128)(2,1)S(1)}, u32[]{:S(2)}, u32[]{:S(2)}) collective-permute-start(bf16[256,128]{1,0:T(8,128)(2,1)S(1)} %get-tuple-element.72), channel_id=1, source_target_pairs={{0,6},{2,0},{4,2},{6,4},{8,14},{10,8},{12,10},{14,12},{16,22},{18,... | collective-permute-start | bytes 196616 | tf_op jit(solution)/shard_map/ppermute | solution.py:379
  46.4 3.7 %collective-permute-start.20 = (bf16[256,128]{1,0:T(8,128)(2,1)S(1)}, bf16[256,128]{1,0:T(8,128)(2,1)S(1)}, u32[]{:S(2)}, u32[]{:S(2)}) collective-permute-start(bf16[256,128]{1,0:T(8,128)(2,1)S(1)} %get-tuple-element.78), channel_id=1, source_target_pairs={{0,2},{2,4},{4,6},{6,0},{8,10},{10,12},{12,14},{14,8},{16,18},{18,... | collective-permute-start | bytes 196616 | tf_op jit(solution)/shard_map/ppermute | solution.py:379

commit v19 on v15

--- a/solution.py
+++ b/solution.py
@@ -212,8 +212,10 @@
         scores = ahead
         if b + 1 < GROUP:
             ahead = product(asks[b + 1], turned[...])
-        peak, sums[b] = attend([scores], [beside[...]])
-        peaks[b] = jnp.broadcast_to(peak, (peak.shape[0], width))
+        peak, mixed = attend([scores], [beside[...]])
+        peaks[b] = by_head(jnp.broadcast_to(peak, (peak.shape[0], width)), rows)
+        sums[b, 0] = by_head(mixed[:, :width], rows)
+        sums[b, 1] = by_head(mixed[:, width:], rows)
 
 
 def lend_kernel(edge_b, edge_a, plane_turned, plane_beside, first, second, turned, ordered, results):
@@ -242,21 +244,20 @@
         if e + 1 < 2 * RADIUS:
             ahead = scores_of(e + 1)
         peak, mixed = attend([scores], [plane_beside[blocks[e]]])
-        mean = by_head(mixed[:, :width], rows) / by_head(mixed[:, width:], rows)
-        results[side, j, :rows] = mean.astype(results.dtype)
-        logs = peak + jnp.log(mixed[:, width:])
-        high = logs.astype(jnp.bfloat16)
-        rest = logs - high.astype(jnp.float32)
-        middle = rest.astype(jnp.bfloat16)
-        low = (rest - middle.astype(jnp.float32)).astype(jnp.bfloat16)
-        picked = jnp.zeros((rows, width), jnp.bfloat16)
-        for h in range(width // HEAD):
-            for n, piece in enumerate((high, middle, low)):
-                picked = jnp.where(lane == 8 * h + n, piece[h * rows : (h + 1) * rows], picked)
+        total = by_head(mixed[:, width:], rows)
+        results[side, j, :rows] = (by_head(mixed[:, :width], rows) / total).astype(results.dtype)
+        logs = by_head(jnp.broadcast_to(peak, (peak.shape[0], width)), rows) + jnp.log(total)
+        high = logs.astype(jnp.bfloat16).astype(jnp.float32)
+        middle = (logs - high).astype(jnp.bfloat16).astype(jnp.float32)
+        low = logs - high - middle
+        picked = jnp.where(lane % HEAD == 0, high, jnp.where(lane % HEAD == 1, middle, low))
         for part in range(rows // width):
-            stats = jnp.transpose(picked[part * width : (part + 1) * width])
+            flipped = jnp.transpose(picked[part * width : (part + 1) * width])
+            stats = [flipped[h : h + STAT_ROWS // 2] for h in range(0, width, HEAD)]
             at = rows + part * STAT_ROWS
-            results[side, j, at : at + STAT_ROWS] = stats[:STAT_ROWS]
+            results[side, j, at : at + STAT_ROWS] = jnp.concatenate(stats, axis=0).astype(
+                results.dtype
+            )
     first[...] = results[1 - odd]
     second[...] = results[odd]
 
@@ -338,13 +339,13 @@
         if b >= GROUP - RADIUS:
             theirs.append((1, b - (GROUP - RADIUS)))
         theirs = [(logs(*t), backs[t[0], t[1], :rows].astype(jnp.float32)) for t in theirs]
-        old = by_head(peaks[b], rows)
+        old = peaks[b]
         top = old
         for log, _ in theirs:
             top = jnp.maximum(top, log)
         factor = jnp.exp(old - top)
-        value = by_head(sums[b, :, :width], rows) * factor
-        total = by_head(sums[b, :, width:], rows) * factor
+        value = sums[b, 0] * factor
+        total = sums[b, 1] * factor
         for log, mean in theirs:
             weight = jnp.exp(log - top)
             value += weight * mean
@@ -440,14 +441,14 @@
     asks = shape((GROUP, heads * rows, 2 * width), bf16)
     peaks, sums, plane_turned, plane_beside = call(
         rows_kernel,
-        [shape((GROUP, heads * rows, n * width), f32) for n in (1, 2)] + [turned, beside],
+        [shape((GROUP, rows, width), f32), shape((GROUP, 2, rows, width), f32), turned, beside],
         [pltpu.VMEM(asks.shape, bf16)],
         flops=16 * GROUP * rows * inside * width,
         moved=8 * inside * width * 2,
         exps=2 * GROUP * rows * inside,
         name="rows",
     )(*packs, *queries, *keys)
-    audio_edges = halo(packs, [], peaks)
+    audio_edges = halo(packs, [])
     back = shape((RADIUS, rows + rows // width * STAT_ROWS, width), bf16)
     lent_a, lent_b, edge_turned = call(
         lend_kernel,

time: 49.2 us -> 48.1 us (0.978)
  starting transfers between devices: 28 us -> 26.3 us
  waiting for transfers between devices: 3.34 us -> 3.88 us
    ppermute x15, starting transfers between devices: 16.2 us -> 15.1 us  [traded(): lax.ppermute(pieces[k], 'tm', pairs(k))]
    ppermute x6, waiting for transfers between devices: 0.02 us -> 0.69 us  [crossed(): lax.ppermute(sent, 'tm', [(p * GROUP + i, q * GROUP + i) for p, q in pair...]
    ppermute x6, starting transfers between devices: 10.3 us -> 9.66 us  [crossed(): lax.ppermute(sent, 'tm', [(p * GROUP + i, q * GROUP + i) for p, q in pair...]
  transfers between devices with their start and end apart: 23 -> 23, of which waited for: 4 -> 4; matrix products, arithmetic and copies ran while one was open for 0% -> 0% of each run, Pallas kernels for 32% -> 33%
where the time goes in v19:
time: 48.1 us; the launch traced here: 47.8 us
  starting transfers between devices  26.3 us (55%)
  Pallas kernels  16.7 us (35%)
  waiting for transfers between devices  3.88 us (8%)
  between operations  1 us (2%)
    ppermute x15, starting transfers between devices, traded(): lax.ppermute(pieces[k], 'tm', pairs(k))  15.1 us
    ppermute x6, starting transfers between devices, crossed(): lax.ppermute(sent, 'tm', [(p * GROUP + i, q * GROUP + i) for p, q in pair...  9.66 us
    pallas_call x1, Pallas kernels, local(): call(rows_kernel, [shape((GROUP, rows, width), f32), shape((GROUP, 2, row...  3.3 us
    ppermute x15, waiting for transfers between devices, traded(): lax.ppermute(pieces[k], 'tm', pairs(k))  2.76 us
    pallas_call x1, Pallas kernels, local(): call(functools.partial(columns_kernel, far), [piece] * len(far) + shared,...  2.65 us
    pallas_call x1, Pallas kernels, local(): call(lend_kernel, [back, back, shape((2 * width, around), bf16)], [pltpu....  2.63 us
    pallas_call x1, Pallas kernels, local(): call(functools.partial(columns_kernel, near), [piece] * len(near), ins=[V...  2.26 us
    pallas_call x1, Pallas kernels, local(): call(prepare_kernel, [part, part, square, square], [pltpu.VMEM((rows, hal...  1.78 us
  transfers between devices with their start and end apart: 23, of which 4 were waited for; matrix products, arithmetic and copies ran while one was open for 0% of the time, Pallas kernels for 33%

profile of v19, /device:TPU:9, one launch (start us, length us, event | category | flops | bytes accessed | tf_op | source)
XLA Modules:
  0.0 47.8 jit_solution(6897591670341787076)
XLA Ops:
  0.6 1.3 %collective-permute-start.1 = (bf16[256,512]{1,0:T(8,128)(2,1)}, bf16[256,512]{1,0:T(8,128)(2,1)S(1)}, u32[]{:S(2)}, u32[]{:S(2)}) collective-permute-start(bf16[256,512]{1,0:T(8,128)(2,1)} %audio.3), channel_id=1, source_target_pairs={{0,1},{1,0},{2,3},{3,2},{4,5},{5,4},{6,7},{7,6},{8,9},{9,8},{10,11... | collective-permute-start | bytes 786440 | tf_op jit(solution)/shard_map/ppermute | solution.py:368
  1.9 0.2 collective-permute-start.7
  2.2 1.2 %split.1 = (bf16[528,128]{1,0:T(8,128)(2,1)S(1)}, bf16[528,128]{1,0:T(8,128)(2,1)S(1)}, bf16[528,128]{1,0:T(8,128)(2,1)S(1)}, bf16[528,128]{1,0:T(8,128)(2,1)S(1)}) custom-call(bf16[256,512]{1,0:T(8,128)(2,1)} %audio.3, bf16[256,512]{1,0:T(8,128)(2,1)} %video.3, s32[2,128]{1,0:T(2,128)} %bitcast.1), custom_call_target="tpu_custom_call" | custom-call | bytes 1048576 | tf_op jit(solution)/shard_map/split/pallas_call | solution.py:390
  3.3 1.3 %collective-permute-start = (bf16[528,128]{1,0:T(8,128)(2,1)S(1)}, bf16[528,128]{1,0:T(8,128)(2,1)S(1)}, u32[]{:S(2)}, u32[]{:S(2)}) collective-permute-start(bf16[528,128]{1,0:T(8,128)(2,1)S(1)} %get-tuple-element.41), channel_id=1, source_target_pairs={{0,2},{2,0},{4,6},{6,4},{8,10},{10,8},{12,14},{14,12},{16,18},{18,... | collective-permute-start | bytes 405512 | tf_op jit(solution)/shard_map/ppermute | solution.py:372
  4.6 1.2 %collective-permute-start.2 = (bf16[528,128]{1,0:T(8,128)(2,1)S(1)}, bf16[528,128]{1,0:T(8,128)(2,1)S(1)}, u32[]{:S(2)}, u32[]{:S(2)}) collective-permute-start(bf16[528,128]{1,0:T(8,128)(2,1)S(1)} %get-tuple-element.44), channel_id=1, source_target_pairs={{0,4},{2,6},{4,0},{6,2},{8,12},{10,14},{12,8},{14,10},{16,20},{18,... | collective-permute-start | bytes 405512 | tf_op jit(solution)/shard_map/ppermute | solution.py:372
  5.9 0.5 %collective-permute-start.6 = (bf16[528,128]{1,0:T(8,128)(2,1)S(1)}, bf16[528,128]{1,0:T(8,128)(2,1)S(1)}, u32[]{:S(2)}, u32[]{:S(2)}) collective-permute-start(bf16[528,128]{1,0:T(8,128)(2,1)S(1)} %get-tuple-element.50), channel_id=1, source_target_pairs={{0,6},{2,4},{4,2},{6,0},{8,14},{10,12},{12,10},{14,8},{16,22},{18,... | collective-permute-start | bytes 405512 | tf_op jit(solution)/shard_map/ppermute | solution.py:372
  6.3 0.0 collective-permute-done.refs_0_.refs_5_.refs_1_
  6.3 1.8 %prepare.1 = (f32[256,512]{1,0:T(8,128)S(1)}, f32[256,512]{1,0:T(8,128)S(1)}, bf16[512,512]{1,0:T(8,128)(2,1)S(1)}, bf16[512,512]{1,0:T(8,128)(2,1)S(1)}) custom-call(bf16[256,512]{1,0:T(8,128)(2,1)} %audio.3, bf16[256,512]{1,0:T(8,128)(2,1)} %video.3, bf16[1024,512]{1,0:T(8,128)(2,1)} %query.1, bf16[1024,512]{1,0:T(8,128)(2,1)} %key.1, ...), custom_call_target="tpu_custom_call" | custom-call | flops 268435456 | bytes 4194304 | tf_op jit(solution)/shard_map/prepare/pallas_call | solution.py:400
  8.1 1.7 %collective-permute-done.2.refs_1_.refs_6_.refs_2_ = bf16[528,128]{1,0:T(8,128)(2,1)S(1)} collective-permute-done((bf16[528,128]{1,0:T(8,128)(2,1)S(1)}, bf16[528,128]{1,0:T(8,128)(2,1)S(1)}, u32[]{:S(2)}, u32[]{:S(2)}) %collective-permute-start.2) | collective-permute-done | bytes 135200 | tf_op jit(solution)/shard_map/ppermute | solution.py:372
  9.8 0.0 collective-permute-done.1.other
  9.8 0.4 project.2
  10.2 1.4 %collective-permute-start.3 = (bf16[256,128]{1,0:T(8,128)(2,1)S(1)}, bf16[256,128]{1,0:T(8,128)(2,1)S(1)}, u32[]{:S(2)}, u32[]{:S(2)}) collective-permute-start(bf16[256,128]{1,0:T(8,128)(2,1)S(1)} %get-tuple-element.46), channel_id=1, source_target_pairs={{0,2},{2,0},{4,6},{6,4},{8,10},{10,8},{12,14},{14,12},{16,18},{18,... | collective-permute-start | bytes 196616 | tf_op jit(solution)/shard_map/ppermute | solution.py:372
  11.6 1.2 %collective-permute-start.4 = (bf16[256,128]{1,0:T(8,128)(2,1)S(1)}, bf16[256,128]{1,0:T(8,128)(2,1)S(1)}, u32[]{:S(2)}, u32[]{:S(2)}) collective-permute-start(bf16[256,128]{1,0:T(8,128)(2,1)S(1)} %get-tuple-element.47), channel_id=1, source_target_pairs={{0,4},{2,6},{4,0},{6,2},{8,12},{10,14},{12,8},{14,10},{16,20},{18,... | collective-permute-start | bytes 196616 | tf_op jit(solution)/shard_map/ppermute | solution.py:372
  12.8 0.5 collective-permute-start.5
  13.3 0.4 collective-permute-done.7.other
  13.7 0.4 project.3
  14.1 1.6 %collective-permute-start.10 = (bf16[256,128]{1,0:T(8,128)(2,1)S(1)}, bf16[256,128]{1,0:T(8,128)(2,1)S(1)}, u32[]{:S(2)}, u32[]{:S(2)}) collective-permute-start(bf16[256,128]{1,0:T(8,128)(2,1)S(1)} %get-tuple-element.56), channel_id=1, source_target_pairs={{0,2},{2,0},{4,6},{6,4},{8,10},{10,8},{12,14},{14,12},{16,18},{18,... | collective-permute-start | bytes 196616 | tf_op jit(solution)/shard_map/ppermute | solution.py:372
  15.7 0.0 collective-permute-done.6.refs_7_.refs_3_
  15.7 1.2 %collective-permute-start.11 = (bf16[256,128]{1,0:T(8,128)(2,1)S(1)}, bf16[256,128]{1,0:T(8,128)(2,1)S(1)}, u32[]{:S(2)}, u32[]{:S(2)}) collective-permute-start(bf16[256,128]{1,0:T(8,128)(2,1)S(1)} %get-tuple-element.57), channel_id=1, source_target_pairs={{0,4},{2,6},{4,0},{6,2},{8,12},{10,14},{12,8},{14,10},{16,20},{18,... | collective-permute-start | bytes 196616 | tf_op jit(solution)/shard_map/ppermute | solution.py:372
  16.9 0.0 collective-permute-done.3.refs_1_.refs_5_
  16.9 0.5 %collective-permute-start.12 = (bf16[256,128]{1,0:T(8,128)(2,1)S(1)}, bf16[256,128]{1,0:T(8,128)(2,1)S(1)}, u32[]{:S(2)}, u32[]{:S(2)}) collective-permute-start(bf16[256,128]{1,0:T(8,128)(2,1)S(1)} %get-tuple-element.58), channel_id=1, source_target_pairs={{0,6},{2,4},{4,2},{6,0},{8,14},{10,12},{12,10},{14,8},{16,22},{18,... | collective-permute-start | bytes 196616 | tf_op jit(solution)/shard_map/ppermute | solution.py:372
  17.4 0.0 collective-permute-done.4.refs_2_.refs_6_
  17.4 0.0 collective-permute-done.5.refs_3_.refs_7_
  17.4 0.1 halo.2
  17.5 3.2 %collective-permute-start.8 = (bf16[3,272,128]{2,1,0:T(8,128)(2,1)S(1)}, bf16[3,272,128]{2,1,0:T(8,128)(2,1)S(1)}, u32[]{:S(2)}, u32[]{:S(2)}) collective-permute-start(bf16[3,272,128]{2,1,0:T(8,128)(2,1)S(1)} %get-tuple-element.54), channel_id=1, source_target_pairs={{8,16},{10,18},{12,20},{14,22},{16,8},{18,10},{20,12},{22,14},{9,1... | collective-permute-start | bytes 626696 | tf_op jit(solution)/shard_map/ppermute | solution.py:377
  20.7 0.1 collective-permute-start.9
  20.8 0.1 halo.3
  20.9 0.0 collective-permute-done.10.refs_9_
  20.9 2.1 %collective-permute-start.15 = (bf16[3,256,128]{2,1,0:T(8,128)(2,1)S(1)}, bf16[3,256,128]{2,1,0:T(8,128)(2,1)S(1)}, u32[]{:S(2)}, u32[]{:S(2)}) collective-permute-start(bf16[3,256,128]{2,1,0:T(8,128)(2,1)S(1)} %get-tuple-element.65), channel_id=1, source_target_pairs={{8,16},{10,18},{12,20},{14,22},{16,8},{18,10},{20,12},{22,14},{9,1... | collective-permute-start | bytes 589832 | tf_op jit(solution)/shard_map/ppermute | solution.py:377
  23.0 0.0 collective-permute-done.11.refs_10_
  23.0 0.1 collective-permute-start.16
  23.1 0.0 collective-permute-done.12.refs_11_
  23.1 3.3 %rows.1 = (f32[4,256,128]{2,1,0:T(8,128)S(1)}, f32[4,2,256,128]{3,2,1,0:T(8,128)S(1)}, bf16[256,1024]{1,0:T(8,128)(2,1)S(1)}, bf16[1024,256]{1,0:T(8,128)(2,1)S(1)}) custom-call(bf16[528,128]{1,0:T(8,128)(2,1)S(1)} %get-tuple-element.49.refs_4_.refs_0_, bf16[528,128]{1,0:T(8,128)(2,1)S(1)} %collective-permute-done.refs_0_.refs_5_.refs_1_, ...), custom_call_target="tpu_custom_call" | custom-call | flops 2147483648 | bytes 2097152 | tf_op jit(solution)/shard_map/rows/pallas_call | solution.py:442
  26.4 0.0 collective-permute-done.8.edge_b
  26.4 0.7 %collective-permute-done.9.edge_a = bf16[3,272,128]{2,1,0:T(8,128)(2,1)S(1)} collective-permute-done((bf16[3,272,128]{2,1,0:T(8,128)(2,1)S(1)}, bf16[3,272,128]{2,1,0:T(8,128)(2,1)S(1)}, u32[]{:S(2)}, u32[]{:S(2)}) %collective-permute-start.9) | collective-permute-done | bytes 208928 | tf_op jit(solution)/shard_map/ppermute | solution.py:377
  27.1 2.6 %lend.1 = (bf16[3,288,128]{2,1,0:T(8,128)(2,1)S(1)}, bf16[3,288,128]{2,1,0:T(8,128)(2,1)S(1)}, bf16[256,1536]{1,0:T(8,128)(2,1)S(1)}) custom-call(bf16[3,272,128]{2,1,0:T(8,128)(2,1)S(1)} %collective-permute-done.8.edge_b, bf16[3,272,128]{2,1,0:T(8,128)(2,1)S(1)} %collective-permute-done.9.edge_a, bf16[256,1024]{1,0:T(8,128)(2,1)S(1)} %get-tuple-element.59.plane_turned, ...), custom_call_target="tpu_custom_call" | custom-call | flops 4831838208 | bytes 3145728 | tf_op jit(solution)/shard_map/lend/pallas_call | solution.py:453
  29.7 0.9 %collective-permute-start.13 = (bf16[3,288,128]{2,1,0:T(8,128)(2,1)S(1)}, bf16[3,288,128]{2,1,0:T(8,128)(2,1)S(1)}, u32[]{:S(2)}, u32[]{:S(2)}) collective-permute-start(bf16[3,288,128]{2,1,0:T(8,128)(2,1)S(1)} %get-tuple-element.61), channel_id=1, source_target_pairs={{0,8},{2,10},{4,12},{6,14},{8,0},{10,2},{12,4},{14,6},{16,24},{18,... | collective-permute-start | bytes 663560 | tf_op jit(solution)/shard_map/ppermute | solution.py:377
  30.6 3.4 %collective-permute-start.14 = (bf16[3,288,128]{2,1,0:T(8,128)(2,1)S(1)}, bf16[3,288,128]{2,1,0:T(8,128)(2,1)S(1)}, u32[]{:S(2)}, u32[]{:S(2)}) collective-permute-start(bf16[3,288,128]{2,1,0:T(8,128)(2,1)S(1)} %get-tuple-element.62), channel_id=1, source_target_pairs={{8,16},{10,18},{12,20},{14,22},{16,8},{18,10},{20,12},{22,14},{9,1... | collective-permute-start | bytes 663560 | tf_op jit(solution)/shard_map/ppermute | solution.py:377
  33.9 0.0 collective-permute-done.15.refs_12_
  33.9 0.0 collective-permute-done.16.refs_13_
  34.0 2.6 %columns.2 = (bf16[256,128]{1,0:T(8,128)(2,1)S(1)}, bf16[256,128]{1,0:T(8,128)(2,1)S(1)}, bf16[256,1024]{1,0:T(8,128)(2,1)S(1)}, bf16[1024,256]{1,0:T(8,128)(2,1...) custom-call(bf16[528,128]{1,0:T(8,128)(2,1)S(1)} %get-tuple-element.49.refs_4_.refs_0_, ...), custom_call_target="tpu_custom_call" | custom-call | flops 1879048192 | bytes 1572864 | tf_op jit(solution)/shard_map/columns/pallas_call | solution.py:472
  36.6 2.7 %collective-permute-start.22 = (bf16[256,128]{1,0:T(8,128)(2,1)S(1)}, bf16[256,128]{1,0:T(8,128)(2,1)S(1)}, u32[]{:S(2)}, u32[]{:S(2)}) collective-permute-start(bf16[256,128]{1,0:T(8,128)(2,1)S(1)} %get-tuple-element.79), channel_id=1, source_target_pairs={{0,6},{2,4},{4,2},{6,0},{8,14},{10,12},{12,10},{14,8},{16,22},{18,... | collective-permute-start | bytes 196616 | tf_op jit(solution)/shard_map/ppermute | solution.py:372
  39.3 0.3 collective-permute-start.21
  39.6 0.0 collective-permute-done.13.back_a
  39.6 0.0 collective-permute-done.14.back_b
  39.6 0.5 %merge.1 = (bf16[256,128]{1,0:T(8,128)(2,1)S(1)}, bf16[256,128]{1,0:T(8,128)(2,1)S(1)}, bf16[256,128]{1,0:T(8,128)(2,1)S(1)}, bf16[256,128]{1,0:T(8,128)(2,1)S(1)}) custom-call(bf16[3,288,128]{2,1,0:T(8,128)(2,1)S(1)} %collective-permute-done.13.back_a, bf16[3,288,128]{2,1,0:T(8,128)(2,1)S(1)} %collective-permute-done.14.back_b, ...), custom_call_target="tpu_custom_call" | custom-call | bytes 2097152 | tf_op jit(solution)/shard_map/merge/pallas_call | solution.py:475
  40.1 0.8 %collective-permute-start.17 = (bf16[256,128]{1,0:T(8,128)(2,1)S(1)}, bf16[256,128]{1,0:T(8,128)(2,1)S(1)}, u32[]{:S(2)}, u32[]{:S(2)}) collective-permute-start(bf16[256,128]{1,0:T(8,128)(2,1)S(1)} %get-tuple-element.70), channel_id=1, source_target_pairs={{0,2},{2,0},{4,6},{6,4},{8,10},{10,8},{12,14},{14,12},{16,18},{18,... | collective-permute-start | bytes 196616 | tf_op jit(solution)/shard_map/ppermute | solution.py:372
  40.9 1.2 %collective-permute-start.18 = (bf16[256,128]{1,0:T(8,128)(2,1)S(1)}, bf16[256,128]{1,0:T(8,128)(2,1)S(1)}, u32[]{:S(2)}, u32[]{:S(2)}) collective-permute-start(bf16[256,128]{1,0:T(8,128)(2,1)S(1)} %get-tuple-element.71), channel_id=1, source_target_pairs={{0,4},{2,6},{4,0},{6,2},{8,12},{10,14},{12,8},{14,10},{16,20},{18,... | collective-permute-start | bytes 196616 | tf_op jit(solution)/shard_map/ppermute | solution.py:372
  42.1 0.5 %collective-permute-start.19 = (bf16[256,128]{1,0:T(8,128)(2,1)S(1)}, bf16[256,128]{1,0:T(8,128)(2,1)S(1)}, u32[]{:S(2)}, u32[]{:S(2)}) collective-permute-start(bf16[256,128]{1,0:T(8,128)(2,1)S(1)} %get-tuple-element.72), channel_id=1, source_target_pairs={{0,6},{2,4},{4,2},{6,0},{8,14},{10,12},{12,10},{14,8},{16,22},{18,... | collective-permute-start | bytes 196616 | tf_op jit(solution)/shard_map/ppermute | solution.py:372
  42.6 2.3 %columns.3 = (bf16[256,128]{1,0:T(8,128)(2,1)S(1)}, bf16[256,128]{1,0:T(8,128)(2,1)S(1)}) custom-call(bf16[256,1536]{1,0:T(8,128)(2,1)S(1)} %get-tuple-element.67.refs_14_.refs_0_, bf16[256,1024]{1,0:T(8,128)(2,1)S(1)} %get-tuple-element.73.refs_1_, bf16[1024,256]{1,0:T(8,128)(2,1)S(1)} %get-tuple-element.74.refs_2_, ...), custom_call_target="tpu_custom_call" | custom-call | flops 1879048192 | bytes 1572864 | tf_op jit(solution)/shard_map/columns/pallas_call | solution.py:485
  44.8 0.0 collective-permute-done.17.refs_1_
  44.8 0.2 collective-permute-start.20
  45.1 0.0 collective-permute-done.18.refs_2_
  45.1 1.1 %collective-permute-done.19.refs_3_ = bf16[256,128]{1,0:T(8,128)(2,1)S(1)} collective-permute-done((bf16[256,128]{1,0:T(8,128)(2,1)S(1)}, bf16[256,128]{1,0:T(8,128)(2,1)S(1)}, u32[]{:S(2)}, u32[]{:S(2)}) %collective-permute-start.19) | collective-permute-done | bytes 65568 | tf_op jit(solution)/shard_map/ppermute | solution.py:372
  46.1 0.7 %join.2 = bf16[256,512]{1,0:T(8,128)(2,1)} custom-call(bf16[256,128]{1,0:T(8,128)(2,1)S(1)} %get-tuple-element.69.refs_0_.refs_5_, bf16[256,128]{1,0:T(8,128)(2,1)S(1)} %collective-permute-done.17.refs_1_, bf16[256,128]{1,0:T(8,128)(2,1)S(1)} %collective-permute-done.18.refs_2_, bf16[256,128]{1,0:T(8,128)(2,1)S(1)} %collective-permute-done.19.refs_3_), custom_call_target="tpu_custom_call" | custom-call | bytes 524288 | tf_op jit(solution)/shard_map/join/pallas_call | solution.py:494
  46.9 0.0 collective-permute-done.22.refs_3_
  46.9 0.0 collective-permute-done.21.refs_2_
  46.9 0.0 collective-permute-done.20.refs_1_
  46.9 0.7 %join.3 = bf16[256,512]{1,0:T(8,128)(2,1)} custom-call(bf16[256,128]{1,0:T(8,128)(2,1)S(1)} %get-tuple-element.77.refs_0_, bf16[256,128]{1,0:T(8,128)(2,1)S(1)} %collective-permute-done.20.refs_1_, bf16[256,128]{1,0:T(8,128)(2,1)S(1)} %collective-permute-done.21.refs_2_, bf16[256,128]{1,0:T(8,128)(2,1)S(1)} %collective-permute-done.22.refs_3_), custom_call_target="tpu_custom_call" | custom-call | bytes 524288 | tf_op jit(solution)/shard_map/join/pallas_call | solution.py:494
Async XLA Ops:
  0.6 9.2 %collective-permute-start.1 = (bf16[256,512]{1,0:T(8,128)(2,1)}, bf16[256,512]{1,0:T(8,128)(2,1)S(1)}, u32[]{:S(2)}, u32[]{:S(2)}) collective-permute-start(bf16[256,512]{1,0:T(8,128)(2,1)} %audio.3), channel_id=1, source_target_pairs={{0,1},{1,0},{2,3},{3,2},{4,5},{5,4},{6,7},{7,6},{8,9},{9,8},{10,11... | collective-permute-start | bytes 786440 | tf_op jit(solution)/shard_map/ppermute | solution.py:368
  1.9 11.8 %collective-permute-start.7 = (bf16[256,512]{1,0:T(8,128)(2,1)}, bf16[256,512]{1,0:T(8,128)(2,1)S(1)}, u32[]{:S(2)}, u32[]{:S(2)}) collective-permute-start(bf16[256,512]{1,0:T(8,128)(2,1)} %video.3), channel_id=1, source_target_pairs={{0,1},{1,0},{2,3},{3,2},{4,5},{5,4},{6,7},{7,6},{8,9},{9,8},{10,11... | collective-permute-start | bytes 786440 | tf_op jit(solution)/shard_map/ppermute | solution.py:368
  3.3 3.0 %collective-permute-start = (bf16[528,128]{1,0:T(8,128)(2,1)S(1)}, bf16[528,128]{1,0:T(8,128)(2,1)S(1)}, u32[]{:S(2)}, u32[]{:S(2)}) collective-permute-start(bf16[528,128]{1,0:T(8,128)(2,1)S(1)} %get-tuple-element.41), channel_id=1, source_target_pairs={{0,2},{2,0},{4,6},{6,4},{8,10},{10,8},{12,14},{14,12},{16,18},{18,... | collective-permute-start | bytes 405512 | tf_op jit(solution)/shard_map/ppermute | solution.py:372
  4.6 5.2 %collective-permute-start.2 = (bf16[528,128]{1,0:T(8,128)(2,1)S(1)}, bf16[528,128]{1,0:T(8,128)(2,1)S(1)}, u32[]{:S(2)}, u32[]{:S(2)}) collective-permute-start(bf16[528,128]{1,0:T(8,128)(2,1)S(1)} %get-tuple-element.44), channel_id=1, source_target_pairs={{0,4},{2,6},{4,0},{6,2},{8,12},{10,14},{12,8},{14,10},{16,20},{18,... | collective-permute-start | bytes 405512 | tf_op jit(solution)/shard_map/ppermute | solution.py:372
  5.9 9.8 %collective-permute-start.6 = (bf16[528,128]{1,0:T(8,128)(2,1)S(1)}, bf16[528,128]{1,0:T(8,128)(2,1)S(1)}, u32[]{:S(2)}, u32[]{:S(2)}) collective-permute-start(bf16[528,128]{1,0:T(8,128)(2,1)S(1)} %get-tuple-element.50), channel_id=1, source_target_pairs={{0,6},{2,4},{4,2},{6,0},{8,14},{10,12},{12,10},{14,8},{16,22},{18,... | collective-permute-start | bytes 405512 | tf_op jit(solution)/shard_map/ppermute | solution.py:372
  10.2 6.7 %collective-permute-start.3 = (bf16[256,128]{1,0:T(8,128)(2,1)S(1)}, bf16[256,128]{1,0:T(8,128)(2,1)S(1)}, u32[]{:S(2)}, u32[]{:S(2)}) collective-permute-start(bf16[256,128]{1,0:T(8,128)(2,1)S(1)} %get-tuple-element.46), channel_id=1, source_target_pairs={{0,2},{2,0},{4,6},{6,4},{8,10},{10,8},{12,14},{14,12},{16,18},{18,... | collective-permute-start | bytes 196616 | tf_op jit(solution)/shard_map/ppermute | solution.py:372
  11.6 5.9 %collective-permute-start.4 = (bf16[256,128]{1,0:T(8,128)(2,1)S(1)}, bf16[256,128]{1,0:T(8,128)(2,1)S(1)}, u32[]{:S(2)}, u32[]{:S(2)}) collective-permute-start(bf16[256,128]{1,0:T(8,128)(2,1)S(1)} %get-tuple-element.47), channel_id=1, source_target_pairs={{0,4},{2,6},{4,0},{6,2},{8,12},{10,14},{12,8},{14,10},{16,20},{18,... | collective-permute-start | bytes 196616 | tf_op jit(solution)/shard_map/ppermute | solution.py:372
  12.8 4.6 %collective-permute-start.5 = (bf16[256,128]{1,0:T(8,128)(2,1)S(1)}, bf16[256,128]{1,0:T(8,128)(2,1)S(1)}, u32[]{:S(2)}, u32[]{:S(2)}) collective-permute-start(bf16[256,128]{1,0:T(8,128)(2,1)S(1)} %get-tuple-element.48), channel_id=1, source_target_pairs={{0,6},{2,4},{4,2},{6,0},{8,14},{10,12},{12,10},{14,8},{16,22},{18,... | collective-permute-start | bytes 196616 | tf_op jit(solution)/shard_map/ppermute | solution.py:372
  14.1 6.8 %collective-permute-start.10 = (bf16[256,128]{1,0:T(8,128)(2,1)S(1)}, bf16[256,128]{1,0:T(8,128)(2,1)S(1)}, u32[]{:S(2)}, u32[]{:S(2)}) collective-permute-start(bf16[256,128]{1,0:T(8,128)(2,1)S(1)} %get-tuple-element.56), channel_id=1, source_target_pairs={{0,2},{2,0},{4,6},{6,4},{8,10},{10,8},{12,14},{14,12},{16,18},{18,... | collective-permute-start | bytes 196616 | tf_op jit(solution)/shard_map/ppermute | solution.py:372
  15.7 7.3 %collective-permute-start.11 = (bf16[256,128]{1,0:T(8,128)(2,1)S(1)}, bf16[256,128]{1,0:T(8,128)(2,1)S(1)}, u32[]{:S(2)}, u32[]{:S(2)}) collective-permute-start(bf16[256,128]{1,0:T(8,128)(2,1)S(1)} %get-tuple-element.57), channel_id=1, source_target_pairs={{0,4},{2,6},{4,0},{6,2},{8,12},{10,14},{12,8},{14,10},{16,20},{18,... | collective-permute-start | bytes 196616 | tf_op jit(solution)/shard_map/ppermute | solution.py:372
  16.9 6.1 %collective-permute-start.12 = (bf16[256,128]{1,0:T(8,128)(2,1)S(1)}, bf16[256,128]{1,0:T(8,128)(2,1)S(1)}, u32[]{:S(2)}, u32[]{:S(2)}) collective-permute-start(bf16[256,128]{1,0:T(8,128)(2,1)S(1)} %get-tuple-element.58), channel_id=1, source_target_pairs={{0,6},{2,4},{4,2},{6,0},{8,14},{10,12},{12,10},{14,8},{16,22},{18,... | collective-permute-start | bytes 196616 | tf_op jit(solution)/shard_map/ppermute | solution.py:372
  17.5 8.9 %collective-permute-start.8 = (bf16[3,272,128]{2,1,0:T(8,128)(2,1)S(1)}, bf16[3,272,128]{2,1,0:T(8,128)(2,1)S(1)}, u32[]{:S(2)}, u32[]{:S(2)}) collective-permute-start(bf16[3,272,128]{2,1,0:T(8,128)(2,1)S(1)} %get-tuple-element.54), channel_id=1, source_target_pairs={{8,16},{10,18},{12,20},{14,22},{16,8},{18,10},{20,12},{22,14},{9,1... | collective-permute-start | bytes 626696 | tf_op jit(solution)/shard_map/ppermute | solution.py:377
  20.7 6.4 %collective-permute-start.9 = (bf16[3,272,128]{2,1,0:T(8,128)(2,1)S(1)}, bf16[3,272,128]{2,1,0:T(8,128)(2,1)S(1)}, u32[]{:S(2)}, u32[]{:S(2)}) collective-permute-start(bf16[3,272,128]{2,1,0:T(8,128)(2,1)S(1)} %get-tuple-element.55), channel_id=1, source_target_pairs={{0,8},{2,10},{4,12},{6,14},{8,0},{10,2},{12,4},{14,6},{16,24},{18,... | collective-permute-start | bytes 626696 | tf_op jit(solution)/shard_map/ppermute | solution.py:377
  20.9 13.1 %collective-permute-start.15 = (bf16[3,256,128]{2,1,0:T(8,128)(2,1)S(1)}, bf16[3,256,128]{2,1,0:T(8,128)(2,1)S(1)}, u32[]{:S(2)}, u32[]{:S(2)}) collective-permute-start(bf16[3,256,128]{2,1,0:T(8,128)(2,1)S(1)} %get-tuple-element.65), channel_id=1, source_target_pairs={{8,16},{10,18},{12,20},{14,22},{16,8},{18,10},{20,12},{22,14},{9,1... | collective-permute-start | bytes 589832 | tf_op jit(solution)/shard_map/ppermute | solution.py:377
  23.0 11.0 %collective-permute-start.16 = (bf16[3,256,128]{2,1,0:T(8,128)(2,1)S(1)}, bf16[3,256,128]{2,1,0:T(8,128)(2,1)S(1)}, u32[]{:S(2)}, u32[]{:S(2)}) collective-permute-start(bf16[3,256,128]{2,1,0:T(8,128)(2,1)S(1)} %get-tuple-element.66), channel_id=1, source_target_pairs={{0,8},{2,10},{4,12},{6,14},{8,0},{10,2},{12,4},{14,6},{16,24},{18,... | collective-permute-start | bytes 589832 | tf_op jit(solution)/shard_map/ppermute | solution.py:377
  29.7 9.9 %collective-permute-start.13 = (bf16[3,288,128]{2,1,0:T(8,128)(2,1)S(1)}, bf16[3,288,128]{2,1,0:T(8,128)(2,1)S(1)}, u32[]{:S(2)}, u32[]{:S(2)}) collective-permute-start(bf16[3,288,128]{2,1,0:T(8,128)(2,1)S(1)} %get-tuple-element.61), channel_id=1, source_target_pairs={{0,8},{2,10},{4,12},{6,14},{8,0},{10,2},{12,4},{14,6},{16,24},{18,... | collective-permute-start | bytes 663560 | tf_op jit(solution)/shard_map/ppermute | solution.py:377
  30.6 9.0 %collective-permute-start.14 = (bf16[3,288,128]{2,1,0:T(8,128)(2,1)S(1)}, bf16[3,288,128]{2,1,0:T(8,128)(2,1)S(1)}, u32[]{:S(2)}, u32[]{:S(2)}) collective-permute-start(bf16[3,288,128]{2,1,0:T(8,128)(2,1)S(1)} %get-tuple-element.62), channel_id=1, source_target_pairs={{8,16},{10,18},{12,20},{14,22},{16,8},{18,10},{20,12},{22,14},{9,1... | collective-permute-start | bytes 663560 | tf_op jit(solution)/shard_map/ppermute | solution.py:377
  36.6 10.3 %collective-permute-start.22 = (bf16[256,128]{1,0:T(8,128)(2,1)S(1)}, bf16[256,128]{1,0:T(8,128)(2,1)S(1)}, u32[]{:S(2)}, u32[]{:S(2)}) collective-permute-start(bf16[256,128]{1,0:T(8,128)(2,1)S(1)} %get-tuple-element.79), channel_id=1, source_target_pairs={{0,6},{2,4},{4,2},{6,0},{8,14},{10,12},{12,10},{14,8},{16,22},{18,... | collective-permute-start | bytes 196616 | tf_op jit(solution)/shard_map/ppermute | solution.py:372
  39.3 7.6 %collective-permute-start.21 = (bf16[256,128]{1,0:T(8,128)(2,1)S(1)}, bf16[256,128]{1,0:T(8,128)(2,1)S(1)}, u32[]{:S(2)}, u32[]{:S(2)}) collective-permute-start(bf16[256,128]{1,0:T(8,128)(2,1)S(1)} %get-tuple-element.68.refs_0_), channel_id=1, source_target_pairs={{0,4},{2,6},{4,0},{6,2},{8,12},{10,14},{12,8},{14,10},{16,20},{18,... | collective-permute-start | bytes 196616 | tf_op jit(solution)/shard_map/ppermute | solution.py:372
  40.1 4.7 %collective-permute-start.17 = (bf16[256,128]{1,0:T(8,128)(2,1)S(1)}, bf16[256,128]{1,0:T(8,128)(2,1)S(1)}, u32[]{:S(2)}, u32[]{:S(2)}) collective-permute-start(bf16[256,128]{1,0:T(8,128)(2,1)S(1)} %get-tuple-element.70), channel_id=1, source_target_pairs={{0,2},{2,0},{4,6},{6,4},{8,10},{10,8},{12,14},{14,12},{16,18},{18,... | collective-permute-start | bytes 196616 | tf_op jit(solution)/shard_map/ppermute | solution.py:372
  40.9 4.2 %collective-permute-start.18 = (bf16[256,128]{1,0:T(8,128)(2,1)S(1)}, bf16[256,128]{1,0:T(8,128)(2,1)S(1)}, u32[]{:S(2)}, u32[]{:S(2)}) collective-permute-start(bf16[256,128]{1,0:T(8,128)(2,1)S(1)} %get-tuple-element.71), channel_id=1, source_target_pairs={{0,4},{2,6},{4,0},{6,2},{8,12},{10,14},{12,8},{14,10},{16,20},{18,... | collective-permute-start | bytes 196616 | tf_op jit(solution)/shard_map/ppermute | solution.py:372
  42.1 4.1 %collective-permute-start.19 = (bf16[256,128]{1,0:T(8,128)(2,1)S(1)}, bf16[256,128]{1,0:T(8,128)(2,1)S(1)}, u32[]{:S(2)}, u32[]{:S(2)}) collective-permute-start(bf16[256,128]{1,0:T(8,128)(2,1)S(1)} %get-tuple-element.72), channel_id=1, source_target_pairs={{0,6},{2,4},{4,2},{6,0},{8,14},{10,12},{12,10},{14,8},{16,22},{18,... | collective-permute-start | bytes 196616 | tf_op jit(solution)/shard_map/ppermute | solution.py:372
  44.8 2.1 %collective-permute-start.20 = (bf16[256,128]{1,0:T(8,128)(2,1)S(1)}, bf16[256,128]{1,0:T(8,128)(2,1)S(1)}, u32[]{:S(2)}, u32[]{:S(2)}) collective-permute-start(bf16[256,128]{1,0:T(8,128)(2,1)S(1)} %get-tuple-element.78), channel_id=1, source_target_pairs={{0,2},{2,0},{4,6},{6,4},{8,10},{10,8},{12,14},{14,12},{16,18},{18,... | collective-permute-start | bytes 196616 | tf_op jit(solution)/shard_map/ppermute | solution.py:372

commit v20 on v19

--- a/solution.py
+++ b/solution.py
@@ -102,21 +102,19 @@
         pieces[k][...] = full[:, pl.ds(pl.multiple_of((mine ^ k) * width, width), width)]
 
 
-def halo_kernel(ids_at, *refs):
-    pieces, id_packs, outs = refs[:GROUP], refs[GROUP : 2 * GROUP], refs[-2:]
-    rows = outs[0].shape[1] - (ID_ROWS if ids_at else 0)
-    mine = place()
-    odd = lax.rem(plane(), 2)
-    for k in range(GROUP):
-        block = mine ^ k
-        for out, skip in zip(outs, ((GROUP - RADIUS) * (1 - odd), (GROUP - RADIUS) * odd)):
-            spot = block - skip
-
-            @pl.when((spot >= 0) & (spot < RADIUS))
-            def _():
-                out[spot, :rows] = pieces[k][:rows]
-                if ids_at:
-                    out[spot, rows:] = id_packs[k][ids_at:]
+def halo_kernel(second, ids_at, *refs):
+    pieces, id_packs, out = refs[:GROUP], refs[GROUP : 2 * GROUP], refs[-1]
+    rows = out.shape[1] - (ID_ROWS if ids_at else 0)
+    mine = place()
+    skip = (GROUP - RADIUS) * lax.rem(plane() + 1 + second, 2)
+    for k in range(GROUP):
+        spot = (mine ^ k) - skip
+
+        @pl.when((spot >= 0) & (spot < RADIUS))
+        def _():
+            out[spot, :rows] = pieces[k][:rows]
+            if ids_at:
+                out[spot, rows:] = id_packs[k][ids_at:]
 
 
 def join_kernel(*refs):
@@ -218,34 +216,45 @@
         sums[b, 1] = by_head(mixed[:, width:], rows)
 
 
-def lend_kernel(edge_b, edge_a, plane_turned, plane_beside, first, second, turned, ordered, results):
-    rows, width = ordered.shape[2] - ID_ROWS, ordered.shape[3]
-    odd = lax.rem(plane(), 2)
-    ordered[1 - odd] = edge_a[...]
-    ordered[odd] = edge_b[...]
+def lend_kernel(second, edge, plane_turned, plane_beside, *refs):
+    result = refs[-1]
+    if second:
+        last = lax.axis_size("tm") // GROUP - 1
+
+        @pl.when((plane() > 0) & (plane() < last))
+        def _():
+            lend(second, edge, plane_turned, plane_beside, result)
+
+    else:
+        refs[1][...] = refs[0][...]
+        lend(second, edge, plane_turned, plane_beside, result)
+
+
+def lend(second, edge, plane_turned, plane_beside, result):
+    rows, width = edge.shape[1] - ID_ROWS, edge.shape[2]
+    above = lax.rem(plane() + 1 + second, 2)
     lane = lax.broadcasted_iota(jnp.int32, (rows, width), 1)
-    blocks = [slice(0, (j + 1) * rows) for j in range(RADIUS)]
-    blocks += [slice((j + 1) * rows, GROUP * rows) for j in range(RADIUS)]
-
-    def scores_of(e):
-        side, j = e // RADIUS, e % RADIUS
-        marks = marks_turned(ordered[side, j, rows:])
-        query = ordered[side, j, :rows]
-        for part, x in enumerate(marks):
-            at = slice(e * rows + part * width, e * rows + (part + 1) * width)
-            turned[:width, at] = jnp.transpose(query[part * width : (part + 1) * width])
-            turned[width:, at] = x
-        return product(stacked_ask(query, marks), plane_turned[:, blocks[e]])
+
+    def block_of(n):
+        return n + above * (RADIUS - 1 - 2 * n)
+
+    def near(n):
+        return pl.ds(pl.multiple_of(above * (GROUP - 1 - n) * rows, rows), (n + 1) * rows)
+
+    def scores_of(n):
+        j = block_of(n)
+        ask = stacked_ask(edge[j, :rows], marks_turned(edge[j, rows:]))
+        return product(ask, plane_turned[:, near(n)])
 
     ahead = scores_of(0)
-    for e in range(2 * RADIUS):
-        side, j = e // RADIUS, e % RADIUS
+    for n in range(RADIUS):
+        j = block_of(n)
         scores = ahead
-        if e + 1 < 2 * RADIUS:
-            ahead = scores_of(e + 1)
-        peak, mixed = attend([scores], [plane_beside[blocks[e]]])
+        if n + 1 < RADIUS:
+            ahead = scores_of(n + 1)
+        peak, mixed = attend([scores], [plane_beside[near(n)]])
         total = by_head(mixed[:, width:], rows)
-        results[side, j, :rows] = (by_head(mixed[:, :width], rows) / total).astype(results.dtype)
+        result[j, :rows] = (by_head(mixed[:, :width], rows) / total).astype(result.dtype)
         logs = by_head(jnp.broadcast_to(peak, (peak.shape[0], width)), rows) + jnp.log(total)
         high = logs.astype(jnp.bfloat16).astype(jnp.float32)
         middle = (logs - high).astype(jnp.bfloat16).astype(jnp.float32)
@@ -255,11 +264,9 @@
             flipped = jnp.transpose(picked[part * width : (part + 1) * width])
             stats = [flipped[h : h + STAT_ROWS // 2] for h in range(0, width, HEAD)]
             at = rows + part * STAT_ROWS
-            results[side, j, at : at + STAT_ROWS] = jnp.concatenate(stats, axis=0).astype(
-                results.dtype
+            result[j, at : at + STAT_ROWS] = jnp.concatenate(stats, axis=0).astype(
+                result.dtype
             )
-    first[...] = results[1 - odd]
-    second[...] = results[odd]
 
 
 def columns_kernel(receivers, *refs):
@@ -267,12 +274,12 @@
     take = lambda count: [refs.pop(0) for _ in range(count)]
     first = 0 not in receivers
     if first:
-        packs, queries, keys, (edge_b, edge_a) = take(GROUP), take(GROUP), take(GROUP), take(2)
-    (edge_turned,) = take(1)
-    if not first:
-        shared, _ = take(4), take(1)
+        packs, queries, keys = take(GROUP), take(GROUP), take(GROUP)
+        (ask_b, ask_a), (edge_b, edge_a) = take(2), take(2)
+    else:
+        shared, _ = take(5), take(1)
     outs = take(len(receivers))
-    turned, beside, asks, edge_beside = take(4) if first else shared
+    turned, beside, asks, edge_beside, edge_turned = take(5) if first else shared
     rows, width = outs[0].shape
     mine = place()
     if first:
@@ -287,10 +294,19 @@
             asks,
         )
         edge_beside[:, width:] = jnp.ones((edge_beside.shape[0], width), beside.dtype)
-        for edge, base in ((edge_a, RADIUS * (1 - odd)), (edge_b, RADIUS * odd)):
+        for ask, edge, base in ((ask_a, edge_a, RADIUS * (1 - odd)), (ask_b, edge_b, RADIUS * odd)):
             for j in range(RADIUS):
-                at = pl.ds(pl.multiple_of((base + j) * rows, rows), rows)
-                edge_beside[at, :width] = edge[j]
+
+                def spot(at, size):
+                    return pl.ds(pl.multiple_of((base + j) * rows + at, size), size)
+
+                edge_beside[spot(0, rows), :width] = edge[j]
+                for part, x in enumerate(marks_turned(ask[j, rows:])):
+                    at = spot(part * width, width)
+                    edge_turned[:width, at] = jnp.transpose(
+                        ask[j, part * width : (part + 1) * width]
+                    )
+                    edge_turned[width:, at] = x
     near = [pl.ds(pl.multiple_of((mine ^ k) * rows, rows), RADIUS * rows) for k in receivers]
 
     def scores_of(n):
@@ -420,20 +436,19 @@
             name="project",
         )(*operands, *after)
 
-    def halo(pieces, id_packs, *after):
-        edge = shape((RADIUS, rows + (ID_ROWS if id_packs else 0), width), bf16)
+    def halo(second, pieces, id_packs, *after):
         sent = call(
-            functools.partial(halo_kernel, 2 * rows if id_packs else 0),
-            [edge, edge],
+            functools.partial(halo_kernel, second, 2 * rows if id_packs else 0),
+            shape((RADIUS, rows + (ID_ROWS if id_packs else 0), width), bf16),
             ins=[VMEM] * (GROUP + len(id_packs)) + [ANY] * len(after),
-            moved=10 * rows * width * 2,
+            moved=5 * rows * width * 2,
             name="halo",
         )(*pieces, *id_packs, *after)
-        return [crossed(sent[i], i) for i in range(2)]
+        return crossed(sent, second)
 
     queries = traded(project(HEAD**-0.5, query_part, other_audio, query_rest, after=packs[1:3]))
     keys = project(1.0, key_part, other_video, key_rest, after=())
-    query_edges = halo(queries, packs, keys[0])
+    query_edges = [halo(i, queries, packs, keys[0]) for i in range(2)]
     keys = traded(keys)
 
     inside, around = GROUP * rows, 2 * RADIUS * rows
@@ -448,17 +463,20 @@
         exps=2 * GROUP * rows * inside,
         name="rows",
     )(*packs, *queries, *keys)
-    audio_edges = halo(packs, [])
+    audio_edges = [halo(0, packs, [], query_edges[1]), halo(1, packs, [])]
     back = shape((RADIUS, rows + rows // width * STAT_ROWS, width), bf16)
-    lent_a, lent_b, edge_turned = call(
-        lend_kernel,
-        [back, back, shape((2 * width, around), bf16)],
-        [pltpu.VMEM((2, RADIUS, rows + ID_ROWS, width), bf16), pltpu.VMEM((2,) + back.shape, bf16)],
-        flops=48 * RADIUS * GROUP * rows * rows * width,
-        moved=8 * around * width * 2,
-        exps=2 * RADIUS * GROUP * rows * rows,
+    lending = dict(
+        flops=24 * RADIUS * GROUP * rows * rows * width,
+        moved=4 * around * width * 2,
+        exps=RADIUS * GROUP * rows * rows,
         name="lend",
-    )(*query_edges[::-1], plane_turned, plane_beside)
+    )
+    lent_b = call(functools.partial(lend_kernel, 1), back, **lending)(
+        query_edges[1], plane_turned, plane_beside
+    )
+    lent_b, lent_a = call(functools.partial(lend_kernel, 0), [back, back], **lending)(
+        query_edges[0], plane_turned, plane_beside, lent_b
+    )
     backs = [crossed(x, i) for i, x in enumerate((lent_a, lent_b))]
 
     half_columns = dict(
@@ -467,11 +485,11 @@
         exps=7 * GROUP * rows * rows,
         name="columns",
     )
-    shared = [turned, beside, asks, shape((around, 2 * width), bf16)]
+    shared = [turned, beside, asks, shape((around, 2 * width), bf16), shape((2 * width, around), bf16)]
     near, far = range(GROUP // 2), range(GROUP // 2, GROUP)
-    *far_pieces, turned, beside, asks, edge_beside = call(
+    *far_pieces, turned, beside, asks, edge_beside, edge_turned = call(
         functools.partial(columns_kernel, far), [piece] * len(far) + shared, **half_columns
-    )(*packs, *queries, *keys, *audio_edges[::-1], edge_turned)
+    )(*packs, *queries, *keys, *query_edges[::-1], *audio_edges[::-1])
     audio_pieces = call(
         merge_kernel,
         [piece] * GROUP,
@@ -487,7 +505,7 @@
         [piece] * len(near),
         ins=[VMEM] * 5 + [ANY],
         **half_columns,
-    )(edge_turned, turned, beside, asks, edge_beside, audio_pieces[0])
+    )(turned, beside, asks, edge_beside, edge_turned, audio_pieces[0])
     video_pieces = traded([*near_pieces, *far_pieces])
 
     def join(pieces):

time: 48.1 us -> 49.9 us (1.037)
  starting transfers between devices: 26.3 us -> 27.4 us
    ppermute x6, waiting for transfers between devices: 0.69 us -> 0.02 us  [crossed(): lax.ppermute(sent, 'tm', [(p * GROUP + i, q * GROUP + i) for p, q in pair...]
    ppermute x6, starting transfers between devices: 9.66 us -> 10.3 us  [crossed(): lax.ppermute(sent, 'tm', [(p * GROUP + i, q * GROUP + i) for p, q in pair...]
    ppermute x15, starting transfers between devices: 15.1 us -> 15.6 us  [traded(): lax.ppermute(pieces[k], 'tm', pairs(k))]
    ppermute x15, waiting for transfers between devices: 2.76 us -> 3.26 us  [traded(): lax.ppermute(pieces[k], 'tm', pairs(k))]
    pallas_call x3 -> x6, Pallas kernels: 2.77 us -> 3.13 us  [the longest x1 1.48 us: local(): call(functools.partial(lend_kernel, 0), [back, back], **lending)]
where the time goes in v20:
time: 49.9 us; the launch traced here: 49.2 us
  starting transfers between devices  27.4 us (55%)
  Pallas kernels  17 us (34%)
  waiting for transfers between devices  3.71 us (7%)
  between operations  1.06 us (2%)
    ppermute x15, starting transfers between devices, traded(): lax.ppermute(pieces[k], 'tm', pairs(k))  15.6 us
    ppermute x6, starting transfers between devices, crossed(): lax.ppermute(sent, 'tm', [(p * GROUP + i, q * GROUP + i) for p, q in pair...  10.3 us
    ppermute x15, waiting for transfers between devices, traded(): lax.ppermute(pieces[k], 'tm', pairs(k))  3.26 us
    pallas_call x1, Pallas kernels, local(): call(rows_kernel, [shape((GROUP, rows, width), f32), shape((GROUP, 2, row...  3.26 us
    pallas_call x1, Pallas kernels, local(): call(functools.partial(columns_kernel, far), [piece] * len(far) + shared,...  2.72 us
    pallas_call x1, Pallas kernels, local(): call(functools.partial(columns_kernel, near), [piece] * len(near), ins=[V...  2.19 us
    pallas_call x1, Pallas kernels, local(): call(prepare_kernel, [part, part, square, square], [pltpu.VMEM((rows, hal...  1.78 us
    ppermute x2, starting transfers between devices, swapped(): return lax.ppermute(x, 'head', [(0, 1), (1, 0)])  1.53 us
  transfers between devices with their start and end apart: 23, of which 4 were waited for; matrix products, arithmetic and copies ran while one was open for 0% of the time, Pallas kernels for 33%

profile of v20, /device:TPU:9, one launch (start us, length us, event | category | flops | bytes accessed | tf_op | source)
XLA Modules:
  0.0 49.2 jit_solution(17793592128121010506)
XLA Ops:
  0.6 1.3 %collective-permute-start.1 = (bf16[256,512]{1,0:T(8,128)(2,1)}, bf16[256,512]{1,0:T(8,128)(2,1)S(1)}, u32[]{:S(2)}, u32[]{:S(2)}) collective-permute-start(bf16[256,512]{1,0:T(8,128)(2,1)} %audio.3), channel_id=1, source_target_pairs={{0,1},{1,0},{2,3},{3,2},{4,5},{5,4},{6,7},{7,6},{8,9},{9,8},{10,11... | collective-permute-start | bytes 786440 | tf_op jit(solution)/shard_map/ppermute | solution.py:384
  1.9 0.2 collective-permute-start.7
  2.2 1.2 %split.1 = (bf16[528,128]{1,0:T(8,128)(2,1)S(1)}, bf16[528,128]{1,0:T(8,128)(2,1)S(1)}, bf16[528,128]{1,0:T(8,128)(2,1)S(1)}, bf16[528,128]{1,0:T(8,128)(2,1)S(1)}) custom-call(bf16[256,512]{1,0:T(8,128)(2,1)} %audio.3, bf16[256,512]{1,0:T(8,128)(2,1)} %video.3, s32[2,128]{1,0:T(2,128)} %bitcast.1), custom_call_target="tpu_custom_call" | custom-call | bytes 1048576 | tf_op jit(solution)/shard_map/split/pallas_call | solution.py:406
  3.3 1.3 %collective-permute-start = (bf16[528,128]{1,0:T(8,128)(2,1)S(1)}, bf16[528,128]{1,0:T(8,128)(2,1)S(1)}, u32[]{:S(2)}, u32[]{:S(2)}) collective-permute-start(bf16[528,128]{1,0:T(8,128)(2,1)S(1)} %get-tuple-element.37), channel_id=1, source_target_pairs={{0,2},{2,0},{4,6},{6,4},{8,10},{10,8},{12,14},{14,12},{16,18},{18,... | collective-permute-start | bytes 405512 | tf_op jit(solution)/shard_map/ppermute | solution.py:388
  4.6 1.2 %collective-permute-start.2 = (bf16[528,128]{1,0:T(8,128)(2,1)S(1)}, bf16[528,128]{1,0:T(8,128)(2,1)S(1)}, u32[]{:S(2)}, u32[]{:S(2)}) collective-permute-start(bf16[528,128]{1,0:T(8,128)(2,1)S(1)} %get-tuple-element.40), channel_id=1, source_target_pairs={{0,4},{2,6},{4,0},{6,2},{8,12},{10,14},{12,8},{14,10},{16,20},{18,... | collective-permute-start | bytes 405512 | tf_op jit(solution)/shard_map/ppermute | solution.py:388
  5.9 0.5 collective-permute-start.6
  6.3 0.0 collective-permute-done.refs_0_.refs_5_.refs_1_
  6.3 1.8 %prepare.1 = (f32[256,512]{1,0:T(8,128)S(1)}, f32[256,512]{1,0:T(8,128)S(1)}, bf16[512,512]{1,0:T(8,128)(2,1)S(1)}, bf16[512,512]{1,0:T(8,128)(2,1)S(1)}) custom-call(bf16[256,512]{1,0:T(8,128)(2,1)} %audio.3, bf16[256,512]{1,0:T(8,128)(2,1)} %video.3, bf16[1024,512]{1,0:T(8,128)(2,1)} %query.1, bf16[1024,512]{1,0:T(8,128)(2,1)} %key.1, ...), custom_call_target="tpu_custom_call" | custom-call | flops 268435456 | bytes 4194304 | tf_op jit(solution)/shard_map/prepare/pallas_call | solution.py:416
  8.1 1.7 %collective-permute-done.2.refs_1_.refs_6_.refs_2_ = bf16[528,128]{1,0:T(8,128)(2,1)S(1)} collective-permute-done((bf16[528,128]{1,0:T(8,128)(2,1)S(1)}, bf16[528,128]{1,0:T(8,128)(2,1)S(1)}, u32[]{:S(2)}, u32[]{:S(2)}) %collective-permute-start.2) | collective-permute-done | bytes 135200 | tf_op jit(solution)/shard_map/ppermute | solution.py:388
  9.8 0.0 collective-permute-done.1.other
  9.8 0.4 project.2
  10.2 1.4 %collective-permute-start.3 = (bf16[256,128]{1,0:T(8,128)(2,1)S(1)}, bf16[256,128]{1,0:T(8,128)(2,1)S(1)}, u32[]{:S(2)}, u32[]{:S(2)}) collective-permute-start(bf16[256,128]{1,0:T(8,128)(2,1)S(1)} %get-tuple-element.42), channel_id=1, source_target_pairs={{0,2},{2,0},{4,6},{6,4},{8,10},{10,8},{12,14},{14,12},{16,18},{18,... | collective-permute-start | bytes 196616 | tf_op jit(solution)/shard_map/ppermute | solution.py:388
  11.6 1.2 %collective-permute-start.4 = (bf16[256,128]{1,0:T(8,128)(2,1)S(1)}, bf16[256,128]{1,0:T(8,128)(2,1)S(1)}, u32[]{:S(2)}, u32[]{:S(2)}) collective-permute-start(bf16[256,128]{1,0:T(8,128)(2,1)S(1)} %get-tuple-element.43), channel_id=1, source_target_pairs={{0,4},{2,6},{4,0},{6,2},{8,12},{10,14},{12,8},{14,10},{16,20},{18,... | collective-permute-start | bytes 196616 | tf_op jit(solution)/shard_map/ppermute | solution.py:388
  12.8 0.5 collective-permute-start.5
  13.3 0.4 collective-permute-done.7.other
  13.7 0.4 project.3
  14.1 1.6 %collective-permute-start.9 = (bf16[256,128]{1,0:T(8,128)(2,1)S(1)}, bf16[256,128]{1,0:T(8,128)(2,1)S(1)}, u32[]{:S(2)}, u32[]{:S(2)}) collective-permute-start(bf16[256,128]{1,0:T(8,128)(2,1)S(1)} %get-tuple-element.50), channel_id=1, source_target_pairs={{0,2},{2,0},{4,6},{6,4},{8,10},{10,8},{12,14},{14,12},{16,18},{18,... | collective-permute-start | bytes 196616 | tf_op jit(solution)/shard_map/ppermute | solution.py:388
  15.7 0.0 collective-permute-done.6.refs_7_.refs_3_
  15.7 1.2 %collective-permute-start.10 = (bf16[256,128]{1,0:T(8,128)(2,1)S(1)}, bf16[256,128]{1,0:T(8,128)(2,1)S(1)}, u32[]{:S(2)}, u32[]{:S(2)}) collective-permute-start(bf16[256,128]{1,0:T(8,128)(2,1)S(1)} %get-tuple-element.51), channel_id=1, source_target_pairs={{0,4},{2,6},{4,0},{6,2},{8,12},{10,14},{12,8},{14,10},{16,20},{18,... | collective-permute-start | bytes 196616 | tf_op jit(solution)/shard_map/ppermute | solution.py:388
  16.9 0.0 collective-permute-done.3.refs_1_.refs_5_
  16.9 0.5 collective-permute-start.11
  17.4 0.0 collective-permute-done.4.refs_2_.refs_6_
  17.4 0.0 collective-permute-done.5.refs_3_.refs_7_
  17.5 3.2 %collective-permute-start.12 = (bf16[3,272,128]{2,1,0:T(8,128)(2,1)S(1)}, bf16[3,272,128]{2,1,0:T(8,128)(2,1)S(1)}, u32[]{:S(2)}, u32[]{:S(2)}) collective-permute-start(bf16[3,272,128]{2,1,0:T(8,128)(2,1)S(1)} %halo.5), channel_id=1, source_target_pairs={{8,16},{10,18},{12,20},{14,22},{16,8},{18,10},{20,12},{22,14},{9,1... | collective-permute-start | bytes 626696 | tf_op jit(solution)/shard_map/ppermute | solution.py:393
  20.7 0.1 halo.6
  20.7 2.1 %collective-permute-start.15 = (bf16[3,256,128]{2,1,0:T(8,128)(2,1)S(1)}, bf16[3,256,128]{2,1,0:T(8,128)(2,1)S(1)}, u32[]{:S(2)}, u32[]{:S(2)}) collective-permute-start(bf16[3,256,128]{2,1,0:T(8,128)(2,1)S(1)} %halo.6), channel_id=1, source_target_pairs={{8,16},{10,18},{12,20},{14,22},{16,8},{18,10},{20,12},{22,14},{9,1... | collective-permute-start | bytes 589832 | tf_op jit(solution)/shard_map/ppermute | solution.py:393
  22.8 0.1 halo.4
  22.9 0.0 collective-permute-done.9.refs_9_
  22.9 0.1 collective-permute-start.8
  23.0 0.0 collective-permute-done.10.refs_10_
  23.0 0.0 collective-permute-done.11.refs_11_
  23.0 3.3 %rows.1 = (f32[4,256,128]{2,1,0:T(8,128)S(1)}, f32[4,2,256,128]{3,2,1,0:T(8,128)S(1)}, bf16[256,1024]{1,0:T(8,128)(2,1)S(1)}, bf16[1024,256]{1,0:T(8,128)(2,1)S(1)}) custom-call(bf16[528,128]{1,0:T(8,128)(2,1)S(1)} %get-tuple-element.45.refs_4_.refs_0_, bf16[528,128]{1,0:T(8,128)(2,1)S(1)} %collective-permute-done.refs_0_.refs_5_.refs_1_, ...), custom_call_target="tpu_custom_call" | custom-call | flops 2147483648 | bytes 2097152 | tf_op jit(solution)/shard_map/rows/pallas_call | solution.py:457
  26.3 0.0 collective-permute-done.12.edge.refs_4_.refs_12_
  26.3 0.1 halo.7
  26.3 1.5 %collective-permute-start.16 = (bf16[3,256,128]{2,1,0:T(8,128)(2,1)S(1)}, bf16[3,256,128]{2,1,0:T(8,128)(2,1)S(1)}, u32[]{:S(2)}, u32[]{:S(2)}) collective-permute-start(bf16[3,256,128]{2,1,0:T(8,128)(2,1)S(1)} %halo.7), channel_id=1, source_target_pairs={{0,8},{2,10},{4,12},{6,14},{8,0},{10,2},{12,4},{14,6},{16,24},{18,... | collective-permute-start | bytes 589832 | tf_op jit(solution)/shard_map/ppermute | solution.py:393
  27.8 1.5 %lend.2.refs_0_ = bf16[3,288,128]{2,1,0:T(8,128)(2,1)S(1)} custom-call(bf16[3,272,128]{2,1,0:T(8,128)(2,1)S(1)} %collective-permute-done.12.edge.refs_4_.refs_12_, bf16[256,1024]{1,0:T(8,128)(2,1)S(1)} %get-tuple-element.53.plane_turned, bf16[1024,256]{1,0:T(8,128)(2,1)S(1)} %get-tuple-element.54.plane_beside), custom_call_target="tpu_custom_call" | custom-call | flops 2415919104 | bytes 1572864 | tf_op jit(solution)/shard_map/lend/pallas_call | solution.py:474
  29.3 0.0 collective-permute-done.8.edge.refs_13_
  29.3 1.5 %lend.3 = (bf16[3,288,128]{2,1,0:T(8,128)(2,1)S(1)}, bf16[3,288,128]{2,1,0:T(8,128)(2,1)S(1)}) custom-call(bf16[3,272,128]{2,1,0:T(8,128)(2,1)S(1)} %collective-permute-done.8.edge.refs_13_, bf16[256,1024]{1,0:T(8,128)(2,1)S(1)} %get-tuple-element.53.plane_turned, bf16[1024,256]{1,0:T(8,128)(2,1)S(1)} %get-tuple-element.54.plane_beside, ...), custom_call_target="tpu_custom_call" | custom-call | flops 2415919104 | bytes 1572864 | tf_op jit(solution)/shard_map/lend/pallas_call | solution.py:477
  30.8 0.1 collective-permute-start.13
  30.9 3.4 %collective-permute-start.14 = (bf16[3,288,128]{2,1,0:T(8,128)(2,1)S(1)}, bf16[3,288,128]{2,1,0:T(8,128)(2,1)S(1)}, u32[]{:S(2)}, u32[]{:S(2)}) collective-permute-start(bf16[3,288,128]{2,1,0:T(8,128)(2,1)S(1)} %get-tuple-element.56), channel_id=1, source_target_pairs={{8,16},{10,18},{12,20},{14,22},{16,8},{18,10},{20,12},{22,14},{9,1... | collective-permute-start | bytes 663560 | tf_op jit(solution)/shard_map/ppermute | solution.py:393
  34.3 0.0 collective-permute-done.15.refs_14_
  34.3 0.0 collective-permute-done.16.refs_15_
  34.3 2.7 %columns.2 = (bf16[256,128]{1,0:T(8,128)(2,1)S(1)}, bf16[256,128]{1,0:T(8,128)(2,1)S(1)}, bf16[256,1024]{1,0:T(8,128)(2,1)S(1)}, bf16[1024,256]{1,0:T(8,128)(2,1...) custom-call(bf16[528,128]{1,0:T(8,128)(2,1)S(1)} %get-tuple-element.45.refs_4_, ...), custom_call_target="tpu_custom_call" | custom-call | flops 1879048192 | bytes 1572864 | tf_op jit(solution)/shard_map/columns/pallas_call | solution.py:490
  37.0 3.6 %collective-permute-start.22 = (bf16[256,128]{1,0:T(8,128)(2,1)S(1)}, bf16[256,128]{1,0:T(8,128)(2,1)S(1)}, u32[]{:S(2)}, u32[]{:S(2)}) collective-permute-start(bf16[256,128]{1,0:T(8,128)(2,1)S(1)} %get-tuple-element.71), channel_id=1, source_target_pairs={{0,6},{2,4},{4,2},{6,0},{8,14},{10,12},{12,10},{14,8},{16,22},{18,... | collective-permute-start | bytes 196616 | tf_op jit(solution)/shard_map/ppermute | solution.py:388
  40.7 0.3 collective-permute-start.21
  40.9 0.0 collective-permute-done.13.back_a
  40.9 0.0 collective-permute-done.14.back_b
  40.9 0.5 %merge.1 = (bf16[256,128]{1,0:T(8,128)(2,1)S(1)}, bf16[256,128]{1,0:T(8,128)(2,1)S(1)}, bf16[256,128]{1,0:T(8,128)(2,1)S(1)}, bf16[256,128]{1,0:T(8,128)(2,1)S(1)}) custom-call(bf16[3,288,128]{2,1,0:T(8,128)(2,1)S(1)} %collective-permute-done.13.back_a, bf16[3,288,128]{2,1,0:T(8,128)(2,1)S(1)} %collective-permute-done.14.back_b, ...), custom_call_target="tpu_custom_call" | custom-call | bytes 2097152 | tf_op jit(solution)/shard_map/merge/pallas_call | solution.py:493
  41.4 0.3 collective-permute-start.17
  41.7 1.1 %collective-permute-start.18 = (bf16[256,128]{1,0:T(8,128)(2,1)S(1)}, bf16[256,128]{1,0:T(8,128)(2,1)S(1)}, u32[]{:S(2)}, u32[]{:S(2)}) collective-permute-start(bf16[256,128]{1,0:T(8,128)(2,1)S(1)} %get-tuple-element.62), channel_id=1, source_target_pairs={{0,4},{2,6},{4,0},{6,2},{8,12},{10,14},{12,8},{14,10},{16,20},{18,... | collective-permute-start | bytes 196616 | tf_op jit(solution)/shard_map/ppermute | solution.py:388
  42.8 0.8 %collective-permute-start.19 = (bf16[256,128]{1,0:T(8,128)(2,1)S(1)}, bf16[256,128]{1,0:T(8,128)(2,1)S(1)}, u32[]{:S(2)}, u32[]{:S(2)}) collective-permute-start(bf16[256,128]{1,0:T(8,128)(2,1)S(1)} %get-tuple-element.63), channel_id=1, source_target_pairs={{0,6},{2,4},{4,2},{6,0},{8,14},{10,12},{12,10},{14,8},{16,22},{18,... | collective-permute-start | bytes 196616 | tf_op jit(solution)/shard_map/ppermute | solution.py:388
  43.6 2.2 %columns.3 = (bf16[256,128]{1,0:T(8,128)(2,1)S(1)}, bf16[256,128]{1,0:T(8,128)(2,1)S(1)}) custom-call(bf16[256,1024]{1,0:T(8,128)(2,1)S(1)} %get-tuple-element.64.refs_0_, bf16[1024,256]{1,0:T(8,128)(2,1)S(1)} %get-tuple-element.65.refs_1_, bf16[4,512,256]{2,1,0:T(8,128)(2,1)S(1)} %get-tuple-element.66.refs_2_, ...), custom_call_target="tpu_custom_call" | custom-call | flops 1879048192 | bytes 1572864 | tf_op jit(solution)/shard_map/columns/pallas_call | solution.py:503
  45.8 0.0 collective-permute-done.17.refs_1_
  45.9 0.1 collective-permute-start.20
  45.9 0.2 collective-permute-done.18.refs_2_
  46.1 1.4 %collective-permute-done.19.refs_3_ = bf16[256,128]{1,0:T(8,128)(2,1)S(1)} collective-permute-done((bf16[256,128]{1,0:T(8,128)(2,1)S(1)}, bf16[256,128]{1,0:T(8,128)(2,1)S(1)}, u32[]{:S(2)}, u32[]{:S(2)}) %collective-permute-start.19) | collective-permute-done | bytes 65568 | tf_op jit(solution)/shard_map/ppermute | solution.py:388
  47.5 0.7 %join.2 = bf16[256,512]{1,0:T(8,128)(2,1)} custom-call(bf16[256,128]{1,0:T(8,128)(2,1)S(1)} %get-tuple-element.60.refs_0_.refs_5_, bf16[256,128]{1,0:T(8,128)(2,1)S(1)} %collective-permute-done.17.refs_1_, bf16[256,128]{1,0:T(8,128)(2,1)S(1)} %collective-permute-done.18.refs_2_, bf16[256,128]{1,0:T(8,128)(2,1)S(1)} %collective-permute-done.19.refs_3_), custom_call_target="tpu_custom_call" | custom-call | bytes 524288 | tf_op jit(solution)/shard_map/join/pallas_call | solution.py:512
  48.2 0.0 collective-permute-done.22.refs_3_
  48.2 0.0 collective-permute-done.21.refs_2_
  48.3 0.0 collective-permute-done.20.refs_1_
  48.3 0.7 %join.3 = bf16[256,512]{1,0:T(8,128)(2,1)} custom-call(bf16[256,128]{1,0:T(8,128)(2,1)S(1)} %get-tuple-element.69.refs_0_, bf16[256,128]{1,0:T(8,128)(2,1)S(1)} %collective-permute-done.20.refs_1_, bf16[256,128]{1,0:T(8,128)(2,1)S(1)} %collective-permute-done.21.refs_2_, bf16[256,128]{1,0:T(8,128)(2,1)S(1)} %collective-permute-done.22.refs_3_), custom_call_target="tpu_custom_call" | custom-call | bytes 524288 | tf_op jit(solution)/shard_map/join/pallas_call | solution.py:512
  (1 shorter events, 0.0 us)
Async XLA Ops:
  0.6 9.2 %collective-permute-start.1 = (bf16[256,512]{1,0:T(8,128)(2,1)}, bf16[256,512]{1,0:T(8,128)(2,1)S(1)}, u32[]{:S(2)}, u32[]{:S(2)}) collective-permute-start(bf16[256,512]{1,0:T(8,128)(2,1)} %audio.3), channel_id=1, source_target_pairs={{0,1},{1,0},{2,3},{3,2},{4,5},{5,4},{6,7},{7,6},{8,9},{9,8},{10,11... | collective-permute-start | bytes 786440 | tf_op jit(solution)/shard_map/ppermute | solution.py:384
  1.9 11.8 %collective-permute-start.7 = (bf16[256,512]{1,0:T(8,128)(2,1)}, bf16[256,512]{1,0:T(8,128)(2,1)S(1)}, u32[]{:S(2)}, u32[]{:S(2)}) collective-permute-start(bf16[256,512]{1,0:T(8,128)(2,1)} %video.3), channel_id=1, source_target_pairs={{0,1},{1,0},{2,3},{3,2},{4,5},{5,4},{6,7},{7,6},{8,9},{9,8},{10,11... | collective-permute-start | bytes 786440 | tf_op jit(solution)/shard_map/ppermute | solution.py:384
  3.3 3.0 %collective-permute-start = (bf16[528,128]{1,0:T(8,128)(2,1)S(1)}, bf16[528,128]{1,0:T(8,128)(2,1)S(1)}, u32[]{:S(2)}, u32[]{:S(2)}) collective-permute-start(bf16[528,128]{1,0:T(8,128)(2,1)S(1)} %get-tuple-element.37), channel_id=1, source_target_pairs={{0,2},{2,0},{4,6},{6,4},{8,10},{10,8},{12,14},{14,12},{16,18},{18,... | collective-permute-start | bytes 405512 | tf_op jit(solution)/shard_map/ppermute | solution.py:388
  4.6 5.2 %collective-permute-start.2 = (bf16[528,128]{1,0:T(8,128)(2,1)S(1)}, bf16[528,128]{1,0:T(8,128)(2,1)S(1)}, u32[]{:S(2)}, u32[]{:S(2)}) collective-permute-start(bf16[528,128]{1,0:T(8,128)(2,1)S(1)} %get-tuple-element.40), channel_id=1, source_target_pairs={{0,4},{2,6},{4,0},{6,2},{8,12},{10,14},{12,8},{14,10},{16,20},{18,... | collective-permute-start | bytes 405512 | tf_op jit(solution)/shard_map/ppermute | solution.py:388
  5.9 9.8 %collective-permute-start.6 = (bf16[528,128]{1,0:T(8,128)(2,1)S(1)}, bf16[528,128]{1,0:T(8,128)(2,1)S(1)}, u32[]{:S(2)}, u32[]{:S(2)}) collective-permute-start(bf16[528,128]{1,0:T(8,128)(2,1)S(1)} %get-tuple-element.46), channel_id=1, source_target_pairs={{0,6},{2,4},{4,2},{6,0},{8,14},{10,12},{12,10},{14,8},{16,22},{18,... | collective-permute-start | bytes 405512 | tf_op jit(solution)/shard_map/ppermute | solution.py:388
  10.2 6.7 %collective-permute-start.3 = (bf16[256,128]{1,0:T(8,128)(2,1)S(1)}, bf16[256,128]{1,0:T(8,128)(2,1)S(1)}, u32[]{:S(2)}, u32[]{:S(2)}) collective-permute-start(bf16[256,128]{1,0:T(8,128)(2,1)S(1)} %get-tuple-element.42), channel_id=1, source_target_pairs={{0,2},{2,0},{4,6},{6,4},{8,10},{10,8},{12,14},{14,12},{16,18},{18,... | collective-permute-start | bytes 196616 | tf_op jit(solution)/shard_map/ppermute | solution.py:388
  11.6 5.9 %collective-permute-start.4 = (bf16[256,128]{1,0:T(8,128)(2,1)S(1)}, bf16[256,128]{1,0:T(8,128)(2,1)S(1)}, u32[]{:S(2)}, u32[]{:S(2)}) collective-permute-start(bf16[256,128]{1,0:T(8,128)(2,1)S(1)} %get-tuple-element.43), channel_id=1, source_target_pairs={{0,4},{2,6},{4,0},{6,2},{8,12},{10,14},{12,8},{14,10},{16,20},{18,... | collective-permute-start | bytes 196616 | tf_op jit(solution)/shard_map/ppermute | solution.py:388
  12.8 4.6 %collective-permute-start.5 = (bf16[256,128]{1,0:T(8,128)(2,1)S(1)}, bf16[256,128]{1,0:T(8,128)(2,1)S(1)}, u32[]{:S(2)}, u32[]{:S(2)}) collective-permute-start(bf16[256,128]{1,0:T(8,128)(2,1)S(1)} %get-tuple-element.44), channel_id=1, source_target_pairs={{0,6},{2,4},{4,2},{6,0},{8,14},{10,12},{12,10},{14,8},{16,22},{18,... | collective-permute-start | bytes 196616 | tf_op jit(solution)/shard_map/ppermute | solution.py:388
  14.1 8.8 %collective-permute-start.9 = (bf16[256,128]{1,0:T(8,128)(2,1)S(1)}, bf16[256,128]{1,0:T(8,128)(2,1)S(1)}, u32[]{:S(2)}, u32[]{:S(2)}) collective-permute-start(bf16[256,128]{1,0:T(8,128)(2,1)S(1)} %get-tuple-element.50), channel_id=1, source_target_pairs={{0,2},{2,0},{4,6},{6,4},{8,10},{10,8},{12,14},{14,12},{16,18},{18,... | collective-permute-start | bytes 196616 | tf_op jit(solution)/shard_map/ppermute | solution.py:388
  15.7 7.3 %collective-permute-start.10 = (bf16[256,128]{1,0:T(8,128)(2,1)S(1)}, bf16[256,128]{1,0:T(8,128)(2,1)S(1)}, u32[]{:S(2)}, u32[]{:S(2)}) collective-permute-start(bf16[256,128]{1,0:T(8,128)(2,1)S(1)} %get-tuple-element.51), channel_id=1, source_target_pairs={{0,4},{2,6},{4,0},{6,2},{8,12},{10,14},{12,8},{14,10},{16,20},{18,... | collective-permute-start | bytes 196616 | tf_op jit(solution)/shard_map/ppermute | solution.py:388
  16.9 6.1 %collective-permute-start.11 = (bf16[256,128]{1,0:T(8,128)(2,1)S(1)}, bf16[256,128]{1,0:T(8,128)(2,1)S(1)}, u32[]{:S(2)}, u32[]{:S(2)}) collective-permute-start(bf16[256,128]{1,0:T(8,128)(2,1)S(1)} %get-tuple-element.52), channel_id=1, source_target_pairs={{0,6},{2,4},{4,2},{6,0},{8,14},{10,12},{12,10},{14,8},{16,22},{18,... | collective-permute-start | bytes 196616 | tf_op jit(solution)/shard_map/ppermute | solution.py:388
  17.5 8.8 %collective-permute-start.12 = (bf16[3,272,128]{2,1,0:T(8,128)(2,1)S(1)}, bf16[3,272,128]{2,1,0:T(8,128)(2,1)S(1)}, u32[]{:S(2)}, u32[]{:S(2)}) collective-permute-start(bf16[3,272,128]{2,1,0:T(8,128)(2,1)S(1)} %halo.5), channel_id=1, source_target_pairs={{8,16},{10,18},{12,20},{14,22},{16,8},{18,10},{20,12},{22,14},{9,1... | collective-permute-start | bytes 626696 | tf_op jit(solution)/shard_map/ppermute | solution.py:393
  20.7 13.6 %collective-permute-start.15 = (bf16[3,256,128]{2,1,0:T(8,128)(2,1)S(1)}, bf16[3,256,128]{2,1,0:T(8,128)(2,1)S(1)}, u32[]{:S(2)}, u32[]{:S(2)}) collective-permute-start(bf16[3,256,128]{2,1,0:T(8,128)(2,1)S(1)} %halo.6), channel_id=1, source_target_pairs={{8,16},{10,18},{12,20},{14,22},{16,8},{18,10},{20,12},{22,14},{9,1... | collective-permute-start | bytes 589832 | tf_op jit(solution)/shard_map/ppermute | solution.py:393
  22.9 6.4 %collective-permute-start.8 = (bf16[3,272,128]{2,1,0:T(8,128)(2,1)S(1)}, bf16[3,272,128]{2,1,0:T(8,128)(2,1)S(1)}, u32[]{:S(2)}, u32[]{:S(2)}) collective-permute-start(bf16[3,272,128]{2,1,0:T(8,128)(2,1)S(1)} %halo.4), channel_id=1, source_target_pairs={{0,8},{2,10},{4,12},{6,14},{8,0},{10,2},{12,4},{14,6},{16,24},{18,... | collective-permute-start | bytes 626696 | tf_op jit(solution)/shard_map/ppermute | solution.py:393
  26.3 8.0 %collective-permute-start.16 = (bf16[3,256,128]{2,1,0:T(8,128)(2,1)S(1)}, bf16[3,256,128]{2,1,0:T(8,128)(2,1)S(1)}, u32[]{:S(2)}, u32[]{:S(2)}) collective-permute-start(bf16[3,256,128]{2,1,0:T(8,128)(2,1)S(1)} %halo.7), channel_id=1, source_target_pairs={{0,8},{2,10},{4,12},{6,14},{8,0},{10,2},{12,4},{14,6},{16,24},{18,... | collective-permute-start | bytes 589832 | tf_op jit(solution)/shard_map/ppermute | solution.py:393
  30.8 10.1 %collective-permute-start.13 = (bf16[3,288,128]{2,1,0:T(8,128)(2,1)S(1)}, bf16[3,288,128]{2,1,0:T(8,128)(2,1)S(1)}, u32[]{:S(2)}, u32[]{:S(2)}) collective-permute-start(bf16[3,288,128]{2,1,0:T(8,128)(2,1)S(1)} %get-tuple-element.55), channel_id=1, source_target_pairs={{0,8},{2,10},{4,12},{6,14},{8,0},{10,2},{12,4},{14,6},{16,24},{18,... | collective-permute-start | bytes 663560 | tf_op jit(solution)/shard_map/ppermute | solution.py:393
  30.9 10.0 %collective-permute-start.14 = (bf16[3,288,128]{2,1,0:T(8,128)(2,1)S(1)}, bf16[3,288,128]{2,1,0:T(8,128)(2,1)S(1)}, u32[]{:S(2)}, u32[]{:S(2)}) collective-permute-start(bf16[3,288,128]{2,1,0:T(8,128)(2,1)S(1)} %get-tuple-element.56), channel_id=1, source_target_pairs={{8,16},{10,18},{12,20},{14,22},{16,8},{18,10},{20,12},{22,14},{9,1... | collective-permute-start | bytes 663560 | tf_op jit(solution)/shard_map/ppermute | solution.py:393
  37.0 11.2 %collective-permute-start.22 = (bf16[256,128]{1,0:T(8,128)(2,1)S(1)}, bf16[256,128]{1,0:T(8,128)(2,1)S(1)}, u32[]{:S(2)}, u32[]{:S(2)}) collective-permute-start(bf16[256,128]{1,0:T(8,128)(2,1)S(1)} %get-tuple-element.71), channel_id=1, source_target_pairs={{0,6},{2,4},{4,2},{6,0},{8,14},{10,12},{12,10},{14,8},{16,22},{18,... | collective-permute-start | bytes 196616 | tf_op jit(solution)/shard_map/ppermute | solution.py:388
  40.7 7.6 %collective-permute-start.21 = (bf16[256,128]{1,0:T(8,128)(2,1)S(1)}, bf16[256,128]{1,0:T(8,128)(2,1)S(1)}, u32[]{:S(2)}, u32[]{:S(2)}) collective-permute-start(bf16[256,128]{1,0:T(8,128)(2,1)S(1)} %get-tuple-element.59.refs_0_), channel_id=1, source_target_pairs={{0,4},{2,6},{4,0},{6,2},{8,12},{10,14},{12,8},{14,10},{16,20},{18,... | collective-permute-start | bytes 196616 | tf_op jit(solution)/shard_map/ppermute | solution.py:388
  41.4 4.4 %collective-permute-start.17 = (bf16[256,128]{1,0:T(8,128)(2,1)S(1)}, bf16[256,128]{1,0:T(8,128)(2,1)S(1)}, u32[]{:S(2)}, u32[]{:S(2)}) collective-permute-start(bf16[256,128]{1,0:T(8,128)(2,1)S(1)} %get-tuple-element.61), channel_id=1, source_target_pairs={{0,2},{2,0},{4,6},{6,4},{8,10},{10,8},{12,14},{14,12},{16,18},{18,... | collective-permute-start | bytes 196616 | tf_op jit(solution)/shard_map/ppermute | solution.py:388
  41.7 4.4 %collective-permute-start.18 = (bf16[256,128]{1,0:T(8,128)(2,1)S(1)}, bf16[256,128]{1,0:T(8,128)(2,1)S(1)}, u32[]{:S(2)}, u32[]{:S(2)}) collective-permute-start(bf16[256,128]{1,0:T(8,128)(2,1)S(1)} %get-tuple-element.62), channel_id=1, source_target_pairs={{0,4},{2,6},{4,0},{6,2},{8,12},{10,14},{12,8},{14,10},{16,20},{18,... | collective-permute-start | bytes 196616 | tf_op jit(solution)/shard_map/ppermute | solution.py:388
  42.8 4.7 %collective-permute-start.19 = (bf16[256,128]{1,0:T(8,128)(2,1)S(1)}, bf16[256,128]{1,0:T(8,128)(2,1)S(1)}, u32[]{:S(2)}, u32[]{:S(2)}) collective-permute-start(bf16[256,128]{1,0:T(8,128)(2,1)S(1)} %get-tuple-element.63), channel_id=1, source_target_pairs={{0,6},{2,4},{4,2},{6,0},{8,14},{10,12},{12,10},{14,8},{16,22},{18,... | collective-permute-start | bytes 196616 | tf_op jit(solution)/shard_map/ppermute | solution.py:388
  45.9 2.4 %collective-permute-start.20 = (bf16[256,128]{1,0:T(8,128)(2,1)S(1)}, bf16[256,128]{1,0:T(8,128)(2,1)S(1)}, u32[]{:S(2)}, u32[]{:S(2)}) collective-permute-start(bf16[256,128]{1,0:T(8,128)(2,1)S(1)} %get-tuple-element.70), channel_id=1, source_target_pairs={{0,2},{2,0},{4,6},{6,4},{8,10},{10,8},{12,14},{14,12},{16,18},{18,... | collective-permute-start | bytes 196616 | tf_op jit(solution)/shard_map/ppermute | solution.py:388

commit v21 on v19

--- a/solution.py
+++ b/solution.py
@@ -448,7 +448,7 @@
         exps=2 * GROUP * rows * inside,
         name="rows",
     )(*packs, *queries, *keys)
-    audio_edges = halo(packs, [])
+    audio_edges = [halo(packs, [], *[peaks])[0], halo(packs, [], *[])[1]]
     back = shape((RADIUS, rows + rows // width * STAT_ROWS, width), bf16)
     lent_a, lent_b, edge_turned = call(
         lend_kernel,

time: 48.1 us -> 49.4 us (1.027)
  Pallas kernels: 16.7 us -> 18.1 us
  waiting for transfers between devices: 3.88 us -> 3.22 us
  starting transfers between devices: 26.3 us -> 26.9 us
    pallas_call x2 -> x3, Pallas kernels: 0.14 us -> 1.57 us  [halo(): call(functools.partial(halo_kernel, 2 * rows if id_packs else 0), [edge,...]
    ppermute x6, waiting for transfers between devices: 0.69 us -> 0.02 us  [crossed(): lax.ppermute(sent, 'tm', [(p * GROUP + i, q * GROUP + i) for p, q in pair...]
    ppermute x6, starting transfers between devices: 9.66 us -> 10.3 us  [crossed(): lax.ppermute(sent, 'tm', [(p * GROUP + i, q * GROUP + i) for p, q in pair...]
  transfers between devices with their start and end apart: 23 -> 23, of which waited for: 4 -> 3; matrix products, arithmetic and copies ran while one was open for 0% -> 0% of each run, Pallas kernels for 33% -> 35%
where the time goes in v21:
time: 49.4 us; the launch traced here: 49.2 us
  starting transfers between devices  26.9 us (54%)
  Pallas kernels  18.1 us (37%)
  waiting for transfers between devices  3.22 us (7%)
  between operations  0.99 us (2%)
    ppermute x15, starting transfers between devices, traded(): lax.ppermute(pieces[k], 'tm', pairs(k))  15.1 us
    ppermute x6, starting transfers between devices, crossed(): lax.ppermute(sent, 'tm', [(p * GROUP + i, q * GROUP + i) for p, q in pair...  10.3 us
    pallas_call x1, Pallas kernels, local(): call(rows_kernel, [shape((GROUP, rows, width), f32), shape((GROUP, 2, row...  3.3 us
    ppermute x15, waiting for transfers between devices, traded(): lax.ppermute(pieces[k], 'tm', pairs(k))  2.77 us
    pallas_call x1, Pallas kernels, local(): call(functools.partial(columns_kernel, far), [piece] * len(far) + shared,...  2.65 us
    pallas_call x1, Pallas kernels, local(): call(lend_kernel, [back, back, shape((2 * width, around), bf16)], [pltpu....  2.63 us
    pallas_call x1, Pallas kernels, local(): call(functools.partial(columns_kernel, near), [piece] * len(near), ins=[V...  2.26 us
    pallas_call x1, Pallas kernels, local(): call(prepare_kernel, [part, part, square, square], [pltpu.VMEM((rows, hal...  1.78 us
  transfers between devices with their start and end apart: 23, of which 3 were waited for; matrix products, arithmetic and copies ran while one was open for 0% of the time, Pallas kernels for 35%

profile of v21, /device:TPU:9, one launch (start us, length us, event | category | flops | bytes accessed | tf_op | source)
XLA Modules:
  0.0 49.2 jit_solution(16063663726140334921)
XLA Ops:
  0.6 1.3 %collective-permute-start.1 = (bf16[256,512]{1,0:T(8,128)(2,1)}, bf16[256,512]{1,0:T(8,128)(2,1)S(1)}, u32[]{:S(2)}, u32[]{:S(2)}) collective-permute-start(bf16[256,512]{1,0:T(8,128)(2,1)} %audio.3), channel_id=1, source_target_pairs={{0,1},{1,0},{2,3},{3,2},{4,5},{5,4},{6,7},{7,6},{8,9},{9,8},{10,11... | collective-permute-start | bytes 786440 | tf_op jit(solution)/shard_map/ppermute | solution.py:368
  1.9 0.2 collective-permute-start.7
  2.2 1.2 %split.1 = (bf16[528,128]{1,0:T(8,128)(2,1)S(1)}, bf16[528,128]{1,0:T(8,128)(2,1)S(1)}, bf16[528,128]{1,0:T(8,128)(2,1)S(1)}, bf16[528,128]{1,0:T(8,128)(2,1)S(1)}) custom-call(bf16[256,512]{1,0:T(8,128)(2,1)} %audio.3, bf16[256,512]{1,0:T(8,128)(2,1)} %video.3, s32[2,128]{1,0:T(2,128)} %bitcast.1), custom_call_target="tpu_custom_call" | custom-call | bytes 1048576 | tf_op jit(solution)/shard_map/split/pallas_call | solution.py:390
  3.3 1.3 %collective-permute-start = (bf16[528,128]{1,0:T(8,128)(2,1)S(1)}, bf16[528,128]{1,0:T(8,128)(2,1)S(1)}, u32[]{:S(2)}, u32[]{:S(2)}) collective-permute-start(bf16[528,128]{1,0:T(8,128)(2,1)S(1)} %get-tuple-element.41), channel_id=1, source_target_pairs={{0,2},{2,0},{4,6},{6,4},{8,10},{10,8},{12,14},{14,12},{16,18},{18,... | collective-permute-start | bytes 405512 | tf_op jit(solution)/shard_map/ppermute | solution.py:372
  4.6 1.2 %collective-permute-start.2 = (bf16[528,128]{1,0:T(8,128)(2,1)S(1)}, bf16[528,128]{1,0:T(8,128)(2,1)S(1)}, u32[]{:S(2)}, u32[]{:S(2)}) collective-permute-start(bf16[528,128]{1,0:T(8,128)(2,1)S(1)} %get-tuple-element.44), channel_id=1, source_target_pairs={{0,4},{2,6},{4,0},{6,2},{8,12},{10,14},{12,8},{14,10},{16,20},{18,... | collective-permute-start | bytes 405512 | tf_op jit(solution)/shard_map/ppermute | solution.py:372
  5.9 0.5 collective-permute-start.6
  6.3 0.0 collective-permute-done.refs_0_.refs_5_.refs_1_
  6.3 1.8 %prepare.1 = (f32[256,512]{1,0:T(8,128)S(1)}, f32[256,512]{1,0:T(8,128)S(1)}, bf16[512,512]{1,0:T(8,128)(2,1)S(1)}, bf16[512,512]{1,0:T(8,128)(2,1)S(1)}) custom-call(bf16[256,512]{1,0:T(8,128)(2,1)} %audio.3, bf16[256,512]{1,0:T(8,128)(2,1)} %video.3, bf16[1024,512]{1,0:T(8,128)(2,1)} %query.1, bf16[1024,512]{1,0:T(8,128)(2,1)} %key.1, ...), custom_call_target="tpu_custom_call" | custom-call | flops 268435456 | bytes 4194304 | tf_op jit(solution)/shard_map/prepare/pallas_call | solution.py:400
  8.1 1.7 %collective-permute-done.2.refs_1_.refs_6_.refs_2_ = bf16[528,128]{1,0:T(8,128)(2,1)S(1)} collective-permute-done((bf16[528,128]{1,0:T(8,128)(2,1)S(1)}, bf16[528,128]{1,0:T(8,128)(2,1)S(1)}, u32[]{:S(2)}, u32[]{:S(2)}) %collective-permute-start.2) | collective-permute-done | bytes 135200 | tf_op jit(solution)/shard_map/ppermute | solution.py:372
  9.8 0.0 collective-permute-done.1.other
  9.8 0.4 project.2
  10.2 1.4 %collective-permute-start.3 = (bf16[256,128]{1,0:T(8,128)(2,1)S(1)}, bf16[256,128]{1,0:T(8,128)(2,1)S(1)}, u32[]{:S(2)}, u32[]{:S(2)}) collective-permute-start(bf16[256,128]{1,0:T(8,128)(2,1)S(1)} %get-tuple-element.46), channel_id=1, source_target_pairs={{0,2},{2,0},{4,6},{6,4},{8,10},{10,8},{12,14},{14,12},{16,18},{18,... | collective-permute-start | bytes 196616 | tf_op jit(solution)/shard_map/ppermute | solution.py:372
  11.6 1.2 %collective-permute-start.4 = (bf16[256,128]{1,0:T(8,128)(2,1)S(1)}, bf16[256,128]{1,0:T(8,128)(2,1)S(1)}, u32[]{:S(2)}, u32[]{:S(2)}) collective-permute-start(bf16[256,128]{1,0:T(8,128)(2,1)S(1)} %get-tuple-element.47), channel_id=1, source_target_pairs={{0,4},{2,6},{4,0},{6,2},{8,12},{10,14},{12,8},{14,10},{16,20},{18,... | collective-permute-start | bytes 196616 | tf_op jit(solution)/shard_map/ppermute | solution.py:372
  12.8 0.5 collective-permute-start.5
  13.3 0.4 collective-permute-done.7.other
  13.7 0.4 project.3
  14.1 1.6 %collective-permute-start.10 = (bf16[256,128]{1,0:T(8,128)(2,1)S(1)}, bf16[256,128]{1,0:T(8,128)(2,1)S(1)}, u32[]{:S(2)}, u32[]{:S(2)}) collective-permute-start(bf16[256,128]{1,0:T(8,128)(2,1)S(1)} %get-tuple-element.56), channel_id=1, source_target_pairs={{0,2},{2,0},{4,6},{6,4},{8,10},{10,8},{12,14},{14,12},{16,18},{18,... | collective-permute-start | bytes 196616 | tf_op jit(solution)/shard_map/ppermute | solution.py:372
  15.7 0.0 collective-permute-done.6.refs_7_.refs_3_
  15.7 1.2 %collective-permute-start.11 = (bf16[256,128]{1,0:T(8,128)(2,1)S(1)}, bf16[256,128]{1,0:T(8,128)(2,1)S(1)}, u32[]{:S(2)}, u32[]{:S(2)}) collective-permute-start(bf16[256,128]{1,0:T(8,128)(2,1)S(1)} %get-tuple-element.57), channel_id=1, source_target_pairs={{0,4},{2,6},{4,0},{6,2},{8,12},{10,14},{12,8},{14,10},{16,20},{18,... | collective-permute-start | bytes 196616 | tf_op jit(solution)/shard_map/ppermute | solution.py:372
  16.9 0.0 collective-permute-done.3.refs_1_.refs_5_
  16.9 0.5 collective-permute-start.12
  17.4 0.0 collective-permute-done.4.refs_2_.refs_6_
  17.4 0.0 collective-permute-done.5.refs_3_.refs_7_
  17.4 0.1 halo.3
  17.5 3.2 %collective-permute-start.8 = (bf16[3,272,128]{2,1,0:T(8,128)(2,1)S(1)}, bf16[3,272,128]{2,1,0:T(8,128)(2,1)S(1)}, u32[]{:S(2)}, u32[]{:S(2)}) collective-permute-start(bf16[3,272,128]{2,1,0:T(8,128)(2,1)S(1)} %get-tuple-element.54), channel_id=1, source_target_pairs={{8,16},{10,18},{12,20},{14,22},{16,8},{18,10},{20,12},{22,14},{9,1... | collective-permute-start | bytes 626696 | tf_op jit(solution)/shard_map/ppermute | solution.py:377
  20.7 0.1 collective-permute-start.9
  20.8 0.8 %halo.4 = (bf16[3,256,128]{2,1,0:T(8,128)(2,1)}, bf16[3,256,128]{2,1,0:T(8,128)(2,1)S(1)}) custom-call(bf16[528,128]{1,0:T(8,128)(2,1)S(1)} %get-tuple-element.49.refs_4_.refs_0_, bf16[528,128]{1,0:T(8,128)(2,1)S(1)} %collective-permute-done.refs_0_.refs_5_.refs_1_, bf16[528,128]{1,0:T(8,128)(2,1)S(1)} %collective-permute-done.2.refs_1_.refs_6_.refs_2_, ...), custom_call_target="tpu_custom_call" | custom-call | bytes 655360 | tf_op jit(solution)/shard_map/halo/pallas_call | solution.py:425
  21.5 0.0 collective-permute-done.10.refs_9_
  21.5 2.1 %collective-permute-start.15 = (bf16[3,256,128]{2,1,0:T(8,128)(2,1)S(1)}, bf16[3,256,128]{2,1,0:T(8,128)(2,1)S(1)}, u32[]{:S(2)}, u32[]{:S(2)}) collective-permute-start(bf16[3,256,128]{2,1,0:T(8,128)(2,1)S(1)} %get-tuple-element.65), channel_id=1, source_target_pairs={{8,16},{10,18},{12,20},{14,22},{16,8},{18,10},{20,12},{22,14},{9,1... | collective-permute-start | bytes 589832 | tf_op jit(solution)/shard_map/ppermute | solution.py:377
  23.6 0.0 collective-permute-done.11.refs_10_
  23.6 0.0 collective-permute-done.12.refs_11_
  23.6 3.3 %rows.1 = (f32[4,256,128]{2,1,0:T(8,128)S(1)}, f32[4,2,256,128]{3,2,1,0:T(8,128)S(1)}, bf16[256,1024]{1,0:T(8,128)(2,1)S(1)}, bf16[1024,256]{1,0:T(8,128)(2,1)S(1)}) custom-call(bf16[528,128]{1,0:T(8,128)(2,1)S(1)} %get-tuple-element.49.refs_4_.refs_0_, bf16[528,128]{1,0:T(8,128)(2,1)S(1)} %collective-permute-done.refs_0_.refs_5_.refs_1_, ...), custom_call_target="tpu_custom_call" | custom-call | flops 2147483648 | bytes 2097152 | tf_op jit(solution)/shard_map/rows/pallas_call | solution.py:442
  26.9 0.8 %halo.5 = (bf16[3,256,128]{2,1,0:T(8,128)(2,1)S(1)}, bf16[3,256,128]{2,1,0:T(8,128)(2,1)}) custom-call(bf16[528,128]{1,0:T(8,128)(2,1)S(1)} %get-tuple-element.49.refs_4_.refs_0_, bf16[528,128]{1,0:T(8,128)(2,1)S(1)} %collective-permute-done.refs_0_.refs_5_.refs_1_, bf16[528,128]{1,0:T(8,128)(2,1)S(1)} %collective-permute-done.2.refs_1_.refs_6_.refs_2_, ...), custom_call_target="tpu_custom_call" | custom-call | bytes 655360 | tf_op jit(solution)/shard_map/halo/pallas_call | solution.py:425
  27.7 0.0 collective-permute-start.16
  27.7 0.0 collective-permute-done.8.edge_b
  27.7 0.0 collective-permute-done.9.edge_a
  27.7 2.6 %lend.1 = (bf16[3,288,128]{2,1,0:T(8,128)(2,1)S(1)}, bf16[3,288,128]{2,1,0:T(8,128)(2,1)S(1)}, bf16[256,1536]{1,0:T(8,128)(2,1)S(1)}) custom-call(bf16[3,272,128]{2,1,0:T(8,128)(2,1)S(1)} %collective-permute-done.8.edge_b, bf16[3,272,128]{2,1,0:T(8,128)(2,1)S(1)} %collective-permute-done.9.edge_a, bf16[256,1024]{1,0:T(8,128)(2,1)S(1)} %get-tuple-element.59.plane_turned, ...), custom_call_target="tpu_custom_call" | custom-call | flops 4831838208 | bytes 3145728 | tf_op jit(solution)/shard_map/lend/pallas_call | solution.py:453
  30.4 1.5 %collective-permute-start.13 = (bf16[3,288,128]{2,1,0:T(8,128)(2,1)S(1)}, bf16[3,288,128]{2,1,0:T(8,128)(2,1)S(1)}, u32[]{:S(2)}, u32[]{:S(2)}) collective-permute-start(bf16[3,288,128]{2,1,0:T(8,128)(2,1)S(1)} %get-tuple-element.61), channel_id=1, source_target_pairs={{0,8},{2,10},{4,12},{6,14},{8,0},{10,2},{12,4},{14,6},{16,24},{18,... | collective-permute-start | bytes 663560 | tf_op jit(solution)/shard_map/ppermute | solution.py:377
  31.9 3.4 %collective-permute-start.14 = (bf16[3,288,128]{2,1,0:T(8,128)(2,1)S(1)}, bf16[3,288,128]{2,1,0:T(8,128)(2,1)S(1)}, u32[]{:S(2)}, u32[]{:S(2)}) collective-permute-start(bf16[3,288,128]{2,1,0:T(8,128)(2,1)S(1)} %get-tuple-element.62), channel_id=1, source_target_pairs={{8,16},{10,18},{12,20},{14,22},{16,8},{18,10},{20,12},{22,14},{9,1... | collective-permute-start | bytes 663560 | tf_op jit(solution)/shard_map/ppermute | solution.py:377
  35.3 0.0 collective-permute-done.15.refs_12_
  35.3 0.0 collective-permute-done.16.refs_13_
  35.3 2.6 %columns.2 = (bf16[256,128]{1,0:T(8,128)(2,1)S(1)}, bf16[256,128]{1,0:T(8,128)(2,1)S(1)}, bf16[256,1024]{1,0:T(8,128)(2,1)S(1)}, bf16[1024,256]{1,0:T(8,128)(2,1...) custom-call(bf16[528,128]{1,0:T(8,128)(2,1)S(1)} %get-tuple-element.49.refs_4_.refs_0_, ...), custom_call_target="tpu_custom_call" | custom-call | flops 1879048192 | bytes 1572864 | tf_op jit(solution)/shard_map/columns/pallas_call | solution.py:472
  37.9 2.7 %collective-permute-start.22 = (bf16[256,128]{1,0:T(8,128)(2,1)S(1)}, bf16[256,128]{1,0:T(8,128)(2,1)S(1)}, u32[]{:S(2)}, u32[]{:S(2)}) collective-permute-start(bf16[256,128]{1,0:T(8,128)(2,1)S(1)} %get-tuple-element.79), channel_id=1, source_target_pairs={{0,6},{2,4},{4,2},{6,0},{8,14},{10,12},{12,10},{14,8},{16,22},{18,... | collective-permute-start | bytes 196616 | tf_op jit(solution)/shard_map/ppermute | solution.py:372
  40.7 0.3 collective-permute-start.21
  40.9 0.0 collective-permute-done.13.back_a
  40.9 0.0 collective-permute-done.14.back_b
  40.9 0.5 %merge.1 = (bf16[256,128]{1,0:T(8,128)(2,1)S(1)}, bf16[256,128]{1,0:T(8,128)(2,1)S(1)}, bf16[256,128]{1,0:T(8,128)(2,1)S(1)}, bf16[256,128]{1,0:T(8,128)(2,1)S(1)}) custom-call(bf16[3,288,128]{2,1,0:T(8,128)(2,1)S(1)} %collective-permute-done.13.back_a, bf16[3,288,128]{2,1,0:T(8,128)(2,1)S(1)} %collective-permute-done.14.back_b, ...), custom_call_target="tpu_custom_call" | custom-call | bytes 2097152 | tf_op jit(solution)/shard_map/merge/pallas_call | solution.py:475
  41.4 0.7 %collective-permute-start.17 = (bf16[256,128]{1,0:T(8,128)(2,1)S(1)}, bf16[256,128]{1,0:T(8,128)(2,1)S(1)}, u32[]{:S(2)}, u32[]{:S(2)}) collective-permute-start(bf16[256,128]{1,0:T(8,128)(2,1)S(1)} %get-tuple-element.70), channel_id=1, source_target_pairs={{0,2},{2,0},{4,6},{6,4},{8,10},{10,8},{12,14},{14,12},{16,18},{18,... | collective-permute-start | bytes 196616 | tf_op jit(solution)/shard_map/ppermute | solution.py:372
  42.2 1.2 %collective-permute-start.18 = (bf16[256,128]{1,0:T(8,128)(2,1)S(1)}, bf16[256,128]{1,0:T(8,128)(2,1)S(1)}, u32[]{:S(2)}, u32[]{:S(2)}) collective-permute-start(bf16[256,128]{1,0:T(8,128)(2,1)S(1)} %get-tuple-element.71), channel_id=1, source_target_pairs={{0,4},{2,6},{4,0},{6,2},{8,12},{10,14},{12,8},{14,10},{16,20},{18,... | collective-permute-start | bytes 196616 | tf_op jit(solution)/shard_map/ppermute | solution.py:372
  43.4 0.5 collective-permute-start.19
  43.9 2.3 %columns.3 = (bf16[256,128]{1,0:T(8,128)(2,1)S(1)}, bf16[256,128]{1,0:T(8,128)(2,1)S(1)}) custom-call(bf16[256,1536]{1,0:T(8,128)(2,1)S(1)} %get-tuple-element.67.refs_14_.refs_0_, bf16[256,1024]{1,0:T(8,128)(2,1)S(1)} %get-tuple-element.73.refs_1_, bf16[1024,256]{1,0:T(8,128)(2,1)S(1)} %get-tuple-element.74.refs_2_, ...), custom_call_target="tpu_custom_call" | custom-call | flops 1879048192 | bytes 1572864 | tf_op jit(solution)/shard_map/columns/pallas_call | solution.py:485
  46.2 0.0 collective-permute-done.17.refs_1_
  46.2 0.2 collective-permute-start.20
  46.4 0.0 collective-permute-done.18.refs_2_
  46.4 1.1 %collective-permute-done.19.refs_3_ = bf16[256,128]{1,0:T(8,128)(2,1)S(1)} collective-permute-done((bf16[256,128]{1,0:T(8,128)(2,1)S(1)}, bf16[256,128]{1,0:T(8,128)(2,1)S(1)}, u32[]{:S(2)}, u32[]{:S(2)}) %collective-permute-start.19) | collective-permute-done | bytes 65568 | tf_op jit(solution)/shard_map/ppermute | solution.py:372
  47.5 0.7 %join.2 = bf16[256,512]{1,0:T(8,128)(2,1)} custom-call(bf16[256,128]{1,0:T(8,128)(2,1)S(1)} %get-tuple-element.69.refs_0_.refs_5_, bf16[256,128]{1,0:T(8,128)(2,1)S(1)} %collective-permute-done.17.refs_1_, bf16[256,128]{1,0:T(8,128)(2,1)S(1)} %collective-permute-done.18.refs_2_, bf16[256,128]{1,0:T(8,128)(2,1)S(1)} %collective-permute-done.19.refs_3_), custom_call_target="tpu_custom_call" | custom-call | bytes 524288 | tf_op jit(solution)/shard_map/join/pallas_call | solution.py:494
  48.2 0.0 collective-permute-done.22.refs_3_
  48.2 0.0 collective-permute-done.21.refs_2_
  48.2 0.0 collective-permute-done.20.refs_1_
  48.3 0.7 %join.3 = bf16[256,512]{1,0:T(8,128)(2,1)} custom-call(bf16[256,128]{1,0:T(8,128)(2,1)S(1)} %get-tuple-element.77.refs_0_, bf16[256,128]{1,0:T(8,128)(2,1)S(1)} %collective-permute-done.20.refs_1_, bf16[256,128]{1,0:T(8,128)(2,1)S(1)} %collective-permute-done.21.refs_2_, bf16[256,128]{1,0:T(8,128)(2,1)S(1)} %collective-permute-done.22.refs_3_), custom_call_target="tpu_custom_call" | custom-call | bytes 524288 | tf_op jit(solution)/shard_map/join/pallas_call | solution.py:494
Async XLA Ops:
  0.6 9.2 %collective-permute-start.1 = (bf16[256,512]{1,0:T(8,128)(2,1)}, bf16[256,512]{1,0:T(8,128)(2,1)S(1)}, u32[]{:S(2)}, u32[]{:S(2)}) collective-permute-start(bf16[256,512]{1,0:T(8,128)(2,1)} %audio.3), channel_id=1, source_target_pairs={{0,1},{1,0},{2,3},{3,2},{4,5},{5,4},{6,7},{7,6},{8,9},{9,8},{10,11... | collective-permute-start | bytes 786440 | tf_op jit(solution)/shard_map/ppermute | solution.py:368
  1.9 11.8 %collective-permute-start.7 = (bf16[256,512]{1,0:T(8,128)(2,1)}, bf16[256,512]{1,0:T(8,128)(2,1)S(1)}, u32[]{:S(2)}, u32[]{:S(2)}) collective-permute-start(bf16[256,512]{1,0:T(8,128)(2,1)} %video.3), channel_id=1, source_target_pairs={{0,1},{1,0},{2,3},{3,2},{4,5},{5,4},{6,7},{7,6},{8,9},{9,8},{10,11... | collective-permute-start | bytes 786440 | tf_op jit(solution)/shard_map/ppermute | solution.py:368
  3.3 3.0 %collective-permute-start = (bf16[528,128]{1,0:T(8,128)(2,1)S(1)}, bf16[528,128]{1,0:T(8,128)(2,1)S(1)}, u32[]{:S(2)}, u32[]{:S(2)}) collective-permute-start(bf16[528,128]{1,0:T(8,128)(2,1)S(1)} %get-tuple-element.41), channel_id=1, source_target_pairs={{0,2},{2,0},{4,6},{6,4},{8,10},{10,8},{12,14},{14,12},{16,18},{18,... | collective-permute-start | bytes 405512 | tf_op jit(solution)/shard_map/ppermute | solution.py:372
  4.6 5.2 %collective-permute-start.2 = (bf16[528,128]{1,0:T(8,128)(2,1)S(1)}, bf16[528,128]{1,0:T(8,128)(2,1)S(1)}, u32[]{:S(2)}, u32[]{:S(2)}) collective-permute-start(bf16[528,128]{1,0:T(8,128)(2,1)S(1)} %get-tuple-element.44), channel_id=1, source_target_pairs={{0,4},{2,6},{4,0},{6,2},{8,12},{10,14},{12,8},{14,10},{16,20},{18,... | collective-permute-start | bytes 405512 | tf_op jit(solution)/shard_map/ppermute | solution.py:372
  5.9 9.8 %collective-permute-start.6 = (bf16[528,128]{1,0:T(8,128)(2,1)S(1)}, bf16[528,128]{1,0:T(8,128)(2,1)S(1)}, u32[]{:S(2)}, u32[]{:S(2)}) collective-permute-start(bf16[528,128]{1,0:T(8,128)(2,1)S(1)} %get-tuple-element.50), channel_id=1, source_target_pairs={{0,6},{2,4},{4,2},{6,0},{8,14},{10,12},{12,10},{14,8},{16,22},{18,... | collective-permute-start | bytes 405512 | tf_op jit(solution)/shard_map/ppermute | solution.py:372
  10.2 6.7 %collective-permute-start.3 = (bf16[256,128]{1,0:T(8,128)(2,1)S(1)}, bf16[256,128]{1,0:T(8,128)(2,1)S(1)}, u32[]{:S(2)}, u32[]{:S(2)}) collective-permute-start(bf16[256,128]{1,0:T(8,128)(2,1)S(1)} %get-tuple-element.46), channel_id=1, source_target_pairs={{0,2},{2,0},{4,6},{6,4},{8,10},{10,8},{12,14},{14,12},{16,18},{18,... | collective-permute-start | bytes 196616 | tf_op jit(solution)/shard_map/ppermute | solution.py:372
  11.6 5.9 %collective-permute-start.4 = (bf16[256,128]{1,0:T(8,128)(2,1)S(1)}, bf16[256,128]{1,0:T(8,128)(2,1)S(1)}, u32[]{:S(2)}, u32[]{:S(2)}) collective-permute-start(bf16[256,128]{1,0:T(8,128)(2,1)S(1)} %get-tuple-element.47), channel_id=1, source_target_pairs={{0,4},{2,6},{4,0},{6,2},{8,12},{10,14},{12,8},{14,10},{16,20},{18,... | collective-permute-start | bytes 196616 | tf_op jit(solution)/shard_map/ppermute | solution.py:372
  12.8 4.6 %collective-permute-start.5 = (bf16[256,128]{1,0:T(8,128)(2,1)S(1)}, bf16[256,128]{1,0:T(8,128)(2,1)S(1)}, u32[]{:S(2)}, u32[]{:S(2)}) collective-permute-start(bf16[256,128]{1,0:T(8,128)(2,1)S(1)} %get-tuple-element.48), channel_id=1, source_target_pairs={{0,6},{2,4},{4,2},{6,0},{8,14},{10,12},{12,10},{14,8},{16,22},{18,... | collective-permute-start | bytes 196616 | tf_op jit(solution)/shard_map/ppermute | solution.py:372
  14.1 7.5 %collective-permute-start.10 = (bf16[256,128]{1,0:T(8,128)(2,1)S(1)}, bf16[256,128]{1,0:T(8,128)(2,1)S(1)}, u32[]{:S(2)}, u32[]{:S(2)}) collective-permute-start(bf16[256,128]{1,0:T(8,128)(2,1)S(1)} %get-tuple-element.56), channel_id=1, source_target_pairs={{0,2},{2,0},{4,6},{6,4},{8,10},{10,8},{12,14},{14,12},{16,18},{18,... | collective-permute-start | bytes 196616 | tf_op jit(solution)/shard_map/ppermute | solution.py:372
  15.7 7.9 %collective-permute-start.11 = (bf16[256,128]{1,0:T(8,128)(2,1)S(1)}, bf16[256,128]{1,0:T(8,128)(2,1)S(1)}, u32[]{:S(2)}, u32[]{:S(2)}) collective-permute-start(bf16[256,128]{1,0:T(8,128)(2,1)S(1)} %get-tuple-element.57), channel_id=1, source_target_pairs={{0,4},{2,6},{4,0},{6,2},{8,12},{10,14},{12,8},{14,10},{16,20},{18,... | collective-permute-start | bytes 196616 | tf_op jit(solution)/shard_map/ppermute | solution.py:372
  16.9 6.7 %collective-permute-start.12 = (bf16[256,128]{1,0:T(8,128)(2,1)S(1)}, bf16[256,128]{1,0:T(8,128)(2,1)S(1)}, u32[]{:S(2)}, u32[]{:S(2)}) collective-permute-start(bf16[256,128]{1,0:T(8,128)(2,1)S(1)} %get-tuple-element.58), channel_id=1, source_target_pairs={{0,6},{2,4},{4,2},{6,0},{8,14},{10,12},{12,10},{14,8},{16,22},{18,... | collective-permute-start | bytes 196616 | tf_op jit(solution)/shard_map/ppermute | solution.py:372
  17.5 10.2 %collective-permute-start.8 = (bf16[3,272,128]{2,1,0:T(8,128)(2,1)S(1)}, bf16[3,272,128]{2,1,0:T(8,128)(2,1)S(1)}, u32[]{:S(2)}, u32[]{:S(2)}) collective-permute-start(bf16[3,272,128]{2,1,0:T(8,128)(2,1)S(1)} %get-tuple-element.54), channel_id=1, source_target_pairs={{8,16},{10,18},{12,20},{14,22},{16,8},{18,10},{20,12},{22,14},{9,1... | collective-permute-start | bytes 626696 | tf_op jit(solution)/shard_map/ppermute | solution.py:377
  20.7 7.0 %collective-permute-start.9 = (bf16[3,272,128]{2,1,0:T(8,128)(2,1)S(1)}, bf16[3,272,128]{2,1,0:T(8,128)(2,1)S(1)}, u32[]{:S(2)}, u32[]{:S(2)}) collective-permute-start(bf16[3,272,128]{2,1,0:T(8,128)(2,1)S(1)} %get-tuple-element.55), channel_id=1, source_target_pairs={{0,8},{2,10},{4,12},{6,14},{8,0},{10,2},{12,4},{14,6},{16,24},{18,... | collective-permute-start | bytes 626696 | tf_op jit(solution)/shard_map/ppermute | solution.py:377
  21.5 13.7 %collective-permute-start.15 = (bf16[3,256,128]{2,1,0:T(8,128)(2,1)S(1)}, bf16[3,256,128]{2,1,0:T(8,128)(2,1)S(1)}, u32[]{:S(2)}, u32[]{:S(2)}) collective-permute-start(bf16[3,256,128]{2,1,0:T(8,128)(2,1)S(1)} %get-tuple-element.65), channel_id=1, source_target_pairs={{8,16},{10,18},{12,20},{14,22},{16,8},{18,10},{20,12},{22,14},{9,1... | collective-permute-start | bytes 589832 | tf_op jit(solution)/shard_map/ppermute | solution.py:377
  27.7 7.6 %collective-permute-start.16 = (bf16[3,256,128]{2,1,0:T(8,128)(2,1)S(1)}, bf16[3,256,128]{2,1,0:T(8,128)(2,1)S(1)}, u32[]{:S(2)}, u32[]{:S(2)}) collective-permute-start(bf16[3,256,128]{2,1,0:T(8,128)(2,1)S(1)} %get-tuple-element.66), channel_id=1, source_target_pairs={{0,8},{2,10},{4,12},{6,14},{8,0},{10,2},{12,4},{14,6},{16,24},{18,... | collective-permute-start | bytes 589832 | tf_op jit(solution)/shard_map/ppermute | solution.py:377
  30.4 10.6 %collective-permute-start.13 = (bf16[3,288,128]{2,1,0:T(8,128)(2,1)S(1)}, bf16[3,288,128]{2,1,0:T(8,128)(2,1)S(1)}, u32[]{:S(2)}, u32[]{:S(2)}) collective-permute-start(bf16[3,288,128]{2,1,0:T(8,128)(2,1)S(1)} %get-tuple-element.61), channel_id=1, source_target_pairs={{0,8},{2,10},{4,12},{6,14},{8,0},{10,2},{12,4},{14,6},{16,24},{18,... | collective-permute-start | bytes 663560 | tf_op jit(solution)/shard_map/ppermute | solution.py:377
  31.9 9.0 %collective-permute-start.14 = (bf16[3,288,128]{2,1,0:T(8,128)(2,1)S(1)}, bf16[3,288,128]{2,1,0:T(8,128)(2,1)S(1)}, u32[]{:S(2)}, u32[]{:S(2)}) collective-permute-start(bf16[3,288,128]{2,1,0:T(8,128)(2,1)S(1)} %get-tuple-element.62), channel_id=1, source_target_pairs={{8,16},{10,18},{12,20},{14,22},{16,8},{18,10},{20,12},{22,14},{9,1... | collective-permute-start | bytes 663560 | tf_op jit(solution)/shard_map/ppermute | solution.py:377
  37.9 10.3 %collective-permute-start.22 = (bf16[256,128]{1,0:T(8,128)(2,1)S(1)}, bf16[256,128]{1,0:T(8,128)(2,1)S(1)}, u32[]{:S(2)}, u32[]{:S(2)}) collective-permute-start(bf16[256,128]{1,0:T(8,128)(2,1)S(1)} %get-tuple-element.79), channel_id=1, source_target_pairs={{0,6},{2,4},{4,2},{6,0},{8,14},{10,12},{12,10},{14,8},{16,22},{18,... | collective-permute-start | bytes 196616 | tf_op jit(solution)/shard_map/ppermute | solution.py:372
  40.7 7.6 %collective-permute-start.21 = (bf16[256,128]{1,0:T(8,128)(2,1)S(1)}, bf16[256,128]{1,0:T(8,128)(2,1)S(1)}, u32[]{:S(2)}, u32[]{:S(2)}) collective-permute-start(bf16[256,128]{1,0:T(8,128)(2,1)S(1)} %get-tuple-element.68.refs_0_), channel_id=1, source_target_pairs={{0,4},{2,6},{4,0},{6,2},{8,12},{10,14},{12,8},{14,10},{16,20},{18,... | collective-permute-start | bytes 196616 | tf_op jit(solution)/shard_map/ppermute | solution.py:372
  41.4 4.7 %collective-permute-start.17 = (bf16[256,128]{1,0:T(8,128)(2,1)S(1)}, bf16[256,128]{1,0:T(8,128)(2,1)S(1)}, u32[]{:S(2)}, u32[]{:S(2)}) collective-permute-start(bf16[256,128]{1,0:T(8,128)(2,1)S(1)} %get-tuple-element.70), channel_id=1, source_target_pairs={{0,2},{2,0},{4,6},{6,4},{8,10},{10,8},{12,14},{14,12},{16,18},{18,... | collective-permute-start | bytes 196616 | tf_op jit(solution)/shard_map/ppermute | solution.py:372
  42.2 4.2 %collective-permute-start.18 = (bf16[256,128]{1,0:T(8,128)(2,1)S(1)}, bf16[256,128]{1,0:T(8,128)(2,1)S(1)}, u32[]{:S(2)}, u32[]{:S(2)}) collective-permute-start(bf16[256,128]{1,0:T(8,128)(2,1)S(1)} %get-tuple-element.71), channel_id=1, source_target_pairs={{0,4},{2,6},{4,0},{6,2},{8,12},{10,14},{12,8},{14,10},{16,20},{18,... | collective-permute-start | bytes 196616 | tf_op jit(solution)/shard_map/ppermute | solution.py:372
  43.4 4.1 %collective-permute-start.19 = (bf16[256,128]{1,0:T(8,128)(2,1)S(1)}, bf16[256,128]{1,0:T(8,128)(2,1)S(1)}, u32[]{:S(2)}, u32[]{:S(2)}) collective-permute-start(bf16[256,128]{1,0:T(8,128)(2,1)S(1)} %get-tuple-element.72), channel_id=1, source_target_pairs={{0,6},{2,4},{4,2},{6,0},{8,14},{10,12},{12,10},{14,8},{16,22},{18,... | collective-permute-start | bytes 196616 | tf_op jit(solution)/shard_map/ppermute | solution.py:372
  46.2 2.1 %collective-permute-start.20 = (bf16[256,128]{1,0:T(8,128)(2,1)S(1)}, bf16[256,128]{1,0:T(8,128)(2,1)S(1)}, u32[]{:S(2)}, u32[]{:S(2)}) collective-permute-start(bf16[256,128]{1,0:T(8,128)(2,1)S(1)} %get-tuple-element.78), channel_id=1, source_target_pairs={{0,2},{2,0},{4,6},{6,4},{8,10},{10,8},{12,14},{14,12},{16,18},{18,... | collective-permute-start | bytes 196616 | tf_op jit(solution)/shard_map/ppermute | solution.py:372

commit v22 on v21

--- a/solution.py
+++ b/solution.py
@@ -102,15 +102,14 @@
         pieces[k][...] = full[:, pl.ds(pl.multiple_of((mine ^ k) * width, width), width)]
 
 
-def halo_kernel(ids_at, *refs):
-    pieces, id_packs, outs = refs[:GROUP], refs[GROUP : 2 * GROUP], refs[-2:]
+def halo_kernel(seconds, ids_at, *refs):
+    pieces, id_packs, outs = refs[:GROUP], refs[GROUP : 2 * GROUP], refs[-len(seconds) :]
     rows = outs[0].shape[1] - (ID_ROWS if ids_at else 0)
     mine = place()
-    odd = lax.rem(plane(), 2)
-    for k in range(GROUP):
-        block = mine ^ k
-        for out, skip in zip(outs, ((GROUP - RADIUS) * (1 - odd), (GROUP - RADIUS) * odd)):
-            spot = block - skip
+    for out, second in zip(outs, seconds):
+        skip = (GROUP - RADIUS) * lax.rem(plane() + 1 + second, 2)
+        for k in range(GROUP):
+            spot = (mine ^ k) - skip
 
             @pl.when((spot >= 0) & (spot < RADIUS))
             def _():
@@ -420,20 +419,20 @@
             name="project",
         )(*operands, *after)
 
-    def halo(pieces, id_packs, *after):
+    def halo(seconds, pieces, id_packs, *after):
         edge = shape((RADIUS, rows + (ID_ROWS if id_packs else 0), width), bf16)
         sent = call(
-            functools.partial(halo_kernel, 2 * rows if id_packs else 0),
-            [edge, edge],
+            functools.partial(halo_kernel, seconds, 2 * rows if id_packs else 0),
+            [edge] * len(seconds),
             ins=[VMEM] * (GROUP + len(id_packs)) + [ANY] * len(after),
-            moved=10 * rows * width * 2,
+            moved=5 * len(seconds) * rows * width * 2,
             name="halo",
         )(*pieces, *id_packs, *after)
-        return [crossed(sent[i], i) for i in range(2)]
+        return [crossed(x, second) for x, second in zip(sent, seconds)]
 
     queries = traded(project(HEAD**-0.5, query_part, other_audio, query_rest, after=packs[1:3]))
     keys = project(1.0, key_part, other_video, key_rest, after=())
-    query_edges = halo(queries, packs, keys[0])
+    query_edges = halo((0, 1), queries, packs, keys[0])
     keys = traded(keys)
 
     inside, around = GROUP * rows, 2 * RADIUS * rows
@@ -448,7 +447,7 @@
         exps=2 * GROUP * rows * inside,
         name="rows",
     )(*packs, *queries, *keys)
-    audio_edges = [halo(packs, [], *[peaks])[0], halo(packs, [], *[])[1]]
+    audio_edges = halo((0,), packs, [], peaks) + halo((1,), packs, [])
     back = shape((RADIUS, rows + rows // width * STAT_ROWS, width), bf16)
     lent_a, lent_b, edge_turned = call(
         lend_kernel,

time: 49.4 us -> 48.1 us (0.974)
  Pallas kernels: 18.1 us -> 16.7 us
  waiting for transfers between devices: 3.22 us -> 3.86 us
  starting transfers between devices: 26.9 us -> 26.3 us
    pallas_call x3, Pallas kernels: 1.57 us -> 0.17 us  [halo(): call(functools.partial(halo_kernel, seconds, 2 * rows if id_packs else 0)...]
    ppermute x6, waiting for transfers between devices: 0.02 us -> 0.65 us  [crossed(): lax.ppermute(sent, 'tm', [(p * GROUP + i, q * GROUP + i) for p, q in pair...]
    ppermute x6, starting transfers between devices: 10.3 us -> 9.69 us  [crossed(): lax.ppermute(sent, 'tm', [(p * GROUP + i, q * GROUP + i) for p, q in pair...]
  transfers between devices with their start and end apart: 23 -> 23, of which waited for: 3 -> 4; matrix products, arithmetic and copies ran while one was open for 0% -> 0% of each run, Pallas kernels for 35% -> 33%
where the time goes in v22:
time: 48.1 us; the launch traced here: 47.9 us
  starting transfers between devices  26.3 us (55%)
  Pallas kernels  16.7 us (35%)
  waiting for transfers between devices  3.86 us (8%)
  between operations  1.01 us (2%)
    ppermute x15, starting transfers between devices, traded(): lax.ppermute(pieces[k], 'tm', pairs(k))  15.1 us
    ppermute x6, starting transfers between devices, crossed(): lax.ppermute(sent, 'tm', [(p * GROUP + i, q * GROUP + i) for p, q in pair...  9.69 us
    pallas_call x1, Pallas kernels, local(): call(rows_kernel, [shape((GROUP, rows, width), f32), shape((GROUP, 2, row...  3.3 us
    ppermute x15, waiting for transfers between devices, traded(): lax.ppermute(pieces[k], 'tm', pairs(k))  2.77 us
    pallas_call x1, Pallas kernels, local(): call(functools.partial(columns_kernel, far), [piece] * len(far) + shared,...  2.65 us
    pallas_call x1, Pallas kernels, local(): call(lend_kernel, [back, back, shape((2 * width, around), bf16)], [pltpu....  2.64 us
    pallas_call x1, Pallas kernels, local(): call(functools.partial(columns_kernel, near), [piece] * len(near), ins=[V...  2.26 us
    pallas_call x1, Pallas kernels, local(): call(prepare_kernel, [part, part, square, square], [pltpu.VMEM((rows, hal...  1.78 us
  transfers between devices with their start and end apart: 23, of which 4 were waited for; matrix products, arithmetic and copies ran while one was open for 0% of the time, Pallas kernels for 33%

profile of v22, /device:TPU:9, one launch (start us, length us, event | category | flops | bytes accessed | tf_op | source)
XLA Modules:
  0.0 47.9 jit_solution(13115313651913257228)
XLA Ops:
  0.6 1.3 %collective-permute-start.1 = (bf16[256,512]{1,0:T(8,128)(2,1)}, bf16[256,512]{1,0:T(8,128)(2,1)S(1)}, u32[]{:S(2)}, u32[]{:S(2)}) collective-permute-start(bf16[256,512]{1,0:T(8,128)(2,1)} %audio.3), channel_id=1, source_target_pairs={{0,1},{1,0},{2,3},{3,2},{4,5},{5,4},{6,7},{7,6},{8,9},{9,8},{10,11... | collective-permute-start | bytes 786440 | tf_op jit(solution)/shard_map/ppermute | solution.py:367
  1.9 0.2 collective-permute-start.7
  2.2 1.2 %split.1 = (bf16[528,128]{1,0:T(8,128)(2,1)S(1)}, bf16[528,128]{1,0:T(8,128)(2,1)S(1)}, bf16[528,128]{1,0:T(8,128)(2,1)S(1)}, bf16[528,128]{1,0:T(8,128)(2,1)S(1)}) custom-call(bf16[256,512]{1,0:T(8,128)(2,1)} %audio.3, bf16[256,512]{1,0:T(8,128)(2,1)} %video.3, s32[2,128]{1,0:T(2,128)} %bitcast.1), custom_call_target="tpu_custom_call" | custom-call | bytes 1048576 | tf_op jit(solution)/shard_map/split/pallas_call | solution.py:389
  3.3 1.3 %collective-permute-start = (bf16[528,128]{1,0:T(8,128)(2,1)S(1)}, bf16[528,128]{1,0:T(8,128)(2,1)S(1)}, u32[]{:S(2)}, u32[]{:S(2)}) collective-permute-start(bf16[528,128]{1,0:T(8,128)(2,1)S(1)} %get-tuple-element.39), channel_id=1, source_target_pairs={{0,2},{2,0},{4,6},{6,4},{8,10},{10,8},{12,14},{14,12},{16,18},{18,... | collective-permute-start | bytes 405512 | tf_op jit(solution)/shard_map/ppermute | solution.py:371
  4.6 1.2 %collective-permute-start.2 = (bf16[528,128]{1,0:T(8,128)(2,1)S(1)}, bf16[528,128]{1,0:T(8,128)(2,1)S(1)}, u32[]{:S(2)}, u32[]{:S(2)}) collective-permute-start(bf16[528,128]{1,0:T(8,128)(2,1)S(1)} %get-tuple-element.42), channel_id=1, source_target_pairs={{0,4},{2,6},{4,0},{6,2},{8,12},{10,14},{12,8},{14,10},{16,20},{18,... | collective-permute-start | bytes 405512 | tf_op jit(solution)/shard_map/ppermute | solution.py:371
  5.9 0.5 %collective-permute-start.6 = (bf16[528,128]{1,0:T(8,128)(2,1)S(1)}, bf16[528,128]{1,0:T(8,128)(2,1)S(1)}, u32[]{:S(2)}, u32[]{:S(2)}) collective-permute-start(bf16[528,128]{1,0:T(8,128)(2,1)S(1)} %get-tuple-element.48), channel_id=1, source_target_pairs={{0,6},{2,4},{4,2},{6,0},{8,14},{10,12},{12,10},{14,8},{16,22},{18,... | collective-permute-start | bytes 405512 | tf_op jit(solution)/shard_map/ppermute | solution.py:371
  6.3 0.0 collective-permute-done.refs_0_.refs_5_.refs_1_
  6.3 1.8 %prepare.1 = (f32[256,512]{1,0:T(8,128)S(1)}, f32[256,512]{1,0:T(8,128)S(1)}, bf16[512,512]{1,0:T(8,128)(2,1)S(1)}, bf16[512,512]{1,0:T(8,128)(2,1)S(1)}) custom-call(bf16[256,512]{1,0:T(8,128)(2,1)} %audio.3, bf16[256,512]{1,0:T(8,128)(2,1)} %video.3, bf16[1024,512]{1,0:T(8,128)(2,1)} %query.1, bf16[1024,512]{1,0:T(8,128)(2,1)} %key.1, ...), custom_call_target="tpu_custom_call" | custom-call | flops 268435456 | bytes 4194304 | tf_op jit(solution)/shard_map/prepare/pallas_call | solution.py:399
  8.1 1.7 %collective-permute-done.2.refs_1_.refs_6_.refs_2_ = bf16[528,128]{1,0:T(8,128)(2,1)S(1)} collective-permute-done((bf16[528,128]{1,0:T(8,128)(2,1)S(1)}, bf16[528,128]{1,0:T(8,128)(2,1)S(1)}, u32[]{:S(2)}, u32[]{:S(2)}) %collective-permute-start.2) | collective-permute-done | bytes 135200 | tf_op jit(solution)/shard_map/ppermute | solution.py:371
  9.8 0.0 collective-permute-done.1.other
  9.8 0.4 project.2
  10.2 1.4 %collective-permute-start.3 = (bf16[256,128]{1,0:T(8,128)(2,1)S(1)}, bf16[256,128]{1,0:T(8,128)(2,1)S(1)}, u32[]{:S(2)}, u32[]{:S(2)}) collective-permute-start(bf16[256,128]{1,0:T(8,128)(2,1)S(1)} %get-tuple-element.44), channel_id=1, source_target_pairs={{0,2},{2,0},{4,6},{6,4},{8,10},{10,8},{12,14},{14,12},{16,18},{18,... | collective-permute-start | bytes 196616 | tf_op jit(solution)/shard_map/ppermute | solution.py:371
  11.6 1.2 %collective-permute-start.4 = (bf16[256,128]{1,0:T(8,128)(2,1)S(1)}, bf16[256,128]{1,0:T(8,128)(2,1)S(1)}, u32[]{:S(2)}, u32[]{:S(2)}) collective-permute-start(bf16[256,128]{1,0:T(8,128)(2,1)S(1)} %get-tuple-element.45), channel_id=1, source_target_pairs={{0,4},{2,6},{4,0},{6,2},{8,12},{10,14},{12,8},{14,10},{16,20},{18,... | collective-permute-start | bytes 196616 | tf_op jit(solution)/shard_map/ppermute | solution.py:371
  12.8 0.5 collective-permute-start.5
  13.3 0.4 collective-permute-done.7.other
  13.7 0.4 project.3
  14.1 1.6 %collective-permute-start.10 = (bf16[256,128]{1,0:T(8,128)(2,1)S(1)}, bf16[256,128]{1,0:T(8,128)(2,1)S(1)}, u32[]{:S(2)}, u32[]{:S(2)}) collective-permute-start(bf16[256,128]{1,0:T(8,128)(2,1)S(1)} %get-tuple-element.54), channel_id=1, source_target_pairs={{0,2},{2,0},{4,6},{6,4},{8,10},{10,8},{12,14},{14,12},{16,18},{18,... | collective-permute-start | bytes 196616 | tf_op jit(solution)/shard_map/ppermute | solution.py:371
  15.7 0.0 collective-permute-done.6.refs_7_.refs_3_
  15.7 1.2 %collective-permute-start.11 = (bf16[256,128]{1,0:T(8,128)(2,1)S(1)}, bf16[256,128]{1,0:T(8,128)(2,1)S(1)}, u32[]{:S(2)}, u32[]{:S(2)}) collective-permute-start(bf16[256,128]{1,0:T(8,128)(2,1)S(1)} %get-tuple-element.55), channel_id=1, source_target_pairs={{0,4},{2,6},{4,0},{6,2},{8,12},{10,14},{12,8},{14,10},{16,20},{18,... | collective-permute-start | bytes 196616 | tf_op jit(solution)/shard_map/ppermute | solution.py:371
  16.9 0.0 collective-permute-done.3.refs_1_.refs_5_
  16.9 0.5 %collective-permute-start.12 = (bf16[256,128]{1,0:T(8,128)(2,1)S(1)}, bf16[256,128]{1,0:T(8,128)(2,1)S(1)}, u32[]{:S(2)}, u32[]{:S(2)}) collective-permute-start(bf16[256,128]{1,0:T(8,128)(2,1)S(1)} %get-tuple-element.56), channel_id=1, source_target_pairs={{0,6},{2,4},{4,2},{6,0},{8,14},{10,12},{12,10},{14,8},{16,22},{18,... | collective-permute-start | bytes 196616 | tf_op jit(solution)/shard_map/ppermute | solution.py:371
  17.4 0.0 collective-permute-done.4.refs_2_.refs_6_
  17.4 0.0 collective-permute-done.5.refs_3_.refs_7_
  17.4 0.1 halo.3
  17.5 3.2 %collective-permute-start.8 = (bf16[3,272,128]{2,1,0:T(8,128)(2,1)S(1)}, bf16[3,272,128]{2,1,0:T(8,128)(2,1)S(1)}, u32[]{:S(2)}, u32[]{:S(2)}) collective-permute-start(bf16[3,272,128]{2,1,0:T(8,128)(2,1)S(1)} %get-tuple-element.52), channel_id=1, source_target_pairs={{8,16},{10,18},{12,20},{14,22},{16,8},{18,10},{20,12},{22,14},{9,1... | collective-permute-start | bytes 626696 | tf_op jit(solution)/shard_map/ppermute | solution.py:376
  20.7 0.1 collective-permute-start.9
  20.8 0.1 halo.4
  20.8 0.0 collective-permute-done.10.refs_9_
  20.9 2.1 %collective-permute-start.15 = (bf16[3,256,128]{2,1,0:T(8,128)(2,1)S(1)}, bf16[3,256,128]{2,1,0:T(8,128)(2,1)S(1)}, u32[]{:S(2)}, u32[]{:S(2)}) collective-permute-start(bf16[3,256,128]{2,1,0:T(8,128)(2,1)S(1)} %halo.4), channel_id=1, source_target_pairs={{8,16},{10,18},{12,20},{14,22},{16,8},{18,10},{20,12},{22,14},{9,1... | collective-permute-start | bytes 589832 | tf_op jit(solution)/shard_map/ppermute | solution.py:376
  22.9 0.0 collective-permute-done.11.refs_10_
  23.0 0.0 collective-permute-done.12.refs_11_
  23.0 3.3 %rows.1 = (f32[4,256,128]{2,1,0:T(8,128)S(1)}, f32[4,2,256,128]{3,2,1,0:T(8,128)S(1)}, bf16[256,1024]{1,0:T(8,128)(2,1)S(1)}, bf16[1024,256]{1,0:T(8,128)(2,1)S(1)}) custom-call(bf16[528,128]{1,0:T(8,128)(2,1)S(1)} %get-tuple-element.47.refs_4_.refs_0_, bf16[528,128]{1,0:T(8,128)(2,1)S(1)} %collective-permute-done.refs_0_.refs_5_.refs_1_, ...), custom_call_target="tpu_custom_call" | custom-call | flops 2147483648 | bytes 2097152 | tf_op jit(solution)/shard_map/rows/pallas_call | solution.py:441
  26.3 0.1 halo.5
  26.3 0.1 collective-permute-start.16
  26.4 0.0 collective-permute-done.8.edge_b
  26.4 0.6 %collective-permute-done.9.edge_a = bf16[3,272,128]{2,1,0:T(8,128)(2,1)S(1)} collective-permute-done((bf16[3,272,128]{2,1,0:T(8,128)(2,1)S(1)}, bf16[3,272,128]{2,1,0:T(8,128)(2,1)S(1)}, u32[]{:S(2)}, u32[]{:S(2)}) %collective-permute-start.9) | collective-permute-done | bytes 208928 | tf_op jit(solution)/shard_map/ppermute | solution.py:376
  27.1 2.6 %lend.1 = (bf16[3,288,128]{2,1,0:T(8,128)(2,1)S(1)}, bf16[3,288,128]{2,1,0:T(8,128)(2,1)S(1)}, bf16[256,1536]{1,0:T(8,128)(2,1)S(1)}) custom-call(bf16[3,272,128]{2,1,0:T(8,128)(2,1)S(1)} %collective-permute-done.8.edge_b, bf16[3,272,128]{2,1,0:T(8,128)(2,1)S(1)} %collective-permute-done.9.edge_a, bf16[256,1024]{1,0:T(8,128)(2,1)S(1)} %get-tuple-element.57.plane_turned, ...), custom_call_target="tpu_custom_call" | custom-call | flops 4831838208 | bytes 3145728 | tf_op jit(solution)/shard_map/lend/pallas_call | solution.py:452
  29.7 0.9 %collective-permute-start.13 = (bf16[3,288,128]{2,1,0:T(8,128)(2,1)S(1)}, bf16[3,288,128]{2,1,0:T(8,128)(2,1)S(1)}, u32[]{:S(2)}, u32[]{:S(2)}) collective-permute-start(bf16[3,288,128]{2,1,0:T(8,128)(2,1)S(1)} %get-tuple-element.59), channel_id=1, source_target_pairs={{0,8},{2,10},{4,12},{6,14},{8,0},{10,2},{12,4},{14,6},{16,24},{18,... | collective-permute-start | bytes 663560 | tf_op jit(solution)/shard_map/ppermute | solution.py:376
  30.6 3.4 %collective-permute-start.14 = (bf16[3,288,128]{2,1,0:T(8,128)(2,1)S(1)}, bf16[3,288,128]{2,1,0:T(8,128)(2,1)S(1)}, u32[]{:S(2)}, u32[]{:S(2)}) collective-permute-start(bf16[3,288,128]{2,1,0:T(8,128)(2,1)S(1)} %get-tuple-element.60), channel_id=1, source_target_pairs={{8,16},{10,18},{12,20},{14,22},{16,8},{18,10},{20,12},{22,14},{9,1... | collective-permute-start | bytes 663560 | tf_op jit(solution)/shard_map/ppermute | solution.py:376
  34.0 0.0 collective-permute-done.15.refs_12_
  34.0 0.0 collective-permute-done.16.refs_13_
  34.0 2.6 %columns.2 = (bf16[256,128]{1,0:T(8,128)(2,1)S(1)}, bf16[256,128]{1,0:T(8,128)(2,1)S(1)}, bf16[256,1024]{1,0:T(8,128)(2,1)S(1)}, bf16[1024,256]{1,0:T(8,128)(2,1...) custom-call(bf16[528,128]{1,0:T(8,128)(2,1)S(1)} %get-tuple-element.47.refs_4_.refs_0_, ...), custom_call_target="tpu_custom_call" | custom-call | flops 1879048192 | bytes 1572864 | tf_op jit(solution)/shard_map/columns/pallas_call | solution.py:471
  36.6 2.7 %collective-permute-start.22 = (bf16[256,128]{1,0:T(8,128)(2,1)S(1)}, bf16[256,128]{1,0:T(8,128)(2,1)S(1)}, u32[]{:S(2)}, u32[]{:S(2)}) collective-permute-start(bf16[256,128]{1,0:T(8,128)(2,1)S(1)} %get-tuple-element.75), channel_id=1, source_target_pairs={{0,6},{2,4},{4,2},{6,0},{8,14},{10,12},{12,10},{14,8},{16,22},{18,... | collective-permute-start | bytes 196616 | tf_op jit(solution)/shard_map/ppermute | solution.py:371
  39.4 0.3 collective-permute-start.21
  39.6 0.0 collective-permute-done.13.back_a
  39.6 0.0 collective-permute-done.14.back_b
  39.6 0.5 %merge.1 = (bf16[256,128]{1,0:T(8,128)(2,1)S(1)}, bf16[256,128]{1,0:T(8,128)(2,1)S(1)}, bf16[256,128]{1,0:T(8,128)(2,1)S(1)}, bf16[256,128]{1,0:T(8,128)(2,1)S(1)}) custom-call(bf16[3,288,128]{2,1,0:T(8,128)(2,1)S(1)} %collective-permute-done.13.back_a, bf16[3,288,128]{2,1,0:T(8,128)(2,1)S(1)} %collective-permute-done.14.back_b, ...), custom_call_target="tpu_custom_call" | custom-call | bytes 2097152 | tf_op jit(solution)/shard_map/merge/pallas_call | solution.py:474
  40.1 0.7 %collective-permute-start.17 = (bf16[256,128]{1,0:T(8,128)(2,1)S(1)}, bf16[256,128]{1,0:T(8,128)(2,1)S(1)}, u32[]{:S(2)}, u32[]{:S(2)}) collective-permute-start(bf16[256,128]{1,0:T(8,128)(2,1)S(1)} %get-tuple-element.66), channel_id=1, source_target_pairs={{0,2},{2,0},{4,6},{6,4},{8,10},{10,8},{12,14},{14,12},{16,18},{18,... | collective-permute-start | bytes 196616 | tf_op jit(solution)/shard_map/ppermute | solution.py:371
  40.9 1.2 %collective-permute-start.18 = (bf16[256,128]{1,0:T(8,128)(2,1)S(1)}, bf16[256,128]{1,0:T(8,128)(2,1)S(1)}, u32[]{:S(2)}, u32[]{:S(2)}) collective-permute-start(bf16[256,128]{1,0:T(8,128)(2,1)S(1)} %get-tuple-element.67), channel_id=1, source_target_pairs={{0,4},{2,6},{4,0},{6,2},{8,12},{10,14},{12,8},{14,10},{16,20},{18,... | collective-permute-start | bytes 196616 | tf_op jit(solution)/shard_map/ppermute | solution.py:371
  42.1 0.5 %collective-permute-start.19 = (bf16[256,128]{1,0:T(8,128)(2,1)S(1)}, bf16[256,128]{1,0:T(8,128)(2,1)S(1)}, u32[]{:S(2)}, u32[]{:S(2)}) collective-permute-start(bf16[256,128]{1,0:T(8,128)(2,1)S(1)} %get-tuple-element.68), channel_id=1, source_target_pairs={{0,6},{2,4},{4,2},{6,0},{8,14},{10,12},{12,10},{14,8},{16,22},{18,... | collective-permute-start | bytes 196616 | tf_op jit(solution)/shard_map/ppermute | solution.py:371
  42.6 2.3 %columns.3 = (bf16[256,128]{1,0:T(8,128)(2,1)S(1)}, bf16[256,128]{1,0:T(8,128)(2,1)S(1)}) custom-call(bf16[256,1536]{1,0:T(8,128)(2,1)S(1)} %get-tuple-element.63.refs_14_.refs_0_, bf16[256,1024]{1,0:T(8,128)(2,1)S(1)} %get-tuple-element.69.refs_1_, bf16[1024,256]{1,0:T(8,128)(2,1)S(1)} %get-tuple-element.70.refs_2_, ...), custom_call_target="tpu_custom_call" | custom-call | flops 1879048192 | bytes 1572864 | tf_op jit(solution)/shard_map/columns/pallas_call | solution.py:484
  44.9 0.0 collective-permute-done.17.refs_1_
  44.9 0.2 collective-permute-start.20
  45.1 0.0 collective-permute-done.18.refs_2_
  45.1 1.1 %collective-permute-done.19.refs_3_ = bf16[256,128]{1,0:T(8,128)(2,1)S(1)} collective-permute-done((bf16[256,128]{1,0:T(8,128)(2,1)S(1)}, bf16[256,128]{1,0:T(8,128)(2,1)S(1)}, u32[]{:S(2)}, u32[]{:S(2)}) %collective-permute-start.19) | collective-permute-done | bytes 65568 | tf_op jit(solution)/shard_map/ppermute | solution.py:371
  46.2 0.7 %join.2 = bf16[256,512]{1,0:T(8,128)(2,1)} custom-call(bf16[256,128]{1,0:T(8,128)(2,1)S(1)} %get-tuple-element.65.refs_0_.refs_5_, bf16[256,128]{1,0:T(8,128)(2,1)S(1)} %collective-permute-done.17.refs_1_, bf16[256,128]{1,0:T(8,128)(2,1)S(1)} %collective-permute-done.18.refs_2_, bf16[256,128]{1,0:T(8,128)(2,1)S(1)} %collective-permute-done.19.refs_3_), custom_call_target="tpu_custom_call" | custom-call | bytes 524288 | tf_op jit(solution)/shard_map/join/pallas_call | solution.py:493
  46.9 0.0 collective-permute-done.22.refs_3_
  46.9 0.0 collective-permute-done.21.refs_2_
  46.9 0.0 collective-permute-done.20.refs_1_
  47.0 0.7 %join.3 = bf16[256,512]{1,0:T(8,128)(2,1)} custom-call(bf16[256,128]{1,0:T(8,128)(2,1)S(1)} %get-tuple-element.73.refs_0_, bf16[256,128]{1,0:T(8,128)(2,1)S(1)} %collective-permute-done.20.refs_1_, bf16[256,128]{1,0:T(8,128)(2,1)S(1)} %collective-permute-done.21.refs_2_, bf16[256,128]{1,0:T(8,128)(2,1)S(1)} %collective-permute-done.22.refs_3_), custom_call_target="tpu_custom_call" | custom-call | bytes 524288 | tf_op jit(solution)/shard_map/join/pallas_call | solution.py:493
Async XLA Ops:
  0.6 9.2 %collective-permute-start.1 = (bf16[256,512]{1,0:T(8,128)(2,1)}, bf16[256,512]{1,0:T(8,128)(2,1)S(1)}, u32[]{:S(2)}, u32[]{:S(2)}) collective-permute-start(bf16[256,512]{1,0:T(8,128)(2,1)} %audio.3), channel_id=1, source_target_pairs={{0,1},{1,0},{2,3},{3,2},{4,5},{5,4},{6,7},{7,6},{8,9},{9,8},{10,11... | collective-permute-start | bytes 786440 | tf_op jit(solution)/shard_map/ppermute | solution.py:367
  1.9 11.8 %collective-permute-start.7 = (bf16[256,512]{1,0:T(8,128)(2,1)}, bf16[256,512]{1,0:T(8,128)(2,1)S(1)}, u32[]{:S(2)}, u32[]{:S(2)}) collective-permute-start(bf16[256,512]{1,0:T(8,128)(2,1)} %video.3), channel_id=1, source_target_pairs={{0,1},{1,0},{2,3},{3,2},{4,5},{5,4},{6,7},{7,6},{8,9},{9,8},{10,11... | collective-permute-start | bytes 786440 | tf_op jit(solution)/shard_map/ppermute | solution.py:367
  3.3 3.0 %collective-permute-start = (bf16[528,128]{1,0:T(8,128)(2,1)S(1)}, bf16[528,128]{1,0:T(8,128)(2,1)S(1)}, u32[]{:S(2)}, u32[]{:S(2)}) collective-permute-start(bf16[528,128]{1,0:T(8,128)(2,1)S(1)} %get-tuple-element.39), channel_id=1, source_target_pairs={{0,2},{2,0},{4,6},{6,4},{8,10},{10,8},{12,14},{14,12},{16,18},{18,... | collective-permute-start | bytes 405512 | tf_op jit(solution)/shard_map/ppermute | solution.py:371
  4.6 5.2 %collective-permute-start.2 = (bf16[528,128]{1,0:T(8,128)(2,1)S(1)}, bf16[528,128]{1,0:T(8,128)(2,1)S(1)}, u32[]{:S(2)}, u32[]{:S(2)}) collective-permute-start(bf16[528,128]{1,0:T(8,128)(2,1)S(1)} %get-tuple-element.42), channel_id=1, source_target_pairs={{0,4},{2,6},{4,0},{6,2},{8,12},{10,14},{12,8},{14,10},{16,20},{18,... | collective-permute-start | bytes 405512 | tf_op jit(solution)/shard_map/ppermute | solution.py:371
  5.9 9.8 %collective-permute-start.6 = (bf16[528,128]{1,0:T(8,128)(2,1)S(1)}, bf16[528,128]{1,0:T(8,128)(2,1)S(1)}, u32[]{:S(2)}, u32[]{:S(2)}) collective-permute-start(bf16[528,128]{1,0:T(8,128)(2,1)S(1)} %get-tuple-element.48), channel_id=1, source_target_pairs={{0,6},{2,4},{4,2},{6,0},{8,14},{10,12},{12,10},{14,8},{16,22},{18,... | collective-permute-start | bytes 405512 | tf_op jit(solution)/shard_map/ppermute | solution.py:371
  10.2 6.7 %collective-permute-start.3 = (bf16[256,128]{1,0:T(8,128)(2,1)S(1)}, bf16[256,128]{1,0:T(8,128)(2,1)S(1)}, u32[]{:S(2)}, u32[]{:S(2)}) collective-permute-start(bf16[256,128]{1,0:T(8,128)(2,1)S(1)} %get-tuple-element.44), channel_id=1, source_target_pairs={{0,2},{2,0},{4,6},{6,4},{8,10},{10,8},{12,14},{14,12},{16,18},{18,... | collective-permute-start | bytes 196616 | tf_op jit(solution)/shard_map/ppermute | solution.py:371
  11.6 5.9 %collective-permute-start.4 = (bf16[256,128]{1,0:T(8,128)(2,1)S(1)}, bf16[256,128]{1,0:T(8,128)(2,1)S(1)}, u32[]{:S(2)}, u32[]{:S(2)}) collective-permute-start(bf16[256,128]{1,0:T(8,128)(2,1)S(1)} %get-tuple-element.45), channel_id=1, source_target_pairs={{0,4},{2,6},{4,0},{6,2},{8,12},{10,14},{12,8},{14,10},{16,20},{18,... | collective-permute-start | bytes 196616 | tf_op jit(solution)/shard_map/ppermute | solution.py:371
  12.8 4.6 %collective-permute-start.5 = (bf16[256,128]{1,0:T(8,128)(2,1)S(1)}, bf16[256,128]{1,0:T(8,128)(2,1)S(1)}, u32[]{:S(2)}, u32[]{:S(2)}) collective-permute-start(bf16[256,128]{1,0:T(8,128)(2,1)S(1)} %get-tuple-element.46), channel_id=1, source_target_pairs={{0,6},{2,4},{4,2},{6,0},{8,14},{10,12},{12,10},{14,8},{16,22},{18,... | collective-permute-start | bytes 196616 | tf_op jit(solution)/shard_map/ppermute | solution.py:371
  14.1 6.8 %collective-permute-start.10 = (bf16[256,128]{1,0:T(8,128)(2,1)S(1)}, bf16[256,128]{1,0:T(8,128)(2,1)S(1)}, u32[]{:S(2)}, u32[]{:S(2)}) collective-permute-start(bf16[256,128]{1,0:T(8,128)(2,1)S(1)} %get-tuple-element.54), channel_id=1, source_target_pairs={{0,2},{2,0},{4,6},{6,4},{8,10},{10,8},{12,14},{14,12},{16,18},{18,... | collective-permute-start | bytes 196616 | tf_op jit(solution)/shard_map/ppermute | solution.py:371
  15.7 7.2 %collective-permute-start.11 = (bf16[256,128]{1,0:T(8,128)(2,1)S(1)}, bf16[256,128]{1,0:T(8,128)(2,1)S(1)}, u32[]{:S(2)}, u32[]{:S(2)}) collective-permute-start(bf16[256,128]{1,0:T(8,128)(2,1)S(1)} %get-tuple-element.55), channel_id=1, source_target_pairs={{0,4},{2,6},{4,0},{6,2},{8,12},{10,14},{12,8},{14,10},{16,20},{18,... | collective-permute-start | bytes 196616 | tf_op jit(solution)/shard_map/ppermute | solution.py:371
  16.9 6.0 %collective-permute-start.12 = (bf16[256,128]{1,0:T(8,128)(2,1)S(1)}, bf16[256,128]{1,0:T(8,128)(2,1)S(1)}, u32[]{:S(2)}, u32[]{:S(2)}) collective-permute-start(bf16[256,128]{1,0:T(8,128)(2,1)S(1)} %get-tuple-element.56), channel_id=1, source_target_pairs={{0,6},{2,4},{4,2},{6,0},{8,14},{10,12},{12,10},{14,8},{16,22},{18,... | collective-permute-start | bytes 196616 | tf_op jit(solution)/shard_map/ppermute | solution.py:371
  17.5 8.9 %collective-permute-start.8 = (bf16[3,272,128]{2,1,0:T(8,128)(2,1)S(1)}, bf16[3,272,128]{2,1,0:T(8,128)(2,1)S(1)}, u32[]{:S(2)}, u32[]{:S(2)}) collective-permute-start(bf16[3,272,128]{2,1,0:T(8,128)(2,1)S(1)} %get-tuple-element.52), channel_id=1, source_target_pairs={{8,16},{10,18},{12,20},{14,22},{16,8},{18,10},{20,12},{22,14},{9,1... | collective-permute-start | bytes 626696 | tf_op jit(solution)/shard_map/ppermute | solution.py:376
  20.7 6.4 %collective-permute-start.9 = (bf16[3,272,128]{2,1,0:T(8,128)(2,1)S(1)}, bf16[3,272,128]{2,1,0:T(8,128)(2,1)S(1)}, u32[]{:S(2)}, u32[]{:S(2)}) collective-permute-start(bf16[3,272,128]{2,1,0:T(8,128)(2,1)S(1)} %get-tuple-element.53), channel_id=1, source_target_pairs={{0,8},{2,10},{4,12},{6,14},{8,0},{10,2},{12,4},{14,6},{16,24},{18,... | collective-permute-start | bytes 626696 | tf_op jit(solution)/shard_map/ppermute | solution.py:376
  20.9 13.1 %collective-permute-start.15 = (bf16[3,256,128]{2,1,0:T(8,128)(2,1)S(1)}, bf16[3,256,128]{2,1,0:T(8,128)(2,1)S(1)}, u32[]{:S(2)}, u32[]{:S(2)}) collective-permute-start(bf16[3,256,128]{2,1,0:T(8,128)(2,1)S(1)} %halo.4), channel_id=1, source_target_pairs={{8,16},{10,18},{12,20},{14,22},{16,8},{18,10},{20,12},{22,14},{9,1... | collective-permute-start | bytes 589832 | tf_op jit(solution)/shard_map/ppermute | solution.py:376
  26.3 7.6 %collective-permute-start.16 = (bf16[3,256,128]{2,1,0:T(8,128)(2,1)S(1)}, bf16[3,256,128]{2,1,0:T(8,128)(2,1)S(1)}, u32[]{:S(2)}, u32[]{:S(2)}) collective-permute-start(bf16[3,256,128]{2,1,0:T(8,128)(2,1)S(1)} %halo.5), channel_id=1, source_target_pairs={{0,8},{2,10},{4,12},{6,14},{8,0},{10,2},{12,4},{14,6},{16,24},{18,... | collective-permute-start | bytes 589832 | tf_op jit(solution)/shard_map/ppermute | solution.py:376
  29.7 9.9 %collective-permute-start.13 = (bf16[3,288,128]{2,1,0:T(8,128)(2,1)S(1)}, bf16[3,288,128]{2,1,0:T(8,128)(2,1)S(1)}, u32[]{:S(2)}, u32[]{:S(2)}) collective-permute-start(bf16[3,288,128]{2,1,0:T(8,128)(2,1)S(1)} %get-tuple-element.59), channel_id=1, source_target_pairs={{0,8},{2,10},{4,12},{6,14},{8,0},{10,2},{12,4},{14,6},{16,24},{18,... | collective-permute-start | bytes 663560 | tf_op jit(solution)/shard_map/ppermute | solution.py:376
  30.6 9.0 %collective-permute-start.14 = (bf16[3,288,128]{2,1,0:T(8,128)(2,1)S(1)}, bf16[3,288,128]{2,1,0:T(8,128)(2,1)S(1)}, u32[]{:S(2)}, u32[]{:S(2)}) collective-permute-start(bf16[3,288,128]{2,1,0:T(8,128)(2,1)S(1)} %get-tuple-element.60), channel_id=1, source_target_pairs={{8,16},{10,18},{12,20},{14,22},{16,8},{18,10},{20,12},{22,14},{9,1... | collective-permute-start | bytes 663560 | tf_op jit(solution)/shard_map/ppermute | solution.py:376
  36.6 10.3 %collective-permute-start.22 = (bf16[256,128]{1,0:T(8,128)(2,1)S(1)}, bf16[256,128]{1,0:T(8,128)(2,1)S(1)}, u32[]{:S(2)}, u32[]{:S(2)}) collective-permute-start(bf16[256,128]{1,0:T(8,128)(2,1)S(1)} %get-tuple-element.75), channel_id=1, source_target_pairs={{0,6},{2,4},{4,2},{6,0},{8,14},{10,12},{12,10},{14,8},{16,22},{18,... | collective-permute-start | bytes 196616 | tf_op jit(solution)/shard_map/ppermute | solution.py:371
  39.4 7.6 %collective-permute-start.21 = (bf16[256,128]{1,0:T(8,128)(2,1)S(1)}, bf16[256,128]{1,0:T(8,128)(2,1)S(1)}, u32[]{:S(2)}, u32[]{:S(2)}) collective-permute-start(bf16[256,128]{1,0:T(8,128)(2,1)S(1)} %get-tuple-element.64.refs_0_), channel_id=1, source_target_pairs={{0,4},{2,6},{4,0},{6,2},{8,12},{10,14},{12,8},{14,10},{16,20},{18,... | collective-permute-start | bytes 196616 | tf_op jit(solution)/shard_map/ppermute | solution.py:371
  40.1 4.7 %collective-permute-start.17 = (bf16[256,128]{1,0:T(8,128)(2,1)S(1)}, bf16[256,128]{1,0:T(8,128)(2,1)S(1)}, u32[]{:S(2)}, u32[]{:S(2)}) collective-permute-start(bf16[256,128]{1,0:T(8,128)(2,1)S(1)} %get-tuple-element.66), channel_id=1, source_target_pairs={{0,2},{2,0},{4,6},{6,4},{8,10},{10,8},{12,14},{14,12},{16,18},{18,... | collective-permute-start | bytes 196616 | tf_op jit(solution)/shard_map/ppermute | solution.py:371
  40.9 4.2 %collective-permute-start.18 = (bf16[256,128]{1,0:T(8,128)(2,1)S(1)}, bf16[256,128]{1,0:T(8,128)(2,1)S(1)}, u32[]{:S(2)}, u32[]{:S(2)}) collective-permute-start(bf16[256,128]{1,0:T(8,128)(2,1)S(1)} %get-tuple-element.67), channel_id=1, source_target_pairs={{0,4},{2,6},{4,0},{6,2},{8,12},{10,14},{12,8},{14,10},{16,20},{18,... | collective-permute-start | bytes 196616 | tf_op jit(solution)/shard_map/ppermute | solution.py:371
  42.1 4.1 %collective-permute-start.19 = (bf16[256,128]{1,0:T(8,128)(2,1)S(1)}, bf16[256,128]{1,0:T(8,128)(2,1)S(1)}, u32[]{:S(2)}, u32[]{:S(2)}) collective-permute-start(bf16[256,128]{1,0:T(8,128)(2,1)S(1)} %get-tuple-element.68), channel_id=1, source_target_pairs={{0,6},{2,4},{4,2},{6,0},{8,14},{10,12},{12,10},{14,8},{16,22},{18,... | collective-permute-start | bytes 196616 | tf_op jit(solution)/shard_map/ppermute | solution.py:371
  44.9 2.1 %collective-permute-start.20 = (bf16[256,128]{1,0:T(8,128)(2,1)S(1)}, bf16[256,128]{1,0:T(8,128)(2,1)S(1)}, u32[]{:S(2)}, u32[]{:S(2)}) collective-permute-start(bf16[256,128]{1,0:T(8,128)(2,1)S(1)} %get-tuple-element.74), channel_id=1, source_target_pairs={{0,2},{2,0},{4,6},{6,4},{8,10},{10,8},{12,14},{14,12},{16,18},{18,... | collective-permute-start | bytes 196616 | tf_op jit(solution)/shard_map/ppermute | solution.py:371

commit v23 on v22

--- a/solution.py
+++ b/solution.py
@@ -119,12 +119,14 @@
 
 
 def join_kernel(*refs):
-    pieces, out, sems = refs[:GROUP], refs[GROUP], refs[GROUP + 1]
+    pieces, outs, sems = refs[: 2 * GROUP], refs[2 * GROUP : 2 * GROUP + 2], refs[-1]
     width = pieces[0].shape[1]
     mine = place()
     copies, fetch = fetcher(sems)
-    for k in range(GROUP):
-        fetch(pieces[k], out.at[:, pl.ds(pl.multiple_of((mine ^ k) * width, width), width)])
+    for i, out in enumerate(outs):
+        for k in range(GROUP):
+            at = pl.ds(pl.multiple_of((mine ^ k) * width, width), width)
+            fetch(pieces[i * GROUP + k], out.at[:, at])
     for copy in copies:
         copy.wait()
 
@@ -269,7 +271,7 @@
         packs, queries, keys, (edge_b, edge_a) = take(GROUP), take(GROUP), take(GROUP), take(2)
     (edge_turned,) = take(1)
     if not first:
-        shared, _ = take(4), take(1)
+        shared, _ = take(4), take(2)
     outs = take(len(receivers))
     turned, beside, asks, edge_beside = take(4) if first else shared
     rows, width = outs[0].shape
@@ -368,7 +370,9 @@
 
     def traded(pieces):
         pairs = lambda k: [(i, i ^ k) for i in range(length)]
-        return [pieces[0]] + [lax.ppermute(pieces[k], "tm", pairs(k)) for k in range(1, GROUP)]
+        return [
+            lax.ppermute(x, "tm", pairs(k)) if k and x is not None else x for k, x in enumerate(pieces)
+        ]
 
     def crossed(sent, second):
         planes = range(second, length // GROUP - second)
@@ -481,26 +485,23 @@
         name="merge",
     )(*backs, peaks, sums, far_pieces[0])
     audio_pieces = traded(audio_pieces)
+    far_pieces = traded([None, None, *far_pieces])[2:]
     near_pieces = call(
         functools.partial(columns_kernel, near),
         [piece] * len(near),
-        ins=[VMEM] * 5 + [ANY],
+        ins=[VMEM] * 5 + [ANY] * 2,
         **half_columns,
-    )(edge_turned, turned, beside, asks, edge_beside, audio_pieces[0])
-    video_pieces = traded([*near_pieces, *far_pieces])
-
-    def join(pieces):
-        return call(
-            join_kernel,
-            shape((rows, half), bf16),
-            [pltpu.SemaphoreType.DMA((GROUP,))],
-            outs_in=HBM,
-            moved=2 * rows * half * 2,
-            name="join",
-        )(*pieces)
-
-    video_attended = join(video_pieces)
-    audio_attended = join(audio_pieces)
+    )(edge_turned, turned, beside, asks, edge_beside, far_pieces[0], audio_pieces[0])
+    video_pieces = [*traded(near_pieces), *far_pieces]
+
+    audio_attended, video_attended = call(
+        join_kernel,
+        [shape((rows, half), bf16)] * 2,
+        [pltpu.SemaphoreType.DMA((2 * GROUP,))],
+        outs_in=[HBM, HBM],
+        moved=4 * rows * half * 2,
+        name="join",
+    )(*audio_pieces, *video_pieces)
     return (audio_attended, video_attended)
 
 

time: 48.1 us -> 47.7 us (level)
  Pallas kernels: 16.7 us -> 16 us
    pallas_call x2 -> x1, Pallas kernels: 1.47 us -> 0.85 us  [local(): call(join_kernel, [shape((rows, half), bf16)] * 2, [pltpu.SemaphoreType.D...]
  transfers between devices with their start and end apart: 23 -> 23, of which waited for: 4 -> 4; matrix products, arithmetic and copies ran while one was open for 0% -> 0% of each run, Pallas kernels for 33% -> 32%
where the time goes in v23:
time: 47.7 us; the launch traced here: 47.2 us
  starting transfers between devices  26.3 us (55%)
  Pallas kernels  16 us (34%)
  waiting for transfers between devices  3.88 us (8%)
  between operations  0.98 us (2%)
    ppermute x15, starting transfers between devices, traded(): lax.ppermute(x, 'tm', pairs(k))  15.1 us
    ppermute x6, starting transfers between devices, crossed(): lax.ppermute(sent, 'tm', [(p * GROUP + i, q * GROUP + i) for p, q in pair...  9.69 us
    pallas_call x1, Pallas kernels, local(): call(rows_kernel, [shape((GROUP, rows, width), f32), shape((GROUP, 2, row...  3.3 us
    ppermute x15, waiting for transfers between devices, traded(): lax.ppermute(x, 'tm', pairs(k))  2.79 us
    pallas_call x1, Pallas kernels, local(): call(lend_kernel, [back, back, shape((2 * width, around), bf16)], [pltpu....  2.64 us
    pallas_call x1, Pallas kernels, local(): call(functools.partial(columns_kernel, far), [piece] * len(far) + shared,...  2.64 us
    pallas_call x1, Pallas kernels, local(): call(functools.partial(columns_kernel, near), [piece] * len(near), ins=[V...  2.25 us
    pallas_call x1, Pallas kernels, local(): call(prepare_kernel, [part, part, square, square], [pltpu.VMEM((rows, hal...  1.78 us
  transfers between devices with their start and end apart: 23, of which 4 were waited for; matrix products, arithmetic and copies ran while one was open for 0% of the time, Pallas kernels for 32%

profile of v23, /device:TPU:9, one launch (start us, length us, event | category | flops | bytes accessed | tf_op | source)
XLA Modules:
  0.0 47.2 jit_solution(3116144331289032364)
XLA Ops:
  0.6 1.3 %collective-permute-start.1 = (bf16[256,512]{1,0:T(8,128)(2,1)}, bf16[256,512]{1,0:T(8,128)(2,1)S(1)}, u32[]{:S(2)}, u32[]{:S(2)}) collective-permute-start(bf16[256,512]{1,0:T(8,128)(2,1)} %audio.3), channel_id=1, source_target_pairs={{0,1},{1,0},{2,3},{3,2},{4,5},{5,4},{6,7},{7,6},{8,9},{9,8},{10,11... | collective-permute-start | bytes 786440 | tf_op jit(solution)/shard_map/ppermute | solution.py:369
  1.9 0.2 collective-permute-start.7
  2.2 1.2 %split.1 = (bf16[528,128]{1,0:T(8,128)(2,1)S(1)}, bf16[528,128]{1,0:T(8,128)(2,1)S(1)}, bf16[528,128]{1,0:T(8,128)(2,1)S(1)}, bf16[528,128]{1,0:T(8,128)(2,1)S(1)}) custom-call(bf16[256,512]{1,0:T(8,128)(2,1)} %audio.3, bf16[256,512]{1,0:T(8,128)(2,1)} %video.3, s32[2,128]{1,0:T(2,128)} %bitcast.1), custom_call_target="tpu_custom_call" | custom-call | bytes 1048576 | tf_op jit(solution)/shard_map/split/pallas_call | solution.py:393
  3.3 1.3 %collective-permute-start = (bf16[528,128]{1,0:T(8,128)(2,1)S(1)}, bf16[528,128]{1,0:T(8,128)(2,1)S(1)}, u32[]{:S(2)}, u32[]{:S(2)}) collective-permute-start(bf16[528,128]{1,0:T(8,128)(2,1)S(1)} %get-tuple-element.39), channel_id=1, source_target_pairs={{0,2},{2,0},{4,6},{6,4},{8,10},{10,8},{12,14},{14,12},{16,18},{18,... | collective-permute-start | bytes 405512 | tf_op jit(solution)/shard_map/ppermute | solution.py:374
  4.6 1.2 %collective-permute-start.2 = (bf16[528,128]{1,0:T(8,128)(2,1)S(1)}, bf16[528,128]{1,0:T(8,128)(2,1)S(1)}, u32[]{:S(2)}, u32[]{:S(2)}) collective-permute-start(bf16[528,128]{1,0:T(8,128)(2,1)S(1)} %get-tuple-element.42), channel_id=1, source_target_pairs={{0,4},{2,6},{4,0},{6,2},{8,12},{10,14},{12,8},{14,10},{16,20},{18,... | collective-permute-start | bytes 405512 | tf_op jit(solution)/shard_map/ppermute | solution.py:374
  5.9 0.5 %collective-permute-start.6 = (bf16[528,128]{1,0:T(8,128)(2,1)S(1)}, bf16[528,128]{1,0:T(8,128)(2,1)S(1)}, u32[]{:S(2)}, u32[]{:S(2)}) collective-permute-start(bf16[528,128]{1,0:T(8,128)(2,1)S(1)} %get-tuple-element.48), channel_id=1, source_target_pairs={{0,6},{2,4},{4,2},{6,0},{8,14},{10,12},{12,10},{14,8},{16,22},{18,... | collective-permute-start | bytes 405512 | tf_op jit(solution)/shard_map/ppermute | solution.py:374
  6.3 0.0 collective-permute-done.refs_0_.refs_5_.refs_1_
  6.3 1.8 %prepare.1 = (f32[256,512]{1,0:T(8,128)S(1)}, f32[256,512]{1,0:T(8,128)S(1)}, bf16[512,512]{1,0:T(8,128)(2,1)S(1)}, bf16[512,512]{1,0:T(8,128)(2,1)S(1)}) custom-call(bf16[256,512]{1,0:T(8,128)(2,1)} %audio.3, bf16[256,512]{1,0:T(8,128)(2,1)} %video.3, bf16[1024,512]{1,0:T(8,128)(2,1)} %query.1, bf16[1024,512]{1,0:T(8,128)(2,1)} %key.1, ...), custom_call_target="tpu_custom_call" | custom-call | flops 268435456 | bytes 4194304 | tf_op jit(solution)/shard_map/prepare/pallas_call | solution.py:403
  8.1 1.7 %collective-permute-done.2.refs_1_.refs_6_.refs_2_ = bf16[528,128]{1,0:T(8,128)(2,1)S(1)} collective-permute-done((bf16[528,128]{1,0:T(8,128)(2,1)S(1)}, bf16[528,128]{1,0:T(8,128)(2,1)S(1)}, u32[]{:S(2)}, u32[]{:S(2)}) %collective-permute-start.2) | collective-permute-done | bytes 135200 | tf_op jit(solution)/shard_map/ppermute | solution.py:374
  9.8 0.0 collective-permute-done.1.other
  9.8 0.4 project.2
  10.2 1.4 %collective-permute-start.3 = (bf16[256,128]{1,0:T(8,128)(2,1)S(1)}, bf16[256,128]{1,0:T(8,128)(2,1)S(1)}, u32[]{:S(2)}, u32[]{:S(2)}) collective-permute-start(bf16[256,128]{1,0:T(8,128)(2,1)S(1)} %get-tuple-element.44), channel_id=1, source_target_pairs={{0,2},{2,0},{4,6},{6,4},{8,10},{10,8},{12,14},{14,12},{16,18},{18,... | collective-permute-start | bytes 196616 | tf_op jit(solution)/shard_map/ppermute | solution.py:374
  11.6 1.2 %collective-permute-start.4 = (bf16[256,128]{1,0:T(8,128)(2,1)S(1)}, bf16[256,128]{1,0:T(8,128)(2,1)S(1)}, u32[]{:S(2)}, u32[]{:S(2)}) collective-permute-start(bf16[256,128]{1,0:T(8,128)(2,1)S(1)} %get-tuple-element.45), channel_id=1, source_target_pairs={{0,4},{2,6},{4,0},{6,2},{8,12},{10,14},{12,8},{14,10},{16,20},{18,... | collective-permute-start | bytes 196616 | tf_op jit(solution)/shard_map/ppermute | solution.py:374
  12.8 0.5 %collective-permute-start.5 = (bf16[256,128]{1,0:T(8,128)(2,1)S(1)}, bf16[256,128]{1,0:T(8,128)(2,1)S(1)}, u32[]{:S(2)}, u32[]{:S(2)}) collective-permute-start(bf16[256,128]{1,0:T(8,128)(2,1)S(1)} %get-tuple-element.46), channel_id=1, source_target_pairs={{0,6},{2,4},{4,2},{6,0},{8,14},{10,12},{12,10},{14,8},{16,22},{18,... | collective-permute-start | bytes 196616 | tf_op jit(solution)/shard_map/ppermute | solution.py:374
  13.3 0.4 collective-permute-done.7.other
  13.7 0.4 project.3
  14.1 1.6 %collective-permute-start.10 = (bf16[256,128]{1,0:T(8,128)(2,1)S(1)}, bf16[256,128]{1,0:T(8,128)(2,1)S(1)}, u32[]{:S(2)}, u32[]{:S(2)}) collective-permute-start(bf16[256,128]{1,0:T(8,128)(2,1)S(1)} %get-tuple-element.54), channel_id=1, source_target_pairs={{0,2},{2,0},{4,6},{6,4},{8,10},{10,8},{12,14},{14,12},{16,18},{18,... | collective-permute-start | bytes 196616 | tf_op jit(solution)/shard_map/ppermute | solution.py:374
  15.7 0.0 collective-permute-done.6.refs_7_.refs_3_
  15.7 1.2 %collective-permute-start.11 = (bf16[256,128]{1,0:T(8,128)(2,1)S(1)}, bf16[256,128]{1,0:T(8,128)(2,1)S(1)}, u32[]{:S(2)}, u32[]{:S(2)}) collective-permute-start(bf16[256,128]{1,0:T(8,128)(2,1)S(1)} %get-tuple-element.55), channel_id=1, source_target_pairs={{0,4},{2,6},{4,0},{6,2},{8,12},{10,14},{12,8},{14,10},{16,20},{18,... | collective-permute-start | bytes 196616 | tf_op jit(solution)/shard_map/ppermute | solution.py:374
  16.9 0.0 collective-permute-done.3.refs_1_.refs_5_
  16.9 0.5 %collective-permute-start.12 = (bf16[256,128]{1,0:T(8,128)(2,1)S(1)}, bf16[256,128]{1,0:T(8,128)(2,1)S(1)}, u32[]{:S(2)}, u32[]{:S(2)}) collective-permute-start(bf16[256,128]{1,0:T(8,128)(2,1)S(1)} %get-tuple-element.56), channel_id=1, source_target_pairs={{0,6},{2,4},{4,2},{6,0},{8,14},{10,12},{12,10},{14,8},{16,22},{18,... | collective-permute-start | bytes 196616 | tf_op jit(solution)/shard_map/ppermute | solution.py:374
  17.4 0.0 collective-permute-done.4.refs_2_.refs_6_
  17.4 0.0 collective-permute-done.5.refs_3_.refs_7_
  17.4 0.1 halo.3
  17.5 3.2 %collective-permute-start.8 = (bf16[3,272,128]{2,1,0:T(8,128)(2,1)S(1)}, bf16[3,272,128]{2,1,0:T(8,128)(2,1)S(1)}, u32[]{:S(2)}, u32[]{:S(2)}) collective-permute-start(bf16[3,272,128]{2,1,0:T(8,128)(2,1)S(1)} %get-tuple-element.52), channel_id=1, source_target_pairs={{8,16},{10,18},{12,20},{14,22},{16,8},{18,10},{20,12},{22,14},{9,1... | collective-permute-start | bytes 626696 | tf_op jit(solution)/shard_map/ppermute | solution.py:380
  20.7 0.1 collective-permute-start.9
  20.8 0.1 halo.4
  20.8 0.0 collective-permute-done.10.refs_9_
  20.9 2.1 %collective-permute-start.15 = (bf16[3,256,128]{2,1,0:T(8,128)(2,1)S(1)}, bf16[3,256,128]{2,1,0:T(8,128)(2,1)S(1)}, u32[]{:S(2)}, u32[]{:S(2)}) collective-permute-start(bf16[3,256,128]{2,1,0:T(8,128)(2,1)S(1)} %halo.4), channel_id=1, source_target_pairs={{8,16},{10,18},{12,20},{14,22},{16,8},{18,10},{20,12},{22,14},{9,1... | collective-permute-start | bytes 589832 | tf_op jit(solution)/shard_map/ppermute | solution.py:380
  22.9 0.0 collective-permute-done.11.refs_10_
  23.0 0.0 collective-permute-done.12.refs_11_
  23.0 3.3 %rows.1 = (f32[4,256,128]{2,1,0:T(8,128)S(1)}, f32[4,2,256,128]{3,2,1,0:T(8,128)S(1)}, bf16[256,1024]{1,0:T(8,128)(2,1)S(1)}, bf16[1024,256]{1,0:T(8,128)(2,1)S(1)}) custom-call(bf16[528,128]{1,0:T(8,128)(2,1)S(1)} %get-tuple-element.47.refs_4_.refs_0_, bf16[528,128]{1,0:T(8,128)(2,1)S(1)} %collective-permute-done.refs_0_.refs_5_.refs_1_, ...), custom_call_target="tpu_custom_call" | custom-call | flops 2147483648 | bytes 2097152 | tf_op jit(solution)/shard_map/rows/pallas_call | solution.py:445
  26.3 0.1 halo.5
  26.3 0.1 collective-permute-start.16
  26.4 0.0 collective-permute-done.8.edge_b
  26.4 0.6 %collective-permute-done.9.edge_a = bf16[3,272,128]{2,1,0:T(8,128)(2,1)S(1)} collective-permute-done((bf16[3,272,128]{2,1,0:T(8,128)(2,1)S(1)}, bf16[3,272,128]{2,1,0:T(8,128)(2,1)S(1)}, u32[]{:S(2)}, u32[]{:S(2)}) %collective-permute-start.9) | collective-permute-done | bytes 208928 | tf_op jit(solution)/shard_map/ppermute | solution.py:380
  27.1 2.6 %lend.1 = (bf16[3,288,128]{2,1,0:T(8,128)(2,1)S(1)}, bf16[3,288,128]{2,1,0:T(8,128)(2,1)S(1)}, bf16[256,1536]{1,0:T(8,128)(2,1)S(1)}) custom-call(bf16[3,272,128]{2,1,0:T(8,128)(2,1)S(1)} %collective-permute-done.8.edge_b, bf16[3,272,128]{2,1,0:T(8,128)(2,1)S(1)} %collective-permute-done.9.edge_a, bf16[256,1024]{1,0:T(8,128)(2,1)S(1)} %get-tuple-element.57.plane_turned, ...), custom_call_target="tpu_custom_call" | custom-call | flops 4831838208 | bytes 3145728 | tf_op jit(solution)/shard_map/lend/pallas_call | solution.py:456
  29.7 0.9 %collective-permute-start.13 = (bf16[3,288,128]{2,1,0:T(8,128)(2,1)S(1)}, bf16[3,288,128]{2,1,0:T(8,128)(2,1)S(1)}, u32[]{:S(2)}, u32[]{:S(2)}) collective-permute-start(bf16[3,288,128]{2,1,0:T(8,128)(2,1)S(1)} %get-tuple-element.59), channel_id=1, source_target_pairs={{0,8},{2,10},{4,12},{6,14},{8,0},{10,2},{12,4},{14,6},{16,24},{18,... | collective-permute-start | bytes 663560 | tf_op jit(solution)/shard_map/ppermute | solution.py:380
  30.6 3.4 %collective-permute-start.14 = (bf16[3,288,128]{2,1,0:T(8,128)(2,1)S(1)}, bf16[3,288,128]{2,1,0:T(8,128)(2,1)S(1)}, u32[]{:S(2)}, u32[]{:S(2)}) collective-permute-start(bf16[3,288,128]{2,1,0:T(8,128)(2,1)S(1)} %get-tuple-element.60), channel_id=1, source_target_pairs={{8,16},{10,18},{12,20},{14,22},{16,8},{18,10},{20,12},{22,14},{9,1... | collective-permute-start | bytes 663560 | tf_op jit(solution)/shard_map/ppermute | solution.py:380
  34.0 0.0 collective-permute-done.15.refs_12_
  34.0 0.0 collective-permute-done.16.refs_13_
  34.0 2.6 %columns.2 = (bf16[256,128]{1,0:T(8,128)(2,1)S(1)}, bf16[256,128]{1,0:T(8,128)(2,1)S(1)}, bf16[256,1024]{1,0:T(8,128)(2,1)S(1)}, bf16[1024,256]{1,0:T(8,128)(2,1...) custom-call(bf16[528,128]{1,0:T(8,128)(2,1)S(1)} %get-tuple-element.47.refs_4_.refs_0_, ...), custom_call_target="tpu_custom_call" | custom-call | flops 1879048192 | bytes 1572864 | tf_op jit(solution)/shard_map/columns/pallas_call | solution.py:475
  36.6 1.3 %collective-permute-start.20 = (bf16[256,128]{1,0:T(8,128)(2,1)S(1)}, bf16[256,128]{1,0:T(8,128)(2,1)S(1)}, u32[]{:S(2)}, u32[]{:S(2)}) collective-permute-start(bf16[256,128]{1,0:T(8,128)(2,1)S(1)} %get-tuple-element.64.refs_0_), channel_id=1, source_target_pairs={{0,4},{2,6},{4,0},{6,2},{8,12},{10,14},{12,8},{14,10},{16,20},{18,... | collective-permute-start | bytes 196616 | tf_op jit(solution)/shard_map/ppermute | solution.py:374
  37.9 2.0 %collective-permute-start.22 = (bf16[256,128]{1,0:T(8,128)(2,1)S(1)}, bf16[256,128]{1,0:T(8,128)(2,1)S(1)}, u32[]{:S(2)}, u32[]{:S(2)}) collective-permute-start(bf16[256,128]{1,0:T(8,128)(2,1)S(1)} %get-tuple-element.75), channel_id=1, source_target_pairs={{0,6},{2,4},{4,2},{6,0},{8,14},{10,12},{12,10},{14,8},{16,22},{18,... | collective-permute-start | bytes 196616 | tf_op jit(solution)/shard_map/ppermute | solution.py:374
  39.9 0.0 collective-permute-done.13.back_a
  39.9 0.0 collective-permute-done.14.back_b
  39.9 0.5 %merge.1 = (bf16[256,128]{1,0:T(8,128)(2,1)S(1)}, bf16[256,128]{1,0:T(8,128)(2,1)S(1)}, bf16[256,128]{1,0:T(8,128)(2,1)S(1)}, bf16[256,128]{1,0:T(8,128)(2,1)S(1)}) custom-call(bf16[3,288,128]{2,1,0:T(8,128)(2,1)S(1)} %collective-permute-done.13.back_a, bf16[3,288,128]{2,1,0:T(8,128)(2,1)S(1)} %collective-permute-done.14.back_b, ...), custom_call_target="tpu_custom_call" | custom-call | bytes 2097152 | tf_op jit(solution)/shard_map/merge/pallas_call | solution.py:478
  40.4 0.5 %collective-permute-start.17 = (bf16[256,128]{1,0:T(8,128)(2,1)S(1)}, bf16[256,128]{1,0:T(8,128)(2,1)S(1)}, u32[]{:S(2)}, u32[]{:S(2)}) collective-permute-start(bf16[256,128]{1,0:T(8,128)(2,1)S(1)} %get-tuple-element.66), channel_id=1, source_target_pairs={{0,2},{2,0},{4,6},{6,4},{8,10},{10,8},{12,14},{14,12},{16,18},{18,... | collective-permute-start | bytes 196616 | tf_op jit(solution)/shard_map/ppermute | solution.py:374
  40.9 1.2 %collective-permute-start.18 = (bf16[256,128]{1,0:T(8,128)(2,1)S(1)}, bf16[256,128]{1,0:T(8,128)(2,1)S(1)}, u32[]{:S(2)}, u32[]{:S(2)}) collective-permute-start(bf16[256,128]{1,0:T(8,128)(2,1)S(1)} %get-tuple-element.67), channel_id=1, source_target_pairs={{0,4},{2,6},{4,0},{6,2},{8,12},{10,14},{12,8},{14,10},{16,20},{18,... | collective-permute-start | bytes 196616 | tf_op jit(solution)/shard_map/ppermute | solution.py:374
  42.1 0.5 %collective-permute-start.19 = (bf16[256,128]{1,0:T(8,128)(2,1)S(1)}, bf16[256,128]{1,0:T(8,128)(2,1)S(1)}, u32[]{:S(2)}, u32[]{:S(2)}) collective-permute-start(bf16[256,128]{1,0:T(8,128)(2,1)S(1)} %get-tuple-element.68), channel_id=1, source_target_pairs={{0,6},{2,4},{4,2},{6,0},{8,14},{10,12},{12,10},{14,8},{16,22},{18,... | collective-permute-start | bytes 196616 | tf_op jit(solution)/shard_map/ppermute | solution.py:374
  42.6 0.0 collective-permute-done.20.refs_5_.refs_6_
  42.6 2.2 %columns.3 = (bf16[256,128]{1,0:T(8,128)(2,1)S(1)}, bf16[256,128]{1,0:T(8,128)(2,1)S(1)}) custom-call(bf16[256,1536]{1,0:T(8,128)(2,1)S(1)} %get-tuple-element.63.refs_14_.refs_0_, bf16[256,1024]{1,0:T(8,128)(2,1)S(1)} %get-tuple-element.69.refs_1_, bf16[1024,256]{1,0:T(8,128)(2,1)S(1)} %get-tuple-element.70.refs_2_, ...), custom_call_target="tpu_custom_call" | custom-call | flops 1879048192 | bytes 1572864 | tf_op jit(solution)/shard_map/columns/pallas_call | solution.py:489
  44.9 0.2 collective-permute-start.21
  45.1 0.0 collective-permute-done.22.refs_7_
  45.1 0.0 collective-permute-done.17.refs_1_
  45.1 0.0 collective-permute-done.18.refs_2_
  45.1 1.1 %collective-permute-done.19.refs_3_ = bf16[256,128]{1,0:T(8,128)(2,1)S(1)} collective-permute-done((bf16[256,128]{1,0:T(8,128)(2,1)S(1)}, bf16[256,128]{1,0:T(8,128)(2,1)S(1)}, u32[]{:S(2)}, u32[]{:S(2)}) %collective-permute-start.19) | collective-permute-done | bytes 65568 | tf_op jit(solution)/shard_map/ppermute | solution.py:374
  46.2 0.0 collective-permute-done.21.refs_5_
  46.2 0.8 %join.1 = (bf16[256,512]{1,0:T(8,128)(2,1)}, bf16[256,512]{1,0:T(8,128)(2,1)}) custom-call(bf16[256,128]{1,0:T(8,128)(2,1)S(1)} %get-tuple-element.65.refs_6_.refs_0_, bf16[256,128]{1,0:T(8,128)(2,1)S(1)} %collective-permute-done.17.refs_1_, bf16[256,128]{1,0:T(8,128)(2,1)S(1)} %collective-permute-done.18.refs_2_, ...), custom_call_target="tpu_custom_call" | custom-call | bytes 1048576 | tf_op jit(solution)/shard_map/join/pallas_call | solution.py:497
Async XLA Ops:
  0.6 9.2 %collective-permute-start.1 = (bf16[256,512]{1,0:T(8,128)(2,1)}, bf16[256,512]{1,0:T(8,128)(2,1)S(1)}, u32[]{:S(2)}, u32[]{:S(2)}) collective-permute-start(bf16[256,512]{1,0:T(8,128)(2,1)} %audio.3), channel_id=1, source_target_pairs={{0,1},{1,0},{2,3},{3,2},{4,5},{5,4},{6,7},{7,6},{8,9},{9,8},{10,11... | collective-permute-start | bytes 786440 | tf_op jit(solution)/shard_map/ppermute | solution.py:369
  1.9 11.8 %collective-permute-start.7 = (bf16[256,512]{1,0:T(8,128)(2,1)}, bf16[256,512]{1,0:T(8,128)(2,1)S(1)}, u32[]{:S(2)}, u32[]{:S(2)}) collective-permute-start(bf16[256,512]{1,0:T(8,128)(2,1)} %video.3), channel_id=1, source_target_pairs={{0,1},{1,0},{2,3},{3,2},{4,5},{5,4},{6,7},{7,6},{8,9},{9,8},{10,11... | collective-permute-start | bytes 786440 | tf_op jit(solution)/shard_map/ppermute | solution.py:369
  3.3 3.0 %collective-permute-start = (bf16[528,128]{1,0:T(8,128)(2,1)S(1)}, bf16[528,128]{1,0:T(8,128)(2,1)S(1)}, u32[]{:S(2)}, u32[]{:S(2)}) collective-permute-start(bf16[528,128]{1,0:T(8,128)(2,1)S(1)} %get-tuple-element.39), channel_id=1, source_target_pairs={{0,2},{2,0},{4,6},{6,4},{8,10},{10,8},{12,14},{14,12},{16,18},{18,... | collective-permute-start | bytes 405512 | tf_op jit(solution)/shard_map/ppermute | solution.py:374
  4.6 5.2 %collective-permute-start.2 = (bf16[528,128]{1,0:T(8,128)(2,1)S(1)}, bf16[528,128]{1,0:T(8,128)(2,1)S(1)}, u32[]{:S(2)}, u32[]{:S(2)}) collective-permute-start(bf16[528,128]{1,0:T(8,128)(2,1)S(1)} %get-tuple-element.42), channel_id=1, source_target_pairs={{0,4},{2,6},{4,0},{6,2},{8,12},{10,14},{12,8},{14,10},{16,20},{18,... | collective-permute-start | bytes 405512 | tf_op jit(solution)/shard_map/ppermute | solution.py:374
  5.9 9.8 %collective-permute-start.6 = (bf16[528,128]{1,0:T(8,128)(2,1)S(1)}, bf16[528,128]{1,0:T(8,128)(2,1)S(1)}, u32[]{:S(2)}, u32[]{:S(2)}) collective-permute-start(bf16[528,128]{1,0:T(8,128)(2,1)S(1)} %get-tuple-element.48), channel_id=1, source_target_pairs={{0,6},{2,4},{4,2},{6,0},{8,14},{10,12},{12,10},{14,8},{16,22},{18,... | collective-permute-start | bytes 405512 | tf_op jit(solution)/shard_map/ppermute | solution.py:374
  10.2 6.7 %collective-permute-start.3 = (bf16[256,128]{1,0:T(8,128)(2,1)S(1)}, bf16[256,128]{1,0:T(8,128)(2,1)S(1)}, u32[]{:S(2)}, u32[]{:S(2)}) collective-permute-start(bf16[256,128]{1,0:T(8,128)(2,1)S(1)} %get-tuple-element.44), channel_id=1, source_target_pairs={{0,2},{2,0},{4,6},{6,4},{8,10},{10,8},{12,14},{14,12},{16,18},{18,... | collective-permute-start | bytes 196616 | tf_op jit(solution)/shard_map/ppermute | solution.py:374
  11.6 5.9 %collective-permute-start.4 = (bf16[256,128]{1,0:T(8,128)(2,1)S(1)}, bf16[256,128]{1,0:T(8,128)(2,1)S(1)}, u32[]{:S(2)}, u32[]{:S(2)}) collective-permute-start(bf16[256,128]{1,0:T(8,128)(2,1)S(1)} %get-tuple-element.45), channel_id=1, source_target_pairs={{0,4},{2,6},{4,0},{6,2},{8,12},{10,14},{12,8},{14,10},{16,20},{18,... | collective-permute-start | bytes 196616 | tf_op jit(solution)/shard_map/ppermute | solution.py:374
  12.8 4.6 %collective-permute-start.5 = (bf16[256,128]{1,0:T(8,128)(2,1)S(1)}, bf16[256,128]{1,0:T(8,128)(2,1)S(1)}, u32[]{:S(2)}, u32[]{:S(2)}) collective-permute-start(bf16[256,128]{1,0:T(8,128)(2,1)S(1)} %get-tuple-element.46), channel_id=1, source_target_pairs={{0,6},{2,4},{4,2},{6,0},{8,14},{10,12},{12,10},{14,8},{16,22},{18,... | collective-permute-start | bytes 196616 | tf_op jit(solution)/shard_map/ppermute | solution.py:374
  14.1 6.8 %collective-permute-start.10 = (bf16[256,128]{1,0:T(8,128)(2,1)S(1)}, bf16[256,128]{1,0:T(8,128)(2,1)S(1)}, u32[]{:S(2)}, u32[]{:S(2)}) collective-permute-start(bf16[256,128]{1,0:T(8,128)(2,1)S(1)} %get-tuple-element.54), channel_id=1, source_target_pairs={{0,2},{2,0},{4,6},{6,4},{8,10},{10,8},{12,14},{14,12},{16,18},{18,... | collective-permute-start | bytes 196616 | tf_op jit(solution)/shard_map/ppermute | solution.py:374
  15.7 7.2 %collective-permute-start.11 = (bf16[256,128]{1,0:T(8,128)(2,1)S(1)}, bf16[256,128]{1,0:T(8,128)(2,1)S(1)}, u32[]{:S(2)}, u32[]{:S(2)}) collective-permute-start(bf16[256,128]{1,0:T(8,128)(2,1)S(1)} %get-tuple-element.55), channel_id=1, source_target_pairs={{0,4},{2,6},{4,0},{6,2},{8,12},{10,14},{12,8},{14,10},{16,20},{18,... | collective-permute-start | bytes 196616 | tf_op jit(solution)/shard_map/ppermute | solution.py:374
  16.9 6.0 %collective-permute-start.12 = (bf16[256,128]{1,0:T(8,128)(2,1)S(1)}, bf16[256,128]{1,0:T(8,128)(2,1)S(1)}, u32[]{:S(2)}, u32[]{:S(2)}) collective-permute-start(bf16[256,128]{1,0:T(8,128)(2,1)S(1)} %get-tuple-element.56), channel_id=1, source_target_pairs={{0,6},{2,4},{4,2},{6,0},{8,14},{10,12},{12,10},{14,8},{16,22},{18,... | collective-permute-start | bytes 196616 | tf_op jit(solution)/shard_map/ppermute | solution.py:374
  17.5 8.9 %collective-permute-start.8 = (bf16[3,272,128]{2,1,0:T(8,128)(2,1)S(1)}, bf16[3,272,128]{2,1,0:T(8,128)(2,1)S(1)}, u32[]{:S(2)}, u32[]{:S(2)}) collective-permute-start(bf16[3,272,128]{2,1,0:T(8,128)(2,1)S(1)} %get-tuple-element.52), channel_id=1, source_target_pairs={{8,16},{10,18},{12,20},{14,22},{16,8},{18,10},{20,12},{22,14},{9,1... | collective-permute-start | bytes 626696 | tf_op jit(solution)/shard_map/ppermute | solution.py:380
  20.7 6.4 %collective-permute-start.9 = (bf16[3,272,128]{2,1,0:T(8,128)(2,1)S(1)}, bf16[3,272,128]{2,1,0:T(8,128)(2,1)S(1)}, u32[]{:S(2)}, u32[]{:S(2)}) collective-permute-start(bf16[3,272,128]{2,1,0:T(8,128)(2,1)S(1)} %get-tuple-element.53), channel_id=1, source_target_pairs={{0,8},{2,10},{4,12},{6,14},{8,0},{10,2},{12,4},{14,6},{16,24},{18,... | collective-permute-start | bytes 626696 | tf_op jit(solution)/shard_map/ppermute | solution.py:380
  20.9 13.1 %collective-permute-start.15 = (bf16[3,256,128]{2,1,0:T(8,128)(2,1)S(1)}, bf16[3,256,128]{2,1,0:T(8,128)(2,1)S(1)}, u32[]{:S(2)}, u32[]{:S(2)}) collective-permute-start(bf16[3,256,128]{2,1,0:T(8,128)(2,1)S(1)} %halo.4), channel_id=1, source_target_pairs={{8,16},{10,18},{12,20},{14,22},{16,8},{18,10},{20,12},{22,14},{9,1... | collective-permute-start | bytes 589832 | tf_op jit(solution)/shard_map/ppermute | solution.py:380
  26.3 7.6 %collective-permute-start.16 = (bf16[3,256,128]{2,1,0:T(8,128)(2,1)S(1)}, bf16[3,256,128]{2,1,0:T(8,128)(2,1)S(1)}, u32[]{:S(2)}, u32[]{:S(2)}) collective-permute-start(bf16[3,256,128]{2,1,0:T(8,128)(2,1)S(1)} %halo.5), channel_id=1, source_target_pairs={{0,8},{2,10},{4,12},{6,14},{8,0},{10,2},{12,4},{14,6},{16,24},{18,... | collective-permute-start | bytes 589832 | tf_op jit(solution)/shard_map/ppermute | solution.py:380
  29.7 10.2 %collective-permute-start.13 = (bf16[3,288,128]{2,1,0:T(8,128)(2,1)S(1)}, bf16[3,288,128]{2,1,0:T(8,128)(2,1)S(1)}, u32[]{:S(2)}, u32[]{:S(2)}) collective-permute-start(bf16[3,288,128]{2,1,0:T(8,128)(2,1)S(1)} %get-tuple-element.59), channel_id=1, source_target_pairs={{0,8},{2,10},{4,12},{6,14},{8,0},{10,2},{12,4},{14,6},{16,24},{18,... | collective-permute-start | bytes 663560 | tf_op jit(solution)/shard_map/ppermute | solution.py:380
  30.6 9.3 %collective-permute-start.14 = (bf16[3,288,128]{2,1,0:T(8,128)(2,1)S(1)}, bf16[3,288,128]{2,1,0:T(8,128)(2,1)S(1)}, u32[]{:S(2)}, u32[]{:S(2)}) collective-permute-start(bf16[3,288,128]{2,1,0:T(8,128)(2,1)S(1)} %get-tuple-element.60), channel_id=1, source_target_pairs={{8,16},{10,18},{12,20},{14,22},{16,8},{18,10},{20,12},{22,14},{9,1... | collective-permute-start | bytes 663560 | tf_op jit(solution)/shard_map/ppermute | solution.py:380
  36.6 6.0 %collective-permute-start.20 = (bf16[256,128]{1,0:T(8,128)(2,1)S(1)}, bf16[256,128]{1,0:T(8,128)(2,1)S(1)}, u32[]{:S(2)}, u32[]{:S(2)}) collective-permute-start(bf16[256,128]{1,0:T(8,128)(2,1)S(1)} %get-tuple-element.64.refs_0_), channel_id=1, source_target_pairs={{0,4},{2,6},{4,0},{6,2},{8,12},{10,14},{12,8},{14,10},{16,20},{18,... | collective-permute-start | bytes 196616 | tf_op jit(solution)/shard_map/ppermute | solution.py:374
  37.9 7.2 %collective-permute-start.22 = (bf16[256,128]{1,0:T(8,128)(2,1)S(1)}, bf16[256,128]{1,0:T(8,128)(2,1)S(1)}, u32[]{:S(2)}, u32[]{:S(2)}) collective-permute-start(bf16[256,128]{1,0:T(8,128)(2,1)S(1)} %get-tuple-element.75), channel_id=1, source_target_pairs={{0,6},{2,4},{4,2},{6,0},{8,14},{10,12},{12,10},{14,8},{16,22},{18,... | collective-permute-start | bytes 196616 | tf_op jit(solution)/shard_map/ppermute | solution.py:374
  40.4 4.7 %collective-permute-start.17 = (bf16[256,128]{1,0:T(8,128)(2,1)S(1)}, bf16[256,128]{1,0:T(8,128)(2,1)S(1)}, u32[]{:S(2)}, u32[]{:S(2)}) collective-permute-start(bf16[256,128]{1,0:T(8,128)(2,1)S(1)} %get-tuple-element.66), channel_id=1, source_target_pairs={{0,2},{2,0},{4,6},{6,4},{8,10},{10,8},{12,14},{14,12},{16,18},{18,... | collective-permute-start | bytes 196616 | tf_op jit(solution)/shard_map/ppermute | solution.py:374
  40.9 4.2 %collective-permute-start.18 = (bf16[256,128]{1,0:T(8,128)(2,1)S(1)}, bf16[256,128]{1,0:T(8,128)(2,1)S(1)}, u32[]{:S(2)}, u32[]{:S(2)}) collective-permute-start(bf16[256,128]{1,0:T(8,128)(2,1)S(1)} %get-tuple-element.67), channel_id=1, source_target_pairs={{0,4},{2,6},{4,0},{6,2},{8,12},{10,14},{12,8},{14,10},{16,20},{18,... | collective-permute-start | bytes 196616 | tf_op jit(solution)/shard_map/ppermute | solution.py:374
  42.1 4.1 %collective-permute-start.19 = (bf16[256,128]{1,0:T(8,128)(2,1)S(1)}, bf16[256,128]{1,0:T(8,128)(2,1)S(1)}, u32[]{:S(2)}, u32[]{:S(2)}) collective-permute-start(bf16[256,128]{1,0:T(8,128)(2,1)S(1)} %get-tuple-element.68), channel_id=1, source_target_pairs={{0,6},{2,4},{4,2},{6,0},{8,14},{10,12},{12,10},{14,8},{16,22},{18,... | collective-permute-start | bytes 196616 | tf_op jit(solution)/shard_map/ppermute | solution.py:374
  44.9 1.3 %collective-permute-start.21 = (bf16[256,128]{1,0:T(8,128)(2,1)S(1)}, bf16[256,128]{1,0:T(8,128)(2,1)S(1)}, u32[]{:S(2)}, u32[]{:S(2)}) collective-permute-start(bf16[256,128]{1,0:T(8,128)(2,1)S(1)} %get-tuple-element.74), channel_id=1, source_target_pairs={{0,2},{2,0},{4,6},{6,4},{8,10},{10,8},{12,14},{14,12},{16,18},{18,... | collective-permute-start | bytes 196616 | tf_op jit(solution)/shard_map/ppermute | solution.py:374

commit v24 on v23

--- a/solution.py
+++ b/solution.py
@@ -251,14 +251,17 @@
         high = logs.astype(jnp.bfloat16).astype(jnp.float32)
         middle = (logs - high).astype(jnp.bfloat16).astype(jnp.float32)
         low = logs - high - middle
-        picked = jnp.where(lane % HEAD == 0, high, jnp.where(lane % HEAD == 1, middle, low))
+        stats = 0.0
         for part in range(rows // width):
-            flipped = jnp.transpose(picked[part * width : (part + 1) * width])
-            stats = [flipped[h : h + STAT_ROWS // 2] for h in range(0, width, HEAD)]
-            at = rows + part * STAT_ROWS
-            results[side, j, at : at + STAT_ROWS] = jnp.concatenate(stats, axis=0).astype(
-                results.dtype
+            at = slice(part * width, (part + 1) * width)
+            picked = jnp.zeros((width, width), jnp.float32)
+            for n, piece in enumerate((high, middle, low)):
+                picked = jnp.where(lane[:width] % HEAD == 3 * part + n, piece[at], picked)
+            flipped = jnp.transpose(picked)
+            stats += jnp.concatenate(
+                [flipped[h : h + STAT_ROWS // 2] for h in range(0, width, HEAD)], axis=0
             )
+        results[side, j, rows:] = stats.astype(results.dtype)
     first[...] = results[1 - odd]
     second[...] = results[odd]
 
@@ -321,12 +324,11 @@
     def logs(side, j):
         squares = []
         for part in range(rows // width):
-            at = rows + part * STAT_ROWS
-            stats = backs[side, j, at : at + STAT_ROWS].astype(jnp.float32)
-            heads = [
-                stats[8 * h : 8 * h + 1] + stats[8 * h + 1 : 8 * h + 2] + stats[8 * h + 2 : 8 * h + 3]
-                for h in range(width // HEAD)
-            ]
+            stats = backs[side, j, rows:].astype(jnp.float32)
+            heads = []
+            for h in range(width // HEAD):
+                at = 8 * h + 3 * part
+                heads.append(stats[at : at + 1] + stats[at + 1 : at + 2] + stats[at + 2 : at + 3])
             turned = jnp.transpose(
                 jnp.concatenate([jnp.broadcast_to(x, (HEAD, width)) for x in heads], axis=0)
             )
@@ -452,7 +454,7 @@
         name="rows",
     )(*packs, *queries, *keys)
     audio_edges = halo((0,), packs, [], peaks) + halo((1,), packs, [])
-    back = shape((RADIUS, rows + rows // width * STAT_ROWS, width), bf16)
+    back = shape((RADIUS, rows + STAT_ROWS, width), bf16)
     lent_a, lent_b, edge_turned = call(
         lend_kernel,
         [back, back, shape((2 * width, around), bf16)],

time: 47.7 us -> 47.5 us (level)
  waiting for transfers between devices: 3.88 us -> 4.37 us
where the time goes in v24:
time: 47.5 us; the launch traced here: 47.3 us
  starting transfers between devices  26.1 us (55%)
  Pallas kernels  15.9 us (33%)
  waiting for transfers between devices  4.37 us (9%)
  between operations  1 us (2%)
    ppermute x15, starting transfers between devices, traded(): lax.ppermute(x, 'tm', pairs(k))  15 us
    ppermute x6, starting transfers between devices, crossed(): lax.ppermute(sent, 'tm', [(p * GROUP + i, q * GROUP + i) for p, q in pair...  9.57 us
    pallas_call x1, Pallas kernels, local(): call(rows_kernel, [shape((GROUP, rows, width), f32), shape((GROUP, 2, row...  3.19 us
    ppermute x15, waiting for transfers between devices, traded(): lax.ppermute(x, 'tm', pairs(k))  3.17 us
    pallas_call x1, Pallas kernels, local(): call(functools.partial(columns_kernel, far), [piece] * len(far) + shared,...  2.63 us
    pallas_call x1, Pallas kernels, local(): call(lend_kernel, [back, back, shape((2 * width, around), bf16)], [pltpu....  2.6 us
    pallas_call x1, Pallas kernels, local(): call(functools.partial(columns_kernel, near), [piece] * len(near), ins=[V...  2.22 us
    pallas_call x1, Pallas kernels, local(): call(prepare_kernel, [part, part, square, square], [pltpu.VMEM((rows, hal...  1.78 us
  transfers between devices with their start and end apart: 23, of which 4 were waited for; matrix products, arithmetic and copies ran while one was open for 0% of the time, Pallas kernels for 32%

profile of v24, /device:TPU:9, one launch (start us, length us, event | category | flops | bytes accessed | tf_op | source)
XLA Modules:
  0.0 47.3 jit_solution(1488347893701797715)
XLA Ops:
  0.6 1.3 %collective-permute-start.1 = (bf16[256,512]{1,0:T(8,128)(2,1)}, bf16[256,512]{1,0:T(8,128)(2,1)S(1)}, u32[]{:S(2)}, u32[]{:S(2)}) collective-permute-start(bf16[256,512]{1,0:T(8,128)(2,1)} %audio.3), channel_id=1, source_target_pairs={{0,1},{1,0},{2,3},{3,2},{4,5},{5,4},{6,7},{7,6},{8,9},{9,8},{10,11... | collective-permute-start | bytes 786440 | tf_op jit(solution)/shard_map/ppermute | solution.py:371
  1.9 0.2 collective-permute-start.7
  2.2 1.2 %split.1 = (bf16[528,128]{1,0:T(8,128)(2,1)S(1)}, bf16[528,128]{1,0:T(8,128)(2,1)S(1)}, bf16[528,128]{1,0:T(8,128)(2,1)S(1)}, bf16[528,128]{1,0:T(8,128)(2,1)S(1)}) custom-call(bf16[256,512]{1,0:T(8,128)(2,1)} %audio.3, bf16[256,512]{1,0:T(8,128)(2,1)} %video.3, s32[2,128]{1,0:T(2,128)} %bitcast.1), custom_call_target="tpu_custom_call" | custom-call | bytes 1048576 | tf_op jit(solution)/shard_map/split/pallas_call | solution.py:395
  3.3 1.3 %collective-permute-start = (bf16[528,128]{1,0:T(8,128)(2,1)S(1)}, bf16[528,128]{1,0:T(8,128)(2,1)S(1)}, u32[]{:S(2)}, u32[]{:S(2)}) collective-permute-start(bf16[528,128]{1,0:T(8,128)(2,1)S(1)} %get-tuple-element.39), channel_id=1, source_target_pairs={{0,2},{2,0},{4,6},{6,4},{8,10},{10,8},{12,14},{14,12},{16,18},{18,... | collective-permute-start | bytes 405512 | tf_op jit(solution)/shard_map/ppermute | solution.py:376
  4.6 1.2 %collective-permute-start.2 = (bf16[528,128]{1,0:T(8,128)(2,1)S(1)}, bf16[528,128]{1,0:T(8,128)(2,1)S(1)}, u32[]{:S(2)}, u32[]{:S(2)}) collective-permute-start(bf16[528,128]{1,0:T(8,128)(2,1)S(1)} %get-tuple-element.42), channel_id=1, source_target_pairs={{0,4},{2,6},{4,0},{6,2},{8,12},{10,14},{12,8},{14,10},{16,20},{18,... | collective-permute-start | bytes 405512 | tf_op jit(solution)/shard_map/ppermute | solution.py:376
  5.9 0.5 %collective-permute-start.6 = (bf16[528,128]{1,0:T(8,128)(2,1)S(1)}, bf16[528,128]{1,0:T(8,128)(2,1)S(1)}, u32[]{:S(2)}, u32[]{:S(2)}) collective-permute-start(bf16[528,128]{1,0:T(8,128)(2,1)S(1)} %get-tuple-element.48), channel_id=1, source_target_pairs={{0,6},{2,4},{4,2},{6,0},{8,14},{10,12},{12,10},{14,8},{16,22},{18,... | collective-permute-start | bytes 405512 | tf_op jit(solution)/shard_map/ppermute | solution.py:376
  6.3 0.0 collective-permute-done.refs_0_.refs_5_.refs_1_
  6.3 1.8 %prepare.1 = (f32[256,512]{1,0:T(8,128)S(1)}, f32[256,512]{1,0:T(8,128)S(1)}, bf16[512,512]{1,0:T(8,128)(2,1)S(1)}, bf16[512,512]{1,0:T(8,128)(2,1)S(1)}) custom-call(bf16[256,512]{1,0:T(8,128)(2,1)} %audio.3, bf16[256,512]{1,0:T(8,128)(2,1)} %video.3, bf16[1024,512]{1,0:T(8,128)(2,1)} %query.1, bf16[1024,512]{1,0:T(8,128)(2,1)} %key.1, ...), custom_call_target="tpu_custom_call" | custom-call | flops 268435456 | bytes 4194304 | tf_op jit(solution)/shard_map/prepare/pallas_call | solution.py:405
  8.1 1.7 %collective-permute-done.2.refs_1_.refs_6_.refs_2_ = bf16[528,128]{1,0:T(8,128)(2,1)S(1)} collective-permute-done((bf16[528,128]{1,0:T(8,128)(2,1)S(1)}, bf16[528,128]{1,0:T(8,128)(2,1)S(1)}, u32[]{:S(2)}, u32[]{:S(2)}) %collective-permute-start.2) | collective-permute-done | bytes 135200 | tf_op jit(solution)/shard_map/ppermute | solution.py:376
  9.8 0.0 collective-permute-done.1.other
  9.8 0.4 project.2
  10.2 1.4 %collective-permute-start.3 = (bf16[256,128]{1,0:T(8,128)(2,1)S(1)}, bf16[256,128]{1,0:T(8,128)(2,1)S(1)}, u32[]{:S(2)}, u32[]{:S(2)}) collective-permute-start(bf16[256,128]{1,0:T(8,128)(2,1)S(1)} %get-tuple-element.44), channel_id=1, source_target_pairs={{0,2},{2,0},{4,6},{6,4},{8,10},{10,8},{12,14},{14,12},{16,18},{18,... | collective-permute-start | bytes 196616 | tf_op jit(solution)/shard_map/ppermute | solution.py:376
  11.6 1.2 %collective-permute-start.4 = (bf16[256,128]{1,0:T(8,128)(2,1)S(1)}, bf16[256,128]{1,0:T(8,128)(2,1)S(1)}, u32[]{:S(2)}, u32[]{:S(2)}) collective-permute-start(bf16[256,128]{1,0:T(8,128)(2,1)S(1)} %get-tuple-element.45), channel_id=1, source_target_pairs={{0,4},{2,6},{4,0},{6,2},{8,12},{10,14},{12,8},{14,10},{16,20},{18,... | collective-permute-start | bytes 196616 | tf_op jit(solution)/shard_map/ppermute | solution.py:376
  12.8 0.5 %collective-permute-start.5 = (bf16[256,128]{1,0:T(8,128)(2,1)S(1)}, bf16[256,128]{1,0:T(8,128)(2,1)S(1)}, u32[]{:S(2)}, u32[]{:S(2)}) collective-permute-start(bf16[256,128]{1,0:T(8,128)(2,1)S(1)} %get-tuple-element.46), channel_id=1, source_target_pairs={{0,6},{2,4},{4,2},{6,0},{8,14},{10,12},{12,10},{14,8},{16,22},{18,... | collective-permute-start | bytes 196616 | tf_op jit(solution)/shard_map/ppermute | solution.py:376
  13.3 0.4 collective-permute-done.7.other
  13.7 0.4 project.3
  14.1 1.6 %collective-permute-start.10 = (bf16[256,128]{1,0:T(8,128)(2,1)S(1)}, bf16[256,128]{1,0:T(8,128)(2,1)S(1)}, u32[]{:S(2)}, u32[]{:S(2)}) collective-permute-start(bf16[256,128]{1,0:T(8,128)(2,1)S(1)} %get-tuple-element.54), channel_id=1, source_target_pairs={{0,2},{2,0},{4,6},{6,4},{8,10},{10,8},{12,14},{14,12},{16,18},{18,... | collective-permute-start | bytes 196616 | tf_op jit(solution)/shard_map/ppermute | solution.py:376
  15.7 0.0 collective-permute-done.6.refs_7_.refs_3_
  15.7 1.2 %collective-permute-start.11 = (bf16[256,128]{1,0:T(8,128)(2,1)S(1)}, bf16[256,128]{1,0:T(8,128)(2,1)S(1)}, u32[]{:S(2)}, u32[]{:S(2)}) collective-permute-start(bf16[256,128]{1,0:T(8,128)(2,1)S(1)} %get-tuple-element.55), channel_id=1, source_target_pairs={{0,4},{2,6},{4,0},{6,2},{8,12},{10,14},{12,8},{14,10},{16,20},{18,... | collective-permute-start | bytes 196616 | tf_op jit(solution)/shard_map/ppermute | solution.py:376
  16.9 0.0 collective-permute-done.3.refs_1_.refs_5_
  16.9 0.5 %collective-permute-start.12 = (bf16[256,128]{1,0:T(8,128)(2,1)S(1)}, bf16[256,128]{1,0:T(8,128)(2,1)S(1)}, u32[]{:S(2)}, u32[]{:S(2)}) collective-permute-start(bf16[256,128]{1,0:T(8,128)(2,1)S(1)} %get-tuple-element.56), channel_id=1, source_target_pairs={{0,6},{2,4},{4,2},{6,0},{8,14},{10,12},{12,10},{14,8},{16,22},{18,... | collective-permute-start | bytes 196616 | tf_op jit(solution)/shard_map/ppermute | solution.py:376
  17.4 0.0 collective-permute-done.4.refs_2_.refs_6_
  17.4 0.0 collective-permute-done.5.refs_3_.refs_7_
  17.4 0.1 halo.3
  17.5 3.2 %collective-permute-start.8 = (bf16[3,272,128]{2,1,0:T(8,128)(2,1)S(1)}, bf16[3,272,128]{2,1,0:T(8,128)(2,1)S(1)}, u32[]{:S(2)}, u32[]{:S(2)}) collective-permute-start(bf16[3,272,128]{2,1,0:T(8,128)(2,1)S(1)} %get-tuple-element.52), channel_id=1, source_target_pairs={{8,16},{10,18},{12,20},{14,22},{16,8},{18,10},{20,12},{22,14},{9,1... | collective-permute-start | bytes 626696 | tf_op jit(solution)/shard_map/ppermute | solution.py:382
  20.7 0.1 collective-permute-start.9
  20.8 0.1 halo.4
  20.8 0.0 collective-permute-done.10.refs_9_
  20.9 2.1 %collective-permute-start.15 = (bf16[3,256,128]{2,1,0:T(8,128)(2,1)S(1)}, bf16[3,256,128]{2,1,0:T(8,128)(2,1)S(1)}, u32[]{:S(2)}, u32[]{:S(2)}) collective-permute-start(bf16[3,256,128]{2,1,0:T(8,128)(2,1)S(1)} %halo.4), channel_id=1, source_target_pairs={{8,16},{10,18},{12,20},{14,22},{16,8},{18,10},{20,12},{22,14},{9,1... | collective-permute-start | bytes 589832 | tf_op jit(solution)/shard_map/ppermute | solution.py:382
  22.9 0.0 collective-permute-done.11.refs_10_
  23.0 0.0 collective-permute-done.12.refs_11_
  23.0 3.2 %rows.1 = (f32[4,256,128]{2,1,0:T(8,128)S(1)}, f32[4,2,256,128]{3,2,1,0:T(8,128)S(1)}, bf16[256,1024]{1,0:T(8,128)(2,1)S(1)}, bf16[1024,256]{1,0:T(8,128)(2,1)S(1)}) custom-call(bf16[528,128]{1,0:T(8,128)(2,1)S(1)} %get-tuple-element.47.refs_4_.refs_0_, bf16[528,128]{1,0:T(8,128)(2,1)S(1)} %collective-permute-done.refs_0_.refs_5_.refs_1_, ...), custom_call_target="tpu_custom_call" | custom-call | flops 2147483648 | bytes 2097152 | tf_op jit(solution)/shard_map/rows/pallas_call | solution.py:447
  26.2 0.1 halo.5
  26.2 0.1 collective-permute-start.16
  26.3 0.0 collective-permute-done.8.edge_b
  26.3 0.8 %collective-permute-done.9.edge_a = bf16[3,272,128]{2,1,0:T(8,128)(2,1)S(1)} collective-permute-done((bf16[3,272,128]{2,1,0:T(8,128)(2,1)S(1)}, bf16[3,272,128]{2,1,0:T(8,128)(2,1)S(1)}, u32[]{:S(2)}, u32[]{:S(2)}) %collective-permute-start.9) | collective-permute-done | bytes 208928 | tf_op jit(solution)/shard_map/ppermute | solution.py:382
  27.1 2.6 %lend.1 = (bf16[3,272,128]{2,1,0:T(8,128)(2,1)S(1)}, bf16[3,272,128]{2,1,0:T(8,128)(2,1)S(1)}, bf16[256,1536]{1,0:T(8,128)(2,1)S(1)}) custom-call(bf16[3,272,128]{2,1,0:T(8,128)(2,1)S(1)} %collective-permute-done.8.edge_b, bf16[3,272,128]{2,1,0:T(8,128)(2,1)S(1)} %collective-permute-done.9.edge_a, bf16[256,1024]{1,0:T(8,128)(2,1)S(1)} %get-tuple-element.57.plane_turned, ...), custom_call_target="tpu_custom_call" | custom-call | flops 4831838208 | bytes 3145728 | tf_op jit(solution)/shard_map/lend/pallas_call | solution.py:458
  29.7 0.8 %collective-permute-start.13 = (bf16[3,272,128]{2,1,0:T(8,128)(2,1)S(1)}, bf16[3,272,128]{2,1,0:T(8,128)(2,1)S(1)}, u32[]{:S(2)}, u32[]{:S(2)}) collective-permute-start(bf16[3,272,128]{2,1,0:T(8,128)(2,1)S(1)} %get-tuple-element.59), channel_id=1, source_target_pairs={{0,8},{2,10},{4,12},{6,14},{8,0},{10,2},{12,4},{14,6},{16,24},{18,... | collective-permute-start | bytes 626696 | tf_op jit(solution)/shard_map/ppermute | solution.py:382
  30.4 3.4 %collective-permute-start.14 = (bf16[3,272,128]{2,1,0:T(8,128)(2,1)S(1)}, bf16[3,272,128]{2,1,0:T(8,128)(2,1)S(1)}, u32[]{:S(2)}, u32[]{:S(2)}) collective-permute-start(bf16[3,272,128]{2,1,0:T(8,128)(2,1)S(1)} %get-tuple-element.60), channel_id=1, source_target_pairs={{8,16},{10,18},{12,20},{14,22},{16,8},{18,10},{20,12},{22,14},{9,1... | collective-permute-start | bytes 626696 | tf_op jit(solution)/shard_map/ppermute | solution.py:382
  33.8 0.0 collective-permute-done.15.refs_12_
  33.8 0.0 collective-permute-done.16.refs_13_
  33.8 2.6 %columns.2 = (bf16[256,128]{1,0:T(8,128)(2,1)S(1)}, bf16[256,128]{1,0:T(8,128)(2,1)S(1)}, bf16[256,1024]{1,0:T(8,128)(2,1)S(1)}, bf16[1024,256]{1,0:T(8,128)(2,1...) custom-call(bf16[528,128]{1,0:T(8,128)(2,1)S(1)} %get-tuple-element.47.refs_4_.refs_0_, ...), custom_call_target="tpu_custom_call" | custom-call | flops 1879048192 | bytes 1572864 | tf_op jit(solution)/shard_map/columns/pallas_call | solution.py:477
  36.5 1.3 %collective-permute-start.20 = (bf16[256,128]{1,0:T(8,128)(2,1)S(1)}, bf16[256,128]{1,0:T(8,128)(2,1)S(1)}, u32[]{:S(2)}, u32[]{:S(2)}) collective-permute-start(bf16[256,128]{1,0:T(8,128)(2,1)S(1)} %get-tuple-element.64.refs_0_), channel_id=1, source_target_pairs={{0,4},{2,6},{4,0},{6,2},{8,12},{10,14},{12,8},{14,10},{16,20},{18,... | collective-permute-start | bytes 196616 | tf_op jit(solution)/shard_map/ppermute | solution.py:376
  37.8 2.0 %collective-permute-start.22 = (bf16[256,128]{1,0:T(8,128)(2,1)S(1)}, bf16[256,128]{1,0:T(8,128)(2,1)S(1)}, u32[]{:S(2)}, u32[]{:S(2)}) collective-permute-start(bf16[256,128]{1,0:T(8,128)(2,1)S(1)} %get-tuple-element.75), channel_id=1, source_target_pairs={{0,6},{2,4},{4,2},{6,0},{8,14},{10,12},{12,10},{14,8},{16,22},{18,... | collective-permute-start | bytes 196616 | tf_op jit(solution)/shard_map/ppermute | solution.py:376
  39.7 0.0 collective-permute-done.13.back_a
  39.7 0.0 collective-permute-done.14.back_b
  39.7 0.5 %merge.1 = (bf16[256,128]{1,0:T(8,128)(2,1)S(1)}, bf16[256,128]{1,0:T(8,128)(2,1)S(1)}, bf16[256,128]{1,0:T(8,128)(2,1)S(1)}, bf16[256,128]{1,0:T(8,128)(2,1)S(1)}) custom-call(bf16[3,272,128]{2,1,0:T(8,128)(2,1)S(1)} %collective-permute-done.13.back_a, bf16[3,272,128]{2,1,0:T(8,128)(2,1)S(1)} %collective-permute-done.14.back_b, ...), custom_call_target="tpu_custom_call" | custom-call | bytes 2097152 | tf_op jit(solution)/shard_map/merge/pallas_call | solution.py:480
  40.2 0.2 collective-permute-start.17
  40.5 1.2 %collective-permute-start.18 = (bf16[256,128]{1,0:T(8,128)(2,1)S(1)}, bf16[256,128]{1,0:T(8,128)(2,1)S(1)}, u32[]{:S(2)}, u32[]{:S(2)}) collective-permute-start(bf16[256,128]{1,0:T(8,128)(2,1)S(1)} %get-tuple-element.67), channel_id=1, source_target_pairs={{0,4},{2,6},{4,0},{6,2},{8,12},{10,14},{12,8},{14,10},{16,20},{18,... | collective-permute-start | bytes 196616 | tf_op jit(solution)/shard_map/ppermute | solution.py:376
  41.7 0.8 %collective-permute-start.19 = (bf16[256,128]{1,0:T(8,128)(2,1)S(1)}, bf16[256,128]{1,0:T(8,128)(2,1)S(1)}, u32[]{:S(2)}, u32[]{:S(2)}) collective-permute-start(bf16[256,128]{1,0:T(8,128)(2,1)S(1)} %get-tuple-element.68), channel_id=1, source_target_pairs={{0,6},{2,4},{4,2},{6,0},{8,14},{10,12},{12,10},{14,8},{16,22},{18,... | collective-permute-start | bytes 196616 | tf_op jit(solution)/shard_map/ppermute | solution.py:376
  42.5 0.0 collective-permute-done.20.refs_5_.refs_6_
  42.5 2.2 %columns.3 = (bf16[256,128]{1,0:T(8,128)(2,1)S(1)}, bf16[256,128]{1,0:T(8,128)(2,1)S(1)}) custom-call(bf16[256,1536]{1,0:T(8,128)(2,1)S(1)} %get-tuple-element.63.refs_14_.refs_0_, bf16[256,1024]{1,0:T(8,128)(2,1)S(1)} %get-tuple-element.69.refs_1_, bf16[1024,256]{1,0:T(8,128)(2,1)S(1)} %get-tuple-element.70.refs_2_, ...), custom_call_target="tpu_custom_call" | custom-call | flops 1879048192 | bytes 1572864 | tf_op jit(solution)/shard_map/columns/pallas_call | solution.py:491
  44.7 0.1 collective-permute-start.21
  44.8 0.0 collective-permute-done.22.refs_7_
  44.8 0.0 collective-permute-done.17.refs_1_
  44.8 0.0 collective-permute-done.18.refs_2_
  44.8 1.5 %collective-permute-done.19.refs_3_ = bf16[256,128]{1,0:T(8,128)(2,1)S(1)} collective-permute-done((bf16[256,128]{1,0:T(8,128)(2,1)S(1)}, bf16[256,128]{1,0:T(8,128)(2,1)S(1)}, u32[]{:S(2)}, u32[]{:S(2)}) %collective-permute-start.19) | collective-permute-done | bytes 65568 | tf_op jit(solution)/shard_map/ppermute | solution.py:376
  46.3 0.0 collective-permute-done.21.refs_5_
  46.3 0.8 %join.1 = (bf16[256,512]{1,0:T(8,128)(2,1)}, bf16[256,512]{1,0:T(8,128)(2,1)}) custom-call(bf16[256,128]{1,0:T(8,128)(2,1)S(1)} %get-tuple-element.65.refs_6_.refs_0_, bf16[256,128]{1,0:T(8,128)(2,1)S(1)} %collective-permute-done.17.refs_1_, bf16[256,128]{1,0:T(8,128)(2,1)S(1)} %collective-permute-done.18.refs_2_, ...), custom_call_target="tpu_custom_call" | custom-call | bytes 1048576 | tf_op jit(solution)/shard_map/join/pallas_call | solution.py:499
Async XLA Ops:
  0.6 9.2 %collective-permute-start.1 = (bf16[256,512]{1,0:T(8,128)(2,1)}, bf16[256,512]{1,0:T(8,128)(2,1)S(1)}, u32[]{:S(2)}, u32[]{:S(2)}) collective-permute-start(bf16[256,512]{1,0:T(8,128)(2,1)} %audio.3), channel_id=1, source_target_pairs={{0,1},{1,0},{2,3},{3,2},{4,5},{5,4},{6,7},{7,6},{8,9},{9,8},{10,11... | collective-permute-start | bytes 786440 | tf_op jit(solution)/shard_map/ppermute | solution.py:371
  1.9 11.8 %collective-permute-start.7 = (bf16[256,512]{1,0:T(8,128)(2,1)}, bf16[256,512]{1,0:T(8,128)(2,1)S(1)}, u32[]{:S(2)}, u32[]{:S(2)}) collective-permute-start(bf16[256,512]{1,0:T(8,128)(2,1)} %video.3), channel_id=1, source_target_pairs={{0,1},{1,0},{2,3},{3,2},{4,5},{5,4},{6,7},{7,6},{8,9},{9,8},{10,11... | collective-permute-start | bytes 786440 | tf_op jit(solution)/shard_map/ppermute | solution.py:371
  3.3 3.0 %collective-permute-start = (bf16[528,128]{1,0:T(8,128)(2,1)S(1)}, bf16[528,128]{1,0:T(8,128)(2,1)S(1)}, u32[]{:S(2)}, u32[]{:S(2)}) collective-permute-start(bf16[528,128]{1,0:T(8,128)(2,1)S(1)} %get-tuple-element.39), channel_id=1, source_target_pairs={{0,2},{2,0},{4,6},{6,4},{8,10},{10,8},{12,14},{14,12},{16,18},{18,... | collective-permute-start | bytes 405512 | tf_op jit(solution)/shard_map/ppermute | solution.py:376
  4.6 5.2 %collective-permute-start.2 = (bf16[528,128]{1,0:T(8,128)(2,1)S(1)}, bf16[528,128]{1,0:T(8,128)(2,1)S(1)}, u32[]{:S(2)}, u32[]{:S(2)}) collective-permute-start(bf16[528,128]{1,0:T(8,128)(2,1)S(1)} %get-tuple-element.42), channel_id=1, source_target_pairs={{0,4},{2,6},{4,0},{6,2},{8,12},{10,14},{12,8},{14,10},{16,20},{18,... | collective-permute-start | bytes 405512 | tf_op jit(solution)/shard_map/ppermute | solution.py:376
  5.9 9.8 %collective-permute-start.6 = (bf16[528,128]{1,0:T(8,128)(2,1)S(1)}, bf16[528,128]{1,0:T(8,128)(2,1)S(1)}, u32[]{:S(2)}, u32[]{:S(2)}) collective-permute-start(bf16[528,128]{1,0:T(8,128)(2,1)S(1)} %get-tuple-element.48), channel_id=1, source_target_pairs={{0,6},{2,4},{4,2},{6,0},{8,14},{10,12},{12,10},{14,8},{16,22},{18,... | collective-permute-start | bytes 405512 | tf_op jit(solution)/shard_map/ppermute | solution.py:376
  10.2 6.7 %collective-permute-start.3 = (bf16[256,128]{1,0:T(8,128)(2,1)S(1)}, bf16[256,128]{1,0:T(8,128)(2,1)S(1)}, u32[]{:S(2)}, u32[]{:S(2)}) collective-permute-start(bf16[256,128]{1,0:T(8,128)(2,1)S(1)} %get-tuple-element.44), channel_id=1, source_target_pairs={{0,2},{2,0},{4,6},{6,4},{8,10},{10,8},{12,14},{14,12},{16,18},{18,... | collective-permute-start | bytes 196616 | tf_op jit(solution)/shard_map/ppermute | solution.py:376
  11.6 5.9 %collective-permute-start.4 = (bf16[256,128]{1,0:T(8,128)(2,1)S(1)}, bf16[256,128]{1,0:T(8,128)(2,1)S(1)}, u32[]{:S(2)}, u32[]{:S(2)}) collective-permute-start(bf16[256,128]{1,0:T(8,128)(2,1)S(1)} %get-tuple-element.45), channel_id=1, source_target_pairs={{0,4},{2,6},{4,0},{6,2},{8,12},{10,14},{12,8},{14,10},{16,20},{18,... | collective-permute-start | bytes 196616 | tf_op jit(solution)/shard_map/ppermute | solution.py:376
  12.8 4.6 %collective-permute-start.5 = (bf16[256,128]{1,0:T(8,128)(2,1)S(1)}, bf16[256,128]{1,0:T(8,128)(2,1)S(1)}, u32[]{:S(2)}, u32[]{:S(2)}) collective-permute-start(bf16[256,128]{1,0:T(8,128)(2,1)S(1)} %get-tuple-element.46), channel_id=1, source_target_pairs={{0,6},{2,4},{4,2},{6,0},{8,14},{10,12},{12,10},{14,8},{16,22},{18,... | collective-permute-start | bytes 196616 | tf_op jit(solution)/shard_map/ppermute | solution.py:376
  14.1 6.8 %collective-permute-start.10 = (bf16[256,128]{1,0:T(8,128)(2,1)S(1)}, bf16[256,128]{1,0:T(8,128)(2,1)S(1)}, u32[]{:S(2)}, u32[]{:S(2)}) collective-permute-start(bf16[256,128]{1,0:T(8,128)(2,1)S(1)} %get-tuple-element.54), channel_id=1, source_target_pairs={{0,2},{2,0},{4,6},{6,4},{8,10},{10,8},{12,14},{14,12},{16,18},{18,... | collective-permute-start | bytes 196616 | tf_op jit(solution)/shard_map/ppermute | solution.py:376
  15.7 7.2 %collective-permute-start.11 = (bf16[256,128]{1,0:T(8,128)(2,1)S(1)}, bf16[256,128]{1,0:T(8,128)(2,1)S(1)}, u32[]{:S(2)}, u32[]{:S(2)}) collective-permute-start(bf16[256,128]{1,0:T(8,128)(2,1)S(1)} %get-tuple-element.55), channel_id=1, source_target_pairs={{0,4},{2,6},{4,0},{6,2},{8,12},{10,14},{12,8},{14,10},{16,20},{18,... | collective-permute-start | bytes 196616 | tf_op jit(solution)/shard_map/ppermute | solution.py:376
  16.9 6.0 %collective-permute-start.12 = (bf16[256,128]{1,0:T(8,128)(2,1)S(1)}, bf16[256,128]{1,0:T(8,128)(2,1)S(1)}, u32[]{:S(2)}, u32[]{:S(2)}) collective-permute-start(bf16[256,128]{1,0:T(8,128)(2,1)S(1)} %get-tuple-element.56), channel_id=1, source_target_pairs={{0,6},{2,4},{4,2},{6,0},{8,14},{10,12},{12,10},{14,8},{16,22},{18,... | collective-permute-start | bytes 196616 | tf_op jit(solution)/shard_map/ppermute | solution.py:376
  17.5 8.8 %collective-permute-start.8 = (bf16[3,272,128]{2,1,0:T(8,128)(2,1)S(1)}, bf16[3,272,128]{2,1,0:T(8,128)(2,1)S(1)}, u32[]{:S(2)}, u32[]{:S(2)}) collective-permute-start(bf16[3,272,128]{2,1,0:T(8,128)(2,1)S(1)} %get-tuple-element.52), channel_id=1, source_target_pairs={{8,16},{10,18},{12,20},{14,22},{16,8},{18,10},{20,12},{22,14},{9,1... | collective-permute-start | bytes 626696 | tf_op jit(solution)/shard_map/ppermute | solution.py:382
  20.7 6.4 %collective-permute-start.9 = (bf16[3,272,128]{2,1,0:T(8,128)(2,1)S(1)}, bf16[3,272,128]{2,1,0:T(8,128)(2,1)S(1)}, u32[]{:S(2)}, u32[]{:S(2)}) collective-permute-start(bf16[3,272,128]{2,1,0:T(8,128)(2,1)S(1)} %get-tuple-element.53), channel_id=1, source_target_pairs={{0,8},{2,10},{4,12},{6,14},{8,0},{10,2},{12,4},{14,6},{16,24},{18,... | collective-permute-start | bytes 626696 | tf_op jit(solution)/shard_map/ppermute | solution.py:382
  20.9 13.0 %collective-permute-start.15 = (bf16[3,256,128]{2,1,0:T(8,128)(2,1)S(1)}, bf16[3,256,128]{2,1,0:T(8,128)(2,1)S(1)}, u32[]{:S(2)}, u32[]{:S(2)}) collective-permute-start(bf16[3,256,128]{2,1,0:T(8,128)(2,1)S(1)} %halo.4), channel_id=1, source_target_pairs={{8,16},{10,18},{12,20},{14,22},{16,8},{18,10},{20,12},{22,14},{9,1... | collective-permute-start | bytes 589832 | tf_op jit(solution)/shard_map/ppermute | solution.py:382
  26.2 7.6 %collective-permute-start.16 = (bf16[3,256,128]{2,1,0:T(8,128)(2,1)S(1)}, bf16[3,256,128]{2,1,0:T(8,128)(2,1)S(1)}, u32[]{:S(2)}, u32[]{:S(2)}) collective-permute-start(bf16[3,256,128]{2,1,0:T(8,128)(2,1)S(1)} %halo.5), channel_id=1, source_target_pairs={{0,8},{2,10},{4,12},{6,14},{8,0},{10,2},{12,4},{14,6},{16,24},{18,... | collective-permute-start | bytes 589832 | tf_op jit(solution)/shard_map/ppermute | solution.py:382
  29.7 10.1 %collective-permute-start.13 = (bf16[3,272,128]{2,1,0:T(8,128)(2,1)S(1)}, bf16[3,272,128]{2,1,0:T(8,128)(2,1)S(1)}, u32[]{:S(2)}, u32[]{:S(2)}) collective-permute-start(bf16[3,272,128]{2,1,0:T(8,128)(2,1)S(1)} %get-tuple-element.59), channel_id=1, source_target_pairs={{0,8},{2,10},{4,12},{6,14},{8,0},{10,2},{12,4},{14,6},{16,24},{18,... | collective-permute-start | bytes 626696 | tf_op jit(solution)/shard_map/ppermute | solution.py:382
  30.4 9.3 %collective-permute-start.14 = (bf16[3,272,128]{2,1,0:T(8,128)(2,1)S(1)}, bf16[3,272,128]{2,1,0:T(8,128)(2,1)S(1)}, u32[]{:S(2)}, u32[]{:S(2)}) collective-permute-start(bf16[3,272,128]{2,1,0:T(8,128)(2,1)S(1)} %get-tuple-element.60), channel_id=1, source_target_pairs={{8,16},{10,18},{12,20},{14,22},{16,8},{18,10},{20,12},{22,14},{9,1... | collective-permute-start | bytes 626696 | tf_op jit(solution)/shard_map/ppermute | solution.py:382
  36.5 6.0 %collective-permute-start.20 = (bf16[256,128]{1,0:T(8,128)(2,1)S(1)}, bf16[256,128]{1,0:T(8,128)(2,1)S(1)}, u32[]{:S(2)}, u32[]{:S(2)}) collective-permute-start(bf16[256,128]{1,0:T(8,128)(2,1)S(1)} %get-tuple-element.64.refs_0_), channel_id=1, source_target_pairs={{0,4},{2,6},{4,0},{6,2},{8,12},{10,14},{12,8},{14,10},{16,20},{18,... | collective-permute-start | bytes 196616 | tf_op jit(solution)/shard_map/ppermute | solution.py:376
  37.8 7.0 %collective-permute-start.22 = (bf16[256,128]{1,0:T(8,128)(2,1)S(1)}, bf16[256,128]{1,0:T(8,128)(2,1)S(1)}, u32[]{:S(2)}, u32[]{:S(2)}) collective-permute-start(bf16[256,128]{1,0:T(8,128)(2,1)S(1)} %get-tuple-element.75), channel_id=1, source_target_pairs={{0,6},{2,4},{4,2},{6,0},{8,14},{10,12},{12,10},{14,8},{16,22},{18,... | collective-permute-start | bytes 196616 | tf_op jit(solution)/shard_map/ppermute | solution.py:376
  40.2 4.5 %collective-permute-start.17 = (bf16[256,128]{1,0:T(8,128)(2,1)S(1)}, bf16[256,128]{1,0:T(8,128)(2,1)S(1)}, u32[]{:S(2)}, u32[]{:S(2)}) collective-permute-start(bf16[256,128]{1,0:T(8,128)(2,1)S(1)} %get-tuple-element.66), channel_id=1, source_target_pairs={{0,2},{2,0},{4,6},{6,4},{8,10},{10,8},{12,14},{14,12},{16,18},{18,... | collective-permute-start | bytes 196616 | tf_op jit(solution)/shard_map/ppermute | solution.py:376
  40.5 4.3 %collective-permute-start.18 = (bf16[256,128]{1,0:T(8,128)(2,1)S(1)}, bf16[256,128]{1,0:T(8,128)(2,1)S(1)}, u32[]{:S(2)}, u32[]{:S(2)}) collective-permute-start(bf16[256,128]{1,0:T(8,128)(2,1)S(1)} %get-tuple-element.67), channel_id=1, source_target_pairs={{0,4},{2,6},{4,0},{6,2},{8,12},{10,14},{12,8},{14,10},{16,20},{18,... | collective-permute-start | bytes 196616 | tf_op jit(solution)/shard_map/ppermute | solution.py:376
  41.7 4.6 %collective-permute-start.19 = (bf16[256,128]{1,0:T(8,128)(2,1)S(1)}, bf16[256,128]{1,0:T(8,128)(2,1)S(1)}, u32[]{:S(2)}, u32[]{:S(2)}) collective-permute-start(bf16[256,128]{1,0:T(8,128)(2,1)S(1)} %get-tuple-element.68), channel_id=1, source_target_pairs={{0,6},{2,4},{4,2},{6,0},{8,14},{10,12},{12,10},{14,8},{16,22},{18,... | collective-permute-start | bytes 196616 | tf_op jit(solution)/shard_map/ppermute | solution.py:376
  44.7 1.6 %collective-permute-start.21 = (bf16[256,128]{1,0:T(8,128)(2,1)S(1)}, bf16[256,128]{1,0:T(8,128)(2,1)S(1)}, u32[]{:S(2)}, u32[]{:S(2)}) collective-permute-start(bf16[256,128]{1,0:T(8,128)(2,1)S(1)} %get-tuple-element.74), channel_id=1, source_target_pairs={{0,2},{2,0},{4,6},{6,4},{8,10},{10,8},{12,14},{14,12},{16,18},{18,... | collective-permute-start | bytes 196616 | tf_op jit(solution)/shard_map/ppermute | solution.py:376

commit v25 on v24

--- a/solution.py
+++ b/solution.py
@@ -228,7 +228,7 @@
     blocks = [slice(0, (j + 1) * rows) for j in range(RADIUS)]
     blocks += [slice((j + 1) * rows, GROUP * rows) for j in range(RADIUS)]
 
-    def scores_of(e):
+    def ask_of(e):
         side, j = e // RADIUS, e % RADIUS
         marks = marks_turned(ordered[side, j, rows:])
         query = ordered[side, j, :rows]
@@ -236,7 +236,12 @@
             at = slice(e * rows + part * width, e * rows + (part + 1) * width)
             turned[:width, at] = jnp.transpose(query[part * width : (part + 1) * width])
             turned[width:, at] = x
-        return product(stacked_ask(query, marks), plane_turned[:, blocks[e]])
+        return stacked_ask(query, marks)
+
+    asks = [ask_of(e) for e in range(2 * RADIUS)]
+
+    def scores_of(e):
+        return product(asks[e], plane_turned[:, blocks[e]])
 
     ahead = scores_of(0)
     for e in range(2 * RADIUS):

time: 47.5 us -> 47.5 us (level)
  no operation moved by 1% of the time
where the time goes in v25:
time: 47.5 us; the launch traced here: 47.2 us
  starting transfers between devices  26.1 us (55%)
  Pallas kernels  15.8 us (33%)
  waiting for transfers between devices  4.38 us (9%)
  between operations  1 us (2%)
    ppermute x15, starting transfers between devices, traded(): lax.ppermute(x, 'tm', pairs(k))  14.9 us
    ppermute x6, starting transfers between devices, crossed(): lax.ppermute(sent, 'tm', [(p * GROUP + i, q * GROUP + i) for p, q in pair...  9.57 us
    pallas_call x1, Pallas kernels, local(): call(rows_kernel, [shape((GROUP, rows, width), f32), shape((GROUP, 2, row...  3.19 us
    ppermute x15, waiting for transfers between devices, traded(): lax.ppermute(x, 'tm', pairs(k))  3.17 us
    pallas_call x1, Pallas kernels, local(): call(functools.partial(columns_kernel, far), [piece] * len(far) + shared,...  2.63 us
    pallas_call x1, Pallas kernels, local(): call(lend_kernel, [back, back, shape((2 * width, around), bf16)], [pltpu....  2.56 us
    pallas_call x1, Pallas kernels, local(): call(functools.partial(columns_kernel, near), [piece] * len(near), ins=[V...  2.22 us
    pallas_call x1, Pallas kernels, local(): call(prepare_kernel, [part, part, square, square], [pltpu.VMEM((rows, hal...  1.78 us
  transfers between devices with their start and end apart: 23, of which 4 were waited for; matrix products, arithmetic and copies ran while one was open for 0% of the time, Pallas kernels for 32%

profile of v25, /device:TPU:9, one launch (start us, length us, event | category | flops | bytes accessed | tf_op | source)
XLA Modules:
  0.0 47.2 jit_solution(986766346329674006)
XLA Ops:
  0.6 1.3 %collective-permute-start.1 = (bf16[256,512]{1,0:T(8,128)(2,1)}, bf16[256,512]{1,0:T(8,128)(2,1)S(1)}, u32[]{:S(2)}, u32[]{:S(2)}) collective-permute-start(bf16[256,512]{1,0:T(8,128)(2,1)} %audio.3), channel_id=1, source_target_pairs={{0,1},{1,0},{2,3},{3,2},{4,5},{5,4},{6,7},{7,6},{8,9},{9,8},{10,11... | collective-permute-start | bytes 786440 | tf_op jit(solution)/shard_map/ppermute | solution.py:376
  1.9 0.2 collective-permute-start.7
  2.2 1.2 %split.1 = (bf16[528,128]{1,0:T(8,128)(2,1)S(1)}, bf16[528,128]{1,0:T(8,128)(2,1)S(1)}, bf16[528,128]{1,0:T(8,128)(2,1)S(1)}, bf16[528,128]{1,0:T(8,128)(2,1)S(1)}) custom-call(bf16[256,512]{1,0:T(8,128)(2,1)} %audio.3, bf16[256,512]{1,0:T(8,128)(2,1)} %video.3, s32[2,128]{1,0:T(2,128)} %bitcast.1), custom_call_target="tpu_custom_call" | custom-call | bytes 1048576 | tf_op jit(solution)/shard_map/split/pallas_call | solution.py:400
  3.3 1.3 %collective-permute-start = (bf16[528,128]{1,0:T(8,128)(2,1)S(1)}, bf16[528,128]{1,0:T(8,128)(2,1)S(1)}, u32[]{:S(2)}, u32[]{:S(2)}) collective-permute-start(bf16[528,128]{1,0:T(8,128)(2,1)S(1)} %get-tuple-element.39), channel_id=1, source_target_pairs={{0,2},{2,0},{4,6},{6,4},{8,10},{10,8},{12,14},{14,12},{16,18},{18,... | collective-permute-start | bytes 405512 | tf_op jit(solution)/shard_map/ppermute | solution.py:381
  4.6 1.2 %collective-permute-start.2 = (bf16[528,128]{1,0:T(8,128)(2,1)S(1)}, bf16[528,128]{1,0:T(8,128)(2,1)S(1)}, u32[]{:S(2)}, u32[]{:S(2)}) collective-permute-start(bf16[528,128]{1,0:T(8,128)(2,1)S(1)} %get-tuple-element.42), channel_id=1, source_target_pairs={{0,4},{2,6},{4,0},{6,2},{8,12},{10,14},{12,8},{14,10},{16,20},{18,... | collective-permute-start | bytes 405512 | tf_op jit(solution)/shard_map/ppermute | solution.py:381
  5.9 0.5 %collective-permute-start.6 = (bf16[528,128]{1,0:T(8,128)(2,1)S(1)}, bf16[528,128]{1,0:T(8,128)(2,1)S(1)}, u32[]{:S(2)}, u32[]{:S(2)}) collective-permute-start(bf16[528,128]{1,0:T(8,128)(2,1)S(1)} %get-tuple-element.48), channel_id=1, source_target_pairs={{0,6},{2,4},{4,2},{6,0},{8,14},{10,12},{12,10},{14,8},{16,22},{18,... | collective-permute-start | bytes 405512 | tf_op jit(solution)/shard_map/ppermute | solution.py:381
  6.3 0.0 collective-permute-done.refs_0_.refs_5_.refs_1_
  6.3 1.8 %prepare.1 = (f32[256,512]{1,0:T(8,128)S(1)}, f32[256,512]{1,0:T(8,128)S(1)}, bf16[512,512]{1,0:T(8,128)(2,1)S(1)}, bf16[512,512]{1,0:T(8,128)(2,1)S(1)}) custom-call(bf16[256,512]{1,0:T(8,128)(2,1)} %audio.3, bf16[256,512]{1,0:T(8,128)(2,1)} %video.3, bf16[1024,512]{1,0:T(8,128)(2,1)} %query.1, bf16[1024,512]{1,0:T(8,128)(2,1)} %key.1, ...), custom_call_target="tpu_custom_call" | custom-call | flops 268435456 | bytes 4194304 | tf_op jit(solution)/shard_map/prepare/pallas_call | solution.py:410
  8.1 1.7 %collective-permute-done.2.refs_1_.refs_6_.refs_2_ = bf16[528,128]{1,0:T(8,128)(2,1)S(1)} collective-permute-done((bf16[528,128]{1,0:T(8,128)(2,1)S(1)}, bf16[528,128]{1,0:T(8,128)(2,1)S(1)}, u32[]{:S(2)}, u32[]{:S(2)}) %collective-permute-start.2) | collective-permute-done | bytes 135200 | tf_op jit(solution)/shard_map/ppermute | solution.py:381
  9.8 0.0 collective-permute-done.1.other
  9.8 0.4 project.2
  10.2 1.4 %collective-permute-start.3 = (bf16[256,128]{1,0:T(8,128)(2,1)S(1)}, bf16[256,128]{1,0:T(8,128)(2,1)S(1)}, u32[]{:S(2)}, u32[]{:S(2)}) collective-permute-start(bf16[256,128]{1,0:T(8,128)(2,1)S(1)} %get-tuple-element.44), channel_id=1, source_target_pairs={{0,2},{2,0},{4,6},{6,4},{8,10},{10,8},{12,14},{14,12},{16,18},{18,... | collective-permute-start | bytes 196616 | tf_op jit(solution)/shard_map/ppermute | solution.py:381
  11.6 1.2 %collective-permute-start.4 = (bf16[256,128]{1,0:T(8,128)(2,1)S(1)}, bf16[256,128]{1,0:T(8,128)(2,1)S(1)}, u32[]{:S(2)}, u32[]{:S(2)}) collective-permute-start(bf16[256,128]{1,0:T(8,128)(2,1)S(1)} %get-tuple-element.45), channel_id=1, source_target_pairs={{0,4},{2,6},{4,0},{6,2},{8,12},{10,14},{12,8},{14,10},{16,20},{18,... | collective-permute-start | bytes 196616 | tf_op jit(solution)/shard_map/ppermute | solution.py:381
  12.8 0.5 %collective-permute-start.5 = (bf16[256,128]{1,0:T(8,128)(2,1)S(1)}, bf16[256,128]{1,0:T(8,128)(2,1)S(1)}, u32[]{:S(2)}, u32[]{:S(2)}) collective-permute-start(bf16[256,128]{1,0:T(8,128)(2,1)S(1)} %get-tuple-element.46), channel_id=1, source_target_pairs={{0,6},{2,4},{4,2},{6,0},{8,14},{10,12},{12,10},{14,8},{16,22},{18,... | collective-permute-start | bytes 196616 | tf_op jit(solution)/shard_map/ppermute | solution.py:381
  13.3 0.4 collective-permute-done.7.other
  13.7 0.4 project.3
  14.1 1.6 %collective-permute-start.10 = (bf16[256,128]{1,0:T(8,128)(2,1)S(1)}, bf16[256,128]{1,0:T(8,128)(2,1)S(1)}, u32[]{:S(2)}, u32[]{:S(2)}) collective-permute-start(bf16[256,128]{1,0:T(8,128)(2,1)S(1)} %get-tuple-element.54), channel_id=1, source_target_pairs={{0,2},{2,0},{4,6},{6,4},{8,10},{10,8},{12,14},{14,12},{16,18},{18,... | collective-permute-start | bytes 196616 | tf_op jit(solution)/shard_map/ppermute | solution.py:381
  15.7 0.0 collective-permute-done.6.refs_7_.refs_3_
  15.7 1.2 %collective-permute-start.11 = (bf16[256,128]{1,0:T(8,128)(2,1)S(1)}, bf16[256,128]{1,0:T(8,128)(2,1)S(1)}, u32[]{:S(2)}, u32[]{:S(2)}) collective-permute-start(bf16[256,128]{1,0:T(8,128)(2,1)S(1)} %get-tuple-element.55), channel_id=1, source_target_pairs={{0,4},{2,6},{4,0},{6,2},{8,12},{10,14},{12,8},{14,10},{16,20},{18,... | collective-permute-start | bytes 196616 | tf_op jit(solution)/shard_map/ppermute | solution.py:381
  16.9 0.0 collective-permute-done.3.refs_1_.refs_5_
  16.9 0.5 %collective-permute-start.12 = (bf16[256,128]{1,0:T(8,128)(2,1)S(1)}, bf16[256,128]{1,0:T(8,128)(2,1)S(1)}, u32[]{:S(2)}, u32[]{:S(2)}) collective-permute-start(bf16[256,128]{1,0:T(8,128)(2,1)S(1)} %get-tuple-element.56), channel_id=1, source_target_pairs={{0,6},{2,4},{4,2},{6,0},{8,14},{10,12},{12,10},{14,8},{16,22},{18,... | collective-permute-start | bytes 196616 | tf_op jit(solution)/shard_map/ppermute | solution.py:381
  17.4 0.0 collective-permute-done.4.refs_2_.refs_6_
  17.4 0.0 collective-permute-done.5.refs_3_.refs_7_
  17.4 0.1 halo.3
  17.5 3.2 %collective-permute-start.8 = (bf16[3,272,128]{2,1,0:T(8,128)(2,1)S(1)}, bf16[3,272,128]{2,1,0:T(8,128)(2,1)S(1)}, u32[]{:S(2)}, u32[]{:S(2)}) collective-permute-start(bf16[3,272,128]{2,1,0:T(8,128)(2,1)S(1)} %get-tuple-element.52), channel_id=1, source_target_pairs={{8,16},{10,18},{12,20},{14,22},{16,8},{18,10},{20,12},{22,14},{9,1... | collective-permute-start | bytes 626696 | tf_op jit(solution)/shard_map/ppermute | solution.py:387
  20.7 0.1 collective-permute-start.9
  20.8 0.1 halo.4
  20.8 0.0 collective-permute-done.10.refs_9_
  20.9 2.1 %collective-permute-start.15 = (bf16[3,256,128]{2,1,0:T(8,128)(2,1)S(1)}, bf16[3,256,128]{2,1,0:T(8,128)(2,1)S(1)}, u32[]{:S(2)}, u32[]{:S(2)}) collective-permute-start(bf16[3,256,128]{2,1,0:T(8,128)(2,1)S(1)} %halo.4), channel_id=1, source_target_pairs={{8,16},{10,18},{12,20},{14,22},{16,8},{18,10},{20,12},{22,14},{9,1... | collective-permute-start | bytes 589832 | tf_op jit(solution)/shard_map/ppermute | solution.py:387
  22.9 0.0 collective-permute-done.11.refs_10_
  23.0 0.0 collective-permute-done.12.refs_11_
  23.0 3.2 %rows.1 = (f32[4,256,128]{2,1,0:T(8,128)S(1)}, f32[4,2,256,128]{3,2,1,0:T(8,128)S(1)}, bf16[256,1024]{1,0:T(8,128)(2,1)S(1)}, bf16[1024,256]{1,0:T(8,128)(2,1)S(1)}) custom-call(bf16[528,128]{1,0:T(8,128)(2,1)S(1)} %get-tuple-element.47.refs_4_.refs_0_, bf16[528,128]{1,0:T(8,128)(2,1)S(1)} %collective-permute-done.refs_0_.refs_5_.refs_1_, ...), custom_call_target="tpu_custom_call" | custom-call | flops 2147483648 | bytes 2097152 | tf_op jit(solution)/shard_map/rows/pallas_call | solution.py:452
  26.2 0.1 halo.5
  26.2 0.1 collective-permute-start.16
  26.3 0.0 collective-permute-done.8.edge_b
  26.3 0.8 %collective-permute-done.9.edge_a = bf16[3,272,128]{2,1,0:T(8,128)(2,1)S(1)} collective-permute-done((bf16[3,272,128]{2,1,0:T(8,128)(2,1)S(1)}, bf16[3,272,128]{2,1,0:T(8,128)(2,1)S(1)}, u32[]{:S(2)}, u32[]{:S(2)}) %collective-permute-start.9) | collective-permute-done | bytes 208928 | tf_op jit(solution)/shard_map/ppermute | solution.py:387
  27.1 2.6 %lend.1 = (bf16[3,272,128]{2,1,0:T(8,128)(2,1)S(1)}, bf16[3,272,128]{2,1,0:T(8,128)(2,1)S(1)}, bf16[256,1536]{1,0:T(8,128)(2,1)S(1)}) custom-call(bf16[3,272,128]{2,1,0:T(8,128)(2,1)S(1)} %collective-permute-done.8.edge_b, bf16[3,272,128]{2,1,0:T(8,128)(2,1)S(1)} %collective-permute-done.9.edge_a, bf16[256,1024]{1,0:T(8,128)(2,1)S(1)} %get-tuple-element.57.plane_turned, ...), custom_call_target="tpu_custom_call" | custom-call | flops 4831838208 | bytes 3145728 | tf_op jit(solution)/shard_map/lend/pallas_call | solution.py:463
  29.6 0.8 %collective-permute-start.13 = (bf16[3,272,128]{2,1,0:T(8,128)(2,1)S(1)}, bf16[3,272,128]{2,1,0:T(8,128)(2,1)S(1)}, u32[]{:S(2)}, u32[]{:S(2)}) collective-permute-start(bf16[3,272,128]{2,1,0:T(8,128)(2,1)S(1)} %get-tuple-element.59), channel_id=1, source_target_pairs={{0,8},{2,10},{4,12},{6,14},{8,0},{10,2},{12,4},{14,6},{16,24},{18,... | collective-permute-start | bytes 626696 | tf_op jit(solution)/shard_map/ppermute | solution.py:387
  30.4 3.4 %collective-permute-start.14 = (bf16[3,272,128]{2,1,0:T(8,128)(2,1)S(1)}, bf16[3,272,128]{2,1,0:T(8,128)(2,1)S(1)}, u32[]{:S(2)}, u32[]{:S(2)}) collective-permute-start(bf16[3,272,128]{2,1,0:T(8,128)(2,1)S(1)} %get-tuple-element.60), channel_id=1, source_target_pairs={{8,16},{10,18},{12,20},{14,22},{16,8},{18,10},{20,12},{22,14},{9,1... | collective-permute-start | bytes 626696 | tf_op jit(solution)/shard_map/ppermute | solution.py:387
  33.8 0.0 collective-permute-done.15.refs_12_
  33.8 0.0 collective-permute-done.16.refs_13_
  33.8 2.6 %columns.2 = (bf16[256,128]{1,0:T(8,128)(2,1)S(1)}, bf16[256,128]{1,0:T(8,128)(2,1)S(1)}, bf16[256,1024]{1,0:T(8,128)(2,1)S(1)}, bf16[1024,256]{1,0:T(8,128)(2,1...) custom-call(bf16[528,128]{1,0:T(8,128)(2,1)S(1)} %get-tuple-element.47.refs_4_.refs_0_, ...), custom_call_target="tpu_custom_call" | custom-call | flops 1879048192 | bytes 1572864 | tf_op jit(solution)/shard_map/columns/pallas_call | solution.py:482
  36.4 1.3 %collective-permute-start.20 = (bf16[256,128]{1,0:T(8,128)(2,1)S(1)}, bf16[256,128]{1,0:T(8,128)(2,1)S(1)}, u32[]{:S(2)}, u32[]{:S(2)}) collective-permute-start(bf16[256,128]{1,0:T(8,128)(2,1)S(1)} %get-tuple-element.64.refs_0_), channel_id=1, source_target_pairs={{0,4},{2,6},{4,0},{6,2},{8,12},{10,14},{12,8},{14,10},{16,20},{18,... | collective-permute-start | bytes 196616 | tf_op jit(solution)/shard_map/ppermute | solution.py:381
  37.7 2.0 %collective-permute-start.22 = (bf16[256,128]{1,0:T(8,128)(2,1)S(1)}, bf16[256,128]{1,0:T(8,128)(2,1)S(1)}, u32[]{:S(2)}, u32[]{:S(2)}) collective-permute-start(bf16[256,128]{1,0:T(8,128)(2,1)S(1)} %get-tuple-element.75), channel_id=1, source_target_pairs={{0,6},{2,4},{4,2},{6,0},{8,14},{10,12},{12,10},{14,8},{16,22},{18,... | collective-permute-start | bytes 196616 | tf_op jit(solution)/shard_map/ppermute | solution.py:381
  39.7 0.0 collective-permute-done.13.back_a
  39.7 0.0 collective-permute-done.14.back_b
  39.7 0.5 %merge.1 = (bf16[256,128]{1,0:T(8,128)(2,1)S(1)}, bf16[256,128]{1,0:T(8,128)(2,1)S(1)}, bf16[256,128]{1,0:T(8,128)(2,1)S(1)}, bf16[256,128]{1,0:T(8,128)(2,1)S(1)}) custom-call(bf16[3,272,128]{2,1,0:T(8,128)(2,1)S(1)} %collective-permute-done.13.back_a, bf16[3,272,128]{2,1,0:T(8,128)(2,1)S(1)} %collective-permute-done.14.back_b, ...), custom_call_target="tpu_custom_call" | custom-call | bytes 2097152 | tf_op jit(solution)/shard_map/merge/pallas_call | solution.py:485
  40.2 0.2 collective-permute-start.17
  40.4 1.2 %collective-permute-start.18 = (bf16[256,128]{1,0:T(8,128)(2,1)S(1)}, bf16[256,128]{1,0:T(8,128)(2,1)S(1)}, u32[]{:S(2)}, u32[]{:S(2)}) collective-permute-start(bf16[256,128]{1,0:T(8,128)(2,1)S(1)} %get-tuple-element.67), channel_id=1, source_target_pairs={{0,4},{2,6},{4,0},{6,2},{8,12},{10,14},{12,8},{14,10},{16,20},{18,... | collective-permute-start | bytes 196616 | tf_op jit(solution)/shard_map/ppermute | solution.py:381
  41.6 0.8 %collective-permute-start.19 = (bf16[256,128]{1,0:T(8,128)(2,1)S(1)}, bf16[256,128]{1,0:T(8,128)(2,1)S(1)}, u32[]{:S(2)}, u32[]{:S(2)}) collective-permute-start(bf16[256,128]{1,0:T(8,128)(2,1)S(1)} %get-tuple-element.68), channel_id=1, source_target_pairs={{0,6},{2,4},{4,2},{6,0},{8,14},{10,12},{12,10},{14,8},{16,22},{18,... | collective-permute-start | bytes 196616 | tf_op jit(solution)/shard_map/ppermute | solution.py:381
  42.4 0.0 collective-permute-done.20.refs_5_.refs_6_
  42.4 2.2 %columns.3 = (bf16[256,128]{1,0:T(8,128)(2,1)S(1)}, bf16[256,128]{1,0:T(8,128)(2,1)S(1)}) custom-call(bf16[256,1536]{1,0:T(8,128)(2,1)S(1)} %get-tuple-element.63.refs_14_.refs_0_, bf16[256,1024]{1,0:T(8,128)(2,1)S(1)} %get-tuple-element.69.refs_1_, bf16[1024,256]{1,0:T(8,128)(2,1)S(1)} %get-tuple-element.70.refs_2_, ...), custom_call_target="tpu_custom_call" | custom-call | flops 1879048192 | bytes 1572864 | tf_op jit(solution)/shard_map/columns/pallas_call | solution.py:496
  44.6 0.1 collective-permute-start.21
  44.7 0.0 collective-permute-done.22.refs_7_
  44.7 0.0 collective-permute-done.17.refs_1_
  44.7 0.0 collective-permute-done.18.refs_2_
  44.8 1.5 %collective-permute-done.19.refs_3_ = bf16[256,128]{1,0:T(8,128)(2,1)S(1)} collective-permute-done((bf16[256,128]{1,0:T(8,128)(2,1)S(1)}, bf16[256,128]{1,0:T(8,128)(2,1)S(1)}, u32[]{:S(2)}, u32[]{:S(2)}) %collective-permute-start.19) | collective-permute-done | bytes 65568 | tf_op jit(solution)/shard_map/ppermute | solution.py:381
  46.2 0.0 collective-permute-done.21.refs_5_
  46.2 0.8 %join.1 = (bf16[256,512]{1,0:T(8,128)(2,1)}, bf16[256,512]{1,0:T(8,128)(2,1)}) custom-call(bf16[256,128]{1,0:T(8,128)(2,1)S(1)} %get-tuple-element.65.refs_6_.refs_0_, bf16[256,128]{1,0:T(8,128)(2,1)S(1)} %collective-permute-done.17.refs_1_, bf16[256,128]{1,0:T(8,128)(2,1)S(1)} %collective-permute-done.18.refs_2_, ...), custom_call_target="tpu_custom_call" | custom-call | bytes 1048576 | tf_op jit(solution)/shard_map/join/pallas_call | solution.py:504
Async XLA Ops:
  0.6 9.2 %collective-permute-start.1 = (bf16[256,512]{1,0:T(8,128)(2,1)}, bf16[256,512]{1,0:T(8,128)(2,1)S(1)}, u32[]{:S(2)}, u32[]{:S(2)}) collective-permute-start(bf16[256,512]{1,0:T(8,128)(2,1)} %audio.3), channel_id=1, source_target_pairs={{0,1},{1,0},{2,3},{3,2},{4,5},{5,4},{6,7},{7,6},{8,9},{9,8},{10,11... | collective-permute-start | bytes 786440 | tf_op jit(solution)/shard_map/ppermute | solution.py:376
  1.9 11.8 %collective-permute-start.7 = (bf16[256,512]{1,0:T(8,128)(2,1)}, bf16[256,512]{1,0:T(8,128)(2,1)S(1)}, u32[]{:S(2)}, u32[]{:S(2)}) collective-permute-start(bf16[256,512]{1,0:T(8,128)(2,1)} %video.3), channel_id=1, source_target_pairs={{0,1},{1,0},{2,3},{3,2},{4,5},{5,4},{6,7},{7,6},{8,9},{9,8},{10,11... | collective-permute-start | bytes 786440 | tf_op jit(solution)/shard_map/ppermute | solution.py:376
  3.3 3.0 %collective-permute-start = (bf16[528,128]{1,0:T(8,128)(2,1)S(1)}, bf16[528,128]{1,0:T(8,128)(2,1)S(1)}, u32[]{:S(2)}, u32[]{:S(2)}) collective-permute-start(bf16[528,128]{1,0:T(8,128)(2,1)S(1)} %get-tuple-element.39), channel_id=1, source_target_pairs={{0,2},{2,0},{4,6},{6,4},{8,10},{10,8},{12,14},{14,12},{16,18},{18,... | collective-permute-start | bytes 405512 | tf_op jit(solution)/shard_map/ppermute | solution.py:381
  4.6 5.2 %collective-permute-start.2 = (bf16[528,128]{1,0:T(8,128)(2,1)S(1)}, bf16[528,128]{1,0:T(8,128)(2,1)S(1)}, u32[]{:S(2)}, u32[]{:S(2)}) collective-permute-start(bf16[528,128]{1,0:T(8,128)(2,1)S(1)} %get-tuple-element.42), channel_id=1, source_target_pairs={{0,4},{2,6},{4,0},{6,2},{8,12},{10,14},{12,8},{14,10},{16,20},{18,... | collective-permute-start | bytes 405512 | tf_op jit(solution)/shard_map/ppermute | solution.py:381
  5.9 9.8 %collective-permute-start.6 = (bf16[528,128]{1,0:T(8,128)(2,1)S(1)}, bf16[528,128]{1,0:T(8,128)(2,1)S(1)}, u32[]{:S(2)}, u32[]{:S(2)}) collective-permute-start(bf16[528,128]{1,0:T(8,128)(2,1)S(1)} %get-tuple-element.48), channel_id=1, source_target_pairs={{0,6},{2,4},{4,2},{6,0},{8,14},{10,12},{12,10},{14,8},{16,22},{18,... | collective-permute-start | bytes 405512 | tf_op jit(solution)/shard_map/ppermute | solution.py:381
  10.2 6.7 %collective-permute-start.3 = (bf16[256,128]{1,0:T(8,128)(2,1)S(1)}, bf16[256,128]{1,0:T(8,128)(2,1)S(1)}, u32[]{:S(2)}, u32[]{:S(2)}) collective-permute-start(bf16[256,128]{1,0:T(8,128)(2,1)S(1)} %get-tuple-element.44), channel_id=1, source_target_pairs={{0,2},{2,0},{4,6},{6,4},{8,10},{10,8},{12,14},{14,12},{16,18},{18,... | collective-permute-start | bytes 196616 | tf_op jit(solution)/shard_map/ppermute | solution.py:381
  11.6 5.9 %collective-permute-start.4 = (bf16[256,128]{1,0:T(8,128)(2,1)S(1)}, bf16[256,128]{1,0:T(8,128)(2,1)S(1)}, u32[]{:S(2)}, u32[]{:S(2)}) collective-permute-start(bf16[256,128]{1,0:T(8,128)(2,1)S(1)} %get-tuple-element.45), channel_id=1, source_target_pairs={{0,4},{2,6},{4,0},{6,2},{8,12},{10,14},{12,8},{14,10},{16,20},{18,... | collective-permute-start | bytes 196616 | tf_op jit(solution)/shard_map/ppermute | solution.py:381
  12.8 4.6 %collective-permute-start.5 = (bf16[256,128]{1,0:T(8,128)(2,1)S(1)}, bf16[256,128]{1,0:T(8,128)(2,1)S(1)}, u32[]{:S(2)}, u32[]{:S(2)}) collective-permute-start(bf16[256,128]{1,0:T(8,128)(2,1)S(1)} %get-tuple-element.46), channel_id=1, source_target_pairs={{0,6},{2,4},{4,2},{6,0},{8,14},{10,12},{12,10},{14,8},{16,22},{18,... | collective-permute-start | bytes 196616 | tf_op jit(solution)/shard_map/ppermute | solution.py:381
  14.1 6.8 %collective-permute-start.10 = (bf16[256,128]{1,0:T(8,128)(2,1)S(1)}, bf16[256,128]{1,0:T(8,128)(2,1)S(1)}, u32[]{:S(2)}, u32[]{:S(2)}) collective-permute-start(bf16[256,128]{1,0:T(8,128)(2,1)S(1)} %get-tuple-element.54), channel_id=1, source_target_pairs={{0,2},{2,0},{4,6},{6,4},{8,10},{10,8},{12,14},{14,12},{16,18},{18,... | collective-permute-start | bytes 196616 | tf_op jit(solution)/shard_map/ppermute | solution.py:381
  15.7 7.2 %collective-permute-start.11 = (bf16[256,128]{1,0:T(8,128)(2,1)S(1)}, bf16[256,128]{1,0:T(8,128)(2,1)S(1)}, u32[]{:S(2)}, u32[]{:S(2)}) collective-permute-start(bf16[256,128]{1,0:T(8,128)(2,1)S(1)} %get-tuple-element.55), channel_id=1, source_target_pairs={{0,4},{2,6},{4,0},{6,2},{8,12},{10,14},{12,8},{14,10},{16,20},{18,... | collective-permute-start | bytes 196616 | tf_op jit(solution)/shard_map/ppermute | solution.py:381
  16.9 6.0 %collective-permute-start.12 = (bf16[256,128]{1,0:T(8,128)(2,1)S(1)}, bf16[256,128]{1,0:T(8,128)(2,1)S(1)}, u32[]{:S(2)}, u32[]{:S(2)}) collective-permute-start(bf16[256,128]{1,0:T(8,128)(2,1)S(1)} %get-tuple-element.56), channel_id=1, source_target_pairs={{0,6},{2,4},{4,2},{6,0},{8,14},{10,12},{12,10},{14,8},{16,22},{18,... | collective-permute-start | bytes 196616 | tf_op jit(solution)/shard_map/ppermute | solution.py:381
  17.5 8.8 %collective-permute-start.8 = (bf16[3,272,128]{2,1,0:T(8,128)(2,1)S(1)}, bf16[3,272,128]{2,1,0:T(8,128)(2,1)S(1)}, u32[]{:S(2)}, u32[]{:S(2)}) collective-permute-start(bf16[3,272,128]{2,1,0:T(8,128)(2,1)S(1)} %get-tuple-element.52), channel_id=1, source_target_pairs={{8,16},{10,18},{12,20},{14,22},{16,8},{18,10},{20,12},{22,14},{9,1... | collective-permute-start | bytes 626696 | tf_op jit(solution)/shard_map/ppermute | solution.py:387
  20.7 6.4 %collective-permute-start.9 = (bf16[3,272,128]{2,1,0:T(8,128)(2,1)S(1)}, bf16[3,272,128]{2,1,0:T(8,128)(2,1)S(1)}, u32[]{:S(2)}, u32[]{:S(2)}) collective-permute-start(bf16[3,272,128]{2,1,0:T(8,128)(2,1)S(1)} %get-tuple-element.53), channel_id=1, source_target_pairs={{0,8},{2,10},{4,12},{6,14},{8,0},{10,2},{12,4},{14,6},{16,24},{18,... | collective-permute-start | bytes 626696 | tf_op jit(solution)/shard_map/ppermute | solution.py:387
  20.9 12.9 %collective-permute-start.15 = (bf16[3,256,128]{2,1,0:T(8,128)(2,1)S(1)}, bf16[3,256,128]{2,1,0:T(8,128)(2,1)S(1)}, u32[]{:S(2)}, u32[]{:S(2)}) collective-permute-start(bf16[3,256,128]{2,1,0:T(8,128)(2,1)S(1)} %halo.4), channel_id=1, source_target_pairs={{8,16},{10,18},{12,20},{14,22},{16,8},{18,10},{20,12},{22,14},{9,1... | collective-permute-start | bytes 589832 | tf_op jit(solution)/shard_map/ppermute | solution.py:387
  26.2 7.6 %collective-permute-start.16 = (bf16[3,256,128]{2,1,0:T(8,128)(2,1)S(1)}, bf16[3,256,128]{2,1,0:T(8,128)(2,1)S(1)}, u32[]{:S(2)}, u32[]{:S(2)}) collective-permute-start(bf16[3,256,128]{2,1,0:T(8,128)(2,1)S(1)} %halo.5), channel_id=1, source_target_pairs={{0,8},{2,10},{4,12},{6,14},{8,0},{10,2},{12,4},{14,6},{16,24},{18,... | collective-permute-start | bytes 589832 | tf_op jit(solution)/shard_map/ppermute | solution.py:387
  29.6 10.1 %collective-permute-start.13 = (bf16[3,272,128]{2,1,0:T(8,128)(2,1)S(1)}, bf16[3,272,128]{2,1,0:T(8,128)(2,1)S(1)}, u32[]{:S(2)}, u32[]{:S(2)}) collective-permute-start(bf16[3,272,128]{2,1,0:T(8,128)(2,1)S(1)} %get-tuple-element.59), channel_id=1, source_target_pairs={{0,8},{2,10},{4,12},{6,14},{8,0},{10,2},{12,4},{14,6},{16,24},{18,... | collective-permute-start | bytes 626696 | tf_op jit(solution)/shard_map/ppermute | solution.py:387
  30.4 9.3 %collective-permute-start.14 = (bf16[3,272,128]{2,1,0:T(8,128)(2,1)S(1)}, bf16[3,272,128]{2,1,0:T(8,128)(2,1)S(1)}, u32[]{:S(2)}, u32[]{:S(2)}) collective-permute-start(bf16[3,272,128]{2,1,0:T(8,128)(2,1)S(1)} %get-tuple-element.60), channel_id=1, source_target_pairs={{8,16},{10,18},{12,20},{14,22},{16,8},{18,10},{20,12},{22,14},{9,1... | collective-permute-start | bytes 626696 | tf_op jit(solution)/shard_map/ppermute | solution.py:387
  36.4 6.0 %collective-permute-start.20 = (bf16[256,128]{1,0:T(8,128)(2,1)S(1)}, bf16[256,128]{1,0:T(8,128)(2,1)S(1)}, u32[]{:S(2)}, u32[]{:S(2)}) collective-permute-start(bf16[256,128]{1,0:T(8,128)(2,1)S(1)} %get-tuple-element.64.refs_0_), channel_id=1, source_target_pairs={{0,4},{2,6},{4,0},{6,2},{8,12},{10,14},{12,8},{14,10},{16,20},{18,... | collective-permute-start | bytes 196616 | tf_op jit(solution)/shard_map/ppermute | solution.py:381
  37.7 7.0 %collective-permute-start.22 = (bf16[256,128]{1,0:T(8,128)(2,1)S(1)}, bf16[256,128]{1,0:T(8,128)(2,1)S(1)}, u32[]{:S(2)}, u32[]{:S(2)}) collective-permute-start(bf16[256,128]{1,0:T(8,128)(2,1)S(1)} %get-tuple-element.75), channel_id=1, source_target_pairs={{0,6},{2,4},{4,2},{6,0},{8,14},{10,12},{12,10},{14,8},{16,22},{18,... | collective-permute-start | bytes 196616 | tf_op jit(solution)/shard_map/ppermute | solution.py:381
  40.2 4.5 %collective-permute-start.17 = (bf16[256,128]{1,0:T(8,128)(2,1)S(1)}, bf16[256,128]{1,0:T(8,128)(2,1)S(1)}, u32[]{:S(2)}, u32[]{:S(2)}) collective-permute-start(bf16[256,128]{1,0:T(8,128)(2,1)S(1)} %get-tuple-element.66), channel_id=1, source_target_pairs={{0,2},{2,0},{4,6},{6,4},{8,10},{10,8},{12,14},{14,12},{16,18},{18,... | collective-permute-start | bytes 196616 | tf_op jit(solution)/shard_map/ppermute | solution.py:381
  40.4 4.3 %collective-permute-start.18 = (bf16[256,128]{1,0:T(8,128)(2,1)S(1)}, bf16[256,128]{1,0:T(8,128)(2,1)S(1)}, u32[]{:S(2)}, u32[]{:S(2)}) collective-permute-start(bf16[256,128]{1,0:T(8,128)(2,1)S(1)} %get-tuple-element.67), channel_id=1, source_target_pairs={{0,4},{2,6},{4,0},{6,2},{8,12},{10,14},{12,8},{14,10},{16,20},{18,... | collective-permute-start | bytes 196616 | tf_op jit(solution)/shard_map/ppermute | solution.py:381
  41.6 4.6 %collective-permute-start.19 = (bf16[256,128]{1,0:T(8,128)(2,1)S(1)}, bf16[256,128]{1,0:T(8,128)(2,1)S(1)}, u32[]{:S(2)}, u32[]{:S(2)}) collective-permute-start(bf16[256,128]{1,0:T(8,128)(2,1)S(1)} %get-tuple-element.68), channel_id=1, source_target_pairs={{0,6},{2,4},{4,2},{6,0},{8,14},{10,12},{12,10},{14,8},{16,22},{18,... | collective-permute-start | bytes 196616 | tf_op jit(solution)/shard_map/ppermute | solution.py:381
  44.6 1.6 %collective-permute-start.21 = (bf16[256,128]{1,0:T(8,128)(2,1)S(1)}, bf16[256,128]{1,0:T(8,128)(2,1)S(1)}, u32[]{:S(2)}, u32[]{:S(2)}) collective-permute-start(bf16[256,128]{1,0:T(8,128)(2,1)S(1)} %get-tuple-element.74), channel_id=1, source_target_pairs={{0,2},{2,0},{4,6},{6,4},{8,10},{10,8},{12,14},{14,12},{16,18},{18,... | collective-permute-start | bytes 196616 | tf_op jit(solution)/shard_map/ppermute | solution.py:381
